TPU v7x, 32 devices: a whole 2x2x4 slice. The times are simulated.
32 devices in a mesh: group: 1, node: 16 (over z, y, core), local: 2 (over x).
Axes of the slice: x: 2, y: 2, z: 4, core: 2. Of those that a mesh axis runs over, the one named last changes fastest.
Arguments:
- moe_rows: bfloat16 [256, 7168], P(('group', 'node', 'local')), may hold values from -6 to 6
- route_ids: int32 [256, 8], P(('group', 'node', 'local')), may hold values from 0 to 15, all different within a row; in each aligned block of 8 rows (0 to 7, 8 to 15, ...) at most 8 rows name the same one
- route_gates: float32 [256, 8], P(('group', 'node', 'local')), may hold values from 0.05 to 1
- w_gate: bfloat16 [16, 7168, 1024], P('node', None, 'local'), may hold values from -0.0625 to 0.0625
- w_up: bfloat16 [16, 7168, 1024], P('node', None, 'local'), may hold values from -0.0625 to 0.0625
- w_down: bfloat16 [16, 1024, 7168], P('node', 'local'), may hold values from -0.1875 to 0.1875
- query_latent: bfloat16 [64, 64, 512], P(('group', 'node', 'local')), may hold values from -16 to 16
- query_rope: bfloat16 [64, 64, 64], P(('group', 'node', 'local')), may hold values from -4 to 4
- cache_latent: bfloat16 [64, 512, 512], P(('group', 'node', 'local')), may hold values from -4 to 4
- cache_rope: bfloat16 [64, 64, 512], P(('group', 'node', 'local')), may hold values from -4 to 4
- cache_lengths: int32 [64], P(('group', 'node', 'local')), may hold values from 64 to 512, as said below
Outputs:
- moe_out: bfloat16 [256, 7168], P(('group', 'node', 'local'))
- attn_latent: bfloat16 [64, 64, 512], P(('group', 'node', 'local'))
Inputs may be any that keep to these rules, and one draw needn't show every extreme that they name: `route_ids`: each row names 8 different experts. In the rows of one device (aligned blocks of 8 rows) no expert is named by more than 8 rows; some expert is named by exactly 8 rows in some block. `cache_lengths`: some row's length is exactly 512.
All inputs are finite; a program needn't handle non-finite values.
Results may differ from a plain program's by a relative error of at most 0.0057.
Values may be sent and summed in bfloat16 or wider, within the bound.
No kernel may reach another device: no remote copies, remote signals or barrier semaphores. Data moves between devices by JAX's collectives and lax.ppermute only.
A program may use at most 128 MiB of HBM per device.

v0:
```python
import jax
import jax.numpy as jnp
from jax import lax
from jax.sharding import PartitionSpec as P

score_scale = 192.0 ** (-0.5)


def slot_numbers(block_ids, expert_count):
    member = jnp.sum(
        (block_ids[:, :, None] == jnp.arange(expert_count, dtype=jnp.int32)[None, None, :]).astype(
            jnp.int32
        ),
        axis=1,
    )
    before = jnp.cumsum(member, axis=0) - member
    return jnp.take_along_axis(before, block_ids, axis=1)


def expert_hidden(row_block, gate_mat, up_mat):
    gate_act = jnp.dot(row_block, gate_mat, preferred_element_type=jnp.float32)
    up_act = jnp.dot(row_block, up_mat, preferred_element_type=jnp.float32)
    return (jax.nn.silu(gate_act) * up_act).astype(jnp.bfloat16)


def body(
    moe_rows,
    route_ids,
    route_gates,
    w_gate,
    w_up,
    w_down,
    query_latent,
    query_rope,
    cache_latent,
    cache_rope,
    cache_lengths,
):
    experts = lax.axis_size("node")
    tok_count, route_count = route_ids.shape
    width = moe_rows.shape[1]
    capacity = max(2, min(tok_count, 2 * tok_count * route_count // experts))
    slot_index = slot_numbers(route_ids, experts)
    slot_codes = route_ids * capacity + slot_index
    places = jnp.arange(experts * capacity, dtype=jnp.int32)
    dispatch = jnp.sum(
        (slot_codes[None, :, :] == places[:, None, None]).astype(jnp.bfloat16), axis=2
    )
    outgoing = jnp.dot(dispatch, moe_rows, preferred_element_type=jnp.float32).astype(jnp.bfloat16)
    outgoing = outgoing.reshape(experts, capacity, width)
    arrived = lax.all_to_all(outgoing, "node", split_axis=0, concat_axis=0, tiled=True)
    gathered = lax.all_gather(arrived, "local", axis=0, tiled=True)
    gathered = gathered.reshape(-1, width)
    gate_mat = w_gate[0]
    up_mat = w_up[0]
    down_mat = w_down[0]
    hidden_piece = expert_hidden(gathered, gate_mat, up_mat)
    partial_value = lax.psum_scatter(
        jnp.dot(hidden_piece, down_mat, preferred_element_type=jnp.float32),
        "local",
        scatter_dimension=0,
        tiled=True,
    )
    expert_out = partial_value.astype(jnp.bfloat16).reshape(experts, capacity, width)
    returned = lax.all_to_all(expert_out, "node", split_axis=0, concat_axis=0, tiled=True).reshape(
        experts * capacity, width
    )
    picked = returned[slot_codes]
    gate_share = 2.5 * route_gates / jnp.sum(route_gates, axis=1, keepdims=True)
    moe_out = jnp.sum(gate_share[:, :, None] * picked.astype(jnp.float32), axis=1).astype(
        jnp.bfloat16
    )
    slot_count = cache_latent.shape[1]
    scores = jnp.einsum(
        "rhc,rjc->rhj", query_latent, cache_latent, preferred_element_type=jnp.float32
    )
    scores = (
        scores
        + jnp.einsum("rhp,rpj->rhj", query_rope, cache_rope, preferred_element_type=jnp.float32)
    ) * score_scale
    in_range = jnp.arange(slot_count, dtype=jnp.int32)[None, None, :] < cache_lengths[:, None, None]
    scores = jnp.where(in_range, scores, -jnp.inf)
    row_peak = jnp.max(scores, axis=-1, keepdims=True)
    lifted = jnp.where(in_range, jnp.exp(scores - row_peak), 0.0)
    weights = (lifted / jnp.sum(lifted, axis=-1, keepdims=True)).astype(jnp.bfloat16)
    attn_latent = jnp.einsum(
        "rhj,rjc->rhc", weights, cache_latent, preferred_element_type=jnp.float32
    ).astype(jnp.bfloat16)
    return (moe_out, attn_latent)


def solution(mesh):
    return jax.shard_map(
        body,
        mesh=mesh,
        in_specs=(
            P(("group", "node", "local"), None),
            P(("group", "node", "local"), None),
            P(("group", "node", "local"), None),
            P("node", None, "local"),
            P("node", None, "local"),
            P("node", "local", None),
            P(("group", "node", "local"), None, None),
            P(("group", "node", "local"), None, None),
            P(("group", "node", "local"), None, None),
            P(("group", "node", "local"), None, None),
            P(("group", "node", "local")),
        ),
        out_specs=(P(("group", "node", "local"), None), P(("group", "node", "local"), None, None)),
        check_vma=False,
    )
```

profile of v0, /device:TPU:0, one launch (start us, length us, event | category | flops | bytes accessed | tf_op | source)
XLA Modules:
  0.0 276.3 jit_solution(10813062069249393089)
XLA Ops:
  7.2 0.9 convert_reduce_fusion
  8.1 0.7 bitcast_or_fusion
  8.8 0.1 reshape.65
  8.9 0.7 gather_fusion.1
  9.6 0.1 reshape.68
  9.7 0.1 fusion.38
  9.8 0.7 fusion.1
  10.5 50.0 %all_to_all.10 = bf16[16,8,7168]{2,1,0:T(8,128)(2,1)} all-to-all(bf16[16,8,7168]{2,1,0:T(8,128)(2,1)S(1)} %fusion.1), channel_id=1, replica_groups=mesh['group'=1,'node'=16,'local'=2] {'node'}, dimensions={0} | all-to-all | bytes 3670016 | tf_op jit(solution)/shard_map/all_to_all | solution.py:51
  60.6 50.3 %all-gather.2.cloned.1.call-done = bf16[32,8,7168]{2,1,0:T(8,128)(2,1)} async-done(((bf16[16,8,7168]{2,1,0:T(8,128)(2,1)}), bf16[32,8,7168]{2,1,0:T(8,128)(2,1)}) %all-gather.2.cloned.1.call-update) | async-done | bytes 3670032 | tf_op jit(solution)/shard_map/all_gather | solution.py:52
  110.9 6.2 %fusion.6 = f32[256,512]{1,0:T(8,128)S(1)} fusion(bf16[1,7168,512]{2,1,0:T(8,128)(2,1)} %param.14, bf16[32,8,7168]{2,1,0:T(8,128)(2,1)} %all-gather.2.cloned.1.call-done), kind=kOutput, calls=%fused_computation.9 | convolution fusion | flops 1879048192 | bytes 11534336 | tf_op jit(solution)/shard_map/dot_general | solution.py:21
  117.2 13.2 %fusion.2 = f32[256,7168]{1,0:T(8,128)} fusion(bf16[1,512,7168]{2,1,0:T(8,128)(2,1)} %param.16, bf16[1,7168,512]{2,1,0:T(8,128)(2,1)} %param.15, bf16[32,8,7168]{2,1,0:T(8,128)(2,1)} %all-gather.2.cloned.1.call-done, f32[256,512]{1,0:T(8,128)S(1)} %fusion.6), kind=kOutput, calls=%fused_computation.5 | convolution fusion | flops 3758882816 | bytes 26214400 | tf_op jit(solution)/shard_map/dot_general | solution.py:59
  130.5 88.5 %reduce-scatter.2.cloned.1.call-done = f32[128,7168]{1,0:T(8,128)} async-done(((f32[256,7168]{1,0:T(8,128)}), f32[128,7168]{1,0:T(8,128)}) %reduce-scatter.2.cloned.1.call-update) | async-done | bytes 3670032 | tf_op jit(solution)/shard_map/reduce_scatter | solution.py:58
  219.0 3.5 %convert_bitcast_fusion = bf16[16,8,7168]{2,1,0:T(8,128)(2,1)} fusion(f32[128,7168]{1,0:T(8,128)} %reduce-scatter.2.cloned.1.call-done), kind=kLoop, calls=%fused_computation.15 | loop fusion | flops 917504 | bytes 5505024 | tf_op jit(solution)/shard_map/reshape | solution.py:64
  222.5 5.8 %all-to-all-start.1 = ((bf16[16,8,7168]{2,1,0:T(8,128)(2,1)}), bf16[16,8,7168]{2,1,0:T(8,128)(2,1)S(1)}, u32[]{:S(2)}, u32[]{:S(2)}) async-start(bf16[16,8,7168]{2,1,0:T(8,128)(2,1)} %convert_bitcast_fusion), calls=%async_computation.2 | async-start | bytes 3670016 | tf_op jit(solution)/shard_map/all_to_all | solution.py:65
  228.3 0.1 reshape.59
  228.4 0.1 reduce_sum.48
  228.5 0.1 iota_compare_fusion.2
  228.6 0.4 fusion.43
  229.1 0.2 fusion.23
  229.2 0.2 fusion.42
  229.5 1.0 convolution_convert_fusion.1
  230.5 34.3 %all-to-all-done.1 = bf16[16,8,7168]{2,1,0:T(8,128)(2,1)S(1)} async-done(((bf16[16,8,7168]{2,1,0:T(8,128)(2,1)}), bf16[16,8,7168]{2,1,0:T(8,128)(2,1)S(1)}, u32[]{:S(2)}, u32[]{:S(2)}) %all-to-all-start.1) | async-done | bytes 1835040 | tf_op jit(solution)/shard_map/all_to_all | solution.py:65
  264.8 2.1 gather_fusion
  266.9 2.6 fusion.10
  (25 shorter events, 0.3 us)
Async XLA Ops:
  7.2 221.4 %copy-start = (bf16[2,512,512]{2,1,0:T(8,128)(2,1)S(1)}, bf16[2,512,512]{2,1,0:T(8,128)(2,1)}, u32[]{:S(2)}) copy-start(bf16[2,512,512]{2,1,0:T(8,128)(2,1)} %param.19) | copy-start | bytes 3145732
  7.2 2.5 copy-start.4
  7.2 2.6 copy-start.3
  7.2 103.7 %all-gather.2.cloned.1.call-start = ((), (), s32[]{:S(2)}) async-start(), calls=%async_computation.3 | async-start | bytes 5505024 | tf_op jit(solution)/shard_map/all_gather | solution.py:52
  60.6 158.4 %reduce-scatter.2.cloned.1.call-start = ((), (), s32[]{:S(2)}) async-start(), calls=%async_computation.4 | async-start | bytes 11010048 | tf_op jit(solution)/shard_map/reduce_scatter | solution.py:58
  130.4 98.0 %copy-start.6 = (f32[8,8]{1,0:T(8,128)S(1)}, f32[8,8]{1,0:T(8,128)}, u32[]{:S(2)}) copy-start(f32[8,8]{1,0:T(8,128)} %param.13) | copy-start | bytes 772
  130.4 98.1 %copy-start.7 = (s32[2]{0:T(128)S(1)}, s32[2]{0:T(128)}, u32[]{:S(2)}) copy-start(s32[2]{0:T(128)} %param.21) | copy-start | bytes 28
  130.5 98.1 %copy-start.2 = (bf16[2,64,512]{2,1,0:T(8,128)(2,1)S(1)}, bf16[2,64,512]{2,1,0:T(8,128)(2,1)}, u32[]{:S(2)}) copy-start(bf16[2,64,512]{2,1,0:T(8,128)(2,1)} %param.17) | copy-start | bytes 393220
  222.5 6.5 %copy-start.1 = (bf16[2,64,512]{2,1,0:T(8,128)(2,1)S(1)}, bf16[2,64,512]{2,1,0:T(8,128)(2,1)}, u32[]{:S(2)}) copy-start(bf16[2,64,512]{2,1,0:T(8,128)(2,1)} %param.20) | copy-start | bytes 393220
  222.5 6.5 %copy-start.5 = (bf16[2,64,64]{2,1,0:T(8,128)(2,1)S(1)}, bf16[2,64,64]{2,1,0:T(8,128)(2,1)}, u32[]{:S(2)}) copy-start(bf16[2,64,64]{2,1,0:T(8,128)(2,1)} %param.18) | copy-start | bytes 49156
  222.5 42.3 %all-to-all-start.1 = ((bf16[16,8,7168]{2,1,0:T(8,128)(2,1)}), bf16[16,8,7168]{2,1,0:T(8,128)(2,1)S(1)}, u32[]{:S(2)}, u32[]{:S(2)}) async-start(bf16[16,8,7168]{2,1,0:T(8,128)(2,1)} %convert_bitcast_fusion), calls=%async_computation.2 | async-start | bytes 3670016 | tf_op jit(solution)/shard_map/all_to_all | solution.py:65
Sparse Core Ops, SparseCore 0:
  60.7 50.1 all-gather.1
  130.6 88.4 reduce-scatter.1
where the time goes:
time: 281 us; the launch traced here: 276 us
  waiting for transfers between devices  173 us (62%)
  blocking collectives  50 us (18%)
  matrix products  21.8 us (8%)
  between operations  14.2 us (5%)
  other arithmetic  8.27 us (3%)
  starting transfers between devices  5.83 us (2%)
  local copies, waits for them, and re-layouts  3.07 us (1%)
    reduce_scatter x1, waiting for transfers between devices, body(): lax.psum_scatter(jnp.dot(hidden_piece, down_mat, preferred_element_type=j...  88.5 us
    all_gather x1, waiting for transfers between devices, body(): gathered = lax.all_gather(arrived, 'local', axis=0, tiled=True)  50.3 us
    all_to_all x1, blocking collectives, body(): lax.all_to_all(outgoing, 'node', split_axis=0, concat_axis=0, tiled=True)  50 us
    all_to_all x1, waiting for transfers between devices, body(): lax.all_to_all(expert_out, 'node', split_axis=0, concat_axis=0, tiled=True)  34.3 us
    dot_general x1, matrix products, body(): jnp.dot(hidden_piece, down_mat, preferred_element_type=jnp.float32)  13.2 us
    dot_general x1, matrix products, expert_hidden(): gate_act = jnp.dot(row_block, gate_mat, preferred_element_type=jnp.float32)  6.25 us
    all_to_all x1, starting transfers between devices, body(): lax.all_to_all(expert_out, 'node', split_axis=0, concat_axis=0, tiled=True)  5.75 us
  transfers between devices with their start and end apart: 3, of which 3 were waited for; matrix products, arithmetic and copies ran while one was open for 1% of the time, Pallas kernels for 0%

commit v1 on v0

v1 whole, which is shorter than its diff:
```python
import jax
import jax.numpy as jnp
import numpy as np
from jax import lax
from jax.sharding import PartitionSpec as P

score_scale = 192.0 ** (-0.5)
whole = ("node", "local")


def attention(query_latent, query_rope, cache_latent, cache_rope, cache_lengths):
    slot_count = cache_latent.shape[1]
    scores = jnp.einsum(
        "rhc,rjc->rhj", query_latent, cache_latent, preferred_element_type=jnp.float32
    )
    scores = (
        scores
        + jnp.einsum("rhp,rpj->rhj", query_rope, cache_rope, preferred_element_type=jnp.float32)
    ) * score_scale
    in_range = jnp.arange(slot_count, dtype=jnp.int32)[None, None, :] < cache_lengths[:, None, None]
    scores = jnp.where(in_range, scores, -jnp.inf)
    row_peak = jnp.max(scores, axis=-1, keepdims=True)
    lifted = jnp.where(in_range, jnp.exp(scores - row_peak), 0.0)
    weights = (lifted / jnp.sum(lifted, axis=-1, keepdims=True)).astype(jnp.bfloat16)
    return jnp.einsum(
        "rhj,rjc->rhc", weights, cache_latent, preferred_element_type=jnp.float32
    ).astype(jnp.bfloat16)


def share_columns(route_ids, route_gates, expert_count):
    gate_share = 2.5 * route_gates / jnp.sum(route_gates, axis=1, keepdims=True)
    chosen = route_ids[:, :, None] == jnp.arange(expert_count, dtype=jnp.int32)[None, None, :]
    table = jnp.sum(jnp.where(chosen, gate_share[:, :, None], 0.0), axis=1)
    high = table.astype(jnp.bfloat16)
    low = (table - high.astype(jnp.float32)).astype(jnp.bfloat16)
    empty = jnp.zeros((table.shape[0], -2 * expert_count % 128), jnp.bfloat16)
    return jnp.concatenate([high, low, empty], axis=1)


class Grid:
    def __init__(self):
        nodes, local = lax.axis_size("node"), lax.axis_size("local")
        self.sizes = (nodes // 4, 2, 2, local)
        node = lax.axis_index("node")
        self.place = (node // 4, node // 2 % 2, node % 2, lax.axis_index("local"))

    def shift(self, value, digit, step):
        pairs = []
        for place in np.ndindex(*self.sizes):
            other = list(place)
            other[digit] = (other[digit] + step) % self.sizes[digit]
            pairs.append(
                (
                    int(np.ravel_multi_index(place, self.sizes)),
                    int(np.ravel_multi_index(other, self.sizes)),
                )
            )
        return lax.ppermute(value, whole, pairs)

    def scatter_sum(self, value, digit, dim):
        size, here = self.sizes[digit], self.place[digit]
        total = lax.dynamic_index_in_dim(value, here, dim, keepdims=False).astype(jnp.float32)
        for step in range(1, size):
            part = lax.dynamic_index_in_dim(value, (here + step) % size, dim, keepdims=False)
            total = total + self.shift(part, digit, step).astype(jnp.float32)
        return total.astype(value.dtype)


HIGH, MIDDLE, CORE, LOCAL = range(4)


def body(
    moe_rows,
    route_ids,
    route_gates,
    w_gate,
    w_up,
    w_down,
    query_latent,
    query_rope,
    cache_latent,
    cache_rope,
    cache_lengths,
):
    grid = Grid()
    experts = lax.axis_size("node")
    width = moe_rows.shape[1]
    outgoing = jnp.concatenate(
        [moe_rows, share_columns(route_ids, route_gates, experts)], axis=1
    )
    gathered = lax.all_gather(outgoing, whole, axis=0, tiled=True)
    attn_latent = attention(query_latent, query_rope, cache_latent, cache_rope, cache_lengths)
    rows = gathered[:, :width]
    table = gathered[:, width : width + 2 * experts].astype(jnp.float32)
    table = table[:, :experts] + table[:, experts:]
    mine = jnp.arange(experts, dtype=jnp.int32) == lax.axis_index("node")
    share = jnp.sum(jnp.where(mine[None, :], table, 0.0), axis=1, keepdims=True)
    gate_act = jnp.dot(rows, w_gate[0], preferred_element_type=jnp.float32)
    up_act = jnp.dot(rows, w_up[0], preferred_element_type=jnp.float32)
    hidden = (jax.nn.silu(gate_act) * up_act).astype(jnp.bfloat16)
    pieces = []
    half = width // 2
    for piece in range(2):
        columns = w_down[0][:, piece * half : (piece + 1) * half]
        product = share * jnp.dot(hidden, columns, preferred_element_type=jnp.float32)
        product = product.astype(jnp.bfloat16).reshape(grid.sizes + (-1, half))
        product = grid.scatter_sum(product, CORE, 2)
        if piece == 0:
            product = grid.scatter_sum(product, LOCAL, 2)
            product = grid.scatter_sum(product, MIDDLE, 1)
        else:
            product = grid.scatter_sum(product, MIDDLE, 1)
            product = grid.scatter_sum(product, LOCAL, 1)
        pieces.append(grid.scatter_sum(product, HIGH, 0))
    moe_out = jnp.concatenate(pieces, axis=1)
    return (moe_out, attn_latent)


def solution(mesh):
    rows = P(("group", "node", "local"), None)
    blocks = P(("group", "node", "local"), None, None)
    return jax.shard_map(
        body,
        mesh=mesh,
        in_specs=(
            rows,
            rows,
            rows,
            P("node", None, "local"),
            P("node", None, "local"),
            P("node", "local", None),
            blocks,
            blocks,
            blocks,
            blocks,
            P(("group", "node", "local")),
        ),
        out_specs=(rows, blocks),
        check_vma=False,
    )
```

time: 281 us -> 135 us (0.48); the launches traced: 276 us -> 135 us
  waiting for transfers between devices: 173 us -> 84 us
  blocking collectives: 50 us -> 0 us
  matrix products: 21.8 us -> 12.4 us
  starting transfers between devices: 5.83 us -> 12.9 us
    reduce_scatter x1 -> x0, waiting for transfers between devices: 88.5 us -> none  [body(): lax.psum_scatter(jnp.dot(hidden_piece, down_mat, preferred_element_type=j...]
    all_to_all x1 -> x0, blocking collectives: 50 us -> none  [body(): lax.all_to_all(outgoing, 'node', split_axis=0, concat_axis=0, tiled=True)]
    all_to_all x1 -> x0, waiting for transfers between devices: 34.3 us -> none  [body(): lax.all_to_all(expert_out, 'node', split_axis=0, concat_axis=0, tiled=True)]
    ppermute x0 -> x12, waiting for transfers between devices: none -> 20.4 us  [shift(): return lax.ppermute(value, whole, pairs)]
    all_gather x1, waiting for transfers between devices: 50.3 us -> 63.6 us  [body(): gathered = lax.all_gather(outgoing, whole, axis=0, tiled=True)]
    ppermute x0 -> x12, starting transfers between devices: none -> 12.9 us  [shift(): return lax.ppermute(value, whole, pairs)]
    dot_general x6 -> x7, matrix products: 21.8 us -> 12.4 us  [the longest x1 6.38 us: body(): gate_act = jnp.dot(rows, w_gate[0], preferred_element_type=jnp.float32)]
    all_to_all x1 -> x0, starting transfers between devices: 5.75 us -> none  [body(): lax.all_to_all(expert_out, 'node', split_axis=0, concat_axis=0, tiled=True)]
  transfers between devices with their start and end apart: 3 -> 13, of which waited for: 3 -> 8; matrix products, arithmetic and copies ran while one was open for 1% -> 3% of each run, Pallas kernels for 0% -> 0%
where the time goes in v1:
time: 135 us
  waiting for transfers between devices  84 us (62%)
  between operations  14.4 us (11%)
  starting transfers between devices  12.9 us (10%)
  matrix products  12.4 us (9%)
  other arithmetic  6.82 us (5%)
  local copies, waits for them, and re-layouts  4.25 us (3%)
    all_gather x1, waiting for transfers between devices, body(): gathered = lax.all_gather(outgoing, whole, axis=0, tiled=True)  63.6 us
    ppermute x12, waiting for transfers between devices, shift(): return lax.ppermute(value, whole, pairs)  20.4 us
    ppermute x12, starting transfers between devices, shift(): return lax.ppermute(value, whole, pairs)  12.9 us
    dot_general x1, matrix products, body(): gate_act = jnp.dot(rows, w_gate[0], preferred_element_type=jnp.float32)  6.38 us
  transfers between devices with their start and end apart: 13, of which 8 were waited for; matrix products, arithmetic and copies ran while one was open for 3% of the time, Pallas kernels for 0%

profile of v1, /device:TPU:0, one launch (start us, length us, event | category | flops | bytes accessed | tf_op | source)
XLA Modules:
  0.0 134.9 jit_solution(386350913856757470)
XLA Ops:
  7.2 0.9 reduce_sum.36
  8.9 0.8 select_reduce_fusion
  9.7 1.6 %concatenate.6 = bf16[8,7296]{1,0:T(8,128)(2,1)} concatenate(bf16[8,7168]{1,0:T(8,128)(2,1)} %param.11, bf16[8,16]{1,0:T(8,128)(2,1)S(1)} %get-tuple-element.3, bf16[8,16]{1,0:T(8,128)(2,1)S(1)} %get-tuple-element.2, bf16[8,96]{1,0:T(8,128)(2,1)S(1)} %broadcast_in_dim.58), dimensions={1} | concatenate | bytes 233472 | tf_op jit(solution)/shard_map/concatenate | solution.py:88
  11.4 63.6 %all-gather.2.cloned.1.call-done = bf16[256,7296]{1,0:T(8,128)(2,1)} async-done(((bf16[8,7296]{1,0:T(8,128)(2,1)}), bf16[256,7296]{1,0:T(8,128)(2,1)}) %all-gather.2.cloned.1.call-update) | async-done | bytes 3735568 | tf_op jit(solution)/shard_map/all_gather | solution.py:91
  75.0 1.0 slice_convert_fusion
  76.2 6.4 %fusion.3 = f32[256,512]{1,0:T(8,128)S(1)} fusion(bf16[1,7168,512]{2,1,0:T(8,128)(2,1)} %param.14, bf16[256,7296]{1,0:T(8,128)(2,1)} %all-gather.2.cloned.1.call-done), kind=kOutput, calls=%fused_computation.3 | convolution fusion | flops 1879048192 | bytes 11534336 | tf_op jit(solution)/shard_map/dot_general | solution.py:98
  82.8 2.1 %fusion.19 = bf16[256,512]{1,0:T(8,128)(2,1)S(1)} fusion(bf16[1,7168,512]{2,1,0:T(8,128)(2,1)S(1)} %bitcast.80, bf16[256,7296]{1,0:T(8,128)(2,1)S(1)} %copy-done.4, f32[256,512]{1,0:T(8,128)S(1)} %fusion.3), kind=kOutput, calls=%fused_computation.19 | convolution fusion | flops 1879834624 | bytes 11796480 | tf_op jit(solution)/shard_map/dot_general | solution.py:99
  84.9 1.2 fusion.5
  86.1 1.2 fusion.6
  87.3 1.2 constant_dynamic-slice_fusion.1
  88.5 1.0 copy.32
  90.7 1.0 convolution_convert_fusion
  92.3 1.7 %fusion.12 = bf16[4,2,2,8,3584]{4,3,0,1,2:T(8,128)(2,1)S(1)} fusion(bf16[4,2,2,8,3584]{4,3,0,1,2:T(8,128)(2,1)} %collective-permute-done, bf16[4,2,1,2,8,3584]{5,4,3,2,1,0:T(8,128)(2,1)} %get-tuple-element.15), kind=kLoop, calls=%fused_computation.16 | loop fusion | flops 1835008 | bytes 2752512 | tf_op jit(solution)/shard_map/convert_element_type | solution.py:66
  94.0 1.5 %collective-permute-start.1 = (bf16[4,2,8,3584]{3,2,0,1:T(8,128)(2,1)S(1)}, bf16[4,2,8,3584]{3,2,0,1:T(8,128)(2,1)S(1)}, u32[]{:S(2)}, u32[]{:S(2)}) collective-permute-start(bf16[4,2,8,3584]{3,2,0,1:T(8,128)(2,1)S(1)} %dynamic-slice_bitcast_fusion.1), channel_id=1, source_target_pairs={{0,1},{1,0},{2,3},{3,2},{4,5},{5,4},{6,7},{7,6},{8,9},{9,8},{10,11... | collective-permute-start | bytes 1376264 | tf_op jit(solution)/shard_map/ppermute | solution.py:58
  96.4 10.3 %collective-permute-done.1 = bf16[4,2,8,3584]{3,2,0,1:T(8,128)(2,1)S(1)} collective-permute-done((bf16[4,2,8,3584]{3,2,0,1:T(8,128)(2,1)S(1)}, bf16[4,2,8,3584]{3,2,0,1:T(8,128)(2,1)S(1)}, u32[]{:S(2)}, u32[]{:S(2)}) %collective-permute-start.1) | collective-permute-done | bytes 458784 | tf_op jit(solution)/shard_map/ppermute | solution.py:58
  106.9 1.5 %collective-permute-start.2 = (bf16[4,8,3584]{2,1,0:T(8,128)(2,1)S(1)}, bf16[4,8,3584]{2,1,0:T(8,128)(2,1)S(1)}, u32[]{:S(2)}, u32[]{:S(2)}) collective-permute-start(bf16[4,8,3584]{2,1,0:T(8,128)(2,1)S(1)} %dynamic-slice_bitcast_fusion.3), channel_id=1, source_target_pairs={{0,4},{1,5},{2,6},{3,7},{4,0},{5,1},{6,2},{7,3},{8,12},{9,13},{10,... | collective-permute-start | bytes 688136 | tf_op jit(solution)/shard_map/ppermute | solution.py:58
  109.2 4.7 %collective-permute-done.2 = bf16[4,8,3584]{2,1,0:T(8,128)(2,1)S(1)} collective-permute-done((bf16[4,8,3584]{2,1,0:T(8,128)(2,1)S(1)}, bf16[4,8,3584]{2,1,0:T(8,128)(2,1)S(1)}, u32[]{:S(2)}, u32[]{:S(2)}) %collective-permute-start.2) | collective-permute-done | bytes 229408 | tf_op jit(solution)/shard_map/ppermute | solution.py:58
  114.0 1.2 collective-permute-start.3
  115.3 1.6 %collective-permute-start.4 = (bf16[8,3584]{1,0:T(8,128)(2,1)S(1)}, bf16[8,3584]{1,0:T(8,128)(2,1)S(1)}, u32[]{:S(2)}, u32[]{:S(2)}) collective-permute-start(bf16[8,3584]{1,0:T(8,128)(2,1)S(1)} %get-tuple-element.10), channel_id=1, source_target_pairs={{0,16},{1,17},{2,18},{3,19},{4,20},{5,21},{6,22},{7,23},{8,24},{9,... | collective-permute-start | bytes 172040 | tf_op jit(solution)/shard_map/ppermute | solution.py:58
  116.8 1.5 %collective-permute-start.5 = (bf16[8,3584]{1,0:T(8,128)(2,1)S(1)}, bf16[8,3584]{1,0:T(8,128)(2,1)S(1)}, u32[]{:S(2)}, u32[]{:S(2)}) collective-permute-start(bf16[8,3584]{1,0:T(8,128)(2,1)S(1)} %get-tuple-element.9), channel_id=1, source_target_pairs={{0,24},{1,25},{2,26},{3,27},{4,28},{5,29},{6,30},{7,31},{8,0},{9,1... | collective-permute-start | bytes 172040 | tf_op jit(solution)/shard_map/ppermute | solution.py:58
  118.4 1.7 %collective-permute-start.10 = (bf16[8,3584]{1,0:T(8,128)(2,1)S(1)}, bf16[8,3584]{1,0:T(8,128)(2,1)S(1)}, u32[]{:S(2)}, u32[]{:S(2)}) collective-permute-start(bf16[8,3584]{1,0:T(8,128)(2,1)S(1)} %get-tuple-element.13), channel_id=1, source_target_pairs={{0,16},{1,17},{2,18},{3,19},{4,20},{5,21},{6,22},{7,23},{8,24},{9,... | collective-permute-start | bytes 172040 | tf_op jit(solution)/shard_map/ppermute | solution.py:58
  120.1 1.3 collective-permute-start.11
  122.8 2.8 %collective-permute-done.10 = bf16[8,3584]{1,0:T(8,128)(2,1)S(1)} collective-permute-done((bf16[8,3584]{1,0:T(8,128)(2,1)S(1)}, bf16[8,3584]{1,0:T(8,128)(2,1)S(1)}, u32[]{:S(2)}, u32[]{:S(2)}) %collective-permute-start.10) | collective-permute-done | bytes 57376 | tf_op jit(solution)/shard_map/ppermute | solution.py:58
  125.6 1.7 %collective-permute-done.9 = bf16[8,3584]{1,0:T(8,128)(2,1)S(1)} collective-permute-done((bf16[8,3584]{1,0:T(8,128)(2,1)S(1)}, bf16[8,3584]{1,0:T(8,128)(2,1)S(1)}, u32[]{:S(2)}, u32[]{:S(2)}) %collective-permute-start.9) | collective-permute-done | bytes 57376 | tf_op jit(solution)/shard_map/ppermute | solution.py:58
  (61 shorter events, 7.0 us)
Async XLA Ops:
  7.2 82.7 %copy-start = (bf16[2,512,512]{2,1,0:T(8,128)(2,1)S(1)}, bf16[2,512,512]{2,1,0:T(8,128)(2,1)}, u32[]{:S(2)}) copy-start(bf16[2,512,512]{2,1,0:T(8,128)(2,1)} %param.19) | copy-start | bytes 3145732
  7.2 67.8 %all-gather.2.cloned.1.call-start = ((), (), s32[]{:S(2)}) async-start(), calls=%async_computation | async-start | bytes 3852288 | tf_op jit(solution)/shard_map/all_gather | solution.py:91
  75.0 7.6 %slice-start = ((s8[7340032]{0:T(1024)(128)(4,1)}), s8[4194304]{0:T(1024)(128)(4,1)S(1)}, s32[]{:S(2)}) async-start(s8[7340032]{0:T(1024)(128)(4,1)} %bitcast.79), calls=%async_computation.1 | async-start | bytes 8388608
  76.2 6.4 %copy-start.4 = (bf16[256,7296]{1,0:T(8,128)(2,1)S(1)}, bf16[256,7296]{1,0:T(8,128)(2,1)}, u32[]{:S(2)}) copy-start(bf16[256,7296]{1,0:T(8,128)(2,1)} %all-gather.2.cloned.1.call-done) | copy-start | bytes 11206660
  76.2 6.6 %slice-start.1 = ((s8[7340032]{0:T(1024)(128)(4,1)}), s8[3145728]{0:T(1024)(128)(4,1)S(1)}, s32[]{:S(2)}) async-start(s8[7340032]{0:T(1024)(128)(4,1)} %bitcast.79), calls=%async_computation.2 | async-start | bytes 6291456
  76.2 8.6 %slice-start.2 = ((s8[7340032]{0:T(1024)(128)(4,1)}), s8[4194304]{0:T(1024)(128)(4,1)S(1)}, s32[]{:S(2)}) async-start(s8[7340032]{0:T(1024)(128)(4,1)} %bitcast.81), calls=%async_computation.3 | async-start | bytes 8388608
  82.8 2.1 %slice-start.3 = ((s8[7340032]{0:T(1024)(128)(4,1)}), s8[3145728]{0:T(1024)(128)(4,1)S(1)}, s32[]{:S(2)}) async-start(s8[7340032]{0:T(1024)(128)(4,1)} %bitcast.81), calls=%async_computation.4 | async-start | bytes 6291456
  87.3 2.5 %copy-start.5 = (s32[2]{0:T(128)S(1)}, s32[2]{0:T(128)}, u32[]{:S(2)}) copy-start(s32[2]{0:T(128)} %param.21) | copy-start | bytes 28
  87.3 2.6 %copy-start.2 = (bf16[2,64,512]{2,1,0:T(8,128)(2,1)S(1)}, bf16[2,64,512]{2,1,0:T(8,128)(2,1)}, u32[]{:S(2)}) copy-start(bf16[2,64,512]{2,1,0:T(8,128)(2,1)} %param.17) | copy-start | bytes 393220
  87.3 3.1 %copy-start.1 = (bf16[2,64,512]{2,1,0:T(8,128)(2,1)S(1)}, bf16[2,64,512]{2,1,0:T(8,128)(2,1)}, u32[]{:S(2)}) copy-start(bf16[2,64,512]{2,1,0:T(8,128)(2,1)} %param.20) | copy-start | bytes 393220
  87.3 3.1 %copy-start.3 = (bf16[2,64,64]{2,1,0:T(8,128)(2,1)S(1)}, bf16[2,64,64]{2,1,0:T(8,128)(2,1)}, u32[]{:S(2)}) copy-start(bf16[2,64,64]{2,1,0:T(8,128)(2,1)} %param.18) | copy-start | bytes 49156
  89.5 2.8 %collective-permute-start = (bf16[4,2,2,8,3584]{4,3,0,1,2:T(8,128)(2,1)}, bf16[4,2,2,8,3584]{4,3,0,1,2:T(8,128)(2,1)}, u32[]{:S(2)}, u32[]{:S(2)}) collective-permute-start(bf16[4,2,2,8,3584]{4,3,0,1,2:T(8,128)(2,1)} %bitcast.75), channel_id=1, source_target_pairs={{0,2},{1,3},{2,0},{3,1},{4,6},{5,7},{6,4},{7,5},{8,10},{9,11},{10,... | collective-permute-start | bytes 2752520 | tf_op jit(solution)/shard_map/ppermute | solution.py:58
  91.8 3.7 %collective-permute-start.6 = (bf16[4,2,2,8,3584]{4,3,0,2,1:T(8,128)(2,1)S(1)}, bf16[4,2,2,8,3584]{4,3,0,2,1:T(8,128)(2,1)S(1)}, u32[]{:S(2)}, u32[]{:S(2)}) collective-permute-start(bf16[4,2,2,8,3584]{4,3,0,2,1:T(8,128)(2,1)S(1)} %bitcast.78), channel_id=1, source_target_pairs={{0,2},{1,3},{2,0},{3,1},{4,6},{5,7},{6,4},{7,5},{8,10},{9,11},{10,... | collective-permute-start | bytes 2752520 | tf_op jit(solution)/shard_map/ppermute | solution.py:58
  94.0 12.8 %collective-permute-start.1 = (bf16[4,2,8,3584]{3,2,0,1:T(8,128)(2,1)S(1)}, bf16[4,2,8,3584]{3,2,0,1:T(8,128)(2,1)S(1)}, u32[]{:S(2)}, u32[]{:S(2)}) collective-permute-start(bf16[4,2,8,3584]{3,2,0,1:T(8,128)(2,1)S(1)} %dynamic-slice_bitcast_fusion.1), channel_id=1, source_target_pairs={{0,1},{1,0},{2,3},{3,2},{4,5},{5,4},{6,7},{7,6},{8,9},{9,8},{10,11... | collective-permute-start | bytes 1376264 | tf_op jit(solution)/shard_map/ppermute | solution.py:58
  95.8 12.7 %collective-permute-start.7 = (bf16[4,2,8,3584]{3,2,0,1:T(8,128)(2,1)S(1)}, bf16[4,2,8,3584]{3,2,0,1:T(8,128)(2,1)S(1)}, u32[]{:S(2)}, u32[]{:S(2)}) collective-permute-start(bf16[4,2,8,3584]{3,2,0,1:T(8,128)(2,1)S(1)} %dynamic-slice_bitcast_fusion), channel_id=1, source_target_pairs={{0,4},{1,5},{2,6},{3,7},{4,0},{5,1},{6,2},{7,3},{8,12},{9,13},{10,... | collective-permute-start | bytes 1376264 | tf_op jit(solution)/shard_map/ppermute | solution.py:58
  106.9 7.0 %collective-permute-start.2 = (bf16[4,8,3584]{2,1,0:T(8,128)(2,1)S(1)}, bf16[4,8,3584]{2,1,0:T(8,128)(2,1)S(1)}, u32[]{:S(2)}, u32[]{:S(2)}) collective-permute-start(bf16[4,8,3584]{2,1,0:T(8,128)(2,1)S(1)} %dynamic-slice_bitcast_fusion.3), channel_id=1, source_target_pairs={{0,4},{1,5},{2,6},{3,7},{4,0},{5,1},{6,2},{7,3},{8,12},{9,13},{10,... | collective-permute-start | bytes 688136 | tf_op jit(solution)/shard_map/ppermute | solution.py:58
  108.6 9.8 %collective-permute-start.8 = (bf16[4,8,3584]{2,1,0:T(8,128)(2,1)S(1)}, bf16[4,8,3584]{2,1,0:T(8,128)(2,1)S(1)}, u32[]{:S(2)}, u32[]{:S(2)}) collective-permute-start(bf16[4,8,3584]{2,1,0:T(8,128)(2,1)S(1)} %dynamic-slice_bitcast_fusion.2), channel_id=1, source_target_pairs={{0,1},{1,0},{2,3},{3,2},{4,5},{5,4},{6,7},{7,6},{8,9},{9,8},{10,11... | collective-permute-start | bytes 688136 | tf_op jit(solution)/shard_map/ppermute | solution.py:58
  114.0 7.4 %collective-permute-start.3 = (bf16[8,3584]{1,0:T(8,128)(2,1)S(1)}, bf16[8,3584]{1,0:T(8,128)(2,1)S(1)}, u32[]{:S(2)}, u32[]{:S(2)}) collective-permute-start(bf16[8,3584]{1,0:T(8,128)(2,1)S(1)} %get-tuple-element.8), channel_id=1, source_target_pairs={{0,8},{1,9},{2,10},{3,11},{4,12},{5,13},{6,14},{7,15},{8,16},{9,17... | collective-permute-start | bytes 172040 | tf_op jit(solution)/shard_map/ppermute | solution.py:58
  115.3 7.4 %collective-permute-start.4 = (bf16[8,3584]{1,0:T(8,128)(2,1)S(1)}, bf16[8,3584]{1,0:T(8,128)(2,1)S(1)}, u32[]{:S(2)}, u32[]{:S(2)}) collective-permute-start(bf16[8,3584]{1,0:T(8,128)(2,1)S(1)} %get-tuple-element.10), channel_id=1, source_target_pairs={{0,16},{1,17},{2,18},{3,19},{4,20},{5,21},{6,22},{7,23},{8,24},{9,... | collective-permute-start | bytes 172040 | tf_op jit(solution)/shard_map/ppermute | solution.py:58
  116.8 5.9 %collective-permute-start.5 = (bf16[8,3584]{1,0:T(8,128)(2,1)S(1)}, bf16[8,3584]{1,0:T(8,128)(2,1)S(1)}, u32[]{:S(2)}, u32[]{:S(2)}) collective-permute-start(bf16[8,3584]{1,0:T(8,128)(2,1)S(1)} %get-tuple-element.9), channel_id=1, source_target_pairs={{0,24},{1,25},{2,26},{3,27},{4,28},{5,29},{6,30},{7,31},{8,0},{9,1... | collective-permute-start | bytes 172040 | tf_op jit(solution)/shard_map/ppermute | solution.py:58
  118.4 7.2 %collective-permute-start.10 = (bf16[8,3584]{1,0:T(8,128)(2,1)S(1)}, bf16[8,3584]{1,0:T(8,128)(2,1)S(1)}, u32[]{:S(2)}, u32[]{:S(2)}) collective-permute-start(bf16[8,3584]{1,0:T(8,128)(2,1)S(1)} %get-tuple-element.13), channel_id=1, source_target_pairs={{0,16},{1,17},{2,18},{3,19},{4,20},{5,21},{6,22},{7,23},{8,24},{9,... | collective-permute-start | bytes 172040 | tf_op jit(solution)/shard_map/ppermute | solution.py:58
  120.1 5.5 %collective-permute-start.11 = (bf16[8,3584]{1,0:T(8,128)(2,1)S(1)}, bf16[8,3584]{1,0:T(8,128)(2,1)S(1)}, u32[]{:S(2)}, u32[]{:S(2)}) collective-permute-start(bf16[8,3584]{1,0:T(8,128)(2,1)S(1)} %get-tuple-element.12), channel_id=1, source_target_pairs={{0,24},{1,25},{2,26},{3,27},{4,28},{5,29},{6,30},{7,31},{8,0},{9,1... | collective-permute-start | bytes 172040 | tf_op jit(solution)/shard_map/ppermute | solution.py:58
  121.4 6.0 %collective-permute-start.9 = (bf16[8,3584]{1,0:T(8,128)(2,1)S(1)}, bf16[8,3584]{1,0:T(8,128)(2,1)S(1)}, u32[]{:S(2)}, u32[]{:S(2)}) collective-permute-start(bf16[8,3584]{1,0:T(8,128)(2,1)S(1)} %get-tuple-element.11), channel_id=1, source_target_pairs={{0,8},{1,9},{2,10},{3,11},{4,12},{5,13},{6,14},{7,15},{8,16},{9,17... | collective-permute-start | bytes 172040 | tf_op jit(solution)/shard_map/ppermute | solution.py:58
Sparse Core Ops, SparseCore 0:
  11.5 63.4 all-gather.1

commit v2 on v1

--- a/solution.py
+++ b/solution.py
@@ -41,8 +41,6 @@
     def __init__(self):
         nodes, local = lax.axis_size("node"), lax.axis_size("local")
         self.sizes = (nodes // 4, 2, 2, local)
-        node = lax.axis_index("node")
-        self.place = (node // 4, node // 2 % 2, node % 2, lax.axis_index("local"))
 
     def shift(self, value, digit, step):
         pairs = []
@@ -57,12 +55,18 @@
             )
         return lax.ppermute(value, whole, pairs)
 
+    def gather(self, value, digit, dim):
+        blocks = [value]
+        for step in range(1, self.sizes[digit]):
+            blocks.append(self.shift(value, digit, step))
+        return jnp.stack(blocks, axis=dim)
+
     def scatter_sum(self, value, digit, dim):
-        size, here = self.sizes[digit], self.place[digit]
-        total = lax.dynamic_index_in_dim(value, here, dim, keepdims=False).astype(jnp.float32)
+        size = self.sizes[digit]
+        total = lax.index_in_dim(value, 0, dim, keepdims=False).astype(jnp.float32)
         for step in range(1, size):
-            part = lax.dynamic_index_in_dim(value, (here + step) % size, dim, keepdims=False)
-            total = total + self.shift(part, digit, step).astype(jnp.float32)
+            part = lax.index_in_dim(value, step, dim, keepdims=False)
+            total = total + self.shift(part, digit, size - step).astype(jnp.float32)
         return total.astype(value.dtype)
 
 
@@ -85,32 +89,44 @@
     grid = Grid()
     experts = lax.axis_size("node")
     width = moe_rows.shape[1]
-    outgoing = jnp.concatenate(
-        [moe_rows, share_columns(route_ids, route_gates, experts)], axis=1
-    )
-    gathered = lax.all_gather(outgoing, whole, axis=0, tiled=True)
+    half = width // 2
+    shares = share_columns(route_ids, route_gates, experts)
+    outgoing = jnp.concatenate([moe_rows, shares], axis=1)
+    column = grid.gather(outgoing, HIGH, 0)
+    first = grid.gather(column[..., :half], LOCAL, 0)
+    second = grid.gather(column[..., half:], MIDDLE, 0)
+    first = grid.gather(first, MIDDLE, 0)
+    second = grid.gather(second, LOCAL, 1)
+    first = grid.gather(first, CORE, 0).reshape(-1, half)
+    second = grid.gather(second, CORE, 0).reshape(first.shape[0], -1)
     attn_latent = attention(query_latent, query_rope, cache_latent, cache_rope, cache_lengths)
-    rows = gathered[:, :width]
-    table = gathered[:, width : width + 2 * experts].astype(jnp.float32)
+    table = second[:, half : half + 2 * experts].astype(jnp.float32)
+    second = second[:, :half]
     table = table[:, :experts] + table[:, experts:]
     mine = jnp.arange(experts, dtype=jnp.int32) == lax.axis_index("node")
     share = jnp.sum(jnp.where(mine[None, :], table, 0.0), axis=1, keepdims=True)
-    gate_act = jnp.dot(rows, w_gate[0], preferred_element_type=jnp.float32)
-    up_act = jnp.dot(rows, w_up[0], preferred_element_type=jnp.float32)
-    hidden = (jax.nn.silu(gate_act) * up_act).astype(jnp.bfloat16)
+
+    def project(weight):
+        lower = jnp.dot(first, weight[:half], preferred_element_type=jnp.float32)
+        upper = jnp.dot(second, weight[half:], preferred_element_type=jnp.float32)
+        return lower + upper
+
+    hidden = (jax.nn.silu(project(w_gate[0])) * project(w_up[0])).astype(jnp.bfloat16)
     pieces = []
-    half = width // 2
     for piece in range(2):
         columns = w_down[0][:, piece * half : (piece + 1) * half]
         product = share * jnp.dot(hidden, columns, preferred_element_type=jnp.float32)
-        product = product.astype(jnp.bfloat16).reshape(grid.sizes + (-1, half))
-        product = grid.scatter_sum(product, CORE, 2)
+        product = product.astype(jnp.bfloat16)
+        product = product.reshape(
+            grid.sizes[CORE], grid.sizes[MIDDLE], grid.sizes[LOCAL], grid.sizes[HIGH], -1, half
+        )
+        product = grid.scatter_sum(product, CORE, 0)
         if piece == 0:
-            product = grid.scatter_sum(product, LOCAL, 2)
-            product = grid.scatter_sum(product, MIDDLE, 1)
+            product = grid.scatter_sum(product, MIDDLE, 0)
+            product = grid.scatter_sum(product, LOCAL, 0)
         else:
-            product = grid.scatter_sum(product, MIDDLE, 1)
             product = grid.scatter_sum(product, LOCAL, 1)
+            product = grid.scatter_sum(product, MIDDLE, 0)
         pieces.append(grid.scatter_sum(product, HIGH, 0))
     moe_out = jnp.concatenate(pieces, axis=1)
     return (moe_out, attn_latent)

time: 135 us -> 99.7 us (0.74)
  waiting for transfers between devices: 84 us -> 34.3 us
  starting transfers between devices: 12.9 us -> 29.9 us
  between operations: 14.4 us -> 0.98 us
  other arithmetic: 6.82 us -> 13.7 us
  matrix products: 12.4 us -> 16.4 us
    all_gather x1 -> x0, waiting for transfers between devices: 63.6 us -> none  [body(): gathered = lax.all_gather(outgoing, whole, axis=0, tiled=True)]
    ppermute x12 -> x21, starting transfers between devices: 12.9 us -> 29.9 us  [shift(): return lax.ppermute(value, whole, pairs)]
    ppermute x12 -> x21, waiting for transfers between devices: 20.4 us -> 34.3 us  [shift(): return lax.ppermute(value, whole, pairs)]
    another operation x0 -> x8, other arithmetic: none -> 8.68 us  [gather(): return jnp.stack(blocks, axis=dim)]
    unnamed x20, local copies, waits for them, and re-layouts: 0.22 us -> 2.46 us
    dynamic_slice x3 -> x0, local copies, waits for them, and re-layouts: 2.22 us -> none  [the longest x1 1.17 us: scatter_sum(): lax.dynamic_index_in_dim(value, here, dim, keepdims=False)]
    dot_general x1, matrix products: 0.16 us -> 1.8 us  [attention(): jnp.einsum('rhp,rpj->rhj', query_rope, cache_rope, preferred_element_type...]
    convert_element_type x8, other arithmetic: 2.28 us -> 0.81 us  [scatter_sum(): return total.astype(value.dtype)]
  transfers between devices with their start and end apart: 13 -> 21, of which waited for: 8 -> 9; matrix products, arithmetic and copies ran while one was open for 3% -> 15% of each run, Pallas kernels for 0% -> 0%
where the time goes in v2:
time: 99.7 us; the launch traced here: 99.2 us
  waiting for transfers between devices  34.3 us (34%)
  starting transfers between devices  29.9 us (30%)
  matrix products  16.4 us (16%)
  other arithmetic  13.7 us (14%)
  local copies, waits for them, and re-layouts  3.91 us (4%)
    ppermute x21, waiting for transfers between devices, shift(): return lax.ppermute(value, whole, pairs)  34.3 us
    ppermute x21, starting transfers between devices, shift(): return lax.ppermute(value, whole, pairs)  29.9 us
    another operation x8, other arithmetic, gather(): return jnp.stack(blocks, axis=dim)  8.68 us
    dot_general x2, matrix products, project(): upper = jnp.dot(second, weight[half:], preferred_element_type=jnp.float32)  6.67 us
    unnamed x20, local copies, waits for them, and re-layouts  2.46 us
    dot_general x2, matrix products, body(): jnp.dot(hidden, columns, preferred_element_type=jnp.float32)  2.26 us
    dot_general x2, matrix products, project(): lower = jnp.dot(first, weight[:half], preferred_element_type=jnp.float32)  2.25 us
    dot_general x1, matrix products, attention(): jnp.einsum('rhj,rjc->rhc', weights, cache_latent, preferred_element_type=...  2.05 us
  transfers between devices with their start and end apart: 21, of which 9 were waited for; matrix products, arithmetic and copies ran while one was open for 15% of the time, Pallas kernels for 0%

profile of v2, /device:TPU:0, one launch (start us, length us, event | category | flops | bytes accessed | tf_op | source)
XLA Modules:
  0.0 99.2 jit_solution(2703582517273773114)
XLA Ops:
  4.1 3.0 %collective-permute-start = (bf16[8,7296]{1,0:T(8,128)(2,1)S(1)}, bf16[8,7296]{1,0:T(8,128)(2,1)S(1)}, u32[]{:S(2)}, u32[]{:S(2)}) collective-permute-start(bf16[8,7296]{1,0:T(8,128)(2,1)S(1)} %concatenate.6), channel_id=1, source_target_pairs={{0,8},{1,9},{2,10},{3,11},{4,12},{5,13},{6,14},{7,15},{8,16},{9,17... | collective-permute-start | bytes 350216 | tf_op jit(solution)/shard_map/ppermute | solution.py:56
  7.1 2.6 %collective-permute-start.1 = (bf16[8,7296]{1,0:T(8,128)(2,1)S(1)}, bf16[8,7296]{1,0:T(8,128)(2,1)S(1)}, u32[]{:S(2)}, u32[]{:S(2)}) collective-permute-start(bf16[8,7296]{1,0:T(8,128)(2,1)S(1)} %concatenate.6), channel_id=1, source_target_pairs={{0,16},{1,17},{2,18},{3,19},{4,20},{5,21},{6,22},{7,23},{8,24},{9,... | collective-permute-start | bytes 350216 | tf_op jit(solution)/shard_map/ppermute | solution.py:56
  13.1 1.8 %fusion.29 = f32[2,64,512]{2,1,0:T(8,128)} fusion(f32[2,64,512]{2,1,0:T(8,128)S(1)} %fusion.54, bf16[2,64,64]{2,1,0:T(8,128)(2,1)} %param.18, bf16[2,64,512]{2,1,0:T(8,128)(2,1)} %param.20, pred[2,512]{1,0:T(4,128)(4,1)S(1)} %iota_compare_fusion.1), kind=kOutput, calls=%fused_computation.32 | convolution fusion | flops 8585216 | bytes 672768 | tf_op jit(solution)/shard_map/rhp,rpj->rhj/dot_general | solution.py:18
  14.9 2.5 %collective-permute-done.1 = bf16[8,7296]{1,0:T(8,128)(2,1)S(1)} collective-permute-done((bf16[8,7296]{1,0:T(8,128)(2,1)S(1)}, bf16[8,7296]{1,0:T(8,128)(2,1)S(1)}, u32[]{:S(2)}, u32[]{:S(2)}) %collective-permute-start.1) | collective-permute-done | bytes 116768 | tf_op jit(solution)/shard_map/ppermute | solution.py:56
  17.5 1.6 %collective-permute-start.6 = (bf16[4,8,3584]{2,1,0:T(8,128)(2,1)S(1)}, bf16[4,8,3584]{2,1,0:T(8,128)(2,1)S(1)}, u32[]{:S(2)}, u32[]{:S(2)}) collective-permute-start(bf16[4,8,3584]{2,1,0:T(8,128)(2,1)S(1)} %pad_maximum_fusion.7), channel_id=1, source_target_pairs={{0,1},{1,0},{2,3},{3,2},{4,5},{5,4},{6,7},{7,6},{8,9},{9,8},{10,11... | collective-permute-start | bytes 688136 | tf_op jit(solution)/shard_map/ppermute | solution.py:56
  19.2 1.6 %collective-permute-start.3 = (bf16[4,8,3712]{2,1,0:T(8,128)(2,1)S(1)}, bf16[4,8,3712]{2,1,0:T(8,128)(2,1)S(1)}, u32[]{:S(2)}, u32[]{:S(2)}) collective-permute-start(bf16[4,8,3712]{2,1,0:T(8,128)(2,1)S(1)} %get-tuple-element.15), channel_id=1, source_target_pairs={{0,4},{1,5},{2,6},{3,7},{4,0},{5,1},{6,2},{7,3},{8,12},{9,13},{10,... | collective-permute-start | bytes 712712 | tf_op jit(solution)/shard_map/ppermute | solution.py:56
  20.8 4.2 %collective-permute-done.6 = bf16[4,8,3584]{2,1,0:T(8,128)(2,1)S(1)} collective-permute-done((bf16[4,8,3584]{2,1,0:T(8,128)(2,1)S(1)}, bf16[4,8,3584]{2,1,0:T(8,128)(2,1)S(1)}, u32[]{:S(2)}, u32[]{:S(2)}) %collective-permute-start.6) | collective-permute-done | bytes 229408 | tf_op jit(solution)/shard_map/ppermute | solution.py:56
  29.8 7.8 %collective-permute-done.7 = bf16[2,4,8,3584]{3,2,1,0:T(8,128)(2,1)S(1)} collective-permute-done((bf16[2,4,8,3584]{3,2,1,0:T(8,128)(2,1)}, bf16[2,4,8,3584]{3,2,1,0:T(8,128)(2,1)S(1)}, u32[]{:S(2)}, u32[]{:S(2)}) %collective-permute-start.7) | collective-permute-done | bytes 458784 | tf_op jit(solution)/shard_map/ppermute | solution.py:56
  38.4 2.1 %fusion.49 = (bf16[1,2,2,4,8,3584]{5,4,3,2,1,0:T(8,128)(2,1)S(1)}, bf16[2,2,4,8,3584]{4,3,2,1,0:T(8,128)(2,1)}) fusion(bf16[1,2,4,8,3584]{4,3,2,1,0:T(8,128)(2,1)} %bitcast.134, bf16[1,2,4,8,3584]{4,3,2,1,0:T(8,128)(2,1)S(1)} %get-tuple-element.16), kind=kLoop, calls=%fused_computation.93 | loop fusion | flops 458752 | bytes 2752512 | tf_op jit(solution)/shard_map/stack | solution.py:62
  41.2 2.1 %fusion.50 = (bf16[1,2,2,4,8,3712]{5,4,3,2,1,0:T(8,128)(2,1)S(1)}, bf16[2,2,4,8,3712]{4,3,2,1,0:T(8,128)(2,1)}) fusion(bf16[2,1,4,8,3712]{4,3,2,1,0:T(8,128)(2,1)} %bitcast.133, bf16[2,1,4,8,3712]{4,3,2,1,0:T(8,128)(2,1)S(1)} %get-tuple-element.12), kind=kLoop, calls=%fused_computation.94 | loop fusion | flops 475136 | bytes 2850816 | tf_op jit(solution)/shard_map/stack | solution.py:62
  44.0 2.0 %convolution_convert_fusion = bf16[2,64,512]{2,1,0:T(8,128)(2,1)} fusion(bf16[2,512,512]{2,1,0:T(8,128)(2,1)S(1)} %copy-done, f32[2,64]{1,0:T(2,128)S(1)} %fusion.53, f32[2,64,512]{2,1,0:T(8,128)} %fusion.29, pred[2,512]{1,0:T(4,128)(4,1)S(1)} %iota_compare_fusion.1), kind=kOutput, calls=%fused_computation.35 | convolution fusion | flops 67437184 | bytes 1443328 | tf_op jit(solution)/shard_map/rhj,rjc->rhc/dot_general | solution.py:25
  48.9 3.3 %fusion.9 = f32[256,512]{1,0:T(8,128)S(1)} fusion(bf16[1,7168,512]{2,1,0:T(8,128)(2,1)} %param.14, bf16[256,3712]{1,0:T(8,128)(2,1)S(1)} %bitcast.116), kind=kOutput, calls=%fused_computation.11 | convolution fusion | flops 939524096 | bytes 6029312 | tf_op jit(solution)/shard_map/dot_general | solution.py:111
  52.2 3.4 %fusion.5 = f32[256,512]{1,0:T(8,128)S(1)} fusion(bf16[1,7168,512]{2,1,0:T(8,128)(2,1)} %param.15, bf16[256,3712]{1,0:T(8,128)(2,1)S(1)} %bitcast.117), kind=kOutput, calls=%fused_computation.7 | convolution fusion | flops 939524096 | bytes 6029312 | tf_op jit(solution)/shard_map/dot_general | solution.py:111
  62.2 1.7 %collective-permute-done.9 = bf16[2,2,4,8,3584]{4,3,2,1,0:T(8,128)(2,1)S(1)} collective-permute-done((bf16[2,2,4,8,3584]{4,3,2,1,0:T(8,128)(2,1)S(1)}, bf16[2,2,4,8,3584]{4,3,2,1,0:T(8,128)(2,1)S(1)}, u32[]{:S(2)}, u32[]{:S(2)}) %collective-permute-start.9) | collective-permute-done | bytes 917536 | tf_op jit(solution)/shard_map/ppermute | solution.py:56
  64.2 1.6 %collective-permute-start.10 = (bf16[2,4,8,3584]{3,2,1,0:T(8,128)(2,1)S(1)}, bf16[2,4,8,3584]{3,2,1,0:T(8,128)(2,1)S(1)}, u32[]{:S(2)}, u32[]{:S(2)}) collective-permute-start(bf16[2,4,8,3584]{3,2,1,0:T(8,128)(2,1)S(1)} %slice_bitcast_fusion.2), channel_id=1, source_target_pairs={{0,4},{1,5},{2,6},{3,7},{4,0},{5,1},{6,2},{7,3},{8,12},{9,13},{10,... | collective-permute-start | bytes 1376264 | tf_op jit(solution)/shard_map/ppermute | solution.py:56
  67.6 9.2 %collective-permute-done.10 = bf16[2,4,8,3584]{3,2,1,0:T(8,128)(2,1)S(1)} collective-permute-done((bf16[2,4,8,3584]{3,2,1,0:T(8,128)(2,1)S(1)}, bf16[2,4,8,3584]{3,2,1,0:T(8,128)(2,1)S(1)}, u32[]{:S(2)}, u32[]{:S(2)}) %collective-permute-start.10) | collective-permute-done | bytes 458784 | tf_op jit(solution)/shard_map/ppermute | solution.py:56
  76.9 1.6 %collective-permute-start.11 = (bf16[4,8,3584]{2,1,0:T(8,128)(2,1)S(1)}, bf16[4,8,3584]{2,1,0:T(8,128)(2,1)S(1)}, u32[]{:S(2)}, u32[]{:S(2)}) collective-permute-start(bf16[4,8,3584]{2,1,0:T(8,128)(2,1)S(1)} %slice_bitcast_fusion.6), channel_id=1, source_target_pairs={{0,1},{1,0},{2,3},{3,2},{4,5},{5,4},{6,7},{7,6},{8,9},{9,8},{10,11... | collective-permute-start | bytes 688136 | tf_op jit(solution)/shard_map/ppermute | solution.py:56
  78.7 1.6 %collective-permute-start.17 = (bf16[4,8,3584]{2,1,0:T(8,128)(2,1)S(1)}, bf16[4,8,3584]{2,1,0:T(8,128)(2,1)S(1)}, u32[]{:S(2)}, u32[]{:S(2)}) collective-permute-start(bf16[4,8,3584]{2,1,0:T(8,128)(2,1)S(1)} %slice_bitcast_fusion.4), channel_id=1, source_target_pairs={{0,4},{1,5},{2,6},{3,7},{4,0},{5,1},{6,2},{7,3},{8,12},{9,13},{10,... | collective-permute-start | bytes 688136 | tf_op jit(solution)/shard_map/ppermute | solution.py:56
  80.3 3.6 %collective-permute-done.11 = bf16[4,8,3584]{2,1,0:T(8,128)(2,1)S(1)} collective-permute-done((bf16[4,8,3584]{2,1,0:T(8,128)(2,1)S(1)}, bf16[4,8,3584]{2,1,0:T(8,128)(2,1)S(1)}, u32[]{:S(2)}, u32[]{:S(2)}) %collective-permute-start.11) | collective-permute-done | bytes 229408 | tf_op jit(solution)/shard_map/ppermute | solution.py:56
  83.9 2.1 %collective-permute-start.12 = (bf16[8,3584]{1,0:T(8,128)(2,1)S(1)}, bf16[8,3584]{1,0:T(8,128)(2,1)S(1)}, u32[]{:S(2)}, u32[]{:S(2)}) collective-permute-start(bf16[8,3584]{1,0:T(8,128)(2,1)S(1)} %get-tuple-element.18), channel_id=1, source_target_pairs={{0,24},{1,25},{2,26},{3,27},{4,28},{5,29},{6,30},{7,31},{8,0},{9,1... | collective-permute-start | bytes 172040 | tf_op jit(solution)/shard_map/ppermute | solution.py:56
  86.0 2.6 %collective-permute-start.13 = (bf16[8,3584]{1,0:T(8,128)(2,1)S(1)}, bf16[8,3584]{1,0:T(8,128)(2,1)S(1)}, u32[]{:S(2)}, u32[]{:S(2)}) collective-permute-start(bf16[8,3584]{1,0:T(8,128)(2,1)S(1)} %get-tuple-element.20), channel_id=1, source_target_pairs={{0,16},{1,17},{2,18},{3,19},{4,20},{5,21},{6,22},{7,23},{8,24},{9,... | collective-permute-start | bytes 172040 | tf_op jit(solution)/shard_map/ppermute | solution.py:56
  88.7 3.9 %collective-permute-start.18 = (bf16[8,3584]{1,0:T(8,128)(2,1)S(1)}, bf16[8,3584]{1,0:T(8,128)(2,1)S(1)}, u32[]{:S(2)}, u32[]{:S(2)}) collective-permute-start(bf16[8,3584]{1,0:T(8,128)(2,1)S(1)} %get-tuple-element.21), channel_id=1, source_target_pairs={{0,24},{1,25},{2,26},{3,27},{4,28},{5,29},{6,30},{7,31},{8,0},{9,1... | collective-permute-start | bytes 172040 | tf_op jit(solution)/shard_map/ppermute | solution.py:56
  93.2 1.8 %collective-permute-done.14 = bf16[8,3584]{1,0:T(8,128)(2,1)S(1)} collective-permute-done((bf16[8,3584]{1,0:T(8,128)(2,1)S(1)}, bf16[8,3584]{1,0:T(8,128)(2,1)S(1)}, u32[]{:S(2)}, u32[]{:S(2)}) %collective-permute-start.14) | collective-permute-done | bytes 57376 | tf_op jit(solution)/shard_map/ppermute | solution.py:56
  95.0 2.6 %collective-permute-done.19 = bf16[8,3584]{1,0:T(8,128)(2,1)S(1)} collective-permute-done((bf16[8,3584]{1,0:T(8,128)(2,1)S(1)}, bf16[8,3584]{1,0:T(8,128)(2,1)S(1)}, u32[]{:S(2)}, u32[]{:S(2)}) %collective-permute-start.19) | collective-permute-done | bytes 57376 | tf_op jit(solution)/shard_map/ppermute | solution.py:56
  (89 shorter events, 28.0 us)
Async XLA Ops:
  0.6 11.2 %copy-start = (bf16[2,512,512]{2,1,0:T(8,128)(2,1)S(1)}, bf16[2,512,512]{2,1,0:T(8,128)(2,1)}, u32[]{:S(2)}) copy-start(bf16[2,512,512]{2,1,0:T(8,128)(2,1)} %param.19) | copy-start | bytes 3145732
  4.1 10.8 %collective-permute-start = (bf16[8,7296]{1,0:T(8,128)(2,1)S(1)}, bf16[8,7296]{1,0:T(8,128)(2,1)S(1)}, u32[]{:S(2)}, u32[]{:S(2)}) collective-permute-start(bf16[8,7296]{1,0:T(8,128)(2,1)S(1)} %concatenate.6), channel_id=1, source_target_pairs={{0,8},{1,9},{2,10},{3,11},{4,12},{5,13},{6,14},{7,15},{8,16},{9,17... | collective-permute-start | bytes 350216 | tf_op jit(solution)/shard_map/ppermute | solution.py:56
  7.1 10.3 %collective-permute-start.1 = (bf16[8,7296]{1,0:T(8,128)(2,1)S(1)}, bf16[8,7296]{1,0:T(8,128)(2,1)S(1)}, u32[]{:S(2)}, u32[]{:S(2)}) collective-permute-start(bf16[8,7296]{1,0:T(8,128)(2,1)S(1)} %concatenate.6), channel_id=1, source_target_pairs={{0,16},{1,17},{2,18},{3,19},{4,20},{5,21},{6,22},{7,23},{8,24},{9,... | collective-permute-start | bytes 350216 | tf_op jit(solution)/shard_map/ppermute | solution.py:56
  9.7 7.7 %collective-permute-start.2 = (bf16[8,7296]{1,0:T(8,128)(2,1)S(1)}, bf16[8,7296]{1,0:T(8,128)(2,1)S(1)}, u32[]{:S(2)}, u32[]{:S(2)}) collective-permute-start(bf16[8,7296]{1,0:T(8,128)(2,1)S(1)} %concatenate.6), channel_id=1, source_target_pairs={{0,24},{1,25},{2,26},{3,27},{4,28},{5,29},{6,30},{7,31},{8,0},{9,1... | collective-permute-start | bytes 350216 | tf_op jit(solution)/shard_map/ppermute | solution.py:56
  17.5 7.5 %collective-permute-start.6 = (bf16[4,8,3584]{2,1,0:T(8,128)(2,1)S(1)}, bf16[4,8,3584]{2,1,0:T(8,128)(2,1)S(1)}, u32[]{:S(2)}, u32[]{:S(2)}) collective-permute-start(bf16[4,8,3584]{2,1,0:T(8,128)(2,1)S(1)} %pad_maximum_fusion.7), channel_id=1, source_target_pairs={{0,1},{1,0},{2,3},{3,2},{4,5},{5,4},{6,7},{7,6},{8,9},{9,8},{10,11... | collective-permute-start | bytes 688136 | tf_op jit(solution)/shard_map/ppermute | solution.py:56
  19.2 8.3 %collective-permute-start.3 = (bf16[4,8,3712]{2,1,0:T(8,128)(2,1)S(1)}, bf16[4,8,3712]{2,1,0:T(8,128)(2,1)S(1)}, u32[]{:S(2)}, u32[]{:S(2)}) collective-permute-start(bf16[4,8,3712]{2,1,0:T(8,128)(2,1)S(1)} %get-tuple-element.15), channel_id=1, source_target_pairs={{0,4},{1,5},{2,6},{3,7},{4,0},{5,1},{6,2},{7,3},{8,12},{9,13},{10,... | collective-permute-start | bytes 712712 | tf_op jit(solution)/shard_map/ppermute | solution.py:56
  25.9 11.7 %collective-permute-start.7 = (bf16[2,4,8,3584]{3,2,1,0:T(8,128)(2,1)}, bf16[2,4,8,3584]{3,2,1,0:T(8,128)(2,1)S(1)}, u32[]{:S(2)}, u32[]{:S(2)}) collective-permute-start(bf16[2,4,8,3584]{3,2,1,0:T(8,128)(2,1)} %get-tuple-element.17), channel_id=1, source_target_pairs={{0,4},{1,5},{2,6},{3,7},{4,0},{5,1},{6,2},{7,3},{8,12},{9,13},{10,... | collective-permute-start | bytes 1376264 | tf_op jit(solution)/shard_map/ppermute | solution.py:56
  28.3 12.1 %collective-permute-start.4 = (bf16[2,4,8,3712]{3,2,1,0:T(8,128)(2,1)}, bf16[2,4,8,3712]{3,2,1,0:T(8,128)(2,1)S(1)}, u32[]{:S(2)}, u32[]{:S(2)}) collective-permute-start(bf16[2,4,8,3712]{3,2,1,0:T(8,128)(2,1)} %get-tuple-element.13), channel_id=1, source_target_pairs={{0,1},{1,0},{2,3},{3,2},{4,5},{5,4},{6,7},{7,6},{8,9},{9,8},{10,11... | collective-permute-start | bytes 1425416 | tf_op jit(solution)/shard_map/ppermute | solution.py:56
  40.4 5.7 %collective-permute-start.8 = (bf16[2,2,4,8,3584]{4,3,2,1,0:T(8,128)(2,1)}, bf16[2,2,4,8,3584]{4,3,2,1,0:T(8,128)(2,1)}, u32[]{:S(2)}, u32[]{:S(2)}) collective-permute-start(bf16[2,2,4,8,3584]{4,3,2,1,0:T(8,128)(2,1)} %get-tuple-element.11), channel_id=1, source_target_pairs={{0,2},{1,3},{2,0},{3,1},{4,6},{5,7},{6,4},{7,5},{8,10},{9,11},{10,... | collective-permute-start | bytes 2752520 | tf_op jit(solution)/shard_map/ppermute | solution.py:56
  43.3 4.1 %collective-permute-start.5 = (bf16[2,2,4,8,3712]{4,3,2,1,0:T(8,128)(2,1)}, bf16[2,2,4,8,3712]{4,3,2,1,0:T(8,128)(2,1)}, u32[]{:S(2)}, u32[]{:S(2)}) collective-permute-start(bf16[2,2,4,8,3712]{4,3,2,1,0:T(8,128)(2,1)} %get-tuple-element.9), channel_id=1, source_target_pairs={{0,2},{1,3},{2,0},{3,1},{4,6},{5,7},{6,4},{7,5},{8,10},{9,11},{10,... | collective-permute-start | bytes 2850824 | tf_op jit(solution)/shard_map/ppermute | solution.py:56
  48.9 6.7 %slice-start = ((s8[7340032]{0:T(1024)(128)(4,1)}), s8[4194304]{0:T(1024)(128)(4,1)S(1)}, s32[]{:S(2)}) async-start(s8[7340032]{0:T(1024)(128)(4,1)} %bitcast.137), calls=%async_computation | async-start | bytes 8388608
  48.9 7.9 %slice-start.2 = ((s8[7340032]{0:T(1024)(128)(4,1)}), s8[4194304]{0:T(1024)(128)(4,1)S(1)}, s32[]{:S(2)}) async-start(s8[7340032]{0:T(1024)(128)(4,1)} %bitcast.139), calls=%async_computation.2 | async-start | bytes 8388608
  61.4 2.5 %collective-permute-start.9 = (bf16[2,2,4,8,3584]{4,3,2,1,0:T(8,128)(2,1)S(1)}, bf16[2,2,4,8,3584]{4,3,2,1,0:T(8,128)(2,1)S(1)}, u32[]{:S(2)}, u32[]{:S(2)}) collective-permute-start(bf16[2,2,4,8,3584]{4,3,2,1,0:T(8,128)(2,1)S(1)} %bitcast.132), channel_id=1, source_target_pairs={{0,2},{1,3},{2,0},{3,1},{4,6},{5,7},{6,4},{7,5},{8,10},{9,11},{10,... | collective-permute-start | bytes 2752520 | tf_op jit(solution)/shard_map/ppermute | solution.py:56
  61.6 4.1 %collective-permute-start.15 = (bf16[2,2,4,8,3584]{4,3,2,0,1:T(8,128)(2,1)S(1)}, bf16[2,2,4,8,3584]{4,3,2,0,1:T(8,128)(2,1)S(1)}, u32[]{:S(2)}, u32[]{:S(2)}) collective-permute-start(bf16[2,2,4,8,3584]{4,3,2,0,1:T(8,128)(2,1)S(1)} %copy.19), channel_id=1, source_target_pairs={{0,2},{1,3},{2,0},{3,1},{4,6},{5,7},{6,4},{7,5},{8,10},{9,11},{10,... | collective-permute-start | bytes 2752520 | tf_op jit(solution)/shard_map/ppermute | solution.py:56
  64.2 12.6 %collective-permute-start.10 = (bf16[2,4,8,3584]{3,2,1,0:T(8,128)(2,1)S(1)}, bf16[2,4,8,3584]{3,2,1,0:T(8,128)(2,1)S(1)}, u32[]{:S(2)}, u32[]{:S(2)}) collective-permute-start(bf16[2,4,8,3584]{3,2,1,0:T(8,128)(2,1)S(1)} %slice_bitcast_fusion.2), channel_id=1, source_target_pairs={{0,4},{1,5},{2,6},{3,7},{4,0},{5,1},{6,2},{7,3},{8,12},{9,13},{10,... | collective-permute-start | bytes 1376264 | tf_op jit(solution)/shard_map/ppermute | solution.py:56
  66.1 12.5 %collective-permute-start.16 = (bf16[2,4,8,3584]{3,2,1,0:T(8,128)(2,1)S(1)}, bf16[2,4,8,3584]{3,2,1,0:T(8,128)(2,1)S(1)}, u32[]{:S(2)}, u32[]{:S(2)}) collective-permute-start(bf16[2,4,8,3584]{3,2,1,0:T(8,128)(2,1)S(1)} %slice_bitcast_fusion), channel_id=1, source_target_pairs={{0,1},{1,0},{2,3},{3,2},{4,5},{5,4},{6,7},{7,6},{8,9},{9,8},{10,11... | collective-permute-start | bytes 1376264 | tf_op jit(solution)/shard_map/ppermute | solution.py:56
  76.9 6.9 %collective-permute-start.11 = (bf16[4,8,3584]{2,1,0:T(8,128)(2,1)S(1)}, bf16[4,8,3584]{2,1,0:T(8,128)(2,1)S(1)}, u32[]{:S(2)}, u32[]{:S(2)}) collective-permute-start(bf16[4,8,3584]{2,1,0:T(8,128)(2,1)S(1)} %slice_bitcast_fusion.6), channel_id=1, source_target_pairs={{0,1},{1,0},{2,3},{3,2},{4,5},{5,4},{6,7},{7,6},{8,9},{9,8},{10,11... | collective-permute-start | bytes 688136 | tf_op jit(solution)/shard_map/ppermute | solution.py:56
  78.7 9.9 %collective-permute-start.17 = (bf16[4,8,3584]{2,1,0:T(8,128)(2,1)S(1)}, bf16[4,8,3584]{2,1,0:T(8,128)(2,1)S(1)}, u32[]{:S(2)}, u32[]{:S(2)}) collective-permute-start(bf16[4,8,3584]{2,1,0:T(8,128)(2,1)S(1)} %slice_bitcast_fusion.4), channel_id=1, source_target_pairs={{0,4},{1,5},{2,6},{3,7},{4,0},{5,1},{6,2},{7,3},{8,12},{9,13},{10,... | collective-permute-start | bytes 688136 | tf_op jit(solution)/shard_map/ppermute | solution.py:56
  83.9 8.7 %collective-permute-start.12 = (bf16[8,3584]{1,0:T(8,128)(2,1)S(1)}, bf16[8,3584]{1,0:T(8,128)(2,1)S(1)}, u32[]{:S(2)}, u32[]{:S(2)}) collective-permute-start(bf16[8,3584]{1,0:T(8,128)(2,1)S(1)} %get-tuple-element.18), channel_id=1, source_target_pairs={{0,24},{1,25},{2,26},{3,27},{4,28},{5,29},{6,30},{7,31},{8,0},{9,1... | collective-permute-start | bytes 172040 | tf_op jit(solution)/shard_map/ppermute | solution.py:56
  86.0 7.2 %collective-permute-start.13 = (bf16[8,3584]{1,0:T(8,128)(2,1)S(1)}, bf16[8,3584]{1,0:T(8,128)(2,1)S(1)}, u32[]{:S(2)}, u32[]{:S(2)}) collective-permute-start(bf16[8,3584]{1,0:T(8,128)(2,1)S(1)} %get-tuple-element.20), channel_id=1, source_target_pairs={{0,16},{1,17},{2,18},{3,19},{4,20},{5,21},{6,22},{7,23},{8,24},{9,... | collective-permute-start | bytes 172040 | tf_op jit(solution)/shard_map/ppermute | solution.py:56
  88.6 6.4 %collective-permute-start.14 = (bf16[8,3584]{1,0:T(8,128)(2,1)S(1)}, bf16[8,3584]{1,0:T(8,128)(2,1)S(1)}, u32[]{:S(2)}, u32[]{:S(2)}) collective-permute-start(bf16[8,3584]{1,0:T(8,128)(2,1)S(1)} %get-tuple-element.19), channel_id=1, source_target_pairs={{0,8},{1,9},{2,10},{3,11},{4,12},{5,13},{6,14},{7,15},{8,16},{9,17... | collective-permute-start | bytes 172040 | tf_op jit(solution)/shard_map/ppermute | solution.py:56
  88.7 6.4 %collective-permute-start.18 = (bf16[8,3584]{1,0:T(8,128)(2,1)S(1)}, bf16[8,3584]{1,0:T(8,128)(2,1)S(1)}, u32[]{:S(2)}, u32[]{:S(2)}) collective-permute-start(bf16[8,3584]{1,0:T(8,128)(2,1)S(1)} %get-tuple-element.21), channel_id=1, source_target_pairs={{0,24},{1,25},{2,26},{3,27},{4,28},{5,29},{6,30},{7,31},{8,0},{9,1... | collective-permute-start | bytes 172040 | tf_op jit(solution)/shard_map/ppermute | solution.py:56
  92.5 5.1 %collective-permute-start.19 = (bf16[8,3584]{1,0:T(8,128)(2,1)S(1)}, bf16[8,3584]{1,0:T(8,128)(2,1)S(1)}, u32[]{:S(2)}, u32[]{:S(2)}) collective-permute-start(bf16[8,3584]{1,0:T(8,128)(2,1)S(1)} %get-tuple-element.23), channel_id=1, source_target_pairs={{0,16},{1,17},{2,18},{3,19},{4,20},{5,21},{6,22},{7,23},{8,24},{9,... | collective-permute-start | bytes 172040 | tf_op jit(solution)/shard_map/ppermute | solution.py:56
  92.6 6.0 %collective-permute-start.20 = (bf16[8,3584]{1,0:T(8,128)(2,1)S(1)}, bf16[8,3584]{1,0:T(8,128)(2,1)S(1)}, u32[]{:S(2)}, u32[]{:S(2)}) collective-permute-start(bf16[8,3584]{1,0:T(8,128)(2,1)S(1)} %get-tuple-element.22), channel_id=1, source_target_pairs={{0,8},{1,9},{2,10},{3,11},{4,12},{5,13},{6,14},{7,15},{8,16},{9,17... | collective-permute-start | bytes 172040 | tf_op jit(solution)/shard_map/ppermute | solution.py:56
  (7 other events, 17.7 us)

commit v3 on v1

v3 whole, which is shorter than its diff:
```python
import functools

import jax
import jax.numpy as jnp
import numpy as np
from jax import lax
from jax.experimental import pallas as pl
from jax.experimental.pallas import tpu as pltpu
from jax.sharding import Mesh
from jax.sharding import PartitionSpec as P

score_scale = 192.0 ** (-0.5)
everyone = ("high", "middle", "core", "local")
MEBI = 1024 * 1024


def attention(query_latent, query_rope, cache_latent, cache_rope, cache_lengths):
    slot_count = cache_latent.shape[1]
    scores = jnp.einsum(
        "rhc,rjc->rhj", query_latent, cache_latent, preferred_element_type=jnp.float32
    )
    scores = (
        scores
        + jnp.einsum("rhp,rpj->rhj", query_rope, cache_rope, preferred_element_type=jnp.float32)
    ) * score_scale
    in_range = jnp.arange(slot_count, dtype=jnp.int32)[None, None, :] < cache_lengths[:, None, None]
    scores = jnp.where(in_range, scores, -jnp.inf)
    row_peak = jnp.max(scores, axis=-1, keepdims=True)
    lifted = jnp.where(in_range, jnp.exp(scores - row_peak), 0.0)
    weights = (lifted / jnp.sum(lifted, axis=-1, keepdims=True)).astype(jnp.bfloat16)
    return jnp.einsum(
        "rhj,rjc->rhc", weights, cache_latent, preferred_element_type=jnp.float32
    ).astype(jnp.bfloat16)


class Grid:
    def __init__(self):
        self.sizes = tuple(lax.axis_size(name) for name in everyone)
        self.mixed = self.sizes[1] == self.sizes[3]

    def shift(self, value, pick, step):
        pairs = []
        for place in np.ndindex(*self.sizes):
            other = list(place)
            digit = pick(place[2])
            other[digit] = (other[digit] + step) % self.sizes[digit]
            pairs.append(
                (
                    int(np.ravel_multi_index(place, self.sizes)),
                    int(np.ravel_multi_index(other, self.sizes)),
                )
            )
        return lax.ppermute(value, everyone, pairs)

    def first(self, core):
        return 1 if self.mixed and core == 1 else 3

    def second(self, core):
        return 3 if self.mixed and core == 1 else 1

    def core(self, core):
        return 2

    def gather(self, line):
        near = [line]
        for step in range(1, self.sizes[self.first(0)]):
            near.append(self.shift(line, self.first, step))
        mine = list(near)
        for step in range(1, self.sizes[self.second(0)]):
            mine += [self.shift(block, self.second, step) for block in near]
        other = [self.shift(block, self.core, 1) for block in mine]
        return mine + other

    def scatter_sum(self, blocks):
        def add(parts):
            total = parts[0].astype(jnp.float32)
            for part in parts[1:]:
                total = total + part.astype(jnp.float32)
            return total.astype(parts[0].dtype)

        count = len(blocks) // 2
        mine = [
            add([blocks[i], self.shift(blocks[count + i], self.core, 1)])
            for i in reversed(range(count))
        ][::-1]
        extent = self.sizes[self.second(0)]
        wide = count // extent
        near = []
        for i in reversed(range(wide)):
            parts = [mine[i]]
            for step in range(1, extent):
                parts.append(self.shift(mine[step * wide + i], self.second, extent - step))
            near.append(add(parts))
        near = near[::-1]
        parts = [near[0]]
        for step in range(1, wide):
            parts.append(self.shift(near[step], self.first, wide - step))
        return add(parts)


def pack_kernel(experts, rows_ref, ids_ref, gates_ref, out_ref):
    copies, _, total = out_ref.shape
    width = rows_ref.shape[1]
    extra = total - width
    gates = gates_ref[...]
    shares = 2.5 * gates / jnp.sum(gates, axis=1, keepdims=True)
    ids = ids_ref[...]
    lane = lax.broadcasted_iota(jnp.int32, (ids.shape[0], extra), 1)
    expert = jnp.where(lane < experts, lane, lane - experts)
    table = jnp.zeros(lane.shape, jnp.float32)
    for k in range(ids.shape[1]):
        table += jnp.where(expert == ids[:, k : k + 1], shares[:, k : k + 1], 0.0)
    high = table.astype(jnp.bfloat16).astype(jnp.float32)
    table = jnp.where(lane < experts, high, jnp.where(lane < 2 * experts, table - high, 0.0))
    table = table.astype(jnp.bfloat16)
    for copy in range(copies):
        out_ref[copy, :, :width] = rows_ref[...]
        out_ref[copy, :, width:] = table


def pack(copies, experts, moe_rows, route_ids, route_gates):
    rows, width = moe_rows.shape
    total = width + pl.cdiv(2 * experts, 128) * 128
    return pl.pallas_call(
        functools.partial(pack_kernel, experts),
        out_shape=jax.ShapeDtypeStruct((copies, rows, total), jnp.bfloat16),
        name="pack",
    )(moe_rows, route_ids, route_gates)


def hidden_kernel(count, experts, node_ref, *refs):
    blocks, tails = refs[:count], refs[count : 2 * count]
    gate_ref, up_ref, hidden_ref, share_ref, gate_sum, up_sum = refs[2 * count :]
    step = pl.program_id(0)

    @pl.when(step == 0)
    def _():
        gate_sum[...] = jnp.zeros_like(gate_sum)
        up_sum[...] = jnp.zeros_like(up_sum)
        table = jnp.concatenate([tail[...] for tail in tails], axis=0).astype(jnp.float32)
        lane = lax.broadcasted_iota(jnp.int32, table.shape, 1)
        mine = (lane == node_ref[0]) | (lane == node_ref[0] + experts)
        share = jnp.sum(jnp.where(mine, table, 0.0), axis=1, keepdims=True)
        share_ref[...] = jnp.broadcast_to(share, share_ref.shape)

    rows = jnp.concatenate([block[...] for block in blocks], axis=0)
    gate_sum[...] += jnp.dot(rows, gate_ref[...], preferred_element_type=jnp.float32)
    up_sum[...] += jnp.dot(rows, up_ref[...], preferred_element_type=jnp.float32)

    @pl.when(step == pl.num_programs(0) - 1)
    def _():
        hidden_ref[...] = (jax.nn.silu(gate_sum[...]) * up_sum[...]).astype(jnp.bfloat16)


def hidden_of(blocks, w_gate, w_up, experts, node):
    width, units = w_gate.shape
    count, size = len(blocks), blocks[0].shape[0]
    tail = blocks[0].shape[1] - width
    rows = count * size
    tile = 1024
    return pl.pallas_call(
        functools.partial(hidden_kernel, count, experts),
        grid_spec=pltpu.PrefetchScalarGridSpec(
            num_scalar_prefetch=1,
            grid=(width // tile,),
            in_specs=[pl.BlockSpec((size, tile), lambda j, node: (0, j))] * count
            + [pl.BlockSpec((size, tail), lambda j, node: (0, width // tail))] * count
            + [pl.BlockSpec((tile, units), lambda j, node: (j, 0))] * 2,
            out_specs=[
                pl.BlockSpec((rows, units), lambda j, node: (0, 0)),
                pl.BlockSpec((rows, 128), lambda j, node: (0, 0)),
            ],
            scratch_shapes=[pltpu.VMEM((rows, units), jnp.float32)] * 2,
        ),
        out_shape=[
            jax.ShapeDtypeStruct((rows, units), jnp.bfloat16),
            jax.ShapeDtypeStruct((rows, 128), jnp.float32),
        ],
        cost_estimate=pl.CostEstimate(
            flops=4 * rows * width * units,
            bytes_accessed=4 * width * units + 2 * rows * width,
            transcendentals=rows * units,
        ),
        compiler_params=pltpu.CompilerParams(vmem_limit_bytes=24 * MEBI),
        name="gate_up",
    )(node, *blocks, *blocks, w_gate, w_up)


def down_kernel(hidden_ref, share_ref, down_ref, *outs):
    product = jnp.dot(hidden_ref[...], down_ref[...], preferred_element_type=jnp.float32)
    product = (product * share_ref[:, :1]).astype(jnp.bfloat16)
    size = outs[0].shape[0]
    for i, out in enumerate(outs):
        out[...] = product[i * size : (i + 1) * size]


def down_of(hidden, share, w_down, count, start, columns):
    rows, units = hidden.shape
    size = rows // count
    tile = 512
    offset = start // tile
    return pl.pallas_call(
        down_kernel,
        grid=(columns // tile,),
        in_specs=[
            pl.BlockSpec((rows, units), lambda j: (0, 0)),
            pl.BlockSpec((rows, 128), lambda j: (0, 0)),
            pl.BlockSpec((units, tile), lambda j: (0, j + offset)),
        ],
        out_specs=[pl.BlockSpec((size, tile), lambda j: (0, j))] * count,
        out_shape=[jax.ShapeDtypeStruct((size, columns), jnp.bfloat16)] * count,
        cost_estimate=pl.CostEstimate(
            flops=2 * rows * columns * units,
            bytes_accessed=2 * columns * (units + rows),
            transcendentals=0,
        ),
        compiler_params=pltpu.CompilerParams(vmem_limit_bytes=16 * MEBI),
        name="down",
    )(hidden, share, w_down)


def body(
    moe_rows,
    route_ids,
    route_gates,
    w_gate,
    w_up,
    w_down,
    query_latent,
    query_rope,
    cache_latent,
    cache_rope,
    cache_lengths,
):
    grid = Grid()
    high, middle, cores, _ = grid.sizes
    experts = high * middle * cores
    tokens, width = moe_rows.shape
    node = lax.axis_index(("high", "middle", "core")).astype(jnp.int32).reshape(1)
    outgoing = pack(high, experts, moe_rows, route_ids, route_gates)
    line = lax.all_to_all(outgoing, "high", split_axis=0, concat_axis=0, tiled=True)
    blocks = grid.gather(line.reshape(high * tokens, -1))
    attn_latent = attention(query_latent, query_rope, cache_latent, cache_rope, cache_lengths)
    hidden, share = hidden_of(blocks, w_gate[0], w_up[0], experts, node)
    pieces = []
    half = width // 2
    for piece in range(2):
        products = down_of(hidden, share, w_down[0], len(blocks), piece * half, half)
        total = grid.scatter_sum(products).reshape(high, tokens, half)
        parts = lax.all_to_all(total, "high", split_axis=0, concat_axis=0, tiled=True)
        pieces.append(jnp.sum(parts.astype(jnp.float32), axis=0).astype(jnp.bfloat16))
    return (jnp.concatenate(pieces, axis=1), attn_latent)


def solution(mesh):
    groups, nodes, local = mesh.devices.shape
    split = Mesh(mesh.devices.reshape(groups, nodes // 4, 2, 2, local), ("group",) + everyone)
    node = ("high", "middle", "core")
    whole = ("group",) + everyone
    rows = P(whole, None)
    blocks = P(whole, None, None)
    return jax.shard_map(
        body,
        mesh=split,
        in_specs=(
            rows,
            rows,
            rows,
            P(node, None, "local"),
            P(node, None, "local"),
            P(node, "local", None),
            blocks,
            blocks,
            blocks,
            blocks,
            P(whole),
        ),
        out_specs=(rows, blocks),
        check_vma=False,
    )
```

time: 135 us -> 111 us (0.82)
  waiting for transfers between devices: 84 us -> 42.5 us
  blocking collectives: 0 us -> 19.6 us
  Pallas kernels: 0 us -> 15.4 us
  between operations: 14.4 us -> 0.88 us
  matrix products: 12.4 us -> 2.67 us
  starting transfers between devices: 12.9 us -> 19.4 us
  other arithmetic: 6.82 us -> 3.66 us
  local copies, waits for them, and re-layouts: 4.25 us -> 6.19 us
    all_gather x1 -> x0, waiting for transfers between devices: 63.6 us -> none  [body(): gathered = lax.all_gather(outgoing, whole, axis=0, tiled=True)]
    all_to_all x0 -> x1, blocking collectives: none -> 19.6 us  [body(): lax.all_to_all(outgoing, 'high', split_axis=0, concat_axis=0, tiled=True)]
    pallas_call x0 -> x4, Pallas kernels: none -> 15.4 us  [the longest x1 8.13 us: hidden_of(): pl.pallas_call(functools.partial(hidden_kernel, count, experts), grid_spe...]
    all_to_all x0 -> x2, waiting for transfers between devices: none -> 12.1 us  [body(): lax.all_to_all(total, 'high', split_axis=0, concat_axis=0, tiled=True)]
    dot_general x4 -> x0, matrix products: 10.8 us -> none  [the longest x1 6.38 us: body(): gate_act = jnp.dot(rows, w_gate[0], preferred_element_type=jnp.float32)]
    ppermute x12 -> x21, waiting for transfers between devices: 20.4 us -> 30.4 us  [shift(): return lax.ppermute(value, everyone, pairs)]
    all_to_all x0 -> x2, starting transfers between devices: none -> 6.77 us  [body(): lax.all_to_all(total, 'high', split_axis=0, concat_axis=0, tiled=True)]
    unnamed x20 -> x14, local copies, waits for them, and re-layouts: 0.22 us -> 6.19 us
  transfers between devices with their start and end apart: 13 -> 23, of which waited for: 8 -> 8; matrix products, arithmetic and copies ran while one was open for 3% -> 5% of each run, Pallas kernels for 0% -> 2%
where the time goes in v3:
time: 111 us; the launch traced here: 110 us
  waiting for transfers between devices  42.5 us (38%)
  blocking collectives  19.6 us (18%)
  starting transfers between devices  19.4 us (17%)
  Pallas kernels  15.4 us (14%)
  local copies, waits for them, and re-layouts  6.19 us (6%)
  other arithmetic  3.66 us (3%)
  matrix products  2.67 us (2%)
    ppermute x21, waiting for transfers between devices, shift(): return lax.ppermute(value, everyone, pairs)  30.4 us
    all_to_all x1, blocking collectives, body(): lax.all_to_all(outgoing, 'high', split_axis=0, concat_axis=0, tiled=True)  19.6 us
    ppermute x21, starting transfers between devices, shift(): return lax.ppermute(value, everyone, pairs)  12.6 us
    all_to_all x2, waiting for transfers between devices, body(): lax.all_to_all(total, 'high', split_axis=0, concat_axis=0, tiled=True)  12.1 us
    pallas_call x1, Pallas kernels, hidden_of(): pl.pallas_call(functools.partial(hidden_kernel, count, experts), grid_spe...  8.13 us
    all_to_all x2, starting transfers between devices, body(): lax.all_to_all(total, 'high', split_axis=0, concat_axis=0, tiled=True)  6.77 us
    unnamed x14, local copies, waits for them, and re-layouts  6.19 us
    pallas_call x2, Pallas kernels, down_of(): pl.pallas_call(down_kernel, grid=(columns // tile,), in_specs=[pl.BlockSp...  5.31 us
  transfers between devices with their start and end apart: 23, of which 8 were waited for; matrix products, arithmetic and copies ran while one was open for 5% of the time, Pallas kernels for 2%

profile of v3, /device:TPU:0, one launch (start us, length us, event | category | flops | bytes accessed | tf_op | source)
XLA Modules:
  0.0 110.3 jit_solution(15296271397165826147)
XLA Ops:
  0.6 2.0 %pack.1 = bf16[4,8,7296]{2,1,0:T(8,128)(2,1)} custom-call(bf16[8,7168]{1,0:T(8,128)(2,1)} %rows_ref.1, s32[8,8]{1,0:T(8,128)} %ids_ref.1, f32[8,8]{1,0:T(8,128)} %gates_ref.1), custom_call_target="tpu_custom_call" | custom-call | tf_op jit(solution)/shard_map/pack/pallas_call | solution.py:124
  2.6 19.6 %all_to_all.15 = bf16[4,8,7296]{2,1,0:T(8,128)(2,1)S(1)} all-to-all(bf16[4,8,7296]{2,1,0:T(8,128)(2,1)} %pack.1), channel_id=1, replica_groups=mesh['group'=1,'high'=4,'middle'=2,'core'=2,'local'=2] {'high'}, dimensions={0} | all-to-all | bytes 933888 | tf_op jit(solution)/shard_map/all_to_all | solution.py:241
  22.2 1.5 %collective-permute-start = (bf16[32,7296]{1,0:T(8,128)(2,1)S(1)}, bf16[32,7296]{1,0:T(8,128)(2,1)S(1)}, u32[]{:S(2)}, u32[]{:S(2)}) collective-permute-start(bf16[32,7296]{1,0:T(8,128)(2,1)S(1)} %bitcast.22), channel_id=1, source_target_pairs={{0,1},{1,0},{2,6},{3,7},{4,5},{5,4},{6,2},{7,3},{8,9},{9,8},{10,14... | collective-permute-start | bytes 1400840 | tf_op jit(solution)/shard_map/ppermute | solution.py:53
  23.7 1.5 %collective-permute-start.1 = (bf16[32,7296]{1,0:T(8,128)(2,1)S(1)}, bf16[32,7296]{1,0:T(8,128)(2,1)S(1)}, u32[]{:S(2)}, u32[]{:S(2)}) collective-permute-start(bf16[32,7296]{1,0:T(8,128)(2,1)S(1)} %bitcast.23), channel_id=1, source_target_pairs={{0,4},{1,5},{2,3},{3,2},{4,0},{5,1},{6,7},{7,6},{8,12},{9,13},{10,... | collective-permute-start | bytes 1400840 | tf_op jit(solution)/shard_map/ppermute | solution.py:53
  25.2 10.5 %collective-permute-done.refs_1_.refs_9_ = bf16[32,7296]{1,0:T(8,128)(2,1)S(1)} collective-permute-done((bf16[32,7296]{1,0:T(8,128)(2,1)S(1)}, bf16[32,7296]{1,0:T(8,128)(2,1)S(1)}, u32[]{:S(2)}, u32[]{:S(2)}) %collective-permute-start) | collective-permute-done | bytes 466976 | tf_op jit(solution)/shard_map/ppermute | solution.py:53
  36.3 8.0 %collective-permute-done.2.refs_3_.refs_11_ = bf16[32,7296]{1,0:T(8,128)(2,1)S(1)} collective-permute-done((bf16[32,7296]{1,0:T(8,128)(2,1)S(1)}, bf16[32,7296]{1,0:T(8,128)(2,1)S(1)}, u32[]{:S(2)}, u32[]{:S(2)}) %collective-permute-start.2) | collective-permute-done | bytes 466976 | tf_op jit(solution)/shard_map/ppermute | solution.py:53
  45.0 1.5 %fusion.12 = f32[2,64,512]{2,1,0:T(8,128)S(1)} fusion(bf16[2,64,512]{2,1,0:T(8,128)(2,1)} %param.17, bf16[2,512,512]{2,1,0:T(8,128)(2,1)S(1)} %copy-done), kind=kOutput, calls=%fused_computation.31 | convolution fusion | flops 67108864 | bytes 1441792 | tf_op jit(solution)/shard_map/rhc,rjc->rhj/dot_general | solution.py:19
  46.6 3.1 %copy-done.1 = bf16[1,7168,512]{2,1,0:T(8,128)(2,1)S(1)} copy-done((bf16[1,7168,512]{2,1,0:T(8,128)(2,1)S(1)}, bf16[1,7168,512]{2,1,0:T(8,128)(2,1)}, u32[]{:S(2)}) %copy-start.1) | copy-done | bytes 7340056
  49.6 3.1 %copy-done.2 = bf16[1,7168,512]{2,1,0:T(8,128)(2,1)S(1)} copy-done((bf16[1,7168,512]{2,1,0:T(8,128)(2,1)S(1)}, bf16[1,7168,512]{2,1,0:T(8,128)(2,1)}, u32[]{:S(2)}) %copy-start.2) | copy-done | bytes 7340056
  52.7 8.1 %gate_up.1 = (bf16[256,512]{1,0:T(8,128)(2,1)S(1)}, f32[256,128]{1,0:T(8,128)S(1)}) custom-call(s32[1]{0:T(128)} %bitcast.node_ref, bf16[32,7296]{1,0:T(8,128)(2,1)S(1)} %bitcast.25, bf16[32,7296]{1,0:T(8,128)(2,1)S(1)} %collective-permute-done.refs_1_.refs_9_, bf16[32,7296]{1,0:T(8,128)(2,1)S(1)} %collective-permute-done.1.refs_2_.refs_10_, ...), custom_call_target="tpu_custom_call" | custom-call | flops 3758096384 | bytes 18350080 | tf_op jit(solution)/shard_map/gate_up/pallas_call | solution.py:161
  60.9 2.7 %down.2 = (bf16[32,3584]{1,0:T(8,128)(2,1)S(1)}, bf16[32,3584]{1,0:T(8,128)(2,1)S(1)}, bf16[32,3584]{1,0:T(8,128)(2,1)S(1)}, bf16[32,3584]{1,0:T(8,128)(2,1)S(1)...) custom-call(bf16[256,512]{1,0:T(8,128)(2,1)S(1)} %get-tuple-element., ...), custom_call_target="tpu_custom_call" | custom-call | flops 939524096 | bytes 5505024 | tf_op jit(solution)/shard_map/down/pallas_call | solution.py:202
  65.0 2.7 %down.3 = (bf16[32,3584]{1,0:T(8,128)(2,1)S(1)}, bf16[32,3584]{1,0:T(8,128)(2,1)S(1)}, bf16[32,3584]{1,0:T(8,128)(2,1)S(1)}, bf16[32,3584]{1,0:T(8,128)(2,1)S(1)...) custom-call(bf16[256,512]{1,0:T(8,128)(2,1)S(1)} %get-tuple-element., ...), custom_call_target="tpu_custom_call" | custom-call | flops 939524096 | bytes 5505024 | tf_op jit(solution)/shard_map/down/pallas_call | solution.py:202
  69.9 2.0 %collective-permute-start.9 = (bf16[32,3584]{1,0:T(8,128)(2,1)S(1)}, bf16[32,3584]{1,0:T(8,128)(2,1)S(1)}, u32[]{:S(2)}, u32[]{:S(2)}) collective-permute-start(bf16[32,3584]{1,0:T(8,128)(2,1)S(1)} %add_convert_fusion.12), channel_id=1, source_target_pairs={{0,4},{1,5},{2,3},{3,2},{4,0},{5,1},{6,7},{7,6},{8,12},{9,13},{10,... | collective-permute-start | bytes 688136 | tf_op jit(solution)/shard_map/ppermute | solution.py:53
  71.9 3.9 %collective-permute-done.12 = bf16[32,3584]{1,0:T(8,128)(2,1)S(1)} collective-permute-done((bf16[32,3584]{1,0:T(8,128)(2,1)S(1)}, bf16[32,3584]{1,0:T(8,128)(2,1)S(1)}, u32[]{:S(2)}, u32[]{:S(2)}) %collective-permute-start.12) | collective-permute-done | bytes 229408 | tf_op jit(solution)/shard_map/ppermute | solution.py:53
  76.0 2.0 %collective-permute-start.16 = (bf16[32,3584]{1,0:T(8,128)(2,1)S(1)}, bf16[32,3584]{1,0:T(8,128)(2,1)S(1)}, u32[]{:S(2)}, u32[]{:S(2)}) collective-permute-start(bf16[32,3584]{1,0:T(8,128)(2,1)S(1)} %add_convert_fusion.5), channel_id=1, source_target_pairs={{0,4},{1,5},{2,3},{3,2},{4,0},{5,1},{6,7},{7,6},{8,12},{9,13},{10,... | collective-permute-start | bytes 688136 | tf_op jit(solution)/shard_map/ppermute | solution.py:53
  78.0 3.8 %collective-permute-done.19 = bf16[32,3584]{1,0:T(8,128)(2,1)S(1)} collective-permute-done((bf16[32,3584]{1,0:T(8,128)(2,1)S(1)}, bf16[32,3584]{1,0:T(8,128)(2,1)S(1)}, u32[]{:S(2)}, u32[]{:S(2)}) %collective-permute-start.19) | collective-permute-done | bytes 229408 | tf_op jit(solution)/shard_map/ppermute | solution.py:53
  81.8 1.5 %collective-permute-start.13 = (bf16[32,3584]{1,0:T(8,128)(2,1)S(1)}, bf16[32,3584]{1,0:T(8,128)(2,1)S(1)}, u32[]{:S(2)}, u32[]{:S(2)}) collective-permute-start(bf16[32,3584]{1,0:T(8,128)(2,1)S(1)} %add_convert_fusion.8), channel_id=1, source_target_pairs={{0,1},{1,0},{2,6},{3,7},{4,5},{5,4},{6,2},{7,3},{8,9},{9,8},{10,14... | collective-permute-start | bytes 688136 | tf_op jit(solution)/shard_map/ppermute | solution.py:53
  84.0 3.8 %collective-permute-done.13 = bf16[32,3584]{1,0:T(8,128)(2,1)S(1)} collective-permute-done((bf16[32,3584]{1,0:T(8,128)(2,1)S(1)}, bf16[32,3584]{1,0:T(8,128)(2,1)S(1)}, u32[]{:S(2)}, u32[]{:S(2)}) %collective-permute-start.13) | collective-permute-done | bytes 229408 | tf_op jit(solution)/shard_map/ppermute | solution.py:53
  88.6 3.4 %all-to-all-start.1 = ((bf16[4,8,3584]{2,1,0:T(8,128)(2,1)}), bf16[4,8,3584]{2,1,0:T(8,128)(2,1)S(1)}, u32[]{:S(2)}, u32[]{:S(2)}) async-start(bf16[4,8,3584]{2,1,0:T(8,128)(2,1)} %fusion.6), calls=%async_computation.1 | async-start | bytes 458752 | tf_op jit(solution)/shard_map/all_to_all | solution.py:250
  92.1 0.8 fusion.7
  92.9 6.9 %all-to-all-done.1 = bf16[4,8,3584]{2,1,0:T(8,128)(2,1)S(1)} async-done(((bf16[4,8,3584]{2,1,0:T(8,128)(2,1)}), bf16[4,8,3584]{2,1,0:T(8,128)(2,1)S(1)}, u32[]{:S(2)}, u32[]{:S(2)}) %all-to-all-start.1) | async-done | bytes 229408 | tf_op jit(solution)/shard_map/all_to_all | solution.py:250
  99.7 3.4 %all-to-all-start.2 = ((bf16[4,8,3584]{2,1,0:T(8,128)(2,1)}), bf16[4,8,3584]{2,1,0:T(8,128)(2,1)S(1)}, u32[]{:S(2)}, u32[]{:S(2)}) async-start(bf16[4,8,3584]{2,1,0:T(8,128)(2,1)} %fusion.7), calls=%async_computation.2 | async-start | bytes 458752 | tf_op jit(solution)/shard_map/all_to_all | solution.py:250
  103.3 1.0 convolution_convert_fusion
  104.4 5.2 %all-to-all-done.2 = bf16[4,8,3584]{2,1,0:T(8,128)(2,1)S(1)} async-done(((bf16[4,8,3584]{2,1,0:T(8,128)(2,1)}), bf16[4,8,3584]{2,1,0:T(8,128)(2,1)S(1)}, u32[]{:S(2)}, u32[]{:S(2)}) %all-to-all-start.2) | async-done | bytes 229408 | tf_op jit(solution)/shard_map/all_to_all | solution.py:250
  (58 shorter events, 7.6 us)
Async XLA Ops:
  0.6 44.4 %copy-start = (bf16[2,512,512]{2,1,0:T(8,128)(2,1)S(1)}, bf16[2,512,512]{2,1,0:T(8,128)(2,1)}, u32[]{:S(2)}) copy-start(bf16[2,512,512]{2,1,0:T(8,128)(2,1)} %param.19) | copy-start | bytes 3145732
  22.2 13.5 %collective-permute-start = (bf16[32,7296]{1,0:T(8,128)(2,1)S(1)}, bf16[32,7296]{1,0:T(8,128)(2,1)S(1)}, u32[]{:S(2)}, u32[]{:S(2)}) collective-permute-start(bf16[32,7296]{1,0:T(8,128)(2,1)S(1)} %bitcast.22), channel_id=1, source_target_pairs={{0,1},{1,0},{2,6},{3,7},{4,5},{5,4},{6,2},{7,3},{8,9},{9,8},{10,14... | collective-permute-start | bytes 1400840 | tf_op jit(solution)/shard_map/ppermute | solution.py:53
  23.7 12.6 %collective-permute-start.1 = (bf16[32,7296]{1,0:T(8,128)(2,1)S(1)}, bf16[32,7296]{1,0:T(8,128)(2,1)S(1)}, u32[]{:S(2)}, u32[]{:S(2)}) collective-permute-start(bf16[32,7296]{1,0:T(8,128)(2,1)S(1)} %bitcast.23), channel_id=1, source_target_pairs={{0,4},{1,5},{2,3},{3,2},{4,0},{5,1},{6,7},{7,6},{8,12},{9,13},{10,... | collective-permute-start | bytes 1400840 | tf_op jit(solution)/shard_map/ppermute | solution.py:53
  35.7 8.6 %collective-permute-start.2 = (bf16[32,7296]{1,0:T(8,128)(2,1)S(1)}, bf16[32,7296]{1,0:T(8,128)(2,1)S(1)}, u32[]{:S(2)}, u32[]{:S(2)}) collective-permute-start(bf16[32,7296]{1,0:T(8,128)(2,1)S(1)} %collective-permute-done.refs_1_.refs_9_), channel_id=1, source_target_pairs={{0,4},{1,5},{2,3},{3,2},{4,0},{5,1},{6,7},{7,6},{8,12},{9,13},{10,... | collective-permute-start | bytes 1400840 | tf_op jit(solution)/shard_map/ppermute | solution.py:53
  35.8 10.7 %collective-permute-start.3 = (bf16[32,7296]{1,0:T(8,128)(2,1)S(1)}, bf16[32,7296]{1,0:T(8,128)(2,1)S(1)}, u32[]{:S(2)}, u32[]{:S(2)}) collective-permute-start(bf16[32,7296]{1,0:T(8,128)(2,1)S(1)} %bitcast.24), channel_id=1, source_target_pairs={{0,2},{1,3},{2,0},{3,1},{4,6},{5,7},{6,4},{7,5},{8,10},{9,11},{10,... | collective-permute-start | bytes 1400840 | tf_op jit(solution)/shard_map/ppermute | solution.py:53
  35.8 10.7 %collective-permute-start.4 = (bf16[32,7296]{1,0:T(8,128)(2,1)S(1)}, bf16[32,7296]{1,0:T(8,128)(2,1)S(1)}, u32[]{:S(2)}, u32[]{:S(2)}) collective-permute-start(bf16[32,7296]{1,0:T(8,128)(2,1)S(1)} %collective-permute-done.refs_1_.refs_9_), channel_id=1, source_target_pairs={{0,2},{1,3},{2,0},{3,1},{4,6},{5,7},{6,4},{7,5},{8,10},{9,11},{10,... | collective-permute-start | bytes 1400840 | tf_op jit(solution)/shard_map/ppermute | solution.py:53
  36.3 10.2 %collective-permute-start.5 = (bf16[32,7296]{1,0:T(8,128)(2,1)S(1)}, bf16[32,7296]{1,0:T(8,128)(2,1)S(1)}, u32[]{:S(2)}, u32[]{:S(2)}) collective-permute-start(bf16[32,7296]{1,0:T(8,128)(2,1)S(1)} %collective-permute-done.1.refs_2_.refs_10_), channel_id=1, source_target_pairs={{0,2},{1,3},{2,0},{3,1},{4,6},{5,7},{6,4},{7,5},{8,10},{9,11},{10,... | collective-permute-start | bytes 1400840 | tf_op jit(solution)/shard_map/ppermute | solution.py:53
  44.3 2.3 %collective-permute-start.6 = (bf16[32,7296]{1,0:T(8,128)(2,1)S(1)}, bf16[32,7296]{1,0:T(8,128)(2,1)S(1)}, u32[]{:S(2)}, u32[]{:S(2)}) collective-permute-start(bf16[32,7296]{1,0:T(8,128)(2,1)S(1)} %collective-permute-done.2.refs_3_.refs_11_), channel_id=1, source_target_pairs={{0,2},{1,3},{2,0},{3,1},{4,6},{5,7},{6,4},{7,5},{8,10},{9,11},{10,... | collective-permute-start | bytes 1400840 | tf_op jit(solution)/shard_map/ppermute | solution.py:53
  63.6 4.6 %collective-permute-start.8 = (bf16[32,3584]{1,0:T(8,128)(2,1)S(1)}, bf16[32,3584]{1,0:T(8,128)(2,1)S(1)}, u32[]{:S(2)}, u32[]{:S(2)}) collective-permute-start(bf16[32,3584]{1,0:T(8,128)(2,1)S(1)} %get-tuple-element.25), channel_id=1, source_target_pairs={{0,2},{1,3},{2,0},{3,1},{4,6},{5,7},{6,4},{7,5},{8,10},{9,11},{10,... | collective-permute-start | bytes 688136 | tf_op jit(solution)/shard_map/ppermute | solution.py:53
  64.3 4.0 %collective-permute-start.11 = (bf16[32,3584]{1,0:T(8,128)(2,1)S(1)}, bf16[32,3584]{1,0:T(8,128)(2,1)S(1)}, u32[]{:S(2)}, u32[]{:S(2)}) collective-permute-start(bf16[32,3584]{1,0:T(8,128)(2,1)S(1)} %get-tuple-element.29), channel_id=1, source_target_pairs={{0,2},{1,3},{2,0},{3,1},{4,6},{5,7},{6,4},{7,5},{8,10},{9,11},{10,... | collective-permute-start | bytes 688136 | tf_op jit(solution)/shard_map/ppermute | solution.py:53
  64.4 5.5 %collective-permute-start.10 = (bf16[32,3584]{1,0:T(8,128)(2,1)S(1)}, bf16[32,3584]{1,0:T(8,128)(2,1)S(1)}, u32[]{:S(2)}, u32[]{:S(2)}) collective-permute-start(bf16[32,3584]{1,0:T(8,128)(2,1)S(1)} %get-tuple-element.27), channel_id=1, source_target_pairs={{0,2},{1,3},{2,0},{3,1},{4,6},{5,7},{6,4},{7,5},{8,10},{9,11},{10,... | collective-permute-start | bytes 688136 | tf_op jit(solution)/shard_map/ppermute | solution.py:53
  64.9 18.5 %collective-permute-start.7 = (bf16[32,3584]{1,0:T(8,128)(2,1)S(1)}, bf16[32,3584]{1,0:T(8,128)(2,1)S(1)}, u32[]{:S(2)}, u32[]{:S(2)}) collective-permute-start(bf16[32,3584]{1,0:T(8,128)(2,1)S(1)} %get-tuple-element.23), channel_id=1, source_target_pairs={{0,2},{1,3},{2,0},{3,1},{4,6},{5,7},{6,4},{7,5},{8,10},{9,11},{10,... | collective-permute-start | bytes 688136 | tf_op jit(solution)/shard_map/ppermute | solution.py:53
  67.6 1.6 %collective-permute-start.15 = (bf16[32,3584]{1,0:T(8,128)(2,1)S(1)}, bf16[32,3584]{1,0:T(8,128)(2,1)S(1)}, u32[]{:S(2)}, u32[]{:S(2)}) collective-permute-start(bf16[32,3584]{1,0:T(8,128)(2,1)S(1)} %get-tuple-element.33), channel_id=1, source_target_pairs={{0,2},{1,3},{2,0},{3,1},{4,6},{5,7},{6,4},{7,5},{8,10},{9,11},{10,... | collective-permute-start | bytes 688136 | tf_op jit(solution)/shard_map/ppermute | solution.py:53
  68.1 1.6 %collective-permute-start.18 = (bf16[32,3584]{1,0:T(8,128)(2,1)S(1)}, bf16[32,3584]{1,0:T(8,128)(2,1)S(1)}, u32[]{:S(2)}, u32[]{:S(2)}) collective-permute-start(bf16[32,3584]{1,0:T(8,128)(2,1)S(1)} %get-tuple-element.37), channel_id=1, source_target_pairs={{0,2},{1,3},{2,0},{3,1},{4,6},{5,7},{6,4},{7,5},{8,10},{9,11},{10,... | collective-permute-start | bytes 688136 | tf_op jit(solution)/shard_map/ppermute | solution.py:53
  68.3 7.7 %collective-permute-start.17 = (bf16[32,3584]{1,0:T(8,128)(2,1)S(1)}, bf16[32,3584]{1,0:T(8,128)(2,1)S(1)}, u32[]{:S(2)}, u32[]{:S(2)}) collective-permute-start(bf16[32,3584]{1,0:T(8,128)(2,1)S(1)} %get-tuple-element.35), channel_id=1, source_target_pairs={{0,2},{1,3},{2,0},{3,1},{4,6},{5,7},{6,4},{7,5},{8,10},{9,11},{10,... | collective-permute-start | bytes 688136 | tf_op jit(solution)/shard_map/ppermute | solution.py:53
  69.3 22.8 %collective-permute-start.14 = (bf16[32,3584]{1,0:T(8,128)(2,1)S(1)}, bf16[32,3584]{1,0:T(8,128)(2,1)S(1)}, u32[]{:S(2)}, u32[]{:S(2)}) collective-permute-start(bf16[32,3584]{1,0:T(8,128)(2,1)S(1)} %get-tuple-element.31), channel_id=1, source_target_pairs={{0,2},{1,3},{2,0},{3,1},{4,6},{5,7},{6,4},{7,5},{8,10},{9,11},{10,... | collective-permute-start | bytes 688136 | tf_op jit(solution)/shard_map/ppermute | solution.py:53
  69.7 6.1 %collective-permute-start.12 = (bf16[32,3584]{1,0:T(8,128)(2,1)S(1)}, bf16[32,3584]{1,0:T(8,128)(2,1)S(1)}, u32[]{:S(2)}, u32[]{:S(2)}) collective-permute-start(bf16[32,3584]{1,0:T(8,128)(2,1)S(1)} %add_convert_fusion.9), channel_id=1, source_target_pairs={{0,4},{1,5},{2,3},{3,2},{4,0},{5,1},{6,7},{7,6},{8,12},{9,13},{10,... | collective-permute-start | bytes 688136 | tf_op jit(solution)/shard_map/ppermute | solution.py:53
  69.9 14.1 %collective-permute-start.9 = (bf16[32,3584]{1,0:T(8,128)(2,1)S(1)}, bf16[32,3584]{1,0:T(8,128)(2,1)S(1)}, u32[]{:S(2)}, u32[]{:S(2)}) collective-permute-start(bf16[32,3584]{1,0:T(8,128)(2,1)S(1)} %add_convert_fusion.12), channel_id=1, source_target_pairs={{0,4},{1,5},{2,3},{3,2},{4,0},{5,1},{6,7},{7,6},{8,12},{9,13},{10,... | collective-permute-start | bytes 688136 | tf_op jit(solution)/shard_map/ppermute | solution.py:53
  75.8 6.0 %collective-permute-start.19 = (bf16[32,3584]{1,0:T(8,128)(2,1)S(1)}, bf16[32,3584]{1,0:T(8,128)(2,1)S(1)}, u32[]{:S(2)}, u32[]{:S(2)}) collective-permute-start(bf16[32,3584]{1,0:T(8,128)(2,1)S(1)} %add_convert_fusion.2), channel_id=1, source_target_pairs={{0,4},{1,5},{2,3},{3,2},{4,0},{5,1},{6,7},{7,6},{8,12},{9,13},{10,... | collective-permute-start | bytes 688136 | tf_op jit(solution)/shard_map/ppermute | solution.py:53
  76.0 16.1 %collective-permute-start.16 = (bf16[32,3584]{1,0:T(8,128)(2,1)S(1)}, bf16[32,3584]{1,0:T(8,128)(2,1)S(1)}, u32[]{:S(2)}, u32[]{:S(2)}) collective-permute-start(bf16[32,3584]{1,0:T(8,128)(2,1)S(1)} %add_convert_fusion.5), channel_id=1, source_target_pairs={{0,4},{1,5},{2,3},{3,2},{4,0},{5,1},{6,7},{7,6},{8,12},{9,13},{10,... | collective-permute-start | bytes 688136 | tf_op jit(solution)/shard_map/ppermute | solution.py:53
  81.8 6.0 %collective-permute-start.13 = (bf16[32,3584]{1,0:T(8,128)(2,1)S(1)}, bf16[32,3584]{1,0:T(8,128)(2,1)S(1)}, u32[]{:S(2)}, u32[]{:S(2)}) collective-permute-start(bf16[32,3584]{1,0:T(8,128)(2,1)S(1)} %add_convert_fusion.8), channel_id=1, source_target_pairs={{0,1},{1,0},{2,6},{3,7},{4,5},{5,4},{6,2},{7,3},{8,9},{9,8},{10,14... | collective-permute-start | bytes 688136 | tf_op jit(solution)/shard_map/ppermute | solution.py:53
  83.4 8.7 %collective-permute-start.20 = (bf16[32,3584]{1,0:T(8,128)(2,1)S(1)}, bf16[32,3584]{1,0:T(8,128)(2,1)S(1)}, u32[]{:S(2)}, u32[]{:S(2)}) collective-permute-start(bf16[32,3584]{1,0:T(8,128)(2,1)S(1)} %add_convert_fusion.1), channel_id=1, source_target_pairs={{0,1},{1,0},{2,6},{3,7},{4,5},{5,4},{6,2},{7,3},{8,9},{9,8},{10,14... | collective-permute-start | bytes 688136 | tf_op jit(solution)/shard_map/ppermute | solution.py:53
  88.6 11.1 %all-to-all-start.1 = ((bf16[4,8,3584]{2,1,0:T(8,128)(2,1)}), bf16[4,8,3584]{2,1,0:T(8,128)(2,1)S(1)}, u32[]{:S(2)}, u32[]{:S(2)}) async-start(bf16[4,8,3584]{2,1,0:T(8,128)(2,1)} %fusion.6), calls=%async_computation.1 | async-start | bytes 458752 | tf_op jit(solution)/shard_map/all_to_all | solution.py:250
  99.7 9.9 %all-to-all-start.2 = ((bf16[4,8,3584]{2,1,0:T(8,128)(2,1)}), bf16[4,8,3584]{2,1,0:T(8,128)(2,1)S(1)}, u32[]{:S(2)}, u32[]{:S(2)}) async-start(bf16[4,8,3584]{2,1,0:T(8,128)(2,1)} %fusion.7), calls=%async_computation.2 | async-start | bytes 458752 | tf_op jit(solution)/shard_map/all_to_all | solution.py:250
  (6 other events, 36.8 us)

commit v4 on v3

v4 whole, which is shorter than its diff:
```python
import functools

import jax
import jax.numpy as jnp
import numpy as np
from jax import lax
from jax.experimental import pallas as pl
from jax.experimental.pallas import tpu as pltpu
from jax.sharding import Mesh
from jax.sharding import PartitionSpec as P

score_scale = 192.0 ** (-0.5)
everyone = ("high", "middle", "core", "local")
MEBI = 1024 * 1024


def attention(query_latent, query_rope, cache_latent, cache_rope, cache_lengths):
    slot_count = cache_latent.shape[1]
    scores = jnp.einsum(
        "rhc,rjc->rhj", query_latent, cache_latent, preferred_element_type=jnp.float32
    )
    scores = (
        scores
        + jnp.einsum("rhp,rpj->rhj", query_rope, cache_rope, preferred_element_type=jnp.float32)
    ) * score_scale
    in_range = jnp.arange(slot_count, dtype=jnp.int32)[None, None, :] < cache_lengths[:, None, None]
    scores = jnp.where(in_range, scores, -jnp.inf)
    row_peak = jnp.max(scores, axis=-1, keepdims=True)
    lifted = jnp.where(in_range, jnp.exp(scores - row_peak), 0.0)
    weights = (lifted / jnp.sum(lifted, axis=-1, keepdims=True)).astype(jnp.bfloat16)
    return jnp.einsum(
        "rhj,rjc->rhc", weights, cache_latent, preferred_element_type=jnp.float32
    ).astype(jnp.bfloat16)


class Grid:
    def __init__(self):
        self.sizes = tuple(lax.axis_size(name) for name in everyone)
        self.mixed = self.sizes[1] == self.sizes[3]

    def swap(self, value, pick, mask):
        pairs = []
        for place in np.ndindex(*self.sizes):
            other = list(place)
            other[pick(place[2])] ^= mask
            pairs.append(
                (
                    int(np.ravel_multi_index(place, self.sizes)),
                    int(np.ravel_multi_index(other, self.sizes)),
                )
            )
        return lax.ppermute(value, everyone, pairs)

    def high(self, core):
        return 0

    def core(self, core):
        return 2

    def first(self, core):
        return 1 if self.mixed and core == 1 else 3

    def second(self, core):
        return 3 if self.mixed and core == 1 else 1

    def extent(self, pick):
        return self.sizes[pick(0)]

    def gather(self, rows):
        lines = [rows] + [self.swap(rows, self.high, m) for m in range(1, self.extent(self.high))]
        half = len(lines) // 2
        places = []
        for lines in (lines[:half], lines[half:]):
            line = jnp.concatenate(lines, axis=0)
            near = [line]
            near += [self.swap(line, self.first, m) for m in range(1, self.extent(self.first))]
            mine = list(near)
            for m in range(1, self.extent(self.second)):
                mine += [self.swap(block, self.second, m) for block in near]
            places.append(mine + [self.swap(block, self.core, 1) for block in mine])
        return [list(blocks) for blocks in zip(*places)]

    def scatter_sum(self, mine, other):
        size = mine[0].shape[0]
        last, rest = [self.swap(part, self.core, 1) for part in other]
        sums = [add([mine[-1], last])]
        for i in range(len(mine) - 1):
            sums.insert(i, add([mine[i], rest[i * size : (i + 1) * size]]))
        wide = self.extent(self.first)
        near = []
        for i in range(wide):
            parts = [sums[i]]
            for m in range(1, self.extent(self.second)):
                parts.append(self.swap(sums[m * wide + i], self.second, m))
            near.append(parts)
        near = [add(parts) for parts in near]
        line = add([near[0]] + [self.swap(near[m], self.first, m) for m in range(1, wide)])
        rows = size // self.extent(self.high)
        parts = [line[:rows]]
        for m in range(1, self.extent(self.high)):
            parts.append(self.swap(line[m * rows : (m + 1) * rows], self.high, m))
        return add(parts)


def add(parts):
    total = parts[0].astype(jnp.float32)
    for part in parts[1:]:
        total = total + part.astype(jnp.float32)
    return total.astype(parts[0].dtype)


def pack_kernel(experts, rows_ref, ids_ref, gates_ref, out_ref):
    width = rows_ref.shape[1]
    extra = out_ref.shape[1] - width
    gates = gates_ref[...]
    shares = 2.5 * gates / jnp.sum(gates, axis=1, keepdims=True)
    ids = ids_ref[...]
    lane = lax.broadcasted_iota(jnp.int32, (ids.shape[0], extra), 1)
    expert = jnp.where(lane < experts, lane, lane - experts)
    table = jnp.zeros(lane.shape, jnp.float32)
    for k in range(ids.shape[1]):
        table += jnp.where(expert == ids[:, k : k + 1], shares[:, k : k + 1], 0.0)
    high = table.astype(jnp.bfloat16).astype(jnp.float32)
    table = jnp.where(lane < experts, high, jnp.where(lane < 2 * experts, table - high, 0.0))
    out_ref[:, :width] = rows_ref[...]
    out_ref[:, width:] = table.astype(jnp.bfloat16)


def pack(experts, moe_rows, route_ids, route_gates):
    rows, width = moe_rows.shape
    total = width + pl.cdiv(2 * experts, 128) * 128
    return pl.pallas_call(
        functools.partial(pack_kernel, experts),
        out_shape=jax.ShapeDtypeStruct((rows, total), jnp.bfloat16),
        name="pack",
    )(moe_rows, route_ids, route_gates)


def spread(product, outs):
    start = 0
    for out, columns in outs:
        size = out.shape[0]
        out[:, columns] = product[start : start + size]
        start += size


def expert_kernel(count, outputs, experts, tile, down_tile, node_ref, *refs):
    blocks = refs[:count]
    gate_hbm, up_hbm, down_hbm, hidden_ref, share_ref = refs[count : count + 5]
    outs = refs[count + 5 : count + 5 + outputs]
    gate, up, down, gate_sum, up_sum, gate_sem, up_sem, down_sem = refs[count + 5 + outputs :]
    width = gate.shape[0]
    columns = down.shape[1]
    steps = [pl.ds(k, tile) for k in range(0, width, tile)]
    down_steps = [pl.ds(k, down_tile) for k in range(0, columns, down_tile)]
    copies = []
    for k, part in enumerate(steps):
        pair = (
            pltpu.make_async_copy(gate_hbm.at[part], gate.at[part], gate_sem.at[k]),
            pltpu.make_async_copy(up_hbm.at[part], up.at[part], up_sem.at[k]),
        )
        for copy in pair:
            copy.start()
        copies.append(pair)
    down_copies = []
    for k, part in enumerate(down_steps):
        copy = pltpu.make_async_copy(down_hbm.at[:, part], down.at[:, part], down_sem.at[k])
        copy.start()
        down_copies.append(copy)

    table = jnp.concatenate([block[:, width:] for block in blocks], axis=0).astype(jnp.float32)
    lane = lax.broadcasted_iota(jnp.int32, table.shape, 1)
    mine = (lane == node_ref[0]) | (lane == node_ref[0] + experts)
    share = jnp.sum(jnp.where(mine, table, 0.0), axis=1, keepdims=True)
    share_ref[...] = jnp.broadcast_to(share, share_ref.shape)

    for k, part in enumerate(steps):
        rows = jnp.concatenate([block[:, part] for block in blocks], axis=0)
        for copy, weight, total in zip(copies[k], (gate, up), (gate_sum, up_sum)):
            copy.wait()
            product = jnp.dot(rows, weight[part], preferred_element_type=jnp.float32)
            if k == 0:
                total[...] = product
            else:
                total[...] += product
    hidden_ref[...] = (jax.nn.silu(gate_sum[...]) * up_sum[...]).astype(jnp.bfloat16)
    for k, part in enumerate(down_steps):
        down_copies[k].wait()
        product = jnp.dot(hidden_ref[...], down[:, part], preferred_element_type=jnp.float32)
        product = (product * share_ref[:, :1]).astype(jnp.bfloat16)
        spread(product, [(out, part) for out in outs])


def expert(blocks, w_gate, w_up, w_down, experts, node, sizes, columns):
    width, units = w_gate.shape
    rows = sum(sizes)
    tile, down_tile = 1024, 512
    return pl.pallas_call(
        functools.partial(
            expert_kernel, len(blocks), len(sizes), experts, tile, down_tile
        ),
        in_specs=[pl.BlockSpec(memory_space=pltpu.SMEM)]
        + [pl.BlockSpec(memory_space=pltpu.VMEM)] * len(blocks)
        + [pl.BlockSpec(memory_space=pl.ANY)] * 3,
        out_specs=[pl.BlockSpec(memory_space=pltpu.VMEM)] * (2 + len(sizes)),
        out_shape=[
            jax.ShapeDtypeStruct((rows, units), jnp.bfloat16),
            jax.ShapeDtypeStruct((rows, 128), jnp.float32),
        ]
        + [jax.ShapeDtypeStruct((size, columns), jnp.bfloat16) for size in sizes],
        scratch_shapes=[
            pltpu.VMEM((width, units), jnp.bfloat16),
            pltpu.VMEM((width, units), jnp.bfloat16),
            pltpu.VMEM((units, columns), jnp.bfloat16),
            pltpu.VMEM((rows, units), jnp.float32),
            pltpu.VMEM((rows, units), jnp.float32),
            pltpu.SemaphoreType.DMA((width // tile,)),
            pltpu.SemaphoreType.DMA((width // tile,)),
            pltpu.SemaphoreType.DMA((columns // down_tile,)),
        ],
        cost_estimate=pl.CostEstimate(
            flops=4 * rows * width * units + 2 * rows * columns * units,
            bytes_accessed=4 * width * units + 2 * units * columns,
            transcendentals=rows * units,
        ),
        compiler_params=pltpu.CompilerParams(vmem_limit_bytes=40 * MEBI),
        name="expert",
    )(node, *blocks, w_gate, w_up, w_down)


def down_kernel(hidden_ref, share_ref, down_ref, *outs):
    product = jnp.dot(hidden_ref[...], down_ref[...], preferred_element_type=jnp.float32)
    product = (product * share_ref[:, :1]).astype(jnp.bfloat16)
    spread(product, [(out, pl.ds(0, product.shape[1])) for out in outs])


def down_of(hidden, share, w_down, sizes, start):
    rows, units = hidden.shape
    columns = w_down.shape[1] - start
    tile = 1024
    offset = start // tile
    return pl.pallas_call(
        down_kernel,
        grid=(columns // tile,),
        in_specs=[
            pl.BlockSpec(memory_space=pltpu.VMEM),
            pl.BlockSpec(memory_space=pltpu.VMEM),
            pl.BlockSpec((units, tile), lambda j: (0, j + offset)),
        ],
        out_specs=[pl.BlockSpec((size, tile), lambda j: (0, j)) for size in sizes],
        out_shape=[jax.ShapeDtypeStruct((size, columns), jnp.bfloat16) for size in sizes],
        cost_estimate=pl.CostEstimate(
            flops=2 * rows * columns * units,
            bytes_accessed=2 * columns * (units + rows),
            transcendentals=0,
        ),
        compiler_params=pltpu.CompilerParams(vmem_limit_bytes=40 * MEBI),
        name="down",
    )(hidden, share, w_down)


def body(
    moe_rows,
    route_ids,
    route_gates,
    w_gate,
    w_up,
    w_down,
    query_latent,
    query_rope,
    cache_latent,
    cache_rope,
    cache_lengths,
):
    grid = Grid()
    high, middle, cores, _ = grid.sizes
    experts = high * middle * cores
    tokens, width = moe_rows.shape
    node = lax.axis_index(("high", "middle", "core")).astype(jnp.int32).reshape(1)
    places = grid.gather(pack(experts, moe_rows, route_ids, route_gates))
    attn_latent = attention(query_latent, query_rope, cache_latent, cache_rope, cache_lengths)
    size = high * tokens
    count = len(places) // 2
    sizes = [size] * count + [size, size * (count - 1)]
    places = places[:count] + places[-1:] + places[count:-1]
    blocks = [block for place in places for block in place]
    split = width * 4 // 7
    hidden, share, *products = expert(
        blocks, w_gate[0], w_up[0], w_down[0], experts, node, sizes, split
    )
    lower = grid.scatter_sum(products[:count], products[count:])
    products = down_of(hidden, share, w_down[0], sizes, split)
    upper = grid.scatter_sum(products[:count], products[count:])
    return (jnp.concatenate([lower, upper], axis=1), attn_latent)


def solution(mesh):
    groups, nodes, local = mesh.devices.shape
    split = Mesh(mesh.devices.reshape(groups, nodes // 4, 2, 2, local), ("group",) + everyone)
    node = ("high", "middle", "core")
    whole = ("group",) + everyone
    rows = P(whole, None)
    blocks = P(whole, None, None)
    return jax.shard_map(
        body,
        mesh=split,
        in_specs=(
            rows,
            rows,
            rows,
            P(node, None, "local"),
            P(node, None, "local"),
            P(node, "local", None),
            blocks,
            blocks,
            blocks,
            blocks,
            P(whole),
        ),
        out_specs=(rows, blocks),
        check_vma=False,
    )
```

time: 111 us -> 94.7 us (0.85)
  blocking collectives: 19.6 us -> 0 us
  starting transfers between devices: 19.4 us -> 30.9 us
  waiting for transfers between devices: 42.5 us -> 31.5 us
  matrix products: 2.67 us -> 5.19 us
  Pallas kernels: 15.4 us -> 13.7 us
  local copies, waits for them, and re-layouts: 6.19 us -> 7.74 us
    all_to_all x1 -> x0, blocking collectives: 19.6 us -> none  [body(): lax.all_to_all(outgoing, 'high', split_axis=0, concat_axis=0, tiled=True)]
    ppermute x21 -> x33, starting transfers between devices: 12.6 us -> 30.9 us  [swap(): return lax.ppermute(value, everyone, pairs)]
    all_to_all x2 -> x0, waiting for transfers between devices: 12.1 us -> none  [body(): lax.all_to_all(total, 'high', split_axis=0, concat_axis=0, tiled=True)]
    all_to_all x2 -> x0, starting transfers between devices: 6.77 us -> none  [body(): lax.all_to_all(total, 'high', split_axis=0, concat_axis=0, tiled=True)]
    pallas_call x2 -> x1, Pallas kernels: 5.31 us -> 1.72 us  [down_of(): pl.pallas_call(down_kernel, grid=(columns // tile,), in_specs=[pl.BlockSp...]
    pallas_call x1, Pallas kernels: 8.13 us -> 10.1 us  [expert(): pl.pallas_call(functools.partial(expert_kernel, len(blocks), len(sizes),...]
    dot_general x1, matrix products: 0.17 us -> 1.81 us  [attention(): jnp.einsum('rhp,rpj->rhj', query_rope, cache_rope, preferred_element_type...]
    reshape x2 -> x0, other arithmetic: 1.61 us -> none  [body(): total = grid.scatter_sum(products).reshape(high, tokens, half)]
  transfers between devices with their start and end apart: 23 -> 33, of which waited for: 8 -> 13; matrix products, arithmetic and copies ran while one was open for 5% -> 9% of each run, Pallas kernels for 2% -> 0%
where the time goes in v4:
time: 94.7 us; the launch traced here: 94.3 us
  waiting for transfers between devices  31.5 us (33%)
  starting transfers between devices  30.9 us (33%)
  Pallas kernels  13.7 us (14%)
  local copies, waits for them, and re-layouts  7.74 us (8%)
  matrix products  5.19 us (5%)
  other arithmetic  4.39 us (5%)
    ppermute x33, waiting for transfers between devices, swap(): return lax.ppermute(value, everyone, pairs)  31.5 us
    ppermute x33, starting transfers between devices, swap(): return lax.ppermute(value, everyone, pairs)  30.9 us
    pallas_call x1, Pallas kernels, expert(): pl.pallas_call(functools.partial(expert_kernel, len(blocks), len(sizes),...  10.1 us
    unnamed x31, local copies, waits for them, and re-layouts  7.69 us
    dot_general x1, matrix products, attention(): jnp.einsum('rhj,rjc->rhc', weights, cache_latent, preferred_element_type=...  2.05 us
  transfers between devices with their start and end apart: 33, of which 13 were waited for; matrix products, arithmetic and copies ran while one was open for 9% of the time, Pallas kernels for 0%

profile of v4, /device:TPU:0, one launch (start us, length us, event | category | flops | bytes accessed | tf_op | source)
XLA Modules:
  0.0 94.3 jit_solution(6797828668271597268)
XLA Ops:
  0.6 1.8 %pack.1 = bf16[8,7296]{1,0:T(8,128)(2,1)} custom-call(bf16[8,7168]{1,0:T(8,128)(2,1)} %rows_ref.1, s32[8,8]{1,0:T(8,128)} %ids_ref.1, f32[8,8]{1,0:T(8,128)} %gates_ref.1), custom_call_target="tpu_custom_call" | custom-call | tf_op jit(solution)/shard_map/pack/pallas_call | solution.py:132
  2.5 4.0 %collective-permute-start.1 = (bf16[8,7296]{1,0:T(8,128)(2,1)}, bf16[8,7296]{1,0:T(8,128)(2,1)S(1)}, u32[]{:S(2)}, u32[]{:S(2)}) collective-permute-start(bf16[8,7296]{1,0:T(8,128)(2,1)} %pack.1), channel_id=1, source_target_pairs={{0,16},{1,17},{2,18},{3,19},{4,20},{5,21},{6,22},{7,23},{8,24},{9,... | collective-permute-start | bytes 350216 | tf_op jit(solution)/shard_map/ppermute | solution.py:52
  8.1 7.7 %collective-permute-done.1 = bf16[8,7296]{1,0:T(8,128)(2,1)S(1)} collective-permute-done((bf16[8,7296]{1,0:T(8,128)(2,1)}, bf16[8,7296]{1,0:T(8,128)(2,1)S(1)}, u32[]{:S(2)}, u32[]{:S(2)}) %collective-permute-start.1) | collective-permute-done | bytes 116768 | tf_op jit(solution)/shard_map/ppermute | solution.py:52
  15.8 1.9 %collective-permute-start.4 = (bf16[16,7296]{1,0:T(8,128)(2,1)S(1)}, bf16[16,7296]{1,0:T(8,128)(2,1)S(1)}, u32[]{:S(2)}, u32[]{:S(2)}) collective-permute-start(bf16[16,7296]{1,0:T(8,128)(2,1)S(1)} %constant_dynamic-update-slice_fusion.refs_1_), channel_id=1, source_target_pairs={{0,1},{1,0},{2,6},{3,7},{4,5},{5,4},{6,2},{7,3},{8,9},{9,8},{10,14... | collective-permute-start | bytes 700424 | tf_op jit(solution)/shard_map/ppermute | solution.py:52
  18.9 1.8 %collective-permute-start.6 = (bf16[16,7296]{1,0:T(8,128)(2,1)S(1)}, bf16[16,7296]{1,0:T(8,128)(2,1)S(1)}, u32[]{:S(2)}, u32[]{:S(2)}) collective-permute-start(bf16[16,7296]{1,0:T(8,128)(2,1)S(1)} %constant_dynamic-update-slice_fusion.refs_1_), channel_id=1, source_target_pairs={{0,4},{1,5},{2,3},{3,2},{4,0},{5,1},{6,7},{7,6},{8,12},{9,13},{10,... | collective-permute-start | bytes 700424 | tf_op jit(solution)/shard_map/ppermute | solution.py:52
  21.0 3.5 %collective-permute-done.4.refs_3_ = bf16[16,7296]{1,0:T(8,128)(2,1)S(1)} collective-permute-done((bf16[16,7296]{1,0:T(8,128)(2,1)S(1)}, bf16[16,7296]{1,0:T(8,128)(2,1)S(1)}, u32[]{:S(2)}, u32[]{:S(2)}) %collective-permute-start.4) | collective-permute-done | bytes 233504 | tf_op jit(solution)/shard_map/ppermute | solution.py:52
  24.4 5.0 %collective-permute-done.3.refs_2_ = bf16[16,7296]{1,0:T(8,128)(2,1)S(1)} collective-permute-done((bf16[16,7296]{1,0:T(8,128)(2,1)S(1)}, bf16[16,7296]{1,0:T(8,128)(2,1)S(1)}, u32[]{:S(2)}, u32[]{:S(2)}) %collective-permute-start.3) | collective-permute-done | bytes 233504 | tf_op jit(solution)/shard_map/ppermute | solution.py:52
  35.5 2.6 %collective-permute-done.7.refs_6_ = bf16[16,7296]{1,0:T(8,128)(2,1)} collective-permute-done((bf16[16,7296]{1,0:T(8,128)(2,1)S(1)}, bf16[16,7296]{1,0:T(8,128)(2,1)}, u32[]{:S(2)}, u32[]{:S(2)}) %collective-permute-start.7) | collective-permute-done | bytes 233504 | tf_op jit(solution)/shard_map/ppermute | solution.py:52
  38.6 1.8 %fusion.3 = f32[2,64,512]{2,1,0:T(8,128)} fusion(f32[2,64,512]{2,1,0:T(8,128)S(1)} %fusion.12, bf16[2,64,64]{2,1,0:T(8,128)(2,1)} %param.18, bf16[2,64,512]{2,1,0:T(8,128)(2,1)} %param.20, pred[2,512]{1,0:T(4,128)(4,1)S(1)} %iota_compare_fusion), kind=kOutput, calls=%fused_computation.4 | convolution fusion | flops 8585216 | bytes 672768 | tf_op jit(solution)/shard_map/rhp,rpj->rhj/dot_general | solution.py:24
  40.4 1.4 %fusion.11 = f32[2,64]{1,0:T(2,128)S(1)} fusion(f32[2,64,512]{2,1,0:T(8,128)} %fusion.3, pred[2,512]{1,0:T(4,128)(4,1)S(1)} %iota_compare_fusion), kind=kOutput, calls=%fused_computation.35 | output fusion | flops 197119 | bytes 263680 | tf_op jit(solution)/shard_map/sub | solution.py:29
  41.9 3.1 %copy-done.1 = bf16[1,7168,512]{2,1,0:T(8,128)(2,1)S(1)} copy-done((bf16[1,7168,512]{2,1,0:T(8,128)(2,1)S(1)}, bf16[1,7168,512]{2,1,0:T(8,128)(2,1)}, u32[]{:S(2)}) %copy-start.1) | copy-done | bytes 7340056
  48.8 10.1 %expert.1 = (bf16[256,512]{1,0:T(8,128)(2,1)S(1)}, f32[256,128]{1,0:T(8,128)S(1)}, bf16[32,4096]{1,0:T(8,128)(2,1)S(1)}, bf16[32,4096]{1,0:T(8,128)(2,1)S(1)}, b...) custom-call(s32[1]{0:T(128)} %bitcast.node_ref, ...), custom_call_target="tpu_custom_call" | custom-call | flops 4831838208 | bytes 18874368 | tf_op jit(solution)/shard_map/expert/pallas_call | solution.py:198
  59.0 1.7 %down.1 = (bf16[32,3072]{1,0:T(8,128)(2,1)S(1)}, bf16[32,3072]{1,0:T(8,128)(2,1)S(1)}, bf16[32,3072]{1,0:T(8,128)(2,1)S(1)}, bf16[32,3072]{1,0:T(8,128)(2,1)S(1)...) custom-call(bf16[256,512]{1,0:T(8,128)(2,1)S(1)} %get-tuple-element.22.hidden_ref, ...), custom_call_target="tpu_custom_call" | custom-call | flops 805306368 | bytes 4718592 | tf_op jit(solution)/shard_map/down/pallas_call | solution.py:242
  61.6 2.0 %convolution_convert_fusion = bf16[2,64,512]{2,1,0:T(8,128)(2,1)} fusion(bf16[2,512,512]{2,1,0:T(8,128)(2,1)S(1)} %copy-done, f32[2,64]{1,0:T(2,128)S(1)} %fusion.11, f32[2,64,512]{2,1,0:T(8,128)} %fusion.3, pred[2,512]{1,0:T(4,128)(4,1)S(1)} %iota_compare_fusion), kind=kOutput, calls=%fused_computation.7 | convolution fusion | flops 67437184 | bytes 1443328 | tf_op jit(solution)/shard_map/rhj,rjc->rhc/dot_general | solution.py:31
  66.9 3.5 %collective-permute-done.28 = bf16[32,3072]{1,0:T(8,128)(2,1)S(1)} collective-permute-done((bf16[32,3072]{1,0:T(8,128)(2,1)S(1)}, bf16[32,3072]{1,0:T(8,128)(2,1)S(1)}, u32[]{:S(2)}, u32[]{:S(2)}) %collective-permute-start.28) | collective-permute-done | bytes 196640 | tf_op jit(solution)/shard_map/ppermute | solution.py:52
  71.4 1.5 %collective-permute-start.29 = (bf16[32,3072]{1,0:T(8,128)(2,1)S(1)}, bf16[32,3072]{1,0:T(8,128)(2,1)S(1)}, u32[]{:S(2)}, u32[]{:S(2)}) collective-permute-start(bf16[32,3072]{1,0:T(8,128)(2,1)S(1)} %get-tuple-element.33), channel_id=1, source_target_pairs={{0,1},{1,0},{2,6},{3,7},{4,5},{5,4},{6,2},{7,3},{8,9},{9,8},{10,14... | collective-permute-start | bytes 589832 | tf_op jit(solution)/shard_map/ppermute | solution.py:52
  74.3 1.9 %collective-permute-start.21 = (bf16[32,4096]{1,0:T(8,128)(2,1)S(1)}, bf16[32,4096]{1,0:T(8,128)(2,1)S(1)}, u32[]{:S(2)}, u32[]{:S(2)}) collective-permute-start(bf16[32,4096]{1,0:T(8,128)(2,1)S(1)} %get-tuple-element.31), channel_id=1, source_target_pairs={{0,1},{1,0},{2,6},{3,7},{4,5},{5,4},{6,2},{7,3},{8,9},{9,8},{10,14... | collective-permute-start | bytes 786440 | tf_op jit(solution)/shard_map/ppermute | solution.py:52
  76.2 2.2 %collective-permute-done.26 = bf16[32,3072]{1,0:T(8,128)(2,1)S(1)} collective-permute-done((bf16[32,3072]{1,0:T(8,128)(2,1)S(1)}, bf16[32,3072]{1,0:T(8,128)(2,1)S(1)}, u32[]{:S(2)}, u32[]{:S(2)}) %collective-permute-start.26) | collective-permute-done | bytes 196640 | tf_op jit(solution)/shard_map/ppermute | solution.py:52
  79.0 1.8 %collective-permute-start.30 = (bf16[8,3072]{1,0:T(8,128)(2,1)S(1)}, bf16[8,3072]{1,0:T(8,128)(2,1)S(1)}, u32[]{:S(2)}, u32[]{:S(2)}) collective-permute-start(bf16[8,3072]{1,0:T(8,128)(2,1)S(1)} %get-tuple-element.37), channel_id=1, source_target_pairs={{0,8},{1,9},{2,10},{3,11},{4,12},{5,13},{6,14},{7,15},{8,0},{9,1},... | collective-permute-start | bytes 147464 | tf_op jit(solution)/shard_map/ppermute | solution.py:52
  80.9 1.9 %collective-permute-start.31 = (bf16[8,3072]{1,0:T(8,128)(2,1)S(1)}, bf16[8,3072]{1,0:T(8,128)(2,1)S(1)}, u32[]{:S(2)}, u32[]{:S(2)}) collective-permute-start(bf16[8,3072]{1,0:T(8,128)(2,1)S(1)} %get-tuple-element.39), channel_id=1, source_target_pairs={{0,16},{1,17},{2,18},{3,19},{4,20},{5,21},{6,22},{7,23},{8,24},{9,... | collective-permute-start | bytes 147464 | tf_op jit(solution)/shard_map/ppermute | solution.py:52
  82.8 1.4 %collective-permute-start.32 = (bf16[8,3072]{1,0:T(8,128)(2,1)S(1)}, bf16[8,3072]{1,0:T(8,128)(2,1)S(1)}, u32[]{:S(2)}, u32[]{:S(2)}) collective-permute-start(bf16[8,3072]{1,0:T(8,128)(2,1)S(1)} %get-tuple-element.38), channel_id=1, source_target_pairs={{0,24},{1,25},{2,26},{3,27},{4,28},{5,29},{6,30},{7,31},{8,16},{9,... | collective-permute-start | bytes 147464 | tf_op jit(solution)/shard_map/ppermute | solution.py:52
  85.0 2.4 %collective-permute-start.23 = (bf16[8,4096]{1,0:T(8,128)(2,1)S(1)}, bf16[8,4096]{1,0:T(8,128)(2,1)S(1)}, u32[]{:S(2)}, u32[]{:S(2)}) collective-permute-start(bf16[8,4096]{1,0:T(8,128)(2,1)S(1)} %get-tuple-element.36), channel_id=1, source_target_pairs={{0,16},{1,17},{2,18},{3,19},{4,20},{5,21},{6,22},{7,23},{8,24},{9,... | collective-permute-start | bytes 196616 | tf_op jit(solution)/shard_map/ppermute | solution.py:52
  87.4 1.4 %collective-permute-start.24 = (bf16[8,4096]{1,0:T(8,128)(2,1)S(1)}, bf16[8,4096]{1,0:T(8,128)(2,1)S(1)}, u32[]{:S(2)}, u32[]{:S(2)}) collective-permute-start(bf16[8,4096]{1,0:T(8,128)(2,1)S(1)} %get-tuple-element.35), channel_id=1, source_target_pairs={{0,24},{1,25},{2,26},{3,27},{4,28},{5,29},{6,30},{7,31},{8,16},{9,... | collective-permute-start | bytes 196616 | tf_op jit(solution)/shard_map/ppermute | solution.py:52
  89.6 3.2 %collective-permute-done.23 = bf16[8,4096]{1,0:T(8,128)(2,1)S(1)} collective-permute-done((bf16[8,4096]{1,0:T(8,128)(2,1)S(1)}, bf16[8,4096]{1,0:T(8,128)(2,1)S(1)}, u32[]{:S(2)}, u32[]{:S(2)}) %collective-permute-start.23) | collective-permute-done | bytes 65568 | tf_op jit(solution)/shard_map/ppermute | solution.py:52
  (95 shorter events, 23.5 us)
Async XLA Ops:
  2.5 13.3 %collective-permute-start.1 = (bf16[8,7296]{1,0:T(8,128)(2,1)}, bf16[8,7296]{1,0:T(8,128)(2,1)S(1)}, u32[]{:S(2)}, u32[]{:S(2)}) collective-permute-start(bf16[8,7296]{1,0:T(8,128)(2,1)} %pack.1), channel_id=1, source_target_pairs={{0,16},{1,17},{2,18},{3,19},{4,20},{5,21},{6,22},{7,23},{8,24},{9,... | collective-permute-start | bytes 350216 | tf_op jit(solution)/shard_map/ppermute | solution.py:52
  6.5 9.3 %collective-permute-start.2 = (bf16[8,7296]{1,0:T(8,128)(2,1)}, bf16[8,7296]{1,0:T(8,128)(2,1)S(1)}, u32[]{:S(2)}, u32[]{:S(2)}) collective-permute-start(bf16[8,7296]{1,0:T(8,128)(2,1)} %pack.1), channel_id=1, source_target_pairs={{0,24},{1,25},{2,26},{3,27},{4,28},{5,29},{6,30},{7,31},{8,16},{9,... | collective-permute-start | bytes 350216 | tf_op jit(solution)/shard_map/ppermute | solution.py:52
  7.9 9.9 %collective-permute-start = (bf16[8,7296]{1,0:T(8,128)(2,1)}, bf16[8,7296]{1,0:T(8,128)(2,1)S(1)}, u32[]{:S(2)}, u32[]{:S(2)}) collective-permute-start(bf16[8,7296]{1,0:T(8,128)(2,1)} %pack.1), channel_id=1, source_target_pairs={{0,8},{1,9},{2,10},{3,11},{4,12},{5,13},{6,14},{7,15},{8,0},{9,1},... | collective-permute-start | bytes 350216 | tf_op jit(solution)/shard_map/ppermute | solution.py:52
  15.8 8.6 %collective-permute-start.4 = (bf16[16,7296]{1,0:T(8,128)(2,1)S(1)}, bf16[16,7296]{1,0:T(8,128)(2,1)S(1)}, u32[]{:S(2)}, u32[]{:S(2)}) collective-permute-start(bf16[16,7296]{1,0:T(8,128)(2,1)S(1)} %constant_dynamic-update-slice_fusion.refs_1_), channel_id=1, source_target_pairs={{0,1},{1,0},{2,6},{3,7},{4,5},{5,4},{6,2},{7,3},{8,9},{9,8},{10,14... | collective-permute-start | bytes 700424 | tf_op jit(solution)/shard_map/ppermute | solution.py:52
  18.7 10.8 %collective-permute-start.3 = (bf16[16,7296]{1,0:T(8,128)(2,1)S(1)}, bf16[16,7296]{1,0:T(8,128)(2,1)S(1)}, u32[]{:S(2)}, u32[]{:S(2)}) collective-permute-start(bf16[16,7296]{1,0:T(8,128)(2,1)S(1)} %pad_maximum_fusion.refs_0_), channel_id=1, source_target_pairs={{0,1},{1,0},{2,6},{3,7},{4,5},{5,4},{6,2},{7,3},{8,9},{9,8},{10,14... | collective-permute-start | bytes 700424 | tf_op jit(solution)/shard_map/ppermute | solution.py:52
  18.9 11.3 %collective-permute-start.6 = (bf16[16,7296]{1,0:T(8,128)(2,1)S(1)}, bf16[16,7296]{1,0:T(8,128)(2,1)S(1)}, u32[]{:S(2)}, u32[]{:S(2)}) collective-permute-start(bf16[16,7296]{1,0:T(8,128)(2,1)S(1)} %constant_dynamic-update-slice_fusion.refs_1_), channel_id=1, source_target_pairs={{0,4},{1,5},{2,3},{3,2},{4,0},{5,1},{6,7},{7,6},{8,12},{9,13},{10,... | collective-permute-start | bytes 700424 | tf_op jit(solution)/shard_map/ppermute | solution.py:52
  20.8 9.5 %collective-permute-start.5 = (bf16[16,7296]{1,0:T(8,128)(2,1)S(1)}, bf16[16,7296]{1,0:T(8,128)(2,1)S(1)}, u32[]{:S(2)}, u32[]{:S(2)}) collective-permute-start(bf16[16,7296]{1,0:T(8,128)(2,1)S(1)} %pad_maximum_fusion.refs_0_), channel_id=1, source_target_pairs={{0,4},{1,5},{2,3},{3,2},{4,0},{5,1},{6,7},{7,6},{8,12},{9,13},{10,... | collective-permute-start | bytes 700424 | tf_op jit(solution)/shard_map/ppermute | solution.py:52
  21.0 12.7 %collective-permute-start.12 = (bf16[16,7296]{1,0:T(8,128)(2,1)S(1)}, bf16[16,7296]{1,0:T(8,128)(2,1)S(1)}, u32[]{:S(2)}, u32[]{:S(2)}) collective-permute-start(bf16[16,7296]{1,0:T(8,128)(2,1)S(1)} %constant_dynamic-update-slice_fusion.refs_1_), channel_id=1, source_target_pairs={{0,2},{1,3},{2,0},{3,1},{4,6},{5,7},{6,4},{7,5},{8,10},{9,11},{10,... | collective-permute-start | bytes 700424 | tf_op jit(solution)/shard_map/ppermute | solution.py:52
  24.4 9.7 %collective-permute-start.11 = (bf16[16,7296]{1,0:T(8,128)(2,1)S(1)}, bf16[16,7296]{1,0:T(8,128)(2,1)S(1)}, u32[]{:S(2)}, u32[]{:S(2)}) collective-permute-start(bf16[16,7296]{1,0:T(8,128)(2,1)S(1)} %pad_maximum_fusion.refs_0_), channel_id=1, source_target_pairs={{0,2},{1,3},{2,0},{3,1},{4,6},{5,7},{6,4},{7,5},{8,10},{9,11},{10,... | collective-permute-start | bytes 700424 | tf_op jit(solution)/shard_map/ppermute | solution.py:52
  30.3 7.8 %collective-permute-start.14 = (bf16[16,7296]{1,0:T(8,128)(2,1)S(1)}, bf16[16,7296]{1,0:T(8,128)(2,1)S(1)}, u32[]{:S(2)}, u32[]{:S(2)}) collective-permute-start(bf16[16,7296]{1,0:T(8,128)(2,1)S(1)} %collective-permute-done.4.refs_3_), channel_id=1, source_target_pairs={{0,2},{1,3},{2,0},{3,1},{4,6},{5,7},{6,4},{7,5},{8,10},{9,11},{10,... | collective-permute-start | bytes 700424 | tf_op jit(solution)/shard_map/ppermute | solution.py:52
  30.3 7.8 %collective-permute-start.7 = (bf16[16,7296]{1,0:T(8,128)(2,1)S(1)}, bf16[16,7296]{1,0:T(8,128)(2,1)}, u32[]{:S(2)}, u32[]{:S(2)}) collective-permute-start(bf16[16,7296]{1,0:T(8,128)(2,1)S(1)} %collective-permute-done.3.refs_2_), channel_id=1, source_target_pairs={{0,4},{1,5},{2,3},{3,2},{4,0},{5,1},{6,7},{7,6},{8,12},{9,13},{10,... | collective-permute-start | bytes 700424 | tf_op jit(solution)/shard_map/ppermute | solution.py:52
  33.6 8.2 %collective-permute-start.13 = (bf16[16,7296]{1,0:T(8,128)(2,1)S(1)}, bf16[16,7296]{1,0:T(8,128)(2,1)}, u32[]{:S(2)}, u32[]{:S(2)}) collective-permute-start(bf16[16,7296]{1,0:T(8,128)(2,1)S(1)} %collective-permute-done.3.refs_2_), channel_id=1, source_target_pairs={{0,2},{1,3},{2,0},{3,1},{4,6},{5,7},{6,4},{7,5},{8,10},{9,11},{10,... | collective-permute-start | bytes 700424 | tf_op jit(solution)/shard_map/ppermute | solution.py:52
  34.2 7.7 %collective-permute-start.16 = (bf16[16,7296]{1,0:T(8,128)(2,1)S(1)}, bf16[16,7296]{1,0:T(8,128)(2,1)}, u32[]{:S(2)}, u32[]{:S(2)}) collective-permute-start(bf16[16,7296]{1,0:T(8,128)(2,1)S(1)} %collective-permute-done.6.refs_5_), channel_id=1, source_target_pairs={{0,2},{1,3},{2,0},{3,1},{4,6},{5,7},{6,4},{7,5},{8,10},{9,11},{10,... | collective-permute-start | bytes 700424 | tf_op jit(solution)/shard_map/ppermute | solution.py:52
  35.5 6.3 %collective-permute-start.15 = (bf16[16,7296]{1,0:T(8,128)(2,1)S(1)}, bf16[16,7296]{1,0:T(8,128)(2,1)}, u32[]{:S(2)}, u32[]{:S(2)}) collective-permute-start(bf16[16,7296]{1,0:T(8,128)(2,1)S(1)} %collective-permute-done.5.refs_4_), channel_id=1, source_target_pairs={{0,2},{1,3},{2,0},{3,1},{4,6},{5,7},{6,4},{7,5},{8,10},{9,11},{10,... | collective-permute-start | bytes 700424 | tf_op jit(solution)/shard_map/ppermute | solution.py:52
  64.1 9.3 %collective-permute-start.17 = (bf16[96,4096]{1,0:T(8,128)(2,1)}, bf16[96,4096]{1,0:T(8,128)(2,1)S(1)}, u32[]{:S(2)}, u32[]{:S(2)}) collective-permute-start(bf16[96,4096]{1,0:T(8,128)(2,1)} %copy-done.10), channel_id=1, source_target_pairs={{0,2},{1,3},{2,0},{3,1},{4,6},{5,7},{6,4},{7,5},{8,10},{9,11},{10,... | collective-permute-start | bytes 2359304 | tf_op jit(solution)/shard_map/ppermute | solution.py:52
  65.6 7.7 %collective-permute-start.20 = (bf16[32,4096]{1,0:T(8,128)(2,1)S(1)}, bf16[32,4096]{1,0:T(8,128)(2,1)S(1)}, u32[]{:S(2)}, u32[]{:S(2)}) collective-permute-start(bf16[32,4096]{1,0:T(8,128)(2,1)S(1)} %add_convert_fusion.2), channel_id=1, source_target_pairs={{0,4},{1,5},{2,3},{3,2},{4,0},{5,1},{6,7},{7,6},{8,12},{9,13},{10,... | collective-permute-start | bytes 786440 | tf_op jit(solution)/shard_map/ppermute | solution.py:52
  70.5 7.9 %collective-permute-start.26 = (bf16[32,3072]{1,0:T(8,128)(2,1)S(1)}, bf16[32,3072]{1,0:T(8,128)(2,1)S(1)}, u32[]{:S(2)}, u32[]{:S(2)}) collective-permute-start(bf16[32,3072]{1,0:T(8,128)(2,1)S(1)} %get-tuple-element.32), channel_id=1, source_target_pairs={{0,4},{1,5},{2,3},{3,2},{4,0},{5,1},{6,7},{7,6},{8,12},{9,13},{10,... | collective-permute-start | bytes 589832 | tf_op jit(solution)/shard_map/ppermute | solution.py:52
  71.4 7.5 %collective-permute-start.29 = (bf16[32,3072]{1,0:T(8,128)(2,1)S(1)}, bf16[32,3072]{1,0:T(8,128)(2,1)S(1)}, u32[]{:S(2)}, u32[]{:S(2)}) collective-permute-start(bf16[32,3072]{1,0:T(8,128)(2,1)S(1)} %get-tuple-element.33), channel_id=1, source_target_pairs={{0,1},{1,0},{2,6},{3,7},{4,5},{5,4},{6,2},{7,3},{8,9},{9,8},{10,14... | collective-permute-start | bytes 589832 | tf_op jit(solution)/shard_map/ppermute | solution.py:52
  73.5 10.7 %collective-permute-start.18 = (bf16[32,4096]{1,0:T(8,128)(2,1)S(1)}, bf16[32,4096]{1,0:T(8,128)(2,1)S(1)}, u32[]{:S(2)}, u32[]{:S(2)}) collective-permute-start(bf16[32,4096]{1,0:T(8,128)(2,1)S(1)} %get-tuple-element.30), channel_id=1, source_target_pairs={{0,4},{1,5},{2,3},{3,2},{4,0},{5,1},{6,7},{7,6},{8,12},{9,13},{10,... | collective-permute-start | bytes 786440 | tf_op jit(solution)/shard_map/ppermute | solution.py:52
  74.3 9.9 %collective-permute-start.21 = (bf16[32,4096]{1,0:T(8,128)(2,1)S(1)}, bf16[32,4096]{1,0:T(8,128)(2,1)S(1)}, u32[]{:S(2)}, u32[]{:S(2)}) collective-permute-start(bf16[32,4096]{1,0:T(8,128)(2,1)S(1)} %get-tuple-element.31), channel_id=1, source_target_pairs={{0,1},{1,0},{2,6},{3,7},{4,5},{5,4},{6,2},{7,3},{8,9},{9,8},{10,14... | collective-permute-start | bytes 786440 | tf_op jit(solution)/shard_map/ppermute | solution.py:52
  79.0 8.4 %collective-permute-start.30 = (bf16[8,3072]{1,0:T(8,128)(2,1)S(1)}, bf16[8,3072]{1,0:T(8,128)(2,1)S(1)}, u32[]{:S(2)}, u32[]{:S(2)}) collective-permute-start(bf16[8,3072]{1,0:T(8,128)(2,1)S(1)} %get-tuple-element.37), channel_id=1, source_target_pairs={{0,8},{1,9},{2,10},{3,11},{4,12},{5,13},{6,14},{7,15},{8,0},{9,1},... | collective-permute-start | bytes 147464 | tf_op jit(solution)/shard_map/ppermute | solution.py:52
  80.9 7.9 %collective-permute-start.31 = (bf16[8,3072]{1,0:T(8,128)(2,1)S(1)}, bf16[8,3072]{1,0:T(8,128)(2,1)S(1)}, u32[]{:S(2)}, u32[]{:S(2)}) collective-permute-start(bf16[8,3072]{1,0:T(8,128)(2,1)S(1)} %get-tuple-element.39), channel_id=1, source_target_pairs={{0,16},{1,17},{2,18},{3,19},{4,20},{5,21},{6,22},{7,23},{8,24},{9,... | collective-permute-start | bytes 147464 | tf_op jit(solution)/shard_map/ppermute | solution.py:52
  82.8 6.4 %collective-permute-start.32 = (bf16[8,3072]{1,0:T(8,128)(2,1)S(1)}, bf16[8,3072]{1,0:T(8,128)(2,1)S(1)}, u32[]{:S(2)}, u32[]{:S(2)}) collective-permute-start(bf16[8,3072]{1,0:T(8,128)(2,1)S(1)} %get-tuple-element.38), channel_id=1, source_target_pairs={{0,24},{1,25},{2,26},{3,27},{4,28},{5,29},{6,30},{7,31},{8,16},{9,... | collective-permute-start | bytes 147464 | tf_op jit(solution)/shard_map/ppermute | solution.py:52
  85.0 7.8 %collective-permute-start.23 = (bf16[8,4096]{1,0:T(8,128)(2,1)S(1)}, bf16[8,4096]{1,0:T(8,128)(2,1)S(1)}, u32[]{:S(2)}, u32[]{:S(2)}) collective-permute-start(bf16[8,4096]{1,0:T(8,128)(2,1)S(1)} %get-tuple-element.36), channel_id=1, source_target_pairs={{0,16},{1,17},{2,18},{3,19},{4,20},{5,21},{6,22},{7,23},{8,24},{9,... | collective-permute-start | bytes 196616 | tf_op jit(solution)/shard_map/ppermute | solution.py:52
  (24 other events, 139.7 us)

commit v5 on v4

v5 whole, which is shorter than its diff:
```python
import functools

import jax
import jax.numpy as jnp
import numpy as np
from jax import lax
from jax.experimental import pallas as pl
from jax.experimental.pallas import tpu as pltpu
from jax.sharding import Mesh
from jax.sharding import PartitionSpec as P

score_scale = 192.0 ** (-0.5)
everyone = ("high", "middle", "core", "local")
MEBI = 1024 * 1024


def attention_kernel(lengths_ref, query_ref, query_rope_ref, cache_ref, cache_rope_ref, out_ref):
    for row in range(query_ref.shape[0]):
        cache = cache_ref[row]
        scores = lax.dot_general(
            query_ref[row], cache, (((1,), (1,)), ((), ())), preferred_element_type=jnp.float32
        )
        scores += jnp.dot(
            query_rope_ref[row], cache_rope_ref[row], preferred_element_type=jnp.float32
        )
        slot = lax.broadcasted_iota(jnp.int32, scores.shape, 1)
        in_range = slot < lengths_ref[row]
        scores = jnp.where(in_range, scores * score_scale, -jnp.inf)
        row_peak = jnp.max(scores, axis=1, keepdims=True)
        lifted = jnp.where(in_range, jnp.exp(scores - row_peak), 0.0)
        weights = (lifted / jnp.sum(lifted, axis=1, keepdims=True)).astype(jnp.bfloat16)
        value = jnp.dot(weights, cache, preferred_element_type=jnp.float32)
        out_ref[row] = value.astype(jnp.bfloat16)


def attention(query_latent, query_rope, cache_latent, cache_rope, cache_lengths):
    rows, heads, latent = query_latent.shape
    slots = cache_latent.shape[1]
    return pl.pallas_call(
        attention_kernel,
        in_specs=[pl.BlockSpec(memory_space=pltpu.SMEM)]
        + [pl.BlockSpec(memory_space=pltpu.VMEM)] * 4,
        out_specs=pl.BlockSpec(memory_space=pltpu.VMEM),
        out_shape=jax.ShapeDtypeStruct(query_latent.shape, jnp.bfloat16),
        cost_estimate=pl.CostEstimate(
            flops=4 * rows * heads * slots * latent,
            bytes_accessed=2 * rows * slots * latent,
            transcendentals=rows * heads * slots,
        ),
        compiler_params=pltpu.CompilerParams(vmem_limit_bytes=8 * MEBI),
        name="attention",
    )(cache_lengths, query_latent, query_rope, cache_latent, cache_rope)


class Grid:
    def __init__(self):
        self.sizes = tuple(lax.axis_size(name) for name in everyone)
        self.mixed = self.sizes[1] == self.sizes[3]

    def swap(self, value, pick, mask):
        pairs = []
        for place in np.ndindex(*self.sizes):
            other = list(place)
            other[pick(place[2])] ^= mask
            pairs.append(
                (
                    int(np.ravel_multi_index(place, self.sizes)),
                    int(np.ravel_multi_index(other, self.sizes)),
                )
            )
        return lax.ppermute(value, everyone, pairs)

    def high(self, core):
        return 0

    def core(self, core):
        return 2

    def first(self, core):
        return 1 if self.mixed and core == 1 else 3

    def second(self, core):
        return 3 if self.mixed and core == 1 else 1

    def extent(self, pick):
        return self.sizes[pick(0)]

    def gather(self, rows, weights):
        weights = list(weights)
        lines = [rows] + [self.swap(rows, self.high, m) for m in range(1, self.extent(self.high))]
        half = len(lines) // 2
        places = []
        for lines in (lines[:half], lines[half:]):
            line = jnp.concatenate(lines, axis=0)
            if places:
                line, places[0][1], weights[0] = lax.optimization_barrier(
                    (line, places[0][1], weights[0])
                )
            near = [line]
            near += [self.swap(line, self.first, m) for m in range(1, self.extent(self.first))]
            if places:
                near[-1], weights[1] = lax.optimization_barrier((near[-1], weights[1]))
            mine = list(near)
            for m in range(1, self.extent(self.second)):
                mine += [self.swap(block, self.second, m) for block in near]
            if places:
                mine[-1], weights[2] = lax.optimization_barrier((mine[-1], weights[2]))
            places.append(mine + [self.swap(block, self.core, 1) for block in mine])
        return [list(blocks) for blocks in zip(*places)], weights

    def last_sum(self, mine, other):
        return add([mine[-1], self.swap(other[0], self.core, 1)])

    def scatter_sum(self, mine, other, last):
        size = mine[0].shape[0]
        rest = self.swap(other[1], self.core, 1)
        sums = [last]
        for i in range(len(mine) - 1):
            sums.insert(i, add([mine[i], rest[i * size : (i + 1) * size]]))
        wide = self.extent(self.first)
        near = []
        for i in range(wide):
            parts = [sums[i]]
            for m in range(1, self.extent(self.second)):
                parts.append(self.swap(sums[m * wide + i], self.second, m))
            near.append(parts)
        near = [add(parts) for parts in near]
        line = add([near[0]] + [self.swap(near[m], self.first, m) for m in range(1, wide)])
        rows = size // self.extent(self.high)
        parts = [line[:rows]]
        for m in range(1, self.extent(self.high)):
            parts.append(self.swap(line[m * rows : (m + 1) * rows], self.high, m))
        return add(parts)


def add(parts):
    total = parts[0].astype(jnp.float32)
    for part in parts[1:]:
        total = total + part.astype(jnp.float32)
    return total.astype(parts[0].dtype)


def pack_kernel(experts, rows_ref, ids_ref, gates_ref, out_ref):
    width = rows_ref.shape[1]
    extra = out_ref.shape[1] - width
    gates = gates_ref[...]
    shares = 2.5 * gates / jnp.sum(gates, axis=1, keepdims=True)
    ids = ids_ref[...]
    lane = lax.broadcasted_iota(jnp.int32, (ids.shape[0], extra), 1)
    expert = jnp.where(lane < experts, lane, lane - experts)
    table = jnp.zeros(lane.shape, jnp.float32)
    for k in range(ids.shape[1]):
        table += jnp.where(expert == ids[:, k : k + 1], shares[:, k : k + 1], 0.0)
    high = table.astype(jnp.bfloat16).astype(jnp.float32)
    table = jnp.where(lane < experts, high, jnp.where(lane < 2 * experts, table - high, 0.0))
    out_ref[:, :width] = rows_ref[...]
    out_ref[:, width:] = table.astype(jnp.bfloat16)


def pack(experts, moe_rows, route_ids, route_gates):
    rows, width = moe_rows.shape
    total = width + pl.cdiv(2 * experts, 128) * 128
    return pl.pallas_call(
        functools.partial(pack_kernel, experts),
        out_shape=jax.ShapeDtypeStruct((rows, total), jnp.bfloat16),
        name="pack",
    )(moe_rows, route_ids, route_gates)


def spread(product, outs):
    start = 0
    for out, columns in outs:
        size = out.shape[0]
        out[:, columns] = product[start : start + size]
        start += size


def bring_kernel(source, target, sems):
    rows = source.shape[0] // sems.shape[0]
    copies = []
    for k in range(sems.shape[0]):
        part = pl.ds(k * rows, rows)
        copies.append(pltpu.make_async_copy(source.at[part], target.at[part], sems.at[k]))
    for copy in copies:
        copy.start()
    for copy in copies:
        copy.wait()


def bring(weight, name):
    return pl.pallas_call(
        bring_kernel,
        in_specs=[pl.BlockSpec(memory_space=pltpu.HBM)],
        out_specs=pl.BlockSpec(memory_space=pltpu.VMEM),
        out_shape=pltpu.VMEM(weight.shape, weight.dtype),
        scratch_shapes=[pltpu.SemaphoreType.DMA((4,))],
        cost_estimate=pl.CostEstimate(
            flops=0, bytes_accessed=2 * weight.size, transcendentals=0
        ),
        compiler_params=pltpu.CompilerParams(vmem_limit_bytes=MEBI),
        name=name,
    )(pltpu.with_memory_space_constraint(weight, pltpu.HBM))


def expert_kernel(count, experts, tile, down_tile, node_ref, *refs):
    blocks = refs[:count]
    gate, up, down, hidden_ref, share_ref = refs[count : count + 5]
    outs = refs[count + 5 : -2]
    gate_sum, up_sum = refs[-2:]
    width = gate.shape[0]
    columns = outs[0].shape[1]

    table = jnp.concatenate([block[:, width:] for block in blocks], axis=0).astype(jnp.float32)
    lane = lax.broadcasted_iota(jnp.int32, table.shape, 1)
    mine = (lane == node_ref[0]) | (lane == node_ref[0] + experts)
    share = jnp.sum(jnp.where(mine, table, 0.0), axis=1, keepdims=True)
    share_ref[...] = jnp.broadcast_to(share, share_ref.shape)

    for k in range(0, width, tile):
        part = pl.ds(k, tile)
        rows = jnp.concatenate([block[:, part] for block in blocks], axis=0)
        for weight, total in ((gate, gate_sum), (up, up_sum)):
            product = jnp.dot(rows, weight[part], preferred_element_type=jnp.float32)
            if k == 0:
                total[...] = product
            else:
                total[...] += product
    hidden_ref[...] = (jax.nn.silu(gate_sum[...]) * up_sum[...]).astype(jnp.bfloat16)
    for k in range(0, columns, down_tile):
        part = pl.ds(k, down_tile)
        product = jnp.dot(hidden_ref[...], down[:, part], preferred_element_type=jnp.float32)
        product = (product * share_ref[:, :1]).astype(jnp.bfloat16)
        spread(product, [(out, part) for out in outs])


def expert(blocks, w_gate, w_up, w_down, experts, node, sizes, columns):
    width, units = w_gate.shape
    rows = sum(sizes)
    return pl.pallas_call(
        functools.partial(expert_kernel, len(blocks), experts, 1024, 512),
        in_specs=[pl.BlockSpec(memory_space=pltpu.SMEM)]
        + [pl.BlockSpec(memory_space=pltpu.VMEM)] * (len(blocks) + 3),
        out_specs=[pl.BlockSpec(memory_space=pltpu.VMEM)] * (2 + len(sizes)),
        out_shape=[
            jax.ShapeDtypeStruct((rows, units), jnp.bfloat16),
            jax.ShapeDtypeStruct((rows, 128), jnp.float32),
        ]
        + [jax.ShapeDtypeStruct((size, columns), jnp.bfloat16) for size in sizes],
        scratch_shapes=[pltpu.VMEM((rows, units), jnp.float32)] * 2,
        cost_estimate=pl.CostEstimate(
            flops=4 * rows * width * units + 2 * rows * columns * units,
            bytes_accessed=4 * width * units + 2 * units * columns,
            transcendentals=rows * units,
        ),
        compiler_params=pltpu.CompilerParams(vmem_limit_bytes=8 * MEBI),
        name="expert",
    )(node, *blocks, w_gate, w_up, w_down)


def down_kernel(start, tile, hidden_ref, share_ref, down_ref, *outs):
    for k in range(0, outs[0].shape[1], tile):
        weight = down_ref[:, pl.ds(start + k, tile)]
        product = jnp.dot(hidden_ref[...], weight, preferred_element_type=jnp.float32)
        product = (product * share_ref[:, :1]).astype(jnp.bfloat16)
        spread(product, [(out, pl.ds(k, tile)) for out in outs])


def down_of(hidden, share, w_down, sizes, start):
    rows, units = hidden.shape
    columns = w_down.shape[1] - start
    return pl.pallas_call(
        functools.partial(down_kernel, start, 512),
        in_specs=[pl.BlockSpec(memory_space=pltpu.VMEM)] * 3,
        out_specs=[pl.BlockSpec(memory_space=pltpu.VMEM)] * len(sizes),
        out_shape=[jax.ShapeDtypeStruct((size, columns), jnp.bfloat16) for size in sizes],
        cost_estimate=pl.CostEstimate(
            flops=2 * rows * columns * units,
            bytes_accessed=2 * columns * (units + rows),
            transcendentals=0,
        ),
        compiler_params=pltpu.CompilerParams(vmem_limit_bytes=8 * MEBI),
        name="down",
    )(hidden, share, w_down)


def body(
    moe_rows,
    route_ids,
    route_gates,
    w_gate,
    w_up,
    w_down,
    query_latent,
    query_rope,
    cache_latent,
    cache_rope,
    cache_lengths,
):
    grid = Grid()
    high, middle, cores, _ = grid.sizes
    experts = high * middle * cores
    tokens, width = moe_rows.shape
    node = lax.axis_index(("high", "middle", "core")).astype(jnp.int32).reshape(1)
    weights = bring(w_gate[0], "gate"), bring(w_up[0], "up"), bring(w_down[0], "down_in")
    outgoing = pack(experts, moe_rows, route_ids, route_gates)
    attn_latent = attention(query_latent, query_rope, cache_latent, cache_rope, cache_lengths)
    places, (gate, up, (down, attn_latent)) = grid.gather(
        outgoing, weights[:2] + ((weights[2], attn_latent),)
    )
    size = high * tokens
    count = len(places) // 2
    sizes = [size] * count + [size, size * (count - 1)]
    places = places[:count] + places[-1:] + places[count:-1]
    blocks = [block for place in places for block in place]
    split = width * 4 // 7
    hidden, share, *products = expert(blocks, gate, up, down, experts, node, sizes, split)
    lower, lower_other = products[:count], products[count:]
    last = grid.last_sum(lower, lower_other)
    hidden, last = lax.optimization_barrier((hidden, last))
    products = down_of(hidden, share, down, sizes, split)
    lower = grid.scatter_sum(lower, lower_other, last)
    upper, upper_other = products[:count], products[count:]
    upper = grid.scatter_sum(upper, upper_other, grid.last_sum(upper, upper_other))
    return (jnp.concatenate([lower, upper], axis=1), attn_latent)


def solution(mesh):
    groups, nodes, local = mesh.devices.shape
    split = Mesh(mesh.devices.reshape(groups, nodes // 4, 2, 2, local), ("group",) + everyone)
    node = ("high", "middle", "core")
    whole = ("group",) + everyone
    rows = P(whole, None)
    blocks = P(whole, None, None)
    return jax.shard_map(
        body,
        mesh=split,
        in_specs=(
            rows,
            rows,
            rows,
            P(node, None, "local"),
            P(node, None, "local"),
            P(node, "local", None),
            blocks,
            blocks,
            blocks,
            blocks,
            P(whole),
        ),
        out_specs=(rows, blocks),
        check_vma=False,
    )
```

time: 94.7 us -> 100 us (1.056)
  local copies, waits for them, and re-layouts: 7.74 us -> 18.1 us
  Pallas kernels: 13.7 us -> 20.9 us
  matrix products: 5.19 us -> 0 us
  other arithmetic: 4.39 us -> 1.37 us
  waiting for transfers between devices: 31.5 us -> 29.1 us
  starting transfers between devices: 30.9 us -> 29.6 us
    unnamed x31 -> x24, local copies, waits for them, and re-layouts: 7.69 us -> 18.1 us
    pallas_call x2 -> x6, Pallas kernels: 11.9 us -> 19.2 us  [the longest x3 9.67 us: bring(): pl.pallas_call(bring_kernel, in_specs=[pl.BlockSpec(memory_space=pltpu.HB...]
    dot_general x3 -> x0, matrix products: 5.19 us -> none  [the longest x1 2.05 us: attention(): jnp.einsum('rhj,rjc->rhc', weights, cache_latent, preferred_element_type=...]
    ppermute x33, waiting for transfers between devices: 31.5 us -> 29.1 us  [swap(): return lax.ppermute(value, everyone, pairs)]
    sub x1 -> x0, other arithmetic: 1.38 us -> none  [attention(): lifted = jnp.where(in_range, jnp.exp(scores - row_peak), 0.0)]
    ppermute x33, starting transfers between devices: 30.9 us -> 29.6 us  [swap(): return lax.ppermute(value, everyone, pairs)]
  transfers between devices with their start and end apart: 33 -> 33, of which waited for: 13 -> 17; matrix products, arithmetic and copies ran while one was open for 9% -> 1% of each run, Pallas kernels for 0% -> 12%
where the time goes in v5:
time: 100 us
  starting transfers between devices  29.6 us (30%)
  waiting for transfers between devices  29.1 us (29%)
  Pallas kernels  20.9 us (21%)
  local copies, waits for them, and re-layouts  18.1 us (18%)
  other arithmetic  1.37 us (1%)
    ppermute x33, starting transfers between devices, swap(): return lax.ppermute(value, everyone, pairs)  29.6 us
    ppermute x33, waiting for transfers between devices, swap(): return lax.ppermute(value, everyone, pairs)  29.1 us
    unnamed x24, local copies, waits for them, and re-layouts  18.1 us
    pallas_call x3, Pallas kernels, bring(): pl.pallas_call(bring_kernel, in_specs=[pl.BlockSpec(memory_space=pltpu.HB...  9.67 us
    pallas_call x1, Pallas kernels, expert(): pl.pallas_call(functools.partial(expert_kernel, len(blocks), experts, 102...  6.13 us
    pallas_call x1, Pallas kernels, attention(): pl.pallas_call(attention_kernel, in_specs=[pl.BlockSpec(memory_space=pltp...  2.36 us
  transfers between devices with their start and end apart: 33, of which 17 were waited for; matrix products, arithmetic and copies ran while one was open for 1% of the time, Pallas kernels for 12%

profile of v5, /device:TPU:0, one launch (start us, length us, event | category | flops | bytes accessed | tf_op | source)
XLA Modules:
  0.0 100.0 jit_solution(9375588514703936213)
XLA Ops:
  2.4 3.0 %collective-permute-start = (bf16[8,7296]{1,0:T(8,128)(2,1)}, bf16[8,7296]{1,0:T(8,128)(2,1)S(1)}, u32[]{:S(2)}, u32[]{:S(2)}) collective-permute-start(bf16[8,7296]{1,0:T(8,128)(2,1)} %pack.1), channel_id=1, source_target_pairs={{0,8},{1,9},{2,10},{3,11},{4,12},{5,13},{6,14},{7,15},{8,0},{9,1},... | collective-permute-start | bytes 350216 | tf_op jit(solution)/shard_map/ppermute | solution.py:71
  5.4 2.5 %collective-permute-start.2 = (bf16[8,7296]{1,0:T(8,128)(2,1)}, bf16[8,7296]{1,0:T(8,128)(2,1)S(1)}, u32[]{:S(2)}, u32[]{:S(2)}) collective-permute-start(bf16[8,7296]{1,0:T(8,128)(2,1)} %pack.1), channel_id=1, source_target_pairs={{0,24},{1,25},{2,26},{3,27},{4,28},{5,29},{6,30},{7,31},{8,16},{9,... | collective-permute-start | bytes 350216 | tf_op jit(solution)/shard_map/ppermute | solution.py:71
  8.0 3.2 %gate.1.refs_16_ = bf16[7168,512]{1,0:T(8,128)(2,1)S(1)} custom-call(bf16[7168,512]{1,0:T(8,128)(2,1)} %bitcast.4), custom_call_target="tpu_custom_call" | custom-call | bytes 7340032 | tf_op jit(solution)/shard_map/gate/pallas_call | solution.py:191
  11.2 2.9 %copy-done.2 = bf16[7168,512]{1,0:T(8,128)(2,1)} copy-done((bf16[7168,512]{1,0:T(8,128)(2,1)}, bf16[7168,512]{1,0:T(8,128)(2,1)S(1)}, u32[]{:S(2)}) %copy-start.2) | copy-done | bytes 7340056
  15.7 3.0 %collective-permute-done.1 = bf16[8,7296]{1,0:T(8,128)(2,1)S(1)} collective-permute-done((bf16[8,7296]{1,0:T(8,128)(2,1)}, bf16[8,7296]{1,0:T(8,128)(2,1)S(1)}, u32[]{:S(2)}, u32[]{:S(2)}) %collective-permute-start.1) | collective-permute-done | bytes 116768 | tf_op jit(solution)/shard_map/ppermute | solution.py:71
  23.3 3.2 %up.1.refs_17_ = bf16[7168,512]{1,0:T(8,128)(2,1)S(1)} custom-call(bf16[7168,512]{1,0:T(8,128)(2,1)} %bitcast.5), custom_call_target="tpu_custom_call" | custom-call | bytes 7340032 | tf_op jit(solution)/shard_map/up/pallas_call | solution.py:191
  26.5 3.0 %copy-done.4 = bf16[7168,512]{1,0:T(8,128)(2,1)} copy-done((bf16[7168,512]{1,0:T(8,128)(2,1)}, bf16[7168,512]{1,0:T(8,128)(2,1)S(1)}, u32[]{:S(2)}) %copy-start.4) | copy-done | bytes 7340056
  32.5 3.0 %collective-permute-done.8.refs_7_ = bf16[16,7296]{1,0:T(8,128)(2,1)S(1)} collective-permute-done((bf16[16,7296]{1,0:T(8,128)(2,1)S(1)}, bf16[16,7296]{1,0:T(8,128)(2,1)S(1)}, u32[]{:S(2)}, u32[]{:S(2)}) %collective-permute-start.8) | collective-permute-done | bytes 233504 | tf_op jit(solution)/shard_map/ppermute | solution.py:71
  35.6 3.3 %down_in.1.refs_18_.down_ref = bf16[512,7168]{1,0:T(8,128)(2,1)S(1)} custom-call(bf16[512,7168]{1,0:T(8,128)(2,1)} %bitcast.6), custom_call_target="tpu_custom_call" | custom-call | bytes 7340032 | tf_op jit(solution)/shard_map/down_in/pallas_call | solution.py:191
  38.9 2.9 %copy-done = bf16[512,7168]{1,0:T(8,128)(2,1)} copy-done((bf16[512,7168]{1,0:T(8,128)(2,1)}, bf16[512,7168]{1,0:T(8,128)(2,1)S(1)}, u32[]{:S(2)}) %copy-start) | copy-done | bytes 7340056
  41.9 2.4 %attention.1 = bf16[2,64,512]{2,1,0:T(8,128)(2,1)} custom-call(s32[2]{0:T(128)S(1)} %copy-done.10, bf16[2,64,512]{2,1,0:T(8,128)(2,1)S(1)} %copy-done.7, bf16[2,64,64]{2,1,0:T(8,128)(2,1)S(1)} %copy-done.9, bf16[2,512,512]{2,1,0:T(8,128)(2,1)S(1)} %copy-done.6, bf16[2,64,512]{2,1,0:T(8,128)(2,1)S(1)} %copy-done.8), custom_call_target="tpu_custom_call" | custom-call | flops 134217728 | bytes 1048576 | tf_op jit(solution)/shard_map/attention/pallas_call | solution.py:39
  47.4 3.1 %copy-done.1 = bf16[512,7168]{1,0:T(8,128)(2,1)S(1)} copy-done((bf16[512,7168]{1,0:T(8,128)(2,1)S(1)}, bf16[512,7168]{1,0:T(8,128)(2,1)}, u32[]{:S(2)}) %copy-start.1) | copy-done | bytes 7340056
  50.4 3.1 %copy-done.3 = bf16[7168,512]{1,0:T(8,128)(2,1)S(1)} copy-done((bf16[7168,512]{1,0:T(8,128)(2,1)S(1)}, bf16[7168,512]{1,0:T(8,128)(2,1)}, u32[]{:S(2)}) %copy-start.3) | copy-done | bytes 7340056
  53.5 3.1 %copy-done.5 = bf16[7168,512]{1,0:T(8,128)(2,1)S(1)} copy-done((bf16[7168,512]{1,0:T(8,128)(2,1)S(1)}, bf16[7168,512]{1,0:T(8,128)(2,1)}, u32[]{:S(2)}) %copy-start.5) | copy-done | bytes 7340056
  56.6 6.1 %expert.1 = (bf16[256,512]{1,0:T(8,128)(2,1)S(1)}, f32[256,128]{1,0:T(8,128)S(1)}, bf16[32,4096]{1,0:T(8,128)(2,1)S(1)}, bf16[32,4096]{1,0:T(8,128)(2,1)S(1)}, b...) custom-call(s32[1]{0:T(128)} %bitcast.node_ref, ...), custom_call_target="tpu_custom_call" | custom-call | flops 4831838208 | bytes 18874368 | tf_op jit(solution)/shard_map/expert/pallas_call | solution.py:239
  68.2 4.2 %collective-permute-done.20 = bf16[32,4096]{1,0:T(8,128)(2,1)S(1)} collective-permute-done((bf16[32,4096]{1,0:T(8,128)(2,1)S(1)}, bf16[32,4096]{1,0:T(8,128)(2,1)S(1)}, u32[]{:S(2)}, u32[]{:S(2)}) %collective-permute-start.20) | collective-permute-done | bytes 262176 | tf_op jit(solution)/shard_map/ppermute | solution.py:71
  76.9 5.0 %collective-permute-done.18 = bf16[32,4096]{1,0:T(8,128)(2,1)S(1)} collective-permute-done((bf16[32,4096]{1,0:T(8,128)(2,1)S(1)}, bf16[32,4096]{1,0:T(8,128)(2,1)S(1)}, u32[]{:S(2)}, u32[]{:S(2)}) %collective-permute-start.18) | collective-permute-done | bytes 262176 | tf_op jit(solution)/shard_map/ppermute | solution.py:71
  82.5 2.3 %collective-permute-done.26 = bf16[32,3072]{1,0:T(8,128)(2,1)S(1)} collective-permute-done((bf16[32,3072]{1,0:T(8,128)(2,1)S(1)}, bf16[32,3072]{1,0:T(8,128)(2,1)S(1)}, u32[]{:S(2)}, u32[]{:S(2)}) %collective-permute-start.26) | collective-permute-done | bytes 196640 | tf_op jit(solution)/shard_map/ppermute | solution.py:71
  84.9 1.9 %collective-permute-start.30 = (bf16[8,3072]{1,0:T(8,128)(2,1)S(1)}, bf16[8,3072]{1,0:T(8,128)(2,1)S(1)}, u32[]{:S(2)}, u32[]{:S(2)}) collective-permute-start(bf16[8,3072]{1,0:T(8,128)(2,1)S(1)} %get-tuple-element.57), channel_id=1, source_target_pairs={{0,8},{1,9},{2,10},{3,11},{4,12},{5,13},{6,14},{7,15},{8,0},{9,1},... | collective-permute-start | bytes 147464 | tf_op jit(solution)/shard_map/ppermute | solution.py:71
  86.8 2.5 %collective-permute-start.32 = (bf16[8,3072]{1,0:T(8,128)(2,1)S(1)}, bf16[8,3072]{1,0:T(8,128)(2,1)S(1)}, u32[]{:S(2)}, u32[]{:S(2)}) collective-permute-start(bf16[8,3072]{1,0:T(8,128)(2,1)S(1)} %get-tuple-element.58), channel_id=1, source_target_pairs={{0,24},{1,25},{2,26},{3,27},{4,28},{5,29},{6,30},{7,31},{8,16},{9,... | collective-permute-start | bytes 147464 | tf_op jit(solution)/shard_map/ppermute | solution.py:71
  89.3 2.0 %collective-permute-start.22 = (bf16[8,4096]{1,0:T(8,128)(2,1)S(1)}, bf16[8,4096]{1,0:T(8,128)(2,1)S(1)}, u32[]{:S(2)}, u32[]{:S(2)}) collective-permute-start(bf16[8,4096]{1,0:T(8,128)(2,1)S(1)} %get-tuple-element.54), channel_id=1, source_target_pairs={{0,8},{1,9},{2,10},{3,11},{4,12},{5,13},{6,14},{7,15},{8,0},{9,1},... | collective-permute-start | bytes 196616 | tf_op jit(solution)/shard_map/ppermute | solution.py:71
  91.2 2.5 %collective-permute-start.24 = (bf16[8,4096]{1,0:T(8,128)(2,1)S(1)}, bf16[8,4096]{1,0:T(8,128)(2,1)S(1)}, u32[]{:S(2)}, u32[]{:S(2)}) collective-permute-start(bf16[8,4096]{1,0:T(8,128)(2,1)S(1)} %get-tuple-element.55), channel_id=1, source_target_pairs={{0,24},{1,25},{2,26},{3,27},{4,28},{5,29},{6,30},{7,31},{8,16},{9,... | collective-permute-start | bytes 196616 | tf_op jit(solution)/shard_map/ppermute | solution.py:71
  93.7 2.6 %collective-permute-done.31 = bf16[8,3072]{1,0:T(8,128)(2,1)S(1)} collective-permute-done((bf16[8,3072]{1,0:T(8,128)(2,1)S(1)}, bf16[8,3072]{1,0:T(8,128)(2,1)S(1)}, u32[]{:S(2)}, u32[]{:S(2)}) %collective-permute-start.31) | collective-permute-done | bytes 49184 | tf_op jit(solution)/shard_map/ppermute | solution.py:71
  97.4 1.9 %collective-permute-done.23 = bf16[8,4096]{1,0:T(8,128)(2,1)S(1)} collective-permute-done((bf16[8,4096]{1,0:T(8,128)(2,1)S(1)}, bf16[8,4096]{1,0:T(8,128)(2,1)S(1)}, u32[]{:S(2)}, u32[]{:S(2)}) %collective-permute-start.23) | collective-permute-done | bytes 65568 | tf_op jit(solution)/shard_map/ppermute | solution.py:71
  (86 shorter events, 26.7 us)
Async XLA Ops:
  2.4 11.7 %collective-permute-start = (bf16[8,7296]{1,0:T(8,128)(2,1)}, bf16[8,7296]{1,0:T(8,128)(2,1)S(1)}, u32[]{:S(2)}, u32[]{:S(2)}) collective-permute-start(bf16[8,7296]{1,0:T(8,128)(2,1)} %pack.1), channel_id=1, source_target_pairs={{0,8},{1,9},{2,10},{3,11},{4,12},{5,13},{6,14},{7,15},{8,0},{9,1},... | collective-permute-start | bytes 350216 | tf_op jit(solution)/shard_map/ppermute | solution.py:71
  5.4 10.3 %collective-permute-start.2 = (bf16[8,7296]{1,0:T(8,128)(2,1)}, bf16[8,7296]{1,0:T(8,128)(2,1)S(1)}, u32[]{:S(2)}, u32[]{:S(2)}) collective-permute-start(bf16[8,7296]{1,0:T(8,128)(2,1)} %pack.1), channel_id=1, source_target_pairs={{0,24},{1,25},{2,26},{3,27},{4,28},{5,29},{6,30},{7,31},{8,16},{9,... | collective-permute-start | bytes 350216 | tf_op jit(solution)/shard_map/ppermute | solution.py:71
  7.9 10.8 %collective-permute-start.1 = (bf16[8,7296]{1,0:T(8,128)(2,1)}, bf16[8,7296]{1,0:T(8,128)(2,1)S(1)}, u32[]{:S(2)}, u32[]{:S(2)}) collective-permute-start(bf16[8,7296]{1,0:T(8,128)(2,1)} %pack.1), channel_id=1, source_target_pairs={{0,16},{1,17},{2,18},{3,19},{4,20},{5,21},{6,22},{7,23},{8,24},{9,... | collective-permute-start | bytes 350216 | tf_op jit(solution)/shard_map/ppermute | solution.py:71
  14.1 6.1 %collective-permute-start.3 = (bf16[16,7296]{1,0:T(8,128)(2,1)S(1)}, bf16[16,7296]{1,0:T(8,128)(2,1)S(1)}, u32[]{:S(2)}, u32[]{:S(2)}) collective-permute-start(bf16[16,7296]{1,0:T(8,128)(2,1)S(1)} %pad_maximum_fusion.refs_0_), channel_id=1, source_target_pairs={{0,1},{1,0},{2,6},{3,7},{4,5},{5,4},{6,2},{7,3},{8,9},{9,8},{10,14... | collective-permute-start | bytes 700424 | tf_op jit(solution)/shard_map/ppermute | solution.py:71
  20.3 9.2 %collective-permute-start.4 = (bf16[16,7296]{1,0:T(8,128)(2,1)S(1)}, bf16[16,7296]{1,0:T(8,128)(2,1)S(1)}, u32[]{:S(2)}, u32[]{:S(2)}) collective-permute-start(bf16[16,7296]{1,0:T(8,128)(2,1)S(1)} %pad_maximum_fusion.1.refs_1_), channel_id=1, source_target_pairs={{0,1},{1,0},{2,6},{3,7},{4,5},{5,4},{6,2},{7,3},{8,9},{9,8},{10,14... | collective-permute-start | bytes 700424 | tf_op jit(solution)/shard_map/ppermute | solution.py:71
  21.8 8.2 %collective-permute-start.5 = (bf16[16,7296]{1,0:T(8,128)(2,1)S(1)}, bf16[16,7296]{1,0:T(8,128)(2,1)S(1)}, u32[]{:S(2)}, u32[]{:S(2)}) collective-permute-start(bf16[16,7296]{1,0:T(8,128)(2,1)S(1)} %pad_maximum_fusion.refs_0_), channel_id=1, source_target_pairs={{0,4},{1,5},{2,3},{3,2},{4,0},{5,1},{6,7},{7,6},{8,12},{9,13},{10,... | collective-permute-start | bytes 700424 | tf_op jit(solution)/shard_map/ppermute | solution.py:71
  30.0 14.2 %collective-permute-start.11 = (bf16[16,7296]{1,0:T(8,128)(2,1)S(1)}, bf16[16,7296]{1,0:T(8,128)(2,1)S(1)}, u32[]{:S(2)}, u32[]{:S(2)}) collective-permute-start(bf16[16,7296]{1,0:T(8,128)(2,1)S(1)} %pad_maximum_fusion.refs_0_), channel_id=1, source_target_pairs={{0,2},{1,3},{2,0},{3,1},{4,6},{5,7},{6,4},{7,5},{8,10},{9,11},{10,... | collective-permute-start | bytes 700424 | tf_op jit(solution)/shard_map/ppermute | solution.py:71
  30.0 14.7 %collective-permute-start.15 = (bf16[16,7296]{1,0:T(8,128)(2,1)S(1)}, bf16[16,7296]{1,0:T(8,128)(2,1)S(1)}, u32[]{:S(2)}, u32[]{:S(2)}) collective-permute-start(bf16[16,7296]{1,0:T(8,128)(2,1)S(1)} %collective-permute-done.5.refs_4_), channel_id=1, source_target_pairs={{0,2},{1,3},{2,0},{3,1},{4,6},{5,7},{6,4},{7,5},{8,10},{9,11},{10,... | collective-permute-start | bytes 700424 | tf_op jit(solution)/shard_map/ppermute | solution.py:71
  30.5 14.3 %collective-permute-start.7 = (bf16[16,7296]{1,0:T(8,128)(2,1)S(1)}, bf16[16,7296]{1,0:T(8,128)(2,1)S(1)}, u32[]{:S(2)}, u32[]{:S(2)}) collective-permute-start(bf16[16,7296]{1,0:T(8,128)(2,1)S(1)} %collective-permute-done.3.refs_2_), channel_id=1, source_target_pairs={{0,4},{1,5},{2,3},{3,2},{4,0},{5,1},{6,7},{7,6},{8,12},{9,13},{10,... | collective-permute-start | bytes 700424 | tf_op jit(solution)/shard_map/ppermute | solution.py:71
  32.0 13.2 %collective-permute-start.6 = (bf16[16,7296]{1,0:T(8,128)(2,1)S(1)}, bf16[16,7296]{1,0:T(8,128)(2,1)S(1)}, u32[]{:S(2)}, u32[]{:S(2)}) collective-permute-start(bf16[16,7296]{1,0:T(8,128)(2,1)S(1)} %pad_maximum_fusion.1.refs_1_), channel_id=1, source_target_pairs={{0,4},{1,5},{2,3},{3,2},{4,0},{5,1},{6,7},{7,6},{8,12},{9,13},{10,... | collective-permute-start | bytes 700424 | tf_op jit(solution)/shard_map/ppermute | solution.py:71
  35.5 9.8 %collective-permute-start.13 = (bf16[16,7296]{1,0:T(8,128)(2,1)S(1)}, bf16[16,7296]{1,0:T(8,128)(2,1)S(1)}, u32[]{:S(2)}, u32[]{:S(2)}) collective-permute-start(bf16[16,7296]{1,0:T(8,128)(2,1)S(1)} %collective-permute-done.3.refs_2_), channel_id=1, source_target_pairs={{0,2},{1,3},{2,0},{3,1},{4,6},{5,7},{6,4},{7,5},{8,10},{9,11},{10,... | collective-permute-start | bytes 700424 | tf_op jit(solution)/shard_map/ppermute | solution.py:71
  65.8 6.6 %collective-permute-start.17 = (bf16[96,4096]{1,0:T(8,128)(2,1)S(1)}, bf16[96,4096]{1,0:T(8,128)(2,1)S(1)}, u32[]{:S(2)}, u32[]{:S(2)}) collective-permute-start(bf16[96,4096]{1,0:T(8,128)(2,1)S(1)} %get-tuple-element.34), channel_id=1, source_target_pairs={{0,2},{1,3},{2,0},{3,1},{4,6},{5,7},{6,4},{7,5},{8,10},{9,11},{10,... | collective-permute-start | bytes 2359304 | tf_op jit(solution)/shard_map/ppermute | solution.py:71
  66.0 6.4 %collective-permute-start.20 = (bf16[32,4096]{1,0:T(8,128)(2,1)S(1)}, bf16[32,4096]{1,0:T(8,128)(2,1)S(1)}, u32[]{:S(2)}, u32[]{:S(2)}) collective-permute-start(bf16[32,4096]{1,0:T(8,128)(2,1)S(1)} %add_convert_fusion.2), channel_id=1, source_target_pairs={{0,4},{1,5},{2,3},{3,2},{4,0},{5,1},{6,7},{7,6},{8,12},{9,13},{10,... | collective-permute-start | bytes 786440 | tf_op jit(solution)/shard_map/ppermute | solution.py:71
  66.5 8.0 %collective-permute-start.25 = (bf16[96,3072]{1,0:T(8,128)(2,1)S(1)}, bf16[96,3072]{1,0:T(8,128)(2,1)S(1)}, u32[]{:S(2)}, u32[]{:S(2)}) collective-permute-start(bf16[96,3072]{1,0:T(8,128)(2,1)S(1)} %get-tuple-element.44), channel_id=1, source_target_pairs={{0,2},{1,3},{2,0},{3,1},{4,6},{5,7},{6,4},{7,5},{8,10},{9,11},{10,... | collective-permute-start | bytes 1769480 | tf_op jit(solution)/shard_map/ppermute | solution.py:71
  67.0 7.5 %collective-permute-start.28 = (bf16[32,3072]{1,0:T(8,128)(2,1)S(1)}, bf16[32,3072]{1,0:T(8,128)(2,1)S(1)}, u32[]{:S(2)}, u32[]{:S(2)}) collective-permute-start(bf16[32,3072]{1,0:T(8,128)(2,1)S(1)} %add_convert_fusion.9), channel_id=1, source_target_pairs={{0,4},{1,5},{2,3},{3,2},{4,0},{5,1},{6,7},{7,6},{8,12},{9,13},{10,... | collective-permute-start | bytes 589832 | tf_op jit(solution)/shard_map/ppermute | solution.py:71
  72.6 9.3 %collective-permute-start.18 = (bf16[32,4096]{1,0:T(8,128)(2,1)S(1)}, bf16[32,4096]{1,0:T(8,128)(2,1)S(1)}, u32[]{:S(2)}, u32[]{:S(2)}) collective-permute-start(bf16[32,4096]{1,0:T(8,128)(2,1)S(1)} %get-tuple-element.50), channel_id=1, source_target_pairs={{0,4},{1,5},{2,3},{3,2},{4,0},{5,1},{6,7},{7,6},{8,12},{9,13},{10,... | collective-permute-start | bytes 786440 | tf_op jit(solution)/shard_map/ppermute | solution.py:71
  73.1 9.2 %collective-permute-start.21 = (bf16[32,4096]{1,0:T(8,128)(2,1)S(1)}, bf16[32,4096]{1,0:T(8,128)(2,1)S(1)}, u32[]{:S(2)}, u32[]{:S(2)}) collective-permute-start(bf16[32,4096]{1,0:T(8,128)(2,1)S(1)} %get-tuple-element.51), channel_id=1, source_target_pairs={{0,1},{1,0},{2,6},{3,7},{4,5},{5,4},{6,2},{7,3},{8,9},{9,8},{10,14... | collective-permute-start | bytes 786440 | tf_op jit(solution)/shard_map/ppermute | solution.py:71
  74.6 10.1 %collective-permute-start.26 = (bf16[32,3072]{1,0:T(8,128)(2,1)S(1)}, bf16[32,3072]{1,0:T(8,128)(2,1)S(1)}, u32[]{:S(2)}, u32[]{:S(2)}) collective-permute-start(bf16[32,3072]{1,0:T(8,128)(2,1)S(1)} %get-tuple-element.52), channel_id=1, source_target_pairs={{0,4},{1,5},{2,3},{3,2},{4,0},{5,1},{6,7},{7,6},{8,12},{9,13},{10,... | collective-permute-start | bytes 589832 | tf_op jit(solution)/shard_map/ppermute | solution.py:71
  75.4 9.4 %collective-permute-start.29 = (bf16[32,3072]{1,0:T(8,128)(2,1)S(1)}, bf16[32,3072]{1,0:T(8,128)(2,1)S(1)}, u32[]{:S(2)}, u32[]{:S(2)}) collective-permute-start(bf16[32,3072]{1,0:T(8,128)(2,1)S(1)} %get-tuple-element.53), channel_id=1, source_target_pairs={{0,1},{1,0},{2,6},{3,7},{4,5},{5,4},{6,2},{7,3},{8,9},{9,8},{10,14... | collective-permute-start | bytes 589832 | tf_op jit(solution)/shard_map/ppermute | solution.py:71
  84.9 8.8 %collective-permute-start.30 = (bf16[8,3072]{1,0:T(8,128)(2,1)S(1)}, bf16[8,3072]{1,0:T(8,128)(2,1)S(1)}, u32[]{:S(2)}, u32[]{:S(2)}) collective-permute-start(bf16[8,3072]{1,0:T(8,128)(2,1)S(1)} %get-tuple-element.57), channel_id=1, source_target_pairs={{0,8},{1,9},{2,10},{3,11},{4,12},{5,13},{6,14},{7,15},{8,0},{9,1},... | collective-permute-start | bytes 147464 | tf_op jit(solution)/shard_map/ppermute | solution.py:71
  86.8 7.0 %collective-permute-start.32 = (bf16[8,3072]{1,0:T(8,128)(2,1)S(1)}, bf16[8,3072]{1,0:T(8,128)(2,1)S(1)}, u32[]{:S(2)}, u32[]{:S(2)}) collective-permute-start(bf16[8,3072]{1,0:T(8,128)(2,1)S(1)} %get-tuple-element.58), channel_id=1, source_target_pairs={{0,24},{1,25},{2,26},{3,27},{4,28},{5,29},{6,30},{7,31},{8,16},{9,... | collective-permute-start | bytes 147464 | tf_op jit(solution)/shard_map/ppermute | solution.py:71
  89.2 7.1 %collective-permute-start.31 = (bf16[8,3072]{1,0:T(8,128)(2,1)S(1)}, bf16[8,3072]{1,0:T(8,128)(2,1)S(1)}, u32[]{:S(2)}, u32[]{:S(2)}) collective-permute-start(bf16[8,3072]{1,0:T(8,128)(2,1)S(1)} %get-tuple-element.59), channel_id=1, source_target_pairs={{0,16},{1,17},{2,18},{3,19},{4,20},{5,21},{6,22},{7,23},{8,24},{9,... | collective-permute-start | bytes 147464 | tf_op jit(solution)/shard_map/ppermute | solution.py:71
  89.3 7.1 %collective-permute-start.22 = (bf16[8,4096]{1,0:T(8,128)(2,1)S(1)}, bf16[8,4096]{1,0:T(8,128)(2,1)S(1)}, u32[]{:S(2)}, u32[]{:S(2)}) collective-permute-start(bf16[8,4096]{1,0:T(8,128)(2,1)S(1)} %get-tuple-element.54), channel_id=1, source_target_pairs={{0,8},{1,9},{2,10},{3,11},{4,12},{5,13},{6,14},{7,15},{8,0},{9,1},... | collective-permute-start | bytes 196616 | tf_op jit(solution)/shard_map/ppermute | solution.py:71
  91.2 6.2 %collective-permute-start.24 = (bf16[8,4096]{1,0:T(8,128)(2,1)S(1)}, bf16[8,4096]{1,0:T(8,128)(2,1)S(1)}, u32[]{:S(2)}, u32[]{:S(2)}) collective-permute-start(bf16[8,4096]{1,0:T(8,128)(2,1)S(1)} %get-tuple-element.55), channel_id=1, source_target_pairs={{0,24},{1,25},{2,26},{3,27},{4,28},{5,29},{6,30},{7,31},{8,16},{9,... | collective-permute-start | bytes 196616 | tf_op jit(solution)/shard_map/ppermute | solution.py:71
  (21 other events, 80.3 us)

commit v6 on v5

--- a/solution.py
+++ b/solution.py
@@ -85,52 +85,78 @@
     def extent(self, pick):
         return self.sizes[pick(0)]
 
+    def far(self, near):
+        return [
+            self.swap(block, self.second, m)
+            for m in range(1, self.extent(self.second))
+            for block in near
+        ]
+
+    def near(self, line):
+        return [line] + [self.swap(line, self.first, m) for m in range(1, self.extent(self.first))]
+
     def gather(self, rows, weights):
-        weights = list(weights)
-        lines = [rows] + [self.swap(rows, self.high, m) for m in range(1, self.extent(self.high))]
-        half = len(lines) // 2
-        places = []
-        for lines in (lines[:half], lines[half:]):
-            line = jnp.concatenate(lines, axis=0)
-            if places:
-                line, places[0][1], weights[0] = lax.optimization_barrier(
-                    (line, places[0][1], weights[0])
-                )
-            near = [line]
-            near += [self.swap(line, self.first, m) for m in range(1, self.extent(self.first))]
-            if places:
-                near[-1], weights[1] = lax.optimization_barrier((near[-1], weights[1]))
-            mine = list(near)
-            for m in range(1, self.extent(self.second)):
-                mine += [self.swap(block, self.second, m) for block in near]
-            if places:
-                mine[-1], weights[2] = lax.optimization_barrier((mine[-1], weights[2]))
-            places.append(mine + [self.swap(block, self.core, 1) for block in mine])
-        return [list(blocks) for blocks in zip(*places)], weights
+        gate, up, down = weights
+        line, m, half = rows, 1, self.extent(self.high) // 2
+        while m < half:
+            line, m = join([line, self.swap(line, self.high, m)]), 2 * m
+        later = self.swap(line, self.high, half)
+        near = self.near(line)
+        far = self.far(near)
+        later, near, far[0], gate = lax.optimization_barrier((later, near, far[0], gate))
+        later_near = self.near(later)
+        later_near[-1], far[-1], up = lax.optimization_barrier((later_near[-1], far[-1], up))
+        later_far = self.far(later_near)
+        later_far[-1], down = lax.optimization_barrier((later_far[-1], down))
+        groups = []
+        for mine in (near + far, later_near + later_far):
+            groups.append(mine + [self.swap(block, self.core, 1) for block in mine])
+        return [list(blocks) for blocks in zip(*groups)], (gate, up, down)
 
     def last_sum(self, mine, other):
         return add([mine[-1], self.swap(other[0], self.core, 1)])
 
-    def scatter_sum(self, mine, other, last):
+    def rest_sums(self, mine, other):
         size = mine[0].shape[0]
         rest = self.swap(other[1], self.core, 1)
-        sums = [last]
-        for i in range(len(mine) - 1):
-            sums.insert(i, add([mine[i], rest[i * size : (i + 1) * size]]))
+        return [
+            add([part, rest[i * size : (i + 1) * size]]) for i, part in enumerate(mine[:-1])
+        ]
+
+    def back(self, sums, place):
+        return self.swap(sums[place], self.second, place // self.extent(self.first))
+
+    def line_sum(self, sums, last):
         wide = self.extent(self.first)
-        near = []
-        for i in range(wide):
-            parts = [sums[i]]
-            for m in range(1, self.extent(self.second)):
-                parts.append(self.swap(sums[m * wide + i], self.second, m))
-            near.append(parts)
+        near = [[part] for part in sums[:wide]]
+        for place in range(wide, len(sums)):
+            moved = last if place == len(sums) - 1 else self.back(sums, place)
+            near[place % wide].append(moved)
         near = [add(parts) for parts in near]
-        line = add([near[0]] + [self.swap(near[m], self.first, m) for m in range(1, wide)])
-        rows = size // self.extent(self.high)
+        return add([near[0]] + [self.swap(near[m], self.first, m) for m in range(1, wide)])
+
+    def high_sum(self, line):
+        rows = line.shape[0] // self.extent(self.high)
         parts = [line[:rows]]
         for m in range(1, self.extent(self.high)):
             parts.append(self.swap(line[m * rows : (m + 1) * rows], self.high, m))
         return add(parts)
+
+
+def join_kernel(*refs):
+    refs[-1][...] = jnp.concatenate([ref[...] for ref in refs[:-1]], axis=0)
+
+
+def join(parts):
+    rows = sum(part.shape[0] for part in parts)
+    return pl.pallas_call(
+        join_kernel,
+        in_specs=[pl.BlockSpec(memory_space=pltpu.VMEM)] * len(parts),
+        out_specs=pl.BlockSpec(memory_space=pltpu.VMEM),
+        out_shape=jax.ShapeDtypeStruct((rows, parts[0].shape[1]), parts[0].dtype),
+        compiler_params=pltpu.CompilerParams(vmem_limit_bytes=2 * MEBI),
+        name="join",
+    )(*parts)
 
 
 def add(parts):
@@ -318,9 +344,17 @@
     last = grid.last_sum(lower, lower_other)
     hidden, last = lax.optimization_barrier((hidden, last))
     products = down_of(hidden, share, down, sizes, split)
-    lower = grid.scatter_sum(lower, lower_other, last)
     upper, upper_other = products[:count], products[count:]
-    upper = grid.scatter_sum(upper, upper_other, grid.last_sum(upper, upper_other))
+    sums = grid.rest_sums(lower, lower_other) + [last]
+    came = grid.back(sums, count - 1)
+    last = grid.last_sum(upper, upper_other)
+    last, came = lax.optimization_barrier((last, came))
+    line = grid.line_sum(sums, came)
+    sums = grid.rest_sums(upper, upper_other)
+    came = grid.back(sums + [last], count - 1)
+    sums, came, line = lax.optimization_barrier((sums, came, line))
+    lower = grid.high_sum(line)
+    upper = grid.high_sum(grid.line_sum(sums + [last], came))
     return (jnp.concatenate([lower, upper], axis=1), attn_latent)
 
 

time: 100 us -> 101 us (1.010)
    ppermute x33 -> x32, waiting for transfers between devices: 29.1 us -> 28.3 us  [swap(): return lax.ppermute(value, everyone, pairs)]
    ppermute x33 -> x32, starting transfers between devices: 29.6 us -> 30 us  [swap(): return lax.ppermute(value, everyone, pairs)]
  transfers between devices with their start and end apart: 33 -> 32, of which waited for: 17 -> 10; matrix products, arithmetic and copies ran while one was open for 1% -> 1% of each run, Pallas kernels for 12% -> 12%
where the time goes in v6:
time: 101 us
  starting transfers between devices  30 us (30%)
  waiting for transfers between devices  28.3 us (28%)
  Pallas kernels  21 us (21%)
  local copies, waits for them, and re-layouts  19 us (19%)
  other arithmetic  1.4 us (1%)
    ppermute x32, starting transfers between devices, swap(): return lax.ppermute(value, everyone, pairs)  30 us
    ppermute x32, waiting for transfers between devices, swap(): return lax.ppermute(value, everyone, pairs)  28.3 us
    unnamed x24, local copies, waits for them, and re-layouts  19 us
    pallas_call x3, Pallas kernels, bring(): pl.pallas_call(bring_kernel, in_specs=[pl.BlockSpec(memory_space=pltpu.HB...  9.65 us
    pallas_call x1, Pallas kernels, expert(): pl.pallas_call(functools.partial(expert_kernel, len(blocks), experts, 102...  6.16 us
    pallas_call x1, Pallas kernels, attention(): pl.pallas_call(attention_kernel, in_specs=[pl.BlockSpec(memory_space=pltp...  2.36 us
  transfers between devices with their start and end apart: 32, of which 10 were waited for; matrix products, arithmetic and copies ran while one was open for 1% of the time, Pallas kernels for 12%

profile of v6, /device:TPU:0, one launch (start us, length us, event | category | flops | bytes accessed | tf_op | source)
XLA Modules:
  0.0 100.5 jit_solution(4127396982397882669)
XLA Ops:
  0.6 1.7 %pack.1.refs_0_ = bf16[8,7296]{1,0:T(8,128)(2,1)} custom-call(bf16[8,7168]{1,0:T(8,128)(2,1)} %rows_ref.1, s32[8,8]{1,0:T(8,128)} %ids_ref.1, f32[8,8]{1,0:T(8,128)} %gates_ref.1), custom_call_target="tpu_custom_call" | custom-call | tf_op jit(solution)/shard_map/pack/pallas_call | solution.py:189
  2.4 3.0 %collective-permute-start = (bf16[8,7296]{1,0:T(8,128)(2,1)}, bf16[8,7296]{1,0:T(8,128)(2,1)S(1)}, u32[]{:S(2)}, u32[]{:S(2)}) collective-permute-start(bf16[8,7296]{1,0:T(8,128)(2,1)} %pack.1.refs_0_), channel_id=1, source_target_pairs={{0,8},{1,9},{2,10},{3,11},{4,12},{5,13},{6,14},{7,15},{8,0},{9,1},... | collective-permute-start | bytes 350216 | tf_op jit(solution)/shard_map/ppermute | solution.py:71
  5.4 3.4 %collective-permute-done.refs_1_ = bf16[8,7296]{1,0:T(8,128)(2,1)S(1)} collective-permute-done((bf16[8,7296]{1,0:T(8,128)(2,1)}, bf16[8,7296]{1,0:T(8,128)(2,1)S(1)}, u32[]{:S(2)}, u32[]{:S(2)}) %collective-permute-start) | collective-permute-done | bytes 116768 | tf_op jit(solution)/shard_map/ppermute | solution.py:71
  9.7 1.8 %collective-permute-start.3 = (bf16[16,7296]{1,0:T(8,128)(2,1)S(1)}, bf16[16,7296]{1,0:T(8,128)(2,1)S(1)}, u32[]{:S(2)}, u32[]{:S(2)}) collective-permute-start(bf16[16,7296]{1,0:T(8,128)(2,1)S(1)} %join.1.refs_0_), channel_id=1, source_target_pairs={{0,4},{1,5},{2,3},{3,2},{4,0},{5,1},{6,7},{7,6},{8,12},{9,13},{10,... | collective-permute-start | bytes 700424 | tf_op jit(solution)/shard_map/ppermute | solution.py:71
  13.0 2.6 %collective-permute-start.1 = (bf16[16,7296]{1,0:T(8,128)(2,1)S(1)}, bf16[16,7296]{1,0:T(8,128)(2,1)S(1)}, u32[]{:S(2)}, u32[]{:S(2)}) collective-permute-start(bf16[16,7296]{1,0:T(8,128)(2,1)S(1)} %join.1.refs_0_), channel_id=1, source_target_pairs={{0,16},{1,17},{2,18},{3,19},{4,20},{5,21},{6,22},{7,23},{8,24},{9,... | collective-permute-start | bytes 700424 | tf_op jit(solution)/shard_map/ppermute | solution.py:71
  15.6 3.2 %gate.1.refs_16_ = bf16[7168,512]{1,0:T(8,128)(2,1)S(1)} custom-call(bf16[7168,512]{1,0:T(8,128)(2,1)} %bitcast.4), custom_call_target="tpu_custom_call" | custom-call | bytes 7340032 | tf_op jit(solution)/shard_map/gate/pallas_call | solution.py:217
  18.8 2.9 %copy-done.2 = bf16[7168,512]{1,0:T(8,128)(2,1)} copy-done((bf16[7168,512]{1,0:T(8,128)(2,1)}, bf16[7168,512]{1,0:T(8,128)(2,1)S(1)}, u32[]{:S(2)}) %copy-start.2) | copy-done | bytes 7340056
  21.7 3.2 %collective-permute-done.1.refs_1_ = bf16[16,7296]{1,0:T(8,128)(2,1)S(1)} collective-permute-done((bf16[16,7296]{1,0:T(8,128)(2,1)S(1)}, bf16[16,7296]{1,0:T(8,128)(2,1)S(1)}, u32[]{:S(2)}, u32[]{:S(2)}) %collective-permute-start.1) | collective-permute-done | bytes 233504 | tf_op jit(solution)/shard_map/ppermute | solution.py:71
  26.1 3.2 %up.1.refs_17_ = bf16[7168,512]{1,0:T(8,128)(2,1)S(1)} custom-call(bf16[7168,512]{1,0:T(8,128)(2,1)} %bitcast.5), custom_call_target="tpu_custom_call" | custom-call | bytes 7340032 | tf_op jit(solution)/shard_map/up/pallas_call | solution.py:217
  29.3 3.0 %copy-done.4 = bf16[7168,512]{1,0:T(8,128)(2,1)} copy-done((bf16[7168,512]{1,0:T(8,128)(2,1)}, bf16[7168,512]{1,0:T(8,128)(2,1)S(1)}, u32[]{:S(2)}) %copy-start.4) | copy-done | bytes 7340056
  35.4 3.3 %down_in.1.refs_18_.down_ref = bf16[512,7168]{1,0:T(8,128)(2,1)S(1)} custom-call(bf16[512,7168]{1,0:T(8,128)(2,1)} %bitcast.6), custom_call_target="tpu_custom_call" | custom-call | bytes 7340032 | tf_op jit(solution)/shard_map/down_in/pallas_call | solution.py:217
  38.7 3.0 %copy-done = bf16[512,7168]{1,0:T(8,128)(2,1)} copy-done((bf16[512,7168]{1,0:T(8,128)(2,1)}, bf16[512,7168]{1,0:T(8,128)(2,1)S(1)}, u32[]{:S(2)}) %copy-start) | copy-done | bytes 7340056
  41.7 2.4 %attention.1 = bf16[2,64,512]{2,1,0:T(8,128)(2,1)} custom-call(s32[2]{0:T(128)S(1)} %copy-done.11, bf16[2,64,512]{2,1,0:T(8,128)(2,1)S(1)} %copy-done.8, bf16[2,64,64]{2,1,0:T(8,128)(2,1)S(1)} %copy-done.10, bf16[2,512,512]{2,1,0:T(8,128)(2,1)S(1)} %copy-done.6, bf16[2,64,512]{2,1,0:T(8,128)(2,1)S(1)} %copy-done.9), custom_call_target="tpu_custom_call" | custom-call | flops 134217728 | bytes 1048576 | tf_op jit(solution)/shard_map/attention/pallas_call | solution.py:39
  47.0 3.1 %copy-done.1 = bf16[512,7168]{1,0:T(8,128)(2,1)S(1)} copy-done((bf16[512,7168]{1,0:T(8,128)(2,1)S(1)}, bf16[512,7168]{1,0:T(8,128)(2,1)}, u32[]{:S(2)}) %copy-start.1) | copy-done | bytes 7340056
  50.1 3.1 %copy-done.3 = bf16[7168,512]{1,0:T(8,128)(2,1)S(1)} copy-done((bf16[7168,512]{1,0:T(8,128)(2,1)S(1)}, bf16[7168,512]{1,0:T(8,128)(2,1)}, u32[]{:S(2)}) %copy-start.3) | copy-done | bytes 7340056
  53.2 3.1 %copy-done.5 = bf16[7168,512]{1,0:T(8,128)(2,1)S(1)} copy-done((bf16[7168,512]{1,0:T(8,128)(2,1)S(1)}, bf16[7168,512]{1,0:T(8,128)(2,1)}, u32[]{:S(2)}) %copy-start.5) | copy-done | bytes 7340056
  56.3 6.2 %expert.1 = (bf16[256,512]{1,0:T(8,128)(2,1)S(1)}, f32[256,128]{1,0:T(8,128)S(1)}, bf16[32,4096]{1,0:T(8,128)(2,1)S(1)}, bf16[32,4096]{1,0:T(8,128)(2,1)S(1)}, b...) custom-call(s32[1]{0:T(128)} %bitcast.node_ref, ...), custom_call_target="tpu_custom_call" | custom-call | flops 4831838208 | bytes 18874368 | tf_op jit(solution)/shard_map/expert/pallas_call | solution.py:265
  66.8 5.3 %collective-permute-done.19 = bf16[32,4096]{1,0:T(8,128)(2,1)S(1)} collective-permute-done((bf16[32,4096]{1,0:T(8,128)(2,1)S(1)}, bf16[32,4096]{1,0:T(8,128)(2,1)S(1)}, u32[]{:S(2)}, u32[]{:S(2)}) %collective-permute-start.19) | collective-permute-done | bytes 262176 | tf_op jit(solution)/shard_map/ppermute | solution.py:71
  75.5 7.9 %collective-permute-done.22 = bf16[32,4096]{1,0:T(8,128)(2,1)S(1)} collective-permute-done((bf16[32,4096]{1,0:T(8,128)(2,1)S(1)}, bf16[32,4096]{1,0:T(8,128)(2,1)S(1)}, u32[]{:S(2)}, u32[]{:S(2)}) %collective-permute-start.22) | collective-permute-done | bytes 262176 | tf_op jit(solution)/shard_map/ppermute | solution.py:71
  84.6 1.5 %collective-permute-start.27 = (bf16[32,3072]{1,0:T(8,128)(2,1)S(1)}, bf16[32,3072]{1,0:T(8,128)(2,1)S(1)}, u32[]{:S(2)}, u32[]{:S(2)}) collective-permute-start(bf16[32,3072]{1,0:T(8,128)(2,1)S(1)} %get-tuple-element.66), channel_id=1, source_target_pairs={{0,4},{1,5},{2,3},{3,2},{4,0},{5,1},{6,7},{7,6},{8,12},{9,13},{10,... | collective-permute-start | bytes 589832 | tf_op jit(solution)/shard_map/ppermute | solution.py:71
  86.9 2.9 %collective-permute-start.26 = (bf16[8,4096]{1,0:T(8,128)(2,1)S(1)}, bf16[8,4096]{1,0:T(8,128)(2,1)S(1)}, u32[]{:S(2)}, u32[]{:S(2)}) collective-permute-start(bf16[8,4096]{1,0:T(8,128)(2,1)S(1)} %get-tuple-element.76), channel_id=1, source_target_pairs={{0,24},{1,25},{2,26},{3,27},{4,28},{5,29},{6,30},{7,31},{8,16},{9,... | collective-permute-start | bytes 196616 | tf_op jit(solution)/shard_map/ppermute | solution.py:71
  91.4 2.9 %collective-permute-start.31 = (bf16[8,3072]{1,0:T(8,128)(2,1)S(1)}, bf16[8,3072]{1,0:T(8,128)(2,1)S(1)}, u32[]{:S(2)}, u32[]{:S(2)}) collective-permute-start(bf16[8,3072]{1,0:T(8,128)(2,1)S(1)} %get-tuple-element.79), channel_id=1, source_target_pairs={{0,24},{1,25},{2,26},{3,27},{4,28},{5,29},{6,30},{7,31},{8,16},{9,... | collective-permute-start | bytes 147464 | tf_op jit(solution)/shard_map/ppermute | solution.py:71
  94.6 2.9 %collective-permute-done.25 = bf16[8,4096]{1,0:T(8,128)(2,1)S(1)} collective-permute-done((bf16[8,4096]{1,0:T(8,128)(2,1)S(1)}, bf16[8,4096]{1,0:T(8,128)(2,1)S(1)}, u32[]{:S(2)}, u32[]{:S(2)}) %collective-permute-start.25) | collective-permute-done | bytes 65568 | tf_op jit(solution)/shard_map/ppermute | solution.py:71
  97.5 2.3 %collective-permute-done.30 = bf16[8,3072]{1,0:T(8,128)(2,1)S(1)} collective-permute-done((bf16[8,3072]{1,0:T(8,128)(2,1)S(1)}, bf16[8,3072]{1,0:T(8,128)(2,1)S(1)}, u32[]{:S(2)}, u32[]{:S(2)}) %collective-permute-start.30) | collective-permute-done | bytes 49184 | tf_op jit(solution)/shard_map/ppermute | solution.py:71
  (84 shorter events, 22.0 us)
Async XLA Ops:
  2.4 6.4 %collective-permute-start = (bf16[8,7296]{1,0:T(8,128)(2,1)}, bf16[8,7296]{1,0:T(8,128)(2,1)S(1)}, u32[]{:S(2)}, u32[]{:S(2)}) collective-permute-start(bf16[8,7296]{1,0:T(8,128)(2,1)} %pack.1.refs_0_), channel_id=1, source_target_pairs={{0,8},{1,9},{2,10},{3,11},{4,12},{5,13},{6,14},{7,15},{8,0},{9,1},... | collective-permute-start | bytes 350216 | tf_op jit(solution)/shard_map/ppermute | solution.py:71
  9.7 11.9 %collective-permute-start.3 = (bf16[16,7296]{1,0:T(8,128)(2,1)S(1)}, bf16[16,7296]{1,0:T(8,128)(2,1)S(1)}, u32[]{:S(2)}, u32[]{:S(2)}) collective-permute-start(bf16[16,7296]{1,0:T(8,128)(2,1)S(1)} %join.1.refs_0_), channel_id=1, source_target_pairs={{0,4},{1,5},{2,3},{3,2},{4,0},{5,1},{6,7},{7,6},{8,12},{9,13},{10,... | collective-permute-start | bytes 700424 | tf_op jit(solution)/shard_map/ppermute | solution.py:71
  11.5 10.2 %collective-permute-start.2 = (bf16[16,7296]{1,0:T(8,128)(2,1)S(1)}, bf16[16,7296]{1,0:T(8,128)(2,1)S(1)}, u32[]{:S(2)}, u32[]{:S(2)}) collective-permute-start(bf16[16,7296]{1,0:T(8,128)(2,1)S(1)} %join.1.refs_0_), channel_id=1, source_target_pairs={{0,1},{1,0},{2,6},{3,7},{4,5},{5,4},{6,2},{7,3},{8,9},{9,8},{10,14... | collective-permute-start | bytes 700424 | tf_op jit(solution)/shard_map/ppermute | solution.py:71
  13.0 11.9 %collective-permute-start.1 = (bf16[16,7296]{1,0:T(8,128)(2,1)S(1)}, bf16[16,7296]{1,0:T(8,128)(2,1)S(1)}, u32[]{:S(2)}, u32[]{:S(2)}) collective-permute-start(bf16[16,7296]{1,0:T(8,128)(2,1)S(1)} %join.1.refs_0_), channel_id=1, source_target_pairs={{0,16},{1,17},{2,18},{3,19},{4,20},{5,21},{6,22},{7,23},{8,24},{9,... | collective-permute-start | bytes 700424 | tf_op jit(solution)/shard_map/ppermute | solution.py:71
  24.9 7.4 %collective-permute-start.5 = (bf16[16,7296]{1,0:T(8,128)(2,1)S(1)}, bf16[16,7296]{1,0:T(8,128)(2,1)S(1)}, u32[]{:S(2)}, u32[]{:S(2)}) collective-permute-start(bf16[16,7296]{1,0:T(8,128)(2,1)S(1)} %collective-permute-done.2.refs_2_), channel_id=1, source_target_pairs={{0,4},{1,5},{2,3},{3,2},{4,0},{5,1},{6,7},{7,6},{8,12},{9,13},{10,... | collective-permute-start | bytes 700424 | tf_op jit(solution)/shard_map/ppermute | solution.py:71
  25.4 6.9 %collective-permute-start.4 = (bf16[16,7296]{1,0:T(8,128)(2,1)S(1)}, bf16[16,7296]{1,0:T(8,128)(2,1)S(1)}, u32[]{:S(2)}, u32[]{:S(2)}) collective-permute-start(bf16[16,7296]{1,0:T(8,128)(2,1)S(1)} %collective-permute-done.1.refs_1_), channel_id=1, source_target_pairs={{0,1},{1,0},{2,6},{3,7},{4,5},{5,4},{6,2},{7,3},{8,9},{9,8},{10,14... | collective-permute-start | bytes 700424 | tf_op jit(solution)/shard_map/ppermute | solution.py:71
  32.3 11.8 %collective-permute-start.7 = (bf16[16,7296]{1,0:T(8,128)(2,1)S(1)}, bf16[16,7296]{1,0:T(8,128)(2,1)S(1)}, u32[]{:S(2)}, u32[]{:S(2)}) collective-permute-start(bf16[16,7296]{1,0:T(8,128)(2,1)S(1)} %collective-permute-done.4.refs_3_), channel_id=1, source_target_pairs={{0,4},{1,5},{2,3},{3,2},{4,0},{5,1},{6,7},{7,6},{8,12},{9,13},{10,... | collective-permute-start | bytes 700424 | tf_op jit(solution)/shard_map/ppermute | solution.py:71
  33.7 10.4 %collective-permute-start.10 = (bf16[16,7296]{1,0:T(8,128)(2,1)S(1)}, bf16[16,7296]{1,0:T(8,128)(2,1)S(1)}, u32[]{:S(2)}, u32[]{:S(2)}) collective-permute-start(bf16[16,7296]{1,0:T(8,128)(2,1)S(1)} %join.1.refs_0_), channel_id=1, source_target_pairs={{0,2},{1,3},{2,0},{3,1},{4,6},{5,7},{6,4},{7,5},{8,10},{9,11},{10,... | collective-permute-start | bytes 700424 | tf_op jit(solution)/shard_map/ppermute | solution.py:71
  33.7 10.9 %collective-permute-start.12 = (bf16[16,7296]{1,0:T(8,128)(2,1)S(1)}, bf16[16,7296]{1,0:T(8,128)(2,1)S(1)}, u32[]{:S(2)}, u32[]{:S(2)}) collective-permute-start(bf16[16,7296]{1,0:T(8,128)(2,1)S(1)} %collective-permute-done.2.refs_2_), channel_id=1, source_target_pairs={{0,2},{1,3},{2,0},{3,1},{4,6},{5,7},{6,4},{7,5},{8,10},{9,11},{10,... | collective-permute-start | bytes 700424 | tf_op jit(solution)/shard_map/ppermute | solution.py:71
  34.2 10.5 %collective-permute-start.6 = (bf16[16,7296]{1,0:T(8,128)(2,1)S(1)}, bf16[16,7296]{1,0:T(8,128)(2,1)S(1)}, u32[]{:S(2)}, u32[]{:S(2)}) collective-permute-start(bf16[16,7296]{1,0:T(8,128)(2,1)S(1)} %collective-permute-done.1.refs_1_), channel_id=1, source_target_pairs={{0,4},{1,5},{2,3},{3,2},{4,0},{5,1},{6,7},{7,6},{8,12},{9,13},{10,... | collective-permute-start | bytes 700424 | tf_op jit(solution)/shard_map/ppermute | solution.py:71
  34.8 10.3 %collective-permute-start.14 = (bf16[16,7296]{1,0:T(8,128)(2,1)S(1)}, bf16[16,7296]{1,0:T(8,128)(2,1)S(1)}, u32[]{:S(2)}, u32[]{:S(2)}) collective-permute-start(bf16[16,7296]{1,0:T(8,128)(2,1)S(1)} %collective-permute-done.3.refs_4_), channel_id=1, source_target_pairs={{0,2},{1,3},{2,0},{3,1},{4,6},{5,7},{6,4},{7,5},{8,10},{9,11},{10,... | collective-permute-start | bytes 700424 | tf_op jit(solution)/shard_map/ppermute | solution.py:71
  65.4 7.7 %collective-permute-start.21 = (bf16[96,4096]{1,0:T(8,128)(2,1)S(1)}, bf16[96,4096]{1,0:T(8,128)(2,1)S(1)}, u32[]{:S(2)}, u32[]{:S(2)}) collective-permute-start(bf16[96,4096]{1,0:T(8,128)(2,1)S(1)} %get-tuple-element.60), channel_id=1, source_target_pairs={{0,2},{1,3},{2,0},{3,1},{4,6},{5,7},{6,4},{7,5},{8,10},{9,11},{10,... | collective-permute-start | bytes 2359304 | tf_op jit(solution)/shard_map/ppermute | solution.py:71
  65.7 6.4 %collective-permute-start.19 = (bf16[32,4096]{1,0:T(8,128)(2,1)S(1)}, bf16[32,4096]{1,0:T(8,128)(2,1)S(1)}, u32[]{:S(2)}, u32[]{:S(2)}) collective-permute-start(bf16[32,4096]{1,0:T(8,128)(2,1)S(1)} %add_convert_fusion.6), channel_id=1, source_target_pairs={{0,4},{1,5},{2,3},{3,2},{4,0},{5,1},{6,7},{7,6},{8,12},{9,13},{10,... | collective-permute-start | bytes 786440 | tf_op jit(solution)/shard_map/ppermute | solution.py:71
  66.7 8.6 %collective-permute-start.17 = (bf16[96,3072]{1,0:T(8,128)(2,1)S(1)}, bf16[96,3072]{1,0:T(8,128)(2,1)S(1)}, u32[]{:S(2)}, u32[]{:S(2)}) collective-permute-start(bf16[96,3072]{1,0:T(8,128)(2,1)S(1)} %get-tuple-element.52), channel_id=1, source_target_pairs={{0,2},{1,3},{2,0},{3,1},{4,6},{5,7},{6,4},{7,5},{8,10},{9,11},{10,... | collective-permute-start | bytes 1769480 | tf_op jit(solution)/shard_map/ppermute | solution.py:71
  72.1 11.4 %collective-permute-start.20 = (bf16[32,3072]{1,0:T(8,128)(2,1)S(1)}, bf16[32,3072]{1,0:T(8,128)(2,1)S(1)}, u32[]{:S(2)}, u32[]{:S(2)}) collective-permute-start(bf16[32,3072]{1,0:T(8,128)(2,1)S(1)} %add_convert_fusion.10), channel_id=1, source_target_pairs={{0,4},{1,5},{2,3},{3,2},{4,0},{5,1},{6,7},{7,6},{8,12},{9,13},{10,... | collective-permute-start | bytes 589832 | tf_op jit(solution)/shard_map/ppermute | solution.py:71
  73.2 10.1 %collective-permute-start.22 = (bf16[32,4096]{1,0:T(8,128)(2,1)S(1)}, bf16[32,4096]{1,0:T(8,128)(2,1)S(1)}, u32[]{:S(2)}, u32[]{:S(2)}) collective-permute-start(bf16[32,4096]{1,0:T(8,128)(2,1)S(1)} %get-tuple-element.70), channel_id=1, source_target_pairs={{0,4},{1,5},{2,3},{3,2},{4,0},{5,1},{6,7},{7,6},{8,12},{9,13},{10,... | collective-permute-start | bytes 786440 | tf_op jit(solution)/shard_map/ppermute | solution.py:71
  74.3 9.0 %collective-permute-start.23 = (bf16[32,4096]{1,0:T(8,128)(2,1)S(1)}, bf16[32,4096]{1,0:T(8,128)(2,1)S(1)}, u32[]{:S(2)}, u32[]{:S(2)}) collective-permute-start(bf16[32,4096]{1,0:T(8,128)(2,1)S(1)} %get-tuple-element.71), channel_id=1, source_target_pairs={{0,1},{1,0},{2,6},{3,7},{4,5},{5,4},{6,2},{7,3},{8,9},{9,8},{10,14... | collective-permute-start | bytes 786440 | tf_op jit(solution)/shard_map/ppermute | solution.py:71
  83.6 6.7 %collective-permute-start.28 = (bf16[32,3072]{1,0:T(8,128)(2,1)S(1)}, bf16[32,3072]{1,0:T(8,128)(2,1)S(1)}, u32[]{:S(2)}, u32[]{:S(2)}) collective-permute-start(bf16[32,3072]{1,0:T(8,128)(2,1)S(1)} %add_convert_fusion.8), channel_id=1, source_target_pairs={{0,1},{1,0},{2,6},{3,7},{4,5},{5,4},{6,2},{7,3},{8,9},{9,8},{10,14... | collective-permute-start | bytes 589832 | tf_op jit(solution)/shard_map/ppermute | solution.py:71
  84.6 5.7 %collective-permute-start.27 = (bf16[32,3072]{1,0:T(8,128)(2,1)S(1)}, bf16[32,3072]{1,0:T(8,128)(2,1)S(1)}, u32[]{:S(2)}, u32[]{:S(2)}) collective-permute-start(bf16[32,3072]{1,0:T(8,128)(2,1)S(1)} %get-tuple-element.66), channel_id=1, source_target_pairs={{0,4},{1,5},{2,3},{3,2},{4,0},{5,1},{6,7},{7,6},{8,12},{9,13},{10,... | collective-permute-start | bytes 589832 | tf_op jit(solution)/shard_map/ppermute | solution.py:71
  86.1 8.2 %collective-permute-start.24 = (bf16[8,4096]{1,0:T(8,128)(2,1)S(1)}, bf16[8,4096]{1,0:T(8,128)(2,1)S(1)}, u32[]{:S(2)}, u32[]{:S(2)}) collective-permute-start(bf16[8,4096]{1,0:T(8,128)(2,1)S(1)} %get-tuple-element.75), channel_id=1, source_target_pairs={{0,8},{1,9},{2,10},{3,11},{4,12},{5,13},{6,14},{7,15},{8,0},{9,1},... | collective-permute-start | bytes 196616 | tf_op jit(solution)/shard_map/ppermute | solution.py:71
  86.9 7.7 %collective-permute-start.26 = (bf16[8,4096]{1,0:T(8,128)(2,1)S(1)}, bf16[8,4096]{1,0:T(8,128)(2,1)S(1)}, u32[]{:S(2)}, u32[]{:S(2)}) collective-permute-start(bf16[8,4096]{1,0:T(8,128)(2,1)S(1)} %get-tuple-element.76), channel_id=1, source_target_pairs={{0,24},{1,25},{2,26},{3,27},{4,28},{5,29},{6,30},{7,31},{8,16},{9,... | collective-permute-start | bytes 196616 | tf_op jit(solution)/shard_map/ppermute | solution.py:71
  89.8 7.7 %collective-permute-start.25 = (bf16[8,4096]{1,0:T(8,128)(2,1)S(1)}, bf16[8,4096]{1,0:T(8,128)(2,1)S(1)}, u32[]{:S(2)}, u32[]{:S(2)}) collective-permute-start(bf16[8,4096]{1,0:T(8,128)(2,1)S(1)} %get-tuple-element.77), channel_id=1, source_target_pairs={{0,16},{1,17},{2,18},{3,19},{4,20},{5,21},{6,22},{7,23},{8,24},{9,... | collective-permute-start | bytes 196616 | tf_op jit(solution)/shard_map/ppermute | solution.py:71
  90.4 7.2 %collective-permute-start.29 = (bf16[8,3072]{1,0:T(8,128)(2,1)S(1)}, bf16[8,3072]{1,0:T(8,128)(2,1)S(1)}, u32[]{:S(2)}, u32[]{:S(2)}) collective-permute-start(bf16[8,3072]{1,0:T(8,128)(2,1)S(1)} %get-tuple-element.78), channel_id=1, source_target_pairs={{0,8},{1,9},{2,10},{3,11},{4,12},{5,13},{6,14},{7,15},{8,0},{9,1},... | collective-permute-start | bytes 147464 | tf_op jit(solution)/shard_map/ppermute | solution.py:71
  91.4 6.1 %collective-permute-start.31 = (bf16[8,3072]{1,0:T(8,128)(2,1)S(1)}, bf16[8,3072]{1,0:T(8,128)(2,1)S(1)}, u32[]{:S(2)}, u32[]{:S(2)}) collective-permute-start(bf16[8,3072]{1,0:T(8,128)(2,1)S(1)} %get-tuple-element.79), channel_id=1, source_target_pairs={{0,24},{1,25},{2,26},{3,27},{4,28},{5,29},{6,30},{7,31},{8,16},{9,... | collective-permute-start | bytes 147464 | tf_op jit(solution)/shard_map/ppermute | solution.py:71
  (20 other events, 69.3 us)

commit v7 on v6

v7 whole, which is shorter than its diff:
```python
import functools

import jax
import jax.numpy as jnp
import numpy as np
from jax import lax
from jax.experimental import pallas as pl
from jax.experimental.pallas import tpu as pltpu
from jax.sharding import Mesh
from jax.sharding import PartitionSpec as P

score_scale = 192.0 ** (-0.5)
everyone = ("high", "middle", "core", "local")
MEBI = 1024 * 1024


def attention_kernel(lengths_ref, query_ref, query_rope_ref, cache_ref, cache_rope_ref, out_ref):
    for row in range(query_ref.shape[0]):
        cache = cache_ref[row]
        scores = lax.dot_general(
            query_ref[row], cache, (((1,), (1,)), ((), ())), preferred_element_type=jnp.float32
        )
        scores += jnp.dot(
            query_rope_ref[row], cache_rope_ref[row], preferred_element_type=jnp.float32
        )
        slot = lax.broadcasted_iota(jnp.int32, scores.shape, 1)
        in_range = slot < lengths_ref[row]
        scores = jnp.where(in_range, scores * score_scale, -jnp.inf)
        row_peak = jnp.max(scores, axis=1, keepdims=True)
        lifted = jnp.where(in_range, jnp.exp(scores - row_peak), 0.0)
        weights = (lifted / jnp.sum(lifted, axis=1, keepdims=True)).astype(jnp.bfloat16)
        value = jnp.dot(weights, cache, preferred_element_type=jnp.float32)
        out_ref[row] = value.astype(jnp.bfloat16)


def attention(query_latent, query_rope, cache_latent, cache_rope, cache_lengths):
    rows, heads, latent = query_latent.shape
    slots = cache_latent.shape[1]
    return pl.pallas_call(
        attention_kernel,
        in_specs=[pl.BlockSpec(memory_space=pltpu.SMEM)]
        + [pl.BlockSpec(memory_space=pltpu.VMEM)] * 4,
        out_specs=pl.BlockSpec(memory_space=pltpu.VMEM),
        out_shape=jax.ShapeDtypeStruct(query_latent.shape, jnp.bfloat16),
        cost_estimate=pl.CostEstimate(
            flops=4 * rows * heads * slots * latent,
            bytes_accessed=2 * rows * slots * latent,
            transcendentals=rows * heads * slots,
        ),
        compiler_params=pltpu.CompilerParams(vmem_limit_bytes=8 * MEBI),
        name="attention",
    )(cache_lengths, query_latent, query_rope, cache_latent, cache_rope)


class Grid:
    def __init__(self):
        self.sizes = tuple(lax.axis_size(name) for name in everyone)
        self.mixed = self.sizes[1] == self.sizes[3]

    def swap(self, value, pick, mask):
        pairs = []
        for place in np.ndindex(*self.sizes):
            other = list(place)
            other[pick(place[2])] ^= mask
            pairs.append(
                (
                    int(np.ravel_multi_index(place, self.sizes)),
                    int(np.ravel_multi_index(other, self.sizes)),
                )
            )
        return lax.ppermute(value, everyone, pairs)

    def high(self, core):
        return 0

    def core(self, core):
        return 2

    def first(self, core):
        return 1 if self.mixed and core == 1 else 3

    def second(self, core):
        return 3 if self.mixed and core == 1 else 1

    def extent(self, pick):
        return self.sizes[pick(0)]

    def masks(self):
        masks, m = [], self.extent(self.high) // 2
        while m:
            masks.append(m)
            m //= 2
        return masks

    def near(self, line):
        return [line] + [self.swap(line, self.first, m) for m in range(1, self.extent(self.first))]

    def far(self, near):
        return [
            self.swap(block, self.second, m)
            for m in range(1, self.extent(self.second))
            for block in near
        ]

    def other(self, mine):
        return [self.swap(block, self.core, 1) for block in mine]

    def last_sum(self, mine, other):
        return add([mine[-1], self.swap(other[0], self.core, 1)])

    def rest_sums(self, mine, other):
        size = mine[0].shape[0]
        rest = self.swap(other[1], self.core, 1)
        return [
            add([part, rest[i * size : (i + 1) * size]]) for i, part in enumerate(mine[:-1])
        ]

    def back(self, sums, place):
        return self.swap(sums[place], self.second, place // self.extent(self.first))

    def line_sum(self, sums, last):
        wide = self.extent(self.first)
        near = [[part] for part in sums[:wide]]
        for place in range(wide, len(sums)):
            moved = last if place == len(sums) - 1 else self.back(sums, place)
            near[place % wide].append(moved)
        near = [add(parts) for parts in near]
        return add([near[0]] + [self.swap(near[m], self.first, m) for m in range(1, wide)])

    def high_sum(self, line):
        for m in reversed(self.masks()):
            half = line.shape[0] // 2
            line = add([line[:half], self.swap(line[half:], self.high, m)])
        return line


def add(parts):
    total = parts[0].astype(jnp.float32)
    for part in parts[1:]:
        total = total + part.astype(jnp.float32)
    return total.astype(parts[0].dtype)


def join_kernel(*refs):
    refs[-1][...] = jnp.concatenate([ref[...] for ref in refs[:-1]], axis=0)


def join(parts):
    rows = sum(part.shape[0] for part in parts)
    return pl.pallas_call(
        join_kernel,
        in_specs=[pl.BlockSpec(memory_space=pltpu.VMEM)] * len(parts),
        out_specs=pl.BlockSpec(memory_space=pltpu.VMEM),
        out_shape=jax.ShapeDtypeStruct((rows, parts[0].shape[1]), parts[0].dtype),
        compiler_params=pltpu.CompilerParams(vmem_limit_bytes=2 * MEBI),
        name="join",
    )(*parts)


def cut_kernel(rows_ref, out_ref):
    out_ref[...] = rows_ref[:, : out_ref.shape[1]]


def cut(columns, moe_rows):
    return pl.pallas_call(
        cut_kernel,
        out_shape=jax.ShapeDtypeStruct((moe_rows.shape[0], columns), moe_rows.dtype),
        compiler_params=pltpu.CompilerParams(vmem_limit_bytes=2 * MEBI),
        name="cut",
    )(moe_rows)


def pack_kernel(experts, rows_ref, ids_ref, gates_ref, out_ref):
    extra = table_width(experts)
    width = out_ref.shape[1] - extra
    gates = gates_ref[...]
    shares = 2.5 * gates / jnp.sum(gates, axis=1, keepdims=True)
    ids = ids_ref[...]
    lane = lax.broadcasted_iota(jnp.int32, (ids.shape[0], extra), 1)
    expert = jnp.where(lane < experts, lane, lane - experts)
    table = jnp.zeros(lane.shape, jnp.float32)
    for k in range(ids.shape[1]):
        table += jnp.where(expert == ids[:, k : k + 1], shares[:, k : k + 1], 0.0)
    high = table.astype(jnp.bfloat16).astype(jnp.float32)
    table = jnp.where(lane < experts, high, jnp.where(lane < 2 * experts, table - high, 0.0))
    out_ref[:, :width] = rows_ref[:, rows_ref.shape[1] - width :]
    out_ref[:, width:] = table.astype(jnp.bfloat16)


def table_width(experts):
    return pl.cdiv(2 * experts, 128) * 128


def pack(columns, experts, moe_rows, route_ids, route_gates):
    total = columns + table_width(experts)
    return pl.pallas_call(
        functools.partial(pack_kernel, experts),
        out_shape=jax.ShapeDtypeStruct((moe_rows.shape[0], total), jnp.bfloat16),
        compiler_params=pltpu.CompilerParams(vmem_limit_bytes=2 * MEBI),
        name="pack",
    )(moe_rows, route_ids, route_gates)


def spread(product, outs):
    start = 0
    for out, columns in outs:
        size = out.shape[0]
        out[:, columns] = product[start : start + size]
        start += size


def in_hbm(weight):
    return pltpu.with_memory_space_constraint(weight, pltpu.HBM)


def fetch(source, target, sems, start, tile, dim):
    copies = []
    for k in range(0, target.shape[dim], tile):
        inside, outside = pl.ds(k, tile), pl.ds(start + k, tile)
        if dim == 1:
            inside, outside = (slice(None), inside), (slice(None), outside)
        copy = pltpu.make_async_copy(source.at[outside], target.at[inside], sems.at[k // tile])
        copy.start()
        copies.append(copy)
    return copies


def fetch_both(gate_hbm, up_hbm, gate, up, gate_sem, up_sem, start, tile):
    copies = []
    for k in range(0, gate.shape[0], tile):
        inside, outside = pl.ds(k, tile), pl.ds(start + k, tile)
        pair = (
            pltpu.make_async_copy(gate_hbm.at[outside], gate.at[inside], gate_sem.at[k // tile]),
            pltpu.make_async_copy(up_hbm.at[outside], up.at[inside], up_sem.at[k // tile]),
        )
        for copy in pair:
            copy.start()
        copies.append(pair)
    return copies


def project(blocks, copies, gate, up, gate_sum, up_sum, tile, fresh):
    for k, pair in enumerate(copies):
        part = pl.ds(k * tile, tile)
        rows = jnp.concatenate([block[:, part] for block in blocks], axis=0)
        for copy, weight, total in zip(pair, (gate, up), (gate_sum, up_sum)):
            copy.wait()
            product = jnp.dot(rows, weight[part], preferred_element_type=jnp.float32)
            if fresh and k == 0:
                total[...] = product
            else:
                total[...] += product


def first_kernel(count, tile, *refs):
    blocks = refs[:count]
    gate_hbm, up_hbm, gate_sum, up_sum, gate, up, gate_sem, up_sem = refs[count:]
    copies = fetch_both(gate_hbm, up_hbm, gate, up, gate_sem, up_sem, 0, tile)
    project(blocks, copies, gate, up, gate_sum, up_sum, tile, True)


def first_sums(blocks, w_gate, w_up):
    units = w_gate.shape[1]
    rows = sum(block.shape[0] for block in blocks)
    columns = blocks[0].shape[1]
    tile = 1024
    return pl.pallas_call(
        functools.partial(first_kernel, len(blocks), tile),
        in_specs=[pl.BlockSpec(memory_space=pltpu.VMEM)] * len(blocks)
        + [pl.BlockSpec(memory_space=pltpu.HBM)] * 2,
        out_specs=[pl.BlockSpec(memory_space=pltpu.VMEM)] * 2,
        out_shape=[jax.ShapeDtypeStruct((rows, units), jnp.float32)] * 2,
        scratch_shapes=[pltpu.VMEM((columns, units), jnp.bfloat16)] * 2
        + [pltpu.SemaphoreType.DMA((columns // tile,))] * 2,
        cost_estimate=pl.CostEstimate(
            flops=4 * rows * columns * units,
            bytes_accessed=4 * columns * units,
            transcendentals=0,
        ),
        compiler_params=pltpu.CompilerParams(vmem_limit_bytes=20 * MEBI),
        name="first_sums",
    )(*blocks, in_hbm(w_gate), in_hbm(w_up))


def expert_kernel(count, experts, tile, down_tile, node_ref, *refs):
    blocks = refs[:count]
    gate_in, up_in, gate_hbm, up_hbm, down_hbm, hidden_ref, share_ref = refs[count : count + 7]
    outs = refs[count + 7 : -8]
    gate, up, down, gate_sum, up_sum, gate_sem, up_sem, down_sem = refs[-8:]
    start = gate_hbm.shape[0] - gate.shape[0]
    copies = fetch_both(gate_hbm, up_hbm, gate, up, gate_sem, up_sem, start, tile)
    down_copies = fetch(down_hbm, down, down_sem, 0, down_tile, 1)

    table = jnp.concatenate([block[:, gate.shape[0] :] for block in blocks], axis=0)
    table = table.astype(jnp.float32)
    lane = lax.broadcasted_iota(jnp.int32, table.shape, 1)
    mine = (lane == node_ref[0]) | (lane == node_ref[0] + experts)
    share = jnp.sum(jnp.where(mine, table, 0.0), axis=1, keepdims=True)
    share_ref[...] = jnp.broadcast_to(share, share_ref.shape)
    gate_sum[...] = gate_in[...]
    up_sum[...] = up_in[...]
    project(blocks, copies, gate, up, gate_sum, up_sum, tile, False)
    hidden_ref[...] = (jax.nn.silu(gate_sum[...]) * up_sum[...]).astype(jnp.bfloat16)
    for k, copy in enumerate(down_copies):
        part = pl.ds(k * down_tile, down_tile)
        copy.wait()
        product = jnp.dot(hidden_ref[...], down[:, part], preferred_element_type=jnp.float32)
        product = (product * share_ref[:, :1]).astype(jnp.bfloat16)
        spread(product, [(out, part) for out in outs])


def expert(blocks, sums, w_gate, w_up, w_down, experts, node, sizes, columns):
    units = w_gate.shape[1]
    rows = sum(sizes)
    tail = blocks[0].shape[1] - table_width(experts)
    tile, down_tile = 1024, 512
    return pl.pallas_call(
        functools.partial(expert_kernel, len(blocks), experts, tile, down_tile),
        in_specs=[pl.BlockSpec(memory_space=pltpu.SMEM)]
        + [pl.BlockSpec(memory_space=pltpu.VMEM)] * (len(blocks) + 2)
        + [pl.BlockSpec(memory_space=pltpu.HBM)] * 3,
        out_specs=[pl.BlockSpec(memory_space=pltpu.VMEM)] * (2 + len(sizes)),
        out_shape=[
            jax.ShapeDtypeStruct((rows, units), jnp.bfloat16),
            jax.ShapeDtypeStruct((rows, 128), jnp.float32),
        ]
        + [jax.ShapeDtypeStruct((size, columns), jnp.bfloat16) for size in sizes],
        scratch_shapes=[
            pltpu.VMEM((tail, units), jnp.bfloat16),
            pltpu.VMEM((tail, units), jnp.bfloat16),
            pltpu.VMEM((units, columns), jnp.bfloat16),
            pltpu.VMEM((rows, units), jnp.float32),
            pltpu.VMEM((rows, units), jnp.float32),
            pltpu.SemaphoreType.DMA((tail // tile,)),
            pltpu.SemaphoreType.DMA((tail // tile,)),
            pltpu.SemaphoreType.DMA((columns // down_tile,)),
        ],
        cost_estimate=pl.CostEstimate(
            flops=4 * rows * tail * units + 2 * rows * columns * units,
            bytes_accessed=4 * tail * units + 2 * units * columns,
            transcendentals=rows * units,
        ),
        compiler_params=pltpu.CompilerParams(vmem_limit_bytes=24 * MEBI),
        name="expert",
    )(node, *blocks, *sums, in_hbm(w_gate), in_hbm(w_up), in_hbm(w_down))


def down_kernel(start, tile, hidden_ref, share_ref, down_hbm, *refs):
    outs = refs[:-2]
    down, down_sem = refs[-2:]
    for k, copy in enumerate(fetch(down_hbm, down, down_sem, start, tile, 1)):
        part = pl.ds(k * tile, tile)
        copy.wait()
        product = jnp.dot(hidden_ref[...], down[:, part], preferred_element_type=jnp.float32)
        product = (product * share_ref[:, :1]).astype(jnp.bfloat16)
        spread(product, [(out, part) for out in outs])


def down_of(hidden, share, w_down, sizes, start):
    rows, units = hidden.shape
    columns = w_down.shape[1] - start
    tile = 512
    return pl.pallas_call(
        functools.partial(down_kernel, start, tile),
        in_specs=[pl.BlockSpec(memory_space=pltpu.VMEM)] * 2
        + [pl.BlockSpec(memory_space=pltpu.HBM)],
        out_specs=[pl.BlockSpec(memory_space=pltpu.VMEM)] * len(sizes),
        out_shape=[jax.ShapeDtypeStruct((size, columns), jnp.bfloat16) for size in sizes],
        scratch_shapes=[
            pltpu.VMEM((units, columns), jnp.bfloat16),
            pltpu.SemaphoreType.DMA((columns // tile,)),
        ],
        cost_estimate=pl.CostEstimate(
            flops=2 * rows * columns * units,
            bytes_accessed=2 * columns * (units + rows),
            transcendentals=0,
        ),
        compiler_params=pltpu.CompilerParams(vmem_limit_bytes=12 * MEBI),
        name="down",
    )(hidden, share, in_hbm(w_down))


def body(
    moe_rows,
    route_ids,
    route_gates,
    w_gate,
    w_up,
    w_down,
    query_latent,
    query_rope,
    cache_latent,
    cache_rope,
    cache_lengths,
):
    grid = Grid()
    high, middle, cores, _ = grid.sizes
    experts = high * middle * cores
    tokens, width = moe_rows.shape
    node = lax.axis_index(("high", "middle", "core")).astype(jnp.int32).reshape(1)
    split = width * 4 // 7
    tied = lax.optimization_barrier
    attn_latent = attention(query_latent, query_rope, cache_latent, cache_rope, cache_lengths)

    head = cut(split, moe_rows)
    tail = pack(width - split, experts, moe_rows, route_ids, route_gates)
    masks = grid.masks()
    came = grid.swap(head, grid.high, masks[0])
    tail, came = tied((tail, came))
    head = join([head, came])
    for m in masks[1:]:
        head = join([head, grid.swap(head, grid.high, m)])
    head, attn_latent = tied((head, attn_latent))
    for m in masks:
        tail = join([tail, grid.swap(tail, grid.high, m)])
    head_near = grid.near(head)
    tail, head_near[-1] = tied((tail, head_near[-1]))
    head_far = grid.far(head_near)
    tail_near = grid.near(tail)
    tail_near[-1], head_far[-1] = tied((tail_near[-1], head_far[-1]))
    tail_far = grid.far(tail_near)
    mine = head_near + head_far
    other = grid.other(mine)
    gate_sum, up_sum = first_sums(mine + other[-1:] + other[:-1], w_gate[0], w_up[0])
    tail_far[-1], gate_sum, up_sum = tied((tail_far[-1], gate_sum, up_sum))
    mine = tail_near + tail_far
    other = grid.other(mine)
    size, count = high * tokens, len(mine)
    sizes = [size] * count + [size, size * (count - 1)]
    hidden, share, *products = expert(
        mine + other[-1:] + other[:-1],
        (gate_sum, up_sum),
        w_gate[0],
        w_up[0],
        w_down[0],
        experts,
        node,
        sizes,
        split,
    )

    lower, lower_other = products[:count], products[count:]
    last = grid.last_sum(lower, lower_other)
    hidden, last = tied((hidden, last))
    products = down_of(hidden, share, w_down[0], sizes, split)
    sums = grid.rest_sums(lower, lower_other) + [last]
    came = grid.back(sums, count - 1)
    products, came = tied((products, came))
    upper, upper_other = products[:count], products[count:]
    last = grid.last_sum(upper, upper_other)
    line = grid.line_sum(sums, came)
    sums = grid.rest_sums(upper, upper_other)
    came = grid.back(sums + [last], count - 1)
    sums, came, line = tied((sums, came, line))
    lower = grid.high_sum(line)
    upper = grid.high_sum(grid.line_sum(sums + [last], came))
    return (jnp.concatenate([lower, upper], axis=1), attn_latent)


def solution(mesh):
    groups, nodes, local = mesh.devices.shape
    split = Mesh(mesh.devices.reshape(groups, nodes // 4, 2, 2, local), ("group",) + everyone)
    node = ("high", "middle", "core")
    whole = ("group",) + everyone
    rows = P(whole, None)
    blocks = P(whole, None, None)
    return jax.shard_map(
        body,
        mesh=split,
        in_specs=(
            rows,
            rows,
            rows,
            P(node, None, "local"),
            P(node, None, "local"),
            P(node, "local", None),
            blocks,
            blocks,
            blocks,
            blocks,
            P(whole),
        ),
        out_specs=(rows, blocks),
        check_vma=False,
    )
```

time: 101 us -> 95.3 us (0.944)
  local copies, waits for them, and re-layouts: 19 us -> 6.74 us
  waiting for transfers between devices: 28.3 us -> 37.3 us
  Pallas kernels: 21 us -> 16.8 us
  starting transfers between devices: 30 us -> 31.9 us
    unnamed x24 -> x16, local copies, waits for them, and re-layouts: 19 us -> 6.71 us
    ppermute x32, waiting for transfers between devices: 28.3 us -> 37.3 us  [swap(): return lax.ppermute(value, everyone, pairs)]
    pallas_call x5 -> x4, Pallas kernels: 16.8 us -> 14.2 us  [the longest x1 7.01 us: expert(): pl.pallas_call(functools.partial(expert_kernel, len(blocks), experts, til...]
    ppermute x32, starting transfers between devices: 30 us -> 31.9 us  [swap(): return lax.ppermute(value, everyone, pairs)]
    pallas_call x1, Pallas kernels: 1.75 us -> 0.18 us  [pack(): pl.pallas_call(functools.partial(pack_kernel, experts), out_shape=jax.Sha...]
  transfers between devices with their start and end apart: 32 -> 32, of which waited for: 10 -> 15; matrix products, arithmetic and copies ran while one was open for 1% -> 1% of each run, Pallas kernels for 12% -> 10%
where the time goes in v7:
time: 95.3 us; the launch traced here: 95 us
  waiting for transfers between devices  37.3 us (39%)
  starting transfers between devices  31.9 us (33%)
  Pallas kernels  16.8 us (18%)
  local copies, waits for them, and re-layouts  6.74 us (7%)
  other arithmetic  1.43 us (2%)
    ppermute x32, waiting for transfers between devices, swap(): return lax.ppermute(value, everyone, pairs)  37.3 us
    ppermute x32, starting transfers between devices, swap(): return lax.ppermute(value, everyone, pairs)  31.9 us
    pallas_call x1, Pallas kernels, expert(): pl.pallas_call(functools.partial(expert_kernel, len(blocks), experts, til...  7.01 us
    unnamed x16, local copies, waits for them, and re-layouts  6.71 us
    pallas_call x1, Pallas kernels, first_sums(): pl.pallas_call(functools.partial(first_kernel, len(blocks), tile), in_spe...  4.21 us
    pallas_call x1, Pallas kernels, down_of(): pl.pallas_call(functools.partial(down_kernel, start, tile), in_specs=[pl....  2.95 us
    pallas_call x1, Pallas kernels, attention(): pl.pallas_call(attention_kernel, in_specs=[pl.BlockSpec(memory_space=pltp...  2.36 us
  transfers between devices with their start and end apart: 32, of which 15 were waited for; matrix products, arithmetic and copies ran while one was open for 1% of the time, Pallas kernels for 10%

profile of v7, /device:TPU:0, one launch (start us, length us, event | category | flops | bytes accessed | tf_op | source)
XLA Modules:
  0.0 95.0 jit_solution(18018467595818002642)
XLA Ops:
  1.5 4.0 %collective-permute-start = (bf16[8,4096]{1,0:T(8,128)(2,1)S(1)}, bf16[8,4096]{1,0:T(8,128)(2,1)S(1)}, u32[]{:S(2)}, u32[]{:S(2)}) collective-permute-start(bf16[8,4096]{1,0:T(8,128)(2,1)S(1)} %cut.1.refs_0_), channel_id=1, source_target_pairs={{0,16},{1,17},{2,18},{3,19},{4,20},{5,21},{6,22},{7,23},{8,24},{9,... | collective-permute-start | bytes 196616 | tf_op jit(solution)/shard_map/ppermute | solution.py:71
  7.1 2.1 %collective-permute-done.refs_1_ = bf16[8,4096]{1,0:T(8,128)(2,1)S(1)} collective-permute-done((bf16[8,4096]{1,0:T(8,128)(2,1)S(1)}, bf16[8,4096]{1,0:T(8,128)(2,1)S(1)}, u32[]{:S(2)}, u32[]{:S(2)}) %collective-permute-start) | collective-permute-done | bytes 65568 | tf_op jit(solution)/shard_map/ppermute | solution.py:71
  14.3 2.4 %attention.1 = bf16[2,64,512]{2,1,0:T(8,128)(2,1)} custom-call(s32[2]{0:T(128)S(1)} %copy-done.7, bf16[2,64,512]{2,1,0:T(8,128)(2,1)S(1)} %copy-done.2, bf16[2,64,64]{2,1,0:T(8,128)(2,1)S(1)} %copy-done.4, bf16[2,512,512]{2,1,0:T(8,128)(2,1)S(1)} %copy-done, bf16[2,64,512]{2,1,0:T(8,128)(2,1)S(1)} %copy-done.3), custom_call_target="tpu_custom_call" | custom-call | flops 134217728 | bytes 1048576 | tf_op jit(solution)/shard_map/attention/pallas_call | solution.py:39
  16.7 1.6 %collective-permute-start.4 = (bf16[32,4096]{1,0:T(8,128)(2,1)S(1)}, bf16[32,4096]{1,0:T(8,128)(2,1)S(1)}, u32[]{:S(2)}, u32[]{:S(2)}) collective-permute-start(bf16[32,4096]{1,0:T(8,128)(2,1)S(1)} %join.7.refs_0_), channel_id=1, source_target_pairs={{0,1},{1,0},{2,6},{3,7},{4,5},{5,4},{6,2},{7,3},{8,9},{9,8},{10,14... | collective-permute-start | bytes 786440 | tf_op jit(solution)/shard_map/ppermute | solution.py:71
  18.3 3.4 %collective-permute-start.1 = (bf16[8,3200]{1,0:T(8,128)(2,1)S(1)}, bf16[8,3200]{1,0:T(8,128)(2,1)S(1)}, u32[]{:S(2)}, u32[]{:S(2)}) collective-permute-start(bf16[8,3200]{1,0:T(8,128)(2,1)S(1)} %pack.1.refs_0_), channel_id=1, source_target_pairs={{0,16},{1,17},{2,18},{3,19},{4,20},{5,21},{6,22},{7,23},{8,24},{9,... | collective-permute-start | bytes 153608 | tf_op jit(solution)/shard_map/ppermute | solution.py:71
  21.7 2.1 %collective-permute-done.1.refs_1_ = bf16[8,3200]{1,0:T(8,128)(2,1)S(1)} collective-permute-done((bf16[8,3200]{1,0:T(8,128)(2,1)S(1)}, bf16[8,3200]{1,0:T(8,128)(2,1)S(1)}, u32[]{:S(2)}, u32[]{:S(2)}) %collective-permute-start.1) | collective-permute-done | bytes 51232 | tf_op jit(solution)/shard_map/ppermute | solution.py:71
  26.6 2.0 %collective-permute-done.2.refs_1_ = bf16[16,3200]{1,0:T(8,128)(2,1)S(1)} collective-permute-done((bf16[16,3200]{1,0:T(8,128)(2,1)S(1)}, bf16[16,3200]{1,0:T(8,128)(2,1)S(1)}, u32[]{:S(2)}, u32[]{:S(2)}) %collective-permute-start.2) | collective-permute-done | bytes 102432 | tf_op jit(solution)/shard_map/ppermute | solution.py:71
  28.6 1.5 %collective-permute-start.6 = (bf16[32,4096]{1,0:T(8,128)(2,1)S(1)}, bf16[32,4096]{1,0:T(8,128)(2,1)S(1)}, u32[]{:S(2)}, u32[]{:S(2)}) collective-permute-start(bf16[32,4096]{1,0:T(8,128)(2,1)S(1)} %collective-permute-done.4.refs_1_), channel_id=1, source_target_pairs={{0,4},{1,5},{2,3},{3,2},{4,0},{5,1},{6,7},{7,6},{8,12},{9,13},{10,... | collective-permute-start | bytes 786440 | tf_op jit(solution)/shard_map/ppermute | solution.py:71
  32.6 3.2 %collective-permute-done.5.refs_1_ = bf16[32,3200]{1,0:T(8,128)(2,1)S(1)} collective-permute-done((bf16[32,3200]{1,0:T(8,128)(2,1)S(1)}, bf16[32,3200]{1,0:T(8,128)(2,1)S(1)}, u32[]{:S(2)}, u32[]{:S(2)}) %collective-permute-start.5) | collective-permute-done | bytes 204832 | tf_op jit(solution)/shard_map/ppermute | solution.py:71
  38.4 3.7 %collective-permute-done.7.refs_2_ = bf16[32,3200]{1,0:T(8,128)(2,1)S(1)} collective-permute-done((bf16[32,3200]{1,0:T(8,128)(2,1)S(1)}, bf16[32,3200]{1,0:T(8,128)(2,1)S(1)}, u32[]{:S(2)}, u32[]{:S(2)}) %collective-permute-start.7) | collective-permute-done | bytes 204832 | tf_op jit(solution)/shard_map/ppermute | solution.py:71
  42.8 4.2 %first_sums.1 = (f32[256,512]{1,0:T(8,128)S(1)}, f32[256,512]{1,0:T(8,128)S(1)}) custom-call(bf16[32,4096]{1,0:T(8,128)(2,1)S(1)} %join.7.refs_0_, bf16[32,4096]{1,0:T(8,128)(2,1)S(1)} %collective-permute-done.4.refs_1_, bf16[32,4096]{1,0:T(8,128)(2,1)S(1)} %collective-permute-done.9.refs_2_, bf16[32,4096]{1,0:T(8,128)(2,1)S(1)} %collective-permute-done.6.refs_3_, ...), custom_call_target="tpu_custom_call" | custom-call | flops 2147483648 | bytes 8388608 | tf_op jit(solution)/shard_map/first_sums/pallas_call | solution.py:267
  48.6 7.0 %expert.1 = (bf16[256,512]{1,0:T(8,128)(2,1)S(1)}, f32[256,128]{1,0:T(8,128)S(1)}, bf16[32,4096]{1,0:T(8,128)(2,1)S(1)}, bf16[32,4096]{1,0:T(8,128)(2,1)S(1)}, b...) custom-call(s32[1]{0:T(128)} %bitcast.node_ref, ...), custom_call_target="tpu_custom_call" | custom-call | flops 2684354560 | bytes 10485760 | tf_op jit(solution)/shard_map/expert/pallas_call | solution.py:317
  57.3 1.6 %collective-permute-start.19 = (bf16[32,4096]{1,0:T(8,128)(2,1)S(1)}, bf16[32,4096]{1,0:T(8,128)(2,1)S(1)}, u32[]{:S(2)}, u32[]{:S(2)}) collective-permute-start(bf16[32,4096]{1,0:T(8,128)(2,1)S(1)} %add_convert_fusion.6), channel_id=1, source_target_pairs={{0,4},{1,5},{2,3},{3,2},{4,0},{5,1},{6,7},{7,6},{8,12},{9,13},{10,... | collective-permute-start | bytes 786440 | tf_op jit(solution)/shard_map/ppermute | solution.py:71
  58.9 2.9 %down.1 = (bf16[32,3072]{1,0:T(8,128)(2,1)S(1)}, bf16[32,3072]{1,0:T(8,128)(2,1)S(1)}, bf16[32,3072]{1,0:T(8,128)(2,1)S(1)}, bf16[32,3072]{1,0:T(8,128)(2,1)S(1)...) custom-call(bf16[256,512]{1,0:T(8,128)(2,1)S(1)} %get-tuple-element.58.hidden_ref, ...), custom_call_target="tpu_custom_call" | custom-call | flops 805306368 | bytes 4718592 | tf_op jit(solution)/shard_map/down/pallas_call | solution.py:363
  61.8 1.9 %collective-permute-done.19 = bf16[32,4096]{1,0:T(8,128)(2,1)S(1)} collective-permute-done((bf16[32,4096]{1,0:T(8,128)(2,1)S(1)}, bf16[32,4096]{1,0:T(8,128)(2,1)S(1)}, u32[]{:S(2)}, u32[]{:S(2)}) %collective-permute-start.19) | collective-permute-done | bytes 262176 | tf_op jit(solution)/shard_map/ppermute | solution.py:71
  64.4 1.6 %collective-permute-start.24 = (bf16[32,4096]{1,0:T(8,128)(2,1)S(1)}, bf16[32,4096]{1,0:T(8,128)(2,1)S(1)}, u32[]{:S(2)}, u32[]{:S(2)}) collective-permute-start(bf16[32,4096]{1,0:T(8,128)(2,1)S(1)} %get-tuple-element.84), channel_id=1, source_target_pairs={{0,4},{1,5},{2,3},{3,2},{4,0},{5,1},{6,7},{7,6},{8,12},{9,13},{10,... | collective-permute-start | bytes 786440 | tf_op jit(solution)/shard_map/ppermute | solution.py:71
  67.0 5.8 %collective-permute-done.24 = bf16[32,4096]{1,0:T(8,128)(2,1)S(1)} collective-permute-done((bf16[32,4096]{1,0:T(8,128)(2,1)S(1)}, bf16[32,4096]{1,0:T(8,128)(2,1)S(1)}, u32[]{:S(2)}, u32[]{:S(2)}) %collective-permute-start.24) | collective-permute-done | bytes 262176 | tf_op jit(solution)/shard_map/ppermute | solution.py:71
  72.8 2.0 %collective-permute-done.25 = bf16[32,4096]{1,0:T(8,128)(2,1)S(1)} collective-permute-done((bf16[32,4096]{1,0:T(8,128)(2,1)S(1)}, bf16[32,4096]{1,0:T(8,128)(2,1)S(1)}, u32[]{:S(2)}, u32[]{:S(2)}) %collective-permute-start.25) | collective-permute-done | bytes 262176 | tf_op jit(solution)/shard_map/ppermute | solution.py:71
  76.3 1.6 %collective-permute-start.28 = (bf16[32,3072]{1,0:T(8,128)(2,1)S(1)}, bf16[32,3072]{1,0:T(8,128)(2,1)S(1)}, u32[]{:S(2)}, u32[]{:S(2)}) collective-permute-start(bf16[32,3072]{1,0:T(8,128)(2,1)S(1)} %get-tuple-element.80), channel_id=1, source_target_pairs={{0,4},{1,5},{2,3},{3,2},{4,0},{5,1},{6,7},{7,6},{8,12},{9,13},{10,... | collective-permute-start | bytes 589832 | tf_op jit(solution)/shard_map/ppermute | solution.py:71
  78.8 4.1 %collective-permute-done.29 = bf16[32,3072]{1,0:T(8,128)(2,1)S(1)} collective-permute-done((bf16[32,3072]{1,0:T(8,128)(2,1)S(1)}, bf16[32,3072]{1,0:T(8,128)(2,1)S(1)}, u32[]{:S(2)}, u32[]{:S(2)}) %collective-permute-start.29) | collective-permute-done | bytes 196640 | tf_op jit(solution)/shard_map/ppermute | solution.py:71
  84.1 2.0 %collective-permute-start.27 = (bf16[8,4096]{1,0:T(8,128)(2,1)S(1)}, bf16[8,4096]{1,0:T(8,128)(2,1)S(1)}, u32[]{:S(2)}, u32[]{:S(2)}) collective-permute-start(bf16[8,4096]{1,0:T(8,128)(2,1)S(1)} %slice.63), channel_id=1, source_target_pairs={{0,16},{1,17},{2,18},{3,19},{4,20},{5,21},{6,22},{7,23},{8,24},{9,... | collective-permute-start | bytes 196616 | tf_op jit(solution)/shard_map/ppermute | solution.py:71
  86.1 2.5 %collective-permute-done.30 = bf16[16,3072]{1,0:T(8,128)(2,1)S(1)} collective-permute-done((bf16[16,3072]{1,0:T(8,128)(2,1)S(1)}, bf16[16,3072]{1,0:T(8,128)(2,1)S(1)}, u32[]{:S(2)}, u32[]{:S(2)}) %collective-permute-start.30) | collective-permute-done | bytes 98336 | tf_op jit(solution)/shard_map/ppermute | solution.py:71
  88.7 1.8 %collective-permute-start.31 = (bf16[8,3072]{1,0:T(8,128)(2,1)S(1)}, bf16[8,3072]{1,0:T(8,128)(2,1)S(1)}, u32[]{:S(2)}, u32[]{:S(2)}) collective-permute-start(bf16[8,3072]{1,0:T(8,128)(2,1)S(1)} %slice.67), channel_id=1, source_target_pairs={{0,16},{1,17},{2,18},{3,19},{4,20},{5,21},{6,22},{7,23},{8,24},{9,... | collective-permute-start | bytes 147464 | tf_op jit(solution)/shard_map/ppermute | solution.py:71
  90.5 3.8 %collective-permute-done.31 = bf16[8,3072]{1,0:T(8,128)(2,1)S(1)} collective-permute-done((bf16[8,3072]{1,0:T(8,128)(2,1)S(1)}, bf16[8,3072]{1,0:T(8,128)(2,1)S(1)}, u32[]{:S(2)}, u32[]{:S(2)}) %collective-permute-start.31) | collective-permute-done | bytes 49184 | tf_op jit(solution)/shard_map/ppermute | solution.py:71
  (82 shorter events, 25.3 us)
Async XLA Ops:
  1.5 7.7 %collective-permute-start = (bf16[8,4096]{1,0:T(8,128)(2,1)S(1)}, bf16[8,4096]{1,0:T(8,128)(2,1)S(1)}, u32[]{:S(2)}, u32[]{:S(2)}) collective-permute-start(bf16[8,4096]{1,0:T(8,128)(2,1)S(1)} %cut.1.refs_0_), channel_id=1, source_target_pairs={{0,16},{1,17},{2,18},{3,19},{4,20},{5,21},{6,22},{7,23},{8,24},{9,... | collective-permute-start | bytes 196616 | tf_op jit(solution)/shard_map/ppermute | solution.py:71
  9.2 7.4 %collective-permute-start.3 = (bf16[16,4096]{1,0:T(8,128)(2,1)S(1)}, bf16[16,4096]{1,0:T(8,128)(2,1)S(1)}, u32[]{:S(2)}, u32[]{:S(2)}) collective-permute-start(bf16[16,4096]{1,0:T(8,128)(2,1)S(1)} %join.6.refs_0_), channel_id=1, source_target_pairs={{0,8},{1,9},{2,10},{3,11},{4,12},{5,13},{6,14},{7,15},{8,0},{9,1},... | collective-permute-start | bytes 393224 | tf_op jit(solution)/shard_map/ppermute | solution.py:71
  16.7 11.8 %collective-permute-start.4 = (bf16[32,4096]{1,0:T(8,128)(2,1)S(1)}, bf16[32,4096]{1,0:T(8,128)(2,1)S(1)}, u32[]{:S(2)}, u32[]{:S(2)}) collective-permute-start(bf16[32,4096]{1,0:T(8,128)(2,1)S(1)} %join.7.refs_0_), channel_id=1, source_target_pairs={{0,1},{1,0},{2,6},{3,7},{4,5},{5,4},{6,2},{7,3},{8,9},{9,8},{10,14... | collective-permute-start | bytes 786440 | tf_op jit(solution)/shard_map/ppermute | solution.py:71
  25.0 7.6 %collective-permute-start.9 = (bf16[32,4096]{1,0:T(8,128)(2,1)S(1)}, bf16[32,4096]{1,0:T(8,128)(2,1)S(1)}, u32[]{:S(2)}, u32[]{:S(2)}) collective-permute-start(bf16[32,4096]{1,0:T(8,128)(2,1)S(1)} %join.7.refs_0_), channel_id=1, source_target_pairs={{0,4},{1,5},{2,3},{3,2},{4,0},{5,1},{6,7},{7,6},{8,12},{9,13},{10,... | collective-permute-start | bytes 786440 | tf_op jit(solution)/shard_map/ppermute | solution.py:71
  28.6 7.8 %collective-permute-start.6 = (bf16[32,4096]{1,0:T(8,128)(2,1)S(1)}, bf16[32,4096]{1,0:T(8,128)(2,1)S(1)}, u32[]{:S(2)}, u32[]{:S(2)}) collective-permute-start(bf16[32,4096]{1,0:T(8,128)(2,1)S(1)} %collective-permute-done.4.refs_1_), channel_id=1, source_target_pairs={{0,4},{1,5},{2,3},{3,2},{4,0},{5,1},{6,7},{7,6},{8,12},{9,13},{10,... | collective-permute-start | bytes 786440 | tf_op jit(solution)/shard_map/ppermute | solution.py:71
  30.1 5.8 %collective-permute-start.5 = (bf16[32,3200]{1,0:T(8,128)(2,1)S(1)}, bf16[32,3200]{1,0:T(8,128)(2,1)S(1)}, u32[]{:S(2)}, u32[]{:S(2)}) collective-permute-start(bf16[32,3200]{1,0:T(8,128)(2,1)S(1)} %join.5.refs_0_), channel_id=1, source_target_pairs={{0,1},{1,0},{2,6},{3,7},{4,5},{5,4},{6,2},{7,3},{8,9},{9,8},{10,14... | collective-permute-start | bytes 614408 | tf_op jit(solution)/shard_map/ppermute | solution.py:71
  30.7 7.2 %collective-permute-start.11 = (bf16[32,4096]{1,0:T(8,128)(2,1)S(1)}, bf16[32,4096]{1,0:T(8,128)(2,1)S(1)}, u32[]{:S(2)}, u32[]{:S(2)}) collective-permute-start(bf16[32,4096]{1,0:T(8,128)(2,1)S(1)} %join.7.refs_0_), channel_id=1, source_target_pairs={{0,2},{1,3},{2,0},{3,1},{4,6},{5,7},{6,4},{7,5},{8,10},{9,11},{10,... | collective-permute-start | bytes 786440 | tf_op jit(solution)/shard_map/ppermute | solution.py:71
  30.7 12.0 %collective-permute-start.12 = (bf16[32,4096]{1,0:T(8,128)(2,1)S(1)}, bf16[32,4096]{1,0:T(8,128)(2,1)S(1)}, u32[]{:S(2)}, u32[]{:S(2)}) collective-permute-start(bf16[32,4096]{1,0:T(8,128)(2,1)S(1)} %collective-permute-done.4.refs_1_), channel_id=1, source_target_pairs={{0,2},{1,3},{2,0},{3,1},{4,6},{5,7},{6,4},{7,5},{8,10},{9,11},{10,... | collective-permute-start | bytes 786440 | tf_op jit(solution)/shard_map/ppermute | solution.py:71
  32.6 9.5 %collective-permute-start.13 = (bf16[32,4096]{1,0:T(8,128)(2,1)S(1)}, bf16[32,4096]{1,0:T(8,128)(2,1)S(1)}, u32[]{:S(2)}, u32[]{:S(2)}) collective-permute-start(bf16[32,4096]{1,0:T(8,128)(2,1)S(1)} %collective-permute-done.9.refs_2_), channel_id=1, source_target_pairs={{0,2},{1,3},{2,0},{3,1},{4,6},{5,7},{6,4},{7,5},{8,10},{9,11},{10,... | collective-permute-start | bytes 786440 | tf_op jit(solution)/shard_map/ppermute | solution.py:71
  36.4 6.4 %collective-permute-start.10 = (bf16[32,4096]{1,0:T(8,128)(2,1)S(1)}, bf16[32,4096]{1,0:T(8,128)(2,1)S(1)}, u32[]{:S(2)}, u32[]{:S(2)}) collective-permute-start(bf16[32,4096]{1,0:T(8,128)(2,1)S(1)} %collective-permute-done.6.refs_3_), channel_id=1, source_target_pairs={{0,2},{1,3},{2,0},{3,1},{4,6},{5,7},{6,4},{7,5},{8,10},{9,11},{10,... | collective-permute-start | bytes 786440 | tf_op jit(solution)/shard_map/ppermute | solution.py:71
  36.4 5.8 %collective-permute-start.7 = (bf16[32,3200]{1,0:T(8,128)(2,1)S(1)}, bf16[32,3200]{1,0:T(8,128)(2,1)S(1)}, u32[]{:S(2)}, u32[]{:S(2)}) collective-permute-start(bf16[32,3200]{1,0:T(8,128)(2,1)S(1)} %join.5.refs_0_), channel_id=1, source_target_pairs={{0,4},{1,5},{2,3},{3,2},{4,0},{5,1},{6,7},{7,6},{8,12},{9,13},{10,... | collective-permute-start | bytes 614408 | tf_op jit(solution)/shard_map/ppermute | solution.py:71
  37.9 9.0 %collective-permute-start.8 = (bf16[32,3200]{1,0:T(8,128)(2,1)S(1)}, bf16[32,3200]{1,0:T(8,128)(2,1)S(1)}, u32[]{:S(2)}, u32[]{:S(2)}) collective-permute-start(bf16[32,3200]{1,0:T(8,128)(2,1)S(1)} %collective-permute-done.5.refs_1_), channel_id=1, source_target_pairs={{0,4},{1,5},{2,3},{3,2},{4,0},{5,1},{6,7},{7,6},{8,12},{9,13},{10,... | collective-permute-start | bytes 614408 | tf_op jit(solution)/shard_map/ppermute | solution.py:71
  56.0 8.2 %collective-permute-start.23 = (bf16[96,4096]{1,0:T(8,128)(2,1)S(1)}, bf16[96,4096]{1,0:T(8,128)(2,1)S(1)}, u32[]{:S(2)}, u32[]{:S(2)}) collective-permute-start(bf16[96,4096]{1,0:T(8,128)(2,1)S(1)} %get-tuple-element.74), channel_id=1, source_target_pairs={{0,2},{1,3},{2,0},{3,1},{4,6},{5,7},{6,4},{7,5},{8,10},{9,11},{10,... | collective-permute-start | bytes 2359304 | tf_op jit(solution)/shard_map/ppermute | solution.py:71
  57.3 6.4 %collective-permute-start.19 = (bf16[32,4096]{1,0:T(8,128)(2,1)S(1)}, bf16[32,4096]{1,0:T(8,128)(2,1)S(1)}, u32[]{:S(2)}, u32[]{:S(2)}) collective-permute-start(bf16[32,4096]{1,0:T(8,128)(2,1)S(1)} %add_convert_fusion.6), channel_id=1, source_target_pairs={{0,4},{1,5},{2,3},{3,2},{4,0},{5,1},{6,7},{7,6},{8,12},{9,13},{10,... | collective-permute-start | bytes 786440 | tf_op jit(solution)/shard_map/ppermute | solution.py:71
  63.7 11.2 %collective-permute-start.20 = (bf16[96,3072]{1,0:T(8,128)(2,1)S(1)}, bf16[96,3072]{1,0:T(8,128)(2,1)S(1)}, u32[]{:S(2)}, u32[]{:S(2)}) collective-permute-start(bf16[96,3072]{1,0:T(8,128)(2,1)S(1)} %get-tuple-element.68), channel_id=1, source_target_pairs={{0,2},{1,3},{2,0},{3,1},{4,6},{5,7},{6,4},{7,5},{8,10},{9,11},{10,... | collective-permute-start | bytes 1769480 | tf_op jit(solution)/shard_map/ppermute | solution.py:71
  64.4 8.4 %collective-permute-start.24 = (bf16[32,4096]{1,0:T(8,128)(2,1)S(1)}, bf16[32,4096]{1,0:T(8,128)(2,1)S(1)}, u32[]{:S(2)}, u32[]{:S(2)}) collective-permute-start(bf16[32,4096]{1,0:T(8,128)(2,1)S(1)} %get-tuple-element.84), channel_id=1, source_target_pairs={{0,4},{1,5},{2,3},{3,2},{4,0},{5,1},{6,7},{7,6},{8,12},{9,13},{10,... | collective-permute-start | bytes 786440 | tf_op jit(solution)/shard_map/ppermute | solution.py:71
  66.0 8.8 %collective-permute-start.25 = (bf16[32,4096]{1,0:T(8,128)(2,1)S(1)}, bf16[32,4096]{1,0:T(8,128)(2,1)S(1)}, u32[]{:S(2)}, u32[]{:S(2)}) collective-permute-start(bf16[32,4096]{1,0:T(8,128)(2,1)S(1)} %get-tuple-element.85), channel_id=1, source_target_pairs={{0,1},{1,0},{2,6},{3,7},{4,5},{5,4},{6,2},{7,3},{8,9},{9,8},{10,14... | collective-permute-start | bytes 786440 | tf_op jit(solution)/shard_map/ppermute | solution.py:71
  66.6 8.5 %collective-permute-start.22 = (bf16[32,3072]{1,0:T(8,128)(2,1)S(1)}, bf16[32,3072]{1,0:T(8,128)(2,1)S(1)}, u32[]{:S(2)}, u32[]{:S(2)}) collective-permute-start(bf16[32,3072]{1,0:T(8,128)(2,1)S(1)} %add_convert_fusion.10), channel_id=1, source_target_pairs={{0,4},{1,5},{2,3},{3,2},{4,0},{5,1},{6,7},{7,6},{8,12},{9,13},{10,... | collective-permute-start | bytes 589832 | tf_op jit(solution)/shard_map/ppermute | solution.py:71
  75.2 7.8 %collective-permute-start.29 = (bf16[32,3072]{1,0:T(8,128)(2,1)S(1)}, bf16[32,3072]{1,0:T(8,128)(2,1)S(1)}, u32[]{:S(2)}, u32[]{:S(2)}) collective-permute-start(bf16[32,3072]{1,0:T(8,128)(2,1)S(1)} %add_convert_fusion.8), channel_id=1, source_target_pairs={{0,1},{1,0},{2,6},{3,7},{4,5},{5,4},{6,2},{7,3},{8,9},{9,8},{10,14... | collective-permute-start | bytes 589832 | tf_op jit(solution)/shard_map/ppermute | solution.py:71
  76.3 6.6 %collective-permute-start.28 = (bf16[32,3072]{1,0:T(8,128)(2,1)S(1)}, bf16[32,3072]{1,0:T(8,128)(2,1)S(1)}, u32[]{:S(2)}, u32[]{:S(2)}) collective-permute-start(bf16[32,3072]{1,0:T(8,128)(2,1)S(1)} %get-tuple-element.80), channel_id=1, source_target_pairs={{0,4},{1,5},{2,3},{3,2},{4,0},{5,1},{6,7},{7,6},{8,12},{9,13},{10,... | collective-permute-start | bytes 589832 | tf_op jit(solution)/shard_map/ppermute | solution.py:71
  77.9 6.1 %collective-permute-start.26 = (bf16[16,4096]{1,0:T(8,128)(2,1)S(1)}, bf16[16,4096]{1,0:T(8,128)(2,1)S(1)}, u32[]{:S(2)}, u32[]{:S(2)}) collective-permute-start(bf16[16,4096]{1,0:T(8,128)(2,1)S(1)} %slice.49), channel_id=1, source_target_pairs={{0,8},{1,9},{2,10},{3,11},{4,12},{5,13},{6,14},{7,15},{8,0},{9,1},... | collective-permute-start | bytes 393224 | tf_op jit(solution)/shard_map/ppermute | solution.py:71
  83.0 5.6 %collective-permute-start.30 = (bf16[16,3072]{1,0:T(8,128)(2,1)S(1)}, bf16[16,3072]{1,0:T(8,128)(2,1)S(1)}, u32[]{:S(2)}, u32[]{:S(2)}) collective-permute-start(bf16[16,3072]{1,0:T(8,128)(2,1)S(1)} %slice.65), channel_id=1, source_target_pairs={{0,8},{1,9},{2,10},{3,11},{4,12},{5,13},{6,14},{7,15},{8,0},{9,1},... | collective-permute-start | bytes 294920 | tf_op jit(solution)/shard_map/ppermute | solution.py:71
  84.1 6.4 %collective-permute-start.27 = (bf16[8,4096]{1,0:T(8,128)(2,1)S(1)}, bf16[8,4096]{1,0:T(8,128)(2,1)S(1)}, u32[]{:S(2)}, u32[]{:S(2)}) collective-permute-start(bf16[8,4096]{1,0:T(8,128)(2,1)S(1)} %slice.63), channel_id=1, source_target_pairs={{0,16},{1,17},{2,18},{3,19},{4,20},{5,21},{6,22},{7,23},{8,24},{9,... | collective-permute-start | bytes 196616 | tf_op jit(solution)/shard_map/ppermute | solution.py:71
  88.7 5.6 %collective-permute-start.31 = (bf16[8,3072]{1,0:T(8,128)(2,1)S(1)}, bf16[8,3072]{1,0:T(8,128)(2,1)S(1)}, u32[]{:S(2)}, u32[]{:S(2)}) collective-permute-start(bf16[8,3072]{1,0:T(8,128)(2,1)S(1)} %slice.67), channel_id=1, source_target_pairs={{0,16},{1,17},{2,18},{3,19},{4,20},{5,21},{6,22},{7,23},{8,24},{9,... | collective-permute-start | bytes 147464 | tf_op jit(solution)/shard_map/ppermute | solution.py:71
  (16 other events, 38.4 us)

commit v8 on v7

--- a/solution.py
+++ b/solution.py
@@ -14,8 +14,22 @@
 MEBI = 1024 * 1024
 
 
-def attention_kernel(lengths_ref, query_ref, query_rope_ref, cache_ref, cache_rope_ref, out_ref):
-    for row in range(query_ref.shape[0]):
+def attention_kernel(lengths_ref, *refs):
+    sources, (out_ref, *targets), sems = refs[:4], refs[4:-1], refs[-1]
+    query_ref, query_rope_ref, cache_ref, cache_rope_ref = targets
+    copies = []
+    for row in range(out_ref.shape[0]):
+        copies.append(
+            [
+                pltpu.make_async_copy(source.at[row], target.at[row], sems.at[row, i])
+                for i, (source, target) in enumerate(zip(sources, targets))
+            ]
+        )
+        for copy in copies[-1]:
+            copy.start()
+    for row in range(out_ref.shape[0]):
+        for copy in copies[row]:
+            copy.wait()
         cache = cache_ref[row]
         scores = lax.dot_general(
             query_ref[row], cache, (((1,), (1,)), ((), ())), preferred_element_type=jnp.float32
@@ -36,12 +50,15 @@
 def attention(query_latent, query_rope, cache_latent, cache_rope, cache_lengths):
     rows, heads, latent = query_latent.shape
     slots = cache_latent.shape[1]
+    sources = (query_latent, query_rope, cache_latent, cache_rope)
     return pl.pallas_call(
         attention_kernel,
         in_specs=[pl.BlockSpec(memory_space=pltpu.SMEM)]
-        + [pl.BlockSpec(memory_space=pltpu.VMEM)] * 4,
+        + [pl.BlockSpec(memory_space=pltpu.HBM)] * 4,
         out_specs=pl.BlockSpec(memory_space=pltpu.VMEM),
         out_shape=jax.ShapeDtypeStruct(query_latent.shape, jnp.bfloat16),
+        scratch_shapes=[pltpu.VMEM(source.shape, source.dtype) for source in sources]
+        + [pltpu.SemaphoreType.DMA((rows, 4))],
         cost_estimate=pl.CostEstimate(
             flops=4 * rows * heads * slots * latent,
             bytes_accessed=2 * rows * slots * latent,
@@ -49,7 +66,11 @@
         ),
         compiler_params=pltpu.CompilerParams(vmem_limit_bytes=8 * MEBI),
         name="attention",
-    )(cache_lengths, query_latent, query_rope, cache_latent, cache_rope)
+    )(cache_lengths, *[in_hbm(source) for source in sources])
+
+
+def in_hbm(array):
+    return pltpu.with_memory_space_constraint(array, pltpu.HBM)
 
 
 class Grid:
@@ -92,40 +113,21 @@
             m //= 2
         return masks
 
-    def near(self, line):
+    def over_first(self, line):
         return [line] + [self.swap(line, self.first, m) for m in range(1, self.extent(self.first))]
 
-    def far(self, near):
-        return [
-            self.swap(block, self.second, m)
-            for m in range(1, self.extent(self.second))
-            for block in near
-        ]
-
-    def other(self, mine):
-        return [self.swap(block, self.core, 1) for block in mine]
-
-    def last_sum(self, mine, other):
-        return add([mine[-1], self.swap(other[0], self.core, 1)])
-
-    def rest_sums(self, mine, other):
-        size = mine[0].shape[0]
-        rest = self.swap(other[1], self.core, 1)
-        return [
-            add([part, rest[i * size : (i + 1) * size]]) for i, part in enumerate(mine[:-1])
-        ]
-
-    def back(self, sums, place):
-        return self.swap(sums[place], self.second, place // self.extent(self.first))
-
-    def line_sum(self, sums, last):
-        wide = self.extent(self.first)
-        near = [[part] for part in sums[:wide]]
-        for place in range(wide, len(sums)):
-            moved = last if place == len(sums) - 1 else self.back(sums, place)
-            near[place % wide].append(moved)
-        near = [add(parts) for parts in near]
-        return add([near[0]] + [self.swap(near[m], self.first, m) for m in range(1, wide)])
+    def over_second(self, near):
+        return [near] + [self.swap(near, self.second, m) for m in range(1, self.extent(self.second))]
+
+    def second_sum(self, parts):
+        return add(parts[:1] + [self.swap(parts[m], self.second, m) for m in range(1, len(parts))])
+
+    def first_sum(self, near):
+        rows = near.shape[0] // self.extent(self.first)
+        parts = [near[:rows]]
+        for m in range(1, self.extent(self.first)):
+            parts.append(self.swap(near[m * rows : (m + 1) * rows], self.first, m))
+        return add(parts)
 
     def high_sum(self, line):
         for m in reversed(self.masks()):
@@ -133,6 +135,16 @@
             line = add([line[:half], self.swap(line[half:], self.high, m)])
         return line
 
+    def high_sum_direct(self, line):
+        order = [0]
+        for m in self.masks():
+            order += [m | other for other in order]
+        rows = line.shape[0] // len(order)
+        parts = [line[:rows]]
+        for i in range(1, len(order)):
+            parts.append(self.swap(line[i * rows : (i + 1) * rows], self.high, order[i]))
+        return add(parts)
+
 
 def add(parts):
     total = parts[0].astype(jnp.float32)
@@ -141,33 +153,26 @@
     return total.astype(parts[0].dtype)
 
 
-def join_kernel(*refs):
-    refs[-1][...] = jnp.concatenate([ref[...] for ref in refs[:-1]], axis=0)
-
-
-def join(parts):
+def join_kernel(count, *refs):
+    start = 0
+    for out in refs[count:]:
+        columns = pl.ds(start, out.shape[1])
+        out[...] = jnp.concatenate([ref[:, columns] for ref in refs[:count]], axis=0)
+        start += out.shape[1]
+
+
+def join(parts, *widths):
     rows = sum(part.shape[0] for part in parts)
-    return pl.pallas_call(
-        join_kernel,
+    widths = widths or parts[0].shape[1:]
+    outs = pl.pallas_call(
+        functools.partial(join_kernel, len(parts)),
         in_specs=[pl.BlockSpec(memory_space=pltpu.VMEM)] * len(parts),
-        out_specs=pl.BlockSpec(memory_space=pltpu.VMEM),
-        out_shape=jax.ShapeDtypeStruct((rows, parts[0].shape[1]), parts[0].dtype),
+        out_specs=[pl.BlockSpec(memory_space=pltpu.VMEM)] * len(widths),
+        out_shape=[jax.ShapeDtypeStruct((rows, width), parts[0].dtype) for width in widths],
         compiler_params=pltpu.CompilerParams(vmem_limit_bytes=2 * MEBI),
         name="join",
     )(*parts)
-
-
-def cut_kernel(rows_ref, out_ref):
-    out_ref[...] = rows_ref[:, : out_ref.shape[1]]
-
-
-def cut(columns, moe_rows):
-    return pl.pallas_call(
-        cut_kernel,
-        out_shape=jax.ShapeDtypeStruct((moe_rows.shape[0], columns), moe_rows.dtype),
-        compiler_params=pltpu.CompilerParams(vmem_limit_bytes=2 * MEBI),
-        name="cut",
-    )(moe_rows)
+    return outs if len(widths) > 1 else outs[0]
 
 
 def pack_kernel(experts, rows_ref, ids_ref, gates_ref, out_ref):
@@ -183,7 +188,7 @@
         table += jnp.where(expert == ids[:, k : k + 1], shares[:, k : k + 1], 0.0)
     high = table.astype(jnp.bfloat16).astype(jnp.float32)
     table = jnp.where(lane < experts, high, jnp.where(lane < 2 * experts, table - high, 0.0))
-    out_ref[:, :width] = rows_ref[:, rows_ref.shape[1] - width :]
+    out_ref[:, :width] = rows_ref[...]
     out_ref[:, width:] = table.astype(jnp.bfloat16)
 
 
@@ -191,8 +196,8 @@
     return pl.cdiv(2 * experts, 128) * 128
 
 
-def pack(columns, experts, moe_rows, route_ids, route_gates):
-    total = columns + table_width(experts)
+def pack(experts, moe_rows, route_ids, route_gates):
+    total = moe_rows.shape[1] + table_width(experts)
     return pl.pallas_call(
         functools.partial(pack_kernel, experts),
         out_shape=jax.ShapeDtypeStruct((moe_rows.shape[0], total), jnp.bfloat16),
@@ -207,10 +212,6 @@
         size = out.shape[0]
         out[:, columns] = product[start : start + size]
         start += size
-
-
-def in_hbm(weight):
-    return pltpu.with_memory_space_constraint(weight, pltpu.HBM)
 
 
 def fetch(source, target, sems, start, tile, dim):
@@ -284,9 +285,9 @@
 
 def expert_kernel(count, experts, tile, down_tile, node_ref, *refs):
     blocks = refs[:count]
-    gate_in, up_in, gate_hbm, up_hbm, down_hbm, hidden_ref, share_ref = refs[count : count + 7]
-    outs = refs[count + 7 : -8]
-    gate, up, down, gate_sum, up_sum, gate_sem, up_sem, down_sem = refs[-8:]
+    gate_in, up_in, gate_hbm, up_hbm, down_hbm = refs[count : count + 5]
+    outs = refs[count + 5 : -10]
+    hidden_ref, share_ref, gate, up, down, gate_sum, up_sum, gate_sem, up_sem, down_sem = refs[-10:]
     start = gate_hbm.shape[0] - gate.shape[0]
     copies = fetch_both(gate_hbm, up_hbm, gate, up, gate_sem, up_sem, start, tile)
     down_copies = fetch(down_hbm, down, down_sem, 0, down_tile, 1)
@@ -306,11 +307,16 @@
         copy.wait()
         product = jnp.dot(hidden_ref[...], down[:, part], preferred_element_type=jnp.float32)
         product = (product * share_ref[:, :1]).astype(jnp.bfloat16)
-        spread(product, [(out, part) for out in outs])
-
-
-def expert(blocks, sums, w_gate, w_up, w_down, experts, node, sizes, columns):
-    units = w_gate.shape[1]
+        start = k * down_tile
+        for chunk in (outs[: len(outs) // 2], outs[len(outs) // 2 :]):
+            if 0 <= start < chunk[0].shape[1]:
+                spread(product, [(out, pl.ds(start, down_tile)) for out in chunk])
+            start -= chunk[0].shape[1]
+
+
+def expert(blocks, sums, w_gate, w_up, w_down, experts, node, split):
+    units, columns = w_down.shape
+    sizes = [block.shape[0] for block in blocks]
     rows = sum(sizes)
     tail = blocks[0].shape[1] - table_width(experts)
     tile, down_tile = 1024, 512
@@ -319,13 +325,15 @@
         in_specs=[pl.BlockSpec(memory_space=pltpu.SMEM)]
         + [pl.BlockSpec(memory_space=pltpu.VMEM)] * (len(blocks) + 2)
         + [pl.BlockSpec(memory_space=pltpu.HBM)] * 3,
-        out_specs=[pl.BlockSpec(memory_space=pltpu.VMEM)] * (2 + len(sizes)),
+        out_specs=[pl.BlockSpec(memory_space=pltpu.VMEM)] * (2 * len(sizes)),
         out_shape=[
-            jax.ShapeDtypeStruct((rows, units), jnp.bfloat16),
-            jax.ShapeDtypeStruct((rows, 128), jnp.float32),
-        ]
-        + [jax.ShapeDtypeStruct((size, columns), jnp.bfloat16) for size in sizes],
+            jax.ShapeDtypeStruct((size, chunk), jnp.bfloat16)
+            for chunk in (split, columns - split)
+            for size in sizes
+        ],
         scratch_shapes=[
+            pltpu.VMEM((rows, units), jnp.bfloat16),
+            pltpu.VMEM((rows, 128), jnp.float32),
             pltpu.VMEM((tail, units), jnp.bfloat16),
             pltpu.VMEM((tail, units), jnp.bfloat16),
             pltpu.VMEM((units, columns), jnp.bfloat16),
@@ -343,41 +351,6 @@
         compiler_params=pltpu.CompilerParams(vmem_limit_bytes=24 * MEBI),
         name="expert",
     )(node, *blocks, *sums, in_hbm(w_gate), in_hbm(w_up), in_hbm(w_down))
-
-
-def down_kernel(start, tile, hidden_ref, share_ref, down_hbm, *refs):
-    outs = refs[:-2]
-    down, down_sem = refs[-2:]
-    for k, copy in enumerate(fetch(down_hbm, down, down_sem, start, tile, 1)):
-        part = pl.ds(k * tile, tile)
-        copy.wait()
-        product = jnp.dot(hidden_ref[...], down[:, part], preferred_element_type=jnp.float32)
-        product = (product * share_ref[:, :1]).astype(jnp.bfloat16)
-        spread(product, [(out, part) for out in outs])
-
-
-def down_of(hidden, share, w_down, sizes, start):
-    rows, units = hidden.shape
-    columns = w_down.shape[1] - start
-    tile = 512
-    return pl.pallas_call(
-        functools.partial(down_kernel, start, tile),
-        in_specs=[pl.BlockSpec(memory_space=pltpu.VMEM)] * 2
-        + [pl.BlockSpec(memory_space=pltpu.HBM)],
-        out_specs=[pl.BlockSpec(memory_space=pltpu.VMEM)] * len(sizes),
-        out_shape=[jax.ShapeDtypeStruct((size, columns), jnp.bfloat16) for size in sizes],
-        scratch_shapes=[
-            pltpu.VMEM((units, columns), jnp.bfloat16),
-            pltpu.SemaphoreType.DMA((columns // tile,)),
-        ],
-        cost_estimate=pl.CostEstimate(
-            flops=2 * rows * columns * units,
-            bytes_accessed=2 * columns * (units + rows),
-            transcendentals=0,
-        ),
-        compiler_params=pltpu.CompilerParams(vmem_limit_bytes=12 * MEBI),
-        name="down",
-    )(hidden, share, in_hbm(w_down))
 
 
 def body(
@@ -402,59 +375,38 @@
     tied = lax.optimization_barrier
     attn_latent = attention(query_latent, query_rope, cache_latent, cache_rope, cache_lengths)
 
-    head = cut(split, moe_rows)
-    tail = pack(width - split, experts, moe_rows, route_ids, route_gates)
+    line = pack(experts, moe_rows, route_ids, route_gates)
     masks = grid.masks()
-    came = grid.swap(head, grid.high, masks[0])
-    tail, came = tied((tail, came))
-    head = join([head, came])
-    for m in masks[1:]:
-        head = join([head, grid.swap(head, grid.high, m)])
-    head, attn_latent = tied((head, attn_latent))
-    for m in masks:
-        tail = join([tail, grid.swap(tail, grid.high, m)])
-    head_near = grid.near(head)
-    tail, head_near[-1] = tied((tail, head_near[-1]))
-    head_far = grid.far(head_near)
-    tail_near = grid.near(tail)
-    tail_near[-1], head_far[-1] = tied((tail_near[-1], head_far[-1]))
-    tail_far = grid.far(tail_near)
-    mine = head_near + head_far
-    other = grid.other(mine)
-    gate_sum, up_sum = first_sums(mine + other[-1:] + other[:-1], w_gate[0], w_up[0])
-    tail_far[-1], gate_sum, up_sum = tied((tail_far[-1], gate_sum, up_sum))
-    mine = tail_near + tail_far
-    other = grid.other(mine)
-    size, count = high * tokens, len(mine)
-    sizes = [size] * count + [size, size * (count - 1)]
-    hidden, share, *products = expert(
-        mine + other[-1:] + other[:-1],
-        (gate_sum, up_sum),
-        w_gate[0],
-        w_up[0],
-        w_down[0],
-        experts,
-        node,
-        sizes,
-        split,
+    for m in masks[:-1]:
+        line = join([line, grid.swap(line, grid.high, m)])
+    came = grid.swap(line, grid.high, masks[-1])
+    came, attn_latent = tied((came, attn_latent))
+    head, tail = join([line, came], split, line.shape[1] - split)
+    head, tail = grid.over_first(head), grid.over_first(tail)
+    head = grid.over_second(join(head))
+    tail = join(tail)
+    tail, head[0] = tied((tail, head[0]))
+    tail = grid.over_second(tail)
+    head += [grid.swap(block, grid.core, 1) for block in head]
+    gate_sum, up_sum = first_sums(head, w_gate[0], w_up[0])
+    tail[-1], gate_sum, up_sum = tied((tail[-1], gate_sum, up_sum))
+    tail += [grid.swap(block, grid.core, 1) for block in tail]
+    count = len(tail) // 2
+    products = expert(
+        tail, (gate_sum, up_sum), w_gate[0], w_up[0], w_down[0], experts, node, split
     )
 
-    lower, lower_other = products[:count], products[count:]
-    last = grid.last_sum(lower, lower_other)
-    hidden, last = tied((hidden, last))
-    products = down_of(hidden, share, w_down[0], sizes, split)
-    sums = grid.rest_sums(lower, lower_other) + [last]
-    came = grid.back(sums, count - 1)
-    products, came = tied((products, came))
-    upper, upper_other = products[:count], products[count:]
-    last = grid.last_sum(upper, upper_other)
-    line = grid.line_sum(sums, came)
-    sums = grid.rest_sums(upper, upper_other)
-    came = grid.back(sums + [last], count - 1)
-    sums, came, line = tied((sums, came, line))
-    lower = grid.high_sum(line)
-    upper = grid.high_sum(grid.line_sum(sums + [last], came))
-    return (jnp.concatenate([lower, upper], axis=1), attn_latent)
+    def core_sum(parts):
+        sums = [add([parts[i], grid.swap(parts[count + i], grid.core, 1)]) for i in range(1, count)]
+        return [add([parts[0], grid.swap(parts[count], grid.core, 1)])] + sums
+
+    head, tail = products[: 2 * count], products[2 * count :]
+    tail, head = tied((tail, core_sum(head)))
+    head = grid.second_sum(head)
+    tail = grid.second_sum(core_sum(tail))
+    head = grid.high_sum(grid.first_sum(head))
+    tail = grid.high_sum_direct(grid.first_sum(tail))
+    return (jnp.concatenate([head, tail], axis=1), attn_latent)
 
 
 def solution(mesh):

time: 95.3 us -> 95.9 us (level)
  waiting for transfers between devices: 37.3 us -> 44.7 us
  starting transfers between devices: 31.9 us -> 27.4 us
  local copies, waits for them, and re-layouts: 6.74 us -> 2.98 us
  Pallas kernels: 16.8 us -> 18.4 us
    ppermute x32 -> x23, waiting for transfers between devices: 37.3 us -> 44.7 us  [swap(): return lax.ppermute(value, everyone, pairs)]
    ppermute x32 -> x23, starting transfers between devices: 31.9 us -> 27.4 us  [swap(): return lax.ppermute(value, everyone, pairs)]
    unnamed x16 -> x8, local copies, waits for them, and re-layouts: 6.71 us -> 2.92 us
    pallas_call x1, Pallas kernels: 7.01 us -> 10.2 us  [expert(): pl.pallas_call(functools.partial(expert_kernel, len(blocks), experts, til...]
    pallas_call x6 -> x4, Pallas kernels: 3.02 us -> 0.13 us  [join(): pl.pallas_call(functools.partial(join_kernel, len(parts)), in_specs=[pl.B...]
    pallas_call x1, Pallas kernels: 2.36 us -> 3.66 us  [attention(): pl.pallas_call(attention_kernel, in_specs=[pl.BlockSpec(memory_space=pltp...]
  transfers between devices with their start and end apart: 32 -> 23, of which waited for: 15 -> 16; matrix products, arithmetic and copies ran while one was open for 1% -> 1% of each run, Pallas kernels for 10% -> 8%
where the time goes in v8:
time: 95.9 us; the launch traced here: 95.7 us
  waiting for transfers between devices  44.7 us (47%)
  starting transfers between devices  27.4 us (29%)
  Pallas kernels  18.4 us (19%)
  local copies, waits for them, and re-layouts  2.98 us (3%)
  other arithmetic  1.45 us (2%)
    ppermute x23, waiting for transfers between devices, swap(): return lax.ppermute(value, everyone, pairs)  44.7 us
    ppermute x23, starting transfers between devices, swap(): return lax.ppermute(value, everyone, pairs)  27.4 us
    pallas_call x1, Pallas kernels, expert(): pl.pallas_call(functools.partial(expert_kernel, len(blocks), experts, til...  10.2 us
    pallas_call x1, Pallas kernels, first_sums(): pl.pallas_call(functools.partial(first_kernel, len(blocks), tile), in_spe...  4.21 us
    pallas_call x1, Pallas kernels, attention(): pl.pallas_call(attention_kernel, in_specs=[pl.BlockSpec(memory_space=pltp...  3.66 us
    unnamed x8, local copies, waits for them, and re-layouts  2.92 us
  transfers between devices with their start and end apart: 23, of which 16 were waited for; matrix products, arithmetic and copies ran while one was open for 1% of the time, Pallas kernels for 8%

profile of v8, /device:TPU:0, one launch (start us, length us, event | category | flops | bytes accessed | tf_op | source)
XLA Modules:
  0.0 95.7 jit_solution(17815687596066074947)
XLA Ops:
  3.1 4.1 %collective-permute-start = (bf16[8,7296]{1,0:T(8,128)(2,1)S(1)}, bf16[8,7296]{1,0:T(8,128)(2,1)S(1)}, u32[]{:S(2)}, u32[]{:S(2)}) collective-permute-start(bf16[8,7296]{1,0:T(8,128)(2,1)S(1)} %pack.1.refs_0_), channel_id=1, source_target_pairs={{0,16},{1,17},{2,18},{3,19},{4,20},{5,21},{6,22},{7,23},{8,24},{9,... | collective-permute-start | bytes 350216 | tf_op jit(solution)/shard_map/ppermute | solution.py:92
  7.2 5.7 %collective-permute-done.refs_1_ = bf16[8,7296]{1,0:T(8,128)(2,1)S(1)} collective-permute-done((bf16[8,7296]{1,0:T(8,128)(2,1)S(1)}, bf16[8,7296]{1,0:T(8,128)(2,1)S(1)}, u32[]{:S(2)}, u32[]{:S(2)}) %collective-permute-start) | collective-permute-done | bytes 116768 | tf_op jit(solution)/shard_map/ppermute | solution.py:92
  14.4 3.7 %attention.1 = bf16[2,64,512]{2,1,0:T(8,128)(2,1)} custom-call(s32[2]{0:T(128)S(1)} %copy-done.3, bf16[2,64,512]{2,1,0:T(8,128)(2,1)} %refs_0_.1, bf16[2,64,64]{2,1,0:T(8,128)(2,1)} %refs_1_.1, bf16[2,512,512]{2,1,0:T(8,128)(2,1)} %refs_2_.1, bf16[2,64,512]{2,1,0:T(8,128)(2,1)} %refs_3_.1), custom_call_target="tpu_custom_call" | custom-call | flops 134217728 | bytes 1048576 | tf_op jit(solution)/shard_map/attention/pallas_call | solution.py:54
  18.0 1.8 %collective-permute-done.1.refs_1_ = bf16[16,7296]{1,0:T(8,128)(2,1)S(1)} collective-permute-done((bf16[16,7296]{1,0:T(8,128)(2,1)S(1)}, bf16[16,7296]{1,0:T(8,128)(2,1)S(1)}, u32[]{:S(2)}, u32[]{:S(2)}) %collective-permute-start.1) | collective-permute-done | bytes 233504 | tf_op jit(solution)/shard_map/ppermute | solution.py:92
  21.2 5.1 %collective-permute-done.3.refs_1_ = bf16[32,4096]{1,0:T(8,128)(2,1)S(1)} collective-permute-done((bf16[32,4096]{1,0:T(8,128)(2,1)S(1)}, bf16[32,4096]{1,0:T(8,128)(2,1)S(1)}, u32[]{:S(2)}, u32[]{:S(2)}) %collective-permute-start.3) | collective-permute-done | bytes 262176 | tf_op jit(solution)/shard_map/ppermute | solution.py:92
  26.4 1.3 %collective-permute-start.5 = (bf16[64,4096]{1,0:T(8,128)(2,1)S(1)}, bf16[64,4096]{1,0:T(8,128)(2,1)S(1)}, u32[]{:S(2)}, u32[]{:S(2)}) collective-permute-start(bf16[64,4096]{1,0:T(8,128)(2,1)S(1)} %join.7.refs_0_), channel_id=1, source_target_pairs={{0,4},{1,5},{2,3},{3,2},{4,0},{5,1},{6,7},{7,6},{8,12},{9,13},{10,... | collective-permute-start | bytes 1572872 | tf_op jit(solution)/shard_map/ppermute | solution.py:92
  27.7 1.5 %collective-permute-start.2 = (bf16[32,3200]{1,0:T(8,128)(2,1)S(1)}, bf16[32,3200]{1,0:T(8,128)(2,1)S(1)}, u32[]{:S(2)}, u32[]{:S(2)}) collective-permute-start(bf16[32,3200]{1,0:T(8,128)(2,1)S(1)} %get-tuple-element.28.refs_0_), channel_id=1, source_target_pairs={{0,1},{1,0},{2,6},{3,7},{4,5},{5,4},{6,2},{7,3},{8,9},{9,8},{10,14... | collective-permute-start | bytes 614408 | tf_op jit(solution)/shard_map/ppermute | solution.py:92
  29.2 5.1 %collective-permute-done.2.refs_1_ = bf16[32,3200]{1,0:T(8,128)(2,1)S(1)} collective-permute-done((bf16[32,3200]{1,0:T(8,128)(2,1)S(1)}, bf16[32,3200]{1,0:T(8,128)(2,1)S(1)}, u32[]{:S(2)}, u32[]{:S(2)}) %collective-permute-start.2) | collective-permute-done | bytes 204832 | tf_op jit(solution)/shard_map/ppermute | solution.py:92
  37.5 4.2 %first_sums.1 = (f32[256,512]{1,0:T(8,128)S(1)}, f32[256,512]{1,0:T(8,128)S(1)}) custom-call(bf16[64,4096]{1,0:T(8,128)(2,1)S(1)} %join.7.refs_0_, bf16[64,4096]{1,0:T(8,128)(2,1)S(1)} %collective-permute-done.5.refs_1_, bf16[64,4096]{1,0:T(8,128)(2,1)S(1)} %collective-permute-done.6.refs_2_, bf16[64,4096]{1,0:T(8,128)(2,1)S(1)} %collective-permute-done.7.refs_3_, ...), custom_call_target="tpu_custom_call" | custom-call | flops 2147483648 | bytes 8388608 | tf_op jit(solution)/shard_map/first_sums/pallas_call | solution.py:268
  41.8 1.8 %collective-permute-done.4.refs_1_ = bf16[64,3200]{1,0:T(8,128)(2,1)S(1)} collective-permute-done((bf16[64,3200]{1,0:T(8,128)(2,1)S(1)}, bf16[64,3200]{1,0:T(8,128)(2,1)S(1)}, u32[]{:S(2)}, u32[]{:S(2)}) %collective-permute-start.4) | collective-permute-done | bytes 409632 | tf_op jit(solution)/shard_map/ppermute | solution.py:92
  43.6 1.7 %collective-permute-done.9.refs_3_ = bf16[64,3200]{1,0:T(8,128)(2,1)S(1)} collective-permute-done((bf16[64,3200]{1,0:T(8,128)(2,1)S(1)}, bf16[64,3200]{1,0:T(8,128)(2,1)S(1)}, u32[]{:S(2)}, u32[]{:S(2)}) %collective-permute-start.9) | collective-permute-done | bytes 409632 | tf_op jit(solution)/shard_map/ppermute | solution.py:92
  45.3 10.2 %expert.1 = (bf16[64,4096]{1,0:T(8,128)(2,1)S(1)}, bf16[64,4096]{1,0:T(8,128)(2,1)S(1)}, bf16[64,4096]{1,0:T(8,128)(2,1)S(1)}, bf16[64,4096]{1,0:T(8,128)(2,1)S(...) custom-call(s32[1]{0:T(128)} %bitcast.node_ref, ...), custom_call_target="tpu_custom_call" | custom-call | flops 3489660928 | bytes 13631488 | tf_op jit(solution)/shard_map/expert/pallas_call | solution.py:323
  56.1 1.4 %collective-permute-done.10 = bf16[64,4096]{1,0:T(8,128)(2,1)S(1)} collective-permute-done((bf16[64,4096]{1,0:T(8,128)(2,1)S(1)}, bf16[64,4096]{1,0:T(8,128)(2,1)S(1)}, u32[]{:S(2)}, u32[]{:S(2)}) %collective-permute-start.10) | collective-permute-done | bytes 524320 | tf_op jit(solution)/shard_map/ppermute | solution.py:92
  58.4 1.3 %collective-permute-start.12 = (bf16[64,4096]{1,0:T(8,128)(2,1)S(1)}, bf16[64,4096]{1,0:T(8,128)(2,1)S(1)}, u32[]{:S(2)}, u32[]{:S(2)}) collective-permute-start(bf16[64,4096]{1,0:T(8,128)(2,1)S(1)} %add_convert_fusion.1), channel_id=1, source_target_pairs={{0,4},{1,5},{2,3},{3,2},{4,0},{5,1},{6,7},{7,6},{8,12},{9,13},{10,... | collective-permute-start | bytes 1572872 | tf_op jit(solution)/shard_map/ppermute | solution.py:92
  60.2 7.4 %collective-permute-done.12 = bf16[64,4096]{1,0:T(8,128)(2,1)S(1)} collective-permute-done((bf16[64,4096]{1,0:T(8,128)(2,1)S(1)}, bf16[64,4096]{1,0:T(8,128)(2,1)S(1)}, u32[]{:S(2)}, u32[]{:S(2)}) %collective-permute-start.12) | collective-permute-done | bytes 524320 | tf_op jit(solution)/shard_map/ppermute | solution.py:92
  69.2 1.6 %collective-permute-start.18 = (bf16[64,3072]{1,0:T(8,128)(2,1)S(1)}, bf16[64,3072]{1,0:T(8,128)(2,1)S(1)}, u32[]{:S(2)}, u32[]{:S(2)}) collective-permute-start(bf16[64,3072]{1,0:T(8,128)(2,1)S(1)} %add_convert_fusion.4), channel_id=1, source_target_pairs={{0,4},{1,5},{2,3},{3,2},{4,0},{5,1},{6,7},{7,6},{8,12},{9,13},{10,... | collective-permute-start | bytes 1179656 | tf_op jit(solution)/shard_map/ppermute | solution.py:92
  70.8 6.2 %collective-permute-done.13 = bf16[32,4096]{1,0:T(8,128)(2,1)S(1)} collective-permute-done((bf16[32,4096]{1,0:T(8,128)(2,1)S(1)}, bf16[32,4096]{1,0:T(8,128)(2,1)S(1)}, u32[]{:S(2)}, u32[]{:S(2)}) %collective-permute-start.13) | collective-permute-done | bytes 262176 | tf_op jit(solution)/shard_map/ppermute | solution.py:92
  77.0 2.3 %collective-permute-start.14 = (bf16[16,4096]{1,0:T(8,128)(2,1)S(1)}, bf16[16,4096]{1,0:T(8,128)(2,1)S(1)}, u32[]{:S(2)}, u32[]{:S(2)}) collective-permute-start(bf16[16,4096]{1,0:T(8,128)(2,1)S(1)} %slice.51), channel_id=1, source_target_pairs={{0,8},{1,9},{2,10},{3,11},{4,12},{5,13},{6,14},{7,15},{8,0},{9,1},... | collective-permute-start | bytes 393224 | tf_op jit(solution)/shard_map/ppermute | solution.py:92
  80.4 1.9 %collective-permute-done.14 = bf16[16,4096]{1,0:T(8,128)(2,1)S(1)} collective-permute-done((bf16[16,4096]{1,0:T(8,128)(2,1)S(1)}, bf16[16,4096]{1,0:T(8,128)(2,1)S(1)}, u32[]{:S(2)}, u32[]{:S(2)}) %collective-permute-start.14) | collective-permute-done | bytes 131104 | tf_op jit(solution)/shard_map/ppermute | solution.py:92
  82.4 4.7 %collective-permute-start.15 = (bf16[8,4096]{1,0:T(8,128)(2,1)S(1)}, bf16[8,4096]{1,0:T(8,128)(2,1)S(1)}, u32[]{:S(2)}, u32[]{:S(2)}) collective-permute-start(bf16[8,4096]{1,0:T(8,128)(2,1)S(1)} %slice.53), channel_id=1, source_target_pairs={{0,16},{1,17},{2,18},{3,19},{4,20},{5,21},{6,22},{7,23},{8,24},{9,... | collective-permute-start | bytes 196616 | tf_op jit(solution)/shard_map/ppermute | solution.py:92
  87.2 1.6 %collective-permute-start.20 = (bf16[8,3072]{1,0:T(8,128)(2,1)S(1)}, bf16[8,3072]{1,0:T(8,128)(2,1)S(1)}, u32[]{:S(2)}, u32[]{:S(2)}) collective-permute-start(bf16[8,3072]{1,0:T(8,128)(2,1)S(1)} %get-tuple-element.52), channel_id=1, source_target_pairs={{0,16},{1,17},{2,18},{3,19},{4,20},{5,21},{6,22},{7,23},{8,24},{9,... | collective-permute-start | bytes 147464 | tf_op jit(solution)/shard_map/ppermute | solution.py:92
  88.8 1.5 %collective-permute-start.22 = (bf16[8,3072]{1,0:T(8,128)(2,1)S(1)}, bf16[8,3072]{1,0:T(8,128)(2,1)S(1)}, u32[]{:S(2)}, u32[]{:S(2)}) collective-permute-start(bf16[8,3072]{1,0:T(8,128)(2,1)S(1)} %get-tuple-element.53), channel_id=1, source_target_pairs={{0,24},{1,25},{2,26},{3,27},{4,28},{5,29},{6,30},{7,31},{8,16},{9,... | collective-permute-start | bytes 147464 | tf_op jit(solution)/shard_map/ppermute | solution.py:92
  90.8 2.2 %collective-permute-done.20 = bf16[8,3072]{1,0:T(8,128)(2,1)S(1)} collective-permute-done((bf16[8,3072]{1,0:T(8,128)(2,1)S(1)}, bf16[8,3072]{1,0:T(8,128)(2,1)S(1)}, u32[]{:S(2)}, u32[]{:S(2)}) %collective-permute-start.20) | collective-permute-done | bytes 49184 | tf_op jit(solution)/shard_map/ppermute | solution.py:92
  93.0 1.8 %collective-permute-done.22 = bf16[8,3072]{1,0:T(8,128)(2,1)S(1)} collective-permute-done((bf16[8,3072]{1,0:T(8,128)(2,1)S(1)}, bf16[8,3072]{1,0:T(8,128)(2,1)S(1)}, u32[]{:S(2)}, u32[]{:S(2)}) %collective-permute-start.22) | collective-permute-done | bytes 49184 | tf_op jit(solution)/shard_map/ppermute | solution.py:92
  (54 shorter events, 14.5 us)
Async XLA Ops:
  0.6 0.9 copy-start
  3.1 9.8 %collective-permute-start = (bf16[8,7296]{1,0:T(8,128)(2,1)S(1)}, bf16[8,7296]{1,0:T(8,128)(2,1)S(1)}, u32[]{:S(2)}, u32[]{:S(2)}) collective-permute-start(bf16[8,7296]{1,0:T(8,128)(2,1)S(1)} %pack.1.refs_0_), channel_id=1, source_target_pairs={{0,16},{1,17},{2,18},{3,19},{4,20},{5,21},{6,22},{7,23},{8,24},{9,... | collective-permute-start | bytes 350216 | tf_op jit(solution)/shard_map/ppermute | solution.py:92
  12.9 6.9 %collective-permute-start.1 = (bf16[16,7296]{1,0:T(8,128)(2,1)S(1)}, bf16[16,7296]{1,0:T(8,128)(2,1)S(1)}, u32[]{:S(2)}, u32[]{:S(2)}) collective-permute-start(bf16[16,7296]{1,0:T(8,128)(2,1)S(1)} %join.4.refs_0_), channel_id=1, source_target_pairs={{0,8},{1,9},{2,10},{3,11},{4,12},{5,13},{6,14},{7,15},{8,0},{9,1},... | collective-permute-start | bytes 700424 | tf_op jit(solution)/shard_map/ppermute | solution.py:92
  19.9 6.4 %collective-permute-start.3 = (bf16[32,4096]{1,0:T(8,128)(2,1)S(1)}, bf16[32,4096]{1,0:T(8,128)(2,1)S(1)}, u32[]{:S(2)}, u32[]{:S(2)}) collective-permute-start(bf16[32,4096]{1,0:T(8,128)(2,1)S(1)} %get-tuple-element.29.refs_0_), channel_id=1, source_target_pairs={{0,1},{1,0},{2,6},{3,7},{4,5},{5,4},{6,2},{7,3},{8,9},{9,8},{10,14... | collective-permute-start | bytes 786440 | tf_op jit(solution)/shard_map/ppermute | solution.py:92
  26.4 9.2 %collective-permute-start.5 = (bf16[64,4096]{1,0:T(8,128)(2,1)S(1)}, bf16[64,4096]{1,0:T(8,128)(2,1)S(1)}, u32[]{:S(2)}, u32[]{:S(2)}) collective-permute-start(bf16[64,4096]{1,0:T(8,128)(2,1)S(1)} %join.7.refs_0_), channel_id=1, source_target_pairs={{0,4},{1,5},{2,3},{3,2},{4,0},{5,1},{6,7},{7,6},{8,12},{9,13},{10,... | collective-permute-start | bytes 1572872 | tf_op jit(solution)/shard_map/ppermute | solution.py:92
  27.7 6.6 %collective-permute-start.2 = (bf16[32,3200]{1,0:T(8,128)(2,1)S(1)}, bf16[32,3200]{1,0:T(8,128)(2,1)S(1)}, u32[]{:S(2)}, u32[]{:S(2)}) collective-permute-start(bf16[32,3200]{1,0:T(8,128)(2,1)S(1)} %get-tuple-element.28.refs_0_), channel_id=1, source_target_pairs={{0,1},{1,0},{2,6},{3,7},{4,5},{5,4},{6,2},{7,3},{8,9},{9,8},{10,14... | collective-permute-start | bytes 614408 | tf_op jit(solution)/shard_map/ppermute | solution.py:92
  34.4 2.7 %collective-permute-start.6 = (bf16[64,4096]{1,0:T(8,128)(2,1)S(1)}, bf16[64,4096]{1,0:T(8,128)(2,1)S(1)}, u32[]{:S(2)}, u32[]{:S(2)}) collective-permute-start(bf16[64,4096]{1,0:T(8,128)(2,1)S(1)} %join.7.refs_0_), channel_id=1, source_target_pairs={{0,2},{1,3},{2,0},{3,1},{4,6},{5,7},{6,4},{7,5},{8,10},{9,11},{10,... | collective-permute-start | bytes 1572872 | tf_op jit(solution)/shard_map/ppermute | solution.py:92
  35.6 1.9 %collective-permute-start.7 = (bf16[64,4096]{1,0:T(8,128)(2,1)S(1)}, bf16[64,4096]{1,0:T(8,128)(2,1)S(1)}, u32[]{:S(2)}, u32[]{:S(2)}) collective-permute-start(bf16[64,4096]{1,0:T(8,128)(2,1)S(1)} %collective-permute-done.5.refs_1_), channel_id=1, source_target_pairs={{0,2},{1,3},{2,0},{3,1},{4,6},{5,7},{6,4},{7,5},{8,10},{9,11},{10,... | collective-permute-start | bytes 1572872 | tf_op jit(solution)/shard_map/ppermute | solution.py:92
  35.6 8.0 %collective-permute-start.4 = (bf16[64,3200]{1,0:T(8,128)(2,1)S(1)}, bf16[64,3200]{1,0:T(8,128)(2,1)S(1)}, u32[]{:S(2)}, u32[]{:S(2)}) collective-permute-start(bf16[64,3200]{1,0:T(8,128)(2,1)S(1)} %join.6.refs_0_), channel_id=1, source_target_pairs={{0,4},{1,5},{2,3},{3,2},{4,0},{5,1},{6,7},{7,6},{8,12},{9,13},{10,... | collective-permute-start | bytes 1228808 | tf_op jit(solution)/shard_map/ppermute | solution.py:92
  36.9 6.7 %collective-permute-start.8 = (bf16[64,3200]{1,0:T(8,128)(2,1)S(1)}, bf16[64,3200]{1,0:T(8,128)(2,1)S(1)}, u32[]{:S(2)}, u32[]{:S(2)}) collective-permute-start(bf16[64,3200]{1,0:T(8,128)(2,1)S(1)} %join.6.refs_0_), channel_id=1, source_target_pairs={{0,2},{1,3},{2,0},{3,1},{4,6},{5,7},{6,4},{7,5},{8,10},{9,11},{10,... | collective-permute-start | bytes 1228808 | tf_op jit(solution)/shard_map/ppermute | solution.py:92
  43.6 1.7 %collective-permute-start.9 = (bf16[64,3200]{1,0:T(8,128)(2,1)S(1)}, bf16[64,3200]{1,0:T(8,128)(2,1)S(1)}, u32[]{:S(2)}, u32[]{:S(2)}) collective-permute-start(bf16[64,3200]{1,0:T(8,128)(2,1)S(1)} %collective-permute-done.4.refs_1_), channel_id=1, source_target_pairs={{0,2},{1,3},{2,0},{3,1},{4,6},{5,7},{6,4},{7,5},{8,10},{9,11},{10,... | collective-permute-start | bytes 1228808 | tf_op jit(solution)/shard_map/ppermute | solution.py:92
  55.5 2.0 %collective-permute-start.10 = (bf16[64,4096]{1,0:T(8,128)(2,1)S(1)}, bf16[64,4096]{1,0:T(8,128)(2,1)S(1)}, u32[]{:S(2)}, u32[]{:S(2)}) collective-permute-start(bf16[64,4096]{1,0:T(8,128)(2,1)S(1)} %get-tuple-element.42), channel_id=1, source_target_pairs={{0,2},{1,3},{2,0},{3,1},{4,6},{5,7},{6,4},{7,5},{8,10},{9,11},{10,... | collective-permute-start | bytes 1572872 | tf_op jit(solution)/shard_map/ppermute | solution.py:92
  55.7 2.5 %collective-permute-start.11 = (bf16[64,4096]{1,0:T(8,128)(2,1)S(1)}, bf16[64,4096]{1,0:T(8,128)(2,1)S(1)}, u32[]{:S(2)}, u32[]{:S(2)}) collective-permute-start(bf16[64,4096]{1,0:T(8,128)(2,1)S(1)} %get-tuple-element.44), channel_id=1, source_target_pairs={{0,2},{1,3},{2,0},{3,1},{4,6},{5,7},{6,4},{7,5},{8,10},{9,11},{10,... | collective-permute-start | bytes 1572872 | tf_op jit(solution)/shard_map/ppermute | solution.py:92
  58.4 9.2 %collective-permute-start.12 = (bf16[64,4096]{1,0:T(8,128)(2,1)S(1)}, bf16[64,4096]{1,0:T(8,128)(2,1)S(1)}, u32[]{:S(2)}, u32[]{:S(2)}) collective-permute-start(bf16[64,4096]{1,0:T(8,128)(2,1)S(1)} %add_convert_fusion.1), channel_id=1, source_target_pairs={{0,4},{1,5},{2,3},{3,2},{4,0},{5,1},{6,7},{7,6},{8,12},{9,13},{10,... | collective-permute-start | bytes 1572872 | tf_op jit(solution)/shard_map/ppermute | solution.py:92
  59.7 19.7 %collective-permute-start.16 = (bf16[64,3072]{1,0:T(8,128)(2,1)S(1)}, bf16[64,3072]{1,0:T(8,128)(2,1)S(1)}, u32[]{:S(2)}, u32[]{:S(2)}) collective-permute-start(bf16[64,3072]{1,0:T(8,128)(2,1)S(1)} %get-tuple-element.48), channel_id=1, source_target_pairs={{0,2},{1,3},{2,0},{3,1},{4,6},{5,7},{6,4},{7,5},{8,10},{9,11},{10,... | collective-permute-start | bytes 1179656 | tf_op jit(solution)/shard_map/ppermute | solution.py:92
  59.7 9.4 %collective-permute-start.17 = (bf16[64,3072]{1,0:T(8,128)(2,1)S(1)}, bf16[64,3072]{1,0:T(8,128)(2,1)S(1)}, u32[]{:S(2)}, u32[]{:S(2)}) collective-permute-start(bf16[64,3072]{1,0:T(8,128)(2,1)S(1)} %get-tuple-element.50), channel_id=1, source_target_pairs={{0,2},{1,3},{2,0},{3,1},{4,6},{5,7},{6,4},{7,5},{8,10},{9,11},{10,... | collective-permute-start | bytes 1179656 | tf_op jit(solution)/shard_map/ppermute | solution.py:92
  67.8 9.2 %collective-permute-start.13 = (bf16[32,4096]{1,0:T(8,128)(2,1)S(1)}, bf16[32,4096]{1,0:T(8,128)(2,1)S(1)}, u32[]{:S(2)}, u32[]{:S(2)}) collective-permute-start(bf16[32,4096]{1,0:T(8,128)(2,1)S(1)} %slice.49), channel_id=1, source_target_pairs={{0,1},{1,0},{2,6},{3,7},{4,5},{5,4},{6,2},{7,3},{8,9},{9,8},{10,14... | collective-permute-start | bytes 786440 | tf_op jit(solution)/shard_map/ppermute | solution.py:92
  69.2 10.2 %collective-permute-start.18 = (bf16[64,3072]{1,0:T(8,128)(2,1)S(1)}, bf16[64,3072]{1,0:T(8,128)(2,1)S(1)}, u32[]{:S(2)}, u32[]{:S(2)}) collective-permute-start(bf16[64,3072]{1,0:T(8,128)(2,1)S(1)} %add_convert_fusion.4), channel_id=1, source_target_pairs={{0,4},{1,5},{2,3},{3,2},{4,0},{5,1},{6,7},{7,6},{8,12},{9,13},{10,... | collective-permute-start | bytes 1179656 | tf_op jit(solution)/shard_map/ppermute | solution.py:92
  77.0 5.3 %collective-permute-start.14 = (bf16[16,4096]{1,0:T(8,128)(2,1)S(1)}, bf16[16,4096]{1,0:T(8,128)(2,1)S(1)}, u32[]{:S(2)}, u32[]{:S(2)}) collective-permute-start(bf16[16,4096]{1,0:T(8,128)(2,1)S(1)} %slice.51), channel_id=1, source_target_pairs={{0,8},{1,9},{2,10},{3,11},{4,12},{5,13},{6,14},{7,15},{8,0},{9,1},... | collective-permute-start | bytes 393224 | tf_op jit(solution)/shard_map/ppermute | solution.py:92
  79.6 7.6 %collective-permute-start.19 = (bf16[32,3072]{1,0:T(8,128)(2,1)S(1)}, bf16[32,3072]{1,0:T(8,128)(2,1)S(1)}, u32[]{:S(2)}, u32[]{:S(2)}) collective-permute-start(bf16[32,3072]{1,0:T(8,128)(2,1)S(1)} %slice.55), channel_id=1, source_target_pairs={{0,1},{1,0},{2,6},{3,7},{4,5},{5,4},{6,2},{7,3},{8,9},{9,8},{10,14... | collective-permute-start | bytes 589832 | tf_op jit(solution)/shard_map/ppermute | solution.py:92
  82.4 8.4 %collective-permute-start.15 = (bf16[8,4096]{1,0:T(8,128)(2,1)S(1)}, bf16[8,4096]{1,0:T(8,128)(2,1)S(1)}, u32[]{:S(2)}, u32[]{:S(2)}) collective-permute-start(bf16[8,4096]{1,0:T(8,128)(2,1)S(1)} %slice.53), channel_id=1, source_target_pairs={{0,16},{1,17},{2,18},{3,19},{4,20},{5,21},{6,22},{7,23},{8,24},{9,... | collective-permute-start | bytes 196616 | tf_op jit(solution)/shard_map/ppermute | solution.py:92
  87.2 5.8 %collective-permute-start.20 = (bf16[8,3072]{1,0:T(8,128)(2,1)S(1)}, bf16[8,3072]{1,0:T(8,128)(2,1)S(1)}, u32[]{:S(2)}, u32[]{:S(2)}) collective-permute-start(bf16[8,3072]{1,0:T(8,128)(2,1)S(1)} %get-tuple-element.52), channel_id=1, source_target_pairs={{0,16},{1,17},{2,18},{3,19},{4,20},{5,21},{6,22},{7,23},{8,24},{9,... | collective-permute-start | bytes 147464 | tf_op jit(solution)/shard_map/ppermute | solution.py:92
  88.8 6.0 %collective-permute-start.22 = (bf16[8,3072]{1,0:T(8,128)(2,1)S(1)}, bf16[8,3072]{1,0:T(8,128)(2,1)S(1)}, u32[]{:S(2)}, u32[]{:S(2)}) collective-permute-start(bf16[8,3072]{1,0:T(8,128)(2,1)S(1)} %get-tuple-element.53), channel_id=1, source_target_pairs={{0,24},{1,25},{2,26},{3,27},{4,28},{5,29},{6,30},{7,31},{8,16},{9,... | collective-permute-start | bytes 147464 | tf_op jit(solution)/shard_map/ppermute | solution.py:92
  90.3 4.6 %collective-permute-start.21 = (bf16[8,3072]{1,0:T(8,128)(2,1)S(1)}, bf16[8,3072]{1,0:T(8,128)(2,1)S(1)}, u32[]{:S(2)}, u32[]{:S(2)}) collective-permute-start(bf16[8,3072]{1,0:T(8,128)(2,1)S(1)} %get-tuple-element.54), channel_id=1, source_target_pairs={{0,8},{1,9},{2,10},{3,11},{4,12},{5,13},{6,14},{7,15},{8,0},{9,1},... | collective-permute-start | bytes 147464 | tf_op jit(solution)/shard_map/ppermute | solution.py:92
  (3 other events, 2.0 us)

commit v9 on v8

v9 whole, which is shorter than its diff:
```python
import functools

import jax
import jax.numpy as jnp
import numpy as np
from jax import lax
from jax.experimental import pallas as pl
from jax.experimental.pallas import tpu as pltpu
from jax.sharding import Mesh
from jax.sharding import PartitionSpec as P

score_scale = 192.0 ** (-0.5)
everyone = ("high", "middle", "core", "local")
MEBI = 1024 * 1024


def attention_kernel(lengths_ref, *refs):
    sources, (out_ref, *targets), sems = refs[:4], refs[4:-1], refs[-1]
    query_ref, query_rope_ref, cache_ref, cache_rope_ref = targets
    copies = []
    for row in range(out_ref.shape[0]):
        copies.append(
            [
                pltpu.make_async_copy(source.at[row], target.at[row], sems.at[row, i])
                for i, (source, target) in enumerate(zip(sources, targets))
            ]
        )
        for copy in copies[-1]:
            copy.start()
    for row in range(out_ref.shape[0]):
        for copy in copies[row]:
            copy.wait()
        cache = cache_ref[row]
        scores = lax.dot_general(
            query_ref[row], cache, (((1,), (1,)), ((), ())), preferred_element_type=jnp.float32
        )
        scores += jnp.dot(
            query_rope_ref[row], cache_rope_ref[row], preferred_element_type=jnp.float32
        )
        slot = lax.broadcasted_iota(jnp.int32, scores.shape, 1)
        in_range = slot < lengths_ref[row]
        scores = jnp.where(in_range, scores * score_scale, -jnp.inf)
        row_peak = jnp.max(scores, axis=1, keepdims=True)
        lifted = jnp.where(in_range, jnp.exp(scores - row_peak), 0.0)
        weights = (lifted / jnp.sum(lifted, axis=1, keepdims=True)).astype(jnp.bfloat16)
        value = jnp.dot(weights, cache, preferred_element_type=jnp.float32)
        out_ref[row] = value.astype(jnp.bfloat16)


def attention(query_latent, query_rope, cache_latent, cache_rope, cache_lengths):
    rows, heads, latent = query_latent.shape
    slots = cache_latent.shape[1]
    sources = (query_latent, query_rope, cache_latent, cache_rope)
    return pl.pallas_call(
        attention_kernel,
        in_specs=[pl.BlockSpec(memory_space=pltpu.SMEM)]
        + [pl.BlockSpec(memory_space=pltpu.HBM)] * 4,
        out_specs=pl.BlockSpec(memory_space=pltpu.VMEM),
        out_shape=jax.ShapeDtypeStruct(query_latent.shape, jnp.bfloat16),
        scratch_shapes=[pltpu.VMEM(source.shape, source.dtype) for source in sources]
        + [pltpu.SemaphoreType.DMA((rows, 4))],
        cost_estimate=pl.CostEstimate(
            flops=4 * rows * heads * slots * latent,
            bytes_accessed=2 * rows * slots * latent,
            transcendentals=rows * heads * slots,
        ),
        compiler_params=pltpu.CompilerParams(vmem_limit_bytes=8 * MEBI),
        name="attention",
    )(cache_lengths, *[in_hbm(source) for source in sources])


def in_hbm(array):
    return pltpu.with_memory_space_constraint(array, pltpu.HBM)


HIGH, MIDDLE, CORE, LOCAL = range(4)


class Grid:
    def __init__(self):
        self.sizes = tuple(lax.axis_size(name) for name in everyone)
        self.masks = []
        while self.sizes[HIGH] >> len(self.masks) > 1:
            self.masks.append(self.sizes[HIGH] >> (len(self.masks) + 1))

    def swap(self, value, digit, mask):
        pairs = []
        for place in np.ndindex(*self.sizes):
            other = list(place)
            other[digit] ^= mask
            pairs.append(
                (
                    int(np.ravel_multi_index(place, self.sizes)),
                    int(np.ravel_multi_index(other, self.sizes)),
                )
            )
        return lax.ppermute(value, everyone, pairs)

    def over(self, block, digit):
        return [block] + [self.swap(block, digit, m) for m in range(1, self.sizes[digit])]

    def sum_over(self, parts, digit):
        return add(parts[:1] + [self.swap(parts[m], digit, m) for m in range(1, len(parts))])

    def sum_rows_over(self, block, digit):
        rows = block.shape[0] // self.sizes[digit]
        parts = [block[m * rows : (m + 1) * rows] for m in range(self.sizes[digit])]
        return self.sum_over(parts, digit)

    def high_sum(self, line):
        for m in reversed(self.masks):
            half = line.shape[0] // 2
            line = add([line[:half], self.swap(line[half:], HIGH, m)])
        return line

    def high_sum_direct(self, line):
        order = [0]
        for m in self.masks:
            order += [m | other for other in order]
        rows = line.shape[0] // len(order)
        parts = [line[:rows]]
        for i in range(1, len(order)):
            parts.append(self.swap(line[i * rows : (i + 1) * rows], HIGH, order[i]))
        return add(parts)


def add(parts):
    total = parts[0].astype(jnp.float32)
    for part in parts[1:]:
        total = total + part.astype(jnp.float32)
    return total.astype(parts[0].dtype)


def join_kernel(count, *refs):
    start = 0
    for out in refs[count:]:
        columns = pl.ds(start, out.shape[1])
        out[...] = jnp.concatenate([ref[:, columns] for ref in refs[:count]], axis=0)
        start += out.shape[1]


def join(parts, *widths):
    rows = sum(part.shape[0] for part in parts)
    widths = widths or parts[0].shape[1:]
    outs = pl.pallas_call(
        functools.partial(join_kernel, len(parts)),
        in_specs=[pl.BlockSpec(memory_space=pltpu.VMEM)] * len(parts),
        out_specs=[pl.BlockSpec(memory_space=pltpu.VMEM)] * len(widths),
        out_shape=[jax.ShapeDtypeStruct((rows, width), parts[0].dtype) for width in widths],
        compiler_params=pltpu.CompilerParams(vmem_limit_bytes=2 * MEBI),
        name="join",
    )(*parts)
    return outs if len(widths) > 1 else outs[0]


def table_width(experts):
    return pl.cdiv(2 * experts, 128) * 128


def pack_kernel(experts, rows_ref, ids_ref, gates_ref, head_ref, tail_ref):
    extra = table_width(experts)
    split, width = head_ref.shape[1], tail_ref.shape[1] - extra
    gates = gates_ref[...]
    shares = 2.5 * gates / jnp.sum(gates, axis=1, keepdims=True)
    ids = ids_ref[...]
    lane = lax.broadcasted_iota(jnp.int32, (ids.shape[0], extra), 1)
    expert = jnp.where(lane < experts, lane, lane - experts)
    table = jnp.zeros(lane.shape, jnp.float32)
    for k in range(ids.shape[1]):
        table += jnp.where(expert == ids[:, k : k + 1], shares[:, k : k + 1], 0.0)
    high = table.astype(jnp.bfloat16).astype(jnp.float32)
    table = jnp.where(lane < experts, high, jnp.where(lane < 2 * experts, table - high, 0.0))
    head_ref[...] = rows_ref[:, :split]
    tail_ref[:, :width] = rows_ref[:, split:]
    tail_ref[:, width:] = table.astype(jnp.bfloat16)


def pack(split, experts, moe_rows, route_ids, route_gates):
    rows, width = moe_rows.shape
    return pl.pallas_call(
        functools.partial(pack_kernel, experts),
        out_shape=[
            jax.ShapeDtypeStruct((rows, columns), jnp.bfloat16)
            for columns in (split, width - split + table_width(experts))
        ],
        compiler_params=pltpu.CompilerParams(vmem_limit_bytes=16 * MEBI),
        name="pack",
    )(moe_rows, route_ids, route_gates)


def line_order(sizes):
    _, middle, _, local = sizes
    ways = [[], []]
    for m in range(middle):
        for n in range(local):
            ways[0].append((m, n))
            ways[1].append((n, m))
    return ways


def gathered_rows(arrays, order, size, columns):
    return [arrays[i][line * size : (line + 1) * size, columns] for i, line in order]


def fetch_both(gate_hbm, up_hbm, gate, up, gate_sem, up_sem, start, tile):
    copies = []
    for k in range(0, gate.shape[0], tile):
        inside, outside = pl.ds(k, tile), pl.ds(start + k, tile)
        pair = (
            pltpu.make_async_copy(gate_hbm.at[outside], gate.at[inside], gate_sem.at[k // tile]),
            pltpu.make_async_copy(up_hbm.at[outside], up.at[inside], up_sem.at[k // tile]),
        )
        for copy in pair:
            copy.start()
        copies.append(pair)
    return copies


def both_cores(arrays, way, sizes, columns):
    order = line_order(sizes)[way]
    arrays = arrays[way]
    count = len(arrays) // 2
    size = arrays[0].shape[0] // (1 + max(line for _, line in order))
    rows = gathered_rows(arrays[:count], order, size, columns)
    rows += gathered_rows(arrays[count:], order, size, columns)
    return jnp.concatenate(rows, axis=0)


def project(arrays, sizes, copies, gate, up, gate_sum, up_sum, tile, fresh):
    half = len(copies) // 2
    for k, pair in enumerate(copies):
        rows = both_cores(arrays, k // half, sizes, pl.ds(k % half * tile, tile))
        for copy, weight, total in zip(pair, (gate, up), (gate_sum, up_sum)):
            copy.wait()
            product = jnp.dot(
                rows, weight[pl.ds(k * tile, tile)], preferred_element_type=jnp.float32
            )
            if fresh and k == 0:
                total[...] = product
            else:
                total[...] += product


def by_way(refs, counts):
    return [refs[: counts[0]], refs[counts[0] : sum(counts)]]


def first_kernel(counts, sizes, tile, *refs):
    arrays, refs = by_way(refs, counts), refs[sum(counts) :]
    gate_hbm, up_hbm, gate_sum, up_sum, gate, up, gate_sem, up_sem = refs
    copies = fetch_both(gate_hbm, up_hbm, gate, up, gate_sem, up_sem, 0, tile)
    project(arrays, sizes, copies, gate, up, gate_sum, up_sum, tile, True)


def first_sums(arrays, sizes, rows, w_gate, w_up):
    units = w_gate.shape[1]
    columns = sum(way[0].shape[1] for way in arrays)
    tile = 1024
    counts = tuple(len(way) for way in arrays)
    return pl.pallas_call(
        functools.partial(first_kernel, counts, sizes, tile),
        in_specs=[pl.BlockSpec(memory_space=pltpu.VMEM)] * sum(counts)
        + [pl.BlockSpec(memory_space=pltpu.HBM)] * 2,
        out_specs=[pl.BlockSpec(memory_space=pltpu.VMEM)] * 2,
        out_shape=[jax.ShapeDtypeStruct((rows, units), jnp.float32)] * 2,
        scratch_shapes=[pltpu.VMEM((columns, units), jnp.bfloat16)] * 2
        + [pltpu.SemaphoreType.DMA((columns // tile,))] * 2,
        cost_estimate=pl.CostEstimate(
            flops=4 * rows * columns * units,
            bytes_accessed=4 * columns * units,
            transcendentals=0,
        ),
        compiler_params=pltpu.CompilerParams(vmem_limit_bytes=20 * MEBI),
        name="first_sums",
    )(*arrays[0], *arrays[1], in_hbm(w_gate), in_hbm(w_up))


def expert_kernel(counts, sizes, experts, tile, node_ref, *refs):
    arrays, refs = by_way(refs, counts), refs[sum(counts) :]
    gate_in, up_in, gate_hbm, up_hbm, down_hbm = refs[:5]
    outs = refs[5:-10]
    hidden_ref, share_ref, gate, up, down, gate_sum, up_sum, gate_sem, up_sem, down_sem = refs[-10:]
    start = gate_hbm.shape[0] - gate.shape[0]
    copies = fetch_both(gate_hbm, up_hbm, gate, up, gate_sem, up_sem, start, tile)
    quarters = down_sem.shape[0]
    quarter = down.shape[1] // quarters
    down_copies = []
    for k in range(quarters):
        part = pl.ds(k * quarter, quarter)
        down_copies.append(
            pltpu.make_async_copy(down_hbm.at[:, part], down.at[:, part], down_sem.at[k])
        )
        down_copies[-1].start()

    width = gate.shape[0] // 2
    behind = pl.ds(width, arrays[1][0].shape[1] - width)
    table = both_cores(arrays, 1, sizes, behind).astype(jnp.float32)
    lane = lax.broadcasted_iota(jnp.int32, table.shape, 1)
    mine = (lane == node_ref[0]) | (lane == node_ref[0] + experts)
    share = jnp.sum(jnp.where(mine, table, 0.0), axis=1, keepdims=True)
    share_ref[...] = jnp.broadcast_to(share, share_ref.shape)
    gate_sum[...] = gate_in[...]
    up_sum[...] = up_in[...]
    project(arrays, sizes, copies, gate, up, gate_sum, up_sum, tile, False)
    hidden_ref[...] = (jax.nn.silu(gate_sum[...]) * up_sum[...]).astype(jnp.bfloat16)
    for k, copy in enumerate(down_copies):
        copy.wait()
        order = line_order(sizes)[k % 2]
        each = 2 + max(i for i, _ in order)
        group, outs = outs[:each], outs[each:]
        size = hidden_ref.shape[0] // (2 * len(order))
        for piece in range(0, quarter, quarter // 2):
            part = pl.ds(k * quarter + piece, quarter // 2)
            product = jnp.dot(hidden_ref[...], down[:, part], preferred_element_type=jnp.float32)
            product = (product * share_ref[:, :1]).astype(jnp.bfloat16)
            columns = pl.ds(piece, quarter // 2)
            for i, line in order:
                row = order.index((i, line)) * size
                group[i][line * size : (line + 1) * size, columns] = product[row : row + size]
                row += len(order) * size
                lines = 1 + max(line for _, line in order)
                place = ((i - 1) % (each - 1)) * lines + line
                group[-1][place * size : (place + 1) * size, columns] = product[row : row + size]


def expert(arrays, sizes, rows, sums, w_gate, w_up, w_down, experts, node):
    units, columns = w_down.shape
    tail = sum(way[0].shape[1] for way in arrays) - table_width(experts)
    tile = 512
    counts = tuple(len(way) for way in arrays)
    out_shapes = []
    for k in range(4):
        places = (sizes[MIDDLE], sizes[LOCAL])[k % 2]
        size = rows // 2 // places
        out_shapes += [(size, columns // 4)] * places + [(rows // 2, columns // 4)]
    return pl.pallas_call(
        functools.partial(expert_kernel, counts, sizes, experts, tile),
        in_specs=[pl.BlockSpec(memory_space=pltpu.SMEM)]
        + [pl.BlockSpec(memory_space=pltpu.VMEM)] * (sum(counts) + 2)
        + [pl.BlockSpec(memory_space=pltpu.HBM)] * 3,
        out_specs=[pl.BlockSpec(memory_space=pltpu.VMEM)] * len(out_shapes),
        out_shape=[jax.ShapeDtypeStruct(shape, jnp.bfloat16) for shape in out_shapes],
        scratch_shapes=[
            pltpu.VMEM((rows, units), jnp.bfloat16),
            pltpu.VMEM((rows, 128), jnp.float32),
            pltpu.VMEM((tail, units), jnp.bfloat16),
            pltpu.VMEM((tail, units), jnp.bfloat16),
            pltpu.VMEM((units, columns), jnp.bfloat16),
            pltpu.VMEM((rows, units), jnp.float32),
            pltpu.VMEM((rows, units), jnp.float32),
            pltpu.SemaphoreType.DMA((tail // tile,)),
            pltpu.SemaphoreType.DMA((tail // tile,)),
            pltpu.SemaphoreType.DMA((4,)),
        ],
        cost_estimate=pl.CostEstimate(
            flops=4 * rows * tail * units + 2 * rows * columns * units,
            bytes_accessed=4 * tail * units + 2 * units * columns,
            transcendentals=rows * units,
        ),
        compiler_params=pltpu.CompilerParams(vmem_limit_bytes=24 * MEBI),
        name="expert",
    )(node, *arrays[0], *arrays[1], *sums, in_hbm(w_gate), in_hbm(w_up), in_hbm(w_down))


def body(
    moe_rows,
    route_ids,
    route_gates,
    w_gate,
    w_up,
    w_down,
    query_latent,
    query_rope,
    cache_latent,
    cache_rope,
    cache_lengths,
):
    grid = Grid()
    high, middle, cores, _ = grid.sizes
    experts = high * middle * cores
    tokens, width = moe_rows.shape
    node = lax.axis_index(("high", "middle", "core")).astype(jnp.int32).reshape(1)
    split = width * 4 // 7
    tied = lax.optimization_barrier
    attn_latent = attention(query_latent, query_rope, cache_latent, cache_rope, cache_lengths)

    def join_halves(parts):
        half = (width - split if parts[0].shape[1] < split else split) // 2
        return join(parts, half, parts[0].shape[1] - half)

    def step(blocks):
        return [grid.over(blocks[0], LOCAL), grid.over(blocks[1], MIDDLE)]

    def second_step(blocks):
        return [grid.over(blocks[0], MIDDLE), grid.over(blocks[1], LOCAL)]

    def with_other_core(ways):
        return [way + [grid.swap(block, CORE, 1) for block in way] for way in ways]

    head, tail = pack(split, experts, moe_rows, route_ids, route_gates)
    came = grid.swap(head, HIGH, grid.masks[0])
    tail, came = tied((tail, came))
    head = [head, came]
    for m in grid.masks[1:]:
        line = join(head)
        head = [line, grid.swap(line, HIGH, m)]
    head = join_halves(head)
    came = grid.swap(tail, HIGH, grid.masks[0])
    head, came = tied((head, came))
    tail = [tail, came]
    for m in grid.masks[1:]:
        line = join(tail)
        tail = [line, grid.swap(line, HIGH, m)]
    tail = join_halves(tail)
    head = step(head)
    head, tail, attn_latent = tied(([join(head[0]), join(head[1])], tail, attn_latent))
    head, tail = tied((second_step(head), step(tail)))
    head = with_other_core(head)
    tail = second_step([join(tail[0]), join(tail[1])])
    rows = 2 * grid.sizes[MIDDLE] * grid.sizes[LOCAL] * high * tokens
    sums = first_sums(head, grid.sizes, rows, w_gate[0], w_up[0])
    tail, sums = tied((tail, sums))
    tail = with_other_core(tail)
    products = expert(
        tail, grid.sizes, rows, sums, w_gate[0], w_up[0], w_down[0], experts, node
    )

    digits = (MIDDLE, LOCAL)

    def core_sums(arrays):
        sums = []
        for way in range(2):
            places = grid.sizes[digits[way]]
            mine, other, arrays = arrays[:places], arrays[places], arrays[places + 1 :]
            other = grid.swap(other, CORE, 1)
            size = mine[0].shape[0]
            sums.append(
                [
                    add([mine[i], other[(i - 1) % places * size :][:size]])
                    for i in range(places)
                ]
            )
        return sums

    def second_sums(sums):
        return [grid.sum_over(sums[way], digits[way]) for way in range(2)]

    def first_axis_sums(blocks):
        return jnp.concatenate(
            [grid.sum_rows_over(blocks[way], digits[1 - way]) for way in range(2)], axis=1
        )

    head, tail = products[: len(products) // 2], products[len(products) // 2 :]
    tail, head = tied((tail, core_sums(head)))
    head = first_axis_sums(second_sums(head))
    head, tail = tied((head, second_sums(core_sums(tail))))
    head = grid.high_sum(head)
    tail = grid.high_sum_direct(first_axis_sums(tail))
    return (jnp.concatenate([head, tail], axis=1), attn_latent)


def solution(mesh):
    groups, nodes, local = mesh.devices.shape
    split = Mesh(mesh.devices.reshape(groups, nodes // 4, 2, 2, local), ("group",) + everyone)
    node = ("high", "middle", "core")
    whole = ("group",) + everyone
    rows = P(whole, None)
    blocks = P(whole, None, None)
    return jax.shard_map(
        body,
        mesh=split,
        in_specs=(
            rows,
            rows,
            rows,
            P(node, None, "local"),
            P(node, None, "local"),
            P(node, "local", None),
            blocks,
            blocks,
            blocks,
            blocks,
            P(whole),
        ),
        out_specs=(rows, blocks),
        check_vma=False,
    )
```

time: 95.9 us -> 95.1 us (level)
  starting transfers between devices: 27.4 us -> 37.7 us
  waiting for transfers between devices: 44.7 us -> 35.6 us
  Pallas kernels: 18.4 us -> 16.2 us
    ppermute x23 -> x37, starting transfers between devices: 27.4 us -> 37.7 us  [swap(): return lax.ppermute(value, everyone, pairs)]
    ppermute x23 -> x37, waiting for transfers between devices: 44.7 us -> 35.6 us  [swap(): return lax.ppermute(value, everyone, pairs)]
    pallas_call x3, Pallas kernels: 14.6 us -> 12.4 us  [the longest x1 7.99 us: expert(): pl.pallas_call(functools.partial(expert_kernel, counts, sizes, experts, t...]
  transfers between devices with their start and end apart: 23 -> 37, of which waited for: 16 -> 19; matrix products, arithmetic and copies ran while one was open for 1% -> 1% of each run, Pallas kernels for 8% -> 8%
where the time goes in v9:
time: 95.1 us; the launch traced here: 94.8 us
  starting transfers between devices  37.7 us (40%)
  waiting for transfers between devices  35.6 us (37%)
  Pallas kernels  16.2 us (17%)
  local copies, waits for them, and re-layouts  2.97 us (3%)
  other arithmetic  1.5 us (2%)
    ppermute x37, starting transfers between devices, swap(): return lax.ppermute(value, everyone, pairs)  37.7 us
    ppermute x37, waiting for transfers between devices, swap(): return lax.ppermute(value, everyone, pairs)  35.6 us
    pallas_call x1, Pallas kernels, expert(): pl.pallas_call(functools.partial(expert_kernel, counts, sizes, experts, t...  7.99 us
    pallas_call x1, Pallas kernels, first_sums(): pl.pallas_call(functools.partial(first_kernel, counts, sizes, tile), in_s...  4.21 us
    pallas_call x1, Pallas kernels, attention(): pl.pallas_call(attention_kernel, in_specs=[pl.BlockSpec(memory_space=pltp...  3.66 us
    unnamed x8, local copies, waits for them, and re-layouts  2.92 us
  transfers between devices with their start and end apart: 37, of which 19 were waited for; matrix products, arithmetic and copies ran while one was open for 1% of the time, Pallas kernels for 8%

profile of v9, /device:TPU:0, one launch (start us, length us, event | category | flops | bytes accessed | tf_op | source)
XLA Modules:
  0.0 94.8 jit_solution(11018088397180120909)
XLA Ops:
  3.1 4.1 %collective-permute-start = (bf16[8,4096]{1,0:T(8,128)(2,1)S(1)}, bf16[8,4096]{1,0:T(8,128)(2,1)S(1)}, u32[]{:S(2)}, u32[]{:S(2)}) collective-permute-start(bf16[8,4096]{1,0:T(8,128)(2,1)S(1)} %get-tuple-element.59.refs_0_), channel_id=1, source_target_pairs={{0,16},{1,17},{2,18},{3,19},{4,20},{5,21},{6,22},{7,23},{8,24},{9,... | collective-permute-start | bytes 196616 | tf_op jit(solution)/shard_map/ppermute | solution.py:97
  7.2 3.6 %collective-permute-done.refs_1_ = bf16[8,4096]{1,0:T(8,128)(2,1)S(1)} collective-permute-done((bf16[8,4096]{1,0:T(8,128)(2,1)S(1)}, bf16[8,4096]{1,0:T(8,128)(2,1)S(1)}, u32[]{:S(2)}, u32[]{:S(2)}) %collective-permute-start) | collective-permute-done | bytes 65568 | tf_op jit(solution)/shard_map/ppermute | solution.py:97
  11.5 3.4 %collective-permute-start.2 = (bf16[8,3200]{1,0:T(8,128)(2,1)S(1)}, bf16[8,3200]{1,0:T(8,128)(2,1)S(1)}, u32[]{:S(2)}, u32[]{:S(2)}) collective-permute-start(bf16[8,3200]{1,0:T(8,128)(2,1)S(1)} %get-tuple-element.64.refs_0_), channel_id=1, source_target_pairs={{0,16},{1,17},{2,18},{3,19},{4,20},{5,21},{6,22},{7,23},{8,24},{9,... | collective-permute-start | bytes 153608 | tf_op jit(solution)/shard_map/ppermute | solution.py:97
  14.9 1.6 %collective-permute-done.1.refs_1_ = bf16[16,4096]{1,0:T(8,128)(2,1)S(1)} collective-permute-done((bf16[16,4096]{1,0:T(8,128)(2,1)S(1)}, bf16[16,4096]{1,0:T(8,128)(2,1)S(1)}, u32[]{:S(2)}, u32[]{:S(2)}) %collective-permute-start.1) | collective-permute-done | bytes 131104 | tf_op jit(solution)/shard_map/ppermute | solution.py:97
  18.8 1.5 %collective-permute-start.4 = (bf16[32,2048]{1,0:T(8,128)(2,1)S(1)}, bf16[32,2048]{1,0:T(8,128)(2,1)S(1)}, u32[]{:S(2)}, u32[]{:S(2)}) collective-permute-start(bf16[32,2048]{1,0:T(8,128)(2,1)S(1)} %get-tuple-element.66.refs_0_), channel_id=1, source_target_pairs={{0,4},{1,5},{2,6},{3,7},{4,0},{5,1},{6,2},{7,3},{8,12},{9,13},{10,... | collective-permute-start | bytes 393224 | tf_op jit(solution)/shard_map/ppermute | solution.py:97
  20.3 2.1 %collective-permute-start.5 = (bf16[16,3200]{1,0:T(8,128)(2,1)S(1)}, bf16[16,3200]{1,0:T(8,128)(2,1)S(1)}, u32[]{:S(2)}, u32[]{:S(2)}) collective-permute-start(bf16[16,3200]{1,0:T(8,128)(2,1)S(1)} %join.12.refs_0_), channel_id=1, source_target_pairs={{0,8},{1,9},{2,10},{3,11},{4,12},{5,13},{6,14},{7,15},{8,0},{9,1},... | collective-permute-start | bytes 307208 | tf_op jit(solution)/shard_map/ppermute | solution.py:97
  23.1 3.7 %attention.1 = bf16[2,64,512]{2,1,0:T(8,128)(2,1)} custom-call(s32[2]{0:T(128)S(1)} %copy-done.3, bf16[2,64,512]{2,1,0:T(8,128)(2,1)} %refs_0_.1, bf16[2,64,64]{2,1,0:T(8,128)(2,1)} %refs_1_.1, bf16[2,512,512]{2,1,0:T(8,128)(2,1)} %refs_2_.1, bf16[2,64,512]{2,1,0:T(8,128)(2,1)} %refs_3_.1), custom_call_target="tpu_custom_call" | custom-call | flops 134217728 | bytes 1048576 | tf_op jit(solution)/shard_map/attention/pallas_call | solution.py:54
  28.0 1.5 %collective-permute-start.9 = (bf16[32,1664]{1,0:T(8,128)(2,1)S(1)}, bf16[32,1664]{1,0:T(8,128)(2,1)S(1)}, u32[]{:S(2)}, u32[]{:S(2)}) collective-permute-start(bf16[32,1664]{1,0:T(8,128)(2,1)S(1)} %get-tuple-element.76.refs_0_), channel_id=1, source_target_pairs={{0,4},{1,5},{2,6},{3,7},{4,0},{5,1},{6,2},{7,3},{8,12},{9,13},{10,... | collective-permute-start | bytes 319496 | tf_op jit(solution)/shard_map/ppermute | solution.py:97
  31.0 4.4 %collective-permute-done.8.refs_1_ = bf16[32,1536]{1,0:T(8,128)(2,1)S(1)} collective-permute-done((bf16[32,1536]{1,0:T(8,128)(2,1)S(1)}, bf16[32,1536]{1,0:T(8,128)(2,1)S(1)}, u32[]{:S(2)}, u32[]{:S(2)}) %collective-permute-start.8) | collective-permute-done | bytes 98336 | tf_op jit(solution)/shard_map/ppermute | solution.py:97
  37.2 1.6 %collective-permute-start.10 = (bf16[64,1536]{1,0:T(8,128)(2,1)S(1)}, bf16[64,1536]{1,0:T(8,128)(2,1)S(1)}, u32[]{:S(2)}, u32[]{:S(2)}) collective-permute-start(bf16[64,1536]{1,0:T(8,128)(2,1)S(1)} %join.14.refs_0_), channel_id=1, source_target_pairs={{0,4},{1,5},{2,6},{3,7},{4,0},{5,1},{6,2},{7,3},{8,12},{9,13},{10,... | collective-permute-start | bytes 589832 | tf_op jit(solution)/shard_map/ppermute | solution.py:97
  38.8 4.2 %first_sums.1 = (f32[256,512]{1,0:T(8,128)S(1)}, f32[256,512]{1,0:T(8,128)S(1)}) custom-call(bf16[64,2048]{1,0:T(8,128)(2,1)S(1)} %join.10.refs_0_, bf16[64,2048]{1,0:T(8,128)(2,1)S(1)} %collective-permute-done.6.refs_1_, bf16[64,2048]{1,0:T(8,128)(2,1)S(1)} %collective-permute-done.12.refs_2_, bf16[64,2048]{1,0:T(8,128)(2,1)S(1)} %collective-permute-done.13.refs_3_, ...), custom_call_target="tpu_custom_call" | custom-call | flops 2147483648 | bytes 8388608 | tf_op jit(solution)/shard_map/first_sums/pallas_call | solution.py:260
  46.3 8.0 %expert.1 = (bf16[64,1792]{1,0:T(8,128)(2,1)S(1)}, bf16[64,1792]{1,0:T(8,128)(2,1)S(1)}, bf16[128,1792]{1,0:T(8,128)(2,1)S(1)}, bf16[64,1792]{1,0:T(8,128)(2,1)S...) custom-call(s32[1]{0:T(128)} %bitcast.node_ref, ...), custom_call_target="tpu_custom_call" | custom-call | flops 3489660928 | bytes 13631488 | tf_op jit(solution)/shard_map/expert/pallas_call | solution.py:336
  57.0 1.6 %collective-permute-start.22 = (bf16[64,1792]{1,0:T(8,128)(2,1)S(1)}, bf16[64,1792]{1,0:T(8,128)(2,1)S(1)}, u32[]{:S(2)}, u32[]{:S(2)}) collective-permute-start(bf16[64,1792]{1,0:T(8,128)(2,1)S(1)} %get-tuple-element.103), channel_id=1, source_target_pairs={{0,4},{1,5},{2,6},{3,7},{4,0},{5,1},{6,2},{7,3},{8,12},{9,13},{10,... | collective-permute-start | bytes 688136 | tf_op jit(solution)/shard_map/ppermute | solution.py:97
  60.4 4.3 %collective-permute-done.22 = bf16[64,1792]{1,0:T(8,128)(2,1)S(1)} collective-permute-done((bf16[64,1792]{1,0:T(8,128)(2,1)S(1)}, bf16[64,1792]{1,0:T(8,128)(2,1)S(1)}, u32[]{:S(2)}, u32[]{:S(2)}) %collective-permute-start.22) | collective-permute-done | bytes 229408 | tf_op jit(solution)/shard_map/ppermute | solution.py:97
  66.3 1.6 %collective-permute-start.25 = (bf16[32,1792]{1,0:T(8,128)(2,1)S(1)}, bf16[32,1792]{1,0:T(8,128)(2,1)S(1)}, u32[]{:S(2)}, u32[]{:S(2)}) collective-permute-start(bf16[32,1792]{1,0:T(8,128)(2,1)S(1)} %slice.103), channel_id=1, source_target_pairs={{0,4},{1,5},{2,6},{3,7},{4,0},{5,1},{6,2},{7,3},{8,12},{9,13},{10,... | collective-permute-start | bytes 344072 | tf_op jit(solution)/shard_map/ppermute | solution.py:97
  67.9 1.8 %collective-permute-done.23 = bf16[32,1792]{1,0:T(8,128)(2,1)S(1)} collective-permute-done((bf16[32,1792]{1,0:T(8,128)(2,1)S(1)}, bf16[32,1792]{1,0:T(8,128)(2,1)S(1)}, u32[]{:S(2)}, u32[]{:S(2)}) %collective-permute-start.23) | collective-permute-done | bytes 114720 | tf_op jit(solution)/shard_map/ppermute | solution.py:97
  71.3 1.6 %collective-permute-start.27 = (bf16[64,1792]{1,0:T(8,128)(2,1)S(1)}, bf16[64,1792]{1,0:T(8,128)(2,1)S(1)}, u32[]{:S(2)}, u32[]{:S(2)}) collective-permute-start(bf16[64,1792]{1,0:T(8,128)(2,1)S(1)} %add_convert_fusion.4), channel_id=1, source_target_pairs={{0,4},{1,5},{2,6},{3,7},{4,0},{5,1},{6,2},{7,3},{8,12},{9,13},{10,... | collective-permute-start | bytes 688136 | tf_op jit(solution)/shard_map/ppermute | solution.py:97
  73.7 3.7 %collective-permute-done.27 = bf16[64,1792]{1,0:T(8,128)(2,1)S(1)} collective-permute-done((bf16[64,1792]{1,0:T(8,128)(2,1)S(1)}, bf16[64,1792]{1,0:T(8,128)(2,1)S(1)}, u32[]{:S(2)}, u32[]{:S(2)}) %collective-permute-start.27) | collective-permute-done | bytes 229408 | tf_op jit(solution)/shard_map/ppermute | solution.py:97
  77.5 1.6 %collective-permute-done.29 = bf16[64,1792]{1,0:T(8,128)(2,1)S(1)} collective-permute-done((bf16[64,1792]{1,0:T(8,128)(2,1)S(1)}, bf16[64,1792]{1,0:T(8,128)(2,1)S(1)}, u32[]{:S(2)}, u32[]{:S(2)}) %collective-permute-start.29) | collective-permute-done | bytes 229408 | tf_op jit(solution)/shard_map/ppermute | solution.py:97
  81.2 3.4 %collective-permute-done.30 = bf16[16,3584]{1,0:T(8,128)(2,1)S(1)} collective-permute-done((bf16[16,3584]{1,0:T(8,128)(2,1)S(1)}, bf16[16,3584]{1,0:T(8,128)(2,1)S(1)}, u32[]{:S(2)}, u32[]{:S(2)}) %collective-permute-start.30) | collective-permute-done | bytes 114720 | tf_op jit(solution)/shard_map/ppermute | solution.py:97
  85.9 1.9 %collective-permute-start.34 = (bf16[8,3584]{1,0:T(8,128)(2,1)S(1)}, bf16[8,3584]{1,0:T(8,128)(2,1)S(1)}, u32[]{:S(2)}, u32[]{:S(2)}) collective-permute-start(bf16[8,3584]{1,0:T(8,128)(2,1)S(1)} %get-tuple-element.120), channel_id=1, source_target_pairs={{0,16},{1,17},{2,18},{3,19},{4,20},{5,21},{6,22},{7,23},{8,24},{9,... | collective-permute-start | bytes 172040 | tf_op jit(solution)/shard_map/ppermute | solution.py:97
  87.8 1.5 %collective-permute-start.36 = (bf16[8,3584]{1,0:T(8,128)(2,1)S(1)}, bf16[8,3584]{1,0:T(8,128)(2,1)S(1)}, u32[]{:S(2)}, u32[]{:S(2)}) collective-permute-start(bf16[8,3584]{1,0:T(8,128)(2,1)S(1)} %get-tuple-element.121), channel_id=1, source_target_pairs={{0,24},{1,25},{2,26},{3,27},{4,28},{5,29},{6,30},{7,31},{8,16},{9,... | collective-permute-start | bytes 172040 | tf_op jit(solution)/shard_map/ppermute | solution.py:97
  89.8 1.9 %collective-permute-done.34 = bf16[8,3584]{1,0:T(8,128)(2,1)S(1)} collective-permute-done((bf16[8,3584]{1,0:T(8,128)(2,1)S(1)}, bf16[8,3584]{1,0:T(8,128)(2,1)S(1)}, u32[]{:S(2)}, u32[]{:S(2)}) %collective-permute-start.34) | collective-permute-done | bytes 57376 | tf_op jit(solution)/shard_map/ppermute | solution.py:97
  91.7 2.2 %collective-permute-done.36 = bf16[8,3584]{1,0:T(8,128)(2,1)S(1)} collective-permute-done((bf16[8,3584]{1,0:T(8,128)(2,1)S(1)}, bf16[8,3584]{1,0:T(8,128)(2,1)S(1)}, u32[]{:S(2)}, u32[]{:S(2)}) %collective-permute-start.36) | collective-permute-done | bytes 57376 | tf_op jit(solution)/shard_map/ppermute | solution.py:97
  (94 shorter events, 27.2 us)
Async XLA Ops:
  3.1 7.8 %collective-permute-start = (bf16[8,4096]{1,0:T(8,128)(2,1)S(1)}, bf16[8,4096]{1,0:T(8,128)(2,1)S(1)}, u32[]{:S(2)}, u32[]{:S(2)}) collective-permute-start(bf16[8,4096]{1,0:T(8,128)(2,1)S(1)} %get-tuple-element.59.refs_0_), channel_id=1, source_target_pairs={{0,16},{1,17},{2,18},{3,19},{4,20},{5,21},{6,22},{7,23},{8,24},{9,... | collective-permute-start | bytes 196616 | tf_op jit(solution)/shard_map/ppermute | solution.py:97
  10.9 5.6 %collective-permute-start.1 = (bf16[16,4096]{1,0:T(8,128)(2,1)S(1)}, bf16[16,4096]{1,0:T(8,128)(2,1)S(1)}, u32[]{:S(2)}, u32[]{:S(2)}) collective-permute-start(bf16[16,4096]{1,0:T(8,128)(2,1)S(1)} %join.8.refs_0_), channel_id=1, source_target_pairs={{0,8},{1,9},{2,10},{3,11},{4,12},{5,13},{6,14},{7,15},{8,0},{9,1},... | collective-permute-start | bytes 393224 | tf_op jit(solution)/shard_map/ppermute | solution.py:97
  11.5 5.8 %collective-permute-start.2 = (bf16[8,3200]{1,0:T(8,128)(2,1)S(1)}, bf16[8,3200]{1,0:T(8,128)(2,1)S(1)}, u32[]{:S(2)}, u32[]{:S(2)}) collective-permute-start(bf16[8,3200]{1,0:T(8,128)(2,1)S(1)} %get-tuple-element.64.refs_0_), channel_id=1, source_target_pairs={{0,16},{1,17},{2,18},{3,19},{4,20},{5,21},{6,22},{7,23},{8,24},{9,... | collective-permute-start | bytes 153608 | tf_op jit(solution)/shard_map/ppermute | solution.py:97
  17.3 9.5 %collective-permute-start.3 = (bf16[32,2048]{1,0:T(8,128)(2,1)S(1)}, bf16[32,2048]{1,0:T(8,128)(2,1)S(1)}, u32[]{:S(2)}, u32[]{:S(2)}) collective-permute-start(bf16[32,2048]{1,0:T(8,128)(2,1)S(1)} %get-tuple-element.65.refs_0_), channel_id=1, source_target_pairs={{0,1},{1,0},{2,3},{3,2},{4,5},{5,4},{6,7},{7,6},{8,9},{9,8},{10,11... | collective-permute-start | bytes 393224 | tf_op jit(solution)/shard_map/ppermute | solution.py:97
  18.8 8.0 %collective-permute-start.4 = (bf16[32,2048]{1,0:T(8,128)(2,1)S(1)}, bf16[32,2048]{1,0:T(8,128)(2,1)S(1)}, u32[]{:S(2)}, u32[]{:S(2)}) collective-permute-start(bf16[32,2048]{1,0:T(8,128)(2,1)S(1)} %get-tuple-element.66.refs_0_), channel_id=1, source_target_pairs={{0,4},{1,5},{2,6},{3,7},{4,0},{5,1},{6,2},{7,3},{8,12},{9,13},{10,... | collective-permute-start | bytes 393224 | tf_op jit(solution)/shard_map/ppermute | solution.py:97
  20.3 6.4 %collective-permute-start.5 = (bf16[16,3200]{1,0:T(8,128)(2,1)S(1)}, bf16[16,3200]{1,0:T(8,128)(2,1)S(1)}, u32[]{:S(2)}, u32[]{:S(2)}) collective-permute-start(bf16[16,3200]{1,0:T(8,128)(2,1)S(1)} %join.12.refs_0_), channel_id=1, source_target_pairs={{0,8},{1,9},{2,10},{3,11},{4,12},{5,13},{6,14},{7,15},{8,0},{9,1},... | collective-permute-start | bytes 307208 | tf_op jit(solution)/shard_map/ppermute | solution.py:97
  26.8 8.6 %collective-permute-start.6 = (bf16[64,2048]{1,0:T(8,128)(2,1)S(1)}, bf16[64,2048]{1,0:T(8,128)(2,1)S(1)}, u32[]{:S(2)}, u32[]{:S(2)}) collective-permute-start(bf16[64,2048]{1,0:T(8,128)(2,1)S(1)} %join.10.refs_0_), channel_id=1, source_target_pairs={{0,4},{1,5},{2,6},{3,7},{4,0},{5,1},{6,2},{7,3},{8,12},{9,13},{10,... | collective-permute-start | bytes 786440 | tf_op jit(solution)/shard_map/ppermute | solution.py:97
  27.4 8.0 %collective-permute-start.7 = (bf16[64,2048]{1,0:T(8,128)(2,1)S(1)}, bf16[64,2048]{1,0:T(8,128)(2,1)S(1)}, u32[]{:S(2)}, u32[]{:S(2)}) collective-permute-start(bf16[64,2048]{1,0:T(8,128)(2,1)S(1)} %join.11.refs_4_), channel_id=1, source_target_pairs={{0,1},{1,0},{2,3},{3,2},{4,5},{5,4},{6,7},{7,6},{8,9},{9,8},{10,11... | collective-permute-start | bytes 786440 | tf_op jit(solution)/shard_map/ppermute | solution.py:97
  28.0 7.5 %collective-permute-start.9 = (bf16[32,1664]{1,0:T(8,128)(2,1)S(1)}, bf16[32,1664]{1,0:T(8,128)(2,1)S(1)}, u32[]{:S(2)}, u32[]{:S(2)}) collective-permute-start(bf16[32,1664]{1,0:T(8,128)(2,1)S(1)} %get-tuple-element.76.refs_0_), channel_id=1, source_target_pairs={{0,4},{1,5},{2,6},{3,7},{4,0},{5,1},{6,2},{7,3},{8,12},{9,13},{10,... | collective-permute-start | bytes 319496 | tf_op jit(solution)/shard_map/ppermute | solution.py:97
  29.5 5.9 %collective-permute-start.8 = (bf16[32,1536]{1,0:T(8,128)(2,1)S(1)}, bf16[32,1536]{1,0:T(8,128)(2,1)S(1)}, u32[]{:S(2)}, u32[]{:S(2)}) collective-permute-start(bf16[32,1536]{1,0:T(8,128)(2,1)S(1)} %get-tuple-element.74.refs_0_), channel_id=1, source_target_pairs={{0,1},{1,0},{2,3},{3,2},{4,5},{5,4},{6,7},{7,6},{8,9},{9,8},{10,11... | collective-permute-start | bytes 294920 | tf_op jit(solution)/shard_map/ppermute | solution.py:97
  36.5 7.4 %collective-permute-start.11 = (bf16[64,1664]{1,0:T(8,128)(2,1)S(1)}, bf16[64,1664]{1,0:T(8,128)(2,1)S(1)}, u32[]{:S(2)}, u32[]{:S(2)}) collective-permute-start(bf16[64,1664]{1,0:T(8,128)(2,1)S(1)} %join.15.refs_4_), channel_id=1, source_target_pairs={{0,1},{1,0},{2,3},{3,2},{4,5},{5,4},{6,7},{7,6},{8,9},{9,8},{10,11... | collective-permute-start | bytes 638984 | tf_op jit(solution)/shard_map/ppermute | solution.py:97
  37.2 6.8 %collective-permute-start.10 = (bf16[64,1536]{1,0:T(8,128)(2,1)S(1)}, bf16[64,1536]{1,0:T(8,128)(2,1)S(1)}, u32[]{:S(2)}, u32[]{:S(2)}) collective-permute-start(bf16[64,1536]{1,0:T(8,128)(2,1)S(1)} %join.14.refs_0_), channel_id=1, source_target_pairs={{0,4},{1,5},{2,6},{3,7},{4,0},{5,1},{6,2},{7,3},{8,12},{9,13},{10,... | collective-permute-start | bytes 589832 | tf_op jit(solution)/shard_map/ppermute | solution.py:97
  57.0 7.8 %collective-permute-start.22 = (bf16[64,1792]{1,0:T(8,128)(2,1)S(1)}, bf16[64,1792]{1,0:T(8,128)(2,1)S(1)}, u32[]{:S(2)}, u32[]{:S(2)}) collective-permute-start(bf16[64,1792]{1,0:T(8,128)(2,1)S(1)} %get-tuple-element.103), channel_id=1, source_target_pairs={{0,4},{1,5},{2,6},{3,7},{4,0},{5,1},{6,2},{7,3},{8,12},{9,13},{10,... | collective-permute-start | bytes 688136 | tf_op jit(solution)/shard_map/ppermute | solution.py:97
  58.5 7.7 %collective-permute-start.24 = (bf16[64,1792]{1,0:T(8,128)(2,1)S(1)}, bf16[64,1792]{1,0:T(8,128)(2,1)S(1)}, u32[]{:S(2)}, u32[]{:S(2)}) collective-permute-start(bf16[64,1792]{1,0:T(8,128)(2,1)S(1)} %get-tuple-element.105), channel_id=1, source_target_pairs={{0,1},{1,0},{2,3},{3,2},{4,5},{5,4},{6,7},{7,6},{8,9},{9,8},{10,11... | collective-permute-start | bytes 688136 | tf_op jit(solution)/shard_map/ppermute | solution.py:97
  59.9 11.3 %collective-permute-start.26 = (bf16[128,1792]{1,0:T(8,128)(2,1)S(1)}, bf16[128,1792]{1,0:T(8,128)(2,1)S(1)}, u32[]{:S(2)}, u32[]{:S(2)}) collective-permute-start(bf16[128,1792]{1,0:T(8,128)(2,1)S(1)} %get-tuple-element.107), channel_id=1, source_target_pairs={{0,2},{1,3},{2,0},{3,1},{4,6},{5,7},{6,4},{7,5},{8,10},{9,11},{10,... | collective-permute-start | bytes 1376264 | tf_op jit(solution)/shard_map/ppermute | solution.py:97
  59.9 13.0 %collective-permute-start.28 = (bf16[128,1792]{1,0:T(8,128)(2,1)S(1)}, bf16[128,1792]{1,0:T(8,128)(2,1)S(1)}, u32[]{:S(2)}, u32[]{:S(2)}) collective-permute-start(bf16[128,1792]{1,0:T(8,128)(2,1)S(1)} %get-tuple-element.110), channel_id=1, source_target_pairs={{0,2},{1,3},{2,0},{3,1},{4,6},{5,7},{6,4},{7,5},{8,10},{9,11},{10,... | collective-permute-start | bytes 1376264 | tf_op jit(solution)/shard_map/ppermute | solution.py:97
  71.3 6.1 %collective-permute-start.27 = (bf16[64,1792]{1,0:T(8,128)(2,1)S(1)}, bf16[64,1792]{1,0:T(8,128)(2,1)S(1)}, u32[]{:S(2)}, u32[]{:S(2)}) collective-permute-start(bf16[64,1792]{1,0:T(8,128)(2,1)S(1)} %add_convert_fusion.4), channel_id=1, source_target_pairs={{0,4},{1,5},{2,6},{3,7},{4,0},{5,1},{6,2},{7,3},{8,12},{9,13},{10,... | collective-permute-start | bytes 688136 | tf_op jit(solution)/shard_map/ppermute | solution.py:97
  73.0 6.1 %collective-permute-start.29 = (bf16[64,1792]{1,0:T(8,128)(2,1)S(1)}, bf16[64,1792]{1,0:T(8,128)(2,1)S(1)}, u32[]{:S(2)}, u32[]{:S(2)}) collective-permute-start(bf16[64,1792]{1,0:T(8,128)(2,1)S(1)} %add_convert_fusion.1), channel_id=1, source_target_pairs={{0,1},{1,0},{2,3},{3,2},{4,5},{5,4},{6,7},{7,6},{8,9},{9,8},{10,11... | collective-permute-start | bytes 688136 | tf_op jit(solution)/shard_map/ppermute | solution.py:97
  79.1 5.5 %collective-permute-start.30 = (bf16[16,3584]{1,0:T(8,128)(2,1)S(1)}, bf16[16,3584]{1,0:T(8,128)(2,1)S(1)}, u32[]{:S(2)}, u32[]{:S(2)}) collective-permute-start(bf16[16,3584]{1,0:T(8,128)(2,1)S(1)} %slice.85), channel_id=1, source_target_pairs={{0,8},{1,9},{2,10},{3,11},{4,12},{5,13},{6,14},{7,15},{8,0},{9,1},... | collective-permute-start | bytes 344072 | tf_op jit(solution)/shard_map/ppermute | solution.py:97
  79.5 6.3 %collective-permute-start.33 = (bf16[32,1792]{1,0:T(8,128)(2,1)S(1)}, bf16[32,1792]{1,0:T(8,128)(2,1)S(1)}, u32[]{:S(2)}, u32[]{:S(2)}) collective-permute-start(bf16[32,1792]{1,0:T(8,128)(2,1)S(1)} %slice.91), channel_id=1, source_target_pairs={{0,4},{1,5},{2,6},{3,7},{4,0},{5,1},{6,2},{7,3},{8,12},{9,13},{10,... | collective-permute-start | bytes 344072 | tf_op jit(solution)/shard_map/ppermute | solution.py:97
  80.1 5.8 %collective-permute-start.32 = (bf16[32,1792]{1,0:T(8,128)(2,1)S(1)}, bf16[32,1792]{1,0:T(8,128)(2,1)S(1)}, u32[]{:S(2)}, u32[]{:S(2)}) collective-permute-start(bf16[32,1792]{1,0:T(8,128)(2,1)S(1)} %slice.89), channel_id=1, source_target_pairs={{0,1},{1,0},{2,3},{3,2},{4,5},{5,4},{6,7},{7,6},{8,9},{9,8},{10,11... | collective-permute-start | bytes 344072 | tf_op jit(solution)/shard_map/ppermute | solution.py:97
  84.7 5.1 %collective-permute-start.31 = (bf16[8,3584]{1,0:T(8,128)(2,1)S(1)}, bf16[8,3584]{1,0:T(8,128)(2,1)S(1)}, u32[]{:S(2)}, u32[]{:S(2)}) collective-permute-start(bf16[8,3584]{1,0:T(8,128)(2,1)S(1)} %slice.109), channel_id=1, source_target_pairs={{0,16},{1,17},{2,18},{3,19},{4,20},{5,21},{6,22},{7,23},{8,24},{9,... | collective-permute-start | bytes 172040 | tf_op jit(solution)/shard_map/ppermute | solution.py:97
  85.9 5.8 %collective-permute-start.34 = (bf16[8,3584]{1,0:T(8,128)(2,1)S(1)}, bf16[8,3584]{1,0:T(8,128)(2,1)S(1)}, u32[]{:S(2)}, u32[]{:S(2)}) collective-permute-start(bf16[8,3584]{1,0:T(8,128)(2,1)S(1)} %get-tuple-element.120), channel_id=1, source_target_pairs={{0,16},{1,17},{2,18},{3,19},{4,20},{5,21},{6,22},{7,23},{8,24},{9,... | collective-permute-start | bytes 172040 | tf_op jit(solution)/shard_map/ppermute | solution.py:97
  87.8 6.1 %collective-permute-start.36 = (bf16[8,3584]{1,0:T(8,128)(2,1)S(1)}, bf16[8,3584]{1,0:T(8,128)(2,1)S(1)}, u32[]{:S(2)}, u32[]{:S(2)}) collective-permute-start(bf16[8,3584]{1,0:T(8,128)(2,1)S(1)} %get-tuple-element.121), channel_id=1, source_target_pairs={{0,24},{1,25},{2,26},{3,27},{4,28},{5,29},{6,30},{7,31},{8,16},{9,... | collective-permute-start | bytes 172040 | tf_op jit(solution)/shard_map/ppermute | solution.py:97
  (17 other events, 40.0 us)

commit v10 on v9

--- a/solution.py
+++ b/solution.py
@@ -99,21 +99,19 @@
     def over(self, block, digit):
         return [block] + [self.swap(block, digit, m) for m in range(1, self.sizes[digit])]
 
-    def sum_over(self, parts, digit):
-        return add(parts[:1] + [self.swap(parts[m], digit, m) for m in range(1, len(parts))])
-
-    def sum_rows_over(self, block, digit):
+    def receive(self, parts, digit):
+        return parts[:1] + [self.swap(parts[m], digit, m) for m in range(1, len(parts))]
+
+    def receive_rows(self, block, digit):
         rows = block.shape[0] // self.sizes[digit]
         parts = [block[m * rows : (m + 1) * rows] for m in range(self.sizes[digit])]
-        return self.sum_over(parts, digit)
-
-    def high_sum(self, line):
-        for m in reversed(self.masks):
-            half = line.shape[0] // 2
-            line = add([line[:half], self.swap(line[half:], HIGH, m)])
-        return line
-
-    def high_sum_direct(self, line):
+        return self.receive(parts, digit)
+
+    def receive_half(self, line, mask):
+        half = line.shape[0] // 2
+        return [line[:half], self.swap(line[half:], HIGH, mask)]
+
+    def receive_high(self, line):
         order = [0]
         for m in self.masks:
             order += [m | other for other in order]
@@ -121,7 +119,7 @@
         parts = [line[:rows]]
         for i in range(1, len(order)):
             parts.append(self.swap(line[i * rows : (i + 1) * rows], HIGH, order[i]))
-        return add(parts)
+        return parts
 
 
 def add(parts):
@@ -157,7 +155,17 @@
     return pl.cdiv(2 * experts, 128) * 128
 
 
-def pack_kernel(experts, rows_ref, ids_ref, gates_ref, head_ref, tail_ref):
+def pack_kernel(experts, *refs):
+    sources, (head_ref, tail_ref, *targets), sems = refs[:3], refs[3:-1], refs[-1]
+    copies = [
+        pltpu.make_async_copy(source, target, sems.at[i])
+        for i, (source, target) in enumerate(zip(sources, targets))
+    ]
+    for copy in copies:
+        copy.start()
+    rows_ref, ids_ref, gates_ref = targets
+    for copy in copies[1:]:
+        copy.wait()
     extra = table_width(experts)
     split, width = head_ref.shape[1], tail_ref.shape[1] - extra
     gates = gates_ref[...]
@@ -170,6 +178,7 @@
         table += jnp.where(expert == ids[:, k : k + 1], shares[:, k : k + 1], 0.0)
     high = table.astype(jnp.bfloat16).astype(jnp.float32)
     table = jnp.where(lane < experts, high, jnp.where(lane < 2 * experts, table - high, 0.0))
+    copies[0].wait()
     head_ref[...] = rows_ref[:, :split]
     tail_ref[:, :width] = rows_ref[:, split:]
     tail_ref[:, width:] = table.astype(jnp.bfloat16)
@@ -177,15 +186,20 @@
 
 def pack(split, experts, moe_rows, route_ids, route_gates):
     rows, width = moe_rows.shape
+    sources = (moe_rows, route_ids, route_gates)
     return pl.pallas_call(
         functools.partial(pack_kernel, experts),
+        in_specs=[pl.BlockSpec(memory_space=pltpu.HBM)] * 3,
+        out_specs=[pl.BlockSpec(memory_space=pltpu.VMEM)] * 2,
+        scratch_shapes=[pltpu.VMEM(source.shape, source.dtype) for source in sources]
+        + [pltpu.SemaphoreType.DMA((3,))],
         out_shape=[
             jax.ShapeDtypeStruct((rows, columns), jnp.bfloat16)
             for columns in (split, width - split + table_width(experts))
         ],
-        compiler_params=pltpu.CompilerParams(vmem_limit_bytes=16 * MEBI),
+        compiler_params=pltpu.CompilerParams(vmem_limit_bytes=4 * MEBI),
         name="pack",
-    )(moe_rows, route_ids, route_gates)
+    )(*[in_hbm(source) for source in sources])
 
 
 def line_order(sizes):
@@ -399,7 +413,7 @@
 
     head, tail = pack(split, experts, moe_rows, route_ids, route_gates)
     came = grid.swap(head, HIGH, grid.masks[0])
-    tail, came = tied((tail, came))
+    tail, came, attn_latent = tied((tail, came, attn_latent))
     head = [head, came]
     for m in grid.masks[1:]:
         line = join(head)
@@ -413,7 +427,7 @@
         tail = [line, grid.swap(line, HIGH, m)]
     tail = join_halves(tail)
     head = step(head)
-    head, tail, attn_latent = tied(([join(head[0]), join(head[1])], tail, attn_latent))
+    head, tail = tied(([join(head[0]), join(head[1])], tail))
     head, tail = tied((second_step(head), step(tail)))
     head = with_other_core(head)
     tail = second_step([join(tail[0]), join(tail[1])])
@@ -442,21 +456,27 @@
             )
         return sums
 
-    def second_sums(sums):
-        return [grid.sum_over(sums[way], digits[way]) for way in range(2)]
-
-    def first_axis_sums(blocks):
-        return jnp.concatenate(
-            [grid.sum_rows_over(blocks[way], digits[1 - way]) for way in range(2)], axis=1
-        )
+    def second_axis(ways):
+        return [grid.receive(ways[way], digits[way]) for way in range(2)]
+
+    def first_axis(ways):
+        return [grid.receive_rows(add(ways[way]), digits[1 - way]) for way in range(2)]
+
+    def line_of(ways):
+        return jnp.concatenate([add(way) for way in ways], axis=1)
 
     head, tail = products[: len(products) // 2], products[len(products) // 2 :]
     tail, head = tied((tail, core_sums(head)))
-    head = first_axis_sums(second_sums(head))
-    head, tail = tied((head, second_sums(core_sums(tail))))
-    head = grid.high_sum(head)
-    tail = grid.high_sum_direct(first_axis_sums(tail))
-    return (jnp.concatenate([head, tail], axis=1), attn_latent)
+    head, tail = tied((second_axis(head), core_sums(tail)))
+    head, tail = tied((first_axis(head), second_axis(tail)))
+    head = line_of(head)
+    masks = grid.masks[::-1]
+    head, tail = tied((grid.receive_half(head, masks[0]), first_axis(tail)))
+    for m in masks[1:]:
+        head = grid.receive_half(add(head), m)
+    tail = grid.receive_high(line_of(tail))
+    head, tail = tied((head, tail))
+    return (jnp.concatenate([add(head), add(tail)], axis=1), attn_latent)
 
 
 def solution(mesh):

time: 95.1 us -> 92.3 us (0.971)
  local copies, waits for them, and re-layouts: 2.97 us -> 0.73 us
  waiting for transfers between devices: 35.6 us -> 34.6 us
    unnamed x8 -> x2, local copies, waits for them, and re-layouts: 2.92 us -> 0.65 us
    ppermute x37, waiting for transfers between devices: 35.6 us -> 34.6 us  [swap(): return lax.ppermute(value, everyone, pairs)]
  transfers between devices with their start and end apart: 37 -> 37, of which waited for: 19 -> 19; matrix products, arithmetic and copies ran while one was open for 1% -> 1% of each run, Pallas kernels for 8% -> 9%
where the time goes in v10:
time: 92.3 us; the launch traced here: 92.1 us
  starting transfers between devices  37.4 us (41%)
  waiting for transfers between devices  34.6 us (37%)
  Pallas kernels  17 us (18%)
  other arithmetic  1.56 us (2%)
    ppermute x37, starting transfers between devices, swap(): return lax.ppermute(value, everyone, pairs)  37.4 us
    ppermute x37, waiting for transfers between devices, swap(): return lax.ppermute(value, everyone, pairs)  34.6 us
    pallas_call x1, Pallas kernels, expert(): pl.pallas_call(functools.partial(expert_kernel, counts, sizes, experts, t...  7.99 us
    pallas_call x1, Pallas kernels, first_sums(): pl.pallas_call(functools.partial(first_kernel, counts, sizes, tile), in_s...  4.21 us
    pallas_call x1, Pallas kernels, attention(): pl.pallas_call(attention_kernel, in_specs=[pl.BlockSpec(memory_space=pltp...  3.66 us
  transfers between devices with their start and end apart: 37, of which 19 were waited for; matrix products, arithmetic and copies ran while one was open for 1% of the time, Pallas kernels for 9%

profile of v10, /device:TPU:0, one launch (start us, length us, event | category | flops | bytes accessed | tf_op | source)
XLA Modules:
  0.0 92.1 jit_solution(8968156952032743084)
XLA Ops:
  1.6 4.1 %collective-permute-start = (bf16[8,4096]{1,0:T(8,128)(2,1)S(1)}, bf16[8,4096]{1,0:T(8,128)(2,1)S(1)}, u32[]{:S(2)}, u32[]{:S(2)}) collective-permute-start(bf16[8,4096]{1,0:T(8,128)(2,1)S(1)} %get-tuple-element.84.refs_0_), channel_id=1, source_target_pairs={{0,16},{1,17},{2,18},{3,19},{4,20},{5,21},{6,22},{7,23},{8,24},{9,... | collective-permute-start | bytes 196616 | tf_op jit(solution)/shard_map/ppermute | solution.py:97
  6.4 3.7 %attention.1 = bf16[2,64,512]{2,1,0:T(8,128)(2,1)} custom-call(s32[2]{0:T(128)S(1)} %copy-done, bf16[2,64,512]{2,1,0:T(8,128)(2,1)} %refs_0_.3, bf16[2,64,64]{2,1,0:T(8,128)(2,1)} %refs_1_.3, bf16[2,512,512]{2,1,0:T(8,128)(2,1)} %refs_2_.3, bf16[2,64,512]{2,1,0:T(8,128)(2,1)} %refs_3_.1), custom_call_target="tpu_custom_call" | custom-call | flops 134217728 | bytes 1048576 | tf_op jit(solution)/shard_map/attention/pallas_call | solution.py:54
  10.1 1.6 %collective-permute-start.1 = (bf16[16,4096]{1,0:T(8,128)(2,1)S(1)}, bf16[16,4096]{1,0:T(8,128)(2,1)S(1)}, u32[]{:S(2)}, u32[]{:S(2)}) collective-permute-start(bf16[16,4096]{1,0:T(8,128)(2,1)S(1)} %join.8.refs_0_), channel_id=1, source_target_pairs={{0,8},{1,9},{2,10},{3,11},{4,12},{5,13},{6,14},{7,15},{8,0},{9,1},... | collective-permute-start | bytes 393224 | tf_op jit(solution)/shard_map/ppermute | solution.py:97
  11.7 1.7 %collective-permute-start.2 = (bf16[8,3200]{1,0:T(8,128)(2,1)S(1)}, bf16[8,3200]{1,0:T(8,128)(2,1)S(1)}, u32[]{:S(2)}, u32[]{:S(2)}) collective-permute-start(bf16[8,3200]{1,0:T(8,128)(2,1)S(1)} %get-tuple-element.89.refs_0_), channel_id=1, source_target_pairs={{0,16},{1,17},{2,18},{3,19},{4,20},{5,21},{6,22},{7,23},{8,24},{9,... | collective-permute-start | bytes 153608 | tf_op jit(solution)/shard_map/ppermute | solution.py:97
  13.4 2.3 %collective-permute-done.1.refs_1_ = bf16[16,4096]{1,0:T(8,128)(2,1)S(1)} collective-permute-done((bf16[16,4096]{1,0:T(8,128)(2,1)S(1)}, bf16[16,4096]{1,0:T(8,128)(2,1)S(1)}, u32[]{:S(2)}, u32[]{:S(2)}) %collective-permute-start.1) | collective-permute-done | bytes 131104 | tf_op jit(solution)/shard_map/ppermute | solution.py:97
  16.8 1.5 %collective-permute-start.3 = (bf16[32,2048]{1,0:T(8,128)(2,1)S(1)}, bf16[32,2048]{1,0:T(8,128)(2,1)S(1)}, u32[]{:S(2)}, u32[]{:S(2)}) collective-permute-start(bf16[32,2048]{1,0:T(8,128)(2,1)S(1)} %get-tuple-element.90.refs_0_), channel_id=1, source_target_pairs={{0,1},{1,0},{2,3},{3,2},{4,5},{5,4},{6,7},{7,6},{8,9},{9,8},{10,11... | collective-permute-start | bytes 393224 | tf_op jit(solution)/shard_map/ppermute | solution.py:97
  18.3 1.5 %collective-permute-start.4 = (bf16[32,2048]{1,0:T(8,128)(2,1)S(1)}, bf16[32,2048]{1,0:T(8,128)(2,1)S(1)}, u32[]{:S(2)}, u32[]{:S(2)}) collective-permute-start(bf16[32,2048]{1,0:T(8,128)(2,1)S(1)} %get-tuple-element.91.refs_0_), channel_id=1, source_target_pairs={{0,4},{1,5},{2,6},{3,7},{4,0},{5,1},{6,2},{7,3},{8,12},{9,13},{10,... | collective-permute-start | bytes 393224 | tf_op jit(solution)/shard_map/ppermute | solution.py:97
  21.0 3.6 %collective-permute-done.5.refs_1_ = bf16[16,3200]{1,0:T(8,128)(2,1)S(1)} collective-permute-done((bf16[16,3200]{1,0:T(8,128)(2,1)S(1)}, bf16[16,3200]{1,0:T(8,128)(2,1)S(1)}, u32[]{:S(2)}, u32[]{:S(2)}) %collective-permute-start.5) | collective-permute-done | bytes 102432 | tf_op jit(solution)/shard_map/ppermute | solution.py:97
  27.3 1.5 %collective-permute-start.8 = (bf16[32,1536]{1,0:T(8,128)(2,1)S(1)}, bf16[32,1536]{1,0:T(8,128)(2,1)S(1)}, u32[]{:S(2)}, u32[]{:S(2)}) collective-permute-start(bf16[32,1536]{1,0:T(8,128)(2,1)S(1)} %get-tuple-element.99.refs_0_), channel_id=1, source_target_pairs={{0,1},{1,0},{2,3},{3,2},{4,5},{5,4},{6,7},{7,6},{8,9},{9,8},{10,11... | collective-permute-start | bytes 294920 | tf_op jit(solution)/shard_map/ppermute | solution.py:97
  28.7 3.9 %collective-permute-done.8.refs_1_ = bf16[32,1536]{1,0:T(8,128)(2,1)S(1)} collective-permute-done((bf16[32,1536]{1,0:T(8,128)(2,1)S(1)}, bf16[32,1536]{1,0:T(8,128)(2,1)S(1)}, u32[]{:S(2)}, u32[]{:S(2)}) %collective-permute-start.8) | collective-permute-done | bytes 98336 | tf_op jit(solution)/shard_map/ppermute | solution.py:97
  36.0 4.2 %first_sums.1 = (f32[256,512]{1,0:T(8,128)S(1)}, f32[256,512]{1,0:T(8,128)S(1)}) custom-call(bf16[64,2048]{1,0:T(8,128)(2,1)S(1)} %join.10.refs_0_, bf16[64,2048]{1,0:T(8,128)(2,1)S(1)} %collective-permute-done.6.refs_1_, bf16[64,2048]{1,0:T(8,128)(2,1)S(1)} %collective-permute-done.12.refs_2_, bf16[64,2048]{1,0:T(8,128)(2,1)S(1)} %collective-permute-done.13.refs_3_, ...), custom_call_target="tpu_custom_call" | custom-call | flops 2147483648 | bytes 8388608 | tf_op jit(solution)/shard_map/first_sums/pallas_call | solution.py:274
  43.6 8.0 %expert.1 = (bf16[64,1792]{1,0:T(8,128)(2,1)S(1)}, bf16[64,1792]{1,0:T(8,128)(2,1)S(1)}, bf16[128,1792]{1,0:T(8,128)(2,1)S(1)}, bf16[64,1792]{1,0:T(8,128)(2,1)S...) custom-call(s32[1]{0:T(128)} %bitcast.node_ref, ...), custom_call_target="tpu_custom_call" | custom-call | flops 3489660928 | bytes 13631488 | tf_op jit(solution)/shard_map/expert/pallas_call | solution.py:350
  54.5 1.5 %collective-permute-start.22 = (bf16[64,1792]{1,0:T(8,128)(2,1)S(1)}, bf16[64,1792]{1,0:T(8,128)(2,1)S(1)}, u32[]{:S(2)}, u32[]{:S(2)}) collective-permute-start(bf16[64,1792]{1,0:T(8,128)(2,1)S(1)} %get-tuple-element.128), channel_id=1, source_target_pairs={{0,4},{1,5},{2,6},{3,7},{4,0},{5,1},{6,2},{7,3},{8,12},{9,13},{10,... | collective-permute-start | bytes 688136 | tf_op jit(solution)/shard_map/ppermute | solution.py:97
  57.4 1.7 %collective-permute-done.25 = bf16[128,1792]{1,0:T(8,128)(2,1)S(1)} collective-permute-done((bf16[128,1792]{1,0:T(8,128)(2,1)S(1)}, bf16[128,1792]{1,0:T(8,128)(2,1)S(1)}, u32[]{:S(2)}, u32[]{:S(2)}) %collective-permute-start.25) | collective-permute-done | bytes 458784 | tf_op jit(solution)/shard_map/ppermute | solution.py:97
  59.3 3.1 %collective-permute-done.22 = bf16[64,1792]{1,0:T(8,128)(2,1)S(1)} collective-permute-done((bf16[64,1792]{1,0:T(8,128)(2,1)S(1)}, bf16[64,1792]{1,0:T(8,128)(2,1)S(1)}, u32[]{:S(2)}, u32[]{:S(2)}) %collective-permute-start.22) | collective-permute-done | bytes 229408 | tf_op jit(solution)/shard_map/ppermute | solution.py:97
  64.3 1.4 %collective-permute-start.28 = (bf16[64,1792]{1,0:T(8,128)(2,1)S(1)}, bf16[64,1792]{1,0:T(8,128)(2,1)S(1)}, u32[]{:S(2)}, u32[]{:S(2)}) collective-permute-start(bf16[64,1792]{1,0:T(8,128)(2,1)S(1)} %get-tuple-element.142), channel_id=1, source_target_pairs={{0,4},{1,5},{2,6},{3,7},{4,0},{5,1},{6,2},{7,3},{8,12},{9,13},{10,... | collective-permute-start | bytes 688136 | tf_op jit(solution)/shard_map/ppermute | solution.py:97
  67.8 1.9 %collective-permute-done.27 = bf16[32,1792]{1,0:T(8,128)(2,1)S(1)} collective-permute-done((bf16[32,1792]{1,0:T(8,128)(2,1)S(1)}, bf16[32,1792]{1,0:T(8,128)(2,1)S(1)}, u32[]{:S(2)}, u32[]{:S(2)}) %collective-permute-start.27) | collective-permute-done | bytes 114720 | tf_op jit(solution)/shard_map/ppermute | solution.py:97
  69.8 4.5 %collective-permute-done.26 = bf16[32,1792]{1,0:T(8,128)(2,1)S(1)} collective-permute-done((bf16[32,1792]{1,0:T(8,128)(2,1)S(1)}, bf16[32,1792]{1,0:T(8,128)(2,1)S(1)}, u32[]{:S(2)}, u32[]{:S(2)}) %collective-permute-start.26) | collective-permute-done | bytes 114720 | tf_op jit(solution)/shard_map/ppermute | solution.py:97
  77.8 1.4 %collective-permute-done.30 = bf16[16,3584]{1,0:T(8,128)(2,1)S(1)} collective-permute-done((bf16[16,3584]{1,0:T(8,128)(2,1)S(1)}, bf16[16,3584]{1,0:T(8,128)(2,1)S(1)}, u32[]{:S(2)}, u32[]{:S(2)}) %collective-permute-start.30) | collective-permute-done | bytes 114720 | tf_op jit(solution)/shard_map/ppermute | solution.py:97
  80.5 1.5 %collective-permute-done.32 = bf16[32,1792]{1,0:T(8,128)(2,1)S(1)} collective-permute-done((bf16[32,1792]{1,0:T(8,128)(2,1)S(1)}, bf16[32,1792]{1,0:T(8,128)(2,1)S(1)}, u32[]{:S(2)}, u32[]{:S(2)}) %collective-permute-start.32) | collective-permute-done | bytes 114720 | tf_op jit(solution)/shard_map/ppermute | solution.py:97
  82.1 1.9 %collective-permute-start.33 = (bf16[8,3584]{1,0:T(8,128)(2,1)S(1)}, bf16[8,3584]{1,0:T(8,128)(2,1)S(1)}, u32[]{:S(2)}, u32[]{:S(2)}) collective-permute-start(bf16[8,3584]{1,0:T(8,128)(2,1)S(1)} %get-tuple-element.188), channel_id=1, source_target_pairs={{0,16},{1,17},{2,18},{3,19},{4,20},{5,21},{6,22},{7,23},{8,24},{9,... | collective-permute-start | bytes 172040 | tf_op jit(solution)/shard_map/ppermute | solution.py:97
  84.1 1.5 %collective-permute-start.36 = (bf16[8,3584]{1,0:T(8,128)(2,1)S(1)}, bf16[8,3584]{1,0:T(8,128)(2,1)S(1)}, u32[]{:S(2)}, u32[]{:S(2)}) collective-permute-start(bf16[8,3584]{1,0:T(8,128)(2,1)S(1)} %get-tuple-element.174), channel_id=1, source_target_pairs={{0,24},{1,25},{2,26},{3,27},{4,28},{5,29},{6,30},{7,31},{8,16},{9,... | collective-permute-start | bytes 172040 | tf_op jit(solution)/shard_map/ppermute | solution.py:97
  86.6 1.9 %collective-permute-start.35 = (bf16[8,3584]{1,0:T(8,128)(2,1)S(1)}, bf16[8,3584]{1,0:T(8,128)(2,1)S(1)}, u32[]{:S(2)}, u32[]{:S(2)}) collective-permute-start(bf16[8,3584]{1,0:T(8,128)(2,1)S(1)} %get-tuple-element.177), channel_id=1, source_target_pairs={{0,8},{1,9},{2,10},{3,11},{4,12},{5,13},{6,14},{7,15},{8,0},{9,1},... | collective-permute-start | bytes 172040 | tf_op jit(solution)/shard_map/ppermute | solution.py:97
  88.5 1.6 %collective-permute-done.36 = bf16[8,3584]{1,0:T(8,128)(2,1)S(1)} collective-permute-done((bf16[8,3584]{1,0:T(8,128)(2,1)S(1)}, bf16[8,3584]{1,0:T(8,128)(2,1)S(1)}, u32[]{:S(2)}, u32[]{:S(2)}) %collective-permute-start.36) | collective-permute-done | bytes 57376 | tf_op jit(solution)/shard_map/ppermute | solution.py:97
  (86 shorter events, 29.7 us)
Async XLA Ops:
  1.6 8.4 %collective-permute-start = (bf16[8,4096]{1,0:T(8,128)(2,1)S(1)}, bf16[8,4096]{1,0:T(8,128)(2,1)S(1)}, u32[]{:S(2)}, u32[]{:S(2)}) collective-permute-start(bf16[8,4096]{1,0:T(8,128)(2,1)S(1)} %get-tuple-element.84.refs_0_), channel_id=1, source_target_pairs={{0,16},{1,17},{2,18},{3,19},{4,20},{5,21},{6,22},{7,23},{8,24},{9,... | collective-permute-start | bytes 196616 | tf_op jit(solution)/shard_map/ppermute | solution.py:97
  10.1 5.6 %collective-permute-start.1 = (bf16[16,4096]{1,0:T(8,128)(2,1)S(1)}, bf16[16,4096]{1,0:T(8,128)(2,1)S(1)}, u32[]{:S(2)}, u32[]{:S(2)}) collective-permute-start(bf16[16,4096]{1,0:T(8,128)(2,1)S(1)} %join.8.refs_0_), channel_id=1, source_target_pairs={{0,8},{1,9},{2,10},{3,11},{4,12},{5,13},{6,14},{7,15},{8,0},{9,1},... | collective-permute-start | bytes 393224 | tf_op jit(solution)/shard_map/ppermute | solution.py:97
  11.7 5.0 %collective-permute-start.2 = (bf16[8,3200]{1,0:T(8,128)(2,1)S(1)}, bf16[8,3200]{1,0:T(8,128)(2,1)S(1)}, u32[]{:S(2)}, u32[]{:S(2)}) collective-permute-start(bf16[8,3200]{1,0:T(8,128)(2,1)S(1)} %get-tuple-element.89.refs_0_), channel_id=1, source_target_pairs={{0,16},{1,17},{2,18},{3,19},{4,20},{5,21},{6,22},{7,23},{8,24},{9,... | collective-permute-start | bytes 153608 | tf_op jit(solution)/shard_map/ppermute | solution.py:97
  16.8 7.8 %collective-permute-start.3 = (bf16[32,2048]{1,0:T(8,128)(2,1)S(1)}, bf16[32,2048]{1,0:T(8,128)(2,1)S(1)}, u32[]{:S(2)}, u32[]{:S(2)}) collective-permute-start(bf16[32,2048]{1,0:T(8,128)(2,1)S(1)} %get-tuple-element.90.refs_0_), channel_id=1, source_target_pairs={{0,1},{1,0},{2,3},{3,2},{4,5},{5,4},{6,7},{7,6},{8,9},{9,8},{10,11... | collective-permute-start | bytes 393224 | tf_op jit(solution)/shard_map/ppermute | solution.py:97
  18.3 6.3 %collective-permute-start.4 = (bf16[32,2048]{1,0:T(8,128)(2,1)S(1)}, bf16[32,2048]{1,0:T(8,128)(2,1)S(1)}, u32[]{:S(2)}, u32[]{:S(2)}) collective-permute-start(bf16[32,2048]{1,0:T(8,128)(2,1)S(1)} %get-tuple-element.91.refs_0_), channel_id=1, source_target_pairs={{0,4},{1,5},{2,6},{3,7},{4,0},{5,1},{6,2},{7,3},{8,12},{9,13},{10,... | collective-permute-start | bytes 393224 | tf_op jit(solution)/shard_map/ppermute | solution.py:97
  24.6 8.0 %collective-permute-start.6 = (bf16[64,2048]{1,0:T(8,128)(2,1)S(1)}, bf16[64,2048]{1,0:T(8,128)(2,1)S(1)}, u32[]{:S(2)}, u32[]{:S(2)}) collective-permute-start(bf16[64,2048]{1,0:T(8,128)(2,1)S(1)} %join.10.refs_0_), channel_id=1, source_target_pairs={{0,4},{1,5},{2,6},{3,7},{4,0},{5,1},{6,2},{7,3},{8,12},{9,13},{10,... | collective-permute-start | bytes 786440 | tf_op jit(solution)/shard_map/ppermute | solution.py:97
  25.2 7.4 %collective-permute-start.7 = (bf16[64,2048]{1,0:T(8,128)(2,1)S(1)}, bf16[64,2048]{1,0:T(8,128)(2,1)S(1)}, u32[]{:S(2)}, u32[]{:S(2)}) collective-permute-start(bf16[64,2048]{1,0:T(8,128)(2,1)S(1)} %join.11.refs_4_), channel_id=1, source_target_pairs={{0,1},{1,0},{2,3},{3,2},{4,5},{5,4},{6,7},{7,6},{8,9},{9,8},{10,11... | collective-permute-start | bytes 786440 | tf_op jit(solution)/shard_map/ppermute | solution.py:97
  25.9 6.8 %collective-permute-start.9 = (bf16[32,1664]{1,0:T(8,128)(2,1)S(1)}, bf16[32,1664]{1,0:T(8,128)(2,1)S(1)}, u32[]{:S(2)}, u32[]{:S(2)}) collective-permute-start(bf16[32,1664]{1,0:T(8,128)(2,1)S(1)} %get-tuple-element.101.refs_0_), channel_id=1, source_target_pairs={{0,4},{1,5},{2,6},{3,7},{4,0},{5,1},{6,2},{7,3},{8,12},{9,13},{10,... | collective-permute-start | bytes 319496 | tf_op jit(solution)/shard_map/ppermute | solution.py:97
  27.3 5.4 %collective-permute-start.8 = (bf16[32,1536]{1,0:T(8,128)(2,1)S(1)}, bf16[32,1536]{1,0:T(8,128)(2,1)S(1)}, u32[]{:S(2)}, u32[]{:S(2)}) collective-permute-start(bf16[32,1536]{1,0:T(8,128)(2,1)S(1)} %get-tuple-element.99.refs_0_), channel_id=1, source_target_pairs={{0,1},{1,0},{2,3},{3,2},{4,5},{5,4},{6,7},{7,6},{8,9},{9,8},{10,11... | collective-permute-start | bytes 294920 | tf_op jit(solution)/shard_map/ppermute | solution.py:97
  33.8 7.5 %collective-permute-start.11 = (bf16[64,1664]{1,0:T(8,128)(2,1)S(1)}, bf16[64,1664]{1,0:T(8,128)(2,1)S(1)}, u32[]{:S(2)}, u32[]{:S(2)}) collective-permute-start(bf16[64,1664]{1,0:T(8,128)(2,1)S(1)} %join.15.refs_4_), channel_id=1, source_target_pairs={{0,1},{1,0},{2,3},{3,2},{4,5},{5,4},{6,7},{7,6},{8,9},{9,8},{10,11... | collective-permute-start | bytes 638984 | tf_op jit(solution)/shard_map/ppermute | solution.py:97
  34.6 6.7 %collective-permute-start.10 = (bf16[64,1536]{1,0:T(8,128)(2,1)S(1)}, bf16[64,1536]{1,0:T(8,128)(2,1)S(1)}, u32[]{:S(2)}, u32[]{:S(2)}) collective-permute-start(bf16[64,1536]{1,0:T(8,128)(2,1)S(1)} %join.14.refs_0_), channel_id=1, source_target_pairs={{0,4},{1,5},{2,6},{3,7},{4,0},{5,1},{6,2},{7,3},{8,12},{9,13},{10,... | collective-permute-start | bytes 589832 | tf_op jit(solution)/shard_map/ppermute | solution.py:97
  54.5 7.8 %collective-permute-start.22 = (bf16[64,1792]{1,0:T(8,128)(2,1)S(1)}, bf16[64,1792]{1,0:T(8,128)(2,1)S(1)}, u32[]{:S(2)}, u32[]{:S(2)}) collective-permute-start(bf16[64,1792]{1,0:T(8,128)(2,1)S(1)} %get-tuple-element.128), channel_id=1, source_target_pairs={{0,4},{1,5},{2,6},{3,7},{4,0},{5,1},{6,2},{7,3},{8,12},{9,13},{10,... | collective-permute-start | bytes 688136 | tf_op jit(solution)/shard_map/ppermute | solution.py:97
  56.0 7.5 %collective-permute-start.23 = (bf16[64,1792]{1,0:T(8,128)(2,1)S(1)}, bf16[64,1792]{1,0:T(8,128)(2,1)S(1)}, u32[]{:S(2)}, u32[]{:S(2)}) collective-permute-start(bf16[64,1792]{1,0:T(8,128)(2,1)S(1)} %get-tuple-element.130), channel_id=1, source_target_pairs={{0,1},{1,0},{2,3},{3,2},{4,5},{5,4},{6,7},{7,6},{8,9},{9,8},{10,11... | collective-permute-start | bytes 688136 | tf_op jit(solution)/shard_map/ppermute | solution.py:97
  63.6 6.1 %collective-permute-start.27 = (bf16[32,1792]{1,0:T(8,128)(2,1)S(1)}, bf16[32,1792]{1,0:T(8,128)(2,1)S(1)}, u32[]{:S(2)}, u32[]{:S(2)}) collective-permute-start(bf16[32,1792]{1,0:T(8,128)(2,1)S(1)} %get-tuple-element.184), channel_id=1, source_target_pairs={{0,4},{1,5},{2,6},{3,7},{4,0},{5,1},{6,2},{7,3},{8,12},{9,13},{10,... | collective-permute-start | bytes 344072 | tf_op jit(solution)/shard_map/ppermute | solution.py:97
  64.3 10.0 %collective-permute-start.28 = (bf16[64,1792]{1,0:T(8,128)(2,1)S(1)}, bf16[64,1792]{1,0:T(8,128)(2,1)S(1)}, u32[]{:S(2)}, u32[]{:S(2)}) collective-permute-start(bf16[64,1792]{1,0:T(8,128)(2,1)S(1)} %get-tuple-element.142), channel_id=1, source_target_pairs={{0,4},{1,5},{2,6},{3,7},{4,0},{5,1},{6,2},{7,3},{8,12},{9,13},{10,... | collective-permute-start | bytes 688136 | tf_op jit(solution)/shard_map/ppermute | solution.py:97
  65.7 8.6 %collective-permute-start.29 = (bf16[64,1792]{1,0:T(8,128)(2,1)S(1)}, bf16[64,1792]{1,0:T(8,128)(2,1)S(1)}, u32[]{:S(2)}, u32[]{:S(2)}) collective-permute-start(bf16[64,1792]{1,0:T(8,128)(2,1)S(1)} %get-tuple-element.144), channel_id=1, source_target_pairs={{0,1},{1,0},{2,3},{3,2},{4,5},{5,4},{6,7},{7,6},{8,9},{9,8},{10,11... | collective-permute-start | bytes 688136 | tf_op jit(solution)/shard_map/ppermute | solution.py:97
  67.1 7.2 %collective-permute-start.26 = (bf16[32,1792]{1,0:T(8,128)(2,1)S(1)}, bf16[32,1792]{1,0:T(8,128)(2,1)S(1)}, u32[]{:S(2)}, u32[]{:S(2)}) collective-permute-start(bf16[32,1792]{1,0:T(8,128)(2,1)S(1)} %get-tuple-element.186), channel_id=1, source_target_pairs={{0,1},{1,0},{2,3},{3,2},{4,5},{5,4},{6,7},{7,6},{8,9},{9,8},{10,11... | collective-permute-start | bytes 344072 | tf_op jit(solution)/shard_map/ppermute | solution.py:97
  74.4 4.9 %collective-permute-start.30 = (bf16[16,3584]{1,0:T(8,128)(2,1)S(1)}, bf16[16,3584]{1,0:T(8,128)(2,1)S(1)}, u32[]{:S(2)}, u32[]{:S(2)}) collective-permute-start(bf16[16,3584]{1,0:T(8,128)(2,1)S(1)} %get-tuple-element.182), channel_id=1, source_target_pairs={{0,8},{1,9},{2,10},{3,11},{4,12},{5,13},{6,14},{7,15},{8,0},{9,1},... | collective-permute-start | bytes 344072 | tf_op jit(solution)/shard_map/ppermute | solution.py:97
  75.7 4.9 %collective-permute-start.31 = (bf16[32,1792]{1,0:T(8,128)(2,1)S(1)}, bf16[32,1792]{1,0:T(8,128)(2,1)S(1)}, u32[]{:S(2)}, u32[]{:S(2)}) collective-permute-start(bf16[32,1792]{1,0:T(8,128)(2,1)S(1)} %get-tuple-element.180), channel_id=1, source_target_pairs={{0,1},{1,0},{2,3},{3,2},{4,5},{5,4},{6,7},{7,6},{8,9},{9,8},{10,11... | collective-permute-start | bytes 344072 | tf_op jit(solution)/shard_map/ppermute | solution.py:97
  77.2 4.9 %collective-permute-start.32 = (bf16[32,1792]{1,0:T(8,128)(2,1)S(1)}, bf16[32,1792]{1,0:T(8,128)(2,1)S(1)}, u32[]{:S(2)}, u32[]{:S(2)}) collective-permute-start(bf16[32,1792]{1,0:T(8,128)(2,1)S(1)} %get-tuple-element.178), channel_id=1, source_target_pairs={{0,4},{1,5},{2,6},{3,7},{4,0},{5,1},{6,2},{7,3},{8,12},{9,13},{10,... | collective-permute-start | bytes 344072 | tf_op jit(solution)/shard_map/ppermute | solution.py:97
  82.1 6.4 %collective-permute-start.33 = (bf16[8,3584]{1,0:T(8,128)(2,1)S(1)}, bf16[8,3584]{1,0:T(8,128)(2,1)S(1)}, u32[]{:S(2)}, u32[]{:S(2)}) collective-permute-start(bf16[8,3584]{1,0:T(8,128)(2,1)S(1)} %get-tuple-element.188), channel_id=1, source_target_pairs={{0,16},{1,17},{2,18},{3,19},{4,20},{5,21},{6,22},{7,23},{8,24},{9,... | collective-permute-start | bytes 172040 | tf_op jit(solution)/shard_map/ppermute | solution.py:97
  84.1 6.0 %collective-permute-start.36 = (bf16[8,3584]{1,0:T(8,128)(2,1)S(1)}, bf16[8,3584]{1,0:T(8,128)(2,1)S(1)}, u32[]{:S(2)}, u32[]{:S(2)}) collective-permute-start(bf16[8,3584]{1,0:T(8,128)(2,1)S(1)} %get-tuple-element.174), channel_id=1, source_target_pairs={{0,24},{1,25},{2,26},{3,27},{4,28},{5,29},{6,30},{7,31},{8,16},{9,... | collective-permute-start | bytes 172040 | tf_op jit(solution)/shard_map/ppermute | solution.py:97
  85.6 5.8 %collective-permute-start.34 = (bf16[8,3584]{1,0:T(8,128)(2,1)S(1)}, bf16[8,3584]{1,0:T(8,128)(2,1)S(1)}, u32[]{:S(2)}, u32[]{:S(2)}) collective-permute-start(bf16[8,3584]{1,0:T(8,128)(2,1)S(1)} %get-tuple-element.176), channel_id=1, source_target_pairs={{0,16},{1,17},{2,18},{3,19},{4,20},{5,21},{6,22},{7,23},{8,24},{9,... | collective-permute-start | bytes 172040 | tf_op jit(solution)/shard_map/ppermute | solution.py:97
  86.6 4.8 %collective-permute-start.35 = (bf16[8,3584]{1,0:T(8,128)(2,1)S(1)}, bf16[8,3584]{1,0:T(8,128)(2,1)S(1)}, u32[]{:S(2)}, u32[]{:S(2)}) collective-permute-start(bf16[8,3584]{1,0:T(8,128)(2,1)S(1)} %get-tuple-element.177), channel_id=1, source_target_pairs={{0,8},{1,9},{2,10},{3,11},{4,12},{5,13},{6,14},{7,15},{8,0},{9,1},... | collective-permute-start | bytes 172040 | tf_op jit(solution)/shard_map/ppermute | solution.py:97
  (14 other events, 32.9 us)

commit v11 on v10

--- a/solution.py
+++ b/solution.py
@@ -129,26 +129,32 @@
     return total.astype(parts[0].dtype)
 
 
-def join_kernel(count, *refs):
-    start = 0
-    for out in refs[count:]:
-        columns = pl.ds(start, out.shape[1])
-        out[...] = jnp.concatenate([ref[:, columns] for ref in refs[:count]], axis=0)
-        start += out.shape[1]
-
-
-def join(parts, *widths):
+def join_kernel(count, ranges, *refs):
+    for out, parts in zip(refs[count:], ranges):
+        start = 0
+        for first, size in parts:
+            columns = pl.ds(first, size)
+            out[:, start : start + size] = jnp.concatenate(
+                [ref[:, columns] for ref in refs[:count]], axis=0
+            )
+            start += size
+
+
+def join(parts, *ranges):
     rows = sum(part.shape[0] for part in parts)
-    widths = widths or parts[0].shape[1:]
+    ranges = ranges or ([(0, parts[0].shape[1])],)
     outs = pl.pallas_call(
-        functools.partial(join_kernel, len(parts)),
+        functools.partial(join_kernel, len(parts), ranges),
         in_specs=[pl.BlockSpec(memory_space=pltpu.VMEM)] * len(parts),
-        out_specs=[pl.BlockSpec(memory_space=pltpu.VMEM)] * len(widths),
-        out_shape=[jax.ShapeDtypeStruct((rows, width), parts[0].dtype) for width in widths],
-        compiler_params=pltpu.CompilerParams(vmem_limit_bytes=2 * MEBI),
+        out_specs=[pl.BlockSpec(memory_space=pltpu.VMEM)] * len(ranges),
+        out_shape=[
+            jax.ShapeDtypeStruct((rows, sum(size for _, size in columns)), parts[0].dtype)
+            for columns in ranges
+        ],
+        compiler_params=pltpu.CompilerParams(vmem_limit_bytes=4 * MEBI),
         name="join",
     )(*parts)
-    return outs if len(widths) > 1 else outs[0]
+    return outs if len(ranges) > 1 else outs[0]
 
 
 def table_width(experts):
@@ -156,7 +162,7 @@
 
 
 def pack_kernel(experts, *refs):
-    sources, (head_ref, tail_ref, *targets), sems = refs[:3], refs[3:-1], refs[-1]
+    sources, (out_ref, *targets), sems = refs[:3], refs[3:-1], refs[-1]
     copies = [
         pltpu.make_async_copy(source, target, sems.at[i])
         for i, (source, target) in enumerate(zip(sources, targets))
@@ -167,7 +173,7 @@
     for copy in copies[1:]:
         copy.wait()
     extra = table_width(experts)
-    split, width = head_ref.shape[1], tail_ref.shape[1] - extra
+    width = rows_ref.shape[1]
     gates = gates_ref[...]
     shares = 2.5 * gates / jnp.sum(gates, axis=1, keepdims=True)
     ids = ids_ref[...]
@@ -178,25 +184,21 @@
         table += jnp.where(expert == ids[:, k : k + 1], shares[:, k : k + 1], 0.0)
     high = table.astype(jnp.bfloat16).astype(jnp.float32)
     table = jnp.where(lane < experts, high, jnp.where(lane < 2 * experts, table - high, 0.0))
+    out_ref[:, width:] = table.astype(jnp.bfloat16)
     copies[0].wait()
-    head_ref[...] = rows_ref[:, :split]
-    tail_ref[:, :width] = rows_ref[:, split:]
-    tail_ref[:, width:] = table.astype(jnp.bfloat16)
-
-
-def pack(split, experts, moe_rows, route_ids, route_gates):
+    out_ref[:, :width] = rows_ref[...]
+
+
+def pack(experts, moe_rows, route_ids, route_gates):
     rows, width = moe_rows.shape
     sources = (moe_rows, route_ids, route_gates)
     return pl.pallas_call(
         functools.partial(pack_kernel, experts),
         in_specs=[pl.BlockSpec(memory_space=pltpu.HBM)] * 3,
-        out_specs=[pl.BlockSpec(memory_space=pltpu.VMEM)] * 2,
+        out_specs=pl.BlockSpec(memory_space=pltpu.VMEM),
         scratch_shapes=[pltpu.VMEM(source.shape, source.dtype) for source in sources]
         + [pltpu.SemaphoreType.DMA((3,))],
-        out_shape=[
-            jax.ShapeDtypeStruct((rows, columns), jnp.bfloat16)
-            for columns in (split, width - split + table_width(experts))
-        ],
+        out_shape=jax.ShapeDtypeStruct((rows, width + table_width(experts)), jnp.bfloat16),
         compiler_params=pltpu.CompilerParams(vmem_limit_bytes=4 * MEBI),
         name="pack",
     )(*[in_hbm(source) for source in sources])
@@ -398,39 +400,28 @@
     tied = lax.optimization_barrier
     attn_latent = attention(query_latent, query_rope, cache_latent, cache_rope, cache_lengths)
 
-    def join_halves(parts):
-        half = (width - split if parts[0].shape[1] < split else split) // 2
-        return join(parts, half, parts[0].shape[1] - half)
-
-    def step(blocks):
-        return [grid.over(blocks[0], LOCAL), grid.over(blocks[1], MIDDLE)]
-
-    def second_step(blocks):
-        return [grid.over(blocks[0], MIDDLE), grid.over(blocks[1], LOCAL)]
+    line = pack(experts, moe_rows, route_ids, route_gates)
+    for m in grid.masks[:-1]:
+        came = grid.swap(line, HIGH, m)
+        came, attn_latent = tied((came, attn_latent))
+        line = join([line, came])
+    came = grid.swap(line, HIGH, grid.masks[-1])
+    half, rest = split // 2, (width - split) // 2
+    last = line.shape[1] - split - rest
+    ways = join(
+        [line, came],
+        [(0, half), (split, rest)],
+        [(half, half), (split + rest, last)],
+    )
+    ways = [grid.over(ways[0], LOCAL), grid.over(ways[1], MIDDLE)]
+    ways = [join(ways[0], [(0, half)], [(half, rest)]), join(ways[1], [(0, half)], [(half, last)])]
+    head = [grid.over(ways[0][0], MIDDLE), grid.over(ways[1][0], LOCAL)]
+    tail = [grid.over(ways[0][1], MIDDLE), grid.over(ways[1][1], LOCAL)]
 
     def with_other_core(ways):
         return [way + [grid.swap(block, CORE, 1) for block in way] for way in ways]
 
-    head, tail = pack(split, experts, moe_rows, route_ids, route_gates)
-    came = grid.swap(head, HIGH, grid.masks[0])
-    tail, came, attn_latent = tied((tail, came, attn_latent))
-    head = [head, came]
-    for m in grid.masks[1:]:
-        line = join(head)
-        head = [line, grid.swap(line, HIGH, m)]
-    head = join_halves(head)
-    came = grid.swap(tail, HIGH, grid.masks[0])
-    head, came = tied((head, came))
-    tail = [tail, came]
-    for m in grid.masks[1:]:
-        line = join(tail)
-        tail = [line, grid.swap(line, HIGH, m)]
-    tail = join_halves(tail)
-    head = step(head)
-    head, tail = tied(([join(head[0]), join(head[1])], tail))
-    head, tail = tied((second_step(head), step(tail)))
     head = with_other_core(head)
-    tail = second_step([join(tail[0]), join(tail[1])])
     rows = 2 * grid.sizes[MIDDLE] * grid.sizes[LOCAL] * high * tokens
     sums = first_sums(head, grid.sizes, rows, w_gate[0], w_up[0])
     tail, sums = tied((tail, sums))
@@ -459,24 +450,26 @@
     def second_axis(ways):
         return [grid.receive(ways[way], digits[way]) for way in range(2)]
 
-    def first_axis(ways):
-        return [grid.receive_rows(add(ways[way]), digits[1 - way]) for way in range(2)]
-
     def line_of(ways):
         return jnp.concatenate([add(way) for way in ways], axis=1)
 
     head, tail = products[: len(products) // 2], products[len(products) // 2 :]
     tail, head = tied((tail, core_sums(head)))
-    head, tail = tied((second_axis(head), core_sums(tail)))
-    head, tail = tied((first_axis(head), second_axis(tail)))
-    head = line_of(head)
-    masks = grid.masks[::-1]
-    head, tail = tied((grid.receive_half(head, masks[0]), first_axis(tail)))
-    for m in masks[1:]:
-        head = grid.receive_half(add(head), m)
-    tail = grid.receive_high(line_of(tail))
+    head, tail = second_axis(head), second_axis(core_sums(tail))
     head, tail = tied((head, tail))
-    return (jnp.concatenate([add(head), add(tail)], axis=1), attn_latent)
+    ways = [
+        grid.receive_rows(
+            jnp.concatenate([add(head[way]), add(tail[way])], axis=1), digits[1 - way]
+        )
+        for way in range(2)
+    ]
+    line = line_of(tied(ways))
+    for m in grid.masks[::-1]:
+        line = add(grid.receive_half(line, m))
+    quarter = width // 4
+    order = (0, 2, 1, 3)
+    moe_out = jnp.concatenate([line[:, i * quarter : (i + 1) * quarter] for i in order], axis=1)
+    return (moe_out, attn_latent)
 
 
 def solution(mesh):

time: 92.3 us -> 92.1 us (level)
  starting transfers between devices: 37.4 us -> 28 us
  waiting for transfers between devices: 34.6 us -> 43.9 us
    ppermute x37 -> x28, starting transfers between devices: 37.4 us -> 28 us  [swap(): return lax.ppermute(value, everyone, pairs)]
    ppermute x37 -> x28, waiting for transfers between devices: 34.6 us -> 43.9 us  [swap(): return lax.ppermute(value, everyone, pairs)]
  transfers between devices with their start and end apart: 37 -> 28, of which waited for: 19 -> 19; matrix products, arithmetic and copies ran while one was open for 1% -> 1% of each run, Pallas kernels for 9% -> 9%
where the time goes in v11:
time: 92.1 us; the launch traced here: 91.9 us
  waiting for transfers between devices  43.9 us (48%)
  starting transfers between devices  28 us (30%)
  Pallas kernels  17 us (18%)
  other arithmetic  1.6 us (2%)
    ppermute x28, waiting for transfers between devices, swap(): return lax.ppermute(value, everyone, pairs)  43.9 us
    ppermute x28, starting transfers between devices, swap(): return lax.ppermute(value, everyone, pairs)  28 us
    pallas_call x1, Pallas kernels, expert(): pl.pallas_call(functools.partial(expert_kernel, counts, sizes, experts, t...  7.99 us
    pallas_call x1, Pallas kernels, first_sums(): pl.pallas_call(functools.partial(first_kernel, counts, sizes, tile), in_s...  4.21 us
    pallas_call x1, Pallas kernels, attention(): pl.pallas_call(attention_kernel, in_specs=[pl.BlockSpec(memory_space=pltp...  3.66 us
  transfers between devices with their start and end apart: 28, of which 19 were waited for; matrix products, arithmetic and copies ran while one was open for 1% of the time, Pallas kernels for 9%

profile of v11, /device:TPU:0, one launch (start us, length us, event | category | flops | bytes accessed | tf_op | source)
XLA Modules:
  0.0 91.9 jit_solution(2685361554657861669)
XLA Ops:
  1.6 4.1 %collective-permute-start = (bf16[8,7296]{1,0:T(8,128)(2,1)S(1)}, bf16[8,7296]{1,0:T(8,128)(2,1)S(1)}, u32[]{:S(2)}, u32[]{:S(2)}) collective-permute-start(bf16[8,7296]{1,0:T(8,128)(2,1)S(1)} %pack.1.refs_0_), channel_id=1, source_target_pairs={{0,16},{1,17},{2,18},{3,19},{4,20},{5,21},{6,22},{7,23},{8,24},{9,... | collective-permute-start | bytes 350216 | tf_op jit(solution)/shard_map/ppermute | solution.py:97
  6.4 3.7 %attention.1 = bf16[2,64,512]{2,1,0:T(8,128)(2,1)} custom-call(s32[2]{0:T(128)S(1)} %copy-done, bf16[2,64,512]{2,1,0:T(8,128)(2,1)} %refs_0_.3, bf16[2,64,64]{2,1,0:T(8,128)(2,1)} %refs_1_.3, bf16[2,512,512]{2,1,0:T(8,128)(2,1)} %refs_2_.3, bf16[2,64,512]{2,1,0:T(8,128)(2,1)} %refs_3_.1), custom_call_target="tpu_custom_call" | custom-call | flops 134217728 | bytes 1048576 | tf_op jit(solution)/shard_map/attention/pallas_call | solution.py:54
  10.0 1.4 %collective-permute-done.refs_1_ = bf16[8,7296]{1,0:T(8,128)(2,1)S(1)} collective-permute-done((bf16[8,7296]{1,0:T(8,128)(2,1)S(1)}, bf16[8,7296]{1,0:T(8,128)(2,1)S(1)}, u32[]{:S(2)}, u32[]{:S(2)}) %collective-permute-start) | collective-permute-done | bytes 116768 | tf_op jit(solution)/shard_map/ppermute | solution.py:97
  12.2 6.2 %collective-permute-done.1.refs_1_ = bf16[16,7296]{1,0:T(8,128)(2,1)S(1)} collective-permute-done((bf16[16,7296]{1,0:T(8,128)(2,1)S(1)}, bf16[16,7296]{1,0:T(8,128)(2,1)S(1)}, u32[]{:S(2)}, u32[]{:S(2)}) %collective-permute-start.1) | collective-permute-done | bytes 233504 | tf_op jit(solution)/shard_map/ppermute | solution.py:97
  18.4 1.3 %collective-permute-start.4 = (bf16[32,3712]{1,0:T(8,128)(2,1)S(1)}, bf16[32,3712]{1,0:T(8,128)(2,1)S(1)}, u32[]{:S(2)}, u32[]{:S(2)}) collective-permute-start(bf16[32,3712]{1,0:T(8,128)(2,1)S(1)} %get-tuple-element.55.refs_0_), channel_id=1, source_target_pairs={{0,4},{1,5},{2,6},{3,7},{4,0},{5,1},{6,2},{7,3},{8,12},{9,13},{10,... | collective-permute-start | bytes 712712 | tf_op jit(solution)/shard_map/ppermute | solution.py:97
  19.8 1.5 %collective-permute-start.2 = (bf16[32,3584]{1,0:T(8,128)(2,1)S(1)}, bf16[32,3584]{1,0:T(8,128)(2,1)S(1)}, u32[]{:S(2)}, u32[]{:S(2)}) collective-permute-start(bf16[32,3584]{1,0:T(8,128)(2,1)S(1)} %get-tuple-element.53.refs_0_), channel_id=1, source_target_pairs={{0,1},{1,0},{2,3},{3,2},{4,5},{5,4},{6,7},{7,6},{8,9},{9,8},{10,11... | collective-permute-start | bytes 688136 | tf_op jit(solution)/shard_map/ppermute | solution.py:97
  21.3 4.5 %collective-permute-done.2.refs_1_ = bf16[32,3584]{1,0:T(8,128)(2,1)S(1)} collective-permute-done((bf16[32,3584]{1,0:T(8,128)(2,1)S(1)}, bf16[32,3584]{1,0:T(8,128)(2,1)S(1)}, u32[]{:S(2)}, u32[]{:S(2)}) %collective-permute-start.2) | collective-permute-done | bytes 229408 | tf_op jit(solution)/shard_map/ppermute | solution.py:97
  26.7 1.3 %collective-permute-start.9 = (bf16[64,2048]{1,0:T(8,128)(2,1)S(1)}, bf16[64,2048]{1,0:T(8,128)(2,1)S(1)}, u32[]{:S(2)}, u32[]{:S(2)}) collective-permute-start(bf16[64,2048]{1,0:T(8,128)(2,1)S(1)} %get-tuple-element.58.refs_4_), channel_id=1, source_target_pairs={{0,1},{1,0},{2,3},{3,2},{4,5},{5,4},{6,7},{7,6},{8,9},{9,8},{10,11... | collective-permute-start | bytes 786440 | tf_op jit(solution)/shard_map/ppermute | solution.py:97
  28.5 3.8 %collective-permute-done.6.refs_1_ = bf16[64,2048]{1,0:T(8,128)(2,1)S(1)} collective-permute-done((bf16[64,2048]{1,0:T(8,128)(2,1)S(1)}, bf16[64,2048]{1,0:T(8,128)(2,1)S(1)}, u32[]{:S(2)}, u32[]{:S(2)}) %collective-permute-start.6) | collective-permute-done | bytes 262176 | tf_op jit(solution)/shard_map/ppermute | solution.py:97
  34.4 1.5 %collective-permute-start.3 = (bf16[64,1536]{1,0:T(8,128)(2,1)S(1)}, bf16[64,1536]{1,0:T(8,128)(2,1)S(1)}, u32[]{:S(2)}, u32[]{:S(2)}) collective-permute-start(bf16[64,1536]{1,0:T(8,128)(2,1)S(1)} %get-tuple-element.61.refs_0_), channel_id=1, source_target_pairs={{0,4},{1,5},{2,6},{3,7},{4,0},{5,1},{6,2},{7,3},{8,12},{9,13},{10,... | collective-permute-start | bytes 589832 | tf_op jit(solution)/shard_map/ppermute | solution.py:97
  35.9 4.2 %first_sums.1 = (f32[256,512]{1,0:T(8,128)S(1)}, f32[256,512]{1,0:T(8,128)S(1)}) custom-call(bf16[64,2048]{1,0:T(8,128)(2,1)S(1)} %get-tuple-element.57.refs_0_, bf16[64,2048]{1,0:T(8,128)(2,1)S(1)} %collective-permute-done.6.refs_1_, bf16[64,2048]{1,0:T(8,128)(2,1)S(1)} %collective-permute-done.7.refs_2_, ...), custom_call_target="tpu_custom_call" | custom-call | flops 2147483648 | bytes 8388608 | tf_op jit(solution)/shard_map/first_sums/pallas_call | solution.py:276
  40.1 1.3 %collective-permute-done.3.refs_1_ = bf16[64,1536]{1,0:T(8,128)(2,1)S(1)} collective-permute-done((bf16[64,1536]{1,0:T(8,128)(2,1)S(1)}, bf16[64,1536]{1,0:T(8,128)(2,1)S(1)}, u32[]{:S(2)}, u32[]{:S(2)}) %collective-permute-start.3) | collective-permute-done | bytes 196640 | tf_op jit(solution)/shard_map/ppermute | solution.py:97
  43.8 8.0 %expert.1 = (bf16[64,1792]{1,0:T(8,128)(2,1)S(1)}, bf16[64,1792]{1,0:T(8,128)(2,1)S(1)}, bf16[128,1792]{1,0:T(8,128)(2,1)S(1)}, bf16[64,1792]{1,0:T(8,128)(2,1)S...) custom-call(s32[1]{0:T(128)} %bitcast.node_ref, ...), custom_call_target="tpu_custom_call" | custom-call | flops 3489660928 | bytes 13631488 | tf_op jit(solution)/shard_map/expert/pallas_call | solution.py:352
  52.3 1.3 %collective-permute-done.16 = bf16[128,1792]{1,0:T(8,128)(2,1)S(1)} collective-permute-done((bf16[128,1792]{1,0:T(8,128)(2,1)S(1)}, bf16[128,1792]{1,0:T(8,128)(2,1)S(1)}, u32[]{:S(2)}, u32[]{:S(2)}) %collective-permute-start.16) | collective-permute-done | bytes 458784 | tf_op jit(solution)/shard_map/ppermute | solution.py:97
  54.7 1.5 %collective-permute-start.18 = (bf16[64,1792]{1,0:T(8,128)(2,1)S(1)}, bf16[64,1792]{1,0:T(8,128)(2,1)S(1)}, u32[]{:S(2)}, u32[]{:S(2)}) collective-permute-start(bf16[64,1792]{1,0:T(8,128)(2,1)S(1)} %get-tuple-element.80), channel_id=1, source_target_pairs={{0,4},{1,5},{2,6},{3,7},{4,0},{5,1},{6,2},{7,3},{8,12},{9,13},{10,... | collective-permute-start | bytes 688136 | tf_op jit(solution)/shard_map/ppermute | solution.py:97
  58.7 1.5 %collective-permute-start.23 = (bf16[64,1792]{1,0:T(8,128)(2,1)S(1)}, bf16[64,1792]{1,0:T(8,128)(2,1)S(1)}, u32[]{:S(2)}, u32[]{:S(2)}) collective-permute-start(bf16[64,1792]{1,0:T(8,128)(2,1)S(1)} %get-tuple-element.106), channel_id=1, source_target_pairs={{0,1},{1,0},{2,3},{3,2},{4,5},{5,4},{6,7},{7,6},{8,9},{9,8},{10,11... | collective-permute-start | bytes 688136 | tf_op jit(solution)/shard_map/ppermute | solution.py:97
  60.2 2.9 %collective-permute-done.18 = bf16[64,1792]{1,0:T(8,128)(2,1)S(1)} collective-permute-done((bf16[64,1792]{1,0:T(8,128)(2,1)S(1)}, bf16[64,1792]{1,0:T(8,128)(2,1)S(1)}, u32[]{:S(2)}, u32[]{:S(2)}) %collective-permute-start.18) | collective-permute-done | bytes 229408 | tf_op jit(solution)/shard_map/ppermute | solution.py:97
  63.1 1.6 %collective-permute-done.19 = bf16[64,1792]{1,0:T(8,128)(2,1)S(1)} collective-permute-done((bf16[64,1792]{1,0:T(8,128)(2,1)S(1)}, bf16[64,1792]{1,0:T(8,128)(2,1)S(1)}, u32[]{:S(2)}, u32[]{:S(2)}) %collective-permute-start.19) | collective-permute-done | bytes 229408 | tf_op jit(solution)/shard_map/ppermute | solution.py:97
  64.7 2.7 %collective-permute-done.21 = bf16[64,1792]{1,0:T(8,128)(2,1)S(1)} collective-permute-done((bf16[64,1792]{1,0:T(8,128)(2,1)S(1)}, bf16[64,1792]{1,0:T(8,128)(2,1)S(1)}, u32[]{:S(2)}, u32[]{:S(2)}) %collective-permute-start.21) | collective-permute-done | bytes 229408 | tf_op jit(solution)/shard_map/ppermute | solution.py:97
  70.4 5.2 %collective-permute-done.24 = bf16[32,3584]{1,0:T(8,128)(2,1)S(1)} collective-permute-done((bf16[32,3584]{1,0:T(8,128)(2,1)S(1)}, bf16[32,3584]{1,0:T(8,128)(2,1)S(1)}, u32[]{:S(2)}, u32[]{:S(2)}) %collective-permute-start.24) | collective-permute-done | bytes 229408 | tf_op jit(solution)/shard_map/ppermute | solution.py:97
  76.3 2.1 %collective-permute-start.26 = (bf16[16,7168]{1,0:T(8,128)(2,1)S(1)}, bf16[16,7168]{1,0:T(8,128)(2,1)S(1)}, u32[]{:S(2)}, u32[]{:S(2)}) collective-permute-start(bf16[16,7168]{1,0:T(8,128)(2,1)S(1)} %pad_maximum_fusion), channel_id=1, source_target_pairs={{0,8},{1,9},{2,10},{3,11},{4,12},{5,13},{6,14},{7,15},{8,0},{9,1},... | collective-permute-start | bytes 688136 | tf_op jit(solution)/shard_map/ppermute | solution.py:97
  78.4 4.0 %collective-permute-done.26 = bf16[16,7168]{1,0:T(8,128)(2,1)S(1)} collective-permute-done((bf16[16,7168]{1,0:T(8,128)(2,1)S(1)}, bf16[16,7168]{1,0:T(8,128)(2,1)S(1)}, u32[]{:S(2)}, u32[]{:S(2)}) %collective-permute-start.26) | collective-permute-done | bytes 229408 | tf_op jit(solution)/shard_map/ppermute | solution.py:97
  82.5 4.7 %collective-permute-start.27 = (bf16[8,7168]{1,0:T(8,128)(2,1)S(1)}, bf16[8,7168]{1,0:T(8,128)(2,1)S(1)}, u32[]{:S(2)}, u32[]{:S(2)}) collective-permute-start(bf16[8,7168]{1,0:T(8,128)(2,1)S(1)} %slice.95), channel_id=1, source_target_pairs={{0,16},{1,17},{2,18},{3,19},{4,20},{5,21},{6,22},{7,23},{8,24},{9,... | collective-permute-start | bytes 344072 | tf_op jit(solution)/shard_map/ppermute | solution.py:97
  87.2 4.0 %collective-permute-done.27 = bf16[8,7168]{1,0:T(8,128)(2,1)S(1)} collective-permute-done((bf16[8,7168]{1,0:T(8,128)(2,1)S(1)}, bf16[8,7168]{1,0:T(8,128)(2,1)S(1)}, u32[]{:S(2)}, u32[]{:S(2)}) %collective-permute-start.27) | collective-permute-done | bytes 114720 | tf_op jit(solution)/shard_map/ppermute | solution.py:97
  (58 shorter events, 16.9 us)
Async XLA Ops:
  1.6 9.8 %collective-permute-start = (bf16[8,7296]{1,0:T(8,128)(2,1)S(1)}, bf16[8,7296]{1,0:T(8,128)(2,1)S(1)}, u32[]{:S(2)}, u32[]{:S(2)}) collective-permute-start(bf16[8,7296]{1,0:T(8,128)(2,1)S(1)} %pack.1.refs_0_), channel_id=1, source_target_pairs={{0,16},{1,17},{2,18},{3,19},{4,20},{5,21},{6,22},{7,23},{8,24},{9,... | collective-permute-start | bytes 350216 | tf_op jit(solution)/shard_map/ppermute | solution.py:97
  11.5 6.9 %collective-permute-start.1 = (bf16[16,7296]{1,0:T(8,128)(2,1)S(1)}, bf16[16,7296]{1,0:T(8,128)(2,1)S(1)}, u32[]{:S(2)}, u32[]{:S(2)}) collective-permute-start(bf16[16,7296]{1,0:T(8,128)(2,1)S(1)} %join.4.refs_0_), channel_id=1, source_target_pairs={{0,8},{1,9},{2,10},{3,11},{4,12},{5,13},{6,14},{7,15},{8,0},{9,1},... | collective-permute-start | bytes 700424 | tf_op jit(solution)/shard_map/ppermute | solution.py:97
  18.4 8.2 %collective-permute-start.4 = (bf16[32,3712]{1,0:T(8,128)(2,1)S(1)}, bf16[32,3712]{1,0:T(8,128)(2,1)S(1)}, u32[]{:S(2)}, u32[]{:S(2)}) collective-permute-start(bf16[32,3712]{1,0:T(8,128)(2,1)S(1)} %get-tuple-element.55.refs_0_), channel_id=1, source_target_pairs={{0,4},{1,5},{2,6},{3,7},{4,0},{5,1},{6,2},{7,3},{8,12},{9,13},{10,... | collective-permute-start | bytes 712712 | tf_op jit(solution)/shard_map/ppermute | solution.py:97
  19.8 6.0 %collective-permute-start.2 = (bf16[32,3584]{1,0:T(8,128)(2,1)S(1)}, bf16[32,3584]{1,0:T(8,128)(2,1)S(1)}, u32[]{:S(2)}, u32[]{:S(2)}) collective-permute-start(bf16[32,3584]{1,0:T(8,128)(2,1)S(1)} %get-tuple-element.53.refs_0_), channel_id=1, source_target_pairs={{0,1},{1,0},{2,3},{3,2},{4,5},{5,4},{6,7},{7,6},{8,9},{9,8},{10,11... | collective-permute-start | bytes 688136 | tf_op jit(solution)/shard_map/ppermute | solution.py:97
  25.8 6.4 %collective-permute-start.6 = (bf16[64,2048]{1,0:T(8,128)(2,1)S(1)}, bf16[64,2048]{1,0:T(8,128)(2,1)S(1)}, u32[]{:S(2)}, u32[]{:S(2)}) collective-permute-start(bf16[64,2048]{1,0:T(8,128)(2,1)S(1)} %get-tuple-element.57.refs_0_), channel_id=1, source_target_pairs={{0,4},{1,5},{2,6},{3,7},{4,0},{5,1},{6,2},{7,3},{8,12},{9,13},{10,... | collective-permute-start | bytes 786440 | tf_op jit(solution)/shard_map/ppermute | solution.py:97
  26.7 6.4 %collective-permute-start.9 = (bf16[64,2048]{1,0:T(8,128)(2,1)S(1)}, bf16[64,2048]{1,0:T(8,128)(2,1)S(1)}, u32[]{:S(2)}, u32[]{:S(2)}) collective-permute-start(bf16[64,2048]{1,0:T(8,128)(2,1)S(1)} %get-tuple-element.58.refs_4_), channel_id=1, source_target_pairs={{0,1},{1,0},{2,3},{3,2},{4,5},{5,4},{6,7},{7,6},{8,9},{9,8},{10,11... | collective-permute-start | bytes 786440 | tf_op jit(solution)/shard_map/ppermute | solution.py:97
  28.0 6.4 %collective-permute-start.7 = (bf16[64,2048]{1,0:T(8,128)(2,1)S(1)}, bf16[64,2048]{1,0:T(8,128)(2,1)S(1)}, u32[]{:S(2)}, u32[]{:S(2)}) collective-permute-start(bf16[64,2048]{1,0:T(8,128)(2,1)S(1)} %get-tuple-element.57.refs_0_), channel_id=1, source_target_pairs={{0,2},{1,3},{2,0},{3,1},{4,6},{5,7},{6,4},{7,5},{8,10},{9,11},{10,... | collective-permute-start | bytes 786440 | tf_op jit(solution)/shard_map/ppermute | solution.py:97
  28.0 7.9 %collective-permute-start.10 = (bf16[64,2048]{1,0:T(8,128)(2,1)S(1)}, bf16[64,2048]{1,0:T(8,128)(2,1)S(1)}, u32[]{:S(2)}, u32[]{:S(2)}) collective-permute-start(bf16[64,2048]{1,0:T(8,128)(2,1)S(1)} %get-tuple-element.58.refs_4_), channel_id=1, source_target_pairs={{0,2},{1,3},{2,0},{3,1},{4,6},{5,7},{6,4},{7,5},{8,10},{9,11},{10,... | collective-permute-start | bytes 786440 | tf_op jit(solution)/shard_map/ppermute | solution.py:97
  32.3 3.6 %collective-permute-start.8 = (bf16[64,2048]{1,0:T(8,128)(2,1)S(1)}, bf16[64,2048]{1,0:T(8,128)(2,1)S(1)}, u32[]{:S(2)}, u32[]{:S(2)}) collective-permute-start(bf16[64,2048]{1,0:T(8,128)(2,1)S(1)} %collective-permute-done.6.refs_1_), channel_id=1, source_target_pairs={{0,2},{1,3},{2,0},{3,1},{4,6},{5,7},{6,4},{7,5},{8,10},{9,11},{10,... | collective-permute-start | bytes 786440 | tf_op jit(solution)/shard_map/ppermute | solution.py:97
  33.1 2.8 %collective-permute-start.11 = (bf16[64,2048]{1,0:T(8,128)(2,1)S(1)}, bf16[64,2048]{1,0:T(8,128)(2,1)S(1)}, u32[]{:S(2)}, u32[]{:S(2)}) collective-permute-start(bf16[64,2048]{1,0:T(8,128)(2,1)S(1)} %collective-permute-done.9.refs_5_), channel_id=1, source_target_pairs={{0,2},{1,3},{2,0},{3,1},{4,6},{5,7},{6,4},{7,5},{8,10},{9,11},{10,... | collective-permute-start | bytes 786440 | tf_op jit(solution)/shard_map/ppermute | solution.py:97
  33.1 8.3 %collective-permute-start.5 = (bf16[64,1664]{1,0:T(8,128)(2,1)S(1)}, bf16[64,1664]{1,0:T(8,128)(2,1)S(1)}, u32[]{:S(2)}, u32[]{:S(2)}) collective-permute-start(bf16[64,1664]{1,0:T(8,128)(2,1)S(1)} %get-tuple-element.63.refs_4_), channel_id=1, source_target_pairs={{0,1},{1,0},{2,3},{3,2},{4,5},{5,4},{6,7},{7,6},{8,9},{9,8},{10,11... | collective-permute-start | bytes 638984 | tf_op jit(solution)/shard_map/ppermute | solution.py:97
  34.4 7.0 %collective-permute-start.3 = (bf16[64,1536]{1,0:T(8,128)(2,1)S(1)}, bf16[64,1536]{1,0:T(8,128)(2,1)S(1)}, u32[]{:S(2)}, u32[]{:S(2)}) collective-permute-start(bf16[64,1536]{1,0:T(8,128)(2,1)S(1)} %get-tuple-element.61.refs_0_), channel_id=1, source_target_pairs={{0,4},{1,5},{2,6},{3,7},{4,0},{5,1},{6,2},{7,3},{8,12},{9,13},{10,... | collective-permute-start | bytes 589832 | tf_op jit(solution)/shard_map/ppermute | solution.py:97
  41.4 2.3 %collective-permute-start.14 = (bf16[64,1664]{1,0:T(8,128)(2,1)S(1)}, bf16[64,1664]{1,0:T(8,128)(2,1)S(1)}, u32[]{:S(2)}, u32[]{:S(2)}) collective-permute-start(bf16[64,1664]{1,0:T(8,128)(2,1)S(1)} %get-tuple-element.63.refs_4_), channel_id=1, source_target_pairs={{0,2},{1,3},{2,0},{3,1},{4,6},{5,7},{6,4},{7,5},{8,10},{9,11},{10,... | collective-permute-start | bytes 638984 | tf_op jit(solution)/shard_map/ppermute | solution.py:97
  41.4 2.3 %collective-permute-start.15 = (bf16[64,1664]{1,0:T(8,128)(2,1)S(1)}, bf16[64,1664]{1,0:T(8,128)(2,1)S(1)}, u32[]{:S(2)}, u32[]{:S(2)}) collective-permute-start(bf16[64,1664]{1,0:T(8,128)(2,1)S(1)} %collective-permute-done.5.refs_5_), channel_id=1, source_target_pairs={{0,2},{1,3},{2,0},{3,1},{4,6},{5,7},{6,4},{7,5},{8,10},{9,11},{10,... | collective-permute-start | bytes 638984 | tf_op jit(solution)/shard_map/ppermute | solution.py:97
  52.0 2.3 %collective-permute-start.17 = (bf16[128,1792]{1,0:T(8,128)(2,1)S(1)}, bf16[128,1792]{1,0:T(8,128)(2,1)S(1)}, u32[]{:S(2)}, u32[]{:S(2)}) collective-permute-start(bf16[128,1792]{1,0:T(8,128)(2,1)S(1)} %get-tuple-element.77), channel_id=1, source_target_pairs={{0,2},{1,3},{2,0},{3,1},{4,6},{5,7},{6,4},{7,5},{8,10},{9,11},{10,... | collective-permute-start | bytes 1376264 | tf_op jit(solution)/shard_map/ppermute | solution.py:97
  54.4 2.4 %collective-permute-start.20 = (bf16[128,1792]{1,0:T(8,128)(2,1)S(1)}, bf16[128,1792]{1,0:T(8,128)(2,1)S(1)}, u32[]{:S(2)}, u32[]{:S(2)}) collective-permute-start(bf16[128,1792]{1,0:T(8,128)(2,1)S(1)} %get-tuple-element.84), channel_id=1, source_target_pairs={{0,2},{1,3},{2,0},{3,1},{4,6},{5,7},{6,4},{7,5},{8,10},{9,11},{10,... | collective-permute-start | bytes 1376264 | tf_op jit(solution)/shard_map/ppermute | solution.py:97
  54.7 8.4 %collective-permute-start.18 = (bf16[64,1792]{1,0:T(8,128)(2,1)S(1)}, bf16[64,1792]{1,0:T(8,128)(2,1)S(1)}, u32[]{:S(2)}, u32[]{:S(2)}) collective-permute-start(bf16[64,1792]{1,0:T(8,128)(2,1)S(1)} %get-tuple-element.80), channel_id=1, source_target_pairs={{0,4},{1,5},{2,6},{3,7},{4,0},{5,1},{6,2},{7,3},{8,12},{9,13},{10,... | collective-permute-start | bytes 688136 | tf_op jit(solution)/shard_map/ppermute | solution.py:97
  56.2 8.5 %collective-permute-start.19 = (bf16[64,1792]{1,0:T(8,128)(2,1)S(1)}, bf16[64,1792]{1,0:T(8,128)(2,1)S(1)}, u32[]{:S(2)}, u32[]{:S(2)}) collective-permute-start(bf16[64,1792]{1,0:T(8,128)(2,1)S(1)} %get-tuple-element.82), channel_id=1, source_target_pairs={{0,1},{1,0},{2,3},{3,2},{4,5},{5,4},{6,7},{7,6},{8,9},{9,8},{10,11... | collective-permute-start | bytes 688136 | tf_op jit(solution)/shard_map/ppermute | solution.py:97
  56.9 10.5 %collective-permute-start.21 = (bf16[64,1792]{1,0:T(8,128)(2,1)S(1)}, bf16[64,1792]{1,0:T(8,128)(2,1)S(1)}, u32[]{:S(2)}, u32[]{:S(2)}) collective-permute-start(bf16[64,1792]{1,0:T(8,128)(2,1)S(1)} %get-tuple-element.108), channel_id=1, source_target_pairs={{0,4},{1,5},{2,6},{3,7},{4,0},{5,1},{6,2},{7,3},{8,12},{9,13},{10,... | collective-permute-start | bytes 688136 | tf_op jit(solution)/shard_map/ppermute | solution.py:97
  58.7 9.9 %collective-permute-start.23 = (bf16[64,1792]{1,0:T(8,128)(2,1)S(1)}, bf16[64,1792]{1,0:T(8,128)(2,1)S(1)}, u32[]{:S(2)}, u32[]{:S(2)}) collective-permute-start(bf16[64,1792]{1,0:T(8,128)(2,1)S(1)} %get-tuple-element.106), channel_id=1, source_target_pairs={{0,1},{1,0},{2,3},{3,2},{4,5},{5,4},{6,7},{7,6},{8,9},{9,8},{10,11... | collective-permute-start | bytes 688136 | tf_op jit(solution)/shard_map/ppermute | solution.py:97
  68.8 6.7 %collective-permute-start.24 = (bf16[32,3584]{1,0:T(8,128)(2,1)S(1)}, bf16[32,3584]{1,0:T(8,128)(2,1)S(1)}, u32[]{:S(2)}, u32[]{:S(2)}) collective-permute-start(bf16[32,3584]{1,0:T(8,128)(2,1)S(1)} %get-tuple-element.104), channel_id=1, source_target_pairs={{0,1},{1,0},{2,3},{3,2},{4,5},{5,4},{6,7},{7,6},{8,9},{9,8},{10,11... | collective-permute-start | bytes 688136 | tf_op jit(solution)/shard_map/ppermute | solution.py:97
  69.6 6.5 %collective-permute-start.25 = (bf16[32,3584]{1,0:T(8,128)(2,1)S(1)}, bf16[32,3584]{1,0:T(8,128)(2,1)S(1)}, u32[]{:S(2)}, u32[]{:S(2)}) collective-permute-start(bf16[32,3584]{1,0:T(8,128)(2,1)S(1)} %get-tuple-element.102), channel_id=1, source_target_pairs={{0,4},{1,5},{2,6},{3,7},{4,0},{5,1},{6,2},{7,3},{8,12},{9,13},{10,... | collective-permute-start | bytes 688136 | tf_op jit(solution)/shard_map/ppermute | solution.py:97
  76.3 6.1 %collective-permute-start.26 = (bf16[16,7168]{1,0:T(8,128)(2,1)S(1)}, bf16[16,7168]{1,0:T(8,128)(2,1)S(1)}, u32[]{:S(2)}, u32[]{:S(2)}) collective-permute-start(bf16[16,7168]{1,0:T(8,128)(2,1)S(1)} %pad_maximum_fusion), channel_id=1, source_target_pairs={{0,8},{1,9},{2,10},{3,11},{4,12},{5,13},{6,14},{7,15},{8,0},{9,1},... | collective-permute-start | bytes 688136 | tf_op jit(solution)/shard_map/ppermute | solution.py:97
  82.5 8.7 %collective-permute-start.27 = (bf16[8,7168]{1,0:T(8,128)(2,1)S(1)}, bf16[8,7168]{1,0:T(8,128)(2,1)S(1)}, u32[]{:S(2)}, u32[]{:S(2)}) collective-permute-start(bf16[8,7168]{1,0:T(8,128)(2,1)S(1)} %slice.95), channel_id=1, source_target_pairs={{0,16},{1,17},{2,18},{3,19},{4,20},{5,21},{6,22},{7,23},{8,24},{9,... | collective-permute-start | bytes 344072 | tf_op jit(solution)/shard_map/ppermute | solution.py:97
  (5 other events, 7.7 us)

commit v12 on v8

--- a/solution.py
+++ b/solution.py
@@ -106,43 +106,49 @@
     def extent(self, pick):
         return self.sizes[pick(0)]
 
-    def masks(self):
-        masks, m = [], self.extent(self.high) // 2
-        while m:
-            masks.append(m)
-            m //= 2
-        return masks
-
-    def over_first(self, line):
+    def lines(self, rows):
+        return [rows] + [self.swap(rows, self.high, m) for m in range(1, self.extent(self.high))]
+
+    def near(self, line):
         return [line] + [self.swap(line, self.first, m) for m in range(1, self.extent(self.first))]
 
-    def over_second(self, near):
-        return [near] + [self.swap(near, self.second, m) for m in range(1, self.extent(self.second))]
-
-    def second_sum(self, parts):
-        return add(parts[:1] + [self.swap(parts[m], self.second, m) for m in range(1, len(parts))])
-
-    def first_sum(self, near):
-        rows = near.shape[0] // self.extent(self.first)
-        parts = [near[:rows]]
-        for m in range(1, self.extent(self.first)):
-            parts.append(self.swap(near[m * rows : (m + 1) * rows], self.first, m))
-        return add(parts)
+    def far(self, near):
+        return [
+            self.swap(block, self.second, m)
+            for m in range(1, self.extent(self.second))
+            for block in near
+        ]
+
+    def other(self, mine):
+        return [self.swap(block, self.core, 1) for block in mine]
+
+    def last_sum(self, mine, other):
+        return add([mine[-1], self.swap(other[0], self.core, 1)])
+
+    def rest_sums(self, mine, other):
+        size = mine[0].shape[0]
+        rest = self.swap(other[1], self.core, 1)
+        return [
+            add([part, rest[i * size : (i + 1) * size]]) for i, part in enumerate(mine[:-1])
+        ]
+
+    def back(self, sums, place):
+        return self.swap(sums[place], self.second, place // self.extent(self.first))
+
+    def line_sum(self, sums, last):
+        wide = self.extent(self.first)
+        near = [[part] for part in sums[:wide]]
+        for place in range(wide, len(sums)):
+            moved = last if place == len(sums) - 1 else self.back(sums, place)
+            near[place % wide].append(moved)
+        near = [add(parts) for parts in near]
+        return add([near[0]] + [self.swap(near[m], self.first, m) for m in range(1, wide)])
 
     def high_sum(self, line):
-        for m in reversed(self.masks()):
-            half = line.shape[0] // 2
-            line = add([line[:half], self.swap(line[half:], self.high, m)])
-        return line
-
-    def high_sum_direct(self, line):
-        order = [0]
-        for m in self.masks():
-            order += [m | other for other in order]
-        rows = line.shape[0] // len(order)
+        rows = line.shape[0] // self.extent(self.high)
         parts = [line[:rows]]
-        for i in range(1, len(order)):
-            parts.append(self.swap(line[i * rows : (i + 1) * rows], self.high, order[i]))
+        for m in range(1, self.extent(self.high)):
+            parts.append(self.swap(line[m * rows : (m + 1) * rows], self.high, m))
         return add(parts)
 
 
@@ -153,31 +159,51 @@
     return total.astype(parts[0].dtype)
 
 
-def join_kernel(count, *refs):
-    start = 0
-    for out in refs[count:]:
-        columns = pl.ds(start, out.shape[1])
-        out[...] = jnp.concatenate([ref[:, columns] for ref in refs[:count]], axis=0)
-        start += out.shape[1]
-
-
-def join(parts, *widths):
+def join_kernel(count, ranges, *refs):
+    for out, parts in zip(refs[count:], ranges):
+        start = 0
+        for first, size in parts:
+            columns = pl.ds(first, size)
+            out[:, start : start + size] = jnp.concatenate(
+                [ref[:, columns] for ref in refs[:count]], axis=0
+            )
+            start += size
+
+
+def join(parts, *ranges):
     rows = sum(part.shape[0] for part in parts)
-    widths = widths or parts[0].shape[1:]
+    ranges = ranges or ([(0, parts[0].shape[1])],)
     outs = pl.pallas_call(
-        functools.partial(join_kernel, len(parts)),
+        functools.partial(join_kernel, len(parts), ranges),
         in_specs=[pl.BlockSpec(memory_space=pltpu.VMEM)] * len(parts),
-        out_specs=[pl.BlockSpec(memory_space=pltpu.VMEM)] * len(widths),
-        out_shape=[jax.ShapeDtypeStruct((rows, width), parts[0].dtype) for width in widths],
-        compiler_params=pltpu.CompilerParams(vmem_limit_bytes=2 * MEBI),
+        out_specs=[pl.BlockSpec(memory_space=pltpu.VMEM)] * len(ranges),
+        out_shape=[
+            jax.ShapeDtypeStruct((rows, sum(size for _, size in columns)), parts[0].dtype)
+            for columns in ranges
+        ],
+        compiler_params=pltpu.CompilerParams(vmem_limit_bytes=4 * MEBI),
         name="join",
     )(*parts)
-    return outs if len(widths) > 1 else outs[0]
-
-
-def pack_kernel(experts, rows_ref, ids_ref, gates_ref, out_ref):
+    return outs if len(ranges) > 1 else outs[0]
+
+
+def table_width(experts):
+    return pl.cdiv(2 * experts, 128) * 128
+
+
+def pack_kernel(experts, *refs):
+    sources, (out_ref, *targets), sems = refs[:3], refs[3:-1], refs[-1]
+    copies = [
+        pltpu.make_async_copy(source, target, sems.at[i])
+        for i, (source, target) in enumerate(zip(sources, targets))
+    ]
+    for copy in copies:
+        copy.start()
+    rows_ref, ids_ref, gates_ref = targets
+    for copy in copies[1:]:
+        copy.wait()
     extra = table_width(experts)
-    width = out_ref.shape[1] - extra
+    width = rows_ref.shape[1]
     gates = gates_ref[...]
     shares = 2.5 * gates / jnp.sum(gates, axis=1, keepdims=True)
     ids = ids_ref[...]
@@ -188,22 +214,24 @@
         table += jnp.where(expert == ids[:, k : k + 1], shares[:, k : k + 1], 0.0)
     high = table.astype(jnp.bfloat16).astype(jnp.float32)
     table = jnp.where(lane < experts, high, jnp.where(lane < 2 * experts, table - high, 0.0))
+    out_ref[:, width:] = table.astype(jnp.bfloat16)
+    copies[0].wait()
     out_ref[:, :width] = rows_ref[...]
-    out_ref[:, width:] = table.astype(jnp.bfloat16)
-
-
-def table_width(experts):
-    return pl.cdiv(2 * experts, 128) * 128
 
 
 def pack(experts, moe_rows, route_ids, route_gates):
-    total = moe_rows.shape[1] + table_width(experts)
+    rows, width = moe_rows.shape
+    sources = (moe_rows, route_ids, route_gates)
     return pl.pallas_call(
         functools.partial(pack_kernel, experts),
-        out_shape=jax.ShapeDtypeStruct((moe_rows.shape[0], total), jnp.bfloat16),
-        compiler_params=pltpu.CompilerParams(vmem_limit_bytes=2 * MEBI),
+        in_specs=[pl.BlockSpec(memory_space=pltpu.HBM)] * 3,
+        out_specs=pl.BlockSpec(memory_space=pltpu.VMEM),
+        scratch_shapes=[pltpu.VMEM(source.shape, source.dtype) for source in sources]
+        + [pltpu.SemaphoreType.DMA((3,))],
+        out_shape=jax.ShapeDtypeStruct((rows, width + table_width(experts)), jnp.bfloat16),
+        compiler_params=pltpu.CompilerParams(vmem_limit_bytes=4 * MEBI),
         name="pack",
-    )(moe_rows, route_ids, route_gates)
+    )(*[in_hbm(source) for source in sources])
 
 
 def spread(product, outs):
@@ -283,14 +311,14 @@
     )(*blocks, in_hbm(w_gate), in_hbm(w_up))
 
 
-def expert_kernel(count, experts, tile, down_tile, node_ref, *refs):
+def expert_kernel(count, experts, tile, down_tile, split, node_ref, *refs):
     blocks = refs[:count]
     gate_in, up_in, gate_hbm, up_hbm, down_hbm = refs[count : count + 5]
     outs = refs[count + 5 : -10]
     hidden_ref, share_ref, gate, up, down, gate_sum, up_sum, gate_sem, up_sem, down_sem = refs[-10:]
     start = gate_hbm.shape[0] - gate.shape[0]
     copies = fetch_both(gate_hbm, up_hbm, gate, up, gate_sem, up_sem, start, tile)
-    down_copies = fetch(down_hbm, down, down_sem, 0, down_tile, 1)
+    down_copies = fetch(down_hbm, down, down_sem, 0, 2 * down_tile, 1)
 
     table = jnp.concatenate([block[:, gate.shape[0] :] for block in blocks], axis=0)
     table = table.astype(jnp.float32)
@@ -302,26 +330,26 @@
     up_sum[...] = up_in[...]
     project(blocks, copies, gate, up, gate_sum, up_sum, tile, False)
     hidden_ref[...] = (jax.nn.silu(gate_sum[...]) * up_sum[...]).astype(jnp.bfloat16)
-    for k, copy in enumerate(down_copies):
-        part = pl.ds(k * down_tile, down_tile)
-        copy.wait()
-        product = jnp.dot(hidden_ref[...], down[:, part], preferred_element_type=jnp.float32)
+    for k in range(0, down.shape[1], down_tile):
+        if k % (2 * down_tile) == 0:
+            down_copies[k // (2 * down_tile)].wait()
+        product = jnp.dot(
+            hidden_ref[...], down[:, pl.ds(k, down_tile)], preferred_element_type=jnp.float32
+        )
         product = (product * share_ref[:, :1]).astype(jnp.bfloat16)
-        start = k * down_tile
-        for chunk in (outs[: len(outs) // 2], outs[len(outs) // 2 :]):
-            if 0 <= start < chunk[0].shape[1]:
-                spread(product, [(out, pl.ds(start, down_tile)) for out in chunk])
-            start -= chunk[0].shape[1]
-
-
-def expert(blocks, sums, w_gate, w_up, w_down, experts, node, split):
+        if k < split:
+            spread(product, [(out, pl.ds(k, down_tile)) for out in outs[: len(outs) // 2]])
+        else:
+            spread(product, [(out, pl.ds(k - split, down_tile)) for out in outs[len(outs) // 2 :]])
+
+
+def expert(blocks, sums, w_gate, w_up, w_down, experts, node, sizes, split):
     units, columns = w_down.shape
-    sizes = [block.shape[0] for block in blocks]
     rows = sum(sizes)
     tail = blocks[0].shape[1] - table_width(experts)
     tile, down_tile = 1024, 512
     return pl.pallas_call(
-        functools.partial(expert_kernel, len(blocks), experts, tile, down_tile),
+        functools.partial(expert_kernel, len(blocks), experts, tile, down_tile, split),
         in_specs=[pl.BlockSpec(memory_space=pltpu.SMEM)]
         + [pl.BlockSpec(memory_space=pltpu.VMEM)] * (len(blocks) + 2)
         + [pl.BlockSpec(memory_space=pltpu.HBM)] * 3,
@@ -341,7 +369,7 @@
             pltpu.VMEM((rows, units), jnp.float32),
             pltpu.SemaphoreType.DMA((tail // tile,)),
             pltpu.SemaphoreType.DMA((tail // tile,)),
-            pltpu.SemaphoreType.DMA((columns // down_tile,)),
+            pltpu.SemaphoreType.DMA((columns // (2 * down_tile),)),
         ],
         cost_estimate=pl.CostEstimate(
             flops=4 * rows * tail * units + 2 * rows * columns * units,
@@ -375,37 +403,39 @@
     tied = lax.optimization_barrier
     attn_latent = attention(query_latent, query_rope, cache_latent, cache_rope, cache_lengths)
 
-    line = pack(experts, moe_rows, route_ids, route_gates)
-    masks = grid.masks()
-    for m in masks[:-1]:
-        line = join([line, grid.swap(line, grid.high, m)])
-    came = grid.swap(line, grid.high, masks[-1])
-    came, attn_latent = tied((came, attn_latent))
-    head, tail = join([line, came], split, line.shape[1] - split)
-    head, tail = grid.over_first(head), grid.over_first(tail)
-    head = grid.over_second(join(head))
-    tail = join(tail)
-    tail, head[0] = tied((tail, head[0]))
-    tail = grid.over_second(tail)
-    head += [grid.swap(block, grid.core, 1) for block in head]
-    gate_sum, up_sum = first_sums(head, w_gate[0], w_up[0])
-    tail[-1], gate_sum, up_sum = tied((tail[-1], gate_sum, up_sum))
-    tail += [grid.swap(block, grid.core, 1) for block in tail]
-    count = len(tail) // 2
+    lines = grid.lines(pack(experts, moe_rows, route_ids, route_gates))
+    lines[-1], attn_latent = tied((lines[-1], attn_latent))
+    total = lines[0].shape[1]
+    head, tail = join(lines, [(0, split)], [(split, total - split)])
+    head, tail = grid.near(head), grid.near(tail)
+    far = grid.far(head)
+    far[-1], tail[-1] = tied((far[-1], tail[-1]))
+    head, tail = head + far, tail + grid.far(tail)
+    other = grid.other(head)
+    sums = first_sums(head + other[-1:] + other[:-1], w_gate[0], w_up[0])
+    tail[-1], sums = tied((tail[-1], sums))
+    other = grid.other(tail)
+    size, count = high * tokens, len(tail)
+    sizes = [size] * count + [size, size * (count - 1)]
     products = expert(
-        tail, (gate_sum, up_sum), w_gate[0], w_up[0], w_down[0], experts, node, split
+        tail + other[-1:] + other[:-1],
+        sums,
+        w_gate[0],
+        w_up[0],
+        w_down[0],
+        experts,
+        node,
+        sizes,
+        split,
     )
 
-    def core_sum(parts):
-        sums = [add([parts[i], grid.swap(parts[count + i], grid.core, 1)]) for i in range(1, count)]
-        return [add([parts[0], grid.swap(parts[count], grid.core, 1)])] + sums
-
-    head, tail = products[: 2 * count], products[2 * count :]
-    tail, head = tied((tail, core_sum(head)))
-    head = grid.second_sum(head)
-    tail = grid.second_sum(core_sum(tail))
-    head = grid.high_sum(grid.first_sum(head))
-    tail = grid.high_sum_direct(grid.first_sum(tail))
+    def returned(parts):
+        mine, other = parts[:count], parts[count:]
+        last = grid.last_sum(mine, other)
+        sums = grid.rest_sums(mine, other) + [last]
+        return grid.high_sum(grid.line_sum(sums, grid.back(sums, count - 1)))
+
+    head, tail = returned(products[: len(sizes)]), returned(products[len(sizes) :])
     return (jnp.concatenate([head, tail], axis=1), attn_latent)
 
 

time: 95.9 us -> 85.8 us (0.89)
  waiting for transfers between devices: 44.7 us -> 35.1 us
  starting transfers between devices: 27.4 us -> 30.2 us
  local copies, waits for them, and re-layouts: 2.98 us -> 0.68 us
    ppermute x23 -> x33, waiting for transfers between devices: 44.7 us -> 35.1 us  [swap(): return lax.ppermute(value, everyone, pairs)]
    ppermute x23 -> x33, starting transfers between devices: 27.4 us -> 30.2 us  [swap(): return lax.ppermute(value, everyone, pairs)]
    unnamed x8 -> x2, local copies, waits for them, and re-layouts: 2.92 us -> 0.65 us
    pallas_call x1, Pallas kernels: 10.2 us -> 8.56 us  [expert(): pl.pallas_call(functools.partial(expert_kernel, len(blocks), experts, til...]
  transfers between devices with their start and end apart: 23 -> 33, of which waited for: 16 -> 15; matrix products, arithmetic and copies ran while one was open for 1% -> 1% of each run, Pallas kernels for 8% -> 9%
where the time goes in v12:
time: 85.8 us; the launch traced here: 85.6 us
  waiting for transfers between devices  35.1 us (41%)
  starting transfers between devices  30.2 us (35%)
  Pallas kernels  17.5 us (20%)
  other arithmetic  1.37 us (2%)
    ppermute x33, waiting for transfers between devices, swap(): return lax.ppermute(value, everyone, pairs)  35.1 us
    ppermute x33, starting transfers between devices, swap(): return lax.ppermute(value, everyone, pairs)  30.2 us
    pallas_call x1, Pallas kernels, expert(): pl.pallas_call(functools.partial(expert_kernel, len(blocks), experts, til...  8.56 us
    pallas_call x1, Pallas kernels, first_sums(): pl.pallas_call(functools.partial(first_kernel, len(blocks), tile), in_spe...  4.21 us
    pallas_call x1, Pallas kernels, attention(): pl.pallas_call(attention_kernel, in_specs=[pl.BlockSpec(memory_space=pltp...  3.66 us
  transfers between devices with their start and end apart: 33, of which 15 were waited for; matrix products, arithmetic and copies ran while one was open for 1% of the time, Pallas kernels for 9%

profile of v12, /device:TPU:0, one launch (start us, length us, event | category | flops | bytes accessed | tf_op | source)
XLA Modules:
  0.0 85.6 jit_solution(6217086161494710690)
XLA Ops:
  1.6 5.1 %collective-permute-start.2 = (bf16[8,7296]{1,0:T(8,128)(2,1)S(1)}, bf16[8,7296]{1,0:T(8,128)(2,1)S(1)}, u32[]{:S(2)}, u32[]{:S(2)}) collective-permute-start(bf16[8,7296]{1,0:T(8,128)(2,1)S(1)} %pack.1.refs_0_), channel_id=1, source_target_pairs={{0,24},{1,25},{2,26},{3,27},{4,28},{5,29},{6,30},{7,31},{8,16},{9,... | collective-permute-start | bytes 350216 | tf_op jit(solution)/shard_map/ppermute | solution.py:92
  8.0 3.7 %attention.1 = bf16[2,64,512]{2,1,0:T(8,128)(2,1)} custom-call(s32[2]{0:T(128)S(1)} %copy-done, bf16[2,64,512]{2,1,0:T(8,128)(2,1)} %refs_0_.3, bf16[2,64,64]{2,1,0:T(8,128)(2,1)} %refs_1_.3, bf16[2,512,512]{2,1,0:T(8,128)(2,1)} %refs_2_.3, bf16[2,64,512]{2,1,0:T(8,128)(2,1)} %refs_3_.1), custom_call_target="tpu_custom_call" | custom-call | flops 134217728 | bytes 1048576 | tf_op jit(solution)/shard_map/attention/pallas_call | solution.py:54
  11.7 4.9 %collective-permute-done.1.refs_2_ = bf16[8,7296]{1,0:T(8,128)(2,1)S(1)} collective-permute-done((bf16[8,7296]{1,0:T(8,128)(2,1)S(1)}, bf16[8,7296]{1,0:T(8,128)(2,1)S(1)}, u32[]{:S(2)}, u32[]{:S(2)}) %collective-permute-start.1) | collective-permute-done | bytes 116768 | tf_op jit(solution)/shard_map/ppermute | solution.py:92
  16.7 1.6 %collective-permute-start.3 = (bf16[32,4096]{1,0:T(8,128)(2,1)S(1)}, bf16[32,4096]{1,0:T(8,128)(2,1)S(1)}, u32[]{:S(2)}, u32[]{:S(2)}) collective-permute-start(bf16[32,4096]{1,0:T(8,128)(2,1)S(1)} %get-tuple-element.27.refs_0_), channel_id=1, source_target_pairs={{0,1},{1,0},{2,6},{3,7},{4,5},{5,4},{6,2},{7,3},{8,9},{9,8},{10,14... | collective-permute-start | bytes 786440 | tf_op jit(solution)/shard_map/ppermute | solution.py:92
  18.2 1.5 %collective-permute-start.8 = (bf16[32,4096]{1,0:T(8,128)(2,1)S(1)}, bf16[32,4096]{1,0:T(8,128)(2,1)S(1)}, u32[]{:S(2)}, u32[]{:S(2)}) collective-permute-start(bf16[32,4096]{1,0:T(8,128)(2,1)S(1)} %get-tuple-element.27.refs_0_), channel_id=1, source_target_pairs={{0,4},{1,5},{2,3},{3,2},{4,0},{5,1},{6,7},{7,6},{8,12},{9,13},{10,... | collective-permute-start | bytes 786440 | tf_op jit(solution)/shard_map/ppermute | solution.py:92
  19.7 6.1 %collective-permute-done.3.refs_1_ = bf16[32,4096]{1,0:T(8,128)(2,1)S(1)} collective-permute-done((bf16[32,4096]{1,0:T(8,128)(2,1)S(1)}, bf16[32,4096]{1,0:T(8,128)(2,1)S(1)}, u32[]{:S(2)}, u32[]{:S(2)}) %collective-permute-start.3) | collective-permute-done | bytes 262176 | tf_op jit(solution)/shard_map/ppermute | solution.py:92
  26.0 1.4 %collective-permute-start.5 = (bf16[32,3200]{1,0:T(8,128)(2,1)S(1)}, bf16[32,3200]{1,0:T(8,128)(2,1)S(1)}, u32[]{:S(2)}, u32[]{:S(2)}) collective-permute-start(bf16[32,3200]{1,0:T(8,128)(2,1)S(1)} %get-tuple-element.26.refs_0_), channel_id=1, source_target_pairs={{0,1},{1,0},{2,6},{3,7},{4,5},{5,4},{6,2},{7,3},{8,9},{9,8},{10,14... | collective-permute-start | bytes 614408 | tf_op jit(solution)/shard_map/ppermute | solution.py:92
  27.9 3.8 %collective-permute-done.5.refs_1_ = bf16[32,3200]{1,0:T(8,128)(2,1)S(1)} collective-permute-done((bf16[32,3200]{1,0:T(8,128)(2,1)S(1)}, bf16[32,3200]{1,0:T(8,128)(2,1)S(1)}, u32[]{:S(2)}, u32[]{:S(2)}) %collective-permute-start.5) | collective-permute-done | bytes 204832 | tf_op jit(solution)/shard_map/ppermute | solution.py:92
  32.2 1.4 %collective-permute-start.6 = (bf16[32,3200]{1,0:T(8,128)(2,1)S(1)}, bf16[32,3200]{1,0:T(8,128)(2,1)S(1)}, u32[]{:S(2)}, u32[]{:S(2)}) collective-permute-start(bf16[32,3200]{1,0:T(8,128)(2,1)S(1)} %get-tuple-element.26.refs_0_), channel_id=1, source_target_pairs={{0,4},{1,5},{2,3},{3,2},{4,0},{5,1},{6,7},{7,6},{8,12},{9,13},{10,... | collective-permute-start | bytes 614408 | tf_op jit(solution)/shard_map/ppermute | solution.py:92
  33.7 4.3 %collective-permute-done.6.refs_2_ = bf16[32,3200]{1,0:T(8,128)(2,1)S(1)} collective-permute-done((bf16[32,3200]{1,0:T(8,128)(2,1)S(1)}, bf16[32,3200]{1,0:T(8,128)(2,1)S(1)}, u32[]{:S(2)}, u32[]{:S(2)}) %collective-permute-start.6) | collective-permute-done | bytes 204832 | tf_op jit(solution)/shard_map/ppermute | solution.py:92
  38.0 1.4 %collective-permute-start.7 = (bf16[32,3200]{1,0:T(8,128)(2,1)S(1)}, bf16[32,3200]{1,0:T(8,128)(2,1)S(1)}, u32[]{:S(2)}, u32[]{:S(2)}) collective-permute-start(bf16[32,3200]{1,0:T(8,128)(2,1)S(1)} %collective-permute-done.5.refs_1_), channel_id=1, source_target_pairs={{0,4},{1,5},{2,3},{3,2},{4,0},{5,1},{6,7},{7,6},{8,12},{9,13},{10,... | collective-permute-start | bytes 614408 | tf_op jit(solution)/shard_map/ppermute | solution.py:92
  40.0 4.2 %first_sums.1 = (f32[256,512]{1,0:T(8,128)S(1)}, f32[256,512]{1,0:T(8,128)S(1)}) custom-call(bf16[32,4096]{1,0:T(8,128)(2,1)S(1)} %get-tuple-element.27.refs_0_, bf16[32,4096]{1,0:T(8,128)(2,1)S(1)} %collective-permute-done.3.refs_1_, bf16[32,4096]{1,0:T(8,128)(2,1)S(1)} %collective-permute-done.8.refs_2_, ...), custom_call_target="tpu_custom_call" | custom-call | flops 2147483648 | bytes 8388608 | tf_op jit(solution)/shard_map/first_sums/pallas_call | solution.py:296
  44.8 1.1 %collective-permute-done.13.refs_4_ = bf16[32,3200]{1,0:T(8,128)(2,1)S(1)} collective-permute-done((bf16[32,3200]{1,0:T(8,128)(2,1)S(1)}, bf16[32,3200]{1,0:T(8,128)(2,1)S(1)}, u32[]{:S(2)}, u32[]{:S(2)}) %collective-permute-start.13) | collective-permute-done | bytes 204832 | tf_op jit(solution)/shard_map/ppermute | solution.py:92
  45.8 8.6 %expert.1 = (bf16[32,4096]{1,0:T(8,128)(2,1)S(1)}, bf16[32,4096]{1,0:T(8,128)(2,1)S(1)}, bf16[32,4096]{1,0:T(8,128)(2,1)S(1)}, bf16[32,4096]{1,0:T(8,128)(2,1)S(...) custom-call(s32[1]{0:T(128)} %bitcast.node_ref, ...), custom_call_target="tpu_custom_call" | custom-call | flops 3489660928 | bytes 13631488 | tf_op jit(solution)/shard_map/expert/pallas_call | solution.py:351
  56.9 1.3 %collective-permute-start.20 = (bf16[32,4096]{1,0:T(8,128)(2,1)S(1)}, bf16[32,4096]{1,0:T(8,128)(2,1)S(1)}, u32[]{:S(2)}, u32[]{:S(2)}) collective-permute-start(bf16[32,4096]{1,0:T(8,128)(2,1)S(1)} %add_convert_fusion.2), channel_id=1, source_target_pairs={{0,4},{1,5},{2,3},{3,2},{4,0},{5,1},{6,7},{7,6},{8,12},{9,13},{10,... | collective-permute-start | bytes 786440 | tf_op jit(solution)/shard_map/ppermute | solution.py:92
  58.2 3.5 %collective-permute-done.28 = bf16[32,3072]{1,0:T(8,128)(2,1)S(1)} collective-permute-done((bf16[32,3072]{1,0:T(8,128)(2,1)S(1)}, bf16[32,3072]{1,0:T(8,128)(2,1)S(1)}, u32[]{:S(2)}, u32[]{:S(2)}) %collective-permute-start.28) | collective-permute-done | bytes 196640 | tf_op jit(solution)/shard_map/ppermute | solution.py:92
  62.7 1.5 %collective-permute-start.29 = (bf16[32,3072]{1,0:T(8,128)(2,1)S(1)}, bf16[32,3072]{1,0:T(8,128)(2,1)S(1)}, u32[]{:S(2)}, u32[]{:S(2)}) collective-permute-start(bf16[32,3072]{1,0:T(8,128)(2,1)S(1)} %get-tuple-element.51), channel_id=1, source_target_pairs={{0,1},{1,0},{2,6},{3,7},{4,5},{5,4},{6,2},{7,3},{8,9},{9,8},{10,14... | collective-permute-start | bytes 589832 | tf_op jit(solution)/shard_map/ppermute | solution.py:92
  65.6 1.8 %collective-permute-start.21 = (bf16[32,4096]{1,0:T(8,128)(2,1)S(1)}, bf16[32,4096]{1,0:T(8,128)(2,1)S(1)}, u32[]{:S(2)}, u32[]{:S(2)}) collective-permute-start(bf16[32,4096]{1,0:T(8,128)(2,1)S(1)} %get-tuple-element.49), channel_id=1, source_target_pairs={{0,1},{1,0},{2,6},{3,7},{4,5},{5,4},{6,2},{7,3},{8,9},{9,8},{10,14... | collective-permute-start | bytes 786440 | tf_op jit(solution)/shard_map/ppermute | solution.py:92
  67.4 2.3 %collective-permute-done.26 = bf16[32,3072]{1,0:T(8,128)(2,1)S(1)} collective-permute-done((bf16[32,3072]{1,0:T(8,128)(2,1)S(1)}, bf16[32,3072]{1,0:T(8,128)(2,1)S(1)}, u32[]{:S(2)}, u32[]{:S(2)}) %collective-permute-start.26) | collective-permute-done | bytes 196640 | tf_op jit(solution)/shard_map/ppermute | solution.py:92
  70.3 2.4 %collective-permute-start.32 = (bf16[8,3072]{1,0:T(8,128)(2,1)S(1)}, bf16[8,3072]{1,0:T(8,128)(2,1)S(1)}, u32[]{:S(2)}, u32[]{:S(2)}) collective-permute-start(bf16[8,3072]{1,0:T(8,128)(2,1)S(1)} %get-tuple-element.56), channel_id=1, source_target_pairs={{0,24},{1,25},{2,26},{3,27},{4,28},{5,29},{6,30},{7,31},{8,16},{9,... | collective-permute-start | bytes 147464 | tf_op jit(solution)/shard_map/ppermute | solution.py:92
  73.6 1.4 %collective-permute-done.18 = bf16[32,4096]{1,0:T(8,128)(2,1)S(1)} collective-permute-done((bf16[32,4096]{1,0:T(8,128)(2,1)S(1)}, bf16[32,4096]{1,0:T(8,128)(2,1)S(1)}, u32[]{:S(2)}, u32[]{:S(2)}) %collective-permute-start.18) | collective-permute-done | bytes 262176 | tf_op jit(solution)/shard_map/ppermute | solution.py:92
  75.4 2.4 %collective-permute-start.24 = (bf16[8,4096]{1,0:T(8,128)(2,1)S(1)}, bf16[8,4096]{1,0:T(8,128)(2,1)S(1)}, u32[]{:S(2)}, u32[]{:S(2)}) collective-permute-start(bf16[8,4096]{1,0:T(8,128)(2,1)S(1)} %get-tuple-element.53), channel_id=1, source_target_pairs={{0,24},{1,25},{2,26},{3,27},{4,28},{5,29},{6,30},{7,31},{8,16},{9,... | collective-permute-start | bytes 196616 | tf_op jit(solution)/shard_map/ppermute | solution.py:92
  79.5 2.4 %collective-permute-done.24 = bf16[8,4096]{1,0:T(8,128)(2,1)S(1)} collective-permute-done((bf16[8,4096]{1,0:T(8,128)(2,1)S(1)}, bf16[8,4096]{1,0:T(8,128)(2,1)S(1)}, u32[]{:S(2)}, u32[]{:S(2)}) %collective-permute-start.24) | collective-permute-done | bytes 65568 | tf_op jit(solution)/shard_map/ppermute | solution.py:92
  81.9 3.0 %collective-permute-done.23 = bf16[8,4096]{1,0:T(8,128)(2,1)S(1)} collective-permute-done((bf16[8,4096]{1,0:T(8,128)(2,1)S(1)}, bf16[8,4096]{1,0:T(8,128)(2,1)S(1)}, u32[]{:S(2)}, u32[]{:S(2)}) %collective-permute-start.23) | collective-permute-done | bytes 65568 | tf_op jit(solution)/shard_map/ppermute | solution.py:92
  (60 shorter events, 13.8 us)
Async XLA Ops:
  1.6 10.1 %collective-permute-start.2 = (bf16[8,7296]{1,0:T(8,128)(2,1)S(1)}, bf16[8,7296]{1,0:T(8,128)(2,1)S(1)}, u32[]{:S(2)}, u32[]{:S(2)}) collective-permute-start(bf16[8,7296]{1,0:T(8,128)(2,1)S(1)} %pack.1.refs_0_), channel_id=1, source_target_pairs={{0,24},{1,25},{2,26},{3,27},{4,28},{5,29},{6,30},{7,31},{8,16},{9,... | collective-permute-start | bytes 350216 | tf_op jit(solution)/shard_map/ppermute | solution.py:92
  6.7 9.8 %collective-permute-start.1 = (bf16[8,7296]{1,0:T(8,128)(2,1)S(1)}, bf16[8,7296]{1,0:T(8,128)(2,1)S(1)}, u32[]{:S(2)}, u32[]{:S(2)}) collective-permute-start(bf16[8,7296]{1,0:T(8,128)(2,1)S(1)} %pack.1.refs_0_), channel_id=1, source_target_pairs={{0,16},{1,17},{2,18},{3,19},{4,20},{5,21},{6,22},{7,23},{8,24},{9,... | collective-permute-start | bytes 350216 | tf_op jit(solution)/shard_map/ppermute | solution.py:92
  6.7 9.8 %collective-permute-start = (bf16[8,7296]{1,0:T(8,128)(2,1)S(1)}, bf16[8,7296]{1,0:T(8,128)(2,1)S(1)}, u32[]{:S(2)}, u32[]{:S(2)}) collective-permute-start(bf16[8,7296]{1,0:T(8,128)(2,1)S(1)} %pack.1.refs_0_), channel_id=1, source_target_pairs={{0,8},{1,9},{2,10},{3,11},{4,12},{5,13},{6,14},{7,15},{8,0},{9,1},... | collective-permute-start | bytes 350216 | tf_op jit(solution)/shard_map/ppermute | solution.py:92
  16.7 9.2 %collective-permute-start.3 = (bf16[32,4096]{1,0:T(8,128)(2,1)S(1)}, bf16[32,4096]{1,0:T(8,128)(2,1)S(1)}, u32[]{:S(2)}, u32[]{:S(2)}) collective-permute-start(bf16[32,4096]{1,0:T(8,128)(2,1)S(1)} %get-tuple-element.27.refs_0_), channel_id=1, source_target_pairs={{0,1},{1,0},{2,6},{3,7},{4,5},{5,4},{6,2},{7,3},{8,9},{9,8},{10,14... | collective-permute-start | bytes 786440 | tf_op jit(solution)/shard_map/ppermute | solution.py:92
  18.2 9.6 %collective-permute-start.8 = (bf16[32,4096]{1,0:T(8,128)(2,1)S(1)}, bf16[32,4096]{1,0:T(8,128)(2,1)S(1)}, u32[]{:S(2)}, u32[]{:S(2)}) collective-permute-start(bf16[32,4096]{1,0:T(8,128)(2,1)S(1)} %get-tuple-element.27.refs_0_), channel_id=1, source_target_pairs={{0,4},{1,5},{2,3},{3,2},{4,0},{5,1},{6,7},{7,6},{8,12},{9,13},{10,... | collective-permute-start | bytes 786440 | tf_op jit(solution)/shard_map/ppermute | solution.py:92
  25.9 6.4 %collective-permute-start.4 = (bf16[32,4096]{1,0:T(8,128)(2,1)S(1)}, bf16[32,4096]{1,0:T(8,128)(2,1)S(1)}, u32[]{:S(2)}, u32[]{:S(2)}) collective-permute-start(bf16[32,4096]{1,0:T(8,128)(2,1)S(1)} %collective-permute-done.3.refs_1_), channel_id=1, source_target_pairs={{0,4},{1,5},{2,3},{3,2},{4,0},{5,1},{6,7},{7,6},{8,12},{9,13},{10,... | collective-permute-start | bytes 786440 | tf_op jit(solution)/shard_map/ppermute | solution.py:92
  27.4 12.1 %collective-permute-start.10 = (bf16[32,4096]{1,0:T(8,128)(2,1)S(1)}, bf16[32,4096]{1,0:T(8,128)(2,1)S(1)}, u32[]{:S(2)}, u32[]{:S(2)}) collective-permute-start(bf16[32,4096]{1,0:T(8,128)(2,1)S(1)} %get-tuple-element.27.refs_0_), channel_id=1, source_target_pairs={{0,2},{1,3},{2,0},{3,1},{4,6},{5,7},{6,4},{7,5},{8,10},{9,11},{10,... | collective-permute-start | bytes 786440 | tf_op jit(solution)/shard_map/ppermute | solution.py:92
  27.4 12.6 %collective-permute-start.11 = (bf16[32,4096]{1,0:T(8,128)(2,1)S(1)}, bf16[32,4096]{1,0:T(8,128)(2,1)S(1)}, u32[]{:S(2)}, u32[]{:S(2)}) collective-permute-start(bf16[32,4096]{1,0:T(8,128)(2,1)S(1)} %collective-permute-done.3.refs_1_), channel_id=1, source_target_pairs={{0,2},{1,3},{2,0},{3,1},{4,6},{5,7},{6,4},{7,5},{8,10},{9,11},{10,... | collective-permute-start | bytes 786440 | tf_op jit(solution)/shard_map/ppermute | solution.py:92
  27.9 11.6 %collective-permute-start.12 = (bf16[32,4096]{1,0:T(8,128)(2,1)S(1)}, bf16[32,4096]{1,0:T(8,128)(2,1)S(1)}, u32[]{:S(2)}, u32[]{:S(2)}) collective-permute-start(bf16[32,4096]{1,0:T(8,128)(2,1)S(1)} %collective-permute-done.8.refs_2_), channel_id=1, source_target_pairs={{0,2},{1,3},{2,0},{3,1},{4,6},{5,7},{6,4},{7,5},{8,10},{9,11},{10,... | collective-permute-start | bytes 786440 | tf_op jit(solution)/shard_map/ppermute | solution.py:92
  32.2 7.8 %collective-permute-start.9 = (bf16[32,4096]{1,0:T(8,128)(2,1)S(1)}, bf16[32,4096]{1,0:T(8,128)(2,1)S(1)}, u32[]{:S(2)}, u32[]{:S(2)}) collective-permute-start(bf16[32,4096]{1,0:T(8,128)(2,1)S(1)} %collective-permute-done.4.refs_3_), channel_id=1, source_target_pairs={{0,2},{1,3},{2,0},{3,1},{4,6},{5,7},{6,4},{7,5},{8,10},{9,11},{10,... | collective-permute-start | bytes 786440 | tf_op jit(solution)/shard_map/ppermute | solution.py:92
  32.2 5.8 %collective-permute-start.6 = (bf16[32,3200]{1,0:T(8,128)(2,1)S(1)}, bf16[32,3200]{1,0:T(8,128)(2,1)S(1)}, u32[]{:S(2)}, u32[]{:S(2)}) collective-permute-start(bf16[32,3200]{1,0:T(8,128)(2,1)S(1)} %get-tuple-element.26.refs_0_), channel_id=1, source_target_pairs={{0,4},{1,5},{2,3},{3,2},{4,0},{5,1},{6,7},{7,6},{8,12},{9,13},{10,... | collective-permute-start | bytes 614408 | tf_op jit(solution)/shard_map/ppermute | solution.py:92
  38.0 6.2 %collective-permute-start.7 = (bf16[32,3200]{1,0:T(8,128)(2,1)S(1)}, bf16[32,3200]{1,0:T(8,128)(2,1)S(1)}, u32[]{:S(2)}, u32[]{:S(2)}) collective-permute-start(bf16[32,3200]{1,0:T(8,128)(2,1)S(1)} %collective-permute-done.5.refs_1_), channel_id=1, source_target_pairs={{0,4},{1,5},{2,3},{3,2},{4,0},{5,1},{6,7},{7,6},{8,12},{9,13},{10,... | collective-permute-start | bytes 614408 | tf_op jit(solution)/shard_map/ppermute | solution.py:92
  55.0 6.7 %collective-permute-start.25 = (bf16[96,3072]{1,0:T(8,128)(2,1)S(1)}, bf16[96,3072]{1,0:T(8,128)(2,1)S(1)}, u32[]{:S(2)}, u32[]{:S(2)}) collective-permute-start(bf16[96,3072]{1,0:T(8,128)(2,1)S(1)} %get-tuple-element.42), channel_id=1, source_target_pairs={{0,2},{1,3},{2,0},{3,1},{4,6},{5,7},{6,4},{7,5},{8,10},{9,11},{10,... | collective-permute-start | bytes 1769480 | tf_op jit(solution)/shard_map/ppermute | solution.py:92
  55.3 9.2 %collective-permute-start.17 = (bf16[96,4096]{1,0:T(8,128)(2,1)S(1)}, bf16[96,4096]{1,0:T(8,128)(2,1)S(1)}, u32[]{:S(2)}, u32[]{:S(2)}) collective-permute-start(bf16[96,4096]{1,0:T(8,128)(2,1)S(1)} %get-tuple-element.36), channel_id=1, source_target_pairs={{0,2},{1,3},{2,0},{3,1},{4,6},{5,7},{6,4},{7,5},{8,10},{9,11},{10,... | collective-permute-start | bytes 2359304 | tf_op jit(solution)/shard_map/ppermute | solution.py:92
  56.9 7.6 %collective-permute-start.20 = (bf16[32,4096]{1,0:T(8,128)(2,1)S(1)}, bf16[32,4096]{1,0:T(8,128)(2,1)S(1)}, u32[]{:S(2)}, u32[]{:S(2)}) collective-permute-start(bf16[32,4096]{1,0:T(8,128)(2,1)S(1)} %add_convert_fusion.2), channel_id=1, source_target_pairs={{0,4},{1,5},{2,3},{3,2},{4,0},{5,1},{6,7},{7,6},{8,12},{9,13},{10,... | collective-permute-start | bytes 786440 | tf_op jit(solution)/shard_map/ppermute | solution.py:92
  61.8 7.8 %collective-permute-start.26 = (bf16[32,3072]{1,0:T(8,128)(2,1)S(1)}, bf16[32,3072]{1,0:T(8,128)(2,1)S(1)}, u32[]{:S(2)}, u32[]{:S(2)}) collective-permute-start(bf16[32,3072]{1,0:T(8,128)(2,1)S(1)} %get-tuple-element.50), channel_id=1, source_target_pairs={{0,4},{1,5},{2,3},{3,2},{4,0},{5,1},{6,7},{7,6},{8,12},{9,13},{10,... | collective-permute-start | bytes 589832 | tf_op jit(solution)/shard_map/ppermute | solution.py:92
  62.7 7.2 %collective-permute-start.29 = (bf16[32,3072]{1,0:T(8,128)(2,1)S(1)}, bf16[32,3072]{1,0:T(8,128)(2,1)S(1)}, u32[]{:S(2)}, u32[]{:S(2)}) collective-permute-start(bf16[32,3072]{1,0:T(8,128)(2,1)S(1)} %get-tuple-element.51), channel_id=1, source_target_pairs={{0,1},{1,0},{2,6},{3,7},{4,5},{5,4},{6,2},{7,3},{8,9},{9,8},{10,14... | collective-permute-start | bytes 589832 | tf_op jit(solution)/shard_map/ppermute | solution.py:92
  64.7 10.4 %collective-permute-start.18 = (bf16[32,4096]{1,0:T(8,128)(2,1)S(1)}, bf16[32,4096]{1,0:T(8,128)(2,1)S(1)}, u32[]{:S(2)}, u32[]{:S(2)}) collective-permute-start(bf16[32,4096]{1,0:T(8,128)(2,1)S(1)} %get-tuple-element.48), channel_id=1, source_target_pairs={{0,4},{1,5},{2,3},{3,2},{4,0},{5,1},{6,7},{7,6},{8,12},{9,13},{10,... | collective-permute-start | bytes 786440 | tf_op jit(solution)/shard_map/ppermute | solution.py:92
  65.6 9.4 %collective-permute-start.21 = (bf16[32,4096]{1,0:T(8,128)(2,1)S(1)}, bf16[32,4096]{1,0:T(8,128)(2,1)S(1)}, u32[]{:S(2)}, u32[]{:S(2)}) collective-permute-start(bf16[32,4096]{1,0:T(8,128)(2,1)S(1)} %get-tuple-element.49), channel_id=1, source_target_pairs={{0,1},{1,0},{2,6},{3,7},{4,5},{5,4},{6,2},{7,3},{8,9},{9,8},{10,14... | collective-permute-start | bytes 786440 | tf_op jit(solution)/shard_map/ppermute | solution.py:92
  70.0 7.8 %collective-permute-start.30 = (bf16[8,3072]{1,0:T(8,128)(2,1)S(1)}, bf16[8,3072]{1,0:T(8,128)(2,1)S(1)}, u32[]{:S(2)}, u32[]{:S(2)}) collective-permute-start(bf16[8,3072]{1,0:T(8,128)(2,1)S(1)} %get-tuple-element.55), channel_id=1, source_target_pairs={{0,8},{1,9},{2,10},{3,11},{4,12},{5,13},{6,14},{7,15},{8,0},{9,1},... | collective-permute-start | bytes 147464 | tf_op jit(solution)/shard_map/ppermute | solution.py:92
  70.3 8.5 %collective-permute-start.32 = (bf16[8,3072]{1,0:T(8,128)(2,1)S(1)}, bf16[8,3072]{1,0:T(8,128)(2,1)S(1)}, u32[]{:S(2)}, u32[]{:S(2)}) collective-permute-start(bf16[8,3072]{1,0:T(8,128)(2,1)S(1)} %get-tuple-element.56), channel_id=1, source_target_pairs={{0,24},{1,25},{2,26},{3,27},{4,28},{5,29},{6,30},{7,31},{8,16},{9,... | collective-permute-start | bytes 147464 | tf_op jit(solution)/shard_map/ppermute | solution.py:92
  72.6 6.1 %collective-permute-start.31 = (bf16[8,3072]{1,0:T(8,128)(2,1)S(1)}, bf16[8,3072]{1,0:T(8,128)(2,1)S(1)}, u32[]{:S(2)}, u32[]{:S(2)}) collective-permute-start(bf16[8,3072]{1,0:T(8,128)(2,1)S(1)} %get-tuple-element.57), channel_id=1, source_target_pairs={{0,16},{1,17},{2,18},{3,19},{4,20},{5,21},{6,22},{7,23},{8,24},{9,... | collective-permute-start | bytes 147464 | tf_op jit(solution)/shard_map/ppermute | solution.py:92
  75.4 6.5 %collective-permute-start.24 = (bf16[8,4096]{1,0:T(8,128)(2,1)S(1)}, bf16[8,4096]{1,0:T(8,128)(2,1)S(1)}, u32[]{:S(2)}, u32[]{:S(2)}) collective-permute-start(bf16[8,4096]{1,0:T(8,128)(2,1)S(1)} %get-tuple-element.53), channel_id=1, source_target_pairs={{0,24},{1,25},{2,26},{3,27},{4,28},{5,29},{6,30},{7,31},{8,16},{9,... | collective-permute-start | bytes 196616 | tf_op jit(solution)/shard_map/ppermute | solution.py:92
  77.8 7.0 %collective-permute-start.23 = (bf16[8,4096]{1,0:T(8,128)(2,1)S(1)}, bf16[8,4096]{1,0:T(8,128)(2,1)S(1)}, u32[]{:S(2)}, u32[]{:S(2)}) collective-permute-start(bf16[8,4096]{1,0:T(8,128)(2,1)S(1)} %get-tuple-element.54), channel_id=1, source_target_pairs={{0,16},{1,17},{2,18},{3,19},{4,20},{5,21},{6,22},{7,23},{8,24},{9,... | collective-permute-start | bytes 196616 | tf_op jit(solution)/shard_map/ppermute | solution.py:92
  (10 other events, 37.0 us)

commit v13 on v12

--- a/solution.py
+++ b/solution.py
@@ -106,8 +106,25 @@
     def extent(self, pick):
         return self.sizes[pick(0)]
 
-    def lines(self, rows):
-        return [rows] + [self.swap(rows, self.high, m) for m in range(1, self.extent(self.high))]
+    def masks(self):
+        masks, m = [], self.extent(self.high) // 2
+        while m:
+            masks.append(m)
+            m //= 2
+        return masks
+
+    def lines(self, rows, masks):
+        if not masks:
+            return [rows]
+        came = self.swap(rows, self.high, masks[0])
+        return self.lines(rows, masks[1:]) + self.lines(came, masks[1:])
+
+    def line_parts(self, parts, masks):
+        if not masks:
+            return parts
+        half = len(parts) // 2
+        far = add(self.line_parts(parts[half:], masks[1:]))
+        return self.line_parts(parts[:half], masks[1:]) + [self.swap(far, self.high, masks[0])]
 
     def near(self, line):
         return [line] + [self.swap(line, self.first, m) for m in range(1, self.extent(self.first))]
@@ -145,11 +162,10 @@
         return add([near[0]] + [self.swap(near[m], self.first, m) for m in range(1, wide)])
 
     def high_sum(self, line):
-        rows = line.shape[0] // self.extent(self.high)
-        parts = [line[:rows]]
-        for m in range(1, self.extent(self.high)):
-            parts.append(self.swap(line[m * rows : (m + 1) * rows], self.high, m))
-        return add(parts)
+        size = self.extent(self.high)
+        rows = line.shape[0] // size
+        parts = [line[i * rows : (i + 1) * rows] for i in range(size)]
+        return add(self.line_parts(parts, self.masks()))
 
 
 def add(parts):
@@ -403,14 +419,15 @@
     tied = lax.optimization_barrier
     attn_latent = attention(query_latent, query_rope, cache_latent, cache_rope, cache_lengths)
 
-    lines = grid.lines(pack(experts, moe_rows, route_ids, route_gates))
+    lines = grid.lines(pack(experts, moe_rows, route_ids, route_gates), grid.masks())
     lines[-1], attn_latent = tied((lines[-1], attn_latent))
     total = lines[0].shape[1]
     head, tail = join(lines, [(0, split)], [(split, total - split)])
     head, tail = grid.near(head), grid.near(tail)
     far = grid.far(head)
-    far[-1], tail[-1] = tied((far[-1], tail[-1]))
-    head, tail = head + far, tail + grid.far(tail)
+    tail_far = grid.far(tail[:1])
+    far[-1], tail[-1], tail_far[0] = tied((far[-1], tail[-1], tail_far[0]))
+    head, tail = head + far, tail + tail_far + grid.far(tail[1:])
     other = grid.other(head)
     sums = first_sums(head + other[-1:] + other[:-1], w_gate[0], w_up[0])
     tail[-1], sums = tied((tail[-1], sums))

time: 85.8 us -> 84.9 us (0.990)
  waiting for transfers between devices: 35.1 us -> 30.8 us
  starting transfers between devices: 30.2 us -> 33.6 us
    ppermute x33, waiting for transfers between devices: 35.1 us -> 30.8 us  [swap(): return lax.ppermute(value, everyone, pairs)]
    ppermute x33, starting transfers between devices: 30.2 us -> 33.6 us  [swap(): return lax.ppermute(value, everyone, pairs)]
  transfers between devices with their start and end apart: 33 -> 33, of which waited for: 15 -> 12; matrix products, arithmetic and copies ran while one was open for 1% -> 1% of each run, Pallas kernels for 9% -> 9%
where the time goes in v13:
time: 84.9 us; the launch traced here: 84.7 us
  starting transfers between devices  33.6 us (40%)
  waiting for transfers between devices  30.8 us (36%)
  Pallas kernels  17.5 us (21%)
  other arithmetic  1.38 us (2%)
    ppermute x33, starting transfers between devices, swap(): return lax.ppermute(value, everyone, pairs)  33.6 us
    ppermute x33, waiting for transfers between devices, swap(): return lax.ppermute(value, everyone, pairs)  30.8 us
    pallas_call x1, Pallas kernels, expert(): pl.pallas_call(functools.partial(expert_kernel, len(blocks), experts, til...  8.54 us
    pallas_call x1, Pallas kernels, first_sums(): pl.pallas_call(functools.partial(first_kernel, len(blocks), tile), in_spe...  4.21 us
    pallas_call x1, Pallas kernels, attention(): pl.pallas_call(attention_kernel, in_specs=[pl.BlockSpec(memory_space=pltp...  3.66 us
  transfers between devices with their start and end apart: 33, of which 12 were waited for; matrix products, arithmetic and copies ran while one was open for 1% of the time, Pallas kernels for 9%

profile of v13, /device:TPU:0, one launch (start us, length us, event | category | flops | bytes accessed | tf_op | source)
XLA Modules:
  0.0 84.7 jit_solution(598182263081298561)
XLA Ops:
  1.6 4.1 %collective-permute-start.1 = (bf16[8,7296]{1,0:T(8,128)(2,1)S(1)}, bf16[8,7296]{1,0:T(8,128)(2,1)S(1)}, u32[]{:S(2)}, u32[]{:S(2)}) collective-permute-start(bf16[8,7296]{1,0:T(8,128)(2,1)S(1)} %pack.1.refs_0_), channel_id=1, source_target_pairs={{0,16},{1,17},{2,18},{3,19},{4,20},{5,21},{6,22},{7,23},{8,24},{9,... | collective-permute-start | bytes 350216 | tf_op jit(solution)/shard_map/ppermute | solution.py:92
  5.7 5.7 %collective-permute-done.1.refs_2_ = bf16[8,7296]{1,0:T(8,128)(2,1)S(1)} collective-permute-done((bf16[8,7296]{1,0:T(8,128)(2,1)S(1)}, bf16[8,7296]{1,0:T(8,128)(2,1)S(1)}, u32[]{:S(2)}, u32[]{:S(2)}) %collective-permute-start.1) | collective-permute-done | bytes 116768 | tf_op jit(solution)/shard_map/ppermute | solution.py:92
  12.1 1.3 %collective-permute-start = (bf16[8,7296]{1,0:T(8,128)(2,1)S(1)}, bf16[8,7296]{1,0:T(8,128)(2,1)S(1)}, u32[]{:S(2)}, u32[]{:S(2)}) collective-permute-start(bf16[8,7296]{1,0:T(8,128)(2,1)S(1)} %pack.1.refs_0_), channel_id=1, source_target_pairs={{0,8},{1,9},{2,10},{3,11},{4,12},{5,13},{6,14},{7,15},{8,0},{9,1},... | collective-permute-start | bytes 350216 | tf_op jit(solution)/shard_map/ppermute | solution.py:92
  14.1 3.7 %attention.1 = bf16[2,64,512]{2,1,0:T(8,128)(2,1)} custom-call(s32[2]{0:T(128)S(1)} %copy-done, bf16[2,64,512]{2,1,0:T(8,128)(2,1)} %refs_0_.3, bf16[2,64,64]{2,1,0:T(8,128)(2,1)} %refs_1_.3, bf16[2,512,512]{2,1,0:T(8,128)(2,1)} %refs_2_.3, bf16[2,64,512]{2,1,0:T(8,128)(2,1)} %refs_3_.1), custom_call_target="tpu_custom_call" | custom-call | flops 134217728 | bytes 1048576 | tf_op jit(solution)/shard_map/attention/pallas_call | solution.py:54
  18.4 1.5 %collective-permute-start.3 = (bf16[32,4096]{1,0:T(8,128)(2,1)S(1)}, bf16[32,4096]{1,0:T(8,128)(2,1)S(1)}, u32[]{:S(2)}, u32[]{:S(2)}) collective-permute-start(bf16[32,4096]{1,0:T(8,128)(2,1)S(1)} %get-tuple-element.28.refs_0_), channel_id=1, source_target_pairs={{0,1},{1,0},{2,6},{3,7},{4,5},{5,4},{6,2},{7,3},{8,9},{9,8},{10,14... | collective-permute-start | bytes 786440 | tf_op jit(solution)/shard_map/ppermute | solution.py:92
  19.9 1.5 %collective-permute-start.8 = (bf16[32,4096]{1,0:T(8,128)(2,1)S(1)}, bf16[32,4096]{1,0:T(8,128)(2,1)S(1)}, u32[]{:S(2)}, u32[]{:S(2)}) collective-permute-start(bf16[32,4096]{1,0:T(8,128)(2,1)S(1)} %get-tuple-element.28.refs_0_), channel_id=1, source_target_pairs={{0,4},{1,5},{2,3},{3,2},{4,0},{5,1},{6,7},{7,6},{8,12},{9,13},{10,... | collective-permute-start | bytes 786440 | tf_op jit(solution)/shard_map/ppermute | solution.py:92
  21.4 6.1 %collective-permute-done.3.refs_1_ = bf16[32,4096]{1,0:T(8,128)(2,1)S(1)} collective-permute-done((bf16[32,4096]{1,0:T(8,128)(2,1)S(1)}, bf16[32,4096]{1,0:T(8,128)(2,1)S(1)}, u32[]{:S(2)}, u32[]{:S(2)}) %collective-permute-start.3) | collective-permute-done | bytes 262176 | tf_op jit(solution)/shard_map/ppermute | solution.py:92
  27.5 2.0 %collective-permute-start.6 = (bf16[32,3200]{1,0:T(8,128)(2,1)S(1)}, bf16[32,3200]{1,0:T(8,128)(2,1)S(1)}, u32[]{:S(2)}, u32[]{:S(2)}) collective-permute-start(bf16[32,3200]{1,0:T(8,128)(2,1)S(1)} %get-tuple-element.27.refs_0_), channel_id=1, source_target_pairs={{0,4},{1,5},{2,3},{3,2},{4,0},{5,1},{6,7},{7,6},{8,12},{9,13},{10,... | collective-permute-start | bytes 614408 | tf_op jit(solution)/shard_map/ppermute | solution.py:92
  29.5 1.5 %collective-permute-start.5 = (bf16[32,3200]{1,0:T(8,128)(2,1)S(1)}, bf16[32,3200]{1,0:T(8,128)(2,1)S(1)}, u32[]{:S(2)}, u32[]{:S(2)}) collective-permute-start(bf16[32,3200]{1,0:T(8,128)(2,1)S(1)} %get-tuple-element.27.refs_0_), channel_id=1, source_target_pairs={{0,1},{1,0},{2,6},{3,7},{4,5},{5,4},{6,2},{7,3},{8,9},{9,8},{10,14... | collective-permute-start | bytes 614408 | tf_op jit(solution)/shard_map/ppermute | solution.py:92
  31.0 5.0 %collective-permute-done.6.refs_2_ = bf16[32,3200]{1,0:T(8,128)(2,1)S(1)} collective-permute-done((bf16[32,3200]{1,0:T(8,128)(2,1)S(1)}, bf16[32,3200]{1,0:T(8,128)(2,1)S(1)}, u32[]{:S(2)}, u32[]{:S(2)}) %collective-permute-start.6) | collective-permute-done | bytes 204832 | tf_op jit(solution)/shard_map/ppermute | solution.py:92
  36.6 1.7 %collective-permute-start.14 = (bf16[32,3200]{1,0:T(8,128)(2,1)S(1)}, bf16[32,3200]{1,0:T(8,128)(2,1)S(1)}, u32[]{:S(2)}, u32[]{:S(2)}) collective-permute-start(bf16[32,3200]{1,0:T(8,128)(2,1)S(1)} %get-tuple-element.27.refs_0_), channel_id=1, source_target_pairs={{0,2},{1,3},{2,0},{3,1},{4,6},{5,7},{6,4},{7,5},{8,10},{9,11},{10,... | collective-permute-start | bytes 614408 | tf_op jit(solution)/shard_map/ppermute | solution.py:92
  38.8 4.2 %first_sums.1 = (f32[256,512]{1,0:T(8,128)S(1)}, f32[256,512]{1,0:T(8,128)S(1)}) custom-call(bf16[32,4096]{1,0:T(8,128)(2,1)S(1)} %get-tuple-element.28.refs_0_, bf16[32,4096]{1,0:T(8,128)(2,1)S(1)} %collective-permute-done.3.refs_1_, bf16[32,4096]{1,0:T(8,128)(2,1)S(1)} %collective-permute-done.8.refs_2_, ...), custom_call_target="tpu_custom_call" | custom-call | flops 2147483648 | bytes 8388608 | tf_op jit(solution)/shard_map/first_sums/pallas_call | solution.py:312
  43.2 1.4 %collective-permute-done.13.refs_4_ = bf16[32,3200]{1,0:T(8,128)(2,1)S(1)} collective-permute-done((bf16[32,3200]{1,0:T(8,128)(2,1)S(1)}, bf16[32,3200]{1,0:T(8,128)(2,1)S(1)}, u32[]{:S(2)}, u32[]{:S(2)}) %collective-permute-start.13) | collective-permute-done | bytes 204832 | tf_op jit(solution)/shard_map/ppermute | solution.py:92
  44.6 8.5 %expert.1 = (bf16[32,4096]{1,0:T(8,128)(2,1)S(1)}, bf16[32,4096]{1,0:T(8,128)(2,1)S(1)}, bf16[32,4096]{1,0:T(8,128)(2,1)S(1)}, bf16[32,4096]{1,0:T(8,128)(2,1)S(...) custom-call(s32[1]{0:T(128)} %bitcast.node_ref, ...), custom_call_target="tpu_custom_call" | custom-call | flops 3489660928 | bytes 13631488 | tf_op jit(solution)/shard_map/expert/pallas_call | solution.py:367
  55.3 1.6 %collective-permute-start.20 = (bf16[32,4096]{1,0:T(8,128)(2,1)S(1)}, bf16[32,4096]{1,0:T(8,128)(2,1)S(1)}, u32[]{:S(2)}, u32[]{:S(2)}) collective-permute-start(bf16[32,4096]{1,0:T(8,128)(2,1)S(1)} %add_convert_fusion.2), channel_id=1, source_target_pairs={{0,4},{1,5},{2,3},{3,2},{4,0},{5,1},{6,7},{7,6},{8,12},{9,13},{10,... | collective-permute-start | bytes 786440 | tf_op jit(solution)/shard_map/ppermute | solution.py:92
  56.9 3.5 %collective-permute-done.28 = bf16[32,3072]{1,0:T(8,128)(2,1)S(1)} collective-permute-done((bf16[32,3072]{1,0:T(8,128)(2,1)S(1)}, bf16[32,3072]{1,0:T(8,128)(2,1)S(1)}, u32[]{:S(2)}, u32[]{:S(2)}) %collective-permute-start.28) | collective-permute-done | bytes 196640 | tf_op jit(solution)/shard_map/ppermute | solution.py:92
  61.1 1.5 %collective-permute-start.29 = (bf16[32,3072]{1,0:T(8,128)(2,1)S(1)}, bf16[32,3072]{1,0:T(8,128)(2,1)S(1)}, u32[]{:S(2)}, u32[]{:S(2)}) collective-permute-start(bf16[32,3072]{1,0:T(8,128)(2,1)S(1)} %get-tuple-element.53), channel_id=1, source_target_pairs={{0,1},{1,0},{2,6},{3,7},{4,5},{5,4},{6,2},{7,3},{8,9},{9,8},{10,14... | collective-permute-start | bytes 589832 | tf_op jit(solution)/shard_map/ppermute | solution.py:92
  64.0 1.7 %collective-permute-start.21 = (bf16[32,4096]{1,0:T(8,128)(2,1)S(1)}, bf16[32,4096]{1,0:T(8,128)(2,1)S(1)}, u32[]{:S(2)}, u32[]{:S(2)}) collective-permute-start(bf16[32,4096]{1,0:T(8,128)(2,1)S(1)} %get-tuple-element.51), channel_id=1, source_target_pairs={{0,1},{1,0},{2,6},{3,7},{4,5},{5,4},{6,2},{7,3},{8,9},{9,8},{10,14... | collective-permute-start | bytes 786440 | tf_op jit(solution)/shard_map/ppermute | solution.py:92
  65.7 2.7 %collective-permute-done.26 = bf16[32,3072]{1,0:T(8,128)(2,1)S(1)} collective-permute-done((bf16[32,3072]{1,0:T(8,128)(2,1)S(1)}, bf16[32,3072]{1,0:T(8,128)(2,1)S(1)}, u32[]{:S(2)}, u32[]{:S(2)}) %collective-permute-start.26) | collective-permute-done | bytes 196640 | tf_op jit(solution)/shard_map/ppermute | solution.py:92
  68.5 1.6 %collective-permute-start.30 = (bf16[8,3072]{1,0:T(8,128)(2,1)S(1)}, bf16[8,3072]{1,0:T(8,128)(2,1)S(1)}, u32[]{:S(2)}, u32[]{:S(2)}) collective-permute-start(bf16[8,3072]{1,0:T(8,128)(2,1)S(1)} %get-tuple-element.56), channel_id=1, source_target_pairs={{0,8},{1,9},{2,10},{3,11},{4,12},{5,13},{6,14},{7,15},{8,0},{9,1},... | collective-permute-start | bytes 147464 | tf_op jit(solution)/shard_map/ppermute | solution.py:92
  70.6 2.6 %collective-permute-done.18 = bf16[32,4096]{1,0:T(8,128)(2,1)S(1)} collective-permute-done((bf16[32,4096]{1,0:T(8,128)(2,1)S(1)}, bf16[32,4096]{1,0:T(8,128)(2,1)S(1)}, u32[]{:S(2)}, u32[]{:S(2)}) %collective-permute-start.18) | collective-permute-done | bytes 262176 | tf_op jit(solution)/shard_map/ppermute | solution.py:92
  73.4 1.6 %collective-permute-start.23 = (bf16[8,4096]{1,0:T(8,128)(2,1)S(1)}, bf16[8,4096]{1,0:T(8,128)(2,1)S(1)}, u32[]{:S(2)}, u32[]{:S(2)}) collective-permute-start(bf16[8,4096]{1,0:T(8,128)(2,1)S(1)} %get-tuple-element.55), channel_id=1, source_target_pairs={{0,8},{1,9},{2,10},{3,11},{4,12},{5,13},{6,14},{7,15},{8,0},{9,1},... | collective-permute-start | bytes 196616 | tf_op jit(solution)/shard_map/ppermute | solution.py:92
  75.0 3.4 %collective-permute-start.32 = (bf16[8,3072]{1,0:T(8,128)(2,1)S(1)}, bf16[8,3072]{1,0:T(8,128)(2,1)S(1)}, u32[]{:S(2)}, u32[]{:S(2)}) collective-permute-start(bf16[8,3072]{1,0:T(8,128)(2,1)S(1)} %add_convert_fusion.17), channel_id=1, source_target_pairs={{0,16},{1,17},{2,18},{3,19},{4,20},{5,21},{6,22},{7,23},{8,24},{9,... | collective-permute-start | bytes 147464 | tf_op jit(solution)/shard_map/ppermute | solution.py:92
  78.8 2.9 %collective-permute-start.24 = (bf16[8,4096]{1,0:T(8,128)(2,1)S(1)}, bf16[8,4096]{1,0:T(8,128)(2,1)S(1)}, u32[]{:S(2)}, u32[]{:S(2)}) collective-permute-start(bf16[8,4096]{1,0:T(8,128)(2,1)S(1)} %add_convert_fusion.15), channel_id=1, source_target_pairs={{0,16},{1,17},{2,18},{3,19},{4,20},{5,21},{6,22},{7,23},{8,24},{9,... | collective-permute-start | bytes 196616 | tf_op jit(solution)/shard_map/ppermute | solution.py:92
  (62 shorter events, 12.7 us)
Async XLA Ops:
  1.6 9.8 %collective-permute-start.1 = (bf16[8,7296]{1,0:T(8,128)(2,1)S(1)}, bf16[8,7296]{1,0:T(8,128)(2,1)S(1)}, u32[]{:S(2)}, u32[]{:S(2)}) collective-permute-start(bf16[8,7296]{1,0:T(8,128)(2,1)S(1)} %pack.1.refs_0_), channel_id=1, source_target_pairs={{0,16},{1,17},{2,18},{3,19},{4,20},{5,21},{6,22},{7,23},{8,24},{9,... | collective-permute-start | bytes 350216 | tf_op jit(solution)/shard_map/ppermute | solution.py:92
  11.4 6.4 %collective-permute-start.2 = (bf16[8,7296]{1,0:T(8,128)(2,1)S(1)}, bf16[8,7296]{1,0:T(8,128)(2,1)S(1)}, u32[]{:S(2)}, u32[]{:S(2)}) collective-permute-start(bf16[8,7296]{1,0:T(8,128)(2,1)S(1)} %collective-permute-done.1.refs_2_), channel_id=1, source_target_pairs={{0,8},{1,9},{2,10},{3,11},{4,12},{5,13},{6,14},{7,15},{8,0},{9,1},... | collective-permute-start | bytes 350216 | tf_op jit(solution)/shard_map/ppermute | solution.py:92
  12.1 6.2 %collective-permute-start = (bf16[8,7296]{1,0:T(8,128)(2,1)S(1)}, bf16[8,7296]{1,0:T(8,128)(2,1)S(1)}, u32[]{:S(2)}, u32[]{:S(2)}) collective-permute-start(bf16[8,7296]{1,0:T(8,128)(2,1)S(1)} %pack.1.refs_0_), channel_id=1, source_target_pairs={{0,8},{1,9},{2,10},{3,11},{4,12},{5,13},{6,14},{7,15},{8,0},{9,1},... | collective-permute-start | bytes 350216 | tf_op jit(solution)/shard_map/ppermute | solution.py:92
  18.4 9.1 %collective-permute-start.3 = (bf16[32,4096]{1,0:T(8,128)(2,1)S(1)}, bf16[32,4096]{1,0:T(8,128)(2,1)S(1)}, u32[]{:S(2)}, u32[]{:S(2)}) collective-permute-start(bf16[32,4096]{1,0:T(8,128)(2,1)S(1)} %get-tuple-element.28.refs_0_), channel_id=1, source_target_pairs={{0,1},{1,0},{2,6},{3,7},{4,5},{5,4},{6,2},{7,3},{8,9},{9,8},{10,14... | collective-permute-start | bytes 786440 | tf_op jit(solution)/shard_map/ppermute | solution.py:92
  19.9 16.2 %collective-permute-start.8 = (bf16[32,4096]{1,0:T(8,128)(2,1)S(1)}, bf16[32,4096]{1,0:T(8,128)(2,1)S(1)}, u32[]{:S(2)}, u32[]{:S(2)}) collective-permute-start(bf16[32,4096]{1,0:T(8,128)(2,1)S(1)} %get-tuple-element.28.refs_0_), channel_id=1, source_target_pairs={{0,4},{1,5},{2,3},{3,2},{4,0},{5,1},{6,7},{7,6},{8,12},{9,13},{10,... | collective-permute-start | bytes 786440 | tf_op jit(solution)/shard_map/ppermute | solution.py:92
  27.5 9.1 %collective-permute-start.4 = (bf16[32,4096]{1,0:T(8,128)(2,1)S(1)}, bf16[32,4096]{1,0:T(8,128)(2,1)S(1)}, u32[]{:S(2)}, u32[]{:S(2)}) collective-permute-start(bf16[32,4096]{1,0:T(8,128)(2,1)S(1)} %collective-permute-done.3.refs_1_), channel_id=1, source_target_pairs={{0,4},{1,5},{2,3},{3,2},{4,0},{5,1},{6,7},{7,6},{8,12},{9,13},{10,... | collective-permute-start | bytes 786440 | tf_op jit(solution)/shard_map/ppermute | solution.py:92
  27.5 8.6 %collective-permute-start.6 = (bf16[32,3200]{1,0:T(8,128)(2,1)S(1)}, bf16[32,3200]{1,0:T(8,128)(2,1)S(1)}, u32[]{:S(2)}, u32[]{:S(2)}) collective-permute-start(bf16[32,3200]{1,0:T(8,128)(2,1)S(1)} %get-tuple-element.27.refs_0_), channel_id=1, source_target_pairs={{0,4},{1,5},{2,3},{3,2},{4,0},{5,1},{6,7},{7,6},{8,12},{9,13},{10,... | collective-permute-start | bytes 614408 | tf_op jit(solution)/shard_map/ppermute | solution.py:92
  29.5 7.1 %collective-permute-start.5 = (bf16[32,3200]{1,0:T(8,128)(2,1)S(1)}, bf16[32,3200]{1,0:T(8,128)(2,1)S(1)}, u32[]{:S(2)}, u32[]{:S(2)}) collective-permute-start(bf16[32,3200]{1,0:T(8,128)(2,1)S(1)} %get-tuple-element.27.refs_0_), channel_id=1, source_target_pairs={{0,1},{1,0},{2,6},{3,7},{4,5},{5,4},{6,2},{7,3},{8,9},{9,8},{10,14... | collective-permute-start | bytes 614408 | tf_op jit(solution)/shard_map/ppermute | solution.py:92
  31.0 5.6 %collective-permute-start.10 = (bf16[32,4096]{1,0:T(8,128)(2,1)S(1)}, bf16[32,4096]{1,0:T(8,128)(2,1)S(1)}, u32[]{:S(2)}, u32[]{:S(2)}) collective-permute-start(bf16[32,4096]{1,0:T(8,128)(2,1)S(1)} %get-tuple-element.28.refs_0_), channel_id=1, source_target_pairs={{0,2},{1,3},{2,0},{3,1},{4,6},{5,7},{6,4},{7,5},{8,10},{9,11},{10,... | collective-permute-start | bytes 786440 | tf_op jit(solution)/shard_map/ppermute | solution.py:92
  36.6 6.4 %collective-permute-start.7 = (bf16[32,3200]{1,0:T(8,128)(2,1)S(1)}, bf16[32,3200]{1,0:T(8,128)(2,1)S(1)}, u32[]{:S(2)}, u32[]{:S(2)}) collective-permute-start(bf16[32,3200]{1,0:T(8,128)(2,1)S(1)} %collective-permute-done.5.refs_1_), channel_id=1, source_target_pairs={{0,4},{1,5},{2,3},{3,2},{4,0},{5,1},{6,7},{7,6},{8,12},{9,13},{10,... | collective-permute-start | bytes 614408 | tf_op jit(solution)/shard_map/ppermute | solution.py:92
  36.6 6.5 %collective-permute-start.14 = (bf16[32,3200]{1,0:T(8,128)(2,1)S(1)}, bf16[32,3200]{1,0:T(8,128)(2,1)S(1)}, u32[]{:S(2)}, u32[]{:S(2)}) collective-permute-start(bf16[32,3200]{1,0:T(8,128)(2,1)S(1)} %get-tuple-element.27.refs_0_), channel_id=1, source_target_pairs={{0,2},{1,3},{2,0},{3,1},{4,6},{5,7},{6,4},{7,5},{8,10},{9,11},{10,... | collective-permute-start | bytes 614408 | tf_op jit(solution)/shard_map/ppermute | solution.py:92
  38.3 4.9 %collective-permute-start.15 = (bf16[32,3200]{1,0:T(8,128)(2,1)S(1)}, bf16[32,3200]{1,0:T(8,128)(2,1)S(1)}, u32[]{:S(2)}, u32[]{:S(2)}) collective-permute-start(bf16[32,3200]{1,0:T(8,128)(2,1)S(1)} %collective-permute-done.5.refs_1_), channel_id=1, source_target_pairs={{0,2},{1,3},{2,0},{3,1},{4,6},{5,7},{6,4},{7,5},{8,10},{9,11},{10,... | collective-permute-start | bytes 614408 | tf_op jit(solution)/shard_map/ppermute | solution.py:92
  53.7 6.7 %collective-permute-start.25 = (bf16[96,3072]{1,0:T(8,128)(2,1)S(1)}, bf16[96,3072]{1,0:T(8,128)(2,1)S(1)}, u32[]{:S(2)}, u32[]{:S(2)}) collective-permute-start(bf16[96,3072]{1,0:T(8,128)(2,1)S(1)} %get-tuple-element.44), channel_id=1, source_target_pairs={{0,2},{1,3},{2,0},{3,1},{4,6},{5,7},{6,4},{7,5},{8,10},{9,11},{10,... | collective-permute-start | bytes 1769480 | tf_op jit(solution)/shard_map/ppermute | solution.py:92
  53.8 9.4 %collective-permute-start.17 = (bf16[96,4096]{1,0:T(8,128)(2,1)S(1)}, bf16[96,4096]{1,0:T(8,128)(2,1)S(1)}, u32[]{:S(2)}, u32[]{:S(2)}) collective-permute-start(bf16[96,4096]{1,0:T(8,128)(2,1)S(1)} %get-tuple-element.38), channel_id=1, source_target_pairs={{0,2},{1,3},{2,0},{3,1},{4,6},{5,7},{6,4},{7,5},{8,10},{9,11},{10,... | collective-permute-start | bytes 2359304 | tf_op jit(solution)/shard_map/ppermute | solution.py:92
  54.7 5.7 %collective-permute-start.28 = (bf16[32,3072]{1,0:T(8,128)(2,1)S(1)}, bf16[32,3072]{1,0:T(8,128)(2,1)S(1)}, u32[]{:S(2)}, u32[]{:S(2)}) collective-permute-start(bf16[32,3072]{1,0:T(8,128)(2,1)S(1)} %add_convert_fusion.9), channel_id=1, source_target_pairs={{0,4},{1,5},{2,3},{3,2},{4,0},{5,1},{6,7},{7,6},{8,12},{9,13},{10,... | collective-permute-start | bytes 589832 | tf_op jit(solution)/shard_map/ppermute | solution.py:92
  55.3 7.9 %collective-permute-start.20 = (bf16[32,4096]{1,0:T(8,128)(2,1)S(1)}, bf16[32,4096]{1,0:T(8,128)(2,1)S(1)}, u32[]{:S(2)}, u32[]{:S(2)}) collective-permute-start(bf16[32,4096]{1,0:T(8,128)(2,1)S(1)} %add_convert_fusion.2), channel_id=1, source_target_pairs={{0,4},{1,5},{2,3},{3,2},{4,0},{5,1},{6,7},{7,6},{8,12},{9,13},{10,... | collective-permute-start | bytes 786440 | tf_op jit(solution)/shard_map/ppermute | solution.py:92
  60.5 7.8 %collective-permute-start.26 = (bf16[32,3072]{1,0:T(8,128)(2,1)S(1)}, bf16[32,3072]{1,0:T(8,128)(2,1)S(1)}, u32[]{:S(2)}, u32[]{:S(2)}) collective-permute-start(bf16[32,3072]{1,0:T(8,128)(2,1)S(1)} %get-tuple-element.52), channel_id=1, source_target_pairs={{0,4},{1,5},{2,3},{3,2},{4,0},{5,1},{6,7},{7,6},{8,12},{9,13},{10,... | collective-permute-start | bytes 589832 | tf_op jit(solution)/shard_map/ppermute | solution.py:92
  61.1 7.2 %collective-permute-start.29 = (bf16[32,3072]{1,0:T(8,128)(2,1)S(1)}, bf16[32,3072]{1,0:T(8,128)(2,1)S(1)}, u32[]{:S(2)}, u32[]{:S(2)}) collective-permute-start(bf16[32,3072]{1,0:T(8,128)(2,1)S(1)} %get-tuple-element.53), channel_id=1, source_target_pairs={{0,1},{1,0},{2,6},{3,7},{4,5},{5,4},{6,2},{7,3},{8,9},{9,8},{10,14... | collective-permute-start | bytes 589832 | tf_op jit(solution)/shard_map/ppermute | solution.py:92
  63.4 9.8 %collective-permute-start.18 = (bf16[32,4096]{1,0:T(8,128)(2,1)S(1)}, bf16[32,4096]{1,0:T(8,128)(2,1)S(1)}, u32[]{:S(2)}, u32[]{:S(2)}) collective-permute-start(bf16[32,4096]{1,0:T(8,128)(2,1)S(1)} %get-tuple-element.50), channel_id=1, source_target_pairs={{0,4},{1,5},{2,3},{3,2},{4,0},{5,1},{6,7},{7,6},{8,12},{9,13},{10,... | collective-permute-start | bytes 786440 | tf_op jit(solution)/shard_map/ppermute | solution.py:92
  64.0 9.2 %collective-permute-start.21 = (bf16[32,4096]{1,0:T(8,128)(2,1)S(1)}, bf16[32,4096]{1,0:T(8,128)(2,1)S(1)}, u32[]{:S(2)}, u32[]{:S(2)}) collective-permute-start(bf16[32,4096]{1,0:T(8,128)(2,1)S(1)} %get-tuple-element.51), channel_id=1, source_target_pairs={{0,1},{1,0},{2,6},{3,7},{4,5},{5,4},{6,2},{7,3},{8,9},{9,8},{10,14... | collective-permute-start | bytes 786440 | tf_op jit(solution)/shard_map/ppermute | solution.py:92
  68.5 13.2 %collective-permute-start.30 = (bf16[8,3072]{1,0:T(8,128)(2,1)S(1)}, bf16[8,3072]{1,0:T(8,128)(2,1)S(1)}, u32[]{:S(2)}, u32[]{:S(2)}) collective-permute-start(bf16[8,3072]{1,0:T(8,128)(2,1)S(1)} %get-tuple-element.56), channel_id=1, source_target_pairs={{0,8},{1,9},{2,10},{3,11},{4,12},{5,13},{6,14},{7,15},{8,0},{9,1},... | collective-permute-start | bytes 147464 | tf_op jit(solution)/shard_map/ppermute | solution.py:92
  73.4 5.4 %collective-permute-start.23 = (bf16[8,4096]{1,0:T(8,128)(2,1)S(1)}, bf16[8,4096]{1,0:T(8,128)(2,1)S(1)}, u32[]{:S(2)}, u32[]{:S(2)}) collective-permute-start(bf16[8,4096]{1,0:T(8,128)(2,1)S(1)} %get-tuple-element.55), channel_id=1, source_target_pairs={{0,8},{1,9},{2,10},{3,11},{4,12},{5,13},{6,14},{7,15},{8,0},{9,1},... | collective-permute-start | bytes 196616 | tf_op jit(solution)/shard_map/ppermute | solution.py:92
  75.0 6.7 %collective-permute-start.32 = (bf16[8,3072]{1,0:T(8,128)(2,1)S(1)}, bf16[8,3072]{1,0:T(8,128)(2,1)S(1)}, u32[]{:S(2)}, u32[]{:S(2)}) collective-permute-start(bf16[8,3072]{1,0:T(8,128)(2,1)S(1)} %add_convert_fusion.17), channel_id=1, source_target_pairs={{0,16},{1,17},{2,18},{3,19},{4,20},{5,21},{6,22},{7,23},{8,24},{9,... | collective-permute-start | bytes 147464 | tf_op jit(solution)/shard_map/ppermute | solution.py:92
  78.8 5.2 %collective-permute-start.24 = (bf16[8,4096]{1,0:T(8,128)(2,1)S(1)}, bf16[8,4096]{1,0:T(8,128)(2,1)S(1)}, u32[]{:S(2)}, u32[]{:S(2)}) collective-permute-start(bf16[8,4096]{1,0:T(8,128)(2,1)S(1)} %add_convert_fusion.15), channel_id=1, source_target_pairs={{0,16},{1,17},{2,18},{3,19},{4,20},{5,21},{6,22},{7,23},{8,24},{9,... | collective-permute-start | bytes 196616 | tf_op jit(solution)/shard_map/ppermute | solution.py:92
  (10 other events, 26.6 us)

commit v14 on v12

--- a/solution.py
+++ b/solution.py
@@ -106,18 +106,27 @@
     def extent(self, pick):
         return self.sizes[pick(0)]
 
-    def lines(self, rows):
-        return [rows] + [self.swap(rows, self.high, m) for m in range(1, self.extent(self.high))]
+    def masks(self):
+        masks, m = [], self.extent(self.high) // 2
+        while m:
+            masks.append(m)
+            m //= 2
+        return masks
+
+    def lines(self, rows, masks, beside):
+        if not masks:
+            return [rows], beside
+        came = self.swap(rows, self.high, masks[0])
+        near, _ = self.lines(rows, masks[1:], ())
+        came, near, beside = lax.optimization_barrier((came, near, beside))
+        far, _ = self.lines(came, masks[1:], ())
+        return near + far, beside
 
     def near(self, line):
         return [line] + [self.swap(line, self.first, m) for m in range(1, self.extent(self.first))]
 
     def far(self, near):
-        return [
-            self.swap(block, self.second, m)
-            for m in range(1, self.extent(self.second))
-            for block in near
-        ]
+        return [self.swap(block, self.second, 1) for block in near]
 
     def other(self, mine):
         return [self.swap(block, self.core, 1) for block in mine]
@@ -242,25 +251,23 @@
         start += size
 
 
-def fetch(source, target, sems, start, tile, dim):
+def fetch_columns(source, target, sems):
+    columns = target.shape[1] // sems.shape[0]
     copies = []
-    for k in range(0, target.shape[dim], tile):
-        inside, outside = pl.ds(k, tile), pl.ds(start + k, tile)
-        if dim == 1:
-            inside, outside = (slice(None), inside), (slice(None), outside)
-        copy = pltpu.make_async_copy(source.at[outside], target.at[inside], sems.at[k // tile])
-        copy.start()
-        copies.append(copy)
+    for k in range(sems.shape[0]):
+        part = pl.ds(k * columns, columns)
+        copies.append(pltpu.make_async_copy(source.at[:, part], target.at[:, part], sems.at[k]))
+        copies[-1].start()
     return copies
 
 
-def fetch_both(gate_hbm, up_hbm, gate, up, gate_sem, up_sem, start, tile):
+def fetch_both(gate_hbm, up_hbm, gate, up, gate_sem, up_sem, tile):
     copies = []
     for k in range(0, gate.shape[0], tile):
-        inside, outside = pl.ds(k, tile), pl.ds(start + k, tile)
+        part = pl.ds(k, tile)
         pair = (
-            pltpu.make_async_copy(gate_hbm.at[outside], gate.at[inside], gate_sem.at[k // tile]),
-            pltpu.make_async_copy(up_hbm.at[outside], up.at[inside], up_sem.at[k // tile]),
+            pltpu.make_async_copy(gate_hbm.at[part], gate.at[part], gate_sem.at[k // tile]),
+            pltpu.make_async_copy(up_hbm.at[part], up.at[part], up_sem.at[k // tile]),
         )
         for copy in pair:
             copy.start()
@@ -268,57 +275,26 @@
     return copies
 
 
-def project(blocks, copies, gate, up, gate_sum, up_sum, tile, fresh):
+def project(blocks, copies, gate, up, gate_sum, up_sum, tile):
     for k, pair in enumerate(copies):
         part = pl.ds(k * tile, tile)
         rows = jnp.concatenate([block[:, part] for block in blocks], axis=0)
         for copy, weight, total in zip(pair, (gate, up), (gate_sum, up_sum)):
             copy.wait()
             product = jnp.dot(rows, weight[part], preferred_element_type=jnp.float32)
-            if fresh and k == 0:
+            if k == 0:
                 total[...] = product
             else:
                 total[...] += product
 
 
-def first_kernel(count, tile, *refs):
-    blocks = refs[:count]
-    gate_hbm, up_hbm, gate_sum, up_sum, gate, up, gate_sem, up_sem = refs[count:]
-    copies = fetch_both(gate_hbm, up_hbm, gate, up, gate_sem, up_sem, 0, tile)
-    project(blocks, copies, gate, up, gate_sum, up_sum, tile, True)
-
-
-def first_sums(blocks, w_gate, w_up):
-    units = w_gate.shape[1]
-    rows = sum(block.shape[0] for block in blocks)
-    columns = blocks[0].shape[1]
-    tile = 1024
-    return pl.pallas_call(
-        functools.partial(first_kernel, len(blocks), tile),
-        in_specs=[pl.BlockSpec(memory_space=pltpu.VMEM)] * len(blocks)
-        + [pl.BlockSpec(memory_space=pltpu.HBM)] * 2,
-        out_specs=[pl.BlockSpec(memory_space=pltpu.VMEM)] * 2,
-        out_shape=[jax.ShapeDtypeStruct((rows, units), jnp.float32)] * 2,
-        scratch_shapes=[pltpu.VMEM((columns, units), jnp.bfloat16)] * 2
-        + [pltpu.SemaphoreType.DMA((columns // tile,))] * 2,
-        cost_estimate=pl.CostEstimate(
-            flops=4 * rows * columns * units,
-            bytes_accessed=4 * columns * units,
-            transcendentals=0,
-        ),
-        compiler_params=pltpu.CompilerParams(vmem_limit_bytes=20 * MEBI),
-        name="first_sums",
-    )(*blocks, in_hbm(w_gate), in_hbm(w_up))
-
-
 def expert_kernel(count, experts, tile, down_tile, split, node_ref, *refs):
     blocks = refs[:count]
-    gate_in, up_in, gate_hbm, up_hbm, down_hbm = refs[count : count + 5]
-    outs = refs[count + 5 : -10]
+    gate_hbm, up_hbm, down_hbm = refs[count : count + 3]
+    outs = refs[count + 3 : -10]
     hidden_ref, share_ref, gate, up, down, gate_sum, up_sum, gate_sem, up_sem, down_sem = refs[-10:]
-    start = gate_hbm.shape[0] - gate.shape[0]
-    copies = fetch_both(gate_hbm, up_hbm, gate, up, gate_sem, up_sem, start, tile)
-    down_copies = fetch(down_hbm, down, down_sem, 0, 2 * down_tile, 1)
+    copies = fetch_both(gate_hbm, up_hbm, gate, up, gate_sem, up_sem, tile)
+    down_copies = fetch_columns(down_hbm, down, down_sem)
 
     table = jnp.concatenate([block[:, gate.shape[0] :] for block in blocks], axis=0)
     table = table.astype(jnp.float32)
@@ -326,13 +302,12 @@
     mine = (lane == node_ref[0]) | (lane == node_ref[0] + experts)
     share = jnp.sum(jnp.where(mine, table, 0.0), axis=1, keepdims=True)
     share_ref[...] = jnp.broadcast_to(share, share_ref.shape)
-    gate_sum[...] = gate_in[...]
-    up_sum[...] = up_in[...]
-    project(blocks, copies, gate, up, gate_sum, up_sum, tile, False)
+    project(blocks, copies, gate, up, gate_sum, up_sum, tile)
     hidden_ref[...] = (jax.nn.silu(gate_sum[...]) * up_sum[...]).astype(jnp.bfloat16)
+    wide = down.shape[1] // len(down_copies)
     for k in range(0, down.shape[1], down_tile):
-        if k % (2 * down_tile) == 0:
-            down_copies[k // (2 * down_tile)].wait()
+        if k % wide == 0:
+            down_copies[k // wide].wait()
         product = jnp.dot(
             hidden_ref[...], down[:, pl.ds(k, down_tile)], preferred_element_type=jnp.float32
         )
@@ -343,42 +318,41 @@
             spread(product, [(out, pl.ds(k - split, down_tile)) for out in outs[len(outs) // 2 :]])
 
 
-def expert(blocks, sums, w_gate, w_up, w_down, experts, node, sizes, split):
-    units, columns = w_down.shape
+def expert(blocks, w_gate, w_up, w_down, experts, node, sizes, split):
+    width, units = w_gate.shape
     rows = sum(sizes)
-    tail = blocks[0].shape[1] - table_width(experts)
     tile, down_tile = 1024, 512
     return pl.pallas_call(
         functools.partial(expert_kernel, len(blocks), experts, tile, down_tile, split),
         in_specs=[pl.BlockSpec(memory_space=pltpu.SMEM)]
-        + [pl.BlockSpec(memory_space=pltpu.VMEM)] * (len(blocks) + 2)
+        + [pl.BlockSpec(memory_space=pltpu.VMEM)] * len(blocks)
         + [pl.BlockSpec(memory_space=pltpu.HBM)] * 3,
         out_specs=[pl.BlockSpec(memory_space=pltpu.VMEM)] * (2 * len(sizes)),
         out_shape=[
             jax.ShapeDtypeStruct((size, chunk), jnp.bfloat16)
-            for chunk in (split, columns - split)
+            for chunk in (split, width - split)
             for size in sizes
         ],
         scratch_shapes=[
             pltpu.VMEM((rows, units), jnp.bfloat16),
             pltpu.VMEM((rows, 128), jnp.float32),
-            pltpu.VMEM((tail, units), jnp.bfloat16),
-            pltpu.VMEM((tail, units), jnp.bfloat16),
-            pltpu.VMEM((units, columns), jnp.bfloat16),
+            pltpu.VMEM((width, units), jnp.bfloat16),
+            pltpu.VMEM((width, units), jnp.bfloat16),
+            pltpu.VMEM((units, width), jnp.bfloat16),
             pltpu.VMEM((rows, units), jnp.float32),
             pltpu.VMEM((rows, units), jnp.float32),
-            pltpu.SemaphoreType.DMA((tail // tile,)),
-            pltpu.SemaphoreType.DMA((tail // tile,)),
-            pltpu.SemaphoreType.DMA((columns // (2 * down_tile),)),
+            pltpu.SemaphoreType.DMA((width // tile,)),
+            pltpu.SemaphoreType.DMA((width // tile,)),
+            pltpu.SemaphoreType.DMA((width // (2 * down_tile),)),
         ],
         cost_estimate=pl.CostEstimate(
-            flops=4 * rows * tail * units + 2 * rows * columns * units,
-            bytes_accessed=4 * tail * units + 2 * units * columns,
+            flops=6 * rows * width * units,
+            bytes_accessed=6 * units * width,
             transcendentals=rows * units,
         ),
-        compiler_params=pltpu.CompilerParams(vmem_limit_bytes=24 * MEBI),
+        compiler_params=pltpu.CompilerParams(vmem_limit_bytes=32 * MEBI),
         name="expert",
-    )(node, *blocks, *sums, in_hbm(w_gate), in_hbm(w_up), in_hbm(w_down))
+    )(node, *blocks, in_hbm(w_gate), in_hbm(w_up), in_hbm(w_down))
 
 
 def body(
@@ -399,27 +373,21 @@
     experts = high * middle * cores
     tokens, width = moe_rows.shape
     node = lax.axis_index(("high", "middle", "core")).astype(jnp.int32).reshape(1)
-    split = width * 4 // 7
     tied = lax.optimization_barrier
     attn_latent = attention(query_latent, query_rope, cache_latent, cache_rope, cache_lengths)
 
-    lines = grid.lines(pack(experts, moe_rows, route_ids, route_gates))
-    lines[-1], attn_latent = tied((lines[-1], attn_latent))
-    total = lines[0].shape[1]
-    head, tail = join(lines, [(0, split)], [(split, total - split)])
-    head, tail = grid.near(head), grid.near(tail)
-    far = grid.far(head)
-    far[-1], tail[-1] = tied((far[-1], tail[-1]))
-    head, tail = head + far, tail + grid.far(tail)
-    other = grid.other(head)
-    sums = first_sums(head + other[-1:] + other[:-1], w_gate[0], w_up[0])
-    tail[-1], sums = tied((tail[-1], sums))
-    other = grid.other(tail)
-    size, count = high * tokens, len(tail)
+    outgoing = pack(experts, moe_rows, route_ids, route_gates)
+    lines, attn_latent = grid.lines(outgoing, grid.masks(), attn_latent)
+    near = grid.near(join(lines))
+    far = grid.far(near[:-1])
+    rows = near[-1].shape[0] // 2
+    mine = near + far + grid.far([near[-1][:rows], near[-1][rows:]])
+    other = grid.other(mine)
+    size, count = high * tokens, len(mine) - 1
     sizes = [size] * count + [size, size * (count - 1)]
+    split = width * 3 // 7
     products = expert(
-        tail + other[-1:] + other[:-1],
-        sums,
+        mine + other[-2:] + other[:-2],
         w_gate[0],
         w_up[0],
         w_down[0],
@@ -429,14 +397,16 @@
         split,
     )
 
-    def returned(parts):
-        mine, other = parts[:count], parts[count:]
-        last = grid.last_sum(mine, other)
-        sums = grid.rest_sums(mine, other) + [last]
+    def returned(parts, last):
+        sums = grid.rest_sums(parts[:count], parts[count:]) + [last]
         return grid.high_sum(grid.line_sum(sums, grid.back(sums, count - 1)))
 
-    head, tail = returned(products[: len(sizes)]), returned(products[len(sizes) :])
-    return (jnp.concatenate([head, tail], axis=1), attn_latent)
+    small, large = products[: len(sizes)], products[len(sizes) :]
+    last = grid.last_sum(large[:count], large[count:])
+    small, last = tied((small, last))
+    large = returned(large, last)
+    small = returned(small, grid.last_sum(small[:count], small[count:]))
+    return (jnp.concatenate([small, large], axis=1), attn_latent)
 
 
 def solution(mesh):

time: 85.8 us -> 89.5 us (1.043)
  waiting for transfers between devices: 35.1 us -> 38.6 us
  starting transfers between devices: 30.2 us -> 31.3 us
  Pallas kernels: 17.5 us -> 16.6 us
    pallas_call x1 -> x0, Pallas kernels: 4.21 us -> none  [first_sums(): pl.pallas_call(functools.partial(first_kernel, len(blocks), tile), in_spe...]
    ppermute x33 -> x28, waiting for transfers between devices: 35.1 us -> 38.6 us  [swap(): return lax.ppermute(value, everyone, pairs)]
    pallas_call x1, Pallas kernels: 8.56 us -> 11.9 us  [expert(): pl.pallas_call(functools.partial(expert_kernel, len(blocks), experts, til...]
    ppermute x33 -> x28, starting transfers between devices: 30.2 us -> 31.3 us  [swap(): return lax.ppermute(value, everyone, pairs)]
  transfers between devices with their start and end apart: 33 -> 28, of which waited for: 15 -> 14; matrix products, arithmetic and copies ran while one was open for 1% -> 1% of each run, Pallas kernels for 9% -> 4%
where the time goes in v14:
time: 89.5 us; the launch traced here: 89.3 us
  waiting for transfers between devices  38.6 us (43%)
  starting transfers between devices  31.3 us (35%)
  Pallas kernels  16.6 us (19%)
  other arithmetic  1.35 us (2%)
    ppermute x28, waiting for transfers between devices, swap(): return lax.ppermute(value, everyone, pairs)  38.6 us
    ppermute x28, starting transfers between devices, swap(): return lax.ppermute(value, everyone, pairs)  31.3 us
    pallas_call x1, Pallas kernels, expert(): pl.pallas_call(functools.partial(expert_kernel, len(blocks), experts, til...  11.9 us
    pallas_call x1, Pallas kernels, attention(): pl.pallas_call(attention_kernel, in_specs=[pl.BlockSpec(memory_space=pltp...  3.66 us
  transfers between devices with their start and end apart: 28, of which 14 were waited for; matrix products, arithmetic and copies ran while one was open for 1% of the time, Pallas kernels for 4%

profile of v14, /device:TPU:0, one launch (start us, length us, event | category | flops | bytes accessed | tf_op | source)
XLA Modules:
  0.0 89.3 jit_solution(12418522987735853112)
XLA Ops:
  1.6 3.1 %collective-permute-start.1 = (bf16[8,7296]{1,0:T(8,128)(2,1)S(1)}, bf16[8,7296]{1,0:T(8,128)(2,1)S(1)}, u32[]{:S(2)}, u32[]{:S(2)}) collective-permute-start(bf16[8,7296]{1,0:T(8,128)(2,1)S(1)} %pack.1.refs_0_), channel_id=1, source_target_pairs={{0,8},{1,9},{2,10},{3,11},{4,12},{5,13},{6,14},{7,15},{8,0},{9,1},... | collective-permute-start | bytes 350216 | tf_op jit(solution)/shard_map/ppermute | solution.py:92
  4.7 2.6 %collective-permute-start = (bf16[8,7296]{1,0:T(8,128)(2,1)S(1)}, bf16[8,7296]{1,0:T(8,128)(2,1)S(1)}, u32[]{:S(2)}, u32[]{:S(2)}) collective-permute-start(bf16[8,7296]{1,0:T(8,128)(2,1)S(1)} %pack.1.refs_0_), channel_id=1, source_target_pairs={{0,16},{1,17},{2,18},{3,19},{4,20},{5,21},{6,22},{7,23},{8,24},{9,... | collective-permute-start | bytes 350216 | tf_op jit(solution)/shard_map/ppermute | solution.py:92
  8.0 3.7 %attention.1 = bf16[2,64,512]{2,1,0:T(8,128)(2,1)} custom-call(s32[2]{0:T(128)S(1)} %copy-done, bf16[2,64,512]{2,1,0:T(8,128)(2,1)} %refs_0_.3, bf16[2,64,64]{2,1,0:T(8,128)(2,1)} %refs_1_.3, bf16[2,512,512]{2,1,0:T(8,128)(2,1)} %refs_2_.3, bf16[2,64,512]{2,1,0:T(8,128)(2,1)} %refs_3_.1), custom_call_target="tpu_custom_call" | custom-call | flops 134217728 | bytes 1048576 | tf_op jit(solution)/shard_map/attention/pallas_call | solution.py:54
  13.2 4.4 %collective-permute-done.2.refs_3_ = bf16[8,7296]{1,0:T(8,128)(2,1)S(1)} collective-permute-done((bf16[8,7296]{1,0:T(8,128)(2,1)S(1)}, bf16[8,7296]{1,0:T(8,128)(2,1)S(1)}, u32[]{:S(2)}, u32[]{:S(2)}) %collective-permute-start.2) | collective-permute-done | bytes 116768 | tf_op jit(solution)/shard_map/ppermute | solution.py:92
  17.7 1.6 %collective-permute-start.3 = (bf16[32,7296]{1,0:T(8,128)(2,1)S(1)}, bf16[32,7296]{1,0:T(8,128)(2,1)S(1)}, u32[]{:S(2)}, u32[]{:S(2)}) collective-permute-start(bf16[32,7296]{1,0:T(8,128)(2,1)S(1)} %join.1.refs_0_), channel_id=1, source_target_pairs={{0,1},{1,0},{2,6},{3,7},{4,5},{5,4},{6,2},{7,3},{8,9},{9,8},{10,14... | collective-permute-start | bytes 1400840 | tf_op jit(solution)/shard_map/ppermute | solution.py:92
  20.8 9.5 %collective-permute-done.3.refs_1_ = bf16[32,7296]{1,0:T(8,128)(2,1)S(1)} collective-permute-done((bf16[32,7296]{1,0:T(8,128)(2,1)S(1)}, bf16[32,7296]{1,0:T(8,128)(2,1)S(1)}, u32[]{:S(2)}, u32[]{:S(2)}) %collective-permute-start.3) | collective-permute-done | bytes 466976 | tf_op jit(solution)/shard_map/ppermute | solution.py:92
  30.3 1.6 %collective-permute-start.6 = (bf16[16,7296]{1,0:T(8,128)(2,1)S(1)}, bf16[16,7296]{1,0:T(8,128)(2,1)S(1)}, u32[]{:S(2)}, u32[]{:S(2)}) collective-permute-start(bf16[16,7296]{1,0:T(8,128)(2,1)S(1)} %get-tuple-element.60), channel_id=1, source_target_pairs={{0,4},{1,5},{2,3},{3,2},{4,0},{5,1},{6,7},{7,6},{8,12},{9,13},{10,... | collective-permute-start | bytes 700424 | tf_op jit(solution)/shard_map/ppermute | solution.py:92
  32.7 1.9 %collective-permute-start.10 = (bf16[32,7296]{1,0:T(8,128)(2,1)S(1)}, bf16[32,7296]{1,0:T(8,128)(2,1)S(1)}, u32[]{:S(2)}, u32[]{:S(2)}) collective-permute-start(bf16[32,7296]{1,0:T(8,128)(2,1)S(1)} %collective-permute-done.3.refs_1_), channel_id=1, source_target_pairs={{0,2},{1,3},{2,0},{3,1},{4,6},{5,7},{6,4},{7,5},{8,10},{9,11},{10,... | collective-permute-start | bytes 1400840 | tf_op jit(solution)/shard_map/ppermute | solution.py:92
  34.6 1.9 %collective-permute-done.6.refs_4_ = bf16[16,7296]{1,0:T(8,128)(2,1)S(1)} collective-permute-done((bf16[16,7296]{1,0:T(8,128)(2,1)S(1)}, bf16[16,7296]{1,0:T(8,128)(2,1)S(1)}, u32[]{:S(2)}, u32[]{:S(2)}) %collective-permute-start.6) | collective-permute-done | bytes 233504 | tf_op jit(solution)/shard_map/ppermute | solution.py:92
  36.5 2.5 %collective-permute-done.5.refs_3_ = bf16[16,7296]{1,0:T(8,128)(2,1)S(1)} collective-permute-done((bf16[16,7296]{1,0:T(8,128)(2,1)S(1)}, bf16[16,7296]{1,0:T(8,128)(2,1)S(1)}, u32[]{:S(2)}, u32[]{:S(2)}) %collective-permute-start.5) | collective-permute-done | bytes 233504 | tf_op jit(solution)/shard_map/ppermute | solution.py:92
  39.0 1.6 %collective-permute-done.7.refs_5_ = bf16[16,7296]{1,0:T(8,128)(2,1)} collective-permute-done((bf16[16,7296]{1,0:T(8,128)(2,1)S(1)}, bf16[16,7296]{1,0:T(8,128)(2,1)}, u32[]{:S(2)}, u32[]{:S(2)}) %collective-permute-start.7) | collective-permute-done | bytes 233504 | tf_op jit(solution)/shard_map/ppermute | solution.py:92
  40.6 11.9 %expert.1 = (bf16[32,3072]{1,0:T(8,128)(2,1)S(1)}, bf16[32,3072]{1,0:T(8,128)(2,1)S(1)}, bf16[32,3072]{1,0:T(8,128)(2,1)S(1)}, bf16[32,3072]{1,0:T(8,128)(2,1)S(...) custom-call(s32[1]{0:T(128)} %bitcast.node_ref, ...), custom_call_target="tpu_custom_call" | custom-call | flops 5637144576 | bytes 22020096 | tf_op jit(solution)/shard_map/expert/pallas_call | solution.py:325
  57.1 1.6 %collective-permute-start.16 = (bf16[32,3072]{1,0:T(8,128)(2,1)S(1)}, bf16[32,3072]{1,0:T(8,128)(2,1)S(1)}, u32[]{:S(2)}, u32[]{:S(2)}) collective-permute-start(bf16[32,3072]{1,0:T(8,128)(2,1)S(1)} %add_convert_fusion.9), channel_id=1, source_target_pairs={{0,4},{1,5},{2,3},{3,2},{4,0},{5,1},{6,7},{7,6},{8,12},{9,13},{10,... | collective-permute-start | bytes 589832 | tf_op jit(solution)/shard_map/ppermute | solution.py:92
  58.7 2.4 %collective-permute-done.23 = bf16[32,4096]{1,0:T(8,128)(2,1)S(1)} collective-permute-done((bf16[32,4096]{1,0:T(8,128)(2,1)S(1)}, bf16[32,4096]{1,0:T(8,128)(2,1)S(1)}, u32[]{:S(2)}, u32[]{:S(2)}) %collective-permute-start.23) | collective-permute-done | bytes 262176 | tf_op jit(solution)/shard_map/ppermute | solution.py:92
  61.3 1.6 %collective-permute-start.22 = (bf16[32,4096]{1,0:T(8,128)(2,1)S(1)}, bf16[32,4096]{1,0:T(8,128)(2,1)S(1)}, u32[]{:S(2)}, u32[]{:S(2)}) collective-permute-start(bf16[32,4096]{1,0:T(8,128)(2,1)S(1)} %get-tuple-element.56), channel_id=1, source_target_pairs={{0,4},{1,5},{2,3},{3,2},{4,0},{5,1},{6,7},{7,6},{8,12},{9,13},{10,... | collective-permute-start | bytes 786440 | tf_op jit(solution)/shard_map/ppermute | solution.py:92
  62.8 2.4 %collective-permute-start.24 = (bf16[32,4096]{1,0:T(8,128)(2,1)S(1)}, bf16[32,4096]{1,0:T(8,128)(2,1)S(1)}, u32[]{:S(2)}, u32[]{:S(2)}) collective-permute-start(bf16[32,4096]{1,0:T(8,128)(2,1)S(1)} %get-tuple-element.57), channel_id=1, source_target_pairs={{0,1},{1,0},{2,6},{3,7},{4,5},{5,4},{6,2},{7,3},{8,9},{9,8},{10,14... | collective-permute-start | bytes 786440 | tf_op jit(solution)/shard_map/ppermute | solution.py:92
  67.4 2.7 %collective-permute-done.22 = bf16[32,4096]{1,0:T(8,128)(2,1)S(1)} collective-permute-done((bf16[32,4096]{1,0:T(8,128)(2,1)S(1)}, bf16[32,4096]{1,0:T(8,128)(2,1)S(1)}, u32[]{:S(2)}, u32[]{:S(2)}) %collective-permute-start.22) | collective-permute-done | bytes 262176 | tf_op jit(solution)/shard_map/ppermute | solution.py:92
  70.1 1.6 %collective-permute-done.24 = bf16[32,4096]{1,0:T(8,128)(2,1)S(1)} collective-permute-done((bf16[32,4096]{1,0:T(8,128)(2,1)S(1)}, bf16[32,4096]{1,0:T(8,128)(2,1)S(1)}, u32[]{:S(2)}, u32[]{:S(2)}) %collective-permute-start.24) | collective-permute-done | bytes 262176 | tf_op jit(solution)/shard_map/ppermute | solution.py:92
  71.9 2.5 %collective-permute-done.14 = bf16[32,3072]{1,0:T(8,128)(2,1)S(1)} collective-permute-done((bf16[32,3072]{1,0:T(8,128)(2,1)S(1)}, bf16[32,3072]{1,0:T(8,128)(2,1)S(1)}, u32[]{:S(2)}, u32[]{:S(2)}) %collective-permute-start.14) | collective-permute-done | bytes 196640 | tf_op jit(solution)/shard_map/ppermute | solution.py:92
  74.9 2.2 %collective-permute-start.20 = (bf16[8,3072]{1,0:T(8,128)(2,1)S(1)}, bf16[8,3072]{1,0:T(8,128)(2,1)S(1)}, u32[]{:S(2)}, u32[]{:S(2)}) collective-permute-start(bf16[8,3072]{1,0:T(8,128)(2,1)S(1)} %get-tuple-element.66), channel_id=1, source_target_pairs={{0,24},{1,25},{2,26},{3,27},{4,28},{5,29},{6,30},{7,31},{8,16},{9,... | collective-permute-start | bytes 147464 | tf_op jit(solution)/shard_map/ppermute | solution.py:92
  79.4 2.2 %collective-permute-start.27 = (bf16[8,4096]{1,0:T(8,128)(2,1)S(1)}, bf16[8,4096]{1,0:T(8,128)(2,1)S(1)}, u32[]{:S(2)}, u32[]{:S(2)}) collective-permute-start(bf16[8,4096]{1,0:T(8,128)(2,1)S(1)} %get-tuple-element.63), channel_id=1, source_target_pairs={{0,24},{1,25},{2,26},{3,27},{4,28},{5,29},{6,30},{7,31},{8,16},{9,... | collective-permute-start | bytes 196616 | tf_op jit(solution)/shard_map/ppermute | solution.py:92
  81.6 1.8 %collective-permute-done.19 = bf16[8,3072]{1,0:T(8,128)(2,1)S(1)} collective-permute-done((bf16[8,3072]{1,0:T(8,128)(2,1)S(1)}, bf16[8,3072]{1,0:T(8,128)(2,1)S(1)}, u32[]{:S(2)}, u32[]{:S(2)}) %collective-permute-start.19) | collective-permute-done | bytes 49184 | tf_op jit(solution)/shard_map/ppermute | solution.py:92
  83.4 2.5 %collective-permute-done.27 = bf16[8,4096]{1,0:T(8,128)(2,1)S(1)} collective-permute-done((bf16[8,4096]{1,0:T(8,128)(2,1)S(1)}, bf16[8,4096]{1,0:T(8,128)(2,1)S(1)}, u32[]{:S(2)}, u32[]{:S(2)}) %collective-permute-start.27) | collective-permute-done | bytes 65568 | tf_op jit(solution)/shard_map/ppermute | solution.py:92
  85.9 2.7 %collective-permute-done.26 = bf16[8,4096]{1,0:T(8,128)(2,1)S(1)} collective-permute-done((bf16[8,4096]{1,0:T(8,128)(2,1)S(1)}, bf16[8,4096]{1,0:T(8,128)(2,1)S(1)}, u32[]{:S(2)}, u32[]{:S(2)}) %collective-permute-start.26) | collective-permute-done | bytes 65568 | tf_op jit(solution)/shard_map/ppermute | solution.py:92
  (50 shorter events, 16.2 us)
Async XLA Ops:
  1.6 10.0 %collective-permute-start.1 = (bf16[8,7296]{1,0:T(8,128)(2,1)S(1)}, bf16[8,7296]{1,0:T(8,128)(2,1)S(1)}, u32[]{:S(2)}, u32[]{:S(2)}) collective-permute-start(bf16[8,7296]{1,0:T(8,128)(2,1)S(1)} %pack.1.refs_0_), channel_id=1, source_target_pairs={{0,8},{1,9},{2,10},{3,11},{4,12},{5,13},{6,14},{7,15},{8,0},{9,1},... | collective-permute-start | bytes 350216 | tf_op jit(solution)/shard_map/ppermute | solution.py:92
  4.7 8.1 %collective-permute-start = (bf16[8,7296]{1,0:T(8,128)(2,1)S(1)}, bf16[8,7296]{1,0:T(8,128)(2,1)S(1)}, u32[]{:S(2)}, u32[]{:S(2)}) collective-permute-start(bf16[8,7296]{1,0:T(8,128)(2,1)S(1)} %pack.1.refs_0_), channel_id=1, source_target_pairs={{0,16},{1,17},{2,18},{3,19},{4,20},{5,21},{6,22},{7,23},{8,24},{9,... | collective-permute-start | bytes 350216 | tf_op jit(solution)/shard_map/ppermute | solution.py:92
  12.8 4.8 %collective-permute-start.2 = (bf16[8,7296]{1,0:T(8,128)(2,1)S(1)}, bf16[8,7296]{1,0:T(8,128)(2,1)S(1)}, u32[]{:S(2)}, u32[]{:S(2)}) collective-permute-start(bf16[8,7296]{1,0:T(8,128)(2,1)S(1)} %collective-permute-done.refs_2_), channel_id=1, source_target_pairs={{0,8},{1,9},{2,10},{3,11},{4,12},{5,13},{6,14},{7,15},{8,0},{9,1},... | collective-permute-start | bytes 350216 | tf_op jit(solution)/shard_map/ppermute | solution.py:92
  17.7 12.6 %collective-permute-start.3 = (bf16[32,7296]{1,0:T(8,128)(2,1)S(1)}, bf16[32,7296]{1,0:T(8,128)(2,1)S(1)}, u32[]{:S(2)}, u32[]{:S(2)}) collective-permute-start(bf16[32,7296]{1,0:T(8,128)(2,1)S(1)} %join.1.refs_0_), channel_id=1, source_target_pairs={{0,1},{1,0},{2,6},{3,7},{4,5},{5,4},{6,2},{7,3},{8,9},{9,8},{10,14... | collective-permute-start | bytes 1400840 | tf_op jit(solution)/shard_map/ppermute | solution.py:92
  19.3 19.7 %collective-permute-start.9 = (bf16[32,7296]{1,0:T(8,128)(2,1)S(1)}, bf16[32,7296]{1,0:T(8,128)(2,1)S(1)}, u32[]{:S(2)}, u32[]{:S(2)}) collective-permute-start(bf16[32,7296]{1,0:T(8,128)(2,1)S(1)} %join.1.refs_0_), channel_id=1, source_target_pairs={{0,2},{1,3},{2,0},{3,1},{4,6},{5,7},{6,4},{7,5},{8,10},{9,11},{10,... | collective-permute-start | bytes 1400840 | tf_op jit(solution)/shard_map/ppermute | solution.py:92
  19.3 12.7 %collective-permute-start.4 = (bf16[32,7296]{1,0:T(8,128)(2,1)S(1)}, bf16[32,7296]{1,0:T(8,128)(2,1)S(1)}, u32[]{:S(2)}, u32[]{:S(2)}) collective-permute-start(bf16[32,7296]{1,0:T(8,128)(2,1)S(1)} %join.1.refs_0_), channel_id=1, source_target_pairs={{0,4},{1,5},{2,3},{3,2},{4,0},{5,1},{6,7},{7,6},{8,12},{9,13},{10,... | collective-permute-start | bytes 1400840 | tf_op jit(solution)/shard_map/ppermute | solution.py:92
  30.3 6.1 %collective-permute-start.6 = (bf16[16,7296]{1,0:T(8,128)(2,1)S(1)}, bf16[16,7296]{1,0:T(8,128)(2,1)S(1)}, u32[]{:S(2)}, u32[]{:S(2)}) collective-permute-start(bf16[16,7296]{1,0:T(8,128)(2,1)S(1)} %get-tuple-element.60), channel_id=1, source_target_pairs={{0,4},{1,5},{2,3},{3,2},{4,0},{5,1},{6,7},{7,6},{8,12},{9,13},{10,... | collective-permute-start | bytes 700424 | tf_op jit(solution)/shard_map/ppermute | solution.py:92
  31.9 7.1 %collective-permute-start.11 = (bf16[32,7296]{1,0:T(8,128)(2,1)S(1)}, bf16[32,7296]{1,0:T(8,128)(2,1)S(1)}, u32[]{:S(2)}, u32[]{:S(2)}) collective-permute-start(bf16[32,7296]{1,0:T(8,128)(2,1)S(1)} %collective-permute-done.4.refs_2_), channel_id=1, source_target_pairs={{0,2},{1,3},{2,0},{3,1},{4,6},{5,7},{6,4},{7,5},{8,10},{9,11},{10,... | collective-permute-start | bytes 1400840 | tf_op jit(solution)/shard_map/ppermute | solution.py:92
  31.9 7.0 %collective-permute-start.5 = (bf16[16,7296]{1,0:T(8,128)(2,1)S(1)}, bf16[16,7296]{1,0:T(8,128)(2,1)S(1)}, u32[]{:S(2)}, u32[]{:S(2)}) collective-permute-start(bf16[16,7296]{1,0:T(8,128)(2,1)S(1)} %get-tuple-element.61), channel_id=1, source_target_pairs={{0,4},{1,5},{2,3},{3,2},{4,0},{5,1},{6,7},{7,6},{8,12},{9,13},{10,... | collective-permute-start | bytes 700424 | tf_op jit(solution)/shard_map/ppermute | solution.py:92
  32.7 7.9 %collective-permute-start.10 = (bf16[32,7296]{1,0:T(8,128)(2,1)S(1)}, bf16[32,7296]{1,0:T(8,128)(2,1)S(1)}, u32[]{:S(2)}, u32[]{:S(2)}) collective-permute-start(bf16[32,7296]{1,0:T(8,128)(2,1)S(1)} %collective-permute-done.3.refs_1_), channel_id=1, source_target_pairs={{0,2},{1,3},{2,0},{3,1},{4,6},{5,7},{6,4},{7,5},{8,10},{9,11},{10,... | collective-permute-start | bytes 1400840 | tf_op jit(solution)/shard_map/ppermute | solution.py:92
  54.3 6.7 %collective-permute-start.21 = (bf16[96,4096]{1,0:T(8,128)(2,1)S(1)}, bf16[96,4096]{1,0:T(8,128)(2,1)S(1)}, u32[]{:S(2)}, u32[]{:S(2)}) collective-permute-start(bf16[96,4096]{1,0:T(8,128)(2,1)S(1)} %get-tuple-element.51), channel_id=1, source_target_pairs={{0,2},{1,3},{2,0},{3,1},{4,6},{5,7},{6,4},{7,5},{8,10},{9,11},{10,... | collective-permute-start | bytes 2359304 | tf_op jit(solution)/shard_map/ppermute | solution.py:92
  54.7 6.4 %collective-permute-start.23 = (bf16[32,4096]{1,0:T(8,128)(2,1)S(1)}, bf16[32,4096]{1,0:T(8,128)(2,1)S(1)}, u32[]{:S(2)}, u32[]{:S(2)}) collective-permute-start(bf16[32,4096]{1,0:T(8,128)(2,1)S(1)} %add_convert_fusion.6), channel_id=1, source_target_pairs={{0,4},{1,5},{2,3},{3,2},{4,0},{5,1},{6,7},{7,6},{8,12},{9,13},{10,... | collective-permute-start | bytes 786440 | tf_op jit(solution)/shard_map/ppermute | solution.py:92
  56.2 9.1 %collective-permute-start.13 = (bf16[96,3072]{1,0:T(8,128)(2,1)S(1)}, bf16[96,3072]{1,0:T(8,128)(2,1)S(1)}, u32[]{:S(2)}, u32[]{:S(2)}) collective-permute-start(bf16[96,3072]{1,0:T(8,128)(2,1)S(1)} %get-tuple-element.45), channel_id=1, source_target_pairs={{0,2},{1,3},{2,0},{3,1},{4,6},{5,7},{6,4},{7,5},{8,10},{9,11},{10,... | collective-permute-start | bytes 1769480 | tf_op jit(solution)/shard_map/ppermute | solution.py:92
  57.1 8.2 %collective-permute-start.16 = (bf16[32,3072]{1,0:T(8,128)(2,1)S(1)}, bf16[32,3072]{1,0:T(8,128)(2,1)S(1)}, u32[]{:S(2)}, u32[]{:S(2)}) collective-permute-start(bf16[32,3072]{1,0:T(8,128)(2,1)S(1)} %add_convert_fusion.9), channel_id=1, source_target_pairs={{0,4},{1,5},{2,3},{3,2},{4,0},{5,1},{6,7},{7,6},{8,12},{9,13},{10,... | collective-permute-start | bytes 589832 | tf_op jit(solution)/shard_map/ppermute | solution.py:92
  61.3 8.8 %collective-permute-start.22 = (bf16[32,4096]{1,0:T(8,128)(2,1)S(1)}, bf16[32,4096]{1,0:T(8,128)(2,1)S(1)}, u32[]{:S(2)}, u32[]{:S(2)}) collective-permute-start(bf16[32,4096]{1,0:T(8,128)(2,1)S(1)} %get-tuple-element.56), channel_id=1, source_target_pairs={{0,4},{1,5},{2,3},{3,2},{4,0},{5,1},{6,7},{7,6},{8,12},{9,13},{10,... | collective-permute-start | bytes 786440 | tf_op jit(solution)/shard_map/ppermute | solution.py:92
  62.8 8.9 %collective-permute-start.24 = (bf16[32,4096]{1,0:T(8,128)(2,1)S(1)}, bf16[32,4096]{1,0:T(8,128)(2,1)S(1)}, u32[]{:S(2)}, u32[]{:S(2)}) collective-permute-start(bf16[32,4096]{1,0:T(8,128)(2,1)S(1)} %get-tuple-element.57), channel_id=1, source_target_pairs={{0,1},{1,0},{2,6},{3,7},{4,5},{5,4},{6,2},{7,3},{8,9},{9,8},{10,14... | collective-permute-start | bytes 786440 | tf_op jit(solution)/shard_map/ppermute | solution.py:92
  65.4 8.9 %collective-permute-start.14 = (bf16[32,3072]{1,0:T(8,128)(2,1)S(1)}, bf16[32,3072]{1,0:T(8,128)(2,1)S(1)}, u32[]{:S(2)}, u32[]{:S(2)}) collective-permute-start(bf16[32,3072]{1,0:T(8,128)(2,1)S(1)} %get-tuple-element.58), channel_id=1, source_target_pairs={{0,4},{1,5},{2,3},{3,2},{4,0},{5,1},{6,7},{7,6},{8,12},{9,13},{10,... | collective-permute-start | bytes 589832 | tf_op jit(solution)/shard_map/ppermute | solution.py:92
  66.0 8.3 %collective-permute-start.17 = (bf16[32,3072]{1,0:T(8,128)(2,1)S(1)}, bf16[32,3072]{1,0:T(8,128)(2,1)S(1)}, u32[]{:S(2)}, u32[]{:S(2)}) collective-permute-start(bf16[32,3072]{1,0:T(8,128)(2,1)S(1)} %get-tuple-element.59), channel_id=1, source_target_pairs={{0,1},{1,0},{2,6},{3,7},{4,5},{5,4},{6,2},{7,3},{8,9},{9,8},{10,14... | collective-permute-start | bytes 589832 | tf_op jit(solution)/shard_map/ppermute | solution.py:92
  74.4 7.2 %collective-permute-start.18 = (bf16[8,3072]{1,0:T(8,128)(2,1)S(1)}, bf16[8,3072]{1,0:T(8,128)(2,1)S(1)}, u32[]{:S(2)}, u32[]{:S(2)}) collective-permute-start(bf16[8,3072]{1,0:T(8,128)(2,1)S(1)} %get-tuple-element.65), channel_id=1, source_target_pairs={{0,8},{1,9},{2,10},{3,11},{4,12},{5,13},{6,14},{7,15},{8,0},{9,1},... | collective-permute-start | bytes 147464 | tf_op jit(solution)/shard_map/ppermute | solution.py:92
  74.9 6.7 %collective-permute-start.20 = (bf16[8,3072]{1,0:T(8,128)(2,1)S(1)}, bf16[8,3072]{1,0:T(8,128)(2,1)S(1)}, u32[]{:S(2)}, u32[]{:S(2)}) collective-permute-start(bf16[8,3072]{1,0:T(8,128)(2,1)S(1)} %get-tuple-element.66), channel_id=1, source_target_pairs={{0,24},{1,25},{2,26},{3,27},{4,28},{5,29},{6,30},{7,31},{8,16},{9,... | collective-permute-start | bytes 147464 | tf_op jit(solution)/shard_map/ppermute | solution.py:92
  77.1 6.3 %collective-permute-start.19 = (bf16[8,3072]{1,0:T(8,128)(2,1)S(1)}, bf16[8,3072]{1,0:T(8,128)(2,1)S(1)}, u32[]{:S(2)}, u32[]{:S(2)}) collective-permute-start(bf16[8,3072]{1,0:T(8,128)(2,1)S(1)} %get-tuple-element.67), channel_id=1, source_target_pairs={{0,16},{1,17},{2,18},{3,19},{4,20},{5,21},{6,22},{7,23},{8,24},{9,... | collective-permute-start | bytes 147464 | tf_op jit(solution)/shard_map/ppermute | solution.py:92
  78.0 5.4 %collective-permute-start.25 = (bf16[8,4096]{1,0:T(8,128)(2,1)S(1)}, bf16[8,4096]{1,0:T(8,128)(2,1)S(1)}, u32[]{:S(2)}, u32[]{:S(2)}) collective-permute-start(bf16[8,4096]{1,0:T(8,128)(2,1)S(1)} %get-tuple-element.62), channel_id=1, source_target_pairs={{0,8},{1,9},{2,10},{3,11},{4,12},{5,13},{6,14},{7,15},{8,0},{9,1},... | collective-permute-start | bytes 196616 | tf_op jit(solution)/shard_map/ppermute | solution.py:92
  79.4 6.5 %collective-permute-start.27 = (bf16[8,4096]{1,0:T(8,128)(2,1)S(1)}, bf16[8,4096]{1,0:T(8,128)(2,1)S(1)}, u32[]{:S(2)}, u32[]{:S(2)}) collective-permute-start(bf16[8,4096]{1,0:T(8,128)(2,1)S(1)} %get-tuple-element.63), channel_id=1, source_target_pairs={{0,24},{1,25},{2,26},{3,27},{4,28},{5,29},{6,30},{7,31},{8,16},{9,... | collective-permute-start | bytes 196616 | tf_op jit(solution)/shard_map/ppermute | solution.py:92
  81.6 7.0 %collective-permute-start.26 = (bf16[8,4096]{1,0:T(8,128)(2,1)S(1)}, bf16[8,4096]{1,0:T(8,128)(2,1)S(1)}, u32[]{:S(2)}, u32[]{:S(2)}) collective-permute-start(bf16[8,4096]{1,0:T(8,128)(2,1)S(1)} %get-tuple-element.64), channel_id=1, source_target_pairs={{0,16},{1,17},{2,18},{3,19},{4,20},{5,21},{6,22},{7,23},{8,24},{9,... | collective-permute-start | bytes 196616 | tf_op jit(solution)/shard_map/ppermute | solution.py:92
  (5 other events, 9.3 us)

commit v15 on v14

--- a/solution.py
+++ b/solution.py
@@ -113,14 +113,11 @@
             m //= 2
         return masks
 
-    def lines(self, rows, masks, beside):
+    def lines(self, rows, masks):
         if not masks:
-            return [rows], beside
+            return [rows]
         came = self.swap(rows, self.high, masks[0])
-        near, _ = self.lines(rows, masks[1:], ())
-        came, near, beside = lax.optimization_barrier((came, near, beside))
-        far, _ = self.lines(came, masks[1:], ())
-        return near + far, beside
+        return self.lines(rows, masks[1:]) + self.lines(came, masks[1:])
 
     def near(self, line):
         return [line] + [self.swap(line, self.first, m) for m in range(1, self.extent(self.first))]
@@ -377,17 +374,31 @@
     attn_latent = attention(query_latent, query_rope, cache_latent, cache_rope, cache_lengths)
 
     outgoing = pack(experts, moe_rows, route_ids, route_gates)
-    lines, attn_latent = grid.lines(outgoing, grid.masks(), attn_latent)
-    near = grid.near(join(lines))
+    masks = grid.masks()
+    came = grid.swap(outgoing, grid.high, masks[0])
+    near = grid.near(join(grid.lines(outgoing, masks[1:])))
     far = grid.far(near[:-1])
-    rows = near[-1].shape[0] // 2
-    mine = near + far + grid.far([near[-1][:rows], near[-1][rows:]])
-    other = grid.other(mine)
-    size, count = high * tokens, len(mine) - 1
+    lines = grid.lines(came, masks[1:])
+    lines[-1], near[-1], far[0] = tied((lines[-1], near[-1], far[0]))
+    later_near = grid.near(join(lines))
+    later_far = grid.far(later_near[:-1])
+    far += grid.far(near[-1:])
+    far[-1], later_near[-1], later_far[0], attn_latent = tied(
+        (far[-1], later_near[-1], later_far[0], attn_latent)
+    )
+    rows = later_near[-1].shape[0] // 2
+    last = grid.far([later_near[-1][:rows], later_near[-1][rows:]])
+    mine = [[block] for block in near + far]
+    for place, block in zip(mine, later_near + later_far):
+        place.append(block)
+    mine[-1] += last
+    other = [grid.other(place) for place in mine]
+    size, count = high * tokens, len(mine)
     sizes = [size] * count + [size, size * (count - 1)]
-    split = width * 3 // 7
+    split = width // 2
+    places = mine + other[-1:] + other[:-1]
     products = expert(
-        mine + other[-2:] + other[:-2],
+        [block for place in places for block in place],
         w_gate[0],
         w_up[0],
         w_down[0],
@@ -397,16 +408,13 @@
         split,
     )
 
-    def returned(parts, last):
+    def returned(parts):
+        last = grid.last_sum(parts[:count], parts[count:])
         sums = grid.rest_sums(parts[:count], parts[count:]) + [last]
         return grid.high_sum(grid.line_sum(sums, grid.back(sums, count - 1)))
 
-    small, large = products[: len(sizes)], products[len(sizes) :]
-    last = grid.last_sum(large[:count], large[count:])
-    small, last = tied((small, last))
-    large = returned(large, last)
-    small = returned(small, grid.last_sum(small[:count], small[count:]))
-    return (jnp.concatenate([small, large], axis=1), attn_latent)
+    head, tail = returned(products[: len(sizes)]), returned(products[len(sizes) :])
+    return (jnp.concatenate([head, tail], axis=1), attn_latent)
 
 
 def solution(mesh):

time: 89.5 us -> 79.4 us (0.89)
  waiting for transfers between devices: 38.6 us -> 26.4 us
  starting transfers between devices: 31.3 us -> 33.3 us
    ppermute x28 -> x35, waiting for transfers between devices: 38.6 us -> 26.4 us  [swap(): return lax.ppermute(value, everyone, pairs)]
    ppermute x28 -> x35, starting transfers between devices: 31.3 us -> 33.3 us  [swap(): return lax.ppermute(value, everyone, pairs)]
  transfers between devices with their start and end apart: 28 -> 35, of which waited for: 14 -> 15; matrix products, arithmetic and copies ran while one was open for 1% -> 1% of each run, Pallas kernels for 4% -> 5%
where the time goes in v15:
time: 79.4 us; the launch traced here: 79.2 us
  starting transfers between devices  33.3 us (42%)
  waiting for transfers between devices  26.4 us (33%)
  Pallas kernels  16.7 us (21%)
  other arithmetic  1.34 us (2%)
    ppermute x35, starting transfers between devices, swap(): return lax.ppermute(value, everyone, pairs)  33.3 us
    ppermute x35, waiting for transfers between devices, swap(): return lax.ppermute(value, everyone, pairs)  26.4 us
    pallas_call x1, Pallas kernels, expert(): pl.pallas_call(functools.partial(expert_kernel, len(blocks), experts, til...  11.9 us
    pallas_call x1, Pallas kernels, attention(): pl.pallas_call(attention_kernel, in_specs=[pl.BlockSpec(memory_space=pltp...  3.66 us
  transfers between devices with their start and end apart: 35, of which 15 were waited for; matrix products, arithmetic and copies ran while one was open for 1% of the time, Pallas kernels for 5%

profile of v15, /device:TPU:0, one launch (start us, length us, event | category | flops | bytes accessed | tf_op | source)
XLA Modules:
  0.0 79.2 jit_solution(3202743907716830663)
XLA Ops:
  1.6 3.1 %collective-permute-start = (bf16[8,7296]{1,0:T(8,128)(2,1)S(1)}, bf16[8,7296]{1,0:T(8,128)(2,1)S(1)}, u32[]{:S(2)}, u32[]{:S(2)}) collective-permute-start(bf16[8,7296]{1,0:T(8,128)(2,1)S(1)} %pack.1.refs_0_), channel_id=1, source_target_pairs={{0,8},{1,9},{2,10},{3,11},{4,12},{5,13},{6,14},{7,15},{8,0},{9,1},... | collective-permute-start | bytes 350216 | tf_op jit(solution)/shard_map/ppermute | solution.py:92
  4.7 2.6 %collective-permute-start.1 = (bf16[8,7296]{1,0:T(8,128)(2,1)S(1)}, bf16[8,7296]{1,0:T(8,128)(2,1)S(1)}, u32[]{:S(2)}, u32[]{:S(2)}) collective-permute-start(bf16[8,7296]{1,0:T(8,128)(2,1)S(1)} %pack.1.refs_0_), channel_id=1, source_target_pairs={{0,16},{1,17},{2,18},{3,19},{4,20},{5,21},{6,22},{7,23},{8,24},{9,... | collective-permute-start | bytes 350216 | tf_op jit(solution)/shard_map/ppermute | solution.py:92
  7.3 1.8 %collective-permute-done.refs_1_ = bf16[8,7296]{1,0:T(8,128)(2,1)S(1)} collective-permute-done((bf16[8,7296]{1,0:T(8,128)(2,1)S(1)}, bf16[8,7296]{1,0:T(8,128)(2,1)S(1)}, u32[]{:S(2)}, u32[]{:S(2)}) %collective-permute-start) | collective-permute-done | bytes 116768 | tf_op jit(solution)/shard_map/ppermute | solution.py:92
  9.2 1.9 %collective-permute-start.4 = (bf16[16,7296]{1,0:T(8,128)(2,1)S(1)}, bf16[16,7296]{1,0:T(8,128)(2,1)S(1)}, u32[]{:S(2)}, u32[]{:S(2)}) collective-permute-start(bf16[16,7296]{1,0:T(8,128)(2,1)S(1)} %join.2.refs_0_), channel_id=1, source_target_pairs={{0,4},{1,5},{2,3},{3,2},{4,0},{5,1},{6,7},{7,6},{8,12},{9,13},{10,... | collective-permute-start | bytes 700424 | tf_op jit(solution)/shard_map/ppermute | solution.py:92
  11.1 1.5 %collective-permute-start.3 = (bf16[16,7296]{1,0:T(8,128)(2,1)S(1)}, bf16[16,7296]{1,0:T(8,128)(2,1)S(1)}, u32[]{:S(2)}, u32[]{:S(2)}) collective-permute-start(bf16[16,7296]{1,0:T(8,128)(2,1)S(1)} %join.2.refs_0_), channel_id=1, source_target_pairs={{0,1},{1,0},{2,6},{3,7},{4,5},{5,4},{6,2},{7,3},{8,9},{9,8},{10,14... | collective-permute-start | bytes 700424 | tf_op jit(solution)/shard_map/ppermute | solution.py:92
  13.2 4.4 %collective-permute-done.2.refs_1_ = bf16[8,7296]{1,0:T(8,128)(2,1)S(1)} collective-permute-done((bf16[8,7296]{1,0:T(8,128)(2,1)S(1)}, bf16[8,7296]{1,0:T(8,128)(2,1)S(1)}, u32[]{:S(2)}, u32[]{:S(2)}) %collective-permute-start.2) | collective-permute-done | bytes 116768 | tf_op jit(solution)/shard_map/ppermute | solution.py:92
  17.7 1.6 %collective-permute-start.7 = (bf16[16,7296]{1,0:T(8,128)(2,1)S(1)}, bf16[16,7296]{1,0:T(8,128)(2,1)S(1)}, u32[]{:S(2)}, u32[]{:S(2)}) collective-permute-start(bf16[16,7296]{1,0:T(8,128)(2,1)S(1)} %join.3.refs_1_), channel_id=1, source_target_pairs={{0,4},{1,5},{2,3},{3,2},{4,0},{5,1},{6,7},{7,6},{8,12},{9,13},{10,... | collective-permute-start | bytes 700424 | tf_op jit(solution)/shard_map/ppermute | solution.py:92
  19.3 1.5 %collective-permute-start.6 = (bf16[16,7296]{1,0:T(8,128)(2,1)S(1)}, bf16[16,7296]{1,0:T(8,128)(2,1)S(1)}, u32[]{:S(2)}, u32[]{:S(2)}) collective-permute-start(bf16[16,7296]{1,0:T(8,128)(2,1)S(1)} %join.3.refs_1_), channel_id=1, source_target_pairs={{0,1},{1,0},{2,6},{3,7},{4,5},{5,4},{6,2},{7,3},{8,9},{9,8},{10,14... | collective-permute-start | bytes 700424 | tf_op jit(solution)/shard_map/ppermute | solution.py:92
  21.9 3.7 %attention.1 = bf16[2,64,512]{2,1,0:T(8,128)(2,1)} custom-call(s32[2]{0:T(128)S(1)} %copy-done, bf16[2,64,512]{2,1,0:T(8,128)(2,1)} %refs_0_.3, bf16[2,64,64]{2,1,0:T(8,128)(2,1)} %refs_1_.3, bf16[2,512,512]{2,1,0:T(8,128)(2,1)} %refs_2_.3, bf16[2,64,512]{2,1,0:T(8,128)(2,1)} %refs_3_.1), custom_call_target="tpu_custom_call" | custom-call | flops 134217728 | bytes 1048576 | tf_op jit(solution)/shard_map/attention/pallas_call | solution.py:54
  26.8 1.4 %collective-permute-start.9 = (bf16[8,7296]{1,0:T(8,128)(2,1)S(1)}, bf16[8,7296]{1,0:T(8,128)(2,1)S(1)}, u32[]{:S(2)}, u32[]{:S(2)}) collective-permute-start(bf16[8,7296]{1,0:T(8,128)(2,1)S(1)} %get-tuple-element.44), channel_id=1, source_target_pairs={{0,4},{1,5},{2,3},{3,2},{4,0},{5,1},{6,7},{7,6},{8,12},{9,13},{10,... | collective-permute-start | bytes 350216 | tf_op jit(solution)/shard_map/ppermute | solution.py:92
  29.5 2.2 %collective-permute-done.9.refs_8_ = bf16[8,7296]{1,0:T(8,128)(2,1)S(1)} collective-permute-done((bf16[8,7296]{1,0:T(8,128)(2,1)S(1)}, bf16[8,7296]{1,0:T(8,128)(2,1)S(1)}, u32[]{:S(2)}, u32[]{:S(2)}) %collective-permute-start.9) | collective-permute-done | bytes 116768 | tf_op jit(solution)/shard_map/ppermute | solution.py:92
  31.7 1.4 %collective-permute-done.8.refs_7_ = bf16[8,7296]{1,0:T(8,128)(2,1)S(1)} collective-permute-done((bf16[8,7296]{1,0:T(8,128)(2,1)S(1)}, bf16[8,7296]{1,0:T(8,128)(2,1)S(1)}, u32[]{:S(2)}, u32[]{:S(2)}) %collective-permute-start.8) | collective-permute-done | bytes 116768 | tf_op jit(solution)/shard_map/ppermute | solution.py:92
  33.2 1.4 %collective-permute-done.11.refs_10_ = bf16[8,7296]{1,0:T(8,128)(2,1)} collective-permute-done((bf16[8,7296]{1,0:T(8,128)(2,1)S(1)}, bf16[8,7296]{1,0:T(8,128)(2,1)}, u32[]{:S(2)}, u32[]{:S(2)}) %collective-permute-start.11) | collective-permute-done | bytes 116768 | tf_op jit(solution)/shard_map/ppermute | solution.py:92
  34.6 11.9 %expert.1 = (bf16[32,3584]{1,0:T(8,128)(2,1)S(1)}, bf16[32,3584]{1,0:T(8,128)(2,1)S(1)}, bf16[32,3584]{1,0:T(8,128)(2,1)S(1)}, bf16[32,3584]{1,0:T(8,128)(2,1)S(...) custom-call(s32[1]{0:T(128)} %bitcast.node_ref, ...), custom_call_target="tpu_custom_call" | custom-call | flops 5637144576 | bytes 22020096 | tf_op jit(solution)/shard_map/expert/pallas_call | solution.py:322
  48.1 1.3 %collective-permute-start.22 = (bf16[32,3584]{1,0:T(8,128)(2,1)S(1)}, bf16[32,3584]{1,0:T(8,128)(2,1)S(1)}, u32[]{:S(2)}, u32[]{:S(2)}) collective-permute-start(bf16[32,3584]{1,0:T(8,128)(2,1)S(1)} %add_convert_fusion.9), channel_id=1, source_target_pairs={{0,4},{1,5},{2,3},{3,2},{4,0},{5,1},{6,7},{7,6},{8,12},{9,13},{10,... | collective-permute-start | bytes 688136 | tf_op jit(solution)/shard_map/ppermute | solution.py:92
  50.4 3.9 %collective-permute-done.22 = bf16[32,3584]{1,0:T(8,128)(2,1)S(1)} collective-permute-done((bf16[32,3584]{1,0:T(8,128)(2,1)S(1)}, bf16[32,3584]{1,0:T(8,128)(2,1)S(1)}, u32[]{:S(2)}, u32[]{:S(2)}) %collective-permute-start.22) | collective-permute-done | bytes 229408 | tf_op jit(solution)/shard_map/ppermute | solution.py:92
  54.4 1.3 %collective-permute-start.20 = (bf16[32,3584]{1,0:T(8,128)(2,1)S(1)}, bf16[32,3584]{1,0:T(8,128)(2,1)S(1)}, u32[]{:S(2)}, u32[]{:S(2)}) collective-permute-start(bf16[32,3584]{1,0:T(8,128)(2,1)S(1)} %get-tuple-element.40), channel_id=1, source_target_pairs={{0,4},{1,5},{2,3},{3,2},{4,0},{5,1},{6,7},{7,6},{8,12},{9,13},{10,... | collective-permute-start | bytes 688136 | tf_op jit(solution)/shard_map/ppermute | solution.py:92
  57.0 1.2 %collective-permute-start.28 = (bf16[32,3584]{1,0:T(8,128)(2,1)S(1)}, bf16[32,3584]{1,0:T(8,128)(2,1)S(1)}, u32[]{:S(2)}, u32[]{:S(2)}) collective-permute-start(bf16[32,3584]{1,0:T(8,128)(2,1)S(1)} %get-tuple-element.42), channel_id=1, source_target_pairs={{0,4},{1,5},{2,3},{3,2},{4,0},{5,1},{6,7},{7,6},{8,12},{9,13},{10,... | collective-permute-start | bytes 688136 | tf_op jit(solution)/shard_map/ppermute | solution.py:92
  59.3 3.6 %collective-permute-done.20 = bf16[32,3584]{1,0:T(8,128)(2,1)S(1)} collective-permute-done((bf16[32,3584]{1,0:T(8,128)(2,1)S(1)}, bf16[32,3584]{1,0:T(8,128)(2,1)S(1)}, u32[]{:S(2)}, u32[]{:S(2)}) %collective-permute-start.20) | collective-permute-done | bytes 229408 | tf_op jit(solution)/shard_map/ppermute | solution.py:92
  64.7 3.2 %collective-permute-start.26 = (bf16[8,3584]{1,0:T(8,128)(2,1)S(1)}, bf16[8,3584]{1,0:T(8,128)(2,1)S(1)}, u32[]{:S(2)}, u32[]{:S(2)}) collective-permute-start(bf16[8,3584]{1,0:T(8,128)(2,1)S(1)} %get-tuple-element.47), channel_id=1, source_target_pairs={{0,24},{1,25},{2,26},{3,27},{4,28},{5,29},{6,30},{7,31},{8,16},{9,... | collective-permute-start | bytes 172040 | tf_op jit(solution)/shard_map/ppermute | solution.py:92
  69.3 3.2 %collective-permute-start.34 = (bf16[8,3584]{1,0:T(8,128)(2,1)S(1)}, bf16[8,3584]{1,0:T(8,128)(2,1)S(1)}, u32[]{:S(2)}, u32[]{:S(2)}) collective-permute-start(bf16[8,3584]{1,0:T(8,128)(2,1)S(1)} %get-tuple-element.50), channel_id=1, source_target_pairs={{0,24},{1,25},{2,26},{3,27},{4,28},{5,29},{6,30},{7,31},{8,16},{9,... | collective-permute-start | bytes 172040 | tf_op jit(solution)/shard_map/ppermute | solution.py:92
  72.5 2.2 %collective-permute-done.25 = bf16[8,3584]{1,0:T(8,128)(2,1)S(1)} collective-permute-done((bf16[8,3584]{1,0:T(8,128)(2,1)S(1)}, bf16[8,3584]{1,0:T(8,128)(2,1)S(1)}, u32[]{:S(2)}, u32[]{:S(2)}) %collective-permute-start.25) | collective-permute-done | bytes 57376 | tf_op jit(solution)/shard_map/ppermute | solution.py:92
  74.7 1.1 %collective-permute-done.34 = bf16[8,3584]{1,0:T(8,128)(2,1)S(1)} collective-permute-done((bf16[8,3584]{1,0:T(8,128)(2,1)S(1)}, bf16[8,3584]{1,0:T(8,128)(2,1)S(1)}, u32[]{:S(2)}, u32[]{:S(2)}) %collective-permute-start.34) | collective-permute-done | bytes 57376 | tf_op jit(solution)/shard_map/ppermute | solution.py:92
  75.8 2.7 %collective-permute-done.33 = bf16[8,3584]{1,0:T(8,128)(2,1)S(1)} collective-permute-done((bf16[8,3584]{1,0:T(8,128)(2,1)S(1)}, bf16[8,3584]{1,0:T(8,128)(2,1)S(1)}, u32[]{:S(2)}, u32[]{:S(2)}) %collective-permute-start.33) | collective-permute-done | bytes 57376 | tf_op jit(solution)/shard_map/ppermute | solution.py:92
  (65 shorter events, 14.5 us)
Async XLA Ops:
  1.6 7.5 %collective-permute-start = (bf16[8,7296]{1,0:T(8,128)(2,1)S(1)}, bf16[8,7296]{1,0:T(8,128)(2,1)S(1)}, u32[]{:S(2)}, u32[]{:S(2)}) collective-permute-start(bf16[8,7296]{1,0:T(8,128)(2,1)S(1)} %pack.1.refs_0_), channel_id=1, source_target_pairs={{0,8},{1,9},{2,10},{3,11},{4,12},{5,13},{6,14},{7,15},{8,0},{9,1},... | collective-permute-start | bytes 350216 | tf_op jit(solution)/shard_map/ppermute | solution.py:92
  4.7 8.1 %collective-permute-start.1 = (bf16[8,7296]{1,0:T(8,128)(2,1)S(1)}, bf16[8,7296]{1,0:T(8,128)(2,1)S(1)}, u32[]{:S(2)}, u32[]{:S(2)}) collective-permute-start(bf16[8,7296]{1,0:T(8,128)(2,1)S(1)} %pack.1.refs_0_), channel_id=1, source_target_pairs={{0,16},{1,17},{2,18},{3,19},{4,20},{5,21},{6,22},{7,23},{8,24},{9,... | collective-permute-start | bytes 350216 | tf_op jit(solution)/shard_map/ppermute | solution.py:92
  9.2 8.5 %collective-permute-start.4 = (bf16[16,7296]{1,0:T(8,128)(2,1)S(1)}, bf16[16,7296]{1,0:T(8,128)(2,1)S(1)}, u32[]{:S(2)}, u32[]{:S(2)}) collective-permute-start(bf16[16,7296]{1,0:T(8,128)(2,1)S(1)} %join.2.refs_0_), channel_id=1, source_target_pairs={{0,4},{1,5},{2,3},{3,2},{4,0},{5,1},{6,7},{7,6},{8,12},{9,13},{10,... | collective-permute-start | bytes 700424 | tf_op jit(solution)/shard_map/ppermute | solution.py:92
  11.1 6.6 %collective-permute-start.3 = (bf16[16,7296]{1,0:T(8,128)(2,1)S(1)}, bf16[16,7296]{1,0:T(8,128)(2,1)S(1)}, u32[]{:S(2)}, u32[]{:S(2)}) collective-permute-start(bf16[16,7296]{1,0:T(8,128)(2,1)S(1)} %join.2.refs_0_), channel_id=1, source_target_pairs={{0,1},{1,0},{2,6},{3,7},{4,5},{5,4},{6,2},{7,3},{8,9},{9,8},{10,14... | collective-permute-start | bytes 700424 | tf_op jit(solution)/shard_map/ppermute | solution.py:92
  17.7 8.5 %collective-permute-start.7 = (bf16[16,7296]{1,0:T(8,128)(2,1)S(1)}, bf16[16,7296]{1,0:T(8,128)(2,1)S(1)}, u32[]{:S(2)}, u32[]{:S(2)}) collective-permute-start(bf16[16,7296]{1,0:T(8,128)(2,1)S(1)} %join.3.refs_1_), channel_id=1, source_target_pairs={{0,4},{1,5},{2,3},{3,2},{4,0},{5,1},{6,7},{7,6},{8,12},{9,13},{10,... | collective-permute-start | bytes 700424 | tf_op jit(solution)/shard_map/ppermute | solution.py:92
  19.3 7.0 %collective-permute-start.6 = (bf16[16,7296]{1,0:T(8,128)(2,1)S(1)}, bf16[16,7296]{1,0:T(8,128)(2,1)S(1)}, u32[]{:S(2)}, u32[]{:S(2)}) collective-permute-start(bf16[16,7296]{1,0:T(8,128)(2,1)S(1)} %join.3.refs_1_), channel_id=1, source_target_pairs={{0,1},{1,0},{2,6},{3,7},{4,5},{5,4},{6,2},{7,3},{8,9},{9,8},{10,14... | collective-permute-start | bytes 700424 | tf_op jit(solution)/shard_map/ppermute | solution.py:92
  20.7 6.1 %collective-permute-start.5 = (bf16[16,7296]{1,0:T(8,128)(2,1)S(1)}, bf16[16,7296]{1,0:T(8,128)(2,1)S(1)}, u32[]{:S(2)}, u32[]{:S(2)}) collective-permute-start(bf16[16,7296]{1,0:T(8,128)(2,1)S(1)} %collective-permute-done.3.refs_2_), channel_id=1, source_target_pairs={{0,4},{1,5},{2,3},{3,2},{4,0},{5,1},{6,7},{7,6},{8,12},{9,13},{10,... | collective-permute-start | bytes 700424 | tf_op jit(solution)/shard_map/ppermute | solution.py:92
  28.9 5.6 %collective-permute-start.18 = (bf16[16,7296]{1,0:T(8,128)(2,1)S(1)}, bf16[16,7296]{1,0:T(8,128)(2,1)S(1)}, u32[]{:S(2)}, u32[]{:S(2)}) collective-permute-start(bf16[16,7296]{1,0:T(8,128)(2,1)S(1)} %collective-permute-done.7.refs_5_), channel_id=1, source_target_pairs={{0,2},{1,3},{2,0},{3,1},{4,6},{5,7},{6,4},{7,5},{8,10},{9,11},{10,... | collective-permute-start | bytes 700424 | tf_op jit(solution)/shard_map/ppermute | solution.py:92
  28.9 5.6 %collective-permute-start.10 = (bf16[16,7296]{1,0:T(8,128)(2,1)S(1)}, bf16[16,7296]{1,0:T(8,128)(2,1)S(1)}, u32[]{:S(2)}, u32[]{:S(2)}) collective-permute-start(bf16[16,7296]{1,0:T(8,128)(2,1)S(1)} %collective-permute-done.5.refs_6_), channel_id=1, source_target_pairs={{0,2},{1,3},{2,0},{3,1},{4,6},{5,7},{6,4},{7,5},{8,10},{9,11},{10,... | collective-permute-start | bytes 700424 | tf_op jit(solution)/shard_map/ppermute | solution.py:92
  29.5 5.1 %collective-permute-start.16 = (bf16[16,7296]{1,0:T(8,128)(2,1)S(1)}, bf16[16,7296]{1,0:T(8,128)(2,1)S(1)}, u32[]{:S(2)}, u32[]{:S(2)}) collective-permute-start(bf16[16,7296]{1,0:T(8,128)(2,1)S(1)} %collective-permute-done.6.refs_3_), channel_id=1, source_target_pairs={{0,2},{1,3},{2,0},{3,1},{4,6},{5,7},{6,4},{7,5},{8,10},{9,11},{10,... | collective-permute-start | bytes 700424 | tf_op jit(solution)/shard_map/ppermute | solution.py:92
  47.1 7.1 %collective-permute-start.19 = (bf16[96,3584]{1,0:T(8,128)(2,1)S(1)}, bf16[96,3584]{1,0:T(8,128)(2,1)S(1)}, u32[]{:S(2)}, u32[]{:S(2)}) collective-permute-start(bf16[96,3584]{1,0:T(8,128)(2,1)S(1)} %get-tuple-element.28), channel_id=1, source_target_pairs={{0,2},{1,3},{2,0},{3,1},{4,6},{5,7},{6,4},{7,5},{8,10},{9,11},{10,... | collective-permute-start | bytes 2064392 | tf_op jit(solution)/shard_map/ppermute | solution.py:92
  47.3 9.6 %collective-permute-start.27 = (bf16[96,3584]{1,0:T(8,128)(2,1)S(1)}, bf16[96,3584]{1,0:T(8,128)(2,1)S(1)}, u32[]{:S(2)}, u32[]{:S(2)}) collective-permute-start(bf16[96,3584]{1,0:T(8,128)(2,1)S(1)} %get-tuple-element.34), channel_id=1, source_target_pairs={{0,2},{1,3},{2,0},{3,1},{4,6},{5,7},{6,4},{7,5},{8,10},{9,11},{10,... | collective-permute-start | bytes 2064392 | tf_op jit(solution)/shard_map/ppermute | solution.py:92
  48.1 6.1 %collective-permute-start.22 = (bf16[32,3584]{1,0:T(8,128)(2,1)S(1)}, bf16[32,3584]{1,0:T(8,128)(2,1)S(1)}, u32[]{:S(2)}, u32[]{:S(2)}) collective-permute-start(bf16[32,3584]{1,0:T(8,128)(2,1)S(1)} %add_convert_fusion.9), channel_id=1, source_target_pairs={{0,4},{1,5},{2,3},{3,2},{4,0},{5,1},{6,7},{7,6},{8,12},{9,13},{10,... | collective-permute-start | bytes 688136 | tf_op jit(solution)/shard_map/ppermute | solution.py:92
  49.5 7.3 %collective-permute-start.30 = (bf16[32,3584]{1,0:T(8,128)(2,1)S(1)}, bf16[32,3584]{1,0:T(8,128)(2,1)S(1)}, u32[]{:S(2)}, u32[]{:S(2)}) collective-permute-start(bf16[32,3584]{1,0:T(8,128)(2,1)S(1)} %add_convert_fusion.2), channel_id=1, source_target_pairs={{0,4},{1,5},{2,3},{3,2},{4,0},{5,1},{6,7},{7,6},{8,12},{9,13},{10,... | collective-permute-start | bytes 688136 | tf_op jit(solution)/shard_map/ppermute | solution.py:92
  54.4 8.5 %collective-permute-start.20 = (bf16[32,3584]{1,0:T(8,128)(2,1)S(1)}, bf16[32,3584]{1,0:T(8,128)(2,1)S(1)}, u32[]{:S(2)}, u32[]{:S(2)}) collective-permute-start(bf16[32,3584]{1,0:T(8,128)(2,1)S(1)} %get-tuple-element.40), channel_id=1, source_target_pairs={{0,4},{1,5},{2,3},{3,2},{4,0},{5,1},{6,7},{7,6},{8,12},{9,13},{10,... | collective-permute-start | bytes 688136 | tf_op jit(solution)/shard_map/ppermute | solution.py:92
  55.7 8.0 %collective-permute-start.23 = (bf16[32,3584]{1,0:T(8,128)(2,1)S(1)}, bf16[32,3584]{1,0:T(8,128)(2,1)S(1)}, u32[]{:S(2)}, u32[]{:S(2)}) collective-permute-start(bf16[32,3584]{1,0:T(8,128)(2,1)S(1)} %get-tuple-element.41), channel_id=1, source_target_pairs={{0,1},{1,0},{2,6},{3,7},{4,5},{5,4},{6,2},{7,3},{8,9},{9,8},{10,14... | collective-permute-start | bytes 688136 | tf_op jit(solution)/shard_map/ppermute | solution.py:92
  57.0 11.4 %collective-permute-start.28 = (bf16[32,3584]{1,0:T(8,128)(2,1)S(1)}, bf16[32,3584]{1,0:T(8,128)(2,1)S(1)}, u32[]{:S(2)}, u32[]{:S(2)}) collective-permute-start(bf16[32,3584]{1,0:T(8,128)(2,1)S(1)} %get-tuple-element.42), channel_id=1, source_target_pairs={{0,4},{1,5},{2,3},{3,2},{4,0},{5,1},{6,7},{7,6},{8,12},{9,13},{10,... | collective-permute-start | bytes 688136 | tf_op jit(solution)/shard_map/ppermute | solution.py:92
  58.1 10.2 %collective-permute-start.31 = (bf16[32,3584]{1,0:T(8,128)(2,1)S(1)}, bf16[32,3584]{1,0:T(8,128)(2,1)S(1)}, u32[]{:S(2)}, u32[]{:S(2)}) collective-permute-start(bf16[32,3584]{1,0:T(8,128)(2,1)S(1)} %get-tuple-element.43), channel_id=1, source_target_pairs={{0,1},{1,0},{2,6},{3,7},{4,5},{5,4},{6,2},{7,3},{8,9},{9,8},{10,14... | collective-permute-start | bytes 688136 | tf_op jit(solution)/shard_map/ppermute | solution.py:92
  63.8 8.6 %collective-permute-start.24 = (bf16[8,3584]{1,0:T(8,128)(2,1)S(1)}, bf16[8,3584]{1,0:T(8,128)(2,1)S(1)}, u32[]{:S(2)}, u32[]{:S(2)}) collective-permute-start(bf16[8,3584]{1,0:T(8,128)(2,1)S(1)} %get-tuple-element.46), channel_id=1, source_target_pairs={{0,8},{1,9},{2,10},{3,11},{4,12},{5,13},{6,14},{7,15},{8,0},{9,1},... | collective-permute-start | bytes 172040 | tf_op jit(solution)/shard_map/ppermute | solution.py:92
  64.7 7.8 %collective-permute-start.26 = (bf16[8,3584]{1,0:T(8,128)(2,1)S(1)}, bf16[8,3584]{1,0:T(8,128)(2,1)S(1)}, u32[]{:S(2)}, u32[]{:S(2)}) collective-permute-start(bf16[8,3584]{1,0:T(8,128)(2,1)S(1)} %get-tuple-element.47), channel_id=1, source_target_pairs={{0,24},{1,25},{2,26},{3,27},{4,28},{5,29},{6,30},{7,31},{8,16},{9,... | collective-permute-start | bytes 172040 | tf_op jit(solution)/shard_map/ppermute | solution.py:92
  67.9 6.8 %collective-permute-start.25 = (bf16[8,3584]{1,0:T(8,128)(2,1)S(1)}, bf16[8,3584]{1,0:T(8,128)(2,1)S(1)}, u32[]{:S(2)}, u32[]{:S(2)}) collective-permute-start(bf16[8,3584]{1,0:T(8,128)(2,1)S(1)} %get-tuple-element.48), channel_id=1, source_target_pairs={{0,16},{1,17},{2,18},{3,19},{4,20},{5,21},{6,22},{7,23},{8,24},{9,... | collective-permute-start | bytes 172040 | tf_op jit(solution)/shard_map/ppermute | solution.py:92
  68.5 6.2 %collective-permute-start.32 = (bf16[8,3584]{1,0:T(8,128)(2,1)S(1)}, bf16[8,3584]{1,0:T(8,128)(2,1)S(1)}, u32[]{:S(2)}, u32[]{:S(2)}) collective-permute-start(bf16[8,3584]{1,0:T(8,128)(2,1)S(1)} %get-tuple-element.49), channel_id=1, source_target_pairs={{0,8},{1,9},{2,10},{3,11},{4,12},{5,13},{6,14},{7,15},{8,0},{9,1},... | collective-permute-start | bytes 172040 | tf_op jit(solution)/shard_map/ppermute | solution.py:92
  69.3 6.5 %collective-permute-start.34 = (bf16[8,3584]{1,0:T(8,128)(2,1)S(1)}, bf16[8,3584]{1,0:T(8,128)(2,1)S(1)}, u32[]{:S(2)}, u32[]{:S(2)}) collective-permute-start(bf16[8,3584]{1,0:T(8,128)(2,1)S(1)} %get-tuple-element.50), channel_id=1, source_target_pairs={{0,24},{1,25},{2,26},{3,27},{4,28},{5,29},{6,30},{7,31},{8,16},{9,... | collective-permute-start | bytes 172040 | tf_op jit(solution)/shard_map/ppermute | solution.py:92
  72.5 6.0 %collective-permute-start.33 = (bf16[8,3584]{1,0:T(8,128)(2,1)S(1)}, bf16[8,3584]{1,0:T(8,128)(2,1)S(1)}, u32[]{:S(2)}, u32[]{:S(2)}) collective-permute-start(bf16[8,3584]{1,0:T(8,128)(2,1)S(1)} %get-tuple-element.51), channel_id=1, source_target_pairs={{0,16},{1,17},{2,18},{3,19},{4,20},{5,21},{6,22},{7,23},{8,24},{9,... | collective-permute-start | bytes 172040 | tf_op jit(solution)/shard_map/ppermute | solution.py:92
  (12 other events, 34.3 us)

commit v16 on v15

--- a/solution.py
+++ b/solution.py
@@ -141,14 +141,9 @@
     def back(self, sums, place):
         return self.swap(sums[place], self.second, place // self.extent(self.first))
 
-    def line_sum(self, sums, last):
-        wide = self.extent(self.first)
-        near = [[part] for part in sums[:wide]]
-        for place in range(wide, len(sums)):
-            moved = last if place == len(sums) - 1 else self.back(sums, place)
-            near[place % wide].append(moved)
-        near = [add(parts) for parts in near]
-        return add([near[0]] + [self.swap(near[m], self.first, m) for m in range(1, wide)])
+    def line_sum(self, sums, came):
+        near = [add(list(parts)) for parts in zip(sums, came)]
+        return add([near[0]] + [self.swap(near[m], self.first, m) for m in range(1, len(near))])
 
     def high_sum(self, line):
         rows = line.shape[0] // self.extent(self.high)
@@ -382,9 +377,10 @@
     lines[-1], near[-1], far[0] = tied((lines[-1], near[-1], far[0]))
     later_near = grid.near(join(lines))
     later_far = grid.far(later_near[:-1])
+    early = grid.other(near + far)
     far += grid.far(near[-1:])
-    far[-1], later_near[-1], later_far[0], attn_latent = tied(
-        (far[-1], later_near[-1], later_far[0], attn_latent)
+    far[-1], later_near[-1], later_far[0], early, attn_latent = tied(
+        (far[-1], later_near[-1], later_far[0], early, attn_latent)
     )
     rows = later_near[-1].shape[0] // 2
     last = grid.far([later_near[-1][:rows], later_near[-1][rows:]])
@@ -392,7 +388,8 @@
     for place, block in zip(mine, later_near + later_far):
         place.append(block)
     mine[-1] += last
-    other = [grid.other(place) for place in mine]
+    other = [[block] + grid.other(place[1:]) for block, place in zip(early, mine)]
+    other.append(grid.other(mine[-1]))
     size, count = high * tokens, len(mine)
     sizes = [size] * count + [size, size * (count - 1)]
     split = width // 2
@@ -408,12 +405,16 @@
         split,
     )
 
-    def returned(parts):
+    def returned(parts, together):
         last = grid.last_sum(parts[:count], parts[count:])
         sums = grid.rest_sums(parts[:count], parts[count:]) + [last]
-        return grid.high_sum(grid.line_sum(sums, grid.back(sums, count - 1)))
-
-    head, tail = returned(products[: len(sizes)]), returned(products[len(sizes) :])
+        came = [grid.back(sums, place) for place in range(count // 2, count)]
+        if together:
+            came = tied(came)
+        return grid.high_sum(grid.line_sum(sums[: count // 2], came))
+
+    head = returned(products[: len(sizes)], False)
+    tail = returned(products[len(sizes) :], True)
     return (jnp.concatenate([head, tail], axis=1), attn_latent)
 
 

time: 79.4 us -> 81.6 us (1.028)
  waiting for transfers between devices: 26.4 us -> 27.6 us
  starting transfers between devices: 33.3 us -> 34.3 us
    ppermute x35, waiting for transfers between devices: 26.4 us -> 27.6 us  [swap(): return lax.ppermute(value, everyone, pairs)]
    ppermute x35, starting transfers between devices: 33.3 us -> 34.3 us  [swap(): return lax.ppermute(value, everyone, pairs)]
  transfers between devices with their start and end apart: 35 -> 35, of which waited for: 15 -> 16; matrix products, arithmetic and copies ran while one was open for 1% -> 1% of each run, Pallas kernels for 5% -> 5%
where the time goes in v16:
time: 81.6 us; the launch traced here: 81.4 us
  starting transfers between devices  34.3 us (42%)
  waiting for transfers between devices  27.6 us (34%)
  Pallas kernels  16.7 us (20%)
  other arithmetic  1.38 us (2%)
    ppermute x35, starting transfers between devices, swap(): return lax.ppermute(value, everyone, pairs)  34.3 us
    ppermute x35, waiting for transfers between devices, swap(): return lax.ppermute(value, everyone, pairs)  27.6 us
    pallas_call x1, Pallas kernels, expert(): pl.pallas_call(functools.partial(expert_kernel, len(blocks), experts, til...  11.9 us
    pallas_call x1, Pallas kernels, attention(): pl.pallas_call(attention_kernel, in_specs=[pl.BlockSpec(memory_space=pltp...  3.66 us
  transfers between devices with their start and end apart: 35, of which 16 were waited for; matrix products, arithmetic and copies ran while one was open for 1% of the time, Pallas kernels for 5%

profile of v16, /device:TPU:0, one launch (start us, length us, event | category | flops | bytes accessed | tf_op | source)
XLA Modules:
  0.0 81.4 jit_solution(5351223361665412525)
XLA Ops:
  1.6 3.1 %collective-permute-start = (bf16[8,7296]{1,0:T(8,128)(2,1)S(1)}, bf16[8,7296]{1,0:T(8,128)(2,1)S(1)}, u32[]{:S(2)}, u32[]{:S(2)}) collective-permute-start(bf16[8,7296]{1,0:T(8,128)(2,1)S(1)} %pack.1.refs_0_), channel_id=1, source_target_pairs={{0,8},{1,9},{2,10},{3,11},{4,12},{5,13},{6,14},{7,15},{8,0},{9,1},... | collective-permute-start | bytes 350216 | tf_op jit(solution)/shard_map/ppermute | solution.py:92
  4.7 2.6 %collective-permute-start.1 = (bf16[8,7296]{1,0:T(8,128)(2,1)S(1)}, bf16[8,7296]{1,0:T(8,128)(2,1)S(1)}, u32[]{:S(2)}, u32[]{:S(2)}) collective-permute-start(bf16[8,7296]{1,0:T(8,128)(2,1)S(1)} %pack.1.refs_0_), channel_id=1, source_target_pairs={{0,16},{1,17},{2,18},{3,19},{4,20},{5,21},{6,22},{7,23},{8,24},{9,... | collective-permute-start | bytes 350216 | tf_op jit(solution)/shard_map/ppermute | solution.py:92
  7.3 1.8 %collective-permute-done.refs_1_ = bf16[8,7296]{1,0:T(8,128)(2,1)S(1)} collective-permute-done((bf16[8,7296]{1,0:T(8,128)(2,1)S(1)}, bf16[8,7296]{1,0:T(8,128)(2,1)S(1)}, u32[]{:S(2)}, u32[]{:S(2)}) %collective-permute-start) | collective-permute-done | bytes 116768 | tf_op jit(solution)/shard_map/ppermute | solution.py:92
  9.2 1.9 %collective-permute-start.4 = (bf16[16,7296]{1,0:T(8,128)(2,1)S(1)}, bf16[16,7296]{1,0:T(8,128)(2,1)S(1)}, u32[]{:S(2)}, u32[]{:S(2)}) collective-permute-start(bf16[16,7296]{1,0:T(8,128)(2,1)S(1)} %join.2.refs_0_), channel_id=1, source_target_pairs={{0,4},{1,5},{2,3},{3,2},{4,0},{5,1},{6,7},{7,6},{8,12},{9,13},{10,... | collective-permute-start | bytes 700424 | tf_op jit(solution)/shard_map/ppermute | solution.py:92
  11.1 1.5 %collective-permute-start.3 = (bf16[16,7296]{1,0:T(8,128)(2,1)S(1)}, bf16[16,7296]{1,0:T(8,128)(2,1)S(1)}, u32[]{:S(2)}, u32[]{:S(2)}) collective-permute-start(bf16[16,7296]{1,0:T(8,128)(2,1)S(1)} %join.2.refs_0_), channel_id=1, source_target_pairs={{0,1},{1,0},{2,6},{3,7},{4,5},{5,4},{6,2},{7,3},{8,9},{9,8},{10,14... | collective-permute-start | bytes 700424 | tf_op jit(solution)/shard_map/ppermute | solution.py:92
  13.2 4.9 %collective-permute-done.2.refs_1_ = bf16[8,7296]{1,0:T(8,128)(2,1)S(1)} collective-permute-done((bf16[8,7296]{1,0:T(8,128)(2,1)S(1)}, bf16[8,7296]{1,0:T(8,128)(2,1)S(1)}, u32[]{:S(2)}, u32[]{:S(2)}) %collective-permute-start.2) | collective-permute-done | bytes 116768 | tf_op jit(solution)/shard_map/ppermute | solution.py:92
  19.3 1.5 %collective-permute-start.6 = (bf16[16,7296]{1,0:T(8,128)(2,1)S(1)}, bf16[16,7296]{1,0:T(8,128)(2,1)S(1)}, u32[]{:S(2)}, u32[]{:S(2)}) collective-permute-start(bf16[16,7296]{1,0:T(8,128)(2,1)S(1)} %join.3.refs_1_), channel_id=1, source_target_pairs={{0,1},{1,0},{2,6},{3,7},{4,5},{5,4},{6,2},{7,3},{8,9},{9,8},{10,14... | collective-permute-start | bytes 700424 | tf_op jit(solution)/shard_map/ppermute | solution.py:92
  22.4 3.7 %attention.1 = bf16[2,64,512]{2,1,0:T(8,128)(2,1)} custom-call(s32[2]{0:T(128)S(1)} %copy-done, bf16[2,64,512]{2,1,0:T(8,128)(2,1)} %refs_0_.3, bf16[2,64,64]{2,1,0:T(8,128)(2,1)} %refs_1_.3, bf16[2,512,512]{2,1,0:T(8,128)(2,1)} %refs_2_.3, bf16[2,64,512]{2,1,0:T(8,128)(2,1)} %refs_3_.1), custom_call_target="tpu_custom_call" | custom-call | flops 134217728 | bytes 1048576 | tf_op jit(solution)/shard_map/attention/pallas_call | solution.py:54
  26.8 1.1 %collective-permute-done.5.refs_6_ = bf16[16,7296]{1,0:T(8,128)(2,1)S(1)} collective-permute-done((bf16[16,7296]{1,0:T(8,128)(2,1)S(1)}, bf16[16,7296]{1,0:T(8,128)(2,1)S(1)}, u32[]{:S(2)}, u32[]{:S(2)}) %collective-permute-start.5) | collective-permute-done | bytes 233504 | tf_op jit(solution)/shard_map/ppermute | solution.py:92
  28.6 1.5 %collective-permute-start.11 = (bf16[8,7296]{1,0:T(8,128)(2,1)S(1)}, bf16[8,7296]{1,0:T(8,128)(2,1)S(1)}, u32[]{:S(2)}, u32[]{:S(2)}) collective-permute-start(bf16[8,7296]{1,0:T(8,128)(2,1)S(1)} %get-tuple-element.53), channel_id=1, source_target_pairs={{0,4},{1,5},{2,3},{3,2},{4,0},{5,1},{6,7},{7,6},{8,12},{9,13},{10,... | collective-permute-start | bytes 350216 | tf_op jit(solution)/shard_map/ppermute | solution.py:92
  30.6 2.3 %collective-permute-done.12.refs_8_ = bf16[8,7296]{1,0:T(8,128)(2,1)S(1)} collective-permute-done((bf16[8,7296]{1,0:T(8,128)(2,1)S(1)}, bf16[8,7296]{1,0:T(8,128)(2,1)S(1)}, u32[]{:S(2)}, u32[]{:S(2)}) %collective-permute-start.12) | collective-permute-done | bytes 116768 | tf_op jit(solution)/shard_map/ppermute | solution.py:92
  32.8 1.2 %collective-permute-done.11.refs_7_ = bf16[8,7296]{1,0:T(8,128)(2,1)S(1)} collective-permute-done((bf16[8,7296]{1,0:T(8,128)(2,1)S(1)}, bf16[8,7296]{1,0:T(8,128)(2,1)S(1)}, u32[]{:S(2)}, u32[]{:S(2)}) %collective-permute-start.11) | collective-permute-done | bytes 116768 | tf_op jit(solution)/shard_map/ppermute | solution.py:92
  34.3 1.3 %collective-permute-done.14.refs_10_ = bf16[8,7296]{1,0:T(8,128)(2,1)} collective-permute-done((bf16[8,7296]{1,0:T(8,128)(2,1)S(1)}, bf16[8,7296]{1,0:T(8,128)(2,1)}, u32[]{:S(2)}, u32[]{:S(2)}) %collective-permute-start.14) | collective-permute-done | bytes 116768 | tf_op jit(solution)/shard_map/ppermute | solution.py:92
  35.5 11.9 %expert.1 = (bf16[32,3584]{1,0:T(8,128)(2,1)S(1)}, bf16[32,3584]{1,0:T(8,128)(2,1)S(1)}, bf16[32,3584]{1,0:T(8,128)(2,1)S(1)}, bf16[32,3584]{1,0:T(8,128)(2,1)S(...) custom-call(s32[1]{0:T(128)} %bitcast.node_ref, ...), custom_call_target="tpu_custom_call" | custom-call | flops 5637144576 | bytes 22020096 | tf_op jit(solution)/shard_map/expert/pallas_call | solution.py:317
  50.0 1.3 %collective-permute-start.30 = (bf16[32,3584]{1,0:T(8,128)(2,1)S(1)}, bf16[32,3584]{1,0:T(8,128)(2,1)S(1)}, u32[]{:S(2)}, u32[]{:S(2)}) collective-permute-start(bf16[32,3584]{1,0:T(8,128)(2,1)S(1)} %add_convert_fusion.4), channel_id=1, source_target_pairs={{0,4},{1,5},{2,3},{3,2},{4,0},{5,1},{6,7},{7,6},{8,12},{9,13},{10,... | collective-permute-start | bytes 688136 | tf_op jit(solution)/shard_map/ppermute | solution.py:92
  52.3 3.0 %collective-permute-done.22 = bf16[32,3584]{1,0:T(8,128)(2,1)S(1)} collective-permute-done((bf16[32,3584]{1,0:T(8,128)(2,1)S(1)}, bf16[32,3584]{1,0:T(8,128)(2,1)S(1)}, u32[]{:S(2)}, u32[]{:S(2)}) %collective-permute-start.22) | collective-permute-done | bytes 229408 | tf_op jit(solution)/shard_map/ppermute | solution.py:92
  56.2 1.7 %collective-permute-start.23 = (bf16[32,3584]{1,0:T(8,128)(2,1)S(1)}, bf16[32,3584]{1,0:T(8,128)(2,1)S(1)}, u32[]{:S(2)}, u32[]{:S(2)}) collective-permute-start(bf16[32,3584]{1,0:T(8,128)(2,1)S(1)} %get-tuple-element.51), channel_id=1, source_target_pairs={{0,1},{1,0},{2,6},{3,7},{4,5},{5,4},{6,2},{7,3},{8,9},{9,8},{10,14... | collective-permute-start | bytes 688136 | tf_op jit(solution)/shard_map/ppermute | solution.py:92
  57.9 3.6 %collective-permute-done.28 = bf16[32,3584]{1,0:T(8,128)(2,1)S(1)} collective-permute-done((bf16[32,3584]{1,0:T(8,128)(2,1)S(1)}, bf16[32,3584]{1,0:T(8,128)(2,1)S(1)}, u32[]{:S(2)}, u32[]{:S(2)}) %collective-permute-start.28) | collective-permute-done | bytes 229408 | tf_op jit(solution)/shard_map/ppermute | solution.py:92
  61.6 3.0 %collective-permute-start.31 = (bf16[32,3584]{1,0:T(8,128)(2,1)S(1)}, bf16[32,3584]{1,0:T(8,128)(2,1)S(1)}, u32[]{:S(2)}, u32[]{:S(2)}) collective-permute-start(bf16[32,3584]{1,0:T(8,128)(2,1)S(1)} %add_convert_fusion.1), channel_id=1, source_target_pairs={{0,1},{1,0},{2,6},{3,7},{4,5},{5,4},{6,2},{7,3},{8,9},{9,8},{10,14... | collective-permute-start | bytes 688136 | tf_op jit(solution)/shard_map/ppermute | solution.py:92
  64.6 1.8 %collective-permute-done.20 = bf16[32,3584]{1,0:T(8,128)(2,1)S(1)} collective-permute-done((bf16[32,3584]{1,0:T(8,128)(2,1)S(1)}, bf16[32,3584]{1,0:T(8,128)(2,1)S(1)}, u32[]{:S(2)}, u32[]{:S(2)}) %collective-permute-start.20) | collective-permute-done | bytes 229408 | tf_op jit(solution)/shard_map/ppermute | solution.py:92
  66.9 4.2 %collective-permute-start.26 = (bf16[8,3584]{1,0:T(8,128)(2,1)S(1)}, bf16[8,3584]{1,0:T(8,128)(2,1)S(1)}, u32[]{:S(2)}, u32[]{:S(2)}) collective-permute-start(bf16[8,3584]{1,0:T(8,128)(2,1)S(1)} %get-tuple-element.55), channel_id=1, source_target_pairs={{0,24},{1,25},{2,26},{3,27},{4,28},{5,29},{6,30},{7,31},{8,16},{9,... | collective-permute-start | bytes 172040 | tf_op jit(solution)/shard_map/ppermute | solution.py:92
  71.8 3.8 %collective-permute-start.34 = (bf16[8,3584]{1,0:T(8,128)(2,1)S(1)}, bf16[8,3584]{1,0:T(8,128)(2,1)S(1)}, u32[]{:S(2)}, u32[]{:S(2)}) collective-permute-start(bf16[8,3584]{1,0:T(8,128)(2,1)S(1)} %get-tuple-element.58), channel_id=1, source_target_pairs={{0,24},{1,25},{2,26},{3,27},{4,28},{5,29},{6,30},{7,31},{8,16},{9,... | collective-permute-start | bytes 172040 | tf_op jit(solution)/shard_map/ppermute | solution.py:92
  75.7 1.8 %collective-permute-done.25 = bf16[8,3584]{1,0:T(8,128)(2,1)S(1)} collective-permute-done((bf16[8,3584]{1,0:T(8,128)(2,1)S(1)}, bf16[8,3584]{1,0:T(8,128)(2,1)S(1)}, u32[]{:S(2)}, u32[]{:S(2)}) %collective-permute-start.25) | collective-permute-done | bytes 57376 | tf_op jit(solution)/shard_map/ppermute | solution.py:92
  78.5 2.2 %collective-permute-done.33 = bf16[8,3584]{1,0:T(8,128)(2,1)S(1)} collective-permute-done((bf16[8,3584]{1,0:T(8,128)(2,1)S(1)}, bf16[8,3584]{1,0:T(8,128)(2,1)S(1)}, u32[]{:S(2)}, u32[]{:S(2)}) %collective-permute-start.33) | collective-permute-done | bytes 57376 | tf_op jit(solution)/shard_map/ppermute | solution.py:92
  (66 shorter events, 14.0 us)
Async XLA Ops:
  1.6 7.5 %collective-permute-start = (bf16[8,7296]{1,0:T(8,128)(2,1)S(1)}, bf16[8,7296]{1,0:T(8,128)(2,1)S(1)}, u32[]{:S(2)}, u32[]{:S(2)}) collective-permute-start(bf16[8,7296]{1,0:T(8,128)(2,1)S(1)} %pack.1.refs_0_), channel_id=1, source_target_pairs={{0,8},{1,9},{2,10},{3,11},{4,12},{5,13},{6,14},{7,15},{8,0},{9,1},... | collective-permute-start | bytes 350216 | tf_op jit(solution)/shard_map/ppermute | solution.py:92
  4.7 8.1 %collective-permute-start.1 = (bf16[8,7296]{1,0:T(8,128)(2,1)S(1)}, bf16[8,7296]{1,0:T(8,128)(2,1)S(1)}, u32[]{:S(2)}, u32[]{:S(2)}) collective-permute-start(bf16[8,7296]{1,0:T(8,128)(2,1)S(1)} %pack.1.refs_0_), channel_id=1, source_target_pairs={{0,16},{1,17},{2,18},{3,19},{4,20},{5,21},{6,22},{7,23},{8,24},{9,... | collective-permute-start | bytes 350216 | tf_op jit(solution)/shard_map/ppermute | solution.py:92
  9.2 9.0 %collective-permute-start.4 = (bf16[16,7296]{1,0:T(8,128)(2,1)S(1)}, bf16[16,7296]{1,0:T(8,128)(2,1)S(1)}, u32[]{:S(2)}, u32[]{:S(2)}) collective-permute-start(bf16[16,7296]{1,0:T(8,128)(2,1)S(1)} %join.2.refs_0_), channel_id=1, source_target_pairs={{0,4},{1,5},{2,3},{3,2},{4,0},{5,1},{6,7},{7,6},{8,12},{9,13},{10,... | collective-permute-start | bytes 700424 | tf_op jit(solution)/shard_map/ppermute | solution.py:92
  11.1 7.1 %collective-permute-start.3 = (bf16[16,7296]{1,0:T(8,128)(2,1)S(1)}, bf16[16,7296]{1,0:T(8,128)(2,1)S(1)}, u32[]{:S(2)}, u32[]{:S(2)}) collective-permute-start(bf16[16,7296]{1,0:T(8,128)(2,1)S(1)} %join.2.refs_0_), channel_id=1, source_target_pairs={{0,1},{1,0},{2,6},{3,7},{4,5},{5,4},{6,2},{7,3},{8,9},{9,8},{10,14... | collective-permute-start | bytes 700424 | tf_op jit(solution)/shard_map/ppermute | solution.py:92
  12.6 8.7 %collective-permute-start.8 = (bf16[16,7296]{1,0:T(8,128)(2,1)S(1)}, bf16[16,7296]{1,0:T(8,128)(2,1)S(1)}, u32[]{:S(2)}, u32[]{:S(2)}) collective-permute-start(bf16[16,7296]{1,0:T(8,128)(2,1)S(1)} %join.2.refs_0_), channel_id=1, source_target_pairs={{0,2},{1,3},{2,0},{3,1},{4,6},{5,7},{6,4},{7,5},{8,10},{9,11},{10,... | collective-permute-start | bytes 700424 | tf_op jit(solution)/shard_map/ppermute | solution.py:92
  18.2 7.9 %collective-permute-start.7 = (bf16[16,7296]{1,0:T(8,128)(2,1)S(1)}, bf16[16,7296]{1,0:T(8,128)(2,1)S(1)}, u32[]{:S(2)}, u32[]{:S(2)}) collective-permute-start(bf16[16,7296]{1,0:T(8,128)(2,1)S(1)} %join.3.refs_1_), channel_id=1, source_target_pairs={{0,4},{1,5},{2,3},{3,2},{4,0},{5,1},{6,7},{7,6},{8,12},{9,13},{10,... | collective-permute-start | bytes 700424 | tf_op jit(solution)/shard_map/ppermute | solution.py:92
  19.3 7.6 %collective-permute-start.6 = (bf16[16,7296]{1,0:T(8,128)(2,1)S(1)}, bf16[16,7296]{1,0:T(8,128)(2,1)S(1)}, u32[]{:S(2)}, u32[]{:S(2)}) collective-permute-start(bf16[16,7296]{1,0:T(8,128)(2,1)S(1)} %join.3.refs_1_), channel_id=1, source_target_pairs={{0,1},{1,0},{2,6},{3,7},{4,5},{5,4},{6,2},{7,3},{8,9},{9,8},{10,14... | collective-permute-start | bytes 700424 | tf_op jit(solution)/shard_map/ppermute | solution.py:92
  20.7 6.1 %collective-permute-start.10 = (bf16[16,7296]{1,0:T(8,128)(2,1)S(1)}, bf16[16,7296]{1,0:T(8,128)(2,1)S(1)}, u32[]{:S(2)}, u32[]{:S(2)}) collective-permute-start(bf16[16,7296]{1,0:T(8,128)(2,1)S(1)} %collective-permute-done.4.refs_4_), channel_id=1, source_target_pairs={{0,2},{1,3},{2,0},{3,1},{4,6},{5,7},{6,4},{7,5},{8,10},{9,11},{10,... | collective-permute-start | bytes 700424 | tf_op jit(solution)/shard_map/ppermute | solution.py:92
  20.8 6.1 %collective-permute-start.9 = (bf16[16,7296]{1,0:T(8,128)(2,1)S(1)}, bf16[16,7296]{1,0:T(8,128)(2,1)S(1)}, u32[]{:S(2)}, u32[]{:S(2)}) collective-permute-start(bf16[16,7296]{1,0:T(8,128)(2,1)S(1)} %collective-permute-done.3.refs_2_), channel_id=1, source_target_pairs={{0,2},{1,3},{2,0},{3,1},{4,6},{5,7},{6,4},{7,5},{8,10},{9,11},{10,... | collective-permute-start | bytes 700424 | tf_op jit(solution)/shard_map/ppermute | solution.py:92
  21.3 6.7 %collective-permute-start.5 = (bf16[16,7296]{1,0:T(8,128)(2,1)S(1)}, bf16[16,7296]{1,0:T(8,128)(2,1)S(1)}, u32[]{:S(2)}, u32[]{:S(2)}) collective-permute-start(bf16[16,7296]{1,0:T(8,128)(2,1)S(1)} %collective-permute-done.3.refs_2_), channel_id=1, source_target_pairs={{0,4},{1,5},{2,3},{3,2},{4,0},{5,1},{6,7},{7,6},{8,12},{9,13},{10,... | collective-permute-start | bytes 700424 | tf_op jit(solution)/shard_map/ppermute | solution.py:92
  28.6 5.5 %collective-permute-start.11 = (bf16[8,7296]{1,0:T(8,128)(2,1)S(1)}, bf16[8,7296]{1,0:T(8,128)(2,1)S(1)}, u32[]{:S(2)}, u32[]{:S(2)}) collective-permute-start(bf16[8,7296]{1,0:T(8,128)(2,1)S(1)} %get-tuple-element.53), channel_id=1, source_target_pairs={{0,4},{1,5},{2,3},{3,2},{4,0},{5,1},{6,7},{7,6},{8,12},{9,13},{10,... | collective-permute-start | bytes 350216 | tf_op jit(solution)/shard_map/ppermute | solution.py:92
  30.0 5.5 %collective-permute-start.18 = (bf16[16,7296]{1,0:T(8,128)(2,1)S(1)}, bf16[16,7296]{1,0:T(8,128)(2,1)S(1)}, u32[]{:S(2)}, u32[]{:S(2)}) collective-permute-start(bf16[16,7296]{1,0:T(8,128)(2,1)S(1)} %collective-permute-done.7.refs_5_), channel_id=1, source_target_pairs={{0,2},{1,3},{2,0},{3,1},{4,6},{5,7},{6,4},{7,5},{8,10},{9,11},{10,... | collective-permute-start | bytes 700424 | tf_op jit(solution)/shard_map/ppermute | solution.py:92
  48.1 7.1 %collective-permute-start.19 = (bf16[96,3584]{1,0:T(8,128)(2,1)S(1)}, bf16[96,3584]{1,0:T(8,128)(2,1)S(1)}, u32[]{:S(2)}, u32[]{:S(2)}) collective-permute-start(bf16[96,3584]{1,0:T(8,128)(2,1)S(1)} %get-tuple-element.36), channel_id=1, source_target_pairs={{0,2},{1,3},{2,0},{3,1},{4,6},{5,7},{6,4},{7,5},{8,10},{9,11},{10,... | collective-permute-start | bytes 2064392 | tf_op jit(solution)/shard_map/ppermute | solution.py:92
  49.1 6.1 %collective-permute-start.22 = (bf16[32,3584]{1,0:T(8,128)(2,1)S(1)}, bf16[32,3584]{1,0:T(8,128)(2,1)S(1)}, u32[]{:S(2)}, u32[]{:S(2)}) collective-permute-start(bf16[32,3584]{1,0:T(8,128)(2,1)S(1)} %add_convert_fusion.9), channel_id=1, source_target_pairs={{0,4},{1,5},{2,3},{3,2},{4,0},{5,1},{6,7},{7,6},{8,12},{9,13},{10,... | collective-permute-start | bytes 688136 | tf_op jit(solution)/shard_map/ppermute | solution.py:92
  50.0 7.9 %collective-permute-start.30 = (bf16[32,3584]{1,0:T(8,128)(2,1)S(1)}, bf16[32,3584]{1,0:T(8,128)(2,1)S(1)}, u32[]{:S(2)}, u32[]{:S(2)}) collective-permute-start(bf16[32,3584]{1,0:T(8,128)(2,1)S(1)} %add_convert_fusion.4), channel_id=1, source_target_pairs={{0,4},{1,5},{2,3},{3,2},{4,0},{5,1},{6,7},{7,6},{8,12},{9,13},{10,... | collective-permute-start | bytes 688136 | tf_op jit(solution)/shard_map/ppermute | solution.py:92
  51.4 10.1 %collective-permute-start.28 = (bf16[32,3584]{1,0:T(8,128)(2,1)S(1)}, bf16[32,3584]{1,0:T(8,128)(2,1)S(1)}, u32[]{:S(2)}, u32[]{:S(2)}) collective-permute-start(bf16[32,3584]{1,0:T(8,128)(2,1)S(1)} %add_convert_fusion.5), channel_id=1, source_target_pairs={{0,4},{1,5},{2,3},{3,2},{4,0},{5,1},{6,7},{7,6},{8,12},{9,13},{10,... | collective-permute-start | bytes 688136 | tf_op jit(solution)/shard_map/ppermute | solution.py:92
  55.4 11.0 %collective-permute-start.20 = (bf16[32,3584]{1,0:T(8,128)(2,1)S(1)}, bf16[32,3584]{1,0:T(8,128)(2,1)S(1)}, u32[]{:S(2)}, u32[]{:S(2)}) collective-permute-start(bf16[32,3584]{1,0:T(8,128)(2,1)S(1)} %get-tuple-element.50), channel_id=1, source_target_pairs={{0,4},{1,5},{2,3},{3,2},{4,0},{5,1},{6,7},{7,6},{8,12},{9,13},{10,... | collective-permute-start | bytes 688136 | tf_op jit(solution)/shard_map/ppermute | solution.py:92
  56.2 10.2 %collective-permute-start.23 = (bf16[32,3584]{1,0:T(8,128)(2,1)S(1)}, bf16[32,3584]{1,0:T(8,128)(2,1)S(1)}, u32[]{:S(2)}, u32[]{:S(2)}) collective-permute-start(bf16[32,3584]{1,0:T(8,128)(2,1)S(1)} %get-tuple-element.51), channel_id=1, source_target_pairs={{0,1},{1,0},{2,6},{3,7},{4,5},{5,4},{6,2},{7,3},{8,9},{9,8},{10,14... | collective-permute-start | bytes 688136 | tf_op jit(solution)/shard_map/ppermute | solution.py:92
  61.6 9.5 %collective-permute-start.31 = (bf16[32,3584]{1,0:T(8,128)(2,1)S(1)}, bf16[32,3584]{1,0:T(8,128)(2,1)S(1)}, u32[]{:S(2)}, u32[]{:S(2)}) collective-permute-start(bf16[32,3584]{1,0:T(8,128)(2,1)S(1)} %add_convert_fusion.1), channel_id=1, source_target_pairs={{0,1},{1,0},{2,6},{3,7},{4,5},{5,4},{6,2},{7,3},{8,9},{9,8},{10,14... | collective-permute-start | bytes 688136 | tf_op jit(solution)/shard_map/ppermute | solution.py:92
  66.5 9.1 %collective-permute-start.24 = (bf16[8,3584]{1,0:T(8,128)(2,1)S(1)}, bf16[8,3584]{1,0:T(8,128)(2,1)S(1)}, u32[]{:S(2)}, u32[]{:S(2)}) collective-permute-start(bf16[8,3584]{1,0:T(8,128)(2,1)S(1)} %get-tuple-element.54), channel_id=1, source_target_pairs={{0,8},{1,9},{2,10},{3,11},{4,12},{5,13},{6,14},{7,15},{8,0},{9,1},... | collective-permute-start | bytes 172040 | tf_op jit(solution)/shard_map/ppermute | solution.py:92
  66.9 8.8 %collective-permute-start.26 = (bf16[8,3584]{1,0:T(8,128)(2,1)S(1)}, bf16[8,3584]{1,0:T(8,128)(2,1)S(1)}, u32[]{:S(2)}, u32[]{:S(2)}) collective-permute-start(bf16[8,3584]{1,0:T(8,128)(2,1)S(1)} %get-tuple-element.55), channel_id=1, source_target_pairs={{0,24},{1,25},{2,26},{3,27},{4,28},{5,29},{6,30},{7,31},{8,16},{9,... | collective-permute-start | bytes 172040 | tf_op jit(solution)/shard_map/ppermute | solution.py:92
  71.0 6.5 %collective-permute-start.25 = (bf16[8,3584]{1,0:T(8,128)(2,1)S(1)}, bf16[8,3584]{1,0:T(8,128)(2,1)S(1)}, u32[]{:S(2)}, u32[]{:S(2)}) collective-permute-start(bf16[8,3584]{1,0:T(8,128)(2,1)S(1)} %get-tuple-element.56), channel_id=1, source_target_pairs={{0,16},{1,17},{2,18},{3,19},{4,20},{5,21},{6,22},{7,23},{8,24},{9,... | collective-permute-start | bytes 172040 | tf_op jit(solution)/shard_map/ppermute | solution.py:92
  71.2 6.3 %collective-permute-start.32 = (bf16[8,3584]{1,0:T(8,128)(2,1)S(1)}, bf16[8,3584]{1,0:T(8,128)(2,1)S(1)}, u32[]{:S(2)}, u32[]{:S(2)}) collective-permute-start(bf16[8,3584]{1,0:T(8,128)(2,1)S(1)} %get-tuple-element.57), channel_id=1, source_target_pairs={{0,8},{1,9},{2,10},{3,11},{4,12},{5,13},{6,14},{7,15},{8,0},{9,1},... | collective-permute-start | bytes 172040 | tf_op jit(solution)/shard_map/ppermute | solution.py:92
  71.8 6.7 %collective-permute-start.34 = (bf16[8,3584]{1,0:T(8,128)(2,1)S(1)}, bf16[8,3584]{1,0:T(8,128)(2,1)S(1)}, u32[]{:S(2)}, u32[]{:S(2)}) collective-permute-start(bf16[8,3584]{1,0:T(8,128)(2,1)S(1)} %get-tuple-element.58), channel_id=1, source_target_pairs={{0,24},{1,25},{2,26},{3,27},{4,28},{5,29},{6,30},{7,31},{8,16},{9,... | collective-permute-start | bytes 172040 | tf_op jit(solution)/shard_map/ppermute | solution.py:92
  (12 other events, 40.8 us)

commit v17 on v15

--- a/solution.py
+++ b/solution.py
@@ -248,16 +248,6 @@
         start += size
 
 
-def fetch_columns(source, target, sems):
-    columns = target.shape[1] // sems.shape[0]
-    copies = []
-    for k in range(sems.shape[0]):
-        part = pl.ds(k * columns, columns)
-        copies.append(pltpu.make_async_copy(source.at[:, part], target.at[:, part], sems.at[k]))
-        copies[-1].start()
-    return copies
-
-
 def fetch_both(gate_hbm, up_hbm, gate, up, gate_sem, up_sem, tile):
     copies = []
     for k in range(0, gate.shape[0], tile):
@@ -287,11 +277,10 @@
 
 def expert_kernel(count, experts, tile, down_tile, split, node_ref, *refs):
     blocks = refs[:count]
-    gate_hbm, up_hbm, down_hbm = refs[count : count + 3]
-    outs = refs[count + 3 : -10]
-    hidden_ref, share_ref, gate, up, down, gate_sum, up_sum, gate_sem, up_sem, down_sem = refs[-10:]
+    gate_hbm, up_hbm, down = refs[count : count + 3]
+    outs = refs[count + 3 : -8]
+    hidden_ref, share_ref, gate, up, gate_sum, up_sum, gate_sem, up_sem = refs[-8:]
     copies = fetch_both(gate_hbm, up_hbm, gate, up, gate_sem, up_sem, tile)
-    down_copies = fetch_columns(down_hbm, down, down_sem)
 
     table = jnp.concatenate([block[:, gate.shape[0] :] for block in blocks], axis=0)
     table = table.astype(jnp.float32)
@@ -301,10 +290,7 @@
     share_ref[...] = jnp.broadcast_to(share, share_ref.shape)
     project(blocks, copies, gate, up, gate_sum, up_sum, tile)
     hidden_ref[...] = (jax.nn.silu(gate_sum[...]) * up_sum[...]).astype(jnp.bfloat16)
-    wide = down.shape[1] // len(down_copies)
     for k in range(0, down.shape[1], down_tile):
-        if k % wide == 0:
-            down_copies[k // wide].wait()
         product = jnp.dot(
             hidden_ref[...], down[:, pl.ds(k, down_tile)], preferred_element_type=jnp.float32
         )
@@ -323,7 +309,8 @@
         functools.partial(expert_kernel, len(blocks), experts, tile, down_tile, split),
         in_specs=[pl.BlockSpec(memory_space=pltpu.SMEM)]
         + [pl.BlockSpec(memory_space=pltpu.VMEM)] * len(blocks)
-        + [pl.BlockSpec(memory_space=pltpu.HBM)] * 3,
+        + [pl.BlockSpec(memory_space=pltpu.HBM)] * 2
+        + [pl.BlockSpec(memory_space=pltpu.VMEM)],
         out_specs=[pl.BlockSpec(memory_space=pltpu.VMEM)] * (2 * len(sizes)),
         out_shape=[
             jax.ShapeDtypeStruct((size, chunk), jnp.bfloat16)
@@ -335,21 +322,19 @@
             pltpu.VMEM((rows, 128), jnp.float32),
             pltpu.VMEM((width, units), jnp.bfloat16),
             pltpu.VMEM((width, units), jnp.bfloat16),
-            pltpu.VMEM((units, width), jnp.bfloat16),
             pltpu.VMEM((rows, units), jnp.float32),
             pltpu.VMEM((rows, units), jnp.float32),
             pltpu.SemaphoreType.DMA((width // tile,)),
             pltpu.SemaphoreType.DMA((width // tile,)),
-            pltpu.SemaphoreType.DMA((width // (2 * down_tile),)),
         ],
         cost_estimate=pl.CostEstimate(
             flops=6 * rows * width * units,
             bytes_accessed=6 * units * width,
             transcendentals=rows * units,
         ),
-        compiler_params=pltpu.CompilerParams(vmem_limit_bytes=32 * MEBI),
+        compiler_params=pltpu.CompilerParams(vmem_limit_bytes=24 * MEBI),
         name="expert",
-    )(node, *blocks, in_hbm(w_gate), in_hbm(w_up), in_hbm(w_down))
+    )(node, *blocks, in_hbm(w_gate), in_hbm(w_up), w_down)
 
 
 def body(

time: 79.4 us -> 79.9 us (level)
  local copies, waits for them, and re-layouts: 0.7 us -> 3.78 us
  Pallas kernels: 16.7 us -> 14.1 us
    unnamed x2 -> x4, local copies, waits for them, and re-layouts: 0.65 us -> 3.73 us
    pallas_call x1, Pallas kernels: 11.9 us -> 9.36 us  [expert(): pl.pallas_call(functools.partial(expert_kernel, len(blocks), experts, til...]
where the time goes in v17:
time: 79.9 us; the launch traced here: 79.7 us
  starting transfers between devices  33.3 us (42%)
  waiting for transfers between devices  26.4 us (33%)
  Pallas kernels  14.1 us (18%)
  local copies, waits for them, and re-layouts  3.78 us (5%)
  other arithmetic  1.35 us (2%)
    ppermute x35, starting transfers between devices, swap(): return lax.ppermute(value, everyone, pairs)  33.3 us
    ppermute x35, waiting for transfers between devices, swap(): return lax.ppermute(value, everyone, pairs)  26.4 us
    pallas_call x1, Pallas kernels, expert(): pl.pallas_call(functools.partial(expert_kernel, len(blocks), experts, til...  9.36 us
    unnamed x4, local copies, waits for them, and re-layouts  3.73 us
    pallas_call x1, Pallas kernels, attention(): pl.pallas_call(attention_kernel, in_specs=[pl.BlockSpec(memory_space=pltp...  3.66 us
  transfers between devices with their start and end apart: 35, of which 15 were waited for; matrix products, arithmetic and copies ran while one was open for 1% of the time, Pallas kernels for 5%

profile of v17, /device:TPU:0, one launch (start us, length us, event | category | flops | bytes accessed | tf_op | source)
XLA Modules:
  0.0 79.7 jit_solution(4443515818291135143)
XLA Ops:
  1.6 3.1 %collective-permute-start = (bf16[8,7296]{1,0:T(8,128)(2,1)S(1)}, bf16[8,7296]{1,0:T(8,128)(2,1)S(1)}, u32[]{:S(2)}, u32[]{:S(2)}) collective-permute-start(bf16[8,7296]{1,0:T(8,128)(2,1)S(1)} %pack.1.refs_0_), channel_id=1, source_target_pairs={{0,8},{1,9},{2,10},{3,11},{4,12},{5,13},{6,14},{7,15},{8,0},{9,1},... | collective-permute-start | bytes 350216 | tf_op jit(solution)/shard_map/ppermute | solution.py:92
  4.7 2.6 %collective-permute-start.1 = (bf16[8,7296]{1,0:T(8,128)(2,1)S(1)}, bf16[8,7296]{1,0:T(8,128)(2,1)S(1)}, u32[]{:S(2)}, u32[]{:S(2)}) collective-permute-start(bf16[8,7296]{1,0:T(8,128)(2,1)S(1)} %pack.1.refs_0_), channel_id=1, source_target_pairs={{0,16},{1,17},{2,18},{3,19},{4,20},{5,21},{6,22},{7,23},{8,24},{9,... | collective-permute-start | bytes 350216 | tf_op jit(solution)/shard_map/ppermute | solution.py:92
  7.3 1.8 %collective-permute-done.refs_1_ = bf16[8,7296]{1,0:T(8,128)(2,1)S(1)} collective-permute-done((bf16[8,7296]{1,0:T(8,128)(2,1)S(1)}, bf16[8,7296]{1,0:T(8,128)(2,1)S(1)}, u32[]{:S(2)}, u32[]{:S(2)}) %collective-permute-start) | collective-permute-done | bytes 116768 | tf_op jit(solution)/shard_map/ppermute | solution.py:92
  9.2 1.9 %collective-permute-start.4 = (bf16[16,7296]{1,0:T(8,128)(2,1)S(1)}, bf16[16,7296]{1,0:T(8,128)(2,1)S(1)}, u32[]{:S(2)}, u32[]{:S(2)}) collective-permute-start(bf16[16,7296]{1,0:T(8,128)(2,1)S(1)} %join.2.refs_0_), channel_id=1, source_target_pairs={{0,4},{1,5},{2,3},{3,2},{4,0},{5,1},{6,7},{7,6},{8,12},{9,13},{10,... | collective-permute-start | bytes 700424 | tf_op jit(solution)/shard_map/ppermute | solution.py:92
  11.1 1.5 %collective-permute-start.3 = (bf16[16,7296]{1,0:T(8,128)(2,1)S(1)}, bf16[16,7296]{1,0:T(8,128)(2,1)S(1)}, u32[]{:S(2)}, u32[]{:S(2)}) collective-permute-start(bf16[16,7296]{1,0:T(8,128)(2,1)S(1)} %join.2.refs_0_), channel_id=1, source_target_pairs={{0,1},{1,0},{2,6},{3,7},{4,5},{5,4},{6,2},{7,3},{8,9},{9,8},{10,14... | collective-permute-start | bytes 700424 | tf_op jit(solution)/shard_map/ppermute | solution.py:92
  13.2 4.4 %collective-permute-done.2.refs_1_ = bf16[8,7296]{1,0:T(8,128)(2,1)S(1)} collective-permute-done((bf16[8,7296]{1,0:T(8,128)(2,1)S(1)}, bf16[8,7296]{1,0:T(8,128)(2,1)S(1)}, u32[]{:S(2)}, u32[]{:S(2)}) %collective-permute-start.2) | collective-permute-done | bytes 116768 | tf_op jit(solution)/shard_map/ppermute | solution.py:92
  17.7 1.6 %collective-permute-start.7 = (bf16[16,7296]{1,0:T(8,128)(2,1)S(1)}, bf16[16,7296]{1,0:T(8,128)(2,1)S(1)}, u32[]{:S(2)}, u32[]{:S(2)}) collective-permute-start(bf16[16,7296]{1,0:T(8,128)(2,1)S(1)} %join.3.refs_1_), channel_id=1, source_target_pairs={{0,4},{1,5},{2,3},{3,2},{4,0},{5,1},{6,7},{7,6},{8,12},{9,13},{10,... | collective-permute-start | bytes 700424 | tf_op jit(solution)/shard_map/ppermute | solution.py:92
  19.3 1.5 %collective-permute-start.6 = (bf16[16,7296]{1,0:T(8,128)(2,1)S(1)}, bf16[16,7296]{1,0:T(8,128)(2,1)S(1)}, u32[]{:S(2)}, u32[]{:S(2)}) collective-permute-start(bf16[16,7296]{1,0:T(8,128)(2,1)S(1)} %join.3.refs_1_), channel_id=1, source_target_pairs={{0,1},{1,0},{2,6},{3,7},{4,5},{5,4},{6,2},{7,3},{8,9},{9,8},{10,14... | collective-permute-start | bytes 700424 | tf_op jit(solution)/shard_map/ppermute | solution.py:92
  21.9 3.7 %attention.1 = bf16[2,64,512]{2,1,0:T(8,128)(2,1)} custom-call(s32[2]{0:T(128)S(1)} %copy-done.1, bf16[2,64,512]{2,1,0:T(8,128)(2,1)} %refs_0_.3, bf16[2,64,64]{2,1,0:T(8,128)(2,1)} %refs_1_.3, bf16[2,512,512]{2,1,0:T(8,128)(2,1)} %refs_2_.3, bf16[2,64,512]{2,1,0:T(8,128)(2,1)} %refs_3_.1), custom_call_target="tpu_custom_call" | custom-call | flops 134217728 | bytes 1048576 | tf_op jit(solution)/shard_map/attention/pallas_call | solution.py:54
  26.8 1.4 %collective-permute-start.9 = (bf16[8,7296]{1,0:T(8,128)(2,1)S(1)}, bf16[8,7296]{1,0:T(8,128)(2,1)S(1)}, u32[]{:S(2)}, u32[]{:S(2)}) collective-permute-start(bf16[8,7296]{1,0:T(8,128)(2,1)S(1)} %get-tuple-element.44), channel_id=1, source_target_pairs={{0,4},{1,5},{2,3},{3,2},{4,0},{5,1},{6,7},{7,6},{8,12},{9,13},{10,... | collective-permute-start | bytes 350216 | tf_op jit(solution)/shard_map/ppermute | solution.py:92
  29.5 2.2 %collective-permute-done.9.refs_8_ = bf16[8,7296]{1,0:T(8,128)(2,1)S(1)} collective-permute-done((bf16[8,7296]{1,0:T(8,128)(2,1)S(1)}, bf16[8,7296]{1,0:T(8,128)(2,1)S(1)}, u32[]{:S(2)}, u32[]{:S(2)}) %collective-permute-start.9) | collective-permute-done | bytes 116768 | tf_op jit(solution)/shard_map/ppermute | solution.py:92
  31.7 1.4 %collective-permute-done.8.refs_7_ = bf16[8,7296]{1,0:T(8,128)(2,1)S(1)} collective-permute-done((bf16[8,7296]{1,0:T(8,128)(2,1)S(1)}, bf16[8,7296]{1,0:T(8,128)(2,1)S(1)}, u32[]{:S(2)}, u32[]{:S(2)}) %collective-permute-start.8) | collective-permute-done | bytes 116768 | tf_op jit(solution)/shard_map/ppermute | solution.py:92
  33.2 1.4 %collective-permute-done.11.refs_10_ = bf16[8,7296]{1,0:T(8,128)(2,1)} collective-permute-done((bf16[8,7296]{1,0:T(8,128)(2,1)S(1)}, bf16[8,7296]{1,0:T(8,128)(2,1)}, u32[]{:S(2)}, u32[]{:S(2)}) %collective-permute-start.11) | collective-permute-done | bytes 116768 | tf_op jit(solution)/shard_map/ppermute | solution.py:92
  34.6 3.1 %copy-done = bf16[1,512,7168]{2,1,0:T(8,128)(2,1)S(1)} copy-done((bf16[1,512,7168]{2,1,0:T(8,128)(2,1)S(1)}, bf16[1,512,7168]{2,1,0:T(8,128)(2,1)}, u32[]{:S(2)}) %copy-start) | copy-done | bytes 7340056
  37.7 9.4 %expert.1 = (bf16[32,3584]{1,0:T(8,128)(2,1)S(1)}, bf16[32,3584]{1,0:T(8,128)(2,1)S(1)}, bf16[32,3584]{1,0:T(8,128)(2,1)S(1)}, bf16[32,3584]{1,0:T(8,128)(2,1)S(...) custom-call(s32[1]{0:T(128)} %bitcast.node_ref, ...), custom_call_target="tpu_custom_call" | custom-call | flops 5637144576 | bytes 22020096 | tf_op jit(solution)/shard_map/expert/pallas_call | solution.py:308
  48.6 1.3 %collective-permute-start.22 = (bf16[32,3584]{1,0:T(8,128)(2,1)S(1)}, bf16[32,3584]{1,0:T(8,128)(2,1)S(1)}, u32[]{:S(2)}, u32[]{:S(2)}) collective-permute-start(bf16[32,3584]{1,0:T(8,128)(2,1)S(1)} %add_convert_fusion.9), channel_id=1, source_target_pairs={{0,4},{1,5},{2,3},{3,2},{4,0},{5,1},{6,7},{7,6},{8,12},{9,13},{10,... | collective-permute-start | bytes 688136 | tf_op jit(solution)/shard_map/ppermute | solution.py:92
  50.9 3.9 %collective-permute-done.22 = bf16[32,3584]{1,0:T(8,128)(2,1)S(1)} collective-permute-done((bf16[32,3584]{1,0:T(8,128)(2,1)S(1)}, bf16[32,3584]{1,0:T(8,128)(2,1)S(1)}, u32[]{:S(2)}, u32[]{:S(2)}) %collective-permute-start.22) | collective-permute-done | bytes 229408 | tf_op jit(solution)/shard_map/ppermute | solution.py:92
  54.9 1.3 %collective-permute-start.20 = (bf16[32,3584]{1,0:T(8,128)(2,1)S(1)}, bf16[32,3584]{1,0:T(8,128)(2,1)S(1)}, u32[]{:S(2)}, u32[]{:S(2)}) collective-permute-start(bf16[32,3584]{1,0:T(8,128)(2,1)S(1)} %get-tuple-element.40), channel_id=1, source_target_pairs={{0,4},{1,5},{2,3},{3,2},{4,0},{5,1},{6,7},{7,6},{8,12},{9,13},{10,... | collective-permute-start | bytes 688136 | tf_op jit(solution)/shard_map/ppermute | solution.py:92
  57.4 1.2 %collective-permute-start.28 = (bf16[32,3584]{1,0:T(8,128)(2,1)S(1)}, bf16[32,3584]{1,0:T(8,128)(2,1)S(1)}, u32[]{:S(2)}, u32[]{:S(2)}) collective-permute-start(bf16[32,3584]{1,0:T(8,128)(2,1)S(1)} %get-tuple-element.42), channel_id=1, source_target_pairs={{0,4},{1,5},{2,3},{3,2},{4,0},{5,1},{6,7},{7,6},{8,12},{9,13},{10,... | collective-permute-start | bytes 688136 | tf_op jit(solution)/shard_map/ppermute | solution.py:92
  59.8 3.6 %collective-permute-done.20 = bf16[32,3584]{1,0:T(8,128)(2,1)S(1)} collective-permute-done((bf16[32,3584]{1,0:T(8,128)(2,1)S(1)}, bf16[32,3584]{1,0:T(8,128)(2,1)S(1)}, u32[]{:S(2)}, u32[]{:S(2)}) %collective-permute-start.20) | collective-permute-done | bytes 229408 | tf_op jit(solution)/shard_map/ppermute | solution.py:92
  65.2 3.2 %collective-permute-start.26 = (bf16[8,3584]{1,0:T(8,128)(2,1)S(1)}, bf16[8,3584]{1,0:T(8,128)(2,1)S(1)}, u32[]{:S(2)}, u32[]{:S(2)}) collective-permute-start(bf16[8,3584]{1,0:T(8,128)(2,1)S(1)} %get-tuple-element.47), channel_id=1, source_target_pairs={{0,24},{1,25},{2,26},{3,27},{4,28},{5,29},{6,30},{7,31},{8,16},{9,... | collective-permute-start | bytes 172040 | tf_op jit(solution)/shard_map/ppermute | solution.py:92
  69.8 3.2 %collective-permute-start.34 = (bf16[8,3584]{1,0:T(8,128)(2,1)S(1)}, bf16[8,3584]{1,0:T(8,128)(2,1)S(1)}, u32[]{:S(2)}, u32[]{:S(2)}) collective-permute-start(bf16[8,3584]{1,0:T(8,128)(2,1)S(1)} %get-tuple-element.50), channel_id=1, source_target_pairs={{0,24},{1,25},{2,26},{3,27},{4,28},{5,29},{6,30},{7,31},{8,16},{9,... | collective-permute-start | bytes 172040 | tf_op jit(solution)/shard_map/ppermute | solution.py:92
  73.0 2.2 %collective-permute-done.25 = bf16[8,3584]{1,0:T(8,128)(2,1)S(1)} collective-permute-done((bf16[8,3584]{1,0:T(8,128)(2,1)S(1)}, bf16[8,3584]{1,0:T(8,128)(2,1)S(1)}, u32[]{:S(2)}, u32[]{:S(2)}) %collective-permute-start.25) | collective-permute-done | bytes 57376 | tf_op jit(solution)/shard_map/ppermute | solution.py:92
  76.3 2.7 %collective-permute-done.33 = bf16[8,3584]{1,0:T(8,128)(2,1)S(1)} collective-permute-done((bf16[8,3584]{1,0:T(8,128)(2,1)S(1)}, bf16[8,3584]{1,0:T(8,128)(2,1)S(1)}, u32[]{:S(2)}, u32[]{:S(2)}) %collective-permute-start.33) | collective-permute-done | bytes 57376 | tf_op jit(solution)/shard_map/ppermute | solution.py:92
  (67 shorter events, 15.6 us)
Async XLA Ops:
  1.6 7.5 %collective-permute-start = (bf16[8,7296]{1,0:T(8,128)(2,1)S(1)}, bf16[8,7296]{1,0:T(8,128)(2,1)S(1)}, u32[]{:S(2)}, u32[]{:S(2)}) collective-permute-start(bf16[8,7296]{1,0:T(8,128)(2,1)S(1)} %pack.1.refs_0_), channel_id=1, source_target_pairs={{0,8},{1,9},{2,10},{3,11},{4,12},{5,13},{6,14},{7,15},{8,0},{9,1},... | collective-permute-start | bytes 350216 | tf_op jit(solution)/shard_map/ppermute | solution.py:92
  4.7 8.1 %collective-permute-start.1 = (bf16[8,7296]{1,0:T(8,128)(2,1)S(1)}, bf16[8,7296]{1,0:T(8,128)(2,1)S(1)}, u32[]{:S(2)}, u32[]{:S(2)}) collective-permute-start(bf16[8,7296]{1,0:T(8,128)(2,1)S(1)} %pack.1.refs_0_), channel_id=1, source_target_pairs={{0,16},{1,17},{2,18},{3,19},{4,20},{5,21},{6,22},{7,23},{8,24},{9,... | collective-permute-start | bytes 350216 | tf_op jit(solution)/shard_map/ppermute | solution.py:92
  9.2 8.5 %collective-permute-start.4 = (bf16[16,7296]{1,0:T(8,128)(2,1)S(1)}, bf16[16,7296]{1,0:T(8,128)(2,1)S(1)}, u32[]{:S(2)}, u32[]{:S(2)}) collective-permute-start(bf16[16,7296]{1,0:T(8,128)(2,1)S(1)} %join.2.refs_0_), channel_id=1, source_target_pairs={{0,4},{1,5},{2,3},{3,2},{4,0},{5,1},{6,7},{7,6},{8,12},{9,13},{10,... | collective-permute-start | bytes 700424 | tf_op jit(solution)/shard_map/ppermute | solution.py:92
  11.1 6.6 %collective-permute-start.3 = (bf16[16,7296]{1,0:T(8,128)(2,1)S(1)}, bf16[16,7296]{1,0:T(8,128)(2,1)S(1)}, u32[]{:S(2)}, u32[]{:S(2)}) collective-permute-start(bf16[16,7296]{1,0:T(8,128)(2,1)S(1)} %join.2.refs_0_), channel_id=1, source_target_pairs={{0,1},{1,0},{2,6},{3,7},{4,5},{5,4},{6,2},{7,3},{8,9},{9,8},{10,14... | collective-permute-start | bytes 700424 | tf_op jit(solution)/shard_map/ppermute | solution.py:92
  17.7 8.5 %collective-permute-start.7 = (bf16[16,7296]{1,0:T(8,128)(2,1)S(1)}, bf16[16,7296]{1,0:T(8,128)(2,1)S(1)}, u32[]{:S(2)}, u32[]{:S(2)}) collective-permute-start(bf16[16,7296]{1,0:T(8,128)(2,1)S(1)} %join.3.refs_1_), channel_id=1, source_target_pairs={{0,4},{1,5},{2,3},{3,2},{4,0},{5,1},{6,7},{7,6},{8,12},{9,13},{10,... | collective-permute-start | bytes 700424 | tf_op jit(solution)/shard_map/ppermute | solution.py:92
  19.3 7.0 %collective-permute-start.6 = (bf16[16,7296]{1,0:T(8,128)(2,1)S(1)}, bf16[16,7296]{1,0:T(8,128)(2,1)S(1)}, u32[]{:S(2)}, u32[]{:S(2)}) collective-permute-start(bf16[16,7296]{1,0:T(8,128)(2,1)S(1)} %join.3.refs_1_), channel_id=1, source_target_pairs={{0,1},{1,0},{2,6},{3,7},{4,5},{5,4},{6,2},{7,3},{8,9},{9,8},{10,14... | collective-permute-start | bytes 700424 | tf_op jit(solution)/shard_map/ppermute | solution.py:92
  20.7 6.1 %collective-permute-start.5 = (bf16[16,7296]{1,0:T(8,128)(2,1)S(1)}, bf16[16,7296]{1,0:T(8,128)(2,1)S(1)}, u32[]{:S(2)}, u32[]{:S(2)}) collective-permute-start(bf16[16,7296]{1,0:T(8,128)(2,1)S(1)} %collective-permute-done.3.refs_2_), channel_id=1, source_target_pairs={{0,4},{1,5},{2,3},{3,2},{4,0},{5,1},{6,7},{7,6},{8,12},{9,13},{10,... | collective-permute-start | bytes 700424 | tf_op jit(solution)/shard_map/ppermute | solution.py:92
  28.9 5.6 %collective-permute-start.18 = (bf16[16,7296]{1,0:T(8,128)(2,1)S(1)}, bf16[16,7296]{1,0:T(8,128)(2,1)S(1)}, u32[]{:S(2)}, u32[]{:S(2)}) collective-permute-start(bf16[16,7296]{1,0:T(8,128)(2,1)S(1)} %collective-permute-done.7.refs_5_), channel_id=1, source_target_pairs={{0,2},{1,3},{2,0},{3,1},{4,6},{5,7},{6,4},{7,5},{8,10},{9,11},{10,... | collective-permute-start | bytes 700424 | tf_op jit(solution)/shard_map/ppermute | solution.py:92
  28.9 5.6 %collective-permute-start.10 = (bf16[16,7296]{1,0:T(8,128)(2,1)S(1)}, bf16[16,7296]{1,0:T(8,128)(2,1)S(1)}, u32[]{:S(2)}, u32[]{:S(2)}) collective-permute-start(bf16[16,7296]{1,0:T(8,128)(2,1)S(1)} %collective-permute-done.5.refs_6_), channel_id=1, source_target_pairs={{0,2},{1,3},{2,0},{3,1},{4,6},{5,7},{6,4},{7,5},{8,10},{9,11},{10,... | collective-permute-start | bytes 700424 | tf_op jit(solution)/shard_map/ppermute | solution.py:92
  29.5 5.1 %collective-permute-start.16 = (bf16[16,7296]{1,0:T(8,128)(2,1)S(1)}, bf16[16,7296]{1,0:T(8,128)(2,1)S(1)}, u32[]{:S(2)}, u32[]{:S(2)}) collective-permute-start(bf16[16,7296]{1,0:T(8,128)(2,1)S(1)} %collective-permute-done.6.refs_3_), channel_id=1, source_target_pairs={{0,2},{1,3},{2,0},{3,1},{4,6},{5,7},{6,4},{7,5},{8,10},{9,11},{10,... | collective-permute-start | bytes 700424 | tf_op jit(solution)/shard_map/ppermute | solution.py:92
  47.6 7.1 %collective-permute-start.19 = (bf16[96,3584]{1,0:T(8,128)(2,1)S(1)}, bf16[96,3584]{1,0:T(8,128)(2,1)S(1)}, u32[]{:S(2)}, u32[]{:S(2)}) collective-permute-start(bf16[96,3584]{1,0:T(8,128)(2,1)S(1)} %get-tuple-element.28), channel_id=1, source_target_pairs={{0,2},{1,3},{2,0},{3,1},{4,6},{5,7},{6,4},{7,5},{8,10},{9,11},{10,... | collective-permute-start | bytes 2064392 | tf_op jit(solution)/shard_map/ppermute | solution.py:92
  47.7 9.6 %collective-permute-start.27 = (bf16[96,3584]{1,0:T(8,128)(2,1)S(1)}, bf16[96,3584]{1,0:T(8,128)(2,1)S(1)}, u32[]{:S(2)}, u32[]{:S(2)}) collective-permute-start(bf16[96,3584]{1,0:T(8,128)(2,1)S(1)} %get-tuple-element.34), channel_id=1, source_target_pairs={{0,2},{1,3},{2,0},{3,1},{4,6},{5,7},{6,4},{7,5},{8,10},{9,11},{10,... | collective-permute-start | bytes 2064392 | tf_op jit(solution)/shard_map/ppermute | solution.py:92
  48.6 6.1 %collective-permute-start.22 = (bf16[32,3584]{1,0:T(8,128)(2,1)S(1)}, bf16[32,3584]{1,0:T(8,128)(2,1)S(1)}, u32[]{:S(2)}, u32[]{:S(2)}) collective-permute-start(bf16[32,3584]{1,0:T(8,128)(2,1)S(1)} %add_convert_fusion.9), channel_id=1, source_target_pairs={{0,4},{1,5},{2,3},{3,2},{4,0},{5,1},{6,7},{7,6},{8,12},{9,13},{10,... | collective-permute-start | bytes 688136 | tf_op jit(solution)/shard_map/ppermute | solution.py:92
  50.0 7.3 %collective-permute-start.30 = (bf16[32,3584]{1,0:T(8,128)(2,1)S(1)}, bf16[32,3584]{1,0:T(8,128)(2,1)S(1)}, u32[]{:S(2)}, u32[]{:S(2)}) collective-permute-start(bf16[32,3584]{1,0:T(8,128)(2,1)S(1)} %add_convert_fusion.2), channel_id=1, source_target_pairs={{0,4},{1,5},{2,3},{3,2},{4,0},{5,1},{6,7},{7,6},{8,12},{9,13},{10,... | collective-permute-start | bytes 688136 | tf_op jit(solution)/shard_map/ppermute | solution.py:92
  54.9 8.5 %collective-permute-start.20 = (bf16[32,3584]{1,0:T(8,128)(2,1)S(1)}, bf16[32,3584]{1,0:T(8,128)(2,1)S(1)}, u32[]{:S(2)}, u32[]{:S(2)}) collective-permute-start(bf16[32,3584]{1,0:T(8,128)(2,1)S(1)} %get-tuple-element.40), channel_id=1, source_target_pairs={{0,4},{1,5},{2,3},{3,2},{4,0},{5,1},{6,7},{7,6},{8,12},{9,13},{10,... | collective-permute-start | bytes 688136 | tf_op jit(solution)/shard_map/ppermute | solution.py:92
  56.2 8.0 %collective-permute-start.23 = (bf16[32,3584]{1,0:T(8,128)(2,1)S(1)}, bf16[32,3584]{1,0:T(8,128)(2,1)S(1)}, u32[]{:S(2)}, u32[]{:S(2)}) collective-permute-start(bf16[32,3584]{1,0:T(8,128)(2,1)S(1)} %get-tuple-element.41), channel_id=1, source_target_pairs={{0,1},{1,0},{2,6},{3,7},{4,5},{5,4},{6,2},{7,3},{8,9},{9,8},{10,14... | collective-permute-start | bytes 688136 | tf_op jit(solution)/shard_map/ppermute | solution.py:92
  57.4 11.4 %collective-permute-start.28 = (bf16[32,3584]{1,0:T(8,128)(2,1)S(1)}, bf16[32,3584]{1,0:T(8,128)(2,1)S(1)}, u32[]{:S(2)}, u32[]{:S(2)}) collective-permute-start(bf16[32,3584]{1,0:T(8,128)(2,1)S(1)} %get-tuple-element.42), channel_id=1, source_target_pairs={{0,4},{1,5},{2,3},{3,2},{4,0},{5,1},{6,7},{7,6},{8,12},{9,13},{10,... | collective-permute-start | bytes 688136 | tf_op jit(solution)/shard_map/ppermute | solution.py:92
  58.6 10.2 %collective-permute-start.31 = (bf16[32,3584]{1,0:T(8,128)(2,1)S(1)}, bf16[32,3584]{1,0:T(8,128)(2,1)S(1)}, u32[]{:S(2)}, u32[]{:S(2)}) collective-permute-start(bf16[32,3584]{1,0:T(8,128)(2,1)S(1)} %get-tuple-element.43), channel_id=1, source_target_pairs={{0,1},{1,0},{2,6},{3,7},{4,5},{5,4},{6,2},{7,3},{8,9},{9,8},{10,14... | collective-permute-start | bytes 688136 | tf_op jit(solution)/shard_map/ppermute | solution.py:92
  64.3 8.6 %collective-permute-start.24 = (bf16[8,3584]{1,0:T(8,128)(2,1)S(1)}, bf16[8,3584]{1,0:T(8,128)(2,1)S(1)}, u32[]{:S(2)}, u32[]{:S(2)}) collective-permute-start(bf16[8,3584]{1,0:T(8,128)(2,1)S(1)} %get-tuple-element.46), channel_id=1, source_target_pairs={{0,8},{1,9},{2,10},{3,11},{4,12},{5,13},{6,14},{7,15},{8,0},{9,1},... | collective-permute-start | bytes 172040 | tf_op jit(solution)/shard_map/ppermute | solution.py:92
  65.2 7.8 %collective-permute-start.26 = (bf16[8,3584]{1,0:T(8,128)(2,1)S(1)}, bf16[8,3584]{1,0:T(8,128)(2,1)S(1)}, u32[]{:S(2)}, u32[]{:S(2)}) collective-permute-start(bf16[8,3584]{1,0:T(8,128)(2,1)S(1)} %get-tuple-element.47), channel_id=1, source_target_pairs={{0,24},{1,25},{2,26},{3,27},{4,28},{5,29},{6,30},{7,31},{8,16},{9,... | collective-permute-start | bytes 172040 | tf_op jit(solution)/shard_map/ppermute | solution.py:92
  68.4 6.8 %collective-permute-start.25 = (bf16[8,3584]{1,0:T(8,128)(2,1)S(1)}, bf16[8,3584]{1,0:T(8,128)(2,1)S(1)}, u32[]{:S(2)}, u32[]{:S(2)}) collective-permute-start(bf16[8,3584]{1,0:T(8,128)(2,1)S(1)} %get-tuple-element.48), channel_id=1, source_target_pairs={{0,16},{1,17},{2,18},{3,19},{4,20},{5,21},{6,22},{7,23},{8,24},{9,... | collective-permute-start | bytes 172040 | tf_op jit(solution)/shard_map/ppermute | solution.py:92
  69.0 6.2 %collective-permute-start.32 = (bf16[8,3584]{1,0:T(8,128)(2,1)S(1)}, bf16[8,3584]{1,0:T(8,128)(2,1)S(1)}, u32[]{:S(2)}, u32[]{:S(2)}) collective-permute-start(bf16[8,3584]{1,0:T(8,128)(2,1)S(1)} %get-tuple-element.49), channel_id=1, source_target_pairs={{0,8},{1,9},{2,10},{3,11},{4,12},{5,13},{6,14},{7,15},{8,0},{9,1},... | collective-permute-start | bytes 172040 | tf_op jit(solution)/shard_map/ppermute | solution.py:92
  69.8 6.5 %collective-permute-start.34 = (bf16[8,3584]{1,0:T(8,128)(2,1)S(1)}, bf16[8,3584]{1,0:T(8,128)(2,1)S(1)}, u32[]{:S(2)}, u32[]{:S(2)}) collective-permute-start(bf16[8,3584]{1,0:T(8,128)(2,1)S(1)} %get-tuple-element.50), channel_id=1, source_target_pairs={{0,24},{1,25},{2,26},{3,27},{4,28},{5,29},{6,30},{7,31},{8,16},{9,... | collective-permute-start | bytes 172040 | tf_op jit(solution)/shard_map/ppermute | solution.py:92
  73.0 6.0 %collective-permute-start.33 = (bf16[8,3584]{1,0:T(8,128)(2,1)S(1)}, bf16[8,3584]{1,0:T(8,128)(2,1)S(1)}, u32[]{:S(2)}, u32[]{:S(2)}) collective-permute-start(bf16[8,3584]{1,0:T(8,128)(2,1)S(1)} %get-tuple-element.51), channel_id=1, source_target_pairs={{0,16},{1,17},{2,18},{3,19},{4,20},{5,21},{6,22},{7,23},{8,24},{9,... | collective-permute-start | bytes 172040 | tf_op jit(solution)/shard_map/ppermute | solution.py:92
  (13 other events, 37.4 us)

commit v18 on v15

--- a/solution.py
+++ b/solution.py
@@ -248,11 +248,10 @@
         start += size
 
 
-def fetch_columns(source, target, sems):
-    columns = target.shape[1] // sems.shape[0]
+def fetch_columns(source, target, sems, tile):
     copies = []
     for k in range(sems.shape[0]):
-        part = pl.ds(k * columns, columns)
+        part = pl.ds(k * tile, min(tile, target.shape[1] - k * tile))
         copies.append(pltpu.make_async_copy(source.at[:, part], target.at[:, part], sems.at[k]))
         copies[-1].start()
     return copies
@@ -291,7 +290,8 @@
     outs = refs[count + 3 : -10]
     hidden_ref, share_ref, gate, up, down, gate_sum, up_sum, gate_sem, up_sem, down_sem = refs[-10:]
     copies = fetch_both(gate_hbm, up_hbm, gate, up, gate_sem, up_sem, tile)
-    down_copies = fetch_columns(down_hbm, down, down_sem)
+    wide = 4 * down_tile
+    down_copies = fetch_columns(down_hbm, down, down_sem, wide)
 
     table = jnp.concatenate([block[:, gate.shape[0] :] for block in blocks], axis=0)
     table = table.astype(jnp.float32)
@@ -301,7 +301,6 @@
     share_ref[...] = jnp.broadcast_to(share, share_ref.shape)
     project(blocks, copies, gate, up, gate_sum, up_sum, tile)
     hidden_ref[...] = (jax.nn.silu(gate_sum[...]) * up_sum[...]).astype(jnp.bfloat16)
-    wide = down.shape[1] // len(down_copies)
     for k in range(0, down.shape[1], down_tile):
         if k % wide == 0:
             down_copies[k // wide].wait()
@@ -340,7 +339,7 @@
             pltpu.VMEM((rows, units), jnp.float32),
             pltpu.SemaphoreType.DMA((width // tile,)),
             pltpu.SemaphoreType.DMA((width // tile,)),
-            pltpu.SemaphoreType.DMA((width // (2 * down_tile),)),
+            pltpu.SemaphoreType.DMA((pl.cdiv(width, 4 * down_tile),)),
         ],
         cost_estimate=pl.CostEstimate(
             flops=6 * rows * width * units,
@@ -387,7 +386,8 @@
         (far[-1], later_near[-1], later_far[0], attn_latent)
     )
     rows = later_near[-1].shape[0] // 2
-    last = grid.far([later_near[-1][:rows], later_near[-1][rows:]])
+    last = grid.far([later_near[-1][:rows]])
+    last.append(grid.swap(later_far[0][rows:], grid.first, grid.extent(grid.first) - 1))
     mine = [[block] for block in near + far]
     for place, block in zip(mine, later_near + later_far):
         place.append(block)
@@ -395,7 +395,7 @@
     other = [grid.other(place) for place in mine]
     size, count = high * tokens, len(mine)
     sizes = [size] * count + [size, size * (count - 1)]
-    split = width // 2
+    split = width * 4 // 7
     places = mine + other[-1:] + other[:-1]
     products = expert(
         [block for place in places for block in place],

time: 79.4 us -> 82.4 us (1.038)
  waiting for transfers between devices: 26.4 us -> 28.7 us
  starting transfers between devices: 33.3 us -> 34.5 us
    ppermute x35, waiting for transfers between devices: 26.4 us -> 28.7 us  [swap(): return lax.ppermute(value, everyone, pairs)]
    ppermute x35, starting transfers between devices: 33.3 us -> 34.5 us  [swap(): return lax.ppermute(value, everyone, pairs)]
  transfers between devices with their start and end apart: 35 -> 35, of which waited for: 15 -> 17; matrix products, arithmetic and copies ran while one was open for 1% -> 1% of each run, Pallas kernels for 5% -> 4%
where the time goes in v18:
time: 82.4 us; the launch traced here: 82.2 us
  starting transfers between devices  34.5 us (42%)
  waiting for transfers between devices  28.7 us (35%)
  Pallas kernels  16.1 us (20%)
  other arithmetic  1.36 us (2%)
    ppermute x35, starting transfers between devices, swap(): return lax.ppermute(value, everyone, pairs)  34.5 us
    ppermute x35, waiting for transfers between devices, swap(): return lax.ppermute(value, everyone, pairs)  28.7 us
    pallas_call x1, Pallas kernels, expert(): pl.pallas_call(functools.partial(expert_kernel, len(blocks), experts, til...  11.4 us
    pallas_call x1, Pallas kernels, attention(): pl.pallas_call(attention_kernel, in_specs=[pl.BlockSpec(memory_space=pltp...  3.66 us
  transfers between devices with their start and end apart: 35, of which 17 were waited for; matrix products, arithmetic and copies ran while one was open for 1% of the time, Pallas kernels for 4%

profile of v18, /device:TPU:0, one launch (start us, length us, event | category | flops | bytes accessed | tf_op | source)
XLA Modules:
  0.0 82.2 jit_solution(7476748371972030754)
XLA Ops:
  1.6 3.1 %collective-permute-start = (bf16[8,7296]{1,0:T(8,128)(2,1)S(1)}, bf16[8,7296]{1,0:T(8,128)(2,1)S(1)}, u32[]{:S(2)}, u32[]{:S(2)}) collective-permute-start(bf16[8,7296]{1,0:T(8,128)(2,1)S(1)} %pack.1.refs_0_), channel_id=1, source_target_pairs={{0,8},{1,9},{2,10},{3,11},{4,12},{5,13},{6,14},{7,15},{8,0},{9,1},... | collective-permute-start | bytes 350216 | tf_op jit(solution)/shard_map/ppermute | solution.py:92
  4.7 2.6 %collective-permute-start.1 = (bf16[8,7296]{1,0:T(8,128)(2,1)S(1)}, bf16[8,7296]{1,0:T(8,128)(2,1)S(1)}, u32[]{:S(2)}, u32[]{:S(2)}) collective-permute-start(bf16[8,7296]{1,0:T(8,128)(2,1)S(1)} %pack.1.refs_0_), channel_id=1, source_target_pairs={{0,16},{1,17},{2,18},{3,19},{4,20},{5,21},{6,22},{7,23},{8,24},{9,... | collective-permute-start | bytes 350216 | tf_op jit(solution)/shard_map/ppermute | solution.py:92
  7.3 1.8 %collective-permute-done.refs_1_ = bf16[8,7296]{1,0:T(8,128)(2,1)S(1)} collective-permute-done((bf16[8,7296]{1,0:T(8,128)(2,1)S(1)}, bf16[8,7296]{1,0:T(8,128)(2,1)S(1)}, u32[]{:S(2)}, u32[]{:S(2)}) %collective-permute-start) | collective-permute-done | bytes 116768 | tf_op jit(solution)/shard_map/ppermute | solution.py:92
  9.2 1.9 %collective-permute-start.4 = (bf16[16,7296]{1,0:T(8,128)(2,1)S(1)}, bf16[16,7296]{1,0:T(8,128)(2,1)S(1)}, u32[]{:S(2)}, u32[]{:S(2)}) collective-permute-start(bf16[16,7296]{1,0:T(8,128)(2,1)S(1)} %join.2.refs_0_), channel_id=1, source_target_pairs={{0,4},{1,5},{2,3},{3,2},{4,0},{5,1},{6,7},{7,6},{8,12},{9,13},{10,... | collective-permute-start | bytes 700424 | tf_op jit(solution)/shard_map/ppermute | solution.py:92
  11.1 1.5 %collective-permute-start.3 = (bf16[16,7296]{1,0:T(8,128)(2,1)S(1)}, bf16[16,7296]{1,0:T(8,128)(2,1)S(1)}, u32[]{:S(2)}, u32[]{:S(2)}) collective-permute-start(bf16[16,7296]{1,0:T(8,128)(2,1)S(1)} %join.2.refs_0_), channel_id=1, source_target_pairs={{0,1},{1,0},{2,6},{3,7},{4,5},{5,4},{6,2},{7,3},{8,9},{9,8},{10,14... | collective-permute-start | bytes 700424 | tf_op jit(solution)/shard_map/ppermute | solution.py:92
  13.2 4.4 %collective-permute-done.2.refs_1_ = bf16[8,7296]{1,0:T(8,128)(2,1)S(1)} collective-permute-done((bf16[8,7296]{1,0:T(8,128)(2,1)S(1)}, bf16[8,7296]{1,0:T(8,128)(2,1)S(1)}, u32[]{:S(2)}, u32[]{:S(2)}) %collective-permute-start.2) | collective-permute-done | bytes 116768 | tf_op jit(solution)/shard_map/ppermute | solution.py:92
  17.7 1.6 %collective-permute-start.7 = (bf16[16,7296]{1,0:T(8,128)(2,1)S(1)}, bf16[16,7296]{1,0:T(8,128)(2,1)S(1)}, u32[]{:S(2)}, u32[]{:S(2)}) collective-permute-start(bf16[16,7296]{1,0:T(8,128)(2,1)S(1)} %join.3.refs_1_), channel_id=1, source_target_pairs={{0,4},{1,5},{2,3},{3,2},{4,0},{5,1},{6,7},{7,6},{8,12},{9,13},{10,... | collective-permute-start | bytes 700424 | tf_op jit(solution)/shard_map/ppermute | solution.py:92
  19.3 1.5 %collective-permute-start.6 = (bf16[16,7296]{1,0:T(8,128)(2,1)S(1)}, bf16[16,7296]{1,0:T(8,128)(2,1)S(1)}, u32[]{:S(2)}, u32[]{:S(2)}) collective-permute-start(bf16[16,7296]{1,0:T(8,128)(2,1)S(1)} %join.3.refs_1_), channel_id=1, source_target_pairs={{0,1},{1,0},{2,6},{3,7},{4,5},{5,4},{6,2},{7,3},{8,9},{9,8},{10,14... | collective-permute-start | bytes 700424 | tf_op jit(solution)/shard_map/ppermute | solution.py:92
  21.8 2.0 %collective-permute-done.7.refs_5_ = bf16[16,7296]{1,0:T(8,128)(2,1)S(1)} collective-permute-done((bf16[16,7296]{1,0:T(8,128)(2,1)S(1)}, bf16[16,7296]{1,0:T(8,128)(2,1)S(1)}, u32[]{:S(2)}, u32[]{:S(2)}) %collective-permute-start.7) | collective-permute-done | bytes 233504 | tf_op jit(solution)/shard_map/ppermute | solution.py:92
  23.8 1.5 %collective-permute-done.6.refs_3_ = bf16[16,7296]{1,0:T(8,128)(2,1)S(1)} collective-permute-done((bf16[16,7296]{1,0:T(8,128)(2,1)S(1)}, bf16[16,7296]{1,0:T(8,128)(2,1)S(1)}, u32[]{:S(2)}, u32[]{:S(2)}) %collective-permute-start.6) | collective-permute-done | bytes 233504 | tf_op jit(solution)/shard_map/ppermute | solution.py:92
  26.0 3.7 %attention.1 = bf16[2,64,512]{2,1,0:T(8,128)(2,1)} custom-call(s32[2]{0:T(128)S(1)} %copy-done, bf16[2,64,512]{2,1,0:T(8,128)(2,1)} %refs_0_.3, bf16[2,64,64]{2,1,0:T(8,128)(2,1)} %refs_1_.3, bf16[2,512,512]{2,1,0:T(8,128)(2,1)} %refs_2_.3, bf16[2,64,512]{2,1,0:T(8,128)(2,1)} %refs_3_.1), custom_call_target="tpu_custom_call" | custom-call | flops 134217728 | bytes 1048576 | tf_op jit(solution)/shard_map/attention/pallas_call | solution.py:54
  30.3 1.6 %collective-permute-start.9 = (bf16[8,7296]{1,0:T(8,128)(2,1)S(1)}, bf16[8,7296]{1,0:T(8,128)(2,1)S(1)}, u32[]{:S(2)}, u32[]{:S(2)}) collective-permute-start(bf16[8,7296]{1,0:T(8,128)(2,1)S(1)} %slice.49), channel_id=1, source_target_pairs={{0,1},{1,0},{2,6},{3,7},{4,5},{5,4},{6,2},{7,3},{8,9},{9,8},{10,14... | collective-permute-start | bytes 350216 | tf_op jit(solution)/shard_map/ppermute | solution.py:92
  33.1 2.8 %collective-permute-done.9.refs_8_ = bf16[8,7296]{1,0:T(8,128)(2,1)S(1)} collective-permute-done((bf16[8,7296]{1,0:T(8,128)(2,1)S(1)}, bf16[8,7296]{1,0:T(8,128)(2,1)S(1)}, u32[]{:S(2)}, u32[]{:S(2)}) %collective-permute-start.9) | collective-permute-done | bytes 116768 | tf_op jit(solution)/shard_map/ppermute | solution.py:92
  38.1 11.4 %expert.1 = (bf16[32,4096]{1,0:T(8,128)(2,1)S(1)}, bf16[32,4096]{1,0:T(8,128)(2,1)S(1)}, bf16[32,4096]{1,0:T(8,128)(2,1)S(1)}, bf16[32,4096]{1,0:T(8,128)(2,1)S(...) custom-call(s32[1]{0:T(128)} %bitcast.node_ref, ...), custom_call_target="tpu_custom_call" | custom-call | flops 5637144576 | bytes 22020096 | tf_op jit(solution)/shard_map/expert/pallas_call | solution.py:321
  53.3 3.5 %collective-permute-done.30 = bf16[32,3072]{1,0:T(8,128)(2,1)S(1)} collective-permute-done((bf16[32,3072]{1,0:T(8,128)(2,1)S(1)}, bf16[32,3072]{1,0:T(8,128)(2,1)S(1)}, u32[]{:S(2)}, u32[]{:S(2)}) %collective-permute-start.30) | collective-permute-done | bytes 196640 | tf_op jit(solution)/shard_map/ppermute | solution.py:92
  57.8 1.4 %collective-permute-start.31 = (bf16[32,3072]{1,0:T(8,128)(2,1)S(1)}, bf16[32,3072]{1,0:T(8,128)(2,1)S(1)}, u32[]{:S(2)}, u32[]{:S(2)}) collective-permute-start(bf16[32,3072]{1,0:T(8,128)(2,1)S(1)} %get-tuple-element.43), channel_id=1, source_target_pairs={{0,1},{1,0},{2,6},{3,7},{4,5},{5,4},{6,2},{7,3},{8,9},{9,8},{10,14... | collective-permute-start | bytes 589832 | tf_op jit(solution)/shard_map/ppermute | solution.py:92
  60.6 1.6 %collective-permute-start.23 = (bf16[32,4096]{1,0:T(8,128)(2,1)S(1)}, bf16[32,4096]{1,0:T(8,128)(2,1)S(1)}, u32[]{:S(2)}, u32[]{:S(2)}) collective-permute-start(bf16[32,4096]{1,0:T(8,128)(2,1)S(1)} %get-tuple-element.41), channel_id=1, source_target_pairs={{0,1},{1,0},{2,6},{3,7},{4,5},{5,4},{6,2},{7,3},{8,9},{9,8},{10,14... | collective-permute-start | bytes 786440 | tf_op jit(solution)/shard_map/ppermute | solution.py:92
  62.2 2.6 %collective-permute-done.28 = bf16[32,3072]{1,0:T(8,128)(2,1)S(1)} collective-permute-done((bf16[32,3072]{1,0:T(8,128)(2,1)S(1)}, bf16[32,3072]{1,0:T(8,128)(2,1)S(1)}, u32[]{:S(2)}, u32[]{:S(2)}) %collective-permute-start.28) | collective-permute-done | bytes 196640 | tf_op jit(solution)/shard_map/ppermute | solution.py:92
  65.3 2.1 %collective-permute-start.32 = (bf16[8,3072]{1,0:T(8,128)(2,1)S(1)}, bf16[8,3072]{1,0:T(8,128)(2,1)S(1)}, u32[]{:S(2)}, u32[]{:S(2)}) collective-permute-start(bf16[8,3072]{1,0:T(8,128)(2,1)S(1)} %get-tuple-element.47), channel_id=1, source_target_pairs={{0,8},{1,9},{2,10},{3,11},{4,12},{5,13},{6,14},{7,15},{8,0},{9,1},... | collective-permute-start | bytes 147464 | tf_op jit(solution)/shard_map/ppermute | solution.py:92
  67.4 3.0 %collective-permute-start.34 = (bf16[8,3072]{1,0:T(8,128)(2,1)S(1)}, bf16[8,3072]{1,0:T(8,128)(2,1)S(1)}, u32[]{:S(2)}, u32[]{:S(2)}) collective-permute-start(bf16[8,3072]{1,0:T(8,128)(2,1)S(1)} %get-tuple-element.48), channel_id=1, source_target_pairs={{0,24},{1,25},{2,26},{3,27},{4,28},{5,29},{6,30},{7,31},{8,16},{9,... | collective-permute-start | bytes 147464 | tf_op jit(solution)/shard_map/ppermute | solution.py:92
  72.0 3.0 %collective-permute-start.26 = (bf16[8,4096]{1,0:T(8,128)(2,1)S(1)}, bf16[8,4096]{1,0:T(8,128)(2,1)S(1)}, u32[]{:S(2)}, u32[]{:S(2)}) collective-permute-start(bf16[8,4096]{1,0:T(8,128)(2,1)S(1)} %get-tuple-element.45), channel_id=1, source_target_pairs={{0,24},{1,25},{2,26},{3,27},{4,28},{5,29},{6,30},{7,31},{8,16},{9,... | collective-permute-start | bytes 196616 | tf_op jit(solution)/shard_map/ppermute | solution.py:92
  75.2 1.9 %collective-permute-done.33 = bf16[8,3072]{1,0:T(8,128)(2,1)S(1)} collective-permute-done((bf16[8,3072]{1,0:T(8,128)(2,1)S(1)}, bf16[8,3072]{1,0:T(8,128)(2,1)S(1)}, u32[]{:S(2)}, u32[]{:S(2)}) %collective-permute-start.33) | collective-permute-done | bytes 49184 | tf_op jit(solution)/shard_map/ppermute | solution.py:92
  77.1 1.7 %collective-permute-done.26 = bf16[8,4096]{1,0:T(8,128)(2,1)S(1)} collective-permute-done((bf16[8,4096]{1,0:T(8,128)(2,1)S(1)}, bf16[8,4096]{1,0:T(8,128)(2,1)S(1)}, u32[]{:S(2)}, u32[]{:S(2)}) %collective-permute-start.26) | collective-permute-done | bytes 65568 | tf_op jit(solution)/shard_map/ppermute | solution.py:92
  78.8 2.7 %collective-permute-done.25 = bf16[8,4096]{1,0:T(8,128)(2,1)S(1)} collective-permute-done((bf16[8,4096]{1,0:T(8,128)(2,1)S(1)}, bf16[8,4096]{1,0:T(8,128)(2,1)S(1)}, u32[]{:S(2)}, u32[]{:S(2)}) %collective-permute-start.25) | collective-permute-done | bytes 65568 | tf_op jit(solution)/shard_map/ppermute | solution.py:92
  (66 shorter events, 16.8 us)
Async XLA Ops:
  1.6 7.5 %collective-permute-start = (bf16[8,7296]{1,0:T(8,128)(2,1)S(1)}, bf16[8,7296]{1,0:T(8,128)(2,1)S(1)}, u32[]{:S(2)}, u32[]{:S(2)}) collective-permute-start(bf16[8,7296]{1,0:T(8,128)(2,1)S(1)} %pack.1.refs_0_), channel_id=1, source_target_pairs={{0,8},{1,9},{2,10},{3,11},{4,12},{5,13},{6,14},{7,15},{8,0},{9,1},... | collective-permute-start | bytes 350216 | tf_op jit(solution)/shard_map/ppermute | solution.py:92
  4.7 8.1 %collective-permute-start.1 = (bf16[8,7296]{1,0:T(8,128)(2,1)S(1)}, bf16[8,7296]{1,0:T(8,128)(2,1)S(1)}, u32[]{:S(2)}, u32[]{:S(2)}) collective-permute-start(bf16[8,7296]{1,0:T(8,128)(2,1)S(1)} %pack.1.refs_0_), channel_id=1, source_target_pairs={{0,16},{1,17},{2,18},{3,19},{4,20},{5,21},{6,22},{7,23},{8,24},{9,... | collective-permute-start | bytes 350216 | tf_op jit(solution)/shard_map/ppermute | solution.py:92
  9.2 8.5 %collective-permute-start.4 = (bf16[16,7296]{1,0:T(8,128)(2,1)S(1)}, bf16[16,7296]{1,0:T(8,128)(2,1)S(1)}, u32[]{:S(2)}, u32[]{:S(2)}) collective-permute-start(bf16[16,7296]{1,0:T(8,128)(2,1)S(1)} %join.2.refs_0_), channel_id=1, source_target_pairs={{0,4},{1,5},{2,3},{3,2},{4,0},{5,1},{6,7},{7,6},{8,12},{9,13},{10,... | collective-permute-start | bytes 700424 | tf_op jit(solution)/shard_map/ppermute | solution.py:92
  11.1 6.6 %collective-permute-start.3 = (bf16[16,7296]{1,0:T(8,128)(2,1)S(1)}, bf16[16,7296]{1,0:T(8,128)(2,1)S(1)}, u32[]{:S(2)}, u32[]{:S(2)}) collective-permute-start(bf16[16,7296]{1,0:T(8,128)(2,1)S(1)} %join.2.refs_0_), channel_id=1, source_target_pairs={{0,1},{1,0},{2,6},{3,7},{4,5},{5,4},{6,2},{7,3},{8,9},{9,8},{10,14... | collective-permute-start | bytes 700424 | tf_op jit(solution)/shard_map/ppermute | solution.py:92
  17.7 6.1 %collective-permute-start.7 = (bf16[16,7296]{1,0:T(8,128)(2,1)S(1)}, bf16[16,7296]{1,0:T(8,128)(2,1)S(1)}, u32[]{:S(2)}, u32[]{:S(2)}) collective-permute-start(bf16[16,7296]{1,0:T(8,128)(2,1)S(1)} %join.3.refs_1_), channel_id=1, source_target_pairs={{0,4},{1,5},{2,3},{3,2},{4,0},{5,1},{6,7},{7,6},{8,12},{9,13},{10,... | collective-permute-start | bytes 700424 | tf_op jit(solution)/shard_map/ppermute | solution.py:92
  20.7 8.9 %collective-permute-start.5 = (bf16[16,7296]{1,0:T(8,128)(2,1)S(1)}, bf16[16,7296]{1,0:T(8,128)(2,1)S(1)}, u32[]{:S(2)}, u32[]{:S(2)}) collective-permute-start(bf16[16,7296]{1,0:T(8,128)(2,1)S(1)} %collective-permute-done.3.refs_2_), channel_id=1, source_target_pairs={{0,4},{1,5},{2,3},{3,2},{4,0},{5,1},{6,7},{7,6},{8,12},{9,13},{10,... | collective-permute-start | bytes 700424 | tf_op jit(solution)/shard_map/ppermute | solution.py:92
  21.3 9.0 %collective-permute-start.13 = (bf16[16,7296]{1,0:T(8,128)(2,1)S(1)}, bf16[16,7296]{1,0:T(8,128)(2,1)S(1)}, u32[]{:S(2)}, u32[]{:S(2)}) collective-permute-start(bf16[16,7296]{1,0:T(8,128)(2,1)S(1)} %join.2.refs_0_), channel_id=1, source_target_pairs={{0,2},{1,3},{2,0},{3,1},{4,6},{5,7},{6,4},{7,5},{8,10},{9,11},{10,... | collective-permute-start | bytes 700424 | tf_op jit(solution)/shard_map/ppermute | solution.py:92
  21.3 10.6 %collective-permute-start.14 = (bf16[16,7296]{1,0:T(8,128)(2,1)S(1)}, bf16[16,7296]{1,0:T(8,128)(2,1)S(1)}, u32[]{:S(2)}, u32[]{:S(2)}) collective-permute-start(bf16[16,7296]{1,0:T(8,128)(2,1)S(1)} %join.3.refs_1_), channel_id=1, source_target_pairs={{0,2},{1,3},{2,0},{3,1},{4,6},{5,7},{6,4},{7,5},{8,10},{9,11},{10,... | collective-permute-start | bytes 700424 | tf_op jit(solution)/shard_map/ppermute | solution.py:92
  23.8 8.8 %collective-permute-start.17 = (bf16[16,7296]{1,0:T(8,128)(2,1)S(1)}, bf16[16,7296]{1,0:T(8,128)(2,1)S(1)}, u32[]{:S(2)}, u32[]{:S(2)}) collective-permute-start(bf16[16,7296]{1,0:T(8,128)(2,1)S(1)} %collective-permute-done.4.refs_4_), channel_id=1, source_target_pairs={{0,2},{1,3},{2,0},{3,1},{4,6},{5,7},{6,4},{7,5},{8,10},{9,11},{10,... | collective-permute-start | bytes 700424 | tf_op jit(solution)/shard_map/ppermute | solution.py:92
  25.3 7.3 %collective-permute-start.15 = (bf16[16,7296]{1,0:T(8,128)(2,1)S(1)}, bf16[16,7296]{1,0:T(8,128)(2,1)S(1)}, u32[]{:S(2)}, u32[]{:S(2)}) collective-permute-start(bf16[16,7296]{1,0:T(8,128)(2,1)S(1)} %collective-permute-done.3.refs_2_), channel_id=1, source_target_pairs={{0,2},{1,3},{2,0},{3,1},{4,6},{5,7},{6,4},{7,5},{8,10},{9,11},{10,... | collective-permute-start | bytes 700424 | tf_op jit(solution)/shard_map/ppermute | solution.py:92
  29.7 8.4 %collective-permute-start.16 = (bf16[16,7296]{1,0:T(8,128)(2,1)S(1)}, bf16[16,7296]{1,0:T(8,128)(2,1)S(1)}, u32[]{:S(2)}, u32[]{:S(2)}) collective-permute-start(bf16[16,7296]{1,0:T(8,128)(2,1)S(1)} %collective-permute-done.6.refs_3_), channel_id=1, source_target_pairs={{0,2},{1,3},{2,0},{3,1},{4,6},{5,7},{6,4},{7,5},{8,10},{9,11},{10,... | collective-permute-start | bytes 700424 | tf_op jit(solution)/shard_map/ppermute | solution.py:92
  50.1 6.7 %collective-permute-start.27 = (bf16[96,3072]{1,0:T(8,128)(2,1)S(1)}, bf16[96,3072]{1,0:T(8,128)(2,1)S(1)}, u32[]{:S(2)}, u32[]{:S(2)}) collective-permute-start(bf16[96,3072]{1,0:T(8,128)(2,1)S(1)} %get-tuple-element.34), channel_id=1, source_target_pairs={{0,2},{1,3},{2,0},{3,1},{4,6},{5,7},{6,4},{7,5},{8,10},{9,11},{10,... | collective-permute-start | bytes 1769480 | tf_op jit(solution)/shard_map/ppermute | solution.py:92
  50.3 9.4 %collective-permute-start.19 = (bf16[96,4096]{1,0:T(8,128)(2,1)S(1)}, bf16[96,4096]{1,0:T(8,128)(2,1)S(1)}, u32[]{:S(2)}, u32[]{:S(2)}) collective-permute-start(bf16[96,4096]{1,0:T(8,128)(2,1)S(1)} %get-tuple-element.28), channel_id=1, source_target_pairs={{0,2},{1,3},{2,0},{3,1},{4,6},{5,7},{6,4},{7,5},{8,10},{9,11},{10,... | collective-permute-start | bytes 2359304 | tf_op jit(solution)/shard_map/ppermute | solution.py:92
  52.0 7.7 %collective-permute-start.22 = (bf16[32,4096]{1,0:T(8,128)(2,1)S(1)}, bf16[32,4096]{1,0:T(8,128)(2,1)S(1)}, u32[]{:S(2)}, u32[]{:S(2)}) collective-permute-start(bf16[32,4096]{1,0:T(8,128)(2,1)S(1)} %add_convert_fusion.2), channel_id=1, source_target_pairs={{0,4},{1,5},{2,3},{3,2},{4,0},{5,1},{6,7},{7,6},{8,12},{9,13},{10,... | collective-permute-start | bytes 786440 | tf_op jit(solution)/shard_map/ppermute | solution.py:92
  56.9 7.8 %collective-permute-start.28 = (bf16[32,3072]{1,0:T(8,128)(2,1)S(1)}, bf16[32,3072]{1,0:T(8,128)(2,1)S(1)}, u32[]{:S(2)}, u32[]{:S(2)}) collective-permute-start(bf16[32,3072]{1,0:T(8,128)(2,1)S(1)} %get-tuple-element.42), channel_id=1, source_target_pairs={{0,4},{1,5},{2,3},{3,2},{4,0},{5,1},{6,7},{7,6},{8,12},{9,13},{10,... | collective-permute-start | bytes 589832 | tf_op jit(solution)/shard_map/ppermute | solution.py:92
  57.8 7.4 %collective-permute-start.31 = (bf16[32,3072]{1,0:T(8,128)(2,1)S(1)}, bf16[32,3072]{1,0:T(8,128)(2,1)S(1)}, u32[]{:S(2)}, u32[]{:S(2)}) collective-permute-start(bf16[32,3072]{1,0:T(8,128)(2,1)S(1)} %get-tuple-element.43), channel_id=1, source_target_pairs={{0,1},{1,0},{2,6},{3,7},{4,5},{5,4},{6,2},{7,3},{8,9},{9,8},{10,14... | collective-permute-start | bytes 589832 | tf_op jit(solution)/shard_map/ppermute | solution.py:92
  59.8 11.1 %collective-permute-start.20 = (bf16[32,4096]{1,0:T(8,128)(2,1)S(1)}, bf16[32,4096]{1,0:T(8,128)(2,1)S(1)}, u32[]{:S(2)}, u32[]{:S(2)}) collective-permute-start(bf16[32,4096]{1,0:T(8,128)(2,1)S(1)} %get-tuple-element.40), channel_id=1, source_target_pairs={{0,4},{1,5},{2,3},{3,2},{4,0},{5,1},{6,7},{7,6},{8,12},{9,13},{10,... | collective-permute-start | bytes 786440 | tf_op jit(solution)/shard_map/ppermute | solution.py:92
  60.6 10.3 %collective-permute-start.23 = (bf16[32,4096]{1,0:T(8,128)(2,1)S(1)}, bf16[32,4096]{1,0:T(8,128)(2,1)S(1)}, u32[]{:S(2)}, u32[]{:S(2)}) collective-permute-start(bf16[32,4096]{1,0:T(8,128)(2,1)S(1)} %get-tuple-element.41), channel_id=1, source_target_pairs={{0,1},{1,0},{2,6},{3,7},{4,5},{5,4},{6,2},{7,3},{8,9},{9,8},{10,14... | collective-permute-start | bytes 786440 | tf_op jit(solution)/shard_map/ppermute | solution.py:92
  65.3 9.7 %collective-permute-start.32 = (bf16[8,3072]{1,0:T(8,128)(2,1)S(1)}, bf16[8,3072]{1,0:T(8,128)(2,1)S(1)}, u32[]{:S(2)}, u32[]{:S(2)}) collective-permute-start(bf16[8,3072]{1,0:T(8,128)(2,1)S(1)} %get-tuple-element.47), channel_id=1, source_target_pairs={{0,8},{1,9},{2,10},{3,11},{4,12},{5,13},{6,14},{7,15},{8,0},{9,1},... | collective-permute-start | bytes 147464 | tf_op jit(solution)/shard_map/ppermute | solution.py:92
  67.4 7.8 %collective-permute-start.34 = (bf16[8,3072]{1,0:T(8,128)(2,1)S(1)}, bf16[8,3072]{1,0:T(8,128)(2,1)S(1)}, u32[]{:S(2)}, u32[]{:S(2)}) collective-permute-start(bf16[8,3072]{1,0:T(8,128)(2,1)S(1)} %get-tuple-element.48), channel_id=1, source_target_pairs={{0,24},{1,25},{2,26},{3,27},{4,28},{5,29},{6,30},{7,31},{8,16},{9,... | collective-permute-start | bytes 147464 | tf_op jit(solution)/shard_map/ppermute | solution.py:92
  70.4 6.7 %collective-permute-start.33 = (bf16[8,3072]{1,0:T(8,128)(2,1)S(1)}, bf16[8,3072]{1,0:T(8,128)(2,1)S(1)}, u32[]{:S(2)}, u32[]{:S(2)}) collective-permute-start(bf16[8,3072]{1,0:T(8,128)(2,1)S(1)} %get-tuple-element.49), channel_id=1, source_target_pairs={{0,16},{1,17},{2,18},{3,19},{4,20},{5,21},{6,22},{7,23},{8,24},{9,... | collective-permute-start | bytes 147464 | tf_op jit(solution)/shard_map/ppermute | solution.py:92
  71.0 6.1 %collective-permute-start.24 = (bf16[8,4096]{1,0:T(8,128)(2,1)S(1)}, bf16[8,4096]{1,0:T(8,128)(2,1)S(1)}, u32[]{:S(2)}, u32[]{:S(2)}) collective-permute-start(bf16[8,4096]{1,0:T(8,128)(2,1)S(1)} %get-tuple-element.44), channel_id=1, source_target_pairs={{0,8},{1,9},{2,10},{3,11},{4,12},{5,13},{6,14},{7,15},{8,0},{9,1},... | collective-permute-start | bytes 196616 | tf_op jit(solution)/shard_map/ppermute | solution.py:92
  72.0 6.7 %collective-permute-start.26 = (bf16[8,4096]{1,0:T(8,128)(2,1)S(1)}, bf16[8,4096]{1,0:T(8,128)(2,1)S(1)}, u32[]{:S(2)}, u32[]{:S(2)}) collective-permute-start(bf16[8,4096]{1,0:T(8,128)(2,1)S(1)} %get-tuple-element.45), channel_id=1, source_target_pairs={{0,24},{1,25},{2,26},{3,27},{4,28},{5,29},{6,30},{7,31},{8,16},{9,... | collective-permute-start | bytes 196616 | tf_op jit(solution)/shard_map/ppermute | solution.py:92
  75.0 6.5 %collective-permute-start.25 = (bf16[8,4096]{1,0:T(8,128)(2,1)S(1)}, bf16[8,4096]{1,0:T(8,128)(2,1)S(1)}, u32[]{:S(2)}, u32[]{:S(2)}) collective-permute-start(bf16[8,4096]{1,0:T(8,128)(2,1)S(1)} %get-tuple-element.46), channel_id=1, source_target_pairs={{0,16},{1,17},{2,18},{3,19},{4,20},{5,21},{6,22},{7,23},{8,24},{9,... | collective-permute-start | bytes 196616 | tf_op jit(solution)/shard_map/ppermute | solution.py:92
  (12 other events, 45.4 us)

commit v19 on v18

--- a/solution.py
+++ b/solution.py
@@ -378,13 +378,11 @@
     near = grid.near(join(grid.lines(outgoing, masks[1:])))
     far = grid.far(near[:-1])
     lines = grid.lines(came, masks[1:])
-    lines[-1], near[-1], far[0] = tied((lines[-1], near[-1], far[0]))
+    lines[-1], near[-1], far[0], attn_latent = tied((lines[-1], near[-1], far[0], attn_latent))
     later_near = grid.near(join(lines))
     later_far = grid.far(later_near[:-1])
     far += grid.far(near[-1:])
-    far[-1], later_near[-1], later_far[0], attn_latent = tied(
-        (far[-1], later_near[-1], later_far[0], attn_latent)
-    )
+    far[-1], later_near[-1], later_far[0] = tied((far[-1], later_near[-1], later_far[0]))
     rows = later_near[-1].shape[0] // 2
     last = grid.far([later_near[-1][:rows]])
     last.append(grid.swap(later_far[0][rows:], grid.first, grid.extent(grid.first) - 1))
@@ -395,7 +393,7 @@
     other = [grid.other(place) for place in mine]
     size, count = high * tokens, len(mine)
     sizes = [size] * count + [size, size * (count - 1)]
-    split = width * 4 // 7
+    split = width // 2
     places = mine + other[-1:] + other[:-1]
     products = expert(
         [block for place in places for block in place],

time: 82.4 us -> 78.8 us (0.956)
  waiting for transfers between devices: 28.7 us -> 25.7 us
    ppermute x35, waiting for transfers between devices: 28.7 us -> 25.7 us  [swap(): return lax.ppermute(value, everyone, pairs)]
  transfers between devices with their start and end apart: 35 -> 35, of which waited for: 17 -> 15; matrix products, arithmetic and copies ran while one was open for 1% -> 1% of each run, Pallas kernels for 4% -> 5%
where the time goes in v19:
time: 78.8 us; the launch traced here: 78.6 us
  starting transfers between devices  34 us (43%)
  waiting for transfers between devices  25.7 us (33%)
  Pallas kernels  16.1 us (20%)
  other arithmetic  1.34 us (2%)
  between operations  0.79 us (1%)
    ppermute x35, starting transfers between devices, swap(): return lax.ppermute(value, everyone, pairs)  34 us
    ppermute x35, waiting for transfers between devices, swap(): return lax.ppermute(value, everyone, pairs)  25.7 us
    pallas_call x1, Pallas kernels, expert(): pl.pallas_call(functools.partial(expert_kernel, len(blocks), experts, til...  11.4 us
    pallas_call x1, Pallas kernels, attention(): pl.pallas_call(attention_kernel, in_specs=[pl.BlockSpec(memory_space=pltp...  3.66 us
  transfers between devices with their start and end apart: 35, of which 15 were waited for; matrix products, arithmetic and copies ran while one was open for 1% of the time, Pallas kernels for 5%

profile of v19, /device:TPU:0, one launch (start us, length us, event | category | flops | bytes accessed | tf_op | source)
XLA Modules:
  0.0 78.6 jit_solution(2185118058814566810)
XLA Ops:
  1.6 3.1 %collective-permute-start = (bf16[8,7296]{1,0:T(8,128)(2,1)S(1)}, bf16[8,7296]{1,0:T(8,128)(2,1)S(1)}, u32[]{:S(2)}, u32[]{:S(2)}) collective-permute-start(bf16[8,7296]{1,0:T(8,128)(2,1)S(1)} %pack.1.refs_0_), channel_id=1, source_target_pairs={{0,8},{1,9},{2,10},{3,11},{4,12},{5,13},{6,14},{7,15},{8,0},{9,1},... | collective-permute-start | bytes 350216 | tf_op jit(solution)/shard_map/ppermute | solution.py:92
  4.7 2.6 %collective-permute-start.1 = (bf16[8,7296]{1,0:T(8,128)(2,1)S(1)}, bf16[8,7296]{1,0:T(8,128)(2,1)S(1)}, u32[]{:S(2)}, u32[]{:S(2)}) collective-permute-start(bf16[8,7296]{1,0:T(8,128)(2,1)S(1)} %pack.1.refs_0_), channel_id=1, source_target_pairs={{0,16},{1,17},{2,18},{3,19},{4,20},{5,21},{6,22},{7,23},{8,24},{9,... | collective-permute-start | bytes 350216 | tf_op jit(solution)/shard_map/ppermute | solution.py:92
  7.3 1.8 %collective-permute-done.refs_1_ = bf16[8,7296]{1,0:T(8,128)(2,1)S(1)} collective-permute-done((bf16[8,7296]{1,0:T(8,128)(2,1)S(1)}, bf16[8,7296]{1,0:T(8,128)(2,1)S(1)}, u32[]{:S(2)}, u32[]{:S(2)}) %collective-permute-start) | collective-permute-done | bytes 116768 | tf_op jit(solution)/shard_map/ppermute | solution.py:92
  9.2 1.9 %collective-permute-start.4 = (bf16[16,7296]{1,0:T(8,128)(2,1)S(1)}, bf16[16,7296]{1,0:T(8,128)(2,1)S(1)}, u32[]{:S(2)}, u32[]{:S(2)}) collective-permute-start(bf16[16,7296]{1,0:T(8,128)(2,1)S(1)} %join.2.refs_0_), channel_id=1, source_target_pairs={{0,4},{1,5},{2,3},{3,2},{4,0},{5,1},{6,7},{7,6},{8,12},{9,13},{10,... | collective-permute-start | bytes 700424 | tf_op jit(solution)/shard_map/ppermute | solution.py:92
  11.1 1.5 %collective-permute-start.3 = (bf16[16,7296]{1,0:T(8,128)(2,1)S(1)}, bf16[16,7296]{1,0:T(8,128)(2,1)S(1)}, u32[]{:S(2)}, u32[]{:S(2)}) collective-permute-start(bf16[16,7296]{1,0:T(8,128)(2,1)S(1)} %join.2.refs_0_), channel_id=1, source_target_pairs={{0,1},{1,0},{2,6},{3,7},{4,5},{5,4},{6,2},{7,3},{8,9},{9,8},{10,14... | collective-permute-start | bytes 700424 | tf_op jit(solution)/shard_map/ppermute | solution.py:92
  13.9 3.7 %attention.1 = bf16[2,64,512]{2,1,0:T(8,128)(2,1)} custom-call(s32[2]{0:T(128)S(1)} %copy-done, bf16[2,64,512]{2,1,0:T(8,128)(2,1)} %refs_0_.3, bf16[2,64,64]{2,1,0:T(8,128)(2,1)} %refs_1_.3, bf16[2,512,512]{2,1,0:T(8,128)(2,1)} %refs_2_.3, bf16[2,64,512]{2,1,0:T(8,128)(2,1)} %refs_3_.1), custom_call_target="tpu_custom_call" | custom-call | flops 134217728 | bytes 1048576 | tf_op jit(solution)/shard_map/attention/pallas_call | solution.py:54
  17.7 1.6 %collective-permute-start.7 = (bf16[16,7296]{1,0:T(8,128)(2,1)S(1)}, bf16[16,7296]{1,0:T(8,128)(2,1)S(1)}, u32[]{:S(2)}, u32[]{:S(2)}) collective-permute-start(bf16[16,7296]{1,0:T(8,128)(2,1)S(1)} %join.3.refs_1_), channel_id=1, source_target_pairs={{0,4},{1,5},{2,3},{3,2},{4,0},{5,1},{6,7},{7,6},{8,12},{9,13},{10,... | collective-permute-start | bytes 700424 | tf_op jit(solution)/shard_map/ppermute | solution.py:92
  19.3 1.5 %collective-permute-start.6 = (bf16[16,7296]{1,0:T(8,128)(2,1)S(1)}, bf16[16,7296]{1,0:T(8,128)(2,1)S(1)}, u32[]{:S(2)}, u32[]{:S(2)}) collective-permute-start(bf16[16,7296]{1,0:T(8,128)(2,1)S(1)} %join.3.refs_1_), channel_id=1, source_target_pairs={{0,1},{1,0},{2,6},{3,7},{4,5},{5,4},{6,2},{7,3},{8,9},{9,8},{10,14... | collective-permute-start | bytes 700424 | tf_op jit(solution)/shard_map/ppermute | solution.py:92
  21.8 3.3 %collective-permute-done.7.refs_5_ = bf16[16,7296]{1,0:T(8,128)(2,1)S(1)} collective-permute-done((bf16[16,7296]{1,0:T(8,128)(2,1)S(1)}, bf16[16,7296]{1,0:T(8,128)(2,1)S(1)}, u32[]{:S(2)}, u32[]{:S(2)}) %collective-permute-start.7) | collective-permute-done | bytes 233504 | tf_op jit(solution)/shard_map/ppermute | solution.py:92
  25.1 1.3 %collective-permute-done.6.refs_3_ = bf16[16,7296]{1,0:T(8,128)(2,1)S(1)} collective-permute-done((bf16[16,7296]{1,0:T(8,128)(2,1)S(1)}, bf16[16,7296]{1,0:T(8,128)(2,1)S(1)}, u32[]{:S(2)}, u32[]{:S(2)}) %collective-permute-start.6) | collective-permute-done | bytes 233504 | tf_op jit(solution)/shard_map/ppermute | solution.py:92
  28.6 1.5 %collective-permute-start.8 = (bf16[8,7296]{1,0:T(8,128)(2,1)S(1)}, bf16[8,7296]{1,0:T(8,128)(2,1)S(1)}, u32[]{:S(2)}, u32[]{:S(2)}) collective-permute-start(bf16[8,7296]{1,0:T(8,128)(2,1)S(1)} %slice.48), channel_id=1, source_target_pairs={{0,4},{1,5},{2,3},{3,2},{4,0},{5,1},{6,7},{7,6},{8,12},{9,13},{10,... | collective-permute-start | bytes 350216 | tf_op jit(solution)/shard_map/ppermute | solution.py:92
  30.6 2.5 %collective-permute-done.9.refs_8_ = bf16[8,7296]{1,0:T(8,128)(2,1)S(1)} collective-permute-done((bf16[8,7296]{1,0:T(8,128)(2,1)S(1)}, bf16[8,7296]{1,0:T(8,128)(2,1)S(1)}, u32[]{:S(2)}, u32[]{:S(2)}) %collective-permute-start.9) | collective-permute-done | bytes 116768 | tf_op jit(solution)/shard_map/ppermute | solution.py:92
  34.9 11.4 %expert.1 = (bf16[32,3584]{1,0:T(8,128)(2,1)S(1)}, bf16[32,3584]{1,0:T(8,128)(2,1)S(1)}, bf16[32,3584]{1,0:T(8,128)(2,1)S(1)}, bf16[32,3584]{1,0:T(8,128)(2,1)S(...) custom-call(s32[1]{0:T(128)} %bitcast.node_ref, ...), custom_call_target="tpu_custom_call" | custom-call | flops 5637144576 | bytes 22020096 | tf_op jit(solution)/shard_map/expert/pallas_call | solution.py:321
  47.9 2.0 %collective-permute-start.22 = (bf16[32,3584]{1,0:T(8,128)(2,1)S(1)}, bf16[32,3584]{1,0:T(8,128)(2,1)S(1)}, u32[]{:S(2)}, u32[]{:S(2)}) collective-permute-start(bf16[32,3584]{1,0:T(8,128)(2,1)S(1)} %add_convert_fusion.9), channel_id=1, source_target_pairs={{0,4},{1,5},{2,3},{3,2},{4,0},{5,1},{6,7},{7,6},{8,12},{9,13},{10,... | collective-permute-start | bytes 688136 | tf_op jit(solution)/shard_map/ppermute | solution.py:92
  50.2 3.8 %collective-permute-done.22 = bf16[32,3584]{1,0:T(8,128)(2,1)S(1)} collective-permute-done((bf16[32,3584]{1,0:T(8,128)(2,1)S(1)}, bf16[32,3584]{1,0:T(8,128)(2,1)S(1)}, u32[]{:S(2)}, u32[]{:S(2)}) %collective-permute-start.22) | collective-permute-done | bytes 229408 | tf_op jit(solution)/shard_map/ppermute | solution.py:92
  54.1 2.0 %collective-permute-start.20 = (bf16[32,3584]{1,0:T(8,128)(2,1)S(1)}, bf16[32,3584]{1,0:T(8,128)(2,1)S(1)}, u32[]{:S(2)}, u32[]{:S(2)}) collective-permute-start(bf16[32,3584]{1,0:T(8,128)(2,1)S(1)} %get-tuple-element.40), channel_id=1, source_target_pairs={{0,4},{1,5},{2,3},{3,2},{4,0},{5,1},{6,7},{7,6},{8,12},{9,13},{10,... | collective-permute-start | bytes 688136 | tf_op jit(solution)/shard_map/ppermute | solution.py:92
  57.1 1.4 %collective-permute-start.28 = (bf16[32,3584]{1,0:T(8,128)(2,1)S(1)}, bf16[32,3584]{1,0:T(8,128)(2,1)S(1)}, u32[]{:S(2)}, u32[]{:S(2)}) collective-permute-start(bf16[32,3584]{1,0:T(8,128)(2,1)S(1)} %get-tuple-element.42), channel_id=1, source_target_pairs={{0,4},{1,5},{2,3},{3,2},{4,0},{5,1},{6,7},{7,6},{8,12},{9,13},{10,... | collective-permute-start | bytes 688136 | tf_op jit(solution)/shard_map/ppermute | solution.py:92
  59.4 3.2 %collective-permute-done.20 = bf16[32,3584]{1,0:T(8,128)(2,1)S(1)} collective-permute-done((bf16[32,3584]{1,0:T(8,128)(2,1)S(1)}, bf16[32,3584]{1,0:T(8,128)(2,1)S(1)}, u32[]{:S(2)}, u32[]{:S(2)}) %collective-permute-start.20) | collective-permute-done | bytes 229408 | tf_op jit(solution)/shard_map/ppermute | solution.py:92
  63.7 1.2 %collective-permute-start.24 = (bf16[8,3584]{1,0:T(8,128)(2,1)S(1)}, bf16[8,3584]{1,0:T(8,128)(2,1)S(1)}, u32[]{:S(2)}, u32[]{:S(2)}) collective-permute-start(bf16[8,3584]{1,0:T(8,128)(2,1)S(1)} %get-tuple-element.44), channel_id=1, source_target_pairs={{0,8},{1,9},{2,10},{3,11},{4,12},{5,13},{6,14},{7,15},{8,0},{9,1},... | collective-permute-start | bytes 172040 | tf_op jit(solution)/shard_map/ppermute | solution.py:92
  65.0 2.9 %collective-permute-start.26 = (bf16[8,3584]{1,0:T(8,128)(2,1)S(1)}, bf16[8,3584]{1,0:T(8,128)(2,1)S(1)}, u32[]{:S(2)}, u32[]{:S(2)}) collective-permute-start(bf16[8,3584]{1,0:T(8,128)(2,1)S(1)} %get-tuple-element.45), channel_id=1, source_target_pairs={{0,24},{1,25},{2,26},{3,27},{4,28},{5,29},{6,30},{7,31},{8,16},{9,... | collective-permute-start | bytes 172040 | tf_op jit(solution)/shard_map/ppermute | solution.py:92
  68.2 1.4 %collective-permute-start.32 = (bf16[8,3584]{1,0:T(8,128)(2,1)S(1)}, bf16[8,3584]{1,0:T(8,128)(2,1)S(1)}, u32[]{:S(2)}, u32[]{:S(2)}) collective-permute-start(bf16[8,3584]{1,0:T(8,128)(2,1)S(1)} %get-tuple-element.47), channel_id=1, source_target_pairs={{0,8},{1,9},{2,10},{3,11},{4,12},{5,13},{6,14},{7,15},{8,0},{9,1},... | collective-permute-start | bytes 172040 | tf_op jit(solution)/shard_map/ppermute | solution.py:92
  69.6 2.9 %collective-permute-start.34 = (bf16[8,3584]{1,0:T(8,128)(2,1)S(1)}, bf16[8,3584]{1,0:T(8,128)(2,1)S(1)}, u32[]{:S(2)}, u32[]{:S(2)}) collective-permute-start(bf16[8,3584]{1,0:T(8,128)(2,1)S(1)} %get-tuple-element.48), channel_id=1, source_target_pairs={{0,24},{1,25},{2,26},{3,27},{4,28},{5,29},{6,30},{7,31},{8,16},{9,... | collective-permute-start | bytes 172040 | tf_op jit(solution)/shard_map/ppermute | solution.py:92
  72.5 3.4 %collective-permute-done.25 = bf16[8,3584]{1,0:T(8,128)(2,1)S(1)} collective-permute-done((bf16[8,3584]{1,0:T(8,128)(2,1)S(1)}, bf16[8,3584]{1,0:T(8,128)(2,1)S(1)}, u32[]{:S(2)}, u32[]{:S(2)}) %collective-permute-start.25) | collective-permute-done | bytes 57376 | tf_op jit(solution)/shard_map/ppermute | solution.py:92
  76.0 1.9 %collective-permute-done.33 = bf16[8,3584]{1,0:T(8,128)(2,1)S(1)} collective-permute-done((bf16[8,3584]{1,0:T(8,128)(2,1)S(1)}, bf16[8,3584]{1,0:T(8,128)(2,1)S(1)}, u32[]{:S(2)}, u32[]{:S(2)}) %collective-permute-start.33) | collective-permute-done | bytes 57376 | tf_op jit(solution)/shard_map/ppermute | solution.py:92
  (66 shorter events, 14.0 us)
Async XLA Ops:
  1.6 7.5 %collective-permute-start = (bf16[8,7296]{1,0:T(8,128)(2,1)S(1)}, bf16[8,7296]{1,0:T(8,128)(2,1)S(1)}, u32[]{:S(2)}, u32[]{:S(2)}) collective-permute-start(bf16[8,7296]{1,0:T(8,128)(2,1)S(1)} %pack.1.refs_0_), channel_id=1, source_target_pairs={{0,8},{1,9},{2,10},{3,11},{4,12},{5,13},{6,14},{7,15},{8,0},{9,1},... | collective-permute-start | bytes 350216 | tf_op jit(solution)/shard_map/ppermute | solution.py:92
  4.7 8.1 %collective-permute-start.1 = (bf16[8,7296]{1,0:T(8,128)(2,1)S(1)}, bf16[8,7296]{1,0:T(8,128)(2,1)S(1)}, u32[]{:S(2)}, u32[]{:S(2)}) collective-permute-start(bf16[8,7296]{1,0:T(8,128)(2,1)S(1)} %pack.1.refs_0_), channel_id=1, source_target_pairs={{0,16},{1,17},{2,18},{3,19},{4,20},{5,21},{6,22},{7,23},{8,24},{9,... | collective-permute-start | bytes 350216 | tf_op jit(solution)/shard_map/ppermute | solution.py:92
  9.2 8.5 %collective-permute-start.4 = (bf16[16,7296]{1,0:T(8,128)(2,1)S(1)}, bf16[16,7296]{1,0:T(8,128)(2,1)S(1)}, u32[]{:S(2)}, u32[]{:S(2)}) collective-permute-start(bf16[16,7296]{1,0:T(8,128)(2,1)S(1)} %join.2.refs_0_), channel_id=1, source_target_pairs={{0,4},{1,5},{2,3},{3,2},{4,0},{5,1},{6,7},{7,6},{8,12},{9,13},{10,... | collective-permute-start | bytes 700424 | tf_op jit(solution)/shard_map/ppermute | solution.py:92
  11.1 6.6 %collective-permute-start.3 = (bf16[16,7296]{1,0:T(8,128)(2,1)S(1)}, bf16[16,7296]{1,0:T(8,128)(2,1)S(1)}, u32[]{:S(2)}, u32[]{:S(2)}) collective-permute-start(bf16[16,7296]{1,0:T(8,128)(2,1)S(1)} %join.2.refs_0_), channel_id=1, source_target_pairs={{0,1},{1,0},{2,6},{3,7},{4,5},{5,4},{6,2},{7,3},{8,9},{9,8},{10,14... | collective-permute-start | bytes 700424 | tf_op jit(solution)/shard_map/ppermute | solution.py:92
  17.7 7.4 %collective-permute-start.7 = (bf16[16,7296]{1,0:T(8,128)(2,1)S(1)}, bf16[16,7296]{1,0:T(8,128)(2,1)S(1)}, u32[]{:S(2)}, u32[]{:S(2)}) collective-permute-start(bf16[16,7296]{1,0:T(8,128)(2,1)S(1)} %join.3.refs_1_), channel_id=1, source_target_pairs={{0,4},{1,5},{2,3},{3,2},{4,0},{5,1},{6,7},{7,6},{8,12},{9,13},{10,... | collective-permute-start | bytes 700424 | tf_op jit(solution)/shard_map/ppermute | solution.py:92
  19.3 7.1 %collective-permute-start.6 = (bf16[16,7296]{1,0:T(8,128)(2,1)S(1)}, bf16[16,7296]{1,0:T(8,128)(2,1)S(1)}, u32[]{:S(2)}, u32[]{:S(2)}) collective-permute-start(bf16[16,7296]{1,0:T(8,128)(2,1)S(1)} %join.3.refs_1_), channel_id=1, source_target_pairs={{0,1},{1,0},{2,6},{3,7},{4,5},{5,4},{6,2},{7,3},{8,9},{9,8},{10,14... | collective-permute-start | bytes 700424 | tf_op jit(solution)/shard_map/ppermute | solution.py:92
  20.7 6.9 %collective-permute-start.5 = (bf16[16,7296]{1,0:T(8,128)(2,1)S(1)}, bf16[16,7296]{1,0:T(8,128)(2,1)S(1)}, u32[]{:S(2)}, u32[]{:S(2)}) collective-permute-start(bf16[16,7296]{1,0:T(8,128)(2,1)S(1)} %collective-permute-done.3.refs_2_), channel_id=1, source_target_pairs={{0,4},{1,5},{2,3},{3,2},{4,0},{5,1},{6,7},{7,6},{8,12},{9,13},{10,... | collective-permute-start | bytes 700424 | tf_op jit(solution)/shard_map/ppermute | solution.py:92
  21.3 6.5 %collective-permute-start.13 = (bf16[16,7296]{1,0:T(8,128)(2,1)S(1)}, bf16[16,7296]{1,0:T(8,128)(2,1)S(1)}, u32[]{:S(2)}, u32[]{:S(2)}) collective-permute-start(bf16[16,7296]{1,0:T(8,128)(2,1)S(1)} %join.2.refs_0_), channel_id=1, source_target_pairs={{0,2},{1,3},{2,0},{3,1},{4,6},{5,7},{6,4},{7,5},{8,10},{9,11},{10,... | collective-permute-start | bytes 700424 | tf_op jit(solution)/shard_map/ppermute | solution.py:92
  21.3 7.3 %collective-permute-start.14 = (bf16[16,7296]{1,0:T(8,128)(2,1)S(1)}, bf16[16,7296]{1,0:T(8,128)(2,1)S(1)}, u32[]{:S(2)}, u32[]{:S(2)}) collective-permute-start(bf16[16,7296]{1,0:T(8,128)(2,1)S(1)} %join.3.refs_1_), channel_id=1, source_target_pairs={{0,2},{1,3},{2,0},{3,1},{4,6},{5,7},{6,4},{7,5},{8,10},{9,11},{10,... | collective-permute-start | bytes 700424 | tf_op jit(solution)/shard_map/ppermute | solution.py:92
  27.6 7.2 %collective-permute-start.16 = (bf16[16,7296]{1,0:T(8,128)(2,1)S(1)}, bf16[16,7296]{1,0:T(8,128)(2,1)S(1)}, u32[]{:S(2)}, u32[]{:S(2)}) collective-permute-start(bf16[16,7296]{1,0:T(8,128)(2,1)S(1)} %collective-permute-done.6.refs_3_), channel_id=1, source_target_pairs={{0,2},{1,3},{2,0},{3,1},{4,6},{5,7},{6,4},{7,5},{8,10},{9,11},{10,... | collective-permute-start | bytes 700424 | tf_op jit(solution)/shard_map/ppermute | solution.py:92
  27.7 5.4 %collective-permute-start.9 = (bf16[8,7296]{1,0:T(8,128)(2,1)S(1)}, bf16[8,7296]{1,0:T(8,128)(2,1)S(1)}, u32[]{:S(2)}, u32[]{:S(2)}) collective-permute-start(bf16[8,7296]{1,0:T(8,128)(2,1)S(1)} %slice.49), channel_id=1, source_target_pairs={{0,1},{1,0},{2,6},{3,7},{4,5},{5,4},{6,2},{7,3},{8,9},{9,8},{10,14... | collective-permute-start | bytes 350216 | tf_op jit(solution)/shard_map/ppermute | solution.py:92
  46.8 7.1 %collective-permute-start.19 = (bf16[96,3584]{1,0:T(8,128)(2,1)S(1)}, bf16[96,3584]{1,0:T(8,128)(2,1)S(1)}, u32[]{:S(2)}, u32[]{:S(2)}) collective-permute-start(bf16[96,3584]{1,0:T(8,128)(2,1)S(1)} %get-tuple-element.28), channel_id=1, source_target_pairs={{0,2},{1,3},{2,0},{3,1},{4,6},{5,7},{6,4},{7,5},{8,10},{9,11},{10,... | collective-permute-start | bytes 2064392 | tf_op jit(solution)/shard_map/ppermute | solution.py:92
  47.1 9.8 %collective-permute-start.27 = (bf16[96,3584]{1,0:T(8,128)(2,1)S(1)}, bf16[96,3584]{1,0:T(8,128)(2,1)S(1)}, u32[]{:S(2)}, u32[]{:S(2)}) collective-permute-start(bf16[96,3584]{1,0:T(8,128)(2,1)S(1)} %get-tuple-element.34), channel_id=1, source_target_pairs={{0,2},{1,3},{2,0},{3,1},{4,6},{5,7},{6,4},{7,5},{8,10},{9,11},{10,... | collective-permute-start | bytes 2064392 | tf_op jit(solution)/shard_map/ppermute | solution.py:92
  47.9 6.1 %collective-permute-start.22 = (bf16[32,3584]{1,0:T(8,128)(2,1)S(1)}, bf16[32,3584]{1,0:T(8,128)(2,1)S(1)}, u32[]{:S(2)}, u32[]{:S(2)}) collective-permute-start(bf16[32,3584]{1,0:T(8,128)(2,1)S(1)} %add_convert_fusion.9), channel_id=1, source_target_pairs={{0,4},{1,5},{2,3},{3,2},{4,0},{5,1},{6,7},{7,6},{8,12},{9,13},{10,... | collective-permute-start | bytes 688136 | tf_op jit(solution)/shard_map/ppermute | solution.py:92
  49.9 7.1 %collective-permute-start.30 = (bf16[32,3584]{1,0:T(8,128)(2,1)S(1)}, bf16[32,3584]{1,0:T(8,128)(2,1)S(1)}, u32[]{:S(2)}, u32[]{:S(2)}) collective-permute-start(bf16[32,3584]{1,0:T(8,128)(2,1)S(1)} %add_convert_fusion.2), channel_id=1, source_target_pairs={{0,4},{1,5},{2,3},{3,2},{4,0},{5,1},{6,7},{7,6},{8,12},{9,13},{10,... | collective-permute-start | bytes 688136 | tf_op jit(solution)/shard_map/ppermute | solution.py:92
  54.1 8.5 %collective-permute-start.20 = (bf16[32,3584]{1,0:T(8,128)(2,1)S(1)}, bf16[32,3584]{1,0:T(8,128)(2,1)S(1)}, u32[]{:S(2)}, u32[]{:S(2)}) collective-permute-start(bf16[32,3584]{1,0:T(8,128)(2,1)S(1)} %get-tuple-element.40), channel_id=1, source_target_pairs={{0,4},{1,5},{2,3},{3,2},{4,0},{5,1},{6,7},{7,6},{8,12},{9,13},{10,... | collective-permute-start | bytes 688136 | tf_op jit(solution)/shard_map/ppermute | solution.py:92
  56.1 7.5 %collective-permute-start.23 = (bf16[32,3584]{1,0:T(8,128)(2,1)S(1)}, bf16[32,3584]{1,0:T(8,128)(2,1)S(1)}, u32[]{:S(2)}, u32[]{:S(2)}) collective-permute-start(bf16[32,3584]{1,0:T(8,128)(2,1)S(1)} %get-tuple-element.41), channel_id=1, source_target_pairs={{0,1},{1,0},{2,6},{3,7},{4,5},{5,4},{6,2},{7,3},{8,9},{9,8},{10,14... | collective-permute-start | bytes 688136 | tf_op jit(solution)/shard_map/ppermute | solution.py:92
  57.1 10.9 %collective-permute-start.28 = (bf16[32,3584]{1,0:T(8,128)(2,1)S(1)}, bf16[32,3584]{1,0:T(8,128)(2,1)S(1)}, u32[]{:S(2)}, u32[]{:S(2)}) collective-permute-start(bf16[32,3584]{1,0:T(8,128)(2,1)S(1)} %get-tuple-element.42), channel_id=1, source_target_pairs={{0,4},{1,5},{2,3},{3,2},{4,0},{5,1},{6,7},{7,6},{8,12},{9,13},{10,... | collective-permute-start | bytes 688136 | tf_op jit(solution)/shard_map/ppermute | solution.py:92
  58.5 9.5 %collective-permute-start.31 = (bf16[32,3584]{1,0:T(8,128)(2,1)S(1)}, bf16[32,3584]{1,0:T(8,128)(2,1)S(1)}, u32[]{:S(2)}, u32[]{:S(2)}) collective-permute-start(bf16[32,3584]{1,0:T(8,128)(2,1)S(1)} %get-tuple-element.43), channel_id=1, source_target_pairs={{0,1},{1,0},{2,6},{3,7},{4,5},{5,4},{6,2},{7,3},{8,9},{9,8},{10,14... | collective-permute-start | bytes 688136 | tf_op jit(solution)/shard_map/ppermute | solution.py:92
  63.7 8.8 %collective-permute-start.24 = (bf16[8,3584]{1,0:T(8,128)(2,1)S(1)}, bf16[8,3584]{1,0:T(8,128)(2,1)S(1)}, u32[]{:S(2)}, u32[]{:S(2)}) collective-permute-start(bf16[8,3584]{1,0:T(8,128)(2,1)S(1)} %get-tuple-element.44), channel_id=1, source_target_pairs={{0,8},{1,9},{2,10},{3,11},{4,12},{5,13},{6,14},{7,15},{8,0},{9,1},... | collective-permute-start | bytes 172040 | tf_op jit(solution)/shard_map/ppermute | solution.py:92
  65.0 7.6 %collective-permute-start.26 = (bf16[8,3584]{1,0:T(8,128)(2,1)S(1)}, bf16[8,3584]{1,0:T(8,128)(2,1)S(1)}, u32[]{:S(2)}, u32[]{:S(2)}) collective-permute-start(bf16[8,3584]{1,0:T(8,128)(2,1)S(1)} %get-tuple-element.45), channel_id=1, source_target_pairs={{0,24},{1,25},{2,26},{3,27},{4,28},{5,29},{6,30},{7,31},{8,16},{9,... | collective-permute-start | bytes 172040 | tf_op jit(solution)/shard_map/ppermute | solution.py:92
  67.9 8.0 %collective-permute-start.25 = (bf16[8,3584]{1,0:T(8,128)(2,1)S(1)}, bf16[8,3584]{1,0:T(8,128)(2,1)S(1)}, u32[]{:S(2)}, u32[]{:S(2)}) collective-permute-start(bf16[8,3584]{1,0:T(8,128)(2,1)S(1)} %get-tuple-element.46), channel_id=1, source_target_pairs={{0,16},{1,17},{2,18},{3,19},{4,20},{5,21},{6,22},{7,23},{8,24},{9,... | collective-permute-start | bytes 172040 | tf_op jit(solution)/shard_map/ppermute | solution.py:92
  68.2 7.8 %collective-permute-start.32 = (bf16[8,3584]{1,0:T(8,128)(2,1)S(1)}, bf16[8,3584]{1,0:T(8,128)(2,1)S(1)}, u32[]{:S(2)}, u32[]{:S(2)}) collective-permute-start(bf16[8,3584]{1,0:T(8,128)(2,1)S(1)} %get-tuple-element.47), channel_id=1, source_target_pairs={{0,8},{1,9},{2,10},{3,11},{4,12},{5,13},{6,14},{7,15},{8,0},{9,1},... | collective-permute-start | bytes 172040 | tf_op jit(solution)/shard_map/ppermute | solution.py:92
  69.6 6.4 %collective-permute-start.34 = (bf16[8,3584]{1,0:T(8,128)(2,1)S(1)}, bf16[8,3584]{1,0:T(8,128)(2,1)S(1)}, u32[]{:S(2)}, u32[]{:S(2)}) collective-permute-start(bf16[8,3584]{1,0:T(8,128)(2,1)S(1)} %get-tuple-element.48), channel_id=1, source_target_pairs={{0,24},{1,25},{2,26},{3,27},{4,28},{5,29},{6,30},{7,31},{8,16},{9,... | collective-permute-start | bytes 172040 | tf_op jit(solution)/shard_map/ppermute | solution.py:92
  (12 other events, 41.6 us)

commit v20 on v19

--- a/solution.py
+++ b/solution.py
@@ -381,15 +381,16 @@
     lines[-1], near[-1], far[0], attn_latent = tied((lines[-1], near[-1], far[0], attn_latent))
     later_near = grid.near(join(lines))
     later_far = grid.far(later_near[:-1])
-    far += grid.far(near[-1:])
-    far[-1], later_near[-1], later_far[0] = tied((far[-1], later_near[-1], later_far[0]))
-    rows = later_near[-1].shape[0] // 2
-    last = grid.far([later_near[-1][:rows]])
-    last.append(grid.swap(later_far[0][rows:], grid.first, grid.extent(grid.first) - 1))
-    mine = [[block] for block in near + far]
-    for place, block in zip(mine, later_near + later_far):
-        place.append(block)
-    mine[-1] += last
+
+    def last_place(near, far):
+        rows = near[-1].shape[0] // 2
+        halves = grid.far([near[-1][:rows]])
+        return halves + [grid.swap(far[0][rows:], grid.first, grid.extent(grid.first) - 1)]
+
+    last = last_place(near, far)
+    last, later_near[-1], later_far[0] = tied((last, later_near[-1], later_far[0]))
+    mine = [list(blocks) for blocks in zip(near + far, later_near + later_far)]
+    mine.append(last + last_place(later_near, later_far))
     other = [grid.other(place) for place in mine]
     size, count = high * tokens, len(mine)
     sizes = [size] * count + [size, size * (count - 1)]

time: 78.8 us -> 79.2 us (level)
    ppermute x35 -> x37, waiting for transfers between devices: 25.7 us -> 26.3 us  [swap(): return lax.ppermute(value, everyone, pairs)]
    ppermute x35 -> x37, starting transfers between devices: 34 us -> 33.8 us  [swap(): return lax.ppermute(value, everyone, pairs)]
  transfers between devices with their start and end apart: 35 -> 37, of which waited for: 15 -> 16; matrix products, arithmetic and copies ran while one was open for 1% -> 1% of each run, Pallas kernels for 5% -> 5%
where the time goes in v20:
time: 79.2 us; the launch traced here: 79 us
  starting transfers between devices  33.8 us (43%)
  waiting for transfers between devices  26.3 us (33%)
  Pallas kernels  16.1 us (20%)
  other arithmetic  1.38 us (2%)
    ppermute x37, starting transfers between devices, swap(): return lax.ppermute(value, everyone, pairs)  33.8 us
    ppermute x37, waiting for transfers between devices, swap(): return lax.ppermute(value, everyone, pairs)  26.3 us
    pallas_call x1, Pallas kernels, expert(): pl.pallas_call(functools.partial(expert_kernel, len(blocks), experts, til...  11.3 us
    pallas_call x1, Pallas kernels, attention(): pl.pallas_call(attention_kernel, in_specs=[pl.BlockSpec(memory_space=pltp...  3.66 us
  transfers between devices with their start and end apart: 37, of which 16 were waited for; matrix products, arithmetic and copies ran while one was open for 1% of the time, Pallas kernels for 5%

profile of v20, /device:TPU:0, one launch (start us, length us, event | category | flops | bytes accessed | tf_op | source)
XLA Modules:
  0.0 79.0 jit_solution(149893148745003818)
XLA Ops:
  1.6 3.1 %collective-permute-start = (bf16[8,7296]{1,0:T(8,128)(2,1)S(1)}, bf16[8,7296]{1,0:T(8,128)(2,1)S(1)}, u32[]{:S(2)}, u32[]{:S(2)}) collective-permute-start(bf16[8,7296]{1,0:T(8,128)(2,1)S(1)} %pack.1.refs_0_), channel_id=1, source_target_pairs={{0,8},{1,9},{2,10},{3,11},{4,12},{5,13},{6,14},{7,15},{8,0},{9,1},... | collective-permute-start | bytes 350216 | tf_op jit(solution)/shard_map/ppermute | solution.py:92
  4.7 2.6 %collective-permute-start.1 = (bf16[8,7296]{1,0:T(8,128)(2,1)S(1)}, bf16[8,7296]{1,0:T(8,128)(2,1)S(1)}, u32[]{:S(2)}, u32[]{:S(2)}) collective-permute-start(bf16[8,7296]{1,0:T(8,128)(2,1)S(1)} %pack.1.refs_0_), channel_id=1, source_target_pairs={{0,16},{1,17},{2,18},{3,19},{4,20},{5,21},{6,22},{7,23},{8,24},{9,... | collective-permute-start | bytes 350216 | tf_op jit(solution)/shard_map/ppermute | solution.py:92
  7.3 1.8 %collective-permute-done.refs_1_ = bf16[8,7296]{1,0:T(8,128)(2,1)S(1)} collective-permute-done((bf16[8,7296]{1,0:T(8,128)(2,1)S(1)}, bf16[8,7296]{1,0:T(8,128)(2,1)S(1)}, u32[]{:S(2)}, u32[]{:S(2)}) %collective-permute-start) | collective-permute-done | bytes 116768 | tf_op jit(solution)/shard_map/ppermute | solution.py:92
  9.2 1.9 %collective-permute-start.4 = (bf16[16,7296]{1,0:T(8,128)(2,1)S(1)}, bf16[16,7296]{1,0:T(8,128)(2,1)S(1)}, u32[]{:S(2)}, u32[]{:S(2)}) collective-permute-start(bf16[16,7296]{1,0:T(8,128)(2,1)S(1)} %join.2.refs_0_), channel_id=1, source_target_pairs={{0,4},{1,5},{2,3},{3,2},{4,0},{5,1},{6,7},{7,6},{8,12},{9,13},{10,... | collective-permute-start | bytes 700424 | tf_op jit(solution)/shard_map/ppermute | solution.py:92
  11.1 1.5 %collective-permute-start.3 = (bf16[16,7296]{1,0:T(8,128)(2,1)S(1)}, bf16[16,7296]{1,0:T(8,128)(2,1)S(1)}, u32[]{:S(2)}, u32[]{:S(2)}) collective-permute-start(bf16[16,7296]{1,0:T(8,128)(2,1)S(1)} %join.2.refs_0_), channel_id=1, source_target_pairs={{0,1},{1,0},{2,6},{3,7},{4,5},{5,4},{6,2},{7,3},{8,9},{9,8},{10,14... | collective-permute-start | bytes 700424 | tf_op jit(solution)/shard_map/ppermute | solution.py:92
  13.9 3.7 %attention.1 = bf16[2,64,512]{2,1,0:T(8,128)(2,1)} custom-call(s32[2]{0:T(128)S(1)} %copy-done, bf16[2,64,512]{2,1,0:T(8,128)(2,1)} %refs_0_.3, bf16[2,64,64]{2,1,0:T(8,128)(2,1)} %refs_1_.3, bf16[2,512,512]{2,1,0:T(8,128)(2,1)} %refs_2_.3, bf16[2,64,512]{2,1,0:T(8,128)(2,1)} %refs_3_.1), custom_call_target="tpu_custom_call" | custom-call | flops 134217728 | bytes 1048576 | tf_op jit(solution)/shard_map/attention/pallas_call | solution.py:54
  17.7 1.6 %collective-permute-start.8 = (bf16[16,7296]{1,0:T(8,128)(2,1)S(1)}, bf16[16,7296]{1,0:T(8,128)(2,1)S(1)}, u32[]{:S(2)}, u32[]{:S(2)}) collective-permute-start(bf16[16,7296]{1,0:T(8,128)(2,1)S(1)} %join.3.refs_1_), channel_id=1, source_target_pairs={{0,4},{1,5},{2,3},{3,2},{4,0},{5,1},{6,7},{7,6},{8,12},{9,13},{10,... | collective-permute-start | bytes 700424 | tf_op jit(solution)/shard_map/ppermute | solution.py:92
  19.3 1.6 %collective-permute-start.6 = (bf16[8,7296]{1,0:T(8,128)(2,1)S(1)}, bf16[8,7296]{1,0:T(8,128)(2,1)S(1)}, u32[]{:S(2)}, u32[]{:S(2)}) collective-permute-start(bf16[8,7296]{1,0:T(8,128)(2,1)S(1)} %slice.55), channel_id=1, source_target_pairs={{0,1},{1,0},{2,6},{3,7},{4,5},{5,4},{6,2},{7,3},{8,9},{9,8},{10,14... | collective-permute-start | bytes 350216 | tf_op jit(solution)/shard_map/ppermute | solution.py:92
  21.9 2.2 %collective-permute-done.6.refs_7_ = bf16[8,7296]{1,0:T(8,128)(2,1)S(1)} collective-permute-done((bf16[8,7296]{1,0:T(8,128)(2,1)S(1)}, bf16[8,7296]{1,0:T(8,128)(2,1)S(1)}, u32[]{:S(2)}, u32[]{:S(2)}) %collective-permute-start.6) | collective-permute-done | bytes 116768 | tf_op jit(solution)/shard_map/ppermute | solution.py:92
  24.2 3.5 %collective-permute-done.5.refs_6_ = bf16[8,7296]{1,0:T(8,128)(2,1)S(1)} collective-permute-done((bf16[8,7296]{1,0:T(8,128)(2,1)S(1)}, bf16[8,7296]{1,0:T(8,128)(2,1)S(1)}, u32[]{:S(2)}, u32[]{:S(2)}) %collective-permute-start.5) | collective-permute-done | bytes 116768 | tf_op jit(solution)/shard_map/ppermute | solution.py:92
  28.2 1.4 %collective-permute-start.10 = (bf16[8,7296]{1,0:T(8,128)(2,1)S(1)}, bf16[8,7296]{1,0:T(8,128)(2,1)S(1)}, u32[]{:S(2)}, u32[]{:S(2)}) collective-permute-start(bf16[8,7296]{1,0:T(8,128)(2,1)S(1)} %slice.57), channel_id=1, source_target_pairs={{0,1},{1,0},{2,6},{3,7},{4,5},{5,4},{6,2},{7,3},{8,9},{9,8},{10,14... | collective-permute-start | bytes 350216 | tf_op jit(solution)/shard_map/ppermute | solution.py:92
  31.2 2.8 %collective-permute-done.10.refs_9_ = bf16[8,7296]{1,0:T(8,128)(2,1)S(1)} collective-permute-done((bf16[8,7296]{1,0:T(8,128)(2,1)S(1)}, bf16[8,7296]{1,0:T(8,128)(2,1)S(1)}, u32[]{:S(2)}, u32[]{:S(2)}) %collective-permute-start.10) | collective-permute-done | bytes 116768 | tf_op jit(solution)/shard_map/ppermute | solution.py:92
  36.1 11.3 %expert.1 = (bf16[32,3584]{1,0:T(8,128)(2,1)S(1)}, bf16[32,3584]{1,0:T(8,128)(2,1)S(1)}, bf16[32,3584]{1,0:T(8,128)(2,1)S(1)}, bf16[32,3584]{1,0:T(8,128)(2,1)S(...) custom-call(s32[1]{0:T(128)} %bitcast.node_ref, ...), custom_call_target="tpu_custom_call" | custom-call | flops 5637144576 | bytes 22020096 | tf_op jit(solution)/shard_map/expert/pallas_call | solution.py:321
  49.1 1.1 %collective-permute-start.24 = (bf16[32,3584]{1,0:T(8,128)(2,1)S(1)}, bf16[32,3584]{1,0:T(8,128)(2,1)S(1)}, u32[]{:S(2)}, u32[]{:S(2)}) collective-permute-start(bf16[32,3584]{1,0:T(8,128)(2,1)S(1)} %add_convert_fusion.9), channel_id=1, source_target_pairs={{0,4},{1,5},{2,3},{3,2},{4,0},{5,1},{6,7},{7,6},{8,12},{9,13},{10,... | collective-permute-start | bytes 688136 | tf_op jit(solution)/shard_map/ppermute | solution.py:92
  51.3 3.9 %collective-permute-done.24 = bf16[32,3584]{1,0:T(8,128)(2,1)S(1)} collective-permute-done((bf16[32,3584]{1,0:T(8,128)(2,1)S(1)}, bf16[32,3584]{1,0:T(8,128)(2,1)S(1)}, u32[]{:S(2)}, u32[]{:S(2)}) %collective-permute-start.24) | collective-permute-done | bytes 229408 | tf_op jit(solution)/shard_map/ppermute | solution.py:92
  55.3 1.1 %collective-permute-start.22 = (bf16[32,3584]{1,0:T(8,128)(2,1)S(1)}, bf16[32,3584]{1,0:T(8,128)(2,1)S(1)}, u32[]{:S(2)}, u32[]{:S(2)}) collective-permute-start(bf16[32,3584]{1,0:T(8,128)(2,1)S(1)} %get-tuple-element.42), channel_id=1, source_target_pairs={{0,4},{1,5},{2,3},{3,2},{4,0},{5,1},{6,7},{7,6},{8,12},{9,13},{10,... | collective-permute-start | bytes 688136 | tf_op jit(solution)/shard_map/ppermute | solution.py:92
  56.4 1.3 %collective-permute-start.25 = (bf16[32,3584]{1,0:T(8,128)(2,1)S(1)}, bf16[32,3584]{1,0:T(8,128)(2,1)S(1)}, u32[]{:S(2)}, u32[]{:S(2)}) collective-permute-start(bf16[32,3584]{1,0:T(8,128)(2,1)S(1)} %get-tuple-element.43), channel_id=1, source_target_pairs={{0,1},{1,0},{2,6},{3,7},{4,5},{5,4},{6,2},{7,3},{8,9},{9,8},{10,14... | collective-permute-start | bytes 688136 | tf_op jit(solution)/shard_map/ppermute | solution.py:92
  59.0 1.3 %collective-permute-start.33 = (bf16[32,3584]{1,0:T(8,128)(2,1)S(1)}, bf16[32,3584]{1,0:T(8,128)(2,1)S(1)}, u32[]{:S(2)}, u32[]{:S(2)}) collective-permute-start(bf16[32,3584]{1,0:T(8,128)(2,1)S(1)} %get-tuple-element.45), channel_id=1, source_target_pairs={{0,1},{1,0},{2,6},{3,7},{4,5},{5,4},{6,2},{7,3},{8,9},{9,8},{10,14... | collective-permute-start | bytes 688136 | tf_op jit(solution)/shard_map/ppermute | solution.py:92
  60.2 3.6 %collective-permute-done.22 = bf16[32,3584]{1,0:T(8,128)(2,1)S(1)} collective-permute-done((bf16[32,3584]{1,0:T(8,128)(2,1)S(1)}, bf16[32,3584]{1,0:T(8,128)(2,1)S(1)}, u32[]{:S(2)}, u32[]{:S(2)}) %collective-permute-start.22) | collective-permute-done | bytes 229408 | tf_op jit(solution)/shard_map/ppermute | solution.py:92
  65.8 2.8 %collective-permute-start.28 = (bf16[8,3584]{1,0:T(8,128)(2,1)S(1)}, bf16[8,3584]{1,0:T(8,128)(2,1)S(1)}, u32[]{:S(2)}, u32[]{:S(2)}) collective-permute-start(bf16[8,3584]{1,0:T(8,128)(2,1)S(1)} %get-tuple-element.47), channel_id=1, source_target_pairs={{0,24},{1,25},{2,26},{3,27},{4,28},{5,29},{6,30},{7,31},{8,16},{9,... | collective-permute-start | bytes 172040 | tf_op jit(solution)/shard_map/ppermute | solution.py:92
  68.9 1.5 %collective-permute-start.34 = (bf16[8,3584]{1,0:T(8,128)(2,1)S(1)}, bf16[8,3584]{1,0:T(8,128)(2,1)S(1)}, u32[]{:S(2)}, u32[]{:S(2)}) collective-permute-start(bf16[8,3584]{1,0:T(8,128)(2,1)S(1)} %get-tuple-element.49), channel_id=1, source_target_pairs={{0,8},{1,9},{2,10},{3,11},{4,12},{5,13},{6,14},{7,15},{8,0},{9,1},... | collective-permute-start | bytes 172040 | tf_op jit(solution)/shard_map/ppermute | solution.py:92
  70.4 2.8 %collective-permute-start.36 = (bf16[8,3584]{1,0:T(8,128)(2,1)S(1)}, bf16[8,3584]{1,0:T(8,128)(2,1)S(1)}, u32[]{:S(2)}, u32[]{:S(2)}) collective-permute-start(bf16[8,3584]{1,0:T(8,128)(2,1)S(1)} %get-tuple-element.50), channel_id=1, source_target_pairs={{0,24},{1,25},{2,26},{3,27},{4,28},{5,29},{6,30},{7,31},{8,16},{9,... | collective-permute-start | bytes 172040 | tf_op jit(solution)/shard_map/ppermute | solution.py:92
  73.2 2.3 %collective-permute-done.27 = bf16[8,3584]{1,0:T(8,128)(2,1)S(1)} collective-permute-done((bf16[8,3584]{1,0:T(8,128)(2,1)S(1)}, bf16[8,3584]{1,0:T(8,128)(2,1)S(1)}, u32[]{:S(2)}, u32[]{:S(2)}) %collective-permute-start.27) | collective-permute-done | bytes 57376 | tf_op jit(solution)/shard_map/ppermute | solution.py:92
  76.4 1.9 %collective-permute-done.35 = bf16[8,3584]{1,0:T(8,128)(2,1)S(1)} collective-permute-done((bf16[8,3584]{1,0:T(8,128)(2,1)S(1)}, bf16[8,3584]{1,0:T(8,128)(2,1)S(1)}, u32[]{:S(2)}, u32[]{:S(2)}) %collective-permute-start.35) | collective-permute-done | bytes 57376 | tf_op jit(solution)/shard_map/ppermute | solution.py:92
  (72 shorter events, 15.7 us)
Async XLA Ops:
  1.6 7.5 %collective-permute-start = (bf16[8,7296]{1,0:T(8,128)(2,1)S(1)}, bf16[8,7296]{1,0:T(8,128)(2,1)S(1)}, u32[]{:S(2)}, u32[]{:S(2)}) collective-permute-start(bf16[8,7296]{1,0:T(8,128)(2,1)S(1)} %pack.1.refs_0_), channel_id=1, source_target_pairs={{0,8},{1,9},{2,10},{3,11},{4,12},{5,13},{6,14},{7,15},{8,0},{9,1},... | collective-permute-start | bytes 350216 | tf_op jit(solution)/shard_map/ppermute | solution.py:92
  4.7 8.1 %collective-permute-start.1 = (bf16[8,7296]{1,0:T(8,128)(2,1)S(1)}, bf16[8,7296]{1,0:T(8,128)(2,1)S(1)}, u32[]{:S(2)}, u32[]{:S(2)}) collective-permute-start(bf16[8,7296]{1,0:T(8,128)(2,1)S(1)} %pack.1.refs_0_), channel_id=1, source_target_pairs={{0,16},{1,17},{2,18},{3,19},{4,20},{5,21},{6,22},{7,23},{8,24},{9,... | collective-permute-start | bytes 350216 | tf_op jit(solution)/shard_map/ppermute | solution.py:92
  9.2 8.5 %collective-permute-start.4 = (bf16[16,7296]{1,0:T(8,128)(2,1)S(1)}, bf16[16,7296]{1,0:T(8,128)(2,1)S(1)}, u32[]{:S(2)}, u32[]{:S(2)}) collective-permute-start(bf16[16,7296]{1,0:T(8,128)(2,1)S(1)} %join.2.refs_0_), channel_id=1, source_target_pairs={{0,4},{1,5},{2,3},{3,2},{4,0},{5,1},{6,7},{7,6},{8,12},{9,13},{10,... | collective-permute-start | bytes 700424 | tf_op jit(solution)/shard_map/ppermute | solution.py:92
  11.1 6.6 %collective-permute-start.3 = (bf16[16,7296]{1,0:T(8,128)(2,1)S(1)}, bf16[16,7296]{1,0:T(8,128)(2,1)S(1)}, u32[]{:S(2)}, u32[]{:S(2)}) collective-permute-start(bf16[16,7296]{1,0:T(8,128)(2,1)S(1)} %join.2.refs_0_), channel_id=1, source_target_pairs={{0,1},{1,0},{2,6},{3,7},{4,5},{5,4},{6,2},{7,3},{8,9},{9,8},{10,14... | collective-permute-start | bytes 700424 | tf_op jit(solution)/shard_map/ppermute | solution.py:92
  17.7 10.0 %collective-permute-start.8 = (bf16[16,7296]{1,0:T(8,128)(2,1)S(1)}, bf16[16,7296]{1,0:T(8,128)(2,1)S(1)}, u32[]{:S(2)}, u32[]{:S(2)}) collective-permute-start(bf16[16,7296]{1,0:T(8,128)(2,1)S(1)} %join.3.refs_1_), channel_id=1, source_target_pairs={{0,4},{1,5},{2,3},{3,2},{4,0},{5,1},{6,7},{7,6},{8,12},{9,13},{10,... | collective-permute-start | bytes 700424 | tf_op jit(solution)/shard_map/ppermute | solution.py:92
  20.8 6.9 %collective-permute-start.5 = (bf16[8,7296]{1,0:T(8,128)(2,1)S(1)}, bf16[8,7296]{1,0:T(8,128)(2,1)S(1)}, u32[]{:S(2)}, u32[]{:S(2)}) collective-permute-start(bf16[8,7296]{1,0:T(8,128)(2,1)S(1)} %slice.54), channel_id=1, source_target_pairs={{0,4},{1,5},{2,3},{3,2},{4,0},{5,1},{6,7},{7,6},{8,12},{9,13},{10,... | collective-permute-start | bytes 350216 | tf_op jit(solution)/shard_map/ppermute | solution.py:92
  21.4 6.8 %collective-permute-start.7 = (bf16[16,7296]{1,0:T(8,128)(2,1)S(1)}, bf16[16,7296]{1,0:T(8,128)(2,1)S(1)}, u32[]{:S(2)}, u32[]{:S(2)}) collective-permute-start(bf16[16,7296]{1,0:T(8,128)(2,1)S(1)} %join.3.refs_1_), channel_id=1, source_target_pairs={{0,1},{1,0},{2,6},{3,7},{4,5},{5,4},{6,2},{7,3},{8,9},{9,8},{10,14... | collective-permute-start | bytes 700424 | tf_op jit(solution)/shard_map/ppermute | solution.py:92
  21.9 7.7 %collective-permute-start.15 = (bf16[16,7296]{1,0:T(8,128)(2,1)S(1)}, bf16[16,7296]{1,0:T(8,128)(2,1)S(1)}, u32[]{:S(2)}, u32[]{:S(2)}) collective-permute-start(bf16[16,7296]{1,0:T(8,128)(2,1)S(1)} %join.2.refs_0_), channel_id=1, source_target_pairs={{0,2},{1,3},{2,0},{3,1},{4,6},{5,7},{6,4},{7,5},{8,10},{9,11},{10,... | collective-permute-start | bytes 700424 | tf_op jit(solution)/shard_map/ppermute | solution.py:92
  24.1 6.5 %collective-permute-start.16 = (bf16[16,7296]{1,0:T(8,128)(2,1)S(1)}, bf16[16,7296]{1,0:T(8,128)(2,1)S(1)}, u32[]{:S(2)}, u32[]{:S(2)}) collective-permute-start(bf16[16,7296]{1,0:T(8,128)(2,1)S(1)} %join.3.refs_1_), channel_id=1, source_target_pairs={{0,2},{1,3},{2,0},{3,1},{4,6},{5,7},{6,4},{7,5},{8,10},{9,11},{10,... | collective-permute-start | bytes 700424 | tf_op jit(solution)/shard_map/ppermute | solution.py:92
  28.2 5.8 %collective-permute-start.10 = (bf16[8,7296]{1,0:T(8,128)(2,1)S(1)}, bf16[8,7296]{1,0:T(8,128)(2,1)S(1)}, u32[]{:S(2)}, u32[]{:S(2)}) collective-permute-start(bf16[8,7296]{1,0:T(8,128)(2,1)S(1)} %slice.57), channel_id=1, source_target_pairs={{0,1},{1,0},{2,6},{3,7},{4,5},{5,4},{6,2},{7,3},{8,9},{9,8},{10,14... | collective-permute-start | bytes 350216 | tf_op jit(solution)/shard_map/ppermute | solution.py:92
  30.7 5.5 %collective-permute-start.18 = (bf16[16,7296]{1,0:T(8,128)(2,1)S(1)}, bf16[16,7296]{1,0:T(8,128)(2,1)S(1)}, u32[]{:S(2)}, u32[]{:S(2)}) collective-permute-start(bf16[16,7296]{1,0:T(8,128)(2,1)S(1)} %collective-permute-done.7.refs_3_), channel_id=1, source_target_pairs={{0,2},{1,3},{2,0},{3,1},{4,6},{5,7},{6,4},{7,5},{8,10},{9,11},{10,... | collective-permute-start | bytes 700424 | tf_op jit(solution)/shard_map/ppermute | solution.py:92
  48.0 7.1 %collective-permute-start.21 = (bf16[96,3584]{1,0:T(8,128)(2,1)S(1)}, bf16[96,3584]{1,0:T(8,128)(2,1)S(1)}, u32[]{:S(2)}, u32[]{:S(2)}) collective-permute-start(bf16[96,3584]{1,0:T(8,128)(2,1)S(1)} %get-tuple-element.30), channel_id=1, source_target_pairs={{0,2},{1,3},{2,0},{3,1},{4,6},{5,7},{6,4},{7,5},{8,10},{9,11},{10,... | collective-permute-start | bytes 2064392 | tf_op jit(solution)/shard_map/ppermute | solution.py:92
  48.4 9.4 %collective-permute-start.29 = (bf16[96,3584]{1,0:T(8,128)(2,1)S(1)}, bf16[96,3584]{1,0:T(8,128)(2,1)S(1)}, u32[]{:S(2)}, u32[]{:S(2)}) collective-permute-start(bf16[96,3584]{1,0:T(8,128)(2,1)S(1)} %get-tuple-element.36), channel_id=1, source_target_pairs={{0,2},{1,3},{2,0},{3,1},{4,6},{5,7},{6,4},{7,5},{8,10},{9,11},{10,... | collective-permute-start | bytes 2064392 | tf_op jit(solution)/shard_map/ppermute | solution.py:92
  49.1 6.1 %collective-permute-start.24 = (bf16[32,3584]{1,0:T(8,128)(2,1)S(1)}, bf16[32,3584]{1,0:T(8,128)(2,1)S(1)}, u32[]{:S(2)}, u32[]{:S(2)}) collective-permute-start(bf16[32,3584]{1,0:T(8,128)(2,1)S(1)} %add_convert_fusion.9), channel_id=1, source_target_pairs={{0,4},{1,5},{2,3},{3,2},{4,0},{5,1},{6,7},{7,6},{8,12},{9,13},{10,... | collective-permute-start | bytes 688136 | tf_op jit(solution)/shard_map/ppermute | solution.py:92
  50.2 7.5 %collective-permute-start.32 = (bf16[32,3584]{1,0:T(8,128)(2,1)S(1)}, bf16[32,3584]{1,0:T(8,128)(2,1)S(1)}, u32[]{:S(2)}, u32[]{:S(2)}) collective-permute-start(bf16[32,3584]{1,0:T(8,128)(2,1)S(1)} %add_convert_fusion.2), channel_id=1, source_target_pairs={{0,4},{1,5},{2,3},{3,2},{4,0},{5,1},{6,7},{7,6},{8,12},{9,13},{10,... | collective-permute-start | bytes 688136 | tf_op jit(solution)/shard_map/ppermute | solution.py:92
  55.3 8.5 %collective-permute-start.22 = (bf16[32,3584]{1,0:T(8,128)(2,1)S(1)}, bf16[32,3584]{1,0:T(8,128)(2,1)S(1)}, u32[]{:S(2)}, u32[]{:S(2)}) collective-permute-start(bf16[32,3584]{1,0:T(8,128)(2,1)S(1)} %get-tuple-element.42), channel_id=1, source_target_pairs={{0,4},{1,5},{2,3},{3,2},{4,0},{5,1},{6,7},{7,6},{8,12},{9,13},{10,... | collective-permute-start | bytes 688136 | tf_op jit(solution)/shard_map/ppermute | solution.py:92
  56.4 8.4 %collective-permute-start.25 = (bf16[32,3584]{1,0:T(8,128)(2,1)S(1)}, bf16[32,3584]{1,0:T(8,128)(2,1)S(1)}, u32[]{:S(2)}, u32[]{:S(2)}) collective-permute-start(bf16[32,3584]{1,0:T(8,128)(2,1)S(1)} %get-tuple-element.43), channel_id=1, source_target_pairs={{0,1},{1,0},{2,6},{3,7},{4,5},{5,4},{6,2},{7,3},{8,9},{9,8},{10,14... | collective-permute-start | bytes 688136 | tf_op jit(solution)/shard_map/ppermute | solution.py:92
  57.9 10.9 %collective-permute-start.30 = (bf16[32,3584]{1,0:T(8,128)(2,1)S(1)}, bf16[32,3584]{1,0:T(8,128)(2,1)S(1)}, u32[]{:S(2)}, u32[]{:S(2)}) collective-permute-start(bf16[32,3584]{1,0:T(8,128)(2,1)S(1)} %get-tuple-element.44), channel_id=1, source_target_pairs={{0,4},{1,5},{2,3},{3,2},{4,0},{5,1},{6,7},{7,6},{8,12},{9,13},{10,... | collective-permute-start | bytes 688136 | tf_op jit(solution)/shard_map/ppermute | solution.py:92
  59.0 9.8 %collective-permute-start.33 = (bf16[32,3584]{1,0:T(8,128)(2,1)S(1)}, bf16[32,3584]{1,0:T(8,128)(2,1)S(1)}, u32[]{:S(2)}, u32[]{:S(2)}) collective-permute-start(bf16[32,3584]{1,0:T(8,128)(2,1)S(1)} %get-tuple-element.45), channel_id=1, source_target_pairs={{0,1},{1,0},{2,6},{3,7},{4,5},{5,4},{6,2},{7,3},{8,9},{9,8},{10,14... | collective-permute-start | bytes 688136 | tf_op jit(solution)/shard_map/ppermute | solution.py:92
  65.0 8.2 %collective-permute-start.26 = (bf16[8,3584]{1,0:T(8,128)(2,1)S(1)}, bf16[8,3584]{1,0:T(8,128)(2,1)S(1)}, u32[]{:S(2)}, u32[]{:S(2)}) collective-permute-start(bf16[8,3584]{1,0:T(8,128)(2,1)S(1)} %get-tuple-element.46), channel_id=1, source_target_pairs={{0,8},{1,9},{2,10},{3,11},{4,12},{5,13},{6,14},{7,15},{8,0},{9,1},... | collective-permute-start | bytes 172040 | tf_op jit(solution)/shard_map/ppermute | solution.py:92
  65.8 7.4 %collective-permute-start.28 = (bf16[8,3584]{1,0:T(8,128)(2,1)S(1)}, bf16[8,3584]{1,0:T(8,128)(2,1)S(1)}, u32[]{:S(2)}, u32[]{:S(2)}) collective-permute-start(bf16[8,3584]{1,0:T(8,128)(2,1)S(1)} %get-tuple-element.47), channel_id=1, source_target_pairs={{0,24},{1,25},{2,26},{3,27},{4,28},{5,29},{6,30},{7,31},{8,16},{9,... | collective-permute-start | bytes 172040 | tf_op jit(solution)/shard_map/ppermute | solution.py:92
  68.6 6.9 %collective-permute-start.27 = (bf16[8,3584]{1,0:T(8,128)(2,1)S(1)}, bf16[8,3584]{1,0:T(8,128)(2,1)S(1)}, u32[]{:S(2)}, u32[]{:S(2)}) collective-permute-start(bf16[8,3584]{1,0:T(8,128)(2,1)S(1)} %get-tuple-element.48), channel_id=1, source_target_pairs={{0,16},{1,17},{2,18},{3,19},{4,20},{5,21},{6,22},{7,23},{8,24},{9,... | collective-permute-start | bytes 172040 | tf_op jit(solution)/shard_map/ppermute | solution.py:92
  68.9 6.6 %collective-permute-start.34 = (bf16[8,3584]{1,0:T(8,128)(2,1)S(1)}, bf16[8,3584]{1,0:T(8,128)(2,1)S(1)}, u32[]{:S(2)}, u32[]{:S(2)}) collective-permute-start(bf16[8,3584]{1,0:T(8,128)(2,1)S(1)} %get-tuple-element.49), channel_id=1, source_target_pairs={{0,8},{1,9},{2,10},{3,11},{4,12},{5,13},{6,14},{7,15},{8,0},{9,1},... | collective-permute-start | bytes 172040 | tf_op jit(solution)/shard_map/ppermute | solution.py:92
  70.4 6.0 %collective-permute-start.36 = (bf16[8,3584]{1,0:T(8,128)(2,1)S(1)}, bf16[8,3584]{1,0:T(8,128)(2,1)S(1)}, u32[]{:S(2)}, u32[]{:S(2)}) collective-permute-start(bf16[8,3584]{1,0:T(8,128)(2,1)S(1)} %get-tuple-element.50), channel_id=1, source_target_pairs={{0,24},{1,25},{2,26},{3,27},{4,28},{5,29},{6,30},{7,31},{8,16},{9,... | collective-permute-start | bytes 172040 | tf_op jit(solution)/shard_map/ppermute | solution.py:92
  (14 other events, 43.8 us)
